TPU v7x, 32 devices: a whole 2x2x4 slice. The times are simulated.
32 devices in a mesh: section: 4 (over y, core), video: 2 (over x), dp: 4 (over z).
Axes of the slice: x: 2, y: 2, z: 4, core: 2. Of those that a mesh axis runs over, the one named last changes fastest.
Arguments:
- grad_latent: bfloat16 [4, 2, 64, 64, 128], P('dp', 'video', 'section'), may hold values from -6 to 6
- input_one: bfloat16 [4, 2, 64, 64, 128], P('dp', 'video', 'section'), may hold values from -6 to 6
- preact_one: bfloat16 [4, 2, 64, 64, 128], P('dp', 'video', 'section'), may hold values from -8 to 8
- input_two: bfloat16 [4, 2, 64, 64, 128], P('dp', 'video', 'section'), may hold values from -6 to 6
- preact_two: bfloat16 [4, 2, 64, 64, 128], P('dp', 'video', 'section'), may hold values from -8 to 8
- spatial_one: bfloat16 [3, 3, 128, 128], replicated, may hold values from -0.1875 to 0.1875
- temporal_one: bfloat16 [3, 128, 128], replicated, may hold values from -0.3125 to 0.3125
- spatial_two: bfloat16 [3, 3, 128, 128], replicated, may hold values from -0.1875 to 0.1875
- temporal_two: bfloat16 [3, 128, 128], replicated, may hold values from -0.3125 to 0.3125
Outputs:
- grad_input: bfloat16 [4, 2, 64, 64, 128], P('dp', 'video', 'section')
- grad_spatial_one: float32 [3, 3, 128, 128], replicated
- grad_temporal_one: float32 [3, 128, 128], replicated
- grad_spatial_two: float32 [3, 3, 128, 128], replicated
- grad_temporal_two: float32 [3, 128, 128], replicated
All inputs are finite; a program needn't handle non-finite values.
Results may differ from a plain program's by a relative error of at most 0.0061.
Values may be sent and summed in bfloat16 or wider, within the bound.
No kernel may reach another device: no remote copies, remote signals or barrier semaphores. Data moves between devices by JAX's collectives and lax.ppermute only.
A program may use at most 64 MiB of HBM per device.

v0:
```python
import math

import jax
import jax.numpy as jnp
from jax import lax
from jax.sharding import PartitionSpec as P


def with_halo(block, sides, width):
    for axis, dim in sides:
        count = lax.axis_size(axis)
        forward = [(i, i + 1) for i in range(count - 1)]
        backward = [(target, source) for source, target in forward]
        low = lax.ppermute(
            lax.slice_in_dim(block, block.shape[dim] - width, None, axis=dim), axis, forward
        )
        high = lax.ppermute(lax.slice_in_dim(block, 0, width, axis=dim), axis, backward)
        block = jnp.concatenate([low, block, high], axis=dim)
    return block


def temporal_terms(gcat, acat, grad_out, kernel):
    width = grad_out.shape[-1]
    flipped = jnp.transpose(kernel, (0, 2, 1)).reshape(3 * width, width)
    flat_g = gcat.reshape(-1, 3 * width)
    flat_a = acat.reshape(-1, 3 * width)
    gact = jnp.dot(flat_g, flipped, preferred_element_type=jnp.float32)
    kgrad = lax.dot_general(
        flat_a,
        grad_out.reshape(-1, width),
        (((0,), (0,)), ((), ())),
        preferred_element_type=jnp.float32,
    )
    return (gact.astype(jnp.bfloat16).reshape(grad_out.shape), kgrad.reshape(3, width, width))


def temporal_back(grad_out, act, kernel):
    band_g, band_a = (
        lax.all_to_all(grad_out, "video", split_axis=2, concat_axis=1, tiled=True),
        lax.all_to_all(act, "video", split_axis=2, concat_axis=1, tiled=True),
    )
    frames = band_g.shape[1]
    gpad = jnp.pad(band_g, ((0, 0), (0, 2), (0, 0), (0, 0), (0, 0)))
    apad = jnp.pad(band_a, ((0, 0), (2, 0), (0, 0), (0, 0), (0, 0)))
    gcat = jnp.concatenate(
        [gpad[:, 2 : 2 + frames], gpad[:, 1 : 1 + frames], gpad[:, 0:frames]], axis=-1
    )
    acat = jnp.concatenate(
        [apad[:, 0:frames], apad[:, 1 : 1 + frames], apad[:, 2 : 2 + frames]], axis=-1
    )
    band_ga, kgrad = temporal_terms(gcat, acat, band_g, kernel)
    gact = lax.all_to_all(band_ga, "video", split_axis=1, concat_axis=2, tiled=True)
    return (gact, kgrad)


def patches(field, rows, cols, sign):
    views = []
    for ky in range(3):
        for kx in range(3):
            top = 1 + sign * (ky - 1)
            left = 1 + sign * (kx - 1)
            views.append(field[top : top + rows, left : left + cols])
    width = field.shape[-1]
    return jnp.concatenate(views, axis=-1).reshape(rows * cols, 9 * width)


def spatial_back(saved_in, gpre, spatial, grad_out):
    rows, cols, width = (saved_in.shape[2], saved_in.shape[3], saved_in.shape[4])
    stacked = jnp.stack((saved_in, gpre))
    padded = with_halo(stacked, (("section", 3),), 1)
    padded = jnp.pad(padded, ((0, 0), (0, 0), (0, 0), (0, 0), (1, 1), (0, 0)))
    in_cols = patches(padded[0, 0, 0], rows, cols, 1)
    grad_cols = patches(padded[1, 0, 0], rows, cols, -1)
    flipped = jnp.transpose(spatial, (0, 1, 3, 2)).reshape(9 * width, width)
    summed = grad_out.astype(jnp.float32).reshape(rows * cols, width) + jnp.dot(
        grad_cols, flipped, preferred_element_type=jnp.float32
    )
    kgrad = lax.dot_general(
        in_cols,
        gpre.reshape(rows * cols, width),
        (((0,), (0,)), ((), ())),
        preferred_element_type=jnp.float32,
    )
    return (summed.astype(jnp.bfloat16).reshape(saved_in.shape), kgrad.reshape(3, 3, width, width))


def block_back(grad_out, saved_in, preact, spatial, temporal):
    hval = preact.astype(jnp.float32)
    sig = jax.nn.sigmoid(hval)
    act = (hval * sig).astype(jnp.bfloat16)
    gact, kgrad_t = temporal_back(grad_out, act, temporal)
    gpre = (gact.astype(jnp.float32) * sig * (1.0 + hval * (1.0 - sig))).astype(jnp.bfloat16)
    grad_in, kgrad_s = spatial_back(saved_in, gpre, spatial, grad_out)
    return (grad_in, kgrad_s, kgrad_t)


def on_device(
    grad_latent,
    input_one,
    preact_one,
    input_two,
    preact_two,
    spatial_one,
    temporal_one,
    spatial_two,
    temporal_two,
):
    pixels = (
        lax.axis_size("dp")
        * lax.axis_size("video")
        * lax.axis_size("section")
        * grad_latent.shape[2]
        * grad_latent.shape[3]
    )
    factor = 1.0 / math.sqrt(pixels)
    grad_mid, gs_two, gt_two = block_back(
        grad_latent, input_two, preact_two, spatial_two, temporal_two
    )
    grad_in, gs_one, gt_one = block_back(grad_mid, input_one, preact_one, spatial_one, temporal_one)
    gs_one, gt_one, gs_two, gt_two = lax.psum(
        (gs_one, gt_one, gs_two, gt_two), ("section", "video", "dp")
    )
    return (grad_in, factor * gs_one, factor * gt_one, factor * gs_two, factor * gt_two)


def solution(mesh):
    return jax.shard_map(
        on_device,
        mesh=mesh,
        in_specs=(
            P("dp", "video", "section", None, None),
            P("dp", "video", "section", None, None),
            P("dp", "video", "section", None, None),
            P("dp", "video", "section", None, None),
            P("dp", "video", "section", None, None),
            P(),
            P(),
            P(),
            P(),
        ),
        out_specs=(P("dp", "video", "section", None, None), P(), P(), P(), P()),
        check_vma=False,
    )
```

profile of v0, /device:TPU:1, one launch (start us, length us, event | category | flops | bytes accessed | tf_op | source)
XLA Modules:
  0.0 235.0 jit_solution(12043106384747858330)
XLA Ops:
  7.2 3.6 %all-to-all-start = ((bf16[1,1,16,64,128]{4,3,1,0,2:T(8,128)(2,1)}), bf16[1,1,16,64,128]{4,3,1,0,2:T(8,128)(2,1)S(1)}, u32[]{:S(2)}, u32[]{:S(2)}) async-start(bf16[1,1,16,64,128]{4,3,1,0,2:T(8,128)(2,1)} %bitcast.138), calls=%async_computation | async-start | bytes 524288 | tf_op jit(solution)/shard_map/all_to_all | solution.py:39
  10.8 1.0 copy.27
  11.8 4.4 %all-to-all-done = bf16[1,1,16,64,128]{4,3,1,0,2:T(8,128)(2,1)S(1)} async-done(((bf16[1,1,16,64,128]{4,3,1,0,2:T(8,128)(2,1)}), bf16[1,1,16,64,128]{4,3,1,0,2:T(8,128)(2,1)S(1)}, u32[]{:S(2)}, u32[]{:S(2)}) %all-to-all-start) | async-done | bytes 262176 | tf_op jit(solution)/shard_map/all_to_all | solution.py:39
  16.7 6.4 %all_to_all.66 = bf16[1,2,8,64,128]{4,3,2,0,1:T(8,128)(2,1)S(1)} all-to-all(bf16[1,2,8,64,128]{4,3,2,0,1:T(8,128)(2,1)S(1)} %bitcast.140), channel_id=1, replica_groups=mesh['section'=4,'video'=2,'dp'=4] {'video'}, dimensions={1} | all-to-all | bytes 524288 | tf_op jit(solution)/shard_map/all_to_all | solution.py:52
  23.1 1.0 fusion.20
  24.1 5.7 %collective-permute-start = (bf16[2,1,1,1,64,128]{5,4,3,2,1,0:T(8,128)(2,1)S(1)}, bf16[2,1,1,1,64,128]{5,4,3,2,1,0:T(8,128)(2,1)S(1)}, u32[]{:S(2)}, u32[]{:S(2)}) collective-permute-start(bf16[2,1,1,1,64,128]{5,4,3,2,1,0:T(8,128)(2,1)S(1)} %get-tuple-element.15), channel_id=1, source_target_pairs={{0,8},{8,16},{16,24},{1,9},{9,17},{17,25},{2,10},{10,18},{18,26},{... | collective-permute-start | bytes 98312 | tf_op jit(solution)/shard_map/ppermute | solution.py:14
  29.7 1.9 collective-permute-start.1
  31.9 3.1 %collective-permute-done.1 = bf16[2,1,1,1,64,128]{5,4,3,2,1,0:T(8,128)(2,1)S(1)} collective-permute-done((bf16[2,1,1,1,64,128]{5,4,3,2,1,0:T(8,128)(2,1)S(1)}, bf16[2,1,1,1,64,128]{5,4,3,2,1,0:T(8,128)(2,1)S(1)}, u32[]{:S(2)}, u32[]{:S(2)}) %collective-permute-start.1) | collective-permute-done | bytes 32800 | tf_op jit(solution)/shard_map/ppermute | solution.py:17
  37.2 1.5 fusion.1
  38.7 3.4 %all-to-all-start.2 = ((bf16[1,1,16,64,128]{4,3,1,0,2:T(8,128)(2,1)}), bf16[1,1,16,64,128]{4,3,1,0,2:T(8,128)(2,1)S(1)}, u32[]{:S(2)}, u32[]{:S(2)}) async-start(bf16[1,1,16,64,128]{4,3,1,0,2:T(8,128)(2,1)} %bitcast.20), calls=%async_computation.2 | async-start | bytes 524288 | tf_op jit(solution)/shard_map/all_to_all | solution.py:39
  42.3 0.9 copy.37
  43.2 2.8 %copy.40 = bf16[1024,1152]{0,1:T(8,128)(2,1)S(1)} copy(bf16[1024,1152]{1,0:T(8,128)(2,1)} %bitcast.119) | data formatting | bytes 4718592 | tf_op jit(solution)/shard_map/reshape | solution.py:64
  46.2 1.1 convolution_convert_fusion
  47.2 4.1 %all-to-all-start.3 = ((bf16[1,2,8,64,128]{4,3,2,0,1:T(8,128)(2,1)}), bf16[1,2,8,64,128]{4,3,2,0,1:T(8,128)(2,1)}, u32[]{:S(2)}, u32[]{:S(2)}) async-start(bf16[1,2,8,64,128]{4,3,2,0,1:T(8,128)(2,1)} %bitcast.27), calls=%async_computation.3 | async-start | bytes 524288 | tf_op jit(solution)/shard_map/all_to_all | solution.py:52
  51.4 1.6 fusion.34
  53.0 3.4 %all-to-all-done.3 = bf16[1,2,8,64,128]{4,3,2,0,1:T(8,128)(2,1)} async-done(((bf16[1,2,8,64,128]{4,3,2,0,1:T(8,128)(2,1)}), bf16[1,2,8,64,128]{4,3,2,0,1:T(8,128)(2,1)}, u32[]{:S(2)}, u32[]{:S(2)}) %all-to-all-start.3) | async-done | bytes 262176 | tf_op jit(solution)/shard_map/all_to_all | solution.py:52
  56.4 3.4 %all-to-all-start.5 = ((bf16[1,1,16,64,128]{4,3,1,0,2:T(8,128)(2,1)}), bf16[1,1,16,64,128]{4,3,1,0,2:T(8,128)(2,1)S(1)}, u32[]{:S(2)}, u32[]{:S(2)}) async-start(bf16[1,1,16,64,128]{4,3,1,0,2:T(8,128)(2,1)} %get-tuple-element.17), calls=%async_computation.5 | async-start | bytes 524288 | tf_op jit(solution)/shard_map/all_to_all | solution.py:40
  59.8 2.0 fusion.27
  61.8 3.3 %collective-permute-start.2 = (bf16[2,1,1,1,64,128]{5,4,3,2,1,0:T(8,128)(2,1)S(1)}, bf16[2,1,1,1,64,128]{5,4,3,2,1,0:T(8,128)(2,1)S(1)}, u32[]{:S(2)}, u32[]{:S(2)}) collective-permute-start(bf16[2,1,1,1,64,128]{5,4,3,2,1,0:T(8,128)(2,1)S(1)} %get-tuple-element.13), channel_id=1, source_target_pairs={{0,8},{8,16},{16,24},{1,9},{9,17},{17,25},{2,10},{10,18},{18,26},{... | collective-permute-start | bytes 98312 | tf_op jit(solution)/shard_map/ppermute | solution.py:14
  65.2 1.9 collective-permute-start.3
  67.9 4.1 %all-to-all-start.4 = ((bf16[1,1,16,64,128]{4,3,1,0,2:T(8,128)(2,1)}), bf16[1,1,16,64,128]{4,3,1,0,2:T(8,128)(2,1)}, u32[]{:S(2)}, u32[]{:S(2)}) async-start(bf16[1,1,16,64,128]{4,3,1,0,2:T(8,128)(2,1)} %get-tuple-element.19), calls=%async_computation.4 | async-start | bytes 524288 | tf_op jit(solution)/shard_map/all_to_all | solution.py:40
  73.3 1.4 copy-done.1
  74.7 2.8 %copy.38 = bf16[1024,1152]{0,1:T(8,128)(2,1)S(1)} copy(bf16[1024,1152]{1,0:T(8,128)(2,1)} %bitcast.120) | data formatting | bytes 4718592 | tf_op jit(solution)/shard_map/reshape | solution.py:64
  81.6 1.6 fusion.32
  84.0 0.9 pad_slice_fusion.1
  84.9 1.4 maximum_bitcast_fusion.1
  87.0 1.1 fusion.35
  88.0 1.1 fusion.33
  91.5 3.2 %fusion.2 = bf16[1024,128]{1,0:T(8,128)(2,1)} fusion(bf16[1024,1152]{1,0:T(8,128)(2,1)} %bitcast.33, bf16[1152,128]{1,0:T(8,128)(2,1)S(1)} %bitcast.136, bf16[1024,128]{1,0:T(8,128)(2,1)} %fusion.1), kind=kOutput, calls=%fused_computation.6 | convolution fusion | flops 302383104 | bytes 3178496 | tf_op jit(solution)/shard_map/dot_general | solution.py:75
  94.6 128.2 %all-reduce.9.cloned.1.call-done = (f32[3,3,128,128]{3,2,1,0:T(8,128)}, f32[3,128,128]{2,1,0:T(8,128)}, f32[3,3,128,128]{3,2,1,0:T(8,128)}, f32[3,128,128]{2,1,0:T(8,128)}) async-done(((f32[3,3,128,128]{3,2,1,0:T(8,128)}, f32[3,128,128]{2,1,0:T(8,128)}, f32[3,3,128,128]{3,2,1,0:T(8,128)}, f32[3,128,128]{2,1,0:T(8,128)}), (f32[3,3,128,128]{3,2,1,0:T(8,128)}, f32[3,128,128]{2,1,0:T(8,128)}, ...) | async-done | bytes 1572880 | tf_op jit(solution)/shard_map/psum | solution.py:120
  222.9 2.0 broadcast_multiply_fusion
  224.8 1.9 broadcast_multiply_fusion.1
  (86 shorter events, 14.2 us)
Async XLA Ops:
  7.2 15.9 %copy-start.9 = (bf16[1,1,16,64,128]{4,3,2,1,0:T(8,128)(2,1)S(1)}, bf16[1,1,16,64,128]{4,3,2,1,0:T(8,128)(2,1)}, u32[]{:S(2)}) copy-start(bf16[1,1,16,64,128]{4,3,2,1,0:T(8,128)(2,1)} %param.13) | copy-start | bytes 786436
  7.2 16.9 %copy-start.3 = (bf16[1,1,16,64,128]{4,3,2,1,0:T(8,128)(2,1)S(1)}, bf16[1,1,16,64,128]{4,3,2,1,0:T(8,128)(2,1)}, u32[]{:S(2)}) copy-start(bf16[1,1,16,64,128]{4,3,2,1,0:T(8,128)(2,1)} %param.12) | copy-start | bytes 786436
  7.2 9.1 %all-to-all-start = ((bf16[1,1,16,64,128]{4,3,1,0,2:T(8,128)(2,1)}), bf16[1,1,16,64,128]{4,3,1,0,2:T(8,128)(2,1)S(1)}, u32[]{:S(2)}, u32[]{:S(2)}) async-start(bf16[1,1,16,64,128]{4,3,1,0,2:T(8,128)(2,1)} %bitcast.138), calls=%async_computation | async-start | bytes 524288 | tf_op jit(solution)/shard_map/all_to_all | solution.py:39
  16.2 15.4 %copy-start.5 = (bf16[3,3,128,128]{3,2,1,0:T(8,128)(2,1)S(1)}, bf16[3,3,128,128]{3,2,1,0:T(8,128)(2,1)}, u32[]{:S(2)}) copy-start(bf16[3,3,128,128]{3,2,1,0:T(8,128)(2,1)} %param.16) | copy-start | bytes 884740
  24.1 7.8 %collective-permute-start = (bf16[2,1,1,1,64,128]{5,4,3,2,1,0:T(8,128)(2,1)S(1)}, bf16[2,1,1,1,64,128]{5,4,3,2,1,0:T(8,128)(2,1)S(1)}, u32[]{:S(2)}, u32[]{:S(2)}) collective-permute-start(bf16[2,1,1,1,64,128]{5,4,3,2,1,0:T(8,128)(2,1)S(1)} %get-tuple-element.15), channel_id=1, source_target_pairs={{0,8},{8,16},{16,24},{1,9},{9,17},{17,25},{2,10},{10,18},{18,26},{... | collective-permute-start | bytes 98312 | tf_op jit(solution)/shard_map/ppermute | solution.py:14
  29.7 5.2 %collective-permute-start.1 = (bf16[2,1,1,1,64,128]{5,4,3,2,1,0:T(8,128)(2,1)S(1)}, bf16[2,1,1,1,64,128]{5,4,3,2,1,0:T(8,128)(2,1)S(1)}, u32[]{:S(2)}, u32[]{:S(2)}) collective-permute-start(bf16[2,1,1,1,64,128]{5,4,3,2,1,0:T(8,128)(2,1)S(1)} %get-tuple-element.16), channel_id=1, source_target_pairs={{8,0},{16,8},{24,16},{9,1},{17,9},{25,17},{10,2},{18,10},{26,18},{... | collective-permute-start | bytes 98312 | tf_op jit(solution)/shard_map/ppermute | solution.py:17
  36.2 1.0 copy-start.8
  37.1 1.5 copy-start
  37.2 5.0 %copy-start.12 = (bf16[3,128,128]{2,1,0:T(8,128)(2,1)S(1)}, bf16[3,128,128]{2,1,0:T(8,128)(2,1)}, u32[]{:S(2)}) copy-start(bf16[3,128,128]{2,1,0:T(8,128)(2,1)} %param.15) | copy-start | bytes 294916
  37.2 5.1 %copy-start.6 = (bf16[3,3,128,128]{3,2,1,0:T(8,128)(2,1)S(1)}, bf16[3,3,128,128]{3,2,1,0:T(8,128)(2,1)}, u32[]{:S(2)}) copy-start(bf16[3,3,128,128]{3,2,1,0:T(8,128)(2,1)} %param.14) | copy-start | bytes 884740
  38.7 7.5 %all-to-all-start.2 = ((bf16[1,1,16,64,128]{4,3,1,0,2:T(8,128)(2,1)}), bf16[1,1,16,64,128]{4,3,1,0,2:T(8,128)(2,1)S(1)}, u32[]{:S(2)}, u32[]{:S(2)}) async-start(bf16[1,1,16,64,128]{4,3,1,0,2:T(8,128)(2,1)} %bitcast.20), calls=%async_computation.2 | async-start | bytes 524288 | tf_op jit(solution)/shard_map/all_to_all | solution.py:39
  47.2 9.1 %all-to-all-start.3 = ((bf16[1,2,8,64,128]{4,3,2,0,1:T(8,128)(2,1)}), bf16[1,2,8,64,128]{4,3,2,0,1:T(8,128)(2,1)}, u32[]{:S(2)}, u32[]{:S(2)}) async-start(bf16[1,2,8,64,128]{4,3,2,0,1:T(8,128)(2,1)} %bitcast.27), calls=%async_computation.3 | async-start | bytes 524288 | tf_op jit(solution)/shard_map/all_to_all | solution.py:52
  51.4 10.5 %copy-start.4 = (bf16[1,1,16,64,128]{4,3,2,1,0:T(8,128)(2,1)S(1)}, bf16[1,1,16,64,128]{4,3,2,1,0:T(8,128)(2,1)}, u32[]{:S(2)}) copy-start(bf16[1,1,16,64,128]{4,3,2,1,0:T(8,128)(2,1)} %param.10) | copy-start | bytes 786436
  56.4 10.7 %all-to-all-start.5 = ((bf16[1,1,16,64,128]{4,3,1,0,2:T(8,128)(2,1)}), bf16[1,1,16,64,128]{4,3,1,0,2:T(8,128)(2,1)S(1)}, u32[]{:S(2)}, u32[]{:S(2)}) async-start(bf16[1,1,16,64,128]{4,3,1,0,2:T(8,128)(2,1)} %get-tuple-element.17), calls=%async_computation.5 | async-start | bytes 524288 | tf_op jit(solution)/shard_map/all_to_all | solution.py:40
  61.8 10.2 %collective-permute-start.2 = (bf16[2,1,1,1,64,128]{5,4,3,2,1,0:T(8,128)(2,1)S(1)}, bf16[2,1,1,1,64,128]{5,4,3,2,1,0:T(8,128)(2,1)S(1)}, u32[]{:S(2)}, u32[]{:S(2)}) collective-permute-start(bf16[2,1,1,1,64,128]{5,4,3,2,1,0:T(8,128)(2,1)S(1)} %get-tuple-element.13), channel_id=1, source_target_pairs={{0,8},{8,16},{16,24},{1,9},{9,17},{17,25},{2,10},{10,18},{18,26},{... | collective-permute-start | bytes 98312 | tf_op jit(solution)/shard_map/ppermute | solution.py:14
  65.2 6.9 %collective-permute-start.3 = (bf16[2,1,1,1,64,128]{5,4,3,2,1,0:T(8,128)(2,1)S(1)}, bf16[2,1,1,1,64,128]{5,4,3,2,1,0:T(8,128)(2,1)S(1)}, u32[]{:S(2)}, u32[]{:S(2)}) collective-permute-start(bf16[2,1,1,1,64,128]{5,4,3,2,1,0:T(8,128)(2,1)S(1)} %get-tuple-element.14), channel_id=1, source_target_pairs={{8,0},{16,8},{24,16},{9,1},{17,9},{25,17},{10,2},{18,10},{26,18},{... | collective-permute-start | bytes 98312 | tf_op jit(solution)/shard_map/ppermute | solution.py:17
  67.1 5.0 %copy-start.2 = (bf16[1,1,16,64,128]{4,3,1,0,2:T(8,128)(2,1)}, bf16[1,1,16,64,128]{4,3,1,0,2:T(8,128)(2,1)S(1)}, u32[]{:S(2)}) copy-start(bf16[1,1,16,64,128]{4,3,1,0,2:T(8,128)(2,1)S(1)} %all-to-all-done.5) | copy-start | bytes 786436
  67.9 16.1 %all-to-all-start.4 = ((bf16[1,1,16,64,128]{4,3,1,0,2:T(8,128)(2,1)}), bf16[1,1,16,64,128]{4,3,1,0,2:T(8,128)(2,1)}, u32[]{:S(2)}, u32[]{:S(2)}) async-start(bf16[1,1,16,64,128]{4,3,1,0,2:T(8,128)(2,1)} %get-tuple-element.19), calls=%async_computation.4 | async-start | bytes 524288 | tf_op jit(solution)/shard_map/all_to_all | solution.py:40
  72.0 150.9 %all-reduce.9.cloned.1.call-start = ((), (), s32[]{:S(2)}) async-start(), calls=%async_computation.6 | async-start | bytes 3145728 | tf_op jit(solution)/shard_map/psum | solution.py:120
  73.3 1.4 copy-start.1
  88.0 3.4 %copy-start.7 = (bf16[3,3,128,128]{2,3,1,0:T(8,128)(2,1)S(1)}, bf16[3,3,128,128]{2,3,1,0:T(8,128)(2,1)}, u32[]{:S(2)}) copy-start(bf16[3,3,128,128]{2,3,1,0:T(8,128)(2,1)} %copy.37) | copy-start | bytes 884740
  222.9 3.9 %copy-start.11 = (f32[3,128,128]{2,1,0:T(8,128)S(1)}, f32[3,128,128]{2,1,0:T(8,128)}, u32[]{:S(2)}) copy-start(f32[3,128,128]{2,1,0:T(8,128)} %get-tuple-element.8) | copy-start | bytes 589828
  222.9 4.6 %copy-start.10 = (f32[3,128,128]{2,1,0:T(8,128)S(1)}, f32[3,128,128]{2,1,0:T(8,128)}, u32[]{:S(2)}) copy-start(f32[3,128,128]{2,1,0:T(8,128)} %get-tuple-element.6) | copy-start | bytes 589828
Sparse Core Ops, SparseCore 0:
  89.2 133.5 all-reduce.8
where the time goes:
time: 237 us; the launch traced here: 235 us
  waiting for transfers between devices  139 us (59%)
  starting transfers between devices  31.5 us (13%)
  local copies, waits for them, and re-layouts  21.6 us (9%)
  between operations  14.5 us (6%)
  matrix products  11.4 us (5%)
  other arithmetic  10.2 us (4%)
  blocking collectives  6.41 us (3%)
    psum x1, waiting for transfers between devices, on_device(): lax.psum((gs_one, gt_one, gs_two, gt_two), ('section', 'video', 'dp'))  128 us
    unnamed x62, local copies, waits for them, and re-layouts  12.4 us
    ppermute x2, starting transfers between devices, with_halo(): lax.ppermute(lax.slice_in_dim(block, block.shape[dim] - width, None, axis...  8.98 us
    all_to_all x2, starting transfers between devices, temporal_back(): lax.all_to_all(act, 'video', split_axis=2, concat_axis=1, tiled=True)  7.55 us
    all_to_all x2, starting transfers between devices, temporal_back(): lax.all_to_all(grad_out, 'video', split_axis=2, concat_axis=1, tiled=True)  7.03 us
    all_to_all x1, blocking collectives, temporal_back(): lax.all_to_all(band_ga, 'video', split_axis=1, concat_axis=2, tiled=True)  6.41 us
    reshape x2, local copies, waits for them, and re-layouts, patches(): return jnp.concatenate(views, axis=-1).reshape(rows * cols, 9 * width)  5.67 us
  transfers between devices with their start and end apart: 10, of which 5 were waited for; matrix products, arithmetic and copies ran while one was open for 11% of the time, Pallas kernels for 0%

commit v1 on v0

v1 whole, which is shorter than its diff:
```python
import functools
import math

import jax
import jax.numpy as jnp
from jax import lax
from jax.experimental import pallas as pl
from jax.experimental.pallas import tpu as pltpu
from jax.sharding import PartitionSpec as P

AXES = ("section", "video", "dp")
VMEM_LIMIT = 24 * 1024 * 1024


def sigmoid(value):
    return 1.0 / (1.0 + jnp.exp(-value))


def from_ahead(block, band_step, frame_step):
    bands, frames = lax.axis_size("section"), lax.axis_size("video")
    pairs = [
        ((band + band_step) * frames + frame + frame_step, band * frames + frame)
        for band in range(bands)
        for frame in range(frames)
        if 0 <= band + band_step < bands and frame + frame_step < frames
    ]
    return lax.ppermute(block, ("section", "video"), pairs)


def beside(gpre, views_ref, start):
    count, cols, ch = gpre.shape
    at = lax.broadcasted_iota(jnp.int32, gpre.shape, 1)
    right = jnp.where(at == cols - 1, 0.0, pltpu.roll(gpre, cols - 1, 1))
    left = jnp.where(at == 0, 0.0, pltpu.roll(gpre, 1, 1))
    here = pl.ds(start, count)
    views_ref[here, :, 0:ch] = right.astype(jnp.bfloat16)
    views_ref[here, :, ch : 2 * ch] = gpre.astype(jnp.bfloat16)
    views_ref[here, :, 2 * ch : 3 * ch] = left.astype(jnp.bfloat16)


def pre_gradient(grads, preact, temporal_ref):
    count, cols, ch = preact.shape
    flat = jnp.concatenate([grad.reshape(count * cols, ch) for grad in grads], axis=1)
    kernel = jnp.concatenate([temporal_ref[2 - step] for step in range(len(grads))], axis=1)
    gact = lax.dot_general(
        flat, kernel, (((1,), (1,)), ((), ())), preferred_element_type=jnp.float32
    )
    gact = gact.astype(jnp.bfloat16).astype(jnp.float32).reshape(preact.shape)
    hval = preact.astype(jnp.float32)
    sig = sigmoid(hval)
    return gact * sig * (1.0 + hval * (1.0 - sig))


def convolved(views_ref, spatial_ref, base, start, count, first):
    cols, width = views_ref.shape[1], views_ref.shape[2]
    total = first
    for ky in range(3):
        view = views_ref[pl.ds(start + base - ky, count)].reshape(count * cols, width)
        kernel = jnp.concatenate([spatial_ref[ky, kx] for kx in range(3)], axis=1)
        total = total + lax.dot_general(
            view, kernel, (((1,), (1,)), ((), ())), preferred_element_type=jnp.float32
        )
    return total


def spatial_sums(saved_t, views_ref, base, rows, out_ref):
    cols, width = views_ref.shape[1], views_ref.shape[2]
    ch = width // 3
    for ky in range(3):
        view = views_ref[base - ky : base - ky + rows].reshape(rows * cols, width)
        sums = jnp.dot(saved_t, view, preferred_element_type=jnp.float32).astype(jnp.bfloat16)
        for kx in range(3):
            out_ref[pl.ds((3 * ky + kx) * ch, ch), :] = sums[:, kx * ch : (kx + 1) * ch]


def temporal_sums(act_t, grads, out_ref):
    pixels, ch = grads[0].shape
    sums = jnp.dot(
        act_t, jnp.concatenate(grads, axis=1), preferred_element_type=jnp.float32
    ).astype(jnp.bfloat16)
    for k in range(3):
        step = 2 - k
        here = pl.ds((9 + k) * ch, ch)
        if step < len(grads):
            out_ref[here, :] = sums[:, step * ch : (step + 1) * ch]
        else:
            out_ref[here, :] = jnp.zeros((ch, ch), jnp.bfloat16)


def mid_kernel(later, *refs):
    grad_ref, preact_ref, low_ref, high_ref = refs[:4]
    later_refs = refs[4 : 4 + 3 * later]
    temporal_ref, spatial_ref, mid_ref, gpre_ref, views_ref = refs[4 + 3 * later :]
    rows, cols, ch = grad_ref.shape

    def part(first, preact, grads):
        gpre = pre_gradient(grads, preact, temporal_ref)
        gpre_ref[pl.ds(first, preact.shape[0])] = gpre.astype(jnp.bfloat16)
        beside(gpre, views_ref, first)

    part(0, low_ref[2:4], [low_ref[0:2]] + [later_refs[3 * n + 1][...] for n in range(later)])
    part(
        rows + 2,
        high_ref[2:4],
        [high_ref[0:2]] + [later_refs[3 * n + 2][...] for n in range(later)],
    )

    step = 4

    @pl.loop(0, rows // step)
    def _(n):
        here = pl.ds(n * step, step)
        part(
            n * step + 2,
            preact_ref[here],
            [grad_ref[here]] + [later_refs[3 * m][here] for m in range(later)],
        )

    def mid(first, start, count):
        total = convolved(
            views_ref,
            spatial_ref,
            2,
            start,
            count,
            first.astype(jnp.float32).reshape(count * cols, ch),
        )
        mid_ref[pl.ds(start, count)] = total.astype(jnp.bfloat16).reshape(count, cols, ch)

    mid(low_ref[1:2], 0, 1)
    mid(high_ref[0:1], rows + 1, 1)

    @pl.loop(0, rows // step)
    def _(n):
        mid(grad_ref[pl.ds(n * step, step)], n * step + 1, step)


def sums_kernel(later, *refs):
    saved_ref, preact_ref, gpre_ref, grad_ref = refs[:4]
    later_refs = refs[4 : 4 + later]
    out_ref, views_ref, act_ref = refs[4 + later :]
    rows, cols, ch = saved_ref.shape
    step = 4

    @pl.loop(0, gpre_ref.shape[0] // step)
    def _(n):
        beside(gpre_ref[pl.ds(n * step, step)].astype(jnp.float32), views_ref, n * step)

    @pl.loop(0, rows // step)
    def _(n):
        here = pl.ds(n * step, step)
        hval = preact_ref[here].astype(jnp.float32)
        act_ref[here] = (hval * sigmoid(hval)).astype(jnp.bfloat16)

    flat = (rows * cols, ch)
    spatial_sums(saved_ref[...].reshape(flat).T, views_ref, 3, rows, out_ref)
    grads = [grad_ref[...].reshape(flat)] + [ref[...].reshape(flat) for ref in later_refs]
    temporal_sums(act_ref[...].reshape(flat).T, grads, out_ref)


def first_kernel(later, bands, *refs):
    saved_ref, preact_ref, low_ref, high_ref, mid_ref = refs[:5]
    later_refs = refs[5 : 5 + later]
    temporal_ref, gpre_ref, out_ref, views_ref, act_ref = refs[5 + later :]
    rows, cols, ch = saved_ref.shape
    band = lax.axis_index("section")
    mids = [mid_ref] + list(later_refs)

    def part(first, preact, inside):
        here = pl.ds(first, preact.shape[0])
        gpre = pre_gradient([ref[here] for ref in mids], preact, temporal_ref)
        if inside is not None:
            gpre = jnp.where(inside, gpre, 0.0)
        gpre_ref[here] = gpre.astype(jnp.bfloat16)
        beside(gpre, views_ref, first)

    part(0, low_ref[4:5], band > 0)
    part(rows + 1, high_ref[4:5], band < bands - 1)
    step = 4

    @pl.loop(0, rows // step)
    def _(n):
        here = pl.ds(n * step, step)
        part(n * step + 1, preact_ref[here], None)
        hval = preact_ref[here].astype(jnp.float32)
        act_ref[here] = (hval * sigmoid(hval)).astype(jnp.bfloat16)

    flat = (rows * cols, ch)
    spatial_sums(saved_ref[...].reshape(flat).T, views_ref, 2, rows, out_ref)
    grads = [ref[1 : rows + 1].reshape(flat) for ref in mids]
    temporal_sums(act_ref[...].reshape(flat).T, grads, out_ref)


def input_kernel(mid_ref, gpre_ref, spatial_ref, out_ref, views_ref):
    rows, cols, ch = out_ref.shape
    step = 6 if gpre_ref.shape[0] % 6 == 0 else 1

    @pl.loop(0, gpre_ref.shape[0] // step)
    def _(n):
        beside(gpre_ref[pl.ds(n * step, step)].astype(jnp.float32), views_ref, n * step)

    step = 4

    @pl.loop(0, rows // step)
    def _(n):
        first = mid_ref[pl.ds(n * step + 1, step)].astype(jnp.float32)
        total = convolved(
            views_ref, spatial_ref, 2, n * step, step, first.reshape(step * cols, ch)
        )
        out_ref[pl.ds(n * step, step)] = total.astype(jnp.bfloat16).reshape(step, cols, ch)


def total_kernel(factor, parts_ref, out_ref):
    total = parts_ref[0].astype(jnp.float32)
    for n in range(1, parts_ref.shape[0]):
        total = total + parts_ref[n].astype(jnp.float32)
    total = (total * factor).astype(jnp.bfloat16)
    for n in range(out_ref.shape[0]):
        out_ref[n] = total


def call(kernel, outs, scratch, flops, *operands):
    single = len(outs) == 1
    moved = sum(math.prod(x.shape) * x.dtype.itemsize for x in (*operands, *outs))
    return pl.pallas_call(
        kernel,
        out_shape=outs[0] if single else tuple(outs),
        in_specs=[pl.BlockSpec(memory_space=pltpu.VMEM)] * len(operands),
        out_specs=pl.BlockSpec(memory_space=pltpu.VMEM)
        if single
        else tuple(pl.BlockSpec(memory_space=pltpu.VMEM) for _ in outs),
        scratch_shapes=scratch,
        compiler_params=pltpu.CompilerParams(vmem_limit_bytes=VMEM_LIMIT),
        cost_estimate=pl.CostEstimate(
            flops=int(flops), bytes_accessed=int(moved), transcendentals=0
        ),
    )(*operands)


def bf16(*shape):
    return jax.ShapeDtypeStruct(shape, jnp.bfloat16)


def summed(parts, factor):
    height, width = parts.shape
    axes, count = [], 1
    for axis in AXES:
        if height % (16 * count * lax.axis_size(axis)) == 0:
            axes.append(axis)
            count *= lax.axis_size(axis)
    rest = tuple(axis for axis in AXES if axis not in axes)
    axes = tuple(axes)
    mine = lax.all_to_all(parts, axes, split_axis=0, concat_axis=0, tiled=True)
    mine = mine.reshape(count, height // count, width)
    if rest:
        total = lax.psum(jnp.sum(mine.astype(jnp.float32), axis=0), rest)
        total = (total * factor).astype(jnp.bfloat16)
        return lax.all_gather(total, axes, axis=0, tiled=True)
    spread = call(
        functools.partial(total_kernel, factor), [bf16(*mine.shape)], [], parts.size, mine
    )
    spread = spread.reshape(height, width)
    return lax.all_to_all(spread, axes, split_axis=0, concat_axis=0, tiled=True)


def on_device(
    grad_latent,
    input_one,
    preact_one,
    input_two,
    preact_two,
    spatial_one,
    temporal_one,
    spatial_two,
    temporal_two,
):
    shape = grad_latent.shape
    rows, cols, ch = shape[2:]
    bands, frames = lax.axis_size("section"), lax.axis_size("video")
    later = min(2, frames - 1)
    pixels = lax.axis_size("dp") * frames * bands * rows * cols
    factor = 1.0 / math.sqrt(pixels)
    grad, saved_one, pre_one, saved_two, pre_two = (
        x.reshape(rows, cols, ch)
        for x in (grad_latent, input_one, preact_one, input_two, preact_two)
    )

    tail, head = grad[rows - 2 :], grad[:2]
    ahead = [[from_ahead(grad, 0, n + 1)] for n in range(later)]
    low = from_ahead(jnp.concatenate([tail, pre_two[rows - 2 :], pre_one[rows - 1 :]]), -1, 0)
    high = from_ahead(jnp.concatenate([head, pre_two[:2], pre_one[:1]]), 1, 0)
    for n in range(later):
        ahead[n].append(from_ahead(tail, -1, n + 1))
        ahead[n].append(from_ahead(head, 1, n + 1))

    area = rows * cols
    conv = 2 * area * 9 * ch * ch
    mid, gpre_two = call(
        functools.partial(mid_kernel, later),
        [bf16(rows + 2, cols, ch), bf16(rows + 4, cols, ch)],
        [pltpu.VMEM((rows + 4, cols, 3 * ch), jnp.bfloat16)],
        2 * conv,
        grad,
        pre_two,
        low,
        high,
        *[x for group in ahead for x in group],
        temporal_two,
        spatial_two,
    )
    mids = [from_ahead(mid, 0, n + 1) for n in range(later)]
    parts_two = call(
        functools.partial(sums_kernel, later),
        [bf16(12 * ch, ch)],
        [
            pltpu.VMEM((rows + 4, cols, 3 * ch), jnp.bfloat16),
            pltpu.VMEM((rows, cols, ch), jnp.bfloat16),
        ],
        2 * conv,
        saved_two,
        pre_two,
        gpre_two,
        grad,
        *[group[0] for group in ahead],
    )
    sums_two = summed(parts_two, factor)
    gpre_one, parts_one = call(
        functools.partial(first_kernel, later, bands),
        [bf16(rows + 2, cols, ch), bf16(12 * ch, ch)],
        [
            pltpu.VMEM((rows + 2, cols, 3 * ch), jnp.bfloat16),
            pltpu.VMEM((rows, cols, ch), jnp.bfloat16),
        ],
        3 * conv,
        saved_one,
        pre_one,
        low,
        high,
        mid,
        *mids,
        temporal_one,
    )
    sums_one = summed(parts_one, factor)
    grad_in = call(
        input_kernel,
        [bf16(rows, cols, ch)],
        [pltpu.VMEM((rows + 2, cols, 3 * ch), jnp.bfloat16)],
        2 * conv,
        mid,
        gpre_one,
        spatial_one,
    )

    def split(sums):
        sums = sums.astype(jnp.float32).reshape(12, ch, ch)
        return sums[:9].reshape(3, 3, ch, ch), sums[9:]

    gs_one, gt_one = split(sums_one)
    gs_two, gt_two = split(sums_two)
    return (grad_in.reshape(shape), gs_one, gt_one, gs_two, gt_two)


def solution(mesh):
    whole = P("dp", "video", "section", None, None)
    return jax.shard_map(
        on_device,
        mesh=mesh,
        in_specs=(whole,) * 5 + (P(),) * 4,
        out_specs=(whole, P(), P(), P(), P()),
        check_vma=False,
    )
```

time: 237 us -> 96.5 us (0.41)
  waiting for transfers between devices: 139 us -> 51.4 us
  local copies, waits for them, and re-layouts: 21.6 us -> 6.47 us
  between operations: 14.5 us -> 0.81 us
  matrix products: 11.4 us -> 0 us
  Pallas kernels: 0 us -> 11 us
  other arithmetic: 10.2 us -> 0.03 us
  blocking collectives: 6.41 us -> 0 us
  starting transfers between devices: 31.5 us -> 25.8 us
    psum x1 -> x0, waiting for transfers between devices: 128 us -> none  [on_device(): lax.psum((gs_one, gt_one, gs_two, gt_two), ('section', 'video', 'dp'))]
    all_to_all x5 -> x4, waiting for transfers between devices: 7.96 us -> 34.4 us  [the longest x2 22 us: summed(): return lax.all_to_all(spread, axes, split_axis=0, concat_axis=0, tiled=True)]
    ppermute x4 -> x6, waiting for transfers between devices: 3.08 us -> 17 us  [from_ahead(): return lax.ppermute(block, ('section', 'video'), pairs)]
    unnamed x62 -> x18, local copies, waits for them, and re-layouts: 12.4 us -> 0.99 us
    dot_general x8 -> x0, matrix products: 11.4 us -> none  [the longest x2 4.64 us: spatial_back(): jnp.dot(grad_cols, flipped, preferred_element_type=jnp.float32)]
    pallas_call x0 -> x6, Pallas kernels: none -> 11 us  [call(): pl.pallas_call(kernel, out_shape=outs[0] if single else tuple(outs), in_s...]
    all_to_all x1 -> x0, blocking collectives: 6.41 us -> none  [temporal_back(): lax.all_to_all(band_ga, 'video', split_axis=1, concat_axis=2, tiled=True)]
    reshape x2 -> x0, local copies, waits for them, and re-layouts: 5.67 us -> none  [patches(): return jnp.concatenate(views, axis=-1).reshape(rows * cols, 9 * width)]
  transfers between devices with their start and end apart: 10 -> 10, of which waited for: 5 -> 6; matrix products, arithmetic and copies ran while one was open for 11% -> 4% of each run, Pallas kernels for 0% -> 7%
where the time goes in v1:
time: 96.5 us; the launch traced here: 95.6 us
  waiting for transfers between devices  51.4 us (53%)
  starting transfers between devices  25.8 us (27%)
  Pallas kernels  11 us (11%)
  local copies, waits for them, and re-layouts  6.47 us (7%)
    all_to_all x2, waiting for transfers between devices, summed(): return lax.all_to_all(spread, axes, split_axis=0, concat_axis=0, tiled=True)  22 us
    ppermute x6, waiting for transfers between devices, from_ahead(): return lax.ppermute(block, ('section', 'video'), pairs)  17 us
    all_to_all x2, waiting for transfers between devices, summed(): mine = lax.all_to_all(parts, axes, split_axis=0, concat_axis=0, tiled=True)  12.4 us
    ppermute x6, starting transfers between devices, from_ahead(): return lax.ppermute(block, ('section', 'video'), pairs)  11.6 us
    pallas_call x6, Pallas kernels, call(): pl.pallas_call(kernel, out_shape=outs[0] if single else tuple(outs), in_s...  11 us
    all_to_all x2, starting transfers between devices, summed(): mine = lax.all_to_all(parts, axes, split_axis=0, concat_axis=0, tiled=True)  9.31 us
    all_to_all x2, starting transfers between devices, summed(): return lax.all_to_all(spread, axes, split_axis=0, concat_axis=0, tiled=True)  4.88 us
    slice x4, local copies, waits for them, and re-layouts, split(): return (sums[:9].reshape(3, 3, ch, ch), sums[9:])  3.09 us
  transfers between devices with their start and end apart: 10, of which 6 were waited for; matrix products, arithmetic and copies ran while one was open for 4% of the time, Pallas kernels for 7%

profile of v1, /device:TPU:1, one launch (start us, length us, event | category | flops | bytes accessed | tf_op | source)
XLA Modules:
  0.0 95.6 jit_solution(13348428442449807813)
XLA Ops:
  0.6 1.3 %collective-permute-start.2 = (bf16[16,64,128]{2,1,0:T(8,128)(2,1)}, bf16[16,64,128]{2,1,0:T(8,128)(2,1)S(1)}, u32[]{:S(2)}, u32[]{:S(2)}) collective-permute-start(bf16[16,64,128]{2,1,0:T(8,128)(2,1)} %bitcast.24), channel_id=1, source_target_pairs={{4,0},{12,8},{20,16},{28,24},{5,1},{13,9},{21,17},{29,25},{6,2},{1... | collective-permute-start | bytes 786440 | tf_op jit(solution)/shard_map/ppermute | solution.py:27
  1.9 0.8 slice_bitcast_fusion.1
  2.8 0.8 slice_bitcast_fusion
  3.6 0.7 slice_bitcast_fusion.4
  4.4 4.5 %collective-permute-start = (bf16[5,64,128]{2,1,0:T(8,128)(2,1)S(1)}, bf16[5,64,128]{2,1,0:T(8,128)(2,1)S(1)}, u32[]{:S(2)}, u32[]{:S(2)}) collective-permute-start(bf16[5,64,128]{2,1,0:T(8,128)(2,1)S(1)} %pad_maximum_fusion), channel_id=1, source_target_pairs={{0,8},{4,12},{8,16},{12,20},{16,24},{20,28},{1,9},{5,13},{9,17},{1... | collective-permute-start | bytes 245768 | tf_op jit(solution)/shard_map/ppermute | solution.py:27
  8.9 1.9 %collective-permute-start.1 = (bf16[5,64,128]{2,1,0:T(8,128)(2,1)S(1)}, bf16[5,64,128]{2,1,0:T(8,128)(2,1)S(1)}, u32[]{:S(2)}, u32[]{:S(2)}) collective-permute-start(bf16[5,64,128]{2,1,0:T(8,128)(2,1)S(1)} %pad_maximum_fusion.1), channel_id=1, source_target_pairs={{8,0},{12,4},{16,8},{20,12},{24,16},{28,20},{9,1},{13,5},{17,9},{2... | collective-permute-start | bytes 245768 | tf_op jit(solution)/shard_map/ppermute | solution.py:27
  10.9 1.3 %collective-permute-start.3 = (bf16[2,64,128]{2,1,0:T(8,128)(2,1)S(1)}, bf16[2,64,128]{2,1,0:T(8,128)(2,1)S(1)}, u32[]{:S(2)}, u32[]{:S(2)}) collective-permute-start(bf16[2,64,128]{2,1,0:T(8,128)(2,1)S(1)} %get-tuple-element.14), channel_id=1, source_target_pairs={{4,8},{12,16},{20,24},{5,9},{13,17},{21,25},{6,10},{14,18},{22,26}... | collective-permute-start | bytes 98312 | tf_op jit(solution)/shard_map/ppermute | solution.py:27
  12.2 1.3 %collective-permute-start.4 = (bf16[2,64,128]{2,1,0:T(8,128)(2,1)S(1)}, bf16[2,64,128]{2,1,0:T(8,128)(2,1)S(1)}, u32[]{:S(2)}, u32[]{:S(2)}) collective-permute-start(bf16[2,64,128]{2,1,0:T(8,128)(2,1)S(1)} %get-tuple-element.13), channel_id=1, source_target_pairs={{12,0},{20,8},{28,16},{13,1},{21,9},{29,17},{14,2},{22,10},{30,18}... | collective-permute-start | bytes 98312 | tf_op jit(solution)/shard_map/ppermute | solution.py:27
  13.5 2.6 %collective-permute-done.3.refs_5_ = bf16[2,64,128]{2,1,0:T(8,128)(2,1)S(1)} collective-permute-done((bf16[2,64,128]{2,1,0:T(8,128)(2,1)S(1)}, bf16[2,64,128]{2,1,0:T(8,128)(2,1)S(1)}, u32[]{:S(2)}, u32[]{:S(2)}) %collective-permute-start.3) | collective-permute-done | bytes 32800 | tf_op jit(solution)/shard_map/ppermute | solution.py:27
  16.1 2.8 %collective-permute-done.4.refs_6_ = bf16[2,64,128]{2,1,0:T(8,128)(2,1)S(1)} collective-permute-done((bf16[2,64,128]{2,1,0:T(8,128)(2,1)S(1)}, bf16[2,64,128]{2,1,0:T(8,128)(2,1)S(1)}, u32[]{:S(2)}, u32[]{:S(2)}) %collective-permute-start.4) | collective-permute-done | bytes 32800 | tf_op jit(solution)/shard_map/ppermute | solution.py:27
  18.9 0.0 collective-permute-done.refs_2_
  18.9 0.0 copy-start.3
  18.9 1.0 copy-done.3
  19.9 2.8 %shard_map.128 = (bf16[18,64,128]{2,1,0:T(8,128)(2,1)S(1)}, bf16[20,64,128]{2,1,0:T(8,128)(2,1)S(1)}) custom-call(bf16[16,64,128]{2,1,0:T(8,128)(2,1)S(1)} %bitcast.25, bf16[16,64,128]{2,1,0:T(8,128)(2,1)S(1)} %bitcast.27, bf16[5,64,128]{2,1,0:T(8,128)(2,1)S(1)} %collective-permute-done.refs_2_, bf16[5,64,128]{2,1,0:T(8,128)(2,1)S(1)} %collective-permute-done.1.refs_3_, ...), custom_call_target="tpu_custom_call" | custom-call | flops 603979776 | bytes 2031616 | tf_op jit(solution)/shard_map/pallas_call | solution.py:225
  22.7 1.8 %shard_map.132 = bf16[1536,128]{1,0:T(8,128)(2,1)} custom-call(bf16[16,64,128]{2,1,0:T(8,128)(2,1)S(1)} %bitcast.30, bf16[16,64,128]{2,1,0:T(8,128)(2,1)S(1)} %bitcast.28, bf16[20,64,128]{2,1,0:T(8,128)(2,1)S(1)} %get-tuple-element.12.refs_2_, bf16[16,64,128]{2,1,0:T(8,128)(2,1)S(1)} %bitcast.26, bf16[16,64,128]{2,1,0:T(8,128)(2,1)S(1)} %collective-permute-done.2.refs_4_), custom_call_target="tpu_custom_call" | custom-call | flops 603979776 | bytes 1769472 | tf_op jit(solution)/shard_map/pallas_call | solution.py:225
  24.5 3.8 %all-to-all-start.2 = ((bf16[32,48,128]{2,1,0:T(8,128)(2,1)}), bf16[32,48,128]{2,1,0:T(8,128)(2,1)S(1)}, u32[]{:S(2)}, u32[]{:S(2)}) async-start(bf16[32,48,128]{2,1,0:T(8,128)(2,1)} %bitcast.15), calls=%async_computation.2 | async-start | bytes 786432 | tf_op jit(solution)/shard_map/all_to_all | solution.py:253
  28.4 1.3 %collective-permute-start.5 = (bf16[18,64,128]{2,1,0:T(8,128)(2,1)S(1)}, bf16[18,64,128]{2,1,0:T(8,128)(2,1)S(1)}, u32[]{:S(2)}, u32[]{:S(2)}) collective-permute-start(bf16[18,64,128]{2,1,0:T(8,128)(2,1)S(1)} %get-tuple-element.9.refs_4_.mid_ref), channel_id=1, source_target_pairs={{4,0},{12,8},{20,16},{28,24},{5,1},{13,9},{21,17},{29,25},{6,2},{1... | collective-permute-start | bytes 884744 | tf_op jit(solution)/shard_map/ppermute | solution.py:27
  29.7 11.6 %collective-permute-done.5.refs_5_ = bf16[18,64,128]{2,1,0:T(8,128)(2,1)S(1)} collective-permute-done((bf16[18,64,128]{2,1,0:T(8,128)(2,1)S(1)}, bf16[18,64,128]{2,1,0:T(8,128)(2,1)S(1)}, u32[]{:S(2)}, u32[]{:S(2)}) %collective-permute-start.5) | collective-permute-done | bytes 294944 | tf_op jit(solution)/shard_map/ppermute | solution.py:27
  41.3 2.5 %shard_map.129 = (bf16[18,64,128]{2,1,0:T(8,128)(2,1)S(1)}, bf16[1536,128]{1,0:T(8,128)(2,1)}) custom-call(bf16[16,64,128]{2,1,0:T(8,128)(2,1)S(1)} %bitcast.31, bf16[16,64,128]{2,1,0:T(8,128)(2,1)S(1)} %bitcast.29, bf16[5,64,128]{2,1,0:T(8,128)(2,1)S(1)} %collective-permute-done.refs_2_, bf16[5,64,128]{2,1,0:T(8,128)(2,1)S(1)} %collective-permute-done.1.refs_3_, ...), custom_call_target="tpu_custom_call" | custom-call | flops 905969664 | bytes 2064384 | tf_op jit(solution)/shard_map/pallas_call | solution.py:225
  43.8 5.5 %all-to-all-start = ((bf16[32,48,128]{2,1,0:T(8,128)(2,1)}), bf16[32,48,128]{2,1,0:T(8,128)(2,1)S(1)}, u32[]{:S(2)}, u32[]{:S(2)}) async-start(bf16[32,48,128]{2,1,0:T(8,128)(2,1)} %bitcast.11), calls=%async_computation | async-start | bytes 786432 | tf_op jit(solution)/shard_map/all_to_all | solution.py:253
  49.3 0.8 shard_map.133
  50.1 12.4 %all-to-all-done.parts_ref = bf16[32,48,128]{2,1,0:T(8,128)(2,1)S(1)} async-done(((bf16[32,48,128]{2,1,0:T(8,128)(2,1)}), bf16[32,48,128]{2,1,0:T(8,128)(2,1)S(1)}, u32[]{:S(2)}, u32[]{:S(2)}) %all-to-all-start) | async-done | bytes 393248 | tf_op jit(solution)/shard_map/all_to_all | solution.py:253
  62.5 2.4 %all-to-all-start.3 = ((bf16[32,48,128]{2,1,0:T(8,128)(2,1)}), bf16[32,48,128]{2,1,0:T(8,128)(2,1)S(1)}, u32[]{:S(2)}, u32[]{:S(2)}) async-start(bf16[32,48,128]{2,1,0:T(8,128)(2,1)} %shard_map.133), calls=%async_computation.3 | async-start | bytes 786432 | tf_op jit(solution)/shard_map/all_to_all | solution.py:263
  64.9 0.8 shard_map.131
  65.7 12.5 %all-to-all-done.3 = bf16[32,48,128]{2,1,0:T(8,128)(2,1)S(1)} async-done(((bf16[32,48,128]{2,1,0:T(8,128)(2,1)}), bf16[32,48,128]{2,1,0:T(8,128)(2,1)S(1)}, u32[]{:S(2)}, u32[]{:S(2)}) %all-to-all-start.3) | async-done | bytes 393248 | tf_op jit(solution)/shard_map/all_to_all | solution.py:263
  78.3 2.4 %all-to-all-start.1 = ((bf16[32,48,128]{2,1,0:T(8,128)(2,1)}), bf16[32,48,128]{2,1,0:T(8,128)(2,1)S(1)}, u32[]{:S(2)}, u32[]{:S(2)}) async-start(bf16[32,48,128]{2,1,0:T(8,128)(2,1)} %shard_map.131), calls=%async_computation.1 | async-start | bytes 786432 | tf_op jit(solution)/shard_map/all_to_all | solution.py:263
  80.7 2.3 %shard_map.130 = bf16[16,64,128]{2,1,0:T(8,128)(2,1)} custom-call(bf16[18,64,128]{2,1,0:T(8,128)(2,1)S(1)} %get-tuple-element.9.refs_4_.mid_ref, bf16[18,64,128]{2,1,0:T(8,128)(2,1)S(1)} %get-tuple-element.10.gpre_ref, bf16[3,3,128,128]{3,2,1,0:T(8,128)(2,1)S(1)} %copy-done.4), custom_call_target="tpu_custom_call" | custom-call | flops 603979776 | bytes 1146880 | tf_op jit(solution)/shard_map/pallas_call | solution.py:225
  83.0 0.9 slice.80
  83.8 0.7 slice.81
  84.5 9.5 %all-to-all-done.1 = bf16[32,48,128]{2,1,0:T(8,128)(2,1)S(1)} async-done(((bf16[32,48,128]{2,1,0:T(8,128)(2,1)}), bf16[32,48,128]{2,1,0:T(8,128)(2,1)S(1)}, u32[]{:S(2)}, u32[]{:S(2)}) %all-to-all-start.1) | async-done | bytes 393248 | tf_op jit(solution)/shard_map/all_to_all | solution.py:263
  94.0 0.9 slice.78
  94.9 0.7 slice.79
  (21 shorter events, 0.1 us)
Async XLA Ops:
  0.6 18.2 %collective-permute-start.2 = (bf16[16,64,128]{2,1,0:T(8,128)(2,1)}, bf16[16,64,128]{2,1,0:T(8,128)(2,1)S(1)}, u32[]{:S(2)}, u32[]{:S(2)}) collective-permute-start(bf16[16,64,128]{2,1,0:T(8,128)(2,1)} %bitcast.24), channel_id=1, source_target_pairs={{4,0},{12,8},{20,16},{28,24},{5,1},{13,9},{21,17},{29,25},{6,2},{1... | collective-permute-start | bytes 786440 | tf_op jit(solution)/shard_map/ppermute | solution.py:27
  1.9 16.9 %copy-start.7 = (bf16[3,128,128]{2,1,0:T(8,128)(2,1)S(1)}, bf16[3,128,128]{2,1,0:T(8,128)(2,1)}, u32[]{:S(2)}) copy-start(bf16[3,128,128]{2,1,0:T(8,128)(2,1)} %refs_7_.1) | copy-start | bytes 294916
  2.8 16.1 %copy-start = (bf16[1,1,16,64,128]{4,3,2,1,0:T(8,128)(2,1)S(1)}, bf16[1,1,16,64,128]{4,3,2,1,0:T(8,128)(2,1)}, u32[]{:S(2)}) copy-start(bf16[1,1,16,64,128]{4,3,2,1,0:T(8,128)(2,1)} %param.9) | copy-start | bytes 786436
  2.8 16.1 %copy-start.1 = (bf16[1,1,16,64,128]{4,3,2,1,0:T(8,128)(2,1)S(1)}, bf16[1,1,16,64,128]{4,3,2,1,0:T(8,128)(2,1)}, u32[]{:S(2)}) copy-start(bf16[1,1,16,64,128]{4,3,2,1,0:T(8,128)(2,1)} %param.13) | copy-start | bytes 786436
  4.4 14.5 %collective-permute-start = (bf16[5,64,128]{2,1,0:T(8,128)(2,1)S(1)}, bf16[5,64,128]{2,1,0:T(8,128)(2,1)S(1)}, u32[]{:S(2)}, u32[]{:S(2)}) collective-permute-start(bf16[5,64,128]{2,1,0:T(8,128)(2,1)S(1)} %pad_maximum_fusion), channel_id=1, source_target_pairs={{0,8},{4,12},{8,16},{12,20},{16,24},{20,28},{1,9},{5,13},{9,17},{1... | collective-permute-start | bytes 245768 | tf_op jit(solution)/shard_map/ppermute | solution.py:27
  8.9 9.9 %collective-permute-start.1 = (bf16[5,64,128]{2,1,0:T(8,128)(2,1)S(1)}, bf16[5,64,128]{2,1,0:T(8,128)(2,1)S(1)}, u32[]{:S(2)}, u32[]{:S(2)}) collective-permute-start(bf16[5,64,128]{2,1,0:T(8,128)(2,1)S(1)} %pad_maximum_fusion.1), channel_id=1, source_target_pairs={{8,0},{12,4},{16,8},{20,12},{24,16},{28,20},{9,1},{13,5},{17,9},{2... | collective-permute-start | bytes 245768 | tf_op jit(solution)/shard_map/ppermute | solution.py:27
  10.9 5.2 %collective-permute-start.3 = (bf16[2,64,128]{2,1,0:T(8,128)(2,1)S(1)}, bf16[2,64,128]{2,1,0:T(8,128)(2,1)S(1)}, u32[]{:S(2)}, u32[]{:S(2)}) collective-permute-start(bf16[2,64,128]{2,1,0:T(8,128)(2,1)S(1)} %get-tuple-element.14), channel_id=1, source_target_pairs={{4,8},{12,16},{20,24},{5,9},{13,17},{21,25},{6,10},{14,18},{22,26}... | collective-permute-start | bytes 98312 | tf_op jit(solution)/shard_map/ppermute | solution.py:27
  12.2 6.7 %collective-permute-start.4 = (bf16[2,64,128]{2,1,0:T(8,128)(2,1)S(1)}, bf16[2,64,128]{2,1,0:T(8,128)(2,1)S(1)}, u32[]{:S(2)}, u32[]{:S(2)}) collective-permute-start(bf16[2,64,128]{2,1,0:T(8,128)(2,1)S(1)} %get-tuple-element.13), channel_id=1, source_target_pairs={{12,0},{20,8},{28,16},{13,1},{21,9},{29,17},{14,2},{22,10},{30,18}... | collective-permute-start | bytes 98312 | tf_op jit(solution)/shard_map/ppermute | solution.py:27
  18.9 1.0 %copy-start.3 = (bf16[3,3,128,128]{3,2,1,0:T(8,128)(2,1)S(1)}, bf16[3,3,128,128]{3,2,1,0:T(8,128)(2,1)}, u32[]{:S(2)}) copy-start(bf16[3,3,128,128]{3,2,1,0:T(8,128)(2,1)} %refs_8_.1) | copy-start | bytes 884740
  19.9 2.8 %copy-start.5 = (bf16[1,1,16,64,128]{4,3,2,1,0:T(8,128)(2,1)S(1)}, bf16[1,1,16,64,128]{4,3,2,1,0:T(8,128)(2,1)}, u32[]{:S(2)}) copy-start(bf16[1,1,16,64,128]{4,3,2,1,0:T(8,128)(2,1)} %param.12) | copy-start | bytes 786436
  24.5 16.8 %copy-start.2 = (bf16[1,1,16,64,128]{4,3,2,1,0:T(8,128)(2,1)S(1)}, bf16[1,1,16,64,128]{4,3,2,1,0:T(8,128)(2,1)}, u32[]{:S(2)}) copy-start(bf16[1,1,16,64,128]{4,3,2,1,0:T(8,128)(2,1)} %param.11) | copy-start | bytes 786436
  24.5 16.8 %copy-start.6 = (bf16[1,1,16,64,128]{4,3,2,1,0:T(8,128)(2,1)S(1)}, bf16[1,1,16,64,128]{4,3,2,1,0:T(8,128)(2,1)}, u32[]{:S(2)}) copy-start(bf16[1,1,16,64,128]{4,3,2,1,0:T(8,128)(2,1)} %param.10) | copy-start | bytes 786436
  24.5 16.8 %copy-start.8 = (bf16[3,128,128]{2,1,0:T(8,128)(2,1)S(1)}, bf16[3,128,128]{2,1,0:T(8,128)(2,1)}, u32[]{:S(2)}) copy-start(bf16[3,128,128]{2,1,0:T(8,128)(2,1)} %refs_6_.1) | copy-start | bytes 294916
  24.5 19.3 %all-to-all-start.2 = ((bf16[32,48,128]{2,1,0:T(8,128)(2,1)}), bf16[32,48,128]{2,1,0:T(8,128)(2,1)S(1)}, u32[]{:S(2)}, u32[]{:S(2)}) async-start(bf16[32,48,128]{2,1,0:T(8,128)(2,1)} %bitcast.15), calls=%async_computation.2 | async-start | bytes 786432 | tf_op jit(solution)/shard_map/all_to_all | solution.py:253
  28.4 12.9 %collective-permute-start.5 = (bf16[18,64,128]{2,1,0:T(8,128)(2,1)S(1)}, bf16[18,64,128]{2,1,0:T(8,128)(2,1)S(1)}, u32[]{:S(2)}, u32[]{:S(2)}) collective-permute-start(bf16[18,64,128]{2,1,0:T(8,128)(2,1)S(1)} %get-tuple-element.9.refs_4_.mid_ref), channel_id=1, source_target_pairs={{4,0},{12,8},{20,16},{28,24},{5,1},{13,9},{21,17},{29,25},{6,2},{1... | collective-permute-start | bytes 884744 | tf_op jit(solution)/shard_map/ppermute | solution.py:27
  43.8 18.7 %all-to-all-start = ((bf16[32,48,128]{2,1,0:T(8,128)(2,1)}), bf16[32,48,128]{2,1,0:T(8,128)(2,1)S(1)}, u32[]{:S(2)}, u32[]{:S(2)}) async-start(bf16[32,48,128]{2,1,0:T(8,128)(2,1)} %bitcast.11), calls=%async_computation | async-start | bytes 786432 | tf_op jit(solution)/shard_map/all_to_all | solution.py:253
  62.5 15.8 %all-to-all-start.3 = ((bf16[32,48,128]{2,1,0:T(8,128)(2,1)}), bf16[32,48,128]{2,1,0:T(8,128)(2,1)S(1)}, u32[]{:S(2)}, u32[]{:S(2)}) async-start(bf16[32,48,128]{2,1,0:T(8,128)(2,1)} %shard_map.133), calls=%async_computation.3 | async-start | bytes 786432 | tf_op jit(solution)/shard_map/all_to_all | solution.py:263
  65.7 15.0 %copy-start.4 = (bf16[3,3,128,128]{3,2,1,0:T(8,128)(2,1)S(1)}, bf16[3,3,128,128]{3,2,1,0:T(8,128)(2,1)}, u32[]{:S(2)}) copy-start(bf16[3,3,128,128]{3,2,1,0:T(8,128)(2,1)} %spatial_ref.1) | copy-start | bytes 884740
  78.3 15.8 %all-to-all-start.1 = ((bf16[32,48,128]{2,1,0:T(8,128)(2,1)}), bf16[32,48,128]{2,1,0:T(8,128)(2,1)S(1)}, u32[]{:S(2)}, u32[]{:S(2)}) async-start(bf16[32,48,128]{2,1,0:T(8,128)(2,1)} %shard_map.131), calls=%async_computation.1 | async-start | bytes 786432 | tf_op jit(solution)/shard_map/all_to_all | solution.py:263

commit v2 on v1

--- a/solution.py
+++ b/solution.py
@@ -87,10 +87,8 @@
             out_ref[here, :] = jnp.zeros((ch, ch), jnp.bfloat16)
 
 
-def mid_kernel(later, *refs):
-    grad_ref, preact_ref, low_ref, high_ref = refs[:4]
-    later_refs = refs[4 : 4 + 3 * later]
-    temporal_ref, spatial_ref, mid_ref, gpre_ref, views_ref = refs[4 + 3 * later :]
+def middle(refs, laters, temporal_ref, spatial_ref, mid_ref, gpre_ref, views_ref):
+    grad_ref, preact_ref, low_ref, high_ref = refs
     rows, cols, ch = grad_ref.shape
 
     def part(first, preact, grads):
@@ -98,23 +96,16 @@
         gpre_ref[pl.ds(first, preact.shape[0])] = gpre.astype(jnp.bfloat16)
         beside(gpre, views_ref, first)
 
-    part(0, low_ref[2:4], [low_ref[0:2]] + [later_refs[3 * n + 1][...] for n in range(later)])
-    part(
-        rows + 2,
-        high_ref[2:4],
-        [high_ref[0:2]] + [later_refs[3 * n + 2][...] for n in range(later)],
-    )
+    part(0, low_ref[2:4], [low_ref[0:2]] + [edge[0:2] for _, edge in laters])
+    part(rows + 2, high_ref[2:4], [high_ref[0:2]] + [edge[2:4] for _, edge in laters])
 
     step = 4
 
     @pl.loop(0, rows // step)
     def _(n):
         here = pl.ds(n * step, step)
-        part(
-            n * step + 2,
-            preact_ref[here],
-            [grad_ref[here]] + [later_refs[3 * m][here] for m in range(later)],
-        )
+        grads = [grad_ref[here]] + [whole[here] for whole, _ in laters]
+        part(n * step + 2, preact_ref[here], grads)
 
     def mid(first, start, count):
         total = convolved(
@@ -135,6 +126,43 @@
         mid(grad_ref[pl.ds(n * step, step)], n * step + 1, step)
 
 
+def pack_kernel(*refs):
+    parts, (up_ref, down_ref) = refs[:6], refs[6:]
+    up_ref[0:2], up_ref[2:4], up_ref[4:5] = (part[...] for part in parts[:3])
+    down_ref[0:2], down_ref[2:4], down_ref[4:5] = (part[...] for part in parts[3:])
+
+
+def last_kernel(*refs):
+    inputs, kernels, outs = refs[:4], refs[4:6], refs[6:]
+    mid_ref, gpre_ref, edge_ref, views_ref = outs
+
+    @pl.when(lax.axis_index("video") == lax.axis_size("video") - 1)
+    def _():
+        edge_ref[0:2] = inputs[2][0:2]
+        edge_ref[2:4] = inputs[3][0:2]
+        middle(inputs, [], *kernels, mid_ref, gpre_ref, views_ref)
+
+
+def mid_kernel(later, *refs):
+    inputs, refs = refs[:4], refs[4:]
+    laters, refs = [refs[2 * n : 2 * n + 2] for n in range(later)], refs[2 * later :]
+    kernels, refs = refs[:2], refs[2:]
+    if len(refs) == 3:
+        middle(inputs, laters, *kernels, *refs)
+        return
+    known, (mid_ref, gpre_ref, views_ref) = refs[:2], refs[2:]
+    last = lax.axis_index("video") == lax.axis_size("video") - 1
+
+    @pl.when(last)
+    def _():
+        mid_ref[...] = known[0][...]
+        gpre_ref[...] = known[1][...]
+
+    @pl.when(jnp.logical_not(last))
+    def _():
+        middle(inputs, laters, *kernels, mid_ref, gpre_ref, views_ref)
+
+
 def sums_kernel(later, *refs):
     saved_ref, preact_ref, gpre_ref, grad_ref = refs[:4]
     later_refs = refs[4 : 4 + later]
@@ -210,6 +238,19 @@
         out_ref[pl.ds(n * step, step)] = total.astype(jnp.bfloat16).reshape(step, cols, ch)
 
 
+def pair_kernel(one_ref, two_ref, out_ref):
+    height = out_ref.shape[2]
+
+    @pl.loop(0, out_ref.shape[0])
+    def _(n):
+        here = pl.ds(pl.multiple_of(n * height, height), height)
+        for block, ref in enumerate((one_ref, two_ref)):
+            total = ref[0, here].astype(jnp.float32)
+            for part in range(1, ref.shape[0]):
+                total = total + ref[part, here].astype(jnp.float32)
+            out_ref[n, block] = total.astype(jnp.bfloat16)
+
+
 def total_kernel(factor, parts_ref, out_ref):
     total = parts_ref[0].astype(jnp.float32)
     for n in range(1, parts_ref.shape[0]):
@@ -219,16 +260,38 @@
         out_ref[n] = total
 
 
-def call(kernel, outs, scratch, flops, *operands):
+def place_kernel(*refs):
+    shares, outs = refs[:4], refs[4:]
+    band = lax.axis_index("section")
+    height = shares[0].shape[2]
+    for flip, share in enumerate(shares):
+        place = jnp.bitwise_xor(band, flip)
+        for block in range(2):
+            spatial_ref, temporal_ref = outs[2 * block : 2 * block + 2]
+
+            @pl.when(place < 3)
+            def _():
+                for n in range(share.shape[0]):
+                    value = share[n, block].astype(jnp.float32)
+                    spatial_ref[place, n * height : (n + 1) * height] = value
+
+            @pl.when(place == 3)
+            def _():
+                for n in range(share.shape[0]):
+                    value = share[n, block].astype(jnp.float32)
+                    temporal_ref[n * height : (n + 1) * height] = value
+
+
+def call(kernel, outs, scratch, flops, *operands, grid=(), in_specs=None):
     single = len(outs) == 1
     moved = sum(math.prod(x.shape) * x.dtype.itemsize for x in (*operands, *outs))
+    vmem = pl.BlockSpec(memory_space=pltpu.VMEM)
     return pl.pallas_call(
         kernel,
         out_shape=outs[0] if single else tuple(outs),
-        in_specs=[pl.BlockSpec(memory_space=pltpu.VMEM)] * len(operands),
-        out_specs=pl.BlockSpec(memory_space=pltpu.VMEM)
-        if single
-        else tuple(pl.BlockSpec(memory_space=pltpu.VMEM) for _ in outs),
+        grid=grid,
+        in_specs=in_specs or [vmem] * len(operands),
+        out_specs=vmem if single else (vmem,) * len(outs),
         scratch_shapes=scratch,
         compiler_params=pltpu.CompilerParams(vmem_limit_bytes=VMEM_LIMIT),
         cost_estimate=pl.CostEstimate(
@@ -241,26 +304,63 @@
     return jax.ShapeDtypeStruct(shape, jnp.bfloat16)
 
 
-def summed(parts, factor):
-    height, width = parts.shape
+def f32(*shape):
+    return jax.ShapeDtypeStruct(shape, jnp.float32)
+
+
+def split(sums, ch):
+    sums = sums.astype(jnp.float32).reshape(12, ch, ch)
+    return sums[:9].reshape(3, 3, ch, ch), sums[9:]
+
+
+def band_sums(parts):
+    bands = lax.axis_size("section")
+    height, ch = parts.shape
+    mine = lax.all_to_all(parts, "section", split_axis=0, concat_axis=0, tiled=True)
+    return mine.reshape(bands, height // bands, ch)
+
+
+def totals(one, two, factor):
+    bands, height, ch = one.shape
     axes, count = [], 1
-    for axis in AXES:
+    for axis in ("video", "dp"):
         if height % (16 * count * lax.axis_size(axis)) == 0:
             axes.append(axis)
             count *= lax.axis_size(axis)
-    rest = tuple(axis for axis in AXES if axis not in axes)
+    rest = tuple(axis for axis in ("video", "dp") if axis not in axes)
     axes = tuple(axes)
-    mine = lax.all_to_all(parts, axes, split_axis=0, concat_axis=0, tiled=True)
-    mine = mine.reshape(count, height // count, width)
+    cut = (count, 2, height // count, ch)
+
+    def exchanged(x):
+        x = x.reshape(2 * height, ch)
+        x = lax.all_to_all(x, axes, split_axis=0, concat_axis=0, tiled=True)
+        return x.reshape(cut)
+
+    mine = exchanged(call(pair_kernel, [bf16(*cut)], [], one.size, one, two))
     if rest:
         total = lax.psum(jnp.sum(mine.astype(jnp.float32), axis=0), rest)
         total = (total * factor).astype(jnp.bfloat16)
-        return lax.all_gather(total, axes, axis=0, tiled=True)
-    spread = call(
-        functools.partial(total_kernel, factor), [bf16(*mine.shape)], [], parts.size, mine
-    )
-    spread = spread.reshape(height, width)
-    return lax.all_to_all(spread, axes, split_axis=0, concat_axis=0, tiled=True)
+        spread = jnp.broadcast_to(total, cut)
+    else:
+        spread = call(functools.partial(total_kernel, factor), [bf16(*cut)], [], one.size, mine)
+    share = exchanged(spread)
+
+    def flipped(x, flip):
+        pairs = [(band ^ flip, band) for band in range(bands)]
+        return lax.ppermute(x, "section", pairs)
+
+    across = flipped(share, 2)
+    outs = call(
+        place_kernel,
+        [f32(3, height, ch), f32(height, ch)] * 2,
+        [],
+        share.size,
+        share,
+        flipped(share, 1),
+        across,
+        flipped(across, 1),
+    )
+    return [x.reshape(3, 3, ch, ch) if x.ndim == 3 else x.reshape(3, ch, ch) for x in outs]
 
 
 def on_device(
@@ -284,53 +384,75 @@
         x.reshape(rows, cols, ch)
         for x in (grad_latent, input_one, preact_one, input_two, preact_two)
     )
-
-    tail, head = grad[rows - 2 :], grad[:2]
-    ahead = [[from_ahead(grad, 0, n + 1)] for n in range(later)]
-    low = from_ahead(jnp.concatenate([tail, pre_two[rows - 2 :], pre_one[rows - 1 :]]), -1, 0)
-    high = from_ahead(jnp.concatenate([head, pre_two[:2], pre_one[:1]]), 1, 0)
-    for n in range(later):
-        ahead[n].append(from_ahead(tail, -1, n + 1))
-        ahead[n].append(from_ahead(head, 1, n + 1))
-
     area = rows * cols
     conv = 2 * area * 9 * ch * ch
+    views_four = pltpu.VMEM((rows + 4, cols, 3 * ch), jnp.bfloat16)
+    views_two = pltpu.VMEM((rows + 2, cols, 3 * ch), jnp.bfloat16)
+    acts = pltpu.VMEM((rows, cols, ch), jnp.bfloat16)
+
+    wholes = [from_ahead(grad, 0, n + 1) for n in range(later)]
+
+    def edge_spec(count, last):
+        return pl.BlockSpec((count, cols, ch), lambda _: (rows // count - 1 if last else 0, 0, 0))
+
+    counts = (2, 2, 1)
+    up, down = call(
+        pack_kernel,
+        [bf16(5, cols, ch)] * 2,
+        [],
+        1,
+        *(grad, pre_two, pre_one) * 2,
+        grid=(1,),
+        in_specs=[edge_spec(n, False) for n in counts] + [edge_spec(n, True) for n in counts],
+    )
+    low = from_ahead(down, -1, 0)
+    high = from_ahead(up, 1, 0)
+    inputs = (grad, pre_two, low, high)
+    kernels = (temporal_two, spatial_two)
+    field = [bf16(rows + 2, cols, ch), bf16(rows + 4, cols, ch)]
+    known = ()
+    if frames == 2:
+        *known, edge = call(
+            last_kernel,
+            field + [bf16(4, cols, ch)],
+            [views_four],
+            2 * conv,
+            *inputs,
+            *kernels,
+        )
+    else:
+        edge = jnp.concatenate([low[:2], high[:2]])
+    edges = [from_ahead(edge, 0, n + 1) for n in range(later)]
+    mids = [from_ahead(known[0], 0, 1)] if known else None
+    laters = [x for pair in zip(wholes, edges) for x in pair]
     mid, gpre_two = call(
         functools.partial(mid_kernel, later),
-        [bf16(rows + 2, cols, ch), bf16(rows + 4, cols, ch)],
-        [pltpu.VMEM((rows + 4, cols, 3 * ch), jnp.bfloat16)],
+        field,
+        [views_four],
         2 * conv,
-        grad,
-        pre_two,
-        low,
-        high,
-        *[x for group in ahead for x in group],
-        temporal_two,
-        spatial_two,
-    )
-    mids = [from_ahead(mid, 0, n + 1) for n in range(later)]
+        *inputs,
+        *laters,
+        *kernels,
+        *known,
+    )
+    if mids is None:
+        mids = [from_ahead(mid, 0, n + 1) for n in range(later)]
     parts_two = call(
         functools.partial(sums_kernel, later),
         [bf16(12 * ch, ch)],
-        [
-            pltpu.VMEM((rows + 4, cols, 3 * ch), jnp.bfloat16),
-            pltpu.VMEM((rows, cols, ch), jnp.bfloat16),
-        ],
+        [views_four, acts],
         2 * conv,
         saved_two,
         pre_two,
         gpre_two,
         grad,
-        *[group[0] for group in ahead],
-    )
-    sums_two = summed(parts_two, factor)
+        *wholes,
+    )
+    shares_two = band_sums(parts_two) if bands == 4 else None
     gpre_one, parts_one = call(
         functools.partial(first_kernel, later, bands),
         [bf16(rows + 2, cols, ch), bf16(12 * ch, ch)],
-        [
-            pltpu.VMEM((rows + 2, cols, 3 * ch), jnp.bfloat16),
-            pltpu.VMEM((rows, cols, ch), jnp.bfloat16),
-        ],
+        [views_two, acts],
         3 * conv,
         saved_one,
         pre_one,
@@ -340,24 +462,21 @@
         *mids,
         temporal_one,
     )
-    sums_one = summed(parts_one, factor)
+    if bands == 4:
+        sums = totals(band_sums(parts_one), shares_two, factor)
+    else:
+        whole = lax.psum((parts_one.astype(jnp.float32), parts_two.astype(jnp.float32)), AXES)
+        sums = [x for total in whole for x in split(factor * total, ch)]
     grad_in = call(
         input_kernel,
         [bf16(rows, cols, ch)],
-        [pltpu.VMEM((rows + 2, cols, 3 * ch), jnp.bfloat16)],
+        [views_two],
         2 * conv,
         mid,
         gpre_one,
         spatial_one,
     )
-
-    def split(sums):
-        sums = sums.astype(jnp.float32).reshape(12, ch, ch)
-        return sums[:9].reshape(3, 3, ch, ch), sums[9:]
-
-    gs_one, gt_one = split(sums_one)
-    gs_two, gt_two = split(sums_two)
-    return (grad_in.reshape(shape), gs_one, gt_one, gs_two, gt_two)
+    return (grad_in.reshape(shape), *sums)
 
 
 def solution(mesh):

time: 96.5 us -> 82.2 us (0.85)
  waiting for transfers between devices: 51.4 us -> 13.8 us
  blocking collectives: 0 us -> 30.8 us
  local copies, waits for them, and re-layouts: 6.47 us -> 2.87 us
  starting transfers between devices: 25.8 us -> 23.4 us
    all_to_all x4 -> x1, waiting for transfers between devices: 34.4 us -> 3.39 us  [band_sums(): lax.all_to_all(parts, 'section', split_axis=0, concat_axis=0, tiled=True)]
    all_to_all x0 -> x3, blocking collectives: none -> 30.8 us  [the longest x2 20.9 us: exchanged(): x = lax.all_to_all(x, axes, split_axis=0, concat_axis=0, tiled=True)]
    all_to_all x4 -> x1, starting transfers between devices: 14.2 us -> 3.58 us  [band_sums(): lax.all_to_all(parts, 'section', split_axis=0, concat_axis=0, tiled=True)]
    ppermute x0 -> x3, starting transfers between devices: none -> 9.32 us  [flipped(): return lax.ppermute(x, 'section', pairs)]
    ppermute x6 -> x5, waiting for transfers between devices: 17 us -> 10.3 us  [from_ahead(): return lax.ppermute(block, ('section', 'video'), pairs)]
    slice x7 -> x0, local copies, waits for them, and re-layouts: 5.48 us -> none  [the longest x4 3.09 us: split(): return (sums[:9].reshape(3, 3, ch, ch), sums[9:])]
    unnamed x18 -> x20, local copies, waits for them, and re-layouts: 0.99 us -> 2.87 us
    ppermute x6 -> x5, starting transfers between devices: 11.6 us -> 10.5 us  [from_ahead(): return lax.ppermute(block, ('section', 'video'), pairs)]
  transfers between devices with their start and end apart: 10 -> 9, of which waited for: 6 -> 4; matrix products, arithmetic and copies ran while one was open for 4% -> 0% of each run, Pallas kernels for 7% -> 11%
where the time goes in v2:
time: 82.2 us; the launch traced here: 81.7 us
  blocking collectives  30.8 us (37%)
  starting transfers between devices  23.4 us (28%)
  waiting for transfers between devices  13.8 us (17%)
  Pallas kernels  10.1 us (12%)
  local copies, waits for them, and re-layouts  2.87 us (3%)
    all_to_all x2, blocking collectives, exchanged(): x = lax.all_to_all(x, axes, split_axis=0, concat_axis=0, tiled=True)  20.9 us
    ppermute x5, starting transfers between devices, from_ahead(): return lax.ppermute(block, ('section', 'video'), pairs)  10.5 us
    ppermute x5, waiting for transfers between devices, from_ahead(): return lax.ppermute(block, ('section', 'video'), pairs)  10.3 us
    pallas_call x9, Pallas kernels, call(): pl.pallas_call(kernel, out_shape=outs[0] if single else tuple(outs), grid...  10.1 us
    all_to_all x1, blocking collectives, band_sums(): lax.all_to_all(parts, 'section', split_axis=0, concat_axis=0, tiled=True)  9.82 us
    ppermute x3, starting transfers between devices, flipped(): return lax.ppermute(x, 'section', pairs)  9.32 us
    all_to_all x1, starting transfers between devices, band_sums(): lax.all_to_all(parts, 'section', split_axis=0, concat_axis=0, tiled=True)  3.58 us
    all_to_all x1, waiting for transfers between devices, band_sums(): lax.all_to_all(parts, 'section', split_axis=0, concat_axis=0, tiled=True)  3.39 us
  transfers between devices with their start and end apart: 9, of which 4 were waited for; matrix products, arithmetic and copies ran while one was open for 0% of the time, Pallas kernels for 11%

profile of v2, /device:TPU:1, one launch (start us, length us, event | category | flops | bytes accessed | tf_op | source)
XLA Modules:
  0.0 81.7 jit_solution(9469092247629414441)
XLA Ops:
  0.6 1.3 %collective-permute-start.2 = (bf16[16,64,128]{2,1,0:T(8,128)(2,1)}, bf16[16,64,128]{2,1,0:T(8,128)(2,1)S(1)}, u32[]{:S(2)}, u32[]{:S(2)}) collective-permute-start(bf16[16,64,128]{2,1,0:T(8,128)(2,1)} %bitcast.16), channel_id=1, source_target_pairs={{4,0},{12,8},{20,16},{28,24},{5,1},{13,9},{21,17},{29,25},{6,2},{1... | collective-permute-start | bytes 786440 | tf_op jit(solution)/shard_map/ppermute | solution.py:27
  1.9 0.9 %copy-done = bf16[1,1,16,64,128]{4,3,2,1,0:T(8,128)(2,1)S(1)} copy-done((bf16[1,1,16,64,128]{4,3,2,1,0:T(8,128)(2,1)S(1)}, bf16[1,1,16,64,128]{4,3,2,1,0:T(8,128)(2,1)}, u32[]{:S(2)}) %copy-start) | copy-done | bytes 262168
  2.9 0.9 %copy-done.1 = bf16[1,1,16,64,128]{4,3,2,1,0:T(8,128)(2,1)S(1)} copy-done((bf16[1,1,16,64,128]{4,3,2,1,0:T(8,128)(2,1)S(1)}, bf16[1,1,16,64,128]{4,3,2,1,0:T(8,128)(2,1)}, u32[]{:S(2)}) %copy-start.1) | copy-done | bytes 262168
  3.8 0.9 %copy-done.2 = bf16[1,1,16,64,128]{4,3,2,1,0:T(8,128)(2,1)S(1)} copy-done((bf16[1,1,16,64,128]{4,3,2,1,0:T(8,128)(2,1)S(1)}, bf16[1,1,16,64,128]{4,3,2,1,0:T(8,128)(2,1)}, u32[]{:S(2)}) %copy-start.2) | copy-done | bytes 262168
  4.8 4.7 %collective-permute-start = (bf16[5,64,128]{2,1,0:T(8,128)(2,1)S(1)}, bf16[5,64,128]{2,1,0:T(8,128)(2,1)S(1)}, u32[]{:S(2)}, u32[]{:S(2)}) collective-permute-start(bf16[5,64,128]{2,1,0:T(8,128)(2,1)S(1)} %get-tuple-element.18), channel_id=1, source_target_pairs={{0,8},{4,12},{8,16},{12,20},{16,24},{20,28},{1,9},{5,13},{9,17},{1... | collective-permute-start | bytes 245768 | tf_op jit(solution)/shard_map/ppermute | solution.py:27
  9.5 1.9 %collective-permute-start.1 = (bf16[5,64,128]{2,1,0:T(8,128)(2,1)S(1)}, bf16[5,64,128]{2,1,0:T(8,128)(2,1)S(1)}, u32[]{:S(2)}, u32[]{:S(2)}) collective-permute-start(bf16[5,64,128]{2,1,0:T(8,128)(2,1)S(1)} %get-tuple-element.19), channel_id=1, source_target_pairs={{8,0},{12,4},{16,8},{20,12},{24,16},{28,20},{9,1},{13,5},{17,9},{2... | collective-permute-start | bytes 245768 | tf_op jit(solution)/shard_map/ppermute | solution.py:27
  11.4 0.0 collective-permute-done.refs_2_
  11.4 3.8 %collective-permute-done.1.refs_3_ = bf16[5,64,128]{2,1,0:T(8,128)(2,1)S(1)} collective-permute-done((bf16[5,64,128]{2,1,0:T(8,128)(2,1)S(1)}, bf16[5,64,128]{2,1,0:T(8,128)(2,1)S(1)}, u32[]{:S(2)}, u32[]{:S(2)}) %collective-permute-start.1) | collective-permute-done | bytes 81952 | tf_op jit(solution)/shard_map/ppermute | solution.py:27
  15.2 0.0 copy-done.4
  15.2 1.3 %collective-permute-start.3 = (bf16[4,64,128]{2,1,0:T(8,128)(2,1)S(1)}, bf16[4,64,128]{2,1,0:T(8,128)(2,1)S(1)}, u32[]{:S(2)}, u32[]{:S(2)}) collective-permute-start(bf16[4,64,128]{2,1,0:T(8,128)(2,1)S(1)} %get-tuple-element.20), channel_id=1, source_target_pairs={{4,0},{12,8},{20,16},{28,24},{5,1},{13,9},{21,17},{29,25},{6,2},{1... | collective-permute-start | bytes 196616 | tf_op jit(solution)/shard_map/ppermute | solution.py:27
  16.5 1.3 %collective-permute-start.4 = (bf16[18,64,128]{2,1,0:T(8,128)(2,1)S(1)}, bf16[18,64,128]{2,1,0:T(8,128)(2,1)S(1)}, u32[]{:S(2)}, u32[]{:S(2)}) collective-permute-start(bf16[18,64,128]{2,1,0:T(8,128)(2,1)S(1)} %get-tuple-element.21.refs_8_), channel_id=1, source_target_pairs={{4,0},{12,8},{20,16},{28,24},{5,1},{13,9},{21,17},{29,25},{6,2},{1... | collective-permute-start | bytes 884744 | tf_op jit(solution)/shard_map/ppermute | solution.py:27
  17.8 6.5 %collective-permute-done.3.refs_5_ = bf16[4,64,128]{2,1,0:T(8,128)(2,1)S(1)} collective-permute-done((bf16[4,64,128]{2,1,0:T(8,128)(2,1)S(1)}, bf16[4,64,128]{2,1,0:T(8,128)(2,1)S(1)}, u32[]{:S(2)}, u32[]{:S(2)}) %collective-permute-start.3) | collective-permute-done | bytes 65568 | tf_op jit(solution)/shard_map/ppermute | solution.py:27
  24.3 0.0 collective-permute-done.2.refs_4_
  24.4 2.8 %shard_map.130 = (bf16[18,64,128]{2,1,0:T(8,128)(2,1)S(1)}, bf16[20,64,128]{2,1,0:T(8,128)(2,1)S(1)}) custom-call(bf16[16,64,128]{2,1,0:T(8,128)(2,1)S(1)} %bitcast.20, bf16[16,64,128]{2,1,0:T(8,128)(2,1)S(1)} %bitcast.25, bf16[5,64,128]{2,1,0:T(8,128)(2,1)S(1)} %collective-permute-done.refs_2_, bf16[5,64,128]{2,1,0:T(8,128)(2,1)S(1)} %collective-permute-done.1.refs_3_, ...), custom_call_target="tpu_custom_call" | custom-call | flops 603979776 | bytes 2654208 | tf_op jit(solution)/shard_map/pallas_call | solution.py:289
  27.2 1.8 %shard_map.133 = bf16[1536,128]{1,0:T(8,128)(2,1)} custom-call(bf16[16,64,128]{2,1,0:T(8,128)(2,1)S(1)} %bitcast.37, bf16[16,64,128]{2,1,0:T(8,128)(2,1)S(1)} %bitcast.26, bf16[20,64,128]{2,1,0:T(8,128)(2,1)S(1)} %get-tuple-element.26.refs_2_, bf16[16,64,128]{2,1,0:T(8,128)(2,1)S(1)} %bitcast.21, bf16[16,64,128]{2,1,0:T(8,128)(2,1)S(1)} %collective-permute-done.2.refs_4_), custom_call_target="tpu_custom_call" | custom-call | flops 603979776 | bytes 1769472 | tf_op jit(solution)/shard_map/pallas_call | solution.py:289
  29.0 3.6 %all-to-all-start.1 = ((bf16[4,384,128]{2,1,0:T(8,128)(2,1)}), bf16[4,384,128]{2,1,0:T(8,128)(2,1)S(1)}, u32[]{:S(2)}, u32[]{:S(2)}) async-start(bf16[4,384,128]{2,1,0:T(8,128)(2,1)} %bitcast.7), calls=%async_computation.1 | async-start | bytes 786432 | tf_op jit(solution)/shard_map/all_to_all | solution.py:319
  32.6 0.0 collective-permute-done.4.refs_5_
  32.7 1.7 %shard_map.131 = (bf16[18,64,128]{2,1,0:T(8,128)(2,1)S(1)}, bf16[1536,128]{1,0:T(8,128)(2,1)S(1)}) custom-call(bf16[16,64,128]{2,1,0:T(8,128)(2,1)S(1)} %bitcast.38, bf16[16,64,128]{2,1,0:T(8,128)(2,1)S(1)} %bitcast.29, bf16[5,64,128]{2,1,0:T(8,128)(2,1)S(1)} %collective-permute-done.refs_2_, bf16[5,64,128]{2,1,0:T(8,128)(2,1)S(1)} %collective-permute-done.1.refs_3_, ...), custom_call_target="tpu_custom_call" | custom-call | flops 905969664 | bytes 2064384 | tf_op jit(solution)/shard_map/pallas_call | solution.py:289
  34.4 3.4 %all-to-all-done.1.two_ref = bf16[4,384,128]{2,1,0:T(8,128)(2,1)S(1)} async-done(((bf16[4,384,128]{2,1,0:T(8,128)(2,1)}), bf16[4,384,128]{2,1,0:T(8,128)(2,1)S(1)}, u32[]{:S(2)}, u32[]{:S(2)}) %all-to-all-start.1) | async-done | bytes 393248 | tf_op jit(solution)/shard_map/all_to_all | solution.py:319
  37.8 9.8 %all_to_all.36.one_ref = bf16[4,384,128]{2,1,0:T(8,128)(2,1)S(1)} all-to-all(bf16[4,384,128]{2,1,0:T(8,128)(2,1)S(1)} %bitcast.36), channel_id=1, replica_groups=mesh['section'=4,'video'=2,'dp'=4] {'section'}, dimensions={0} | all-to-all | bytes 786432 | tf_op jit(solution)/shard_map/all_to_all | solution.py:319
  47.6 0.1 shard_map.134
  47.8 11.3 %all_to_all.37 = bf16[8,96,128]{2,1,0:T(8,128)(2,1)S(1)} all-to-all(bf16[8,96,128]{2,1,0:T(8,128)(2,1)S(1)} %bitcast.35), channel_id=1, replica_groups=mesh['section'=4,'video'=2,'dp'=4] {'video','dp'}, dimensions={0} | all-to-all | bytes 393216 | tf_op jit(solution)/shard_map/all_to_all | solution.py:336
  59.2 0.0 copy-start.5
  59.2 9.6 %all_to_all.38 = bf16[8,96,128]{2,1,0:T(8,128)(2,1)S(1)} all-to-all(bf16[8,96,128]{2,1,0:T(8,128)(2,1)S(1)} %bitcast.31), channel_id=1, replica_groups=mesh['section'=4,'video'=2,'dp'=4] {'video','dp'}, dimensions={0} | all-to-all | bytes 393216 | tf_op jit(solution)/shard_map/all_to_all | solution.py:336
  68.8 0.8 %collective-permute-start.6 = (bf16[8,2,48,128]{3,2,1,0:T(8,128)(2,1)S(1)}, bf16[8,2,48,128]{3,2,1,0:T(8,128)(2,1)S(1)}, u32[]{:S(2)}, u32[]{:S(2)}) collective-permute-start(bf16[8,2,48,128]{3,2,1,0:T(8,128)(2,1)S(1)} %bitcast.32), channel_id=1, source_target_pairs={{16,0},{24,8},{0,16},{8,24},{17,1},{25,9},{1,17},{9,25},{18,2},{26... | collective-permute-start | bytes 589832 | tf_op jit(solution)/shard_map/ppermute | solution.py:350
  69.6 3.6 %collective-permute-start.5 = (bf16[8,2,48,128]{3,2,1,0:T(8,128)(2,1)S(1)}, bf16[8,2,48,128]{3,2,1,0:T(8,128)(2,1)S(1)}, u32[]{:S(2)}, u32[]{:S(2)}) collective-permute-start(bf16[8,2,48,128]{3,2,1,0:T(8,128)(2,1)S(1)} %bitcast.33), channel_id=1, source_target_pairs={{8,0},{0,8},{24,16},{16,24},{9,1},{1,9},{25,17},{17,25},{10,2},{2,... | collective-permute-start | bytes 589832 | tf_op jit(solution)/shard_map/ppermute | solution.py:350
  73.2 0.1 collective-permute-done.6.refs_2_
  73.3 4.9 %collective-permute-start.7 = (bf16[8,2,48,128]{3,2,1,0:T(8,128)(2,1)S(1)}, bf16[8,2,48,128]{3,2,1,0:T(8,128)(2,1)S(1)}, u32[]{:S(2)}, u32[]{:S(2)}) collective-permute-start(bf16[8,2,48,128]{3,2,1,0:T(8,128)(2,1)S(1)} %collective-permute-done.6.refs_2_), channel_id=1, source_target_pairs={{8,0},{0,8},{24,16},{16,24},{9,1},{1,9},{25,17},{17,25},{10,2},{2,... | collective-permute-start | bytes 589832 | tf_op jit(solution)/shard_map/ppermute | solution.py:350
  78.2 2.2 %shard_map.132 = bf16[16,64,128]{2,1,0:T(8,128)(2,1)} custom-call(bf16[18,64,128]{2,1,0:T(8,128)(2,1)S(1)} %get-tuple-element.23.refs_4_.mid_ref, bf16[18,64,128]{2,1,0:T(8,128)(2,1)S(1)} %get-tuple-element.24.gpre_ref, bf16[3,3,128,128]{3,2,1,0:T(8,128)(2,1)S(1)} %copy-done.5), custom_call_target="tpu_custom_call" | custom-call | flops 603979776 | bytes 1146880 | tf_op jit(solution)/shard_map/pallas_call | solution.py:289
  80.4 0.0 collective-permute-done.5.refs_1_
  80.4 0.0 collective-permute-done.7.refs_3_
  80.4 1.3 %shard_map.136 = (f32[3,384,128]{2,1,0:T(8,128)}, f32[384,128]{1,0:T(8,128)}, f32[3,384,128]{2,1,0:T(8,128)}, f32[384,128]{1,0:T(8,128)}) custom-call(bf16[8,2,48,128]{3,2,1,0:T(8,128)(2,1)S(1)} %bitcast.34, bf16[8,2,48,128]{3,2,1,0:T(8,128)(2,1)S(1)} %collective-permute-done.5.refs_1_, bf16[8,2,48,128]{3,2,1,0:T(8,128)(2,1)S(1)} %collective-permute-done.6.refs_2_, ...), custom_call_target="tpu_custom_call" | custom-call | flops 98304 | bytes 2359296 | tf_op jit(solution)/shard_map/pallas_call | solution.py:289
  (18 shorter events, 0.1 us)
Async XLA Ops:
  0.6 23.7 %collective-permute-start.2 = (bf16[16,64,128]{2,1,0:T(8,128)(2,1)}, bf16[16,64,128]{2,1,0:T(8,128)(2,1)S(1)}, u32[]{:S(2)}, u32[]{:S(2)}) collective-permute-start(bf16[16,64,128]{2,1,0:T(8,128)(2,1)} %bitcast.16), channel_id=1, source_target_pairs={{4,0},{12,8},{20,16},{28,24},{5,1},{13,9},{21,17},{29,25},{6,2},{1... | collective-permute-start | bytes 786440 | tf_op jit(solution)/shard_map/ppermute | solution.py:27
  1.9 1.0 %copy-start = (bf16[1,1,16,64,128]{4,3,2,1,0:T(8,128)(2,1)S(1)}, bf16[1,1,16,64,128]{4,3,2,1,0:T(8,128)(2,1)}, u32[]{:S(2)}) copy-start(bf16[1,1,16,64,128]{4,3,2,1,0:T(8,128)(2,1)} %param.9) | copy-start | bytes 786436
  2.9 0.9 %copy-start.1 = (bf16[1,1,16,64,128]{4,3,2,1,0:T(8,128)(2,1)S(1)}, bf16[1,1,16,64,128]{4,3,2,1,0:T(8,128)(2,1)}, u32[]{:S(2)}) copy-start(bf16[1,1,16,64,128]{4,3,2,1,0:T(8,128)(2,1)} %param.13) | copy-start | bytes 786436
  3.8 0.9 %copy-start.2 = (bf16[1,1,16,64,128]{4,3,2,1,0:T(8,128)(2,1)S(1)}, bf16[1,1,16,64,128]{4,3,2,1,0:T(8,128)(2,1)}, u32[]{:S(2)}) copy-start(bf16[1,1,16,64,128]{4,3,2,1,0:T(8,128)(2,1)} %param.11) | copy-start | bytes 786436
  4.8 10.5 %copy-start.4 = (bf16[3,3,128,128]{3,2,1,0:T(8,128)(2,1)S(1)}, bf16[3,3,128,128]{3,2,1,0:T(8,128)(2,1)}, u32[]{:S(2)}) copy-start(bf16[3,3,128,128]{3,2,1,0:T(8,128)(2,1)} %refs_7_.1) | copy-start | bytes 884740
  4.8 10.5 %copy-start.8 = (bf16[3,128,128]{2,1,0:T(8,128)(2,1)S(1)}, bf16[3,128,128]{2,1,0:T(8,128)(2,1)}, u32[]{:S(2)}) copy-start(bf16[3,128,128]{2,1,0:T(8,128)(2,1)} %refs_6_.2) | copy-start | bytes 294916
  4.8 6.6 %collective-permute-start = (bf16[5,64,128]{2,1,0:T(8,128)(2,1)S(1)}, bf16[5,64,128]{2,1,0:T(8,128)(2,1)S(1)}, u32[]{:S(2)}, u32[]{:S(2)}) collective-permute-start(bf16[5,64,128]{2,1,0:T(8,128)(2,1)S(1)} %get-tuple-element.18), channel_id=1, source_target_pairs={{0,8},{4,12},{8,16},{12,20},{16,24},{20,28},{1,9},{5,13},{9,17},{1... | collective-permute-start | bytes 245768 | tf_op jit(solution)/shard_map/ppermute | solution.py:27
  9.5 5.8 %collective-permute-start.1 = (bf16[5,64,128]{2,1,0:T(8,128)(2,1)S(1)}, bf16[5,64,128]{2,1,0:T(8,128)(2,1)S(1)}, u32[]{:S(2)}, u32[]{:S(2)}) collective-permute-start(bf16[5,64,128]{2,1,0:T(8,128)(2,1)S(1)} %get-tuple-element.19), channel_id=1, source_target_pairs={{8,0},{12,4},{16,8},{20,12},{24,16},{28,20},{9,1},{13,5},{17,9},{2... | collective-permute-start | bytes 245768 | tf_op jit(solution)/shard_map/ppermute | solution.py:27
  15.2 9.1 %collective-permute-start.3 = (bf16[4,64,128]{2,1,0:T(8,128)(2,1)S(1)}, bf16[4,64,128]{2,1,0:T(8,128)(2,1)S(1)}, u32[]{:S(2)}, u32[]{:S(2)}) collective-permute-start(bf16[4,64,128]{2,1,0:T(8,128)(2,1)S(1)} %get-tuple-element.20), channel_id=1, source_target_pairs={{4,0},{12,8},{20,16},{28,24},{5,1},{13,9},{21,17},{29,25},{6,2},{1... | collective-permute-start | bytes 196616 | tf_op jit(solution)/shard_map/ppermute | solution.py:27
  16.5 16.1 %collective-permute-start.4 = (bf16[18,64,128]{2,1,0:T(8,128)(2,1)S(1)}, bf16[18,64,128]{2,1,0:T(8,128)(2,1)S(1)}, u32[]{:S(2)}, u32[]{:S(2)}) collective-permute-start(bf16[18,64,128]{2,1,0:T(8,128)(2,1)S(1)} %get-tuple-element.21.refs_8_), channel_id=1, source_target_pairs={{4,0},{12,8},{20,16},{28,24},{5,1},{13,9},{21,17},{29,25},{6,2},{1... | collective-permute-start | bytes 884744 | tf_op jit(solution)/shard_map/ppermute | solution.py:27
  24.4 2.8 %copy-start.6 = (bf16[1,1,16,64,128]{4,3,2,1,0:T(8,128)(2,1)S(1)}, bf16[1,1,16,64,128]{4,3,2,1,0:T(8,128)(2,1)}, u32[]{:S(2)}) copy-start(bf16[1,1,16,64,128]{4,3,2,1,0:T(8,128)(2,1)} %param.12) | copy-start | bytes 786436
  29.0 3.6 %copy-start.3 = (bf16[1,1,16,64,128]{4,3,2,1,0:T(8,128)(2,1)S(1)}, bf16[1,1,16,64,128]{4,3,2,1,0:T(8,128)(2,1)}, u32[]{:S(2)}) copy-start(bf16[1,1,16,64,128]{4,3,2,1,0:T(8,128)(2,1)} %param.11) | copy-start | bytes 786436
  29.0 3.6 %copy-start.7 = (bf16[1,1,16,64,128]{4,3,2,1,0:T(8,128)(2,1)S(1)}, bf16[1,1,16,64,128]{4,3,2,1,0:T(8,128)(2,1)}, u32[]{:S(2)}) copy-start(bf16[1,1,16,64,128]{4,3,2,1,0:T(8,128)(2,1)} %param.10) | copy-start | bytes 786436
  29.0 3.6 %copy-start.9 = (bf16[3,128,128]{2,1,0:T(8,128)(2,1)S(1)}, bf16[3,128,128]{2,1,0:T(8,128)(2,1)}, u32[]{:S(2)}) copy-start(bf16[3,128,128]{2,1,0:T(8,128)(2,1)} %refs_6_.3) | copy-start | bytes 294916
  29.0 8.8 %all-to-all-start.1 = ((bf16[4,384,128]{2,1,0:T(8,128)(2,1)}), bf16[4,384,128]{2,1,0:T(8,128)(2,1)S(1)}, u32[]{:S(2)}, u32[]{:S(2)}) async-start(bf16[4,384,128]{2,1,0:T(8,128)(2,1)} %bitcast.7), calls=%async_computation.1 | async-start | bytes 786432 | tf_op jit(solution)/shard_map/all_to_all | solution.py:319
  59.2 19.0 %copy-start.5 = (bf16[3,3,128,128]{3,2,1,0:T(8,128)(2,1)S(1)}, bf16[3,3,128,128]{3,2,1,0:T(8,128)(2,1)}, u32[]{:S(2)}) copy-start(bf16[3,3,128,128]{3,2,1,0:T(8,128)(2,1)} %spatial_ref.1) | copy-start | bytes 884740
  68.8 4.5 %collective-permute-start.6 = (bf16[8,2,48,128]{3,2,1,0:T(8,128)(2,1)S(1)}, bf16[8,2,48,128]{3,2,1,0:T(8,128)(2,1)S(1)}, u32[]{:S(2)}, u32[]{:S(2)}) collective-permute-start(bf16[8,2,48,128]{3,2,1,0:T(8,128)(2,1)S(1)} %bitcast.32), channel_id=1, source_target_pairs={{16,0},{24,8},{0,16},{8,24},{17,1},{25,9},{1,17},{9,25},{18,2},{26... | collective-permute-start | bytes 589832 | tf_op jit(solution)/shard_map/ppermute | solution.py:350
  69.6 10.8 %collective-permute-start.5 = (bf16[8,2,48,128]{3,2,1,0:T(8,128)(2,1)S(1)}, bf16[8,2,48,128]{3,2,1,0:T(8,128)(2,1)S(1)}, u32[]{:S(2)}, u32[]{:S(2)}) collective-permute-start(bf16[8,2,48,128]{3,2,1,0:T(8,128)(2,1)S(1)} %bitcast.33), channel_id=1, source_target_pairs={{8,0},{0,8},{24,16},{16,24},{9,1},{1,9},{25,17},{17,25},{10,2},{2,... | collective-permute-start | bytes 589832 | tf_op jit(solution)/shard_map/ppermute | solution.py:350
  73.3 7.1 %collective-permute-start.7 = (bf16[8,2,48,128]{3,2,1,0:T(8,128)(2,1)S(1)}, bf16[8,2,48,128]{3,2,1,0:T(8,128)(2,1)S(1)}, u32[]{:S(2)}, u32[]{:S(2)}) collective-permute-start(bf16[8,2,48,128]{3,2,1,0:T(8,128)(2,1)S(1)} %collective-permute-done.6.refs_2_), channel_id=1, source_target_pairs={{8,0},{0,8},{24,16},{16,24},{9,1},{1,9},{25,17},{17,25},{10,2},{2,... | collective-permute-start | bytes 589832 | tf_op jit(solution)/shard_map/ppermute | solution.py:350

commit v3 on v0

v3 whole, which is shorter than its diff:
```python
import functools
import math

import jax
import jax.numpy as jnp
from jax import lax
from jax.experimental import pallas as pl
from jax.experimental.pallas import tpu as pltpu
from jax.sharding import PartitionSpec as P

MIB = 1024 * 1024


def sigmoid(value):
    return 1.0 / (1.0 + jnp.exp(-value))


def bf16(*shape):
    return jax.ShapeDtypeStruct(shape, jnp.bfloat16)


def f32(*shape):
    return jax.ShapeDtypeStruct(shape, jnp.float32)


def call(kernel, outs, scratch, flops, *operands, grid=(), in_specs=None, limit=24):
    single = len(outs) == 1
    moved = sum(math.prod(x.shape) * x.dtype.itemsize for x in (*operands, *outs))
    vmem = pl.BlockSpec(memory_space=pltpu.VMEM)
    return pl.pallas_call(
        kernel,
        out_shape=outs[0] if single else tuple(outs),
        grid=grid,
        in_specs=in_specs or [vmem] * len(operands),
        out_specs=vmem if single else (vmem,) * len(outs),
        scratch_shapes=scratch,
        compiler_params=pltpu.CompilerParams(vmem_limit_bytes=limit * MIB),
        cost_estimate=pl.CostEstimate(
            flops=int(flops), bytes_accessed=int(moved), transcendentals=0
        ),
    )(*operands)


def from_ahead(block, band_step, frame_step):
    bands, frames = lax.axis_size("section"), lax.axis_size("video")
    pairs = [
        ((band + band_step) * frames + frame + frame_step, band * frames + frame)
        for band in range(bands)
        for frame in range(frames)
        if 0 <= band + band_step < bands and frame + frame_step < frames
    ]
    return lax.ppermute(block, ("section", "video"), pairs)


def flipped(block, axis, flip):
    count = lax.axis_size(axis)
    return lax.ppermute(block, axis, [(place ^ flip, place) for place in range(count)])


def beside(gpre, views_ref, start):
    count, cols, ch = gpre.shape
    at = lax.broadcasted_iota(jnp.int32, gpre.shape, 1)
    right = jnp.where(at == cols - 1, 0.0, pltpu.roll(gpre, cols - 1, 1))
    left = jnp.where(at == 0, 0.0, pltpu.roll(gpre, 1, 1))
    here = pl.ds(start, count)
    views_ref[here, :, 0:ch] = right.astype(jnp.bfloat16)
    views_ref[here, :, ch : 2 * ch] = gpre.astype(jnp.bfloat16)
    views_ref[here, :, 2 * ch : 3 * ch] = left.astype(jnp.bfloat16)


def pre_gradient(grads, preact, temporal_ref):
    count, cols, ch = preact.shape
    flat = jnp.concatenate([grad.reshape(count * cols, ch) for grad in grads], axis=1)
    kernel = jnp.concatenate([temporal_ref[2 - step] for step in range(len(grads))], axis=1)
    gact = lax.dot_general(
        flat, kernel, (((1,), (1,)), ((), ())), preferred_element_type=jnp.float32
    )
    gact = gact.astype(jnp.bfloat16).astype(jnp.float32).reshape(preact.shape)
    hval = preact.astype(jnp.float32)
    sig = sigmoid(hval)
    return gact * sig * (1.0 + hval * (1.0 - sig))


def convolved(views_ref, spatial_ref, start, first):
    count, cols, ch = first.shape
    total = first.astype(jnp.float32).reshape(count * cols, ch)
    for ky in range(3):
        view = views_ref[pl.ds(start + 2 - ky, count)].reshape(count * cols, 3 * ch)
        kernel = jnp.concatenate([spatial_ref[ky, kx] for kx in range(3)], axis=1)
        total = total + lax.dot_general(
            view, kernel, (((1,), (1,)), ((), ())), preferred_element_type=jnp.float32
        )
    return total.astype(jnp.bfloat16).reshape(first.shape)


def kernel_sums(saved_ref, above, below, act, grads, views, sums_ref):
    rows, cols, ch = saved_ref.shape
    flat = (rows * cols, ch)
    saved = [
        jnp.concatenate([above, saved_ref[: rows - 1]], axis=0),
        saved_ref[...],
        jnp.concatenate([saved_ref[1:], below], axis=0),
    ]
    for ky in range(3):
        sums = jnp.dot(saved[ky].reshape(flat).T, views, preferred_element_type=jnp.float32)
        for kx in range(3):
            sums_ref[ky, kx * ch : (kx + 1) * ch] = sums[:, kx * ch : (kx + 1) * ch]
    sums = jnp.dot(
        act.reshape(flat).T,
        jnp.concatenate([grad.reshape(flat) for grad in grads], axis=1),
        preferred_element_type=jnp.float32,
    )
    for k in range(3):
        step = 2 - k
        here = slice(k * ch, (k + 1) * ch)
        if step < len(grads):
            sums_ref[3, here] = sums[:, step * ch : (step + 1) * ch]
        else:
            sums_ref[3, here] = jnp.zeros((ch, ch), jnp.float32)


def hand_out(sums_ref, outs):
    band = lax.axis_index("section")
    outs[0][...] = sums_ref[band]
    for flip in range(1, 4):
        outs[flip][...] = sums_ref[jnp.bitwise_xor(band, flip)].astype(jnp.bfloat16)


def pack_kernel(*refs):
    parts, (up_ref, down_ref) = refs[:8], refs[8:]
    for n in range(4):
        up_ref[n : n + 1] = parts[n][...]
        down_ref[n : n + 1] = parts[n + 4][...]


def interior(grad_ref, preact_ref, wholes, temporal_ref, spatial_ref, inner_ref, gpre_ref, views_ref):
    rows, cols, ch = grad_ref.shape
    step = 4

    @pl.loop(0, rows // step)
    def _(n):
        here = pl.ds(n * step, step)
        grads = [ref[here] for ref in (grad_ref, *wholes)]
        gpre = pre_gradient(grads, preact_ref[here], temporal_ref)
        gpre_ref[here] = gpre.astype(jnp.bfloat16)
        beside(gpre, views_ref, n * step)

    half = rows // 2 - 1

    @pl.loop(0, 2)
    def _(n):
        first = grad_ref[pl.ds(n * half + 1, half)]
        inner_ref[pl.ds(n * half, half)] = convolved(views_ref, spatial_ref, n * half, first)


def edge_rows(grad_ref, low_ref, high_ref, afters, gpre_ref, temporal_ref, spatial_ref, views_ref):
    rows, cols, ch = grad_ref.shape
    above = [low_ref[0:1]] + [ref[2:3] for ref in afters]
    below = [high_ref[0:1]] + [ref[3:4] for ref in afters]
    beside(pre_gradient(above, low_ref[1:2], temporal_ref), views_ref, 0)
    beside(gpre_ref[0:2].astype(jnp.float32), views_ref, 1)
    beside(gpre_ref[rows - 2 : rows].astype(jnp.float32), views_ref, 3)
    beside(pre_gradient(below, high_ref[1:2], temporal_ref), views_ref, 5)
    return (
        convolved(views_ref, spatial_ref, 0, grad_ref[0:1]),
        convolved(views_ref, spatial_ref, 3, grad_ref[rows - 1 : rows]),
    )


def on_last(body):
    pl.when(lax.axis_index("video") == lax.axis_size("video") - 1)(body)


def last_inner_kernel(grad_ref, preact_ref, temporal_ref, spatial_ref, inner_ref, gpre_ref, views_ref):
    on_last(
        lambda: interior(
            grad_ref, preact_ref, [], temporal_ref, spatial_ref, inner_ref, gpre_ref, views_ref
        )
    )


def last_edge_kernel(grad_ref, low_ref, high_ref, gpre_ref, temporal_ref, spatial_ref, edge_ref, views_ref):
    def body():
        edge_ref[0:1], edge_ref[1:2] = edge_rows(
            grad_ref, low_ref, high_ref, [], gpre_ref, temporal_ref, spatial_ref, views_ref
        )
        edge_ref[2:3] = low_ref[0:1]
        edge_ref[3:4] = high_ref[0:1]

    on_last(body)


def inner_kernel(later, *refs):
    inputs, wholes, kernels = refs[:2], refs[2 : 2 + later], refs[2 + later : 4 + later]
    known, outs = refs[4 + later : -3], refs[-3:]
    if not known:
        interior(*inputs, wholes, *kernels, *outs)
        return

    def copied():
        outs[0][...] = known[0][...]
        outs[1][...] = known[1][...]

    on_last(copied)

    @pl.when(lax.axis_index("video") < lax.axis_size("video") - 1)
    def _():
        interior(*inputs, wholes, *kernels, *outs)


def mid_kernel(later, *refs):
    grad_ref, low_ref, high_ref, inner_ref, gpre_ref = refs[:5]
    afters, (temporal_ref, spatial_ref, mid_ref, views_ref) = refs[5 : 5 + later], refs[5 + later :]
    rows = grad_ref.shape[0]
    first, last = edge_rows(
        grad_ref, low_ref, high_ref, afters, gpre_ref, temporal_ref, spatial_ref, views_ref
    )
    mid_ref[0:1], mid_ref[rows - 1 : rows] = first, last
    mid_ref[1 : rows - 1] = inner_ref[...]


def two_kernel(later, *refs):
    saved_ref, preact_ref, gpre_ref, low_ref, high_ref, grad_ref = refs[:6]
    wholes, outs = refs[6 : 6 + later], refs[6 + later : 10 + later]
    views_ref, act_ref, sums_ref = refs[10 + later :]
    rows, cols, ch = saved_ref.shape
    step = 4

    @pl.loop(0, rows // step)
    def _(n):
        here = pl.ds(n * step, step)
        beside(gpre_ref[here].astype(jnp.float32), views_ref, n * step)
        hval = preact_ref[here].astype(jnp.float32)
        act_ref[here] = (hval * sigmoid(hval)).astype(jnp.bfloat16)

    views = views_ref[...].reshape(rows * cols, 3 * ch)
    grads = [ref[...] for ref in (grad_ref, *wholes)]
    kernel_sums(saved_ref, low_ref[2:3], high_ref[2:3], act_ref[...], grads, views, sums_ref)
    hand_out(sums_ref, outs)


def block_one(saved_ref, preact_ref, low_ref, high_ref, mids, temporal_ref, outs, scratch):
    gpre_ref, first_ref, last_ref = outs[:3]
    views_ref, act_ref, sums_ref = scratch
    rows, cols, ch = saved_ref.shape
    step = 4

    @pl.loop(0, rows // step)
    def _(n):
        here = pl.ds(n * step, step)
        gpre = pre_gradient([ref[here] for ref in mids], preact_ref[here], temporal_ref)
        gpre_ref[here] = gpre.astype(jnp.bfloat16)
        beside(gpre, views_ref, n * step)
        hval = preact_ref[here].astype(jnp.float32)
        act_ref[here] = (hval * sigmoid(hval)).astype(jnp.bfloat16)

    first_ref[...] = gpre_ref[0:1]
    last_ref[...] = gpre_ref[rows - 1 : rows]
    views = views_ref[...].reshape(rows * cols, 3 * ch)
    grads = [ref[...] for ref in mids]
    kernel_sums(saved_ref, low_ref[3:4], high_ref[3:4], act_ref[...], grads, views, sums_ref)
    hand_out(sums_ref, outs[3:])


def one_kernel(later, *refs):
    saved_ref, preact_ref, low_ref, high_ref, mid_ref = refs[:5]
    nexts, temporal_ref = refs[5 : 5 + later], refs[5 + later]
    outs, scratch = refs[6 + later : 13 + later], refs[13 + later :]
    block_one(
        saved_ref, preact_ref, low_ref, high_ref, [mid_ref, *nexts], temporal_ref, outs, scratch
    )


def mid_one_kernel(*refs):
    grad_ref, low_ref, high_ref, inner_ref, gpre_two_ref, after_inner_ref, after_edge_ref = refs[:7]
    temporal_two_ref, spatial_two_ref, saved_ref, preact_ref, temporal_ref = refs[7:12]
    mid_ref, outs, scratch = refs[12], refs[13:20], refs[20:23]
    next_ref, edge_views_ref = refs[23:]
    rows = grad_ref.shape[0]
    mid_kernel(
        1,
        grad_ref,
        low_ref,
        high_ref,
        inner_ref,
        gpre_two_ref,
        after_edge_ref,
        temporal_two_ref,
        spatial_two_ref,
        mid_ref,
        edge_views_ref,
    )
    next_ref[0:1] = after_edge_ref[0:1]
    next_ref[1 : rows - 1] = after_inner_ref[...]
    next_ref[rows - 1 : rows] = after_edge_ref[1:2]
    block_one(
        saved_ref, preact_ref, low_ref, high_ref, [mid_ref, next_ref], temporal_ref, outs, scratch
    )


def input_kernel(mid_ref, gpre_ref, above_ref, below_ref, spatial_ref, out_ref, views_ref):
    rows, cols, ch = out_ref.shape
    step = 4
    beside(above_ref[...].astype(jnp.float32), views_ref, 0)
    beside(below_ref[...].astype(jnp.float32), views_ref, rows + 1)

    @pl.loop(0, rows // step)
    def _(n):
        gpre = gpre_ref[pl.ds(n * step, step)].astype(jnp.float32)
        beside(gpre, views_ref, n * step + 1)

    @pl.loop(0, rows // step)
    def _(n):
        here = pl.ds(n * step, step)
        out_ref[here] = convolved(views_ref, spatial_ref, n * step, mid_ref[here])


def added(refs, rows):
    total = refs[0][rows].astype(jnp.float32)
    for ref in refs[1:]:
        total = total + ref[rows].astype(jnp.float32)
    return total


def band_kernel(own_ref, *refs):
    parts, (keep_ref, send_ref) = refs[:3], refs[3:]
    half = keep_ref.shape[0]
    frame = lax.axis_index("video")
    mine = pl.ds(pl.multiple_of(frame * half, half), half)
    other = pl.ds(pl.multiple_of((1 - frame) * half, half), half)
    keep_ref[...] = added((own_ref, *parts), mine)
    send_ref[...] = added((own_ref, *parts), other).astype(jnp.bfloat16)


def frame_kernel(keep_ref, part_ref, out_ref):
    out_ref[...] = (keep_ref[...] + part_ref[...].astype(jnp.float32)).astype(jnp.bfloat16)


def clip_kernel(factor, *refs):
    out_ref = refs[-1]
    for block in range(2):
        a, b, c, d = (ref[...].astype(jnp.float32) for ref in refs[4 * block : 4 * block + 4])
        out_ref[block] = (((a + b) + (c + d)) * factor).astype(jnp.bfloat16)


def join_kernel(own_ref, other_ref, out_ref):
    frame = lax.axis_index("video")
    out_ref[frame] = own_ref[...]
    out_ref[1 - frame] = other_ref[...]


def place_kernel(*refs):
    shares, outs = refs[:4], refs[4:]
    band = lax.axis_index("section")
    parts, _, height, _ = shares[0].shape
    for flip, share in enumerate(shares):
        place = jnp.bitwise_xor(band, flip)

        @pl.when(place < 3)
        def _():
            for block in range(2):
                for n in range(parts):
                    here = slice(n * height, (n + 1) * height)
                    outs[2 * block][place, here] = share[n, block].astype(jnp.float32)

        @pl.when(place == 3)
        def _():
            for block in range(2):
                for n in range(parts):
                    here = slice(n * height, (n + 1) * height)
                    outs[2 * block + 1][here] = share[n, block].astype(jnp.float32)


def frames_summed(own, *parts):
    height, ch = own.shape
    half = height // 2
    keep, send = call(band_kernel, [f32(half, ch), bf16(half, ch)], [], own.size, own, *parts)
    other = flipped(send, "video", 1)
    return call(frame_kernel, [bf16(half, ch)], [], half * ch, keep, other)


def totals(one, two, factor):
    height, ch = one[0].shape
    one, two = (
        [own] + [flipped(part, "section", flip + 1) for flip, part in enumerate(parts)]
        for own, *parts in (one, two)
    )
    if lax.axis_size("video") == 2 and lax.axis_size("dp") == 4:
        two, one = frames_summed(*two), frames_summed(*one)
        parts = [
            x
            for own in (one, two)
            for x in [own] + [flipped(own, "dp", flip) for flip in range(1, 4)]
        ]
        half = height // 2
        own = call(
            functools.partial(clip_kernel, factor), [bf16(2, half, ch)], [], 8 * height * ch, *parts
        )
        other = flipped(own, "video", 1)
        share = call(join_kernel, [bf16(2, 2, half, ch)], [], 1, own, other)
    else:
        own = [sum(x.astype(jnp.float32) for x in parts) for parts in (one, two)]
        share = lax.psum(jnp.stack(own), ("video", "dp")) * factor
        share = share.astype(jnp.bfloat16)[None]
    across = flipped(share, "section", 2)
    outs = call(
        place_kernel,
        [f32(3, height, ch), f32(height, ch)] * 2,
        [],
        share.size,
        share,
        flipped(share, "section", 1),
        across,
        flipped(across, "section", 1),
    )
    return [x.reshape(3, 3, ch, ch) if x.ndim == 3 else x.reshape(3, ch, ch) for x in outs]


def on_device(
    grad_latent,
    input_one,
    preact_one,
    input_two,
    preact_two,
    spatial_one,
    temporal_one,
    spatial_two,
    temporal_two,
):
    shape = grad_latent.shape
    rows, cols, ch = shape[2:]
    bands, frames = lax.axis_size("section"), lax.axis_size("video")
    later = min(2, frames - 1)
    pixels = lax.axis_size("dp") * frames * bands * rows * cols
    factor = 1.0 / math.sqrt(pixels)
    grad, saved_one, pre_one, saved_two, pre_two = (
        x.reshape(rows, cols, ch)
        for x in (grad_latent, input_one, preact_one, input_two, preact_two)
    )
    conv = 2 * rows * cols * 9 * ch * ch
    views = pltpu.VMEM((rows, cols, 3 * ch), jnp.bfloat16)
    edge_views = pltpu.VMEM((6, cols, 3 * ch), jnp.bfloat16)
    act = pltpu.VMEM((rows, cols, ch), jnp.bfloat16)
    sums = pltpu.VMEM((4, 3 * ch, ch), jnp.float32)
    handed = [f32(3 * ch, ch)] + [bf16(3 * ch, ch)] * 3
    inner_outs = [bf16(rows - 2, cols, ch), bf16(rows, cols, ch)]
    kernels = (temporal_two, spatial_two)

    wholes = [from_ahead(grad, 0, n + 1) for n in range(later)]
    edges = [pl.BlockSpec((1, cols, ch), lambda _, at=at: (at, 0, 0)) for at in (0, rows - 1)]
    up, down = call(
        pack_kernel,
        [bf16(4, cols, ch)] * 2,
        [],
        1,
        *(grad, pre_two, saved_two, saved_one) * 2,
        grid=(1,),
        in_specs=[edges[0]] * 4 + [edges[1]] * 4,
        limit=56,
    )
    low = from_ahead(down, -1, 0)
    high = from_ahead(up, 1, 0)

    known = ()
    if frames == 2:
        known = call(last_inner_kernel, inner_outs, [views], 1.2 * conv, grad, pre_two, *kernels)
        after_inner = from_ahead(known[0], 0, 1)
        edge = call(
            last_edge_kernel,
            [bf16(4, cols, ch)],
            [edge_views],
            conv // 8,
            grad,
            low,
            high,
            known[1],
            *kernels,
        )
    else:
        edge = jnp.concatenate([grad[:1], grad[rows - 1 :], low[:1], high[:1]])
    after_edges = [from_ahead(edge, 0, n + 1) for n in range(later)]
    inner, gpre_two = call(
        functools.partial(inner_kernel, later),
        inner_outs,
        [views],
        1.2 * conv,
        grad,
        pre_two,
        *wholes,
        *kernels,
        *known,
    )
    parts_two = call(
        functools.partial(two_kernel, later),
        handed,
        [views, act, sums],
        1.2 * conv,
        saved_two,
        pre_two,
        gpre_two,
        low,
        high,
        grad,
        *wholes,
    )
    mid_inputs = (grad, low, high, inner, gpre_two)
    one_inputs = (saved_one, pre_one)
    mid_outs = [bf16(rows, cols, ch)]
    one_outs = [bf16(rows, cols, ch)] + [bf16(1, cols, ch)] * 2 + handed
    if frames == 2:
        mid, gpre_one, first, last, *parts_one = call(
            mid_one_kernel,
            mid_outs + one_outs,
            [views, act, sums, act, edge_views],
            1.5 * conv,
            *mid_inputs,
            after_inner,
            *after_edges,
            *kernels,
            *one_inputs,
            temporal_one,
        )
    else:
        mid = call(
            functools.partial(mid_kernel, later),
            mid_outs,
            [edge_views],
            conv // 8,
            *mid_inputs,
            *after_edges,
            *kernels,
        )
        gpre_one, first, last, *parts_one = call(
            functools.partial(one_kernel, later),
            one_outs,
            [views, act, sums],
            1.2 * conv,
            *one_inputs,
            low,
            high,
            mid,
            *[from_ahead(mid, 0, n + 1) for n in range(later)],
            temporal_one,
        )
    sums = totals(parts_one, parts_two, factor)
    grad_in = call(
        input_kernel,
        [bf16(rows, cols, ch)],
        [pltpu.VMEM((rows + 2, cols, 3 * ch), jnp.bfloat16)],
        conv,
        mid,
        gpre_one,
        from_ahead(last, -1, 0),
        from_ahead(first, 1, 0),
        spatial_one,
    )
    return (grad_in.reshape(shape), *sums)


def solution(mesh):
    whole = P("dp", "video", "section", None, None)
    return jax.shard_map(
        on_device,
        mesh=mesh,
        in_specs=(whole,) * 5 + (P(),) * 4,
        out_specs=(whole, P(), P(), P(), P()),
        check_vma=False,
    )
```

time: 237 us -> 72.8 us (0.31)
  waiting for transfers between devices: 139 us -> 19.3 us
  local copies, waits for them, and re-layouts: 21.6 us -> 3.8 us
  between operations: 14.5 us -> 0.93 us
  matrix products: 11.4 us -> 0 us
  Pallas kernels: 0 us -> 10.2 us
  other arithmetic: 10.2 us -> 0 us
  starting transfers between devices: 31.5 us -> 38.2 us
  blocking collectives: 6.41 us -> 0 us
    psum x1 -> x0, waiting for transfers between devices: 128 us -> none  [on_device(): lax.psum((gs_one, gt_one, gs_two, gt_two), ('section', 'video', 'dp'))]
    ppermute x4 -> x25, starting transfers between devices: 12.8 us -> 38.2 us  [the longest x18 23.3 us: flipped(): lax.ppermute(block, axis, [(place ^ flip, place) for place in range(count)])]
    all_to_all x5 -> x0, starting transfers between devices: 18.7 us -> none  [the longest x2 7.55 us: temporal_back(): lax.all_to_all(act, 'video', split_axis=2, concat_axis=1, tiled=True)]
    ppermute x4 -> x25, waiting for transfers between devices: 3.08 us -> 19.3 us  [the longest x18 11.3 us: flipped(): lax.ppermute(block, axis, [(place ^ flip, place) for place in range(count)])]
    dot_general x8 -> x0, matrix products: 11.4 us -> none  [the longest x2 4.64 us: spatial_back(): jnp.dot(grad_cols, flipped, preferred_element_type=jnp.float32)]
    pallas_call x0 -> x14, Pallas kernels: none -> 10.2 us  [call(): pl.pallas_call(kernel, out_shape=outs[0] if single else tuple(outs), grid...]
    unnamed x62 -> x26, local copies, waits for them, and re-layouts: 12.4 us -> 3.8 us
    all_to_all x5 -> x0, waiting for transfers between devices: 7.96 us -> none  [the longest x2 4.56 us: temporal_back(): lax.all_to_all(grad_out, 'video', split_axis=2, concat_axis=1, tiled=True)]
  transfers between devices with their start and end apart: 10 -> 25, of which waited for: 5 -> 9; matrix products, arithmetic and copies ran while one was open for 11% -> 0% of each run, Pallas kernels for 0% -> 12%
where the time goes in v3:
time: 72.8 us; the launch traced here: 72.4 us
  starting transfers between devices  38.2 us (52%)
  waiting for transfers between devices  19.3 us (27%)
  Pallas kernels  10.2 us (14%)
  local copies, waits for them, and re-layouts  3.8 us (5%)
  between operations  0.93 us (1%)
    ppermute x18, starting transfers between devices, flipped(): lax.ppermute(block, axis, [(place ^ flip, place) for place in range(count)])  23.3 us
    ppermute x7, starting transfers between devices, from_ahead(): return lax.ppermute(block, ('section', 'video'), pairs)  14.9 us
    ppermute x18, waiting for transfers between devices, flipped(): lax.ppermute(block, axis, [(place ^ flip, place) for place in range(count)])  11.3 us
    pallas_call x14, Pallas kernels, call(): pl.pallas_call(kernel, out_shape=outs[0] if single else tuple(outs), grid...  10.2 us
    ppermute x7, waiting for transfers between devices, from_ahead(): return lax.ppermute(block, ('section', 'video'), pairs)  8.08 us
    unnamed x26, local copies, waits for them, and re-layouts  3.8 us
  transfers between devices with their start and end apart: 25, of which 9 were waited for; matrix products, arithmetic and copies ran while one was open for 0% of the time, Pallas kernels for 12%

profile of v3, /device:TPU:1, one launch (start us, length us, event | category | flops | bytes accessed | tf_op | source)
XLA Modules:
  0.0 72.4 jit_solution(587028319580479588)
XLA Ops:
  0.6 1.3 %collective-permute-start.2 = (bf16[16,64,128]{2,1,0:T(8,128)(2,1)}, bf16[16,64,128]{2,1,0:T(8,128)(2,1)S(1)}, u32[]{:S(2)}, u32[]{:S(2)}) collective-permute-start(bf16[16,64,128]{2,1,0:T(8,128)(2,1)} %bitcast.10), channel_id=1, source_target_pairs={{4,0},{12,8},{20,16},{28,24},{5,1},{13,9},{21,17},{29,25},{6,2},{1... | collective-permute-start | bytes 786440 | tf_op jit(solution)/shard_map/ppermute | solution.py:52
  1.9 0.9 %copy-done = bf16[1,1,16,64,128]{4,3,2,1,0:T(8,128)(2,1)S(1)} copy-done((bf16[1,1,16,64,128]{4,3,2,1,0:T(8,128)(2,1)S(1)}, bf16[1,1,16,64,128]{4,3,2,1,0:T(8,128)(2,1)}, u32[]{:S(2)}) %copy-start) | copy-done | bytes 262168
  2.9 0.9 %copy-done.2 = bf16[1,1,16,64,128]{4,3,2,1,0:T(8,128)(2,1)S(1)} copy-done((bf16[1,1,16,64,128]{4,3,2,1,0:T(8,128)(2,1)S(1)}, bf16[1,1,16,64,128]{4,3,2,1,0:T(8,128)(2,1)}, u32[]{:S(2)}) %copy-start.2) | copy-done | bytes 262168
  3.8 1.0 %copy-done.4 = bf16[3,3,128,128]{3,2,1,0:T(8,128)(2,1)S(1)} copy-done((bf16[3,3,128,128]{3,2,1,0:T(8,128)(2,1)S(1)}, bf16[3,3,128,128]{3,2,1,0:T(8,128)(2,1)}, u32[]{:S(2)}) %copy-start.4) | copy-done | bytes 294936
  5.7 1.3 %collective-permute-start.3 = (bf16[14,64,128]{2,1,0:T(8,128)(2,1)S(1)}, bf16[14,64,128]{2,1,0:T(8,128)(2,1)S(1)}, u32[]{:S(2)}, u32[]{:S(2)}) collective-permute-start(bf16[14,64,128]{2,1,0:T(8,128)(2,1)S(1)} %get-tuple-element.33.refs_5_), channel_id=1, source_target_pairs={{4,0},{12,8},{20,16},{28,24},{5,1},{13,9},{21,17},{29,25},{6,2},{1... | collective-permute-start | bytes 688136 | tf_op jit(solution)/shard_map/ppermute | solution.py:52
  7.0 1.5 %shard_map.128 = (bf16[4,64,128]{2,1,0:T(8,128)(2,1)}, bf16[4,64,128]{2,1,0:T(8,128)(2,1)}) custom-call(bf16[16,64,128]{2,1,0:T(8,128)(2,1)} %bitcast.11, bf16[16,64,128]{2,1,0:T(8,128)(2,1)} %bitcast.18, bf16[16,64,128]{2,1,0:T(8,128)(2,1)} %bitcast.26, bf16[16,64,128]{2,1,0:T(8,128)(2,1)} %bitcast.23, bf16[16,64,128]{2,1,0:T(8,128)(2,1)} %bitcast.12, ...), custom_call_target="tpu_custom_call" | custom-call | flops 1 | bytes 2228224 | tf_op jit(solution)/shard_map/pallas_call | solution.py:30
  8.6 4.5 %collective-permute-start = (bf16[4,64,128]{2,1,0:T(8,128)(2,1)}, bf16[4,64,128]{2,1,0:T(8,128)(2,1)S(1)}, u32[]{:S(2)}, u32[]{:S(2)}) collective-permute-start(bf16[4,64,128]{2,1,0:T(8,128)(2,1)} %get-tuple-element.31), channel_id=1, source_target_pairs={{0,8},{4,12},{8,16},{12,20},{16,24},{20,28},{1,9},{5,13},{9,17},{1... | collective-permute-start | bytes 196616 | tf_op jit(solution)/shard_map/ppermute | solution.py:52
  13.1 1.9 %collective-permute-start.1 = (bf16[4,64,128]{2,1,0:T(8,128)(2,1)}, bf16[4,64,128]{2,1,0:T(8,128)(2,1)S(1)}, u32[]{:S(2)}, u32[]{:S(2)}) collective-permute-start(bf16[4,64,128]{2,1,0:T(8,128)(2,1)} %get-tuple-element.32), channel_id=1, source_target_pairs={{8,0},{12,4},{16,8},{20,12},{24,16},{28,20},{9,1},{13,5},{17,9},{2... | collective-permute-start | bytes 196616 | tf_op jit(solution)/shard_map/ppermute | solution.py:52
  15.0 3.9 %collective-permute-done.1.high_ref.refs_2_.refs_4_ = bf16[4,64,128]{2,1,0:T(8,128)(2,1)S(1)} collective-permute-done((bf16[4,64,128]{2,1,0:T(8,128)(2,1)}, bf16[4,64,128]{2,1,0:T(8,128)(2,1)S(1)}, u32[]{:S(2)}, u32[]{:S(2)}) %collective-permute-start.1) | collective-permute-done | bytes 65568 | tf_op jit(solution)/shard_map/ppermute | solution.py:52
  18.9 1.4 %collective-permute-start.4 = (bf16[4,64,128]{2,1,0:T(8,128)(2,1)S(1)}, bf16[4,64,128]{2,1,0:T(8,128)(2,1)S(1)}, u32[]{:S(2)}, u32[]{:S(2)}) collective-permute-start(bf16[4,64,128]{2,1,0:T(8,128)(2,1)S(1)} %shard_map.131), channel_id=1, source_target_pairs={{4,0},{12,8},{20,16},{28,24},{5,1},{13,9},{21,17},{29,25},{6,2},{1... | collective-permute-start | bytes 196616 | tf_op jit(solution)/shard_map/ppermute | solution.py:52
  20.4 1.8 %shard_map.130 = (bf16[14,64,128]{2,1,0:T(8,128)(2,1)S(1)}, bf16[16,64,128]{2,1,0:T(8,128)(2,1)S(1)}) custom-call(bf16[16,64,128]{2,1,0:T(8,128)(2,1)S(1)} %bitcast.15, bf16[16,64,128]{2,1,0:T(8,128)(2,1)S(1)} %bitcast.21, bf16[16,64,128]{2,1,0:T(8,128)(2,1)S(1)} %collective-permute-done.2.refs_2_.refs_6_, bf16[3,128,128]{2,1,0:T(8,128)(2,1)S(1)} %copy-done.9, ...), custom_call_target="tpu_custom_call" | custom-call | flops 362387872 | bytes 2162688 | tf_op jit(solution)/shard_map/pallas_call | solution.py:30
  22.2 1.1 %shard_map.136 = (f32[384,128]{1,0:T(8,128)S(1)}, bf16[384,128]{1,0:T(8,128)(2,1)S(1)}, bf16[384,128]{1,0:T(8,128)(2,1)S(1)}, bf16[384,128]{1,0:T(8,128)(2,1)S(1)}) custom-call(bf16[16,64,128]{2,1,0:T(8,128)(2,1)S(1)} %bitcast.28, bf16[16,64,128]{2,1,0:T(8,128)(2,1)S(1)} %bitcast.22, bf16[16,64,128]{2,1,0:T(8,128)(2,1)S(1)} %get-tuple-element.36.refs_4_.refs_2_, ...), custom_call_target="tpu_custom_call" | custom-call | flops 362387872 | bytes 1933312 | tf_op jit(solution)/shard_map/pallas_call | solution.py:30
  23.6 1.9 %collective-permute-start.16 = (bf16[384,128]{1,0:T(8,128)(2,1)S(1)}, bf16[384,128]{1,0:T(8,128)(2,1)S(1)}, u32[]{:S(2)}, u32[]{:S(2)}) collective-permute-start(bf16[384,128]{1,0:T(8,128)(2,1)S(1)} %get-tuple-element.50), channel_id=1, source_target_pairs={{24,0},{16,8},{8,16},{0,24},{25,1},{17,9},{9,17},{1,25},{26,2},{18... | collective-permute-start | bytes 294920 | tf_op jit(solution)/shard_map/ppermute | solution.py:57
  25.5 1.1 %collective-permute-done.4.refs_6_ = bf16[4,64,128]{2,1,0:T(8,128)(2,1)S(1)} collective-permute-done((bf16[4,64,128]{2,1,0:T(8,128)(2,1)S(1)}, bf16[4,64,128]{2,1,0:T(8,128)(2,1)S(1)}, u32[]{:S(2)}, u32[]{:S(2)}) %collective-permute-start.4) | collective-permute-done | bytes 65568 | tf_op jit(solution)/shard_map/ppermute | solution.py:52
  26.6 2.1 %shard_map.132 = (bf16[16,64,128]{2,1,0:T(8,128)(2,1)S(1)}, bf16[16,64,128]{2,1,0:T(8,128)(2,1)S(1)}, bf16[1,64,128]{2,1,0:T(8,128)(2,1)S(1)}, bf16[1,64,128]{2,...) custom-call(bf16[16,64,128]{2,1,0:T(8,128)(2,1)S(1)} %bitcast.17, ...), custom_call_target="tpu_custom_call" | custom-call | flops 452984832 | bytes 3244032 | tf_op jit(solution)/shard_map/pallas_call | solution.py:30
  28.8 1.0 %collective-permute-start.8 = (bf16[384,128]{1,0:T(8,128)(2,1)S(1)}, bf16[384,128]{1,0:T(8,128)(2,1)S(1)}, u32[]{:S(2)}, u32[]{:S(2)}) collective-permute-start(bf16[384,128]{1,0:T(8,128)(2,1)S(1)} %get-tuple-element.43), channel_id=1, source_target_pairs={{16,0},{24,8},{0,16},{8,24},{17,1},{25,9},{1,17},{9,25},{18,2},{26... | collective-permute-start | bytes 294920 | tf_op jit(solution)/shard_map/ppermute | solution.py:57
  29.8 1.1 %collective-permute-start.9 = (bf16[384,128]{1,0:T(8,128)(2,1)S(1)}, bf16[384,128]{1,0:T(8,128)(2,1)S(1)}, u32[]{:S(2)}, u32[]{:S(2)}) collective-permute-start(bf16[384,128]{1,0:T(8,128)(2,1)S(1)} %get-tuple-element.44), channel_id=1, source_target_pairs={{24,0},{16,8},{8,16},{0,24},{25,1},{17,9},{9,17},{1,25},{26,2},{18... | collective-permute-start | bytes 294920 | tf_op jit(solution)/shard_map/ppermute | solution.py:57
  31.0 2.1 %collective-permute-start.17 = (bf16[192,128]{1,0:T(8,128)(2,1)S(1)}, bf16[192,128]{1,0:T(8,128)(2,1)S(1)}, u32[]{:S(2)}, u32[]{:S(2)}) collective-permute-start(bf16[192,128]{1,0:T(8,128)(2,1)S(1)} %get-tuple-element.52), channel_id=1, source_target_pairs={{4,0},{0,4},{5,1},{1,5},{6,2},{2,6},{7,3},{3,7},{12,8},{8,12},{13,... | collective-permute-start | bytes 147464 | tf_op jit(solution)/shard_map/ppermute | solution.py:57
  33.1 2.4 %collective-permute-done.9.refs_2_ = bf16[384,128]{1,0:T(8,128)(2,1)S(1)} collective-permute-done((bf16[384,128]{1,0:T(8,128)(2,1)S(1)}, bf16[384,128]{1,0:T(8,128)(2,1)S(1)}, u32[]{:S(2)}, u32[]{:S(2)}) %collective-permute-start.9) | collective-permute-done | bytes 98336 | tf_op jit(solution)/shard_map/ppermute | solution.py:57
  35.5 1.9 %collective-permute-start.10 = (bf16[192,128]{1,0:T(8,128)(2,1)S(1)}, bf16[192,128]{1,0:T(8,128)(2,1)S(1)}, u32[]{:S(2)}, u32[]{:S(2)}) collective-permute-start(bf16[192,128]{1,0:T(8,128)(2,1)S(1)} %get-tuple-element.46), channel_id=1, source_target_pairs={{4,0},{0,4},{5,1},{1,5},{6,2},{2,6},{7,3},{3,7},{12,8},{8,12},{13,... | collective-permute-start | bytes 147464 | tf_op jit(solution)/shard_map/ppermute | solution.py:57
  37.4 3.4 %collective-permute-start.20 = (bf16[192,128]{1,0:T(8,128)(2,1)S(1)}, bf16[192,128]{1,0:T(8,128)(2,1)S(1)}, u32[]{:S(2)}, u32[]{:S(2)}) collective-permute-start(bf16[192,128]{1,0:T(8,128)(2,1)S(1)} %shard_map.138.refs_4_), channel_id=1, source_target_pairs={{3,0},{2,1},{1,2},{0,3},{7,4},{6,5},{5,6},{4,7},{11,8},{10,9},{9,1... | collective-permute-start | bytes 147464 | tf_op jit(solution)/shard_map/ppermute | solution.py:57
  41.2 3.3 %collective-permute-start.13 = (bf16[192,128]{1,0:T(8,128)(2,1)S(1)}, bf16[192,128]{1,0:T(8,128)(2,1)S(1)}, u32[]{:S(2)}, u32[]{:S(2)}) collective-permute-start(bf16[192,128]{1,0:T(8,128)(2,1)S(1)} %shard_map.135.refs_0_), channel_id=1, source_target_pairs={{3,0},{2,1},{1,2},{0,3},{7,4},{6,5},{5,6},{4,7},{11,8},{10,9},{9,1... | collective-permute-start | bytes 147464 | tf_op jit(solution)/shard_map/ppermute | solution.py:57
  45.3 1.1 %collective-permute-done.13.refs_3_ = bf16[192,128]{1,0:T(8,128)(2,1)S(1)} collective-permute-done((bf16[192,128]{1,0:T(8,128)(2,1)S(1)}, bf16[192,128]{1,0:T(8,128)(2,1)S(1)}, u32[]{:S(2)}, u32[]{:S(2)}) %collective-permute-start.13) | collective-permute-done | bytes 49184 | tf_op jit(solution)/shard_map/ppermute | solution.py:57
  46.5 2.8 %collective-permute-done.12.refs_2_ = bf16[192,128]{1,0:T(8,128)(2,1)S(1)} collective-permute-done((bf16[192,128]{1,0:T(8,128)(2,1)S(1)}, bf16[192,128]{1,0:T(8,128)(2,1)S(1)}, u32[]{:S(2)}, u32[]{:S(2)}) %collective-permute-start.12) | collective-permute-done | bytes 49184 | tf_op jit(solution)/shard_map/ppermute | solution.py:57
  49.5 3.5 %collective-permute-done.21.other_ref = bf16[2,192,128]{2,1,0:T(8,128)(2,1)S(1)} collective-permute-done((bf16[2,192,128]{2,1,0:T(8,128)(2,1)S(1)}, bf16[2,192,128]{2,1,0:T(8,128)(2,1)S(1)}, u32[]{:S(2)}, u32[]{:S(2)}) %collective-permute-start.21) | collective-permute-done | bytes 98336 | tf_op jit(solution)/shard_map/ppermute | solution.py:57
  53.4 3.3 %collective-permute-start.22 = (bf16[2,2,192,128]{3,2,1,0:T(8,128)(2,1)S(1)}, bf16[2,2,192,128]{3,2,1,0:T(8,128)(2,1)S(1)}, u32[]{:S(2)}, u32[]{:S(2)}) collective-permute-start(bf16[2,2,192,128]{3,2,1,0:T(8,128)(2,1)S(1)} %shard_map.140.refs_0_), channel_id=1, source_target_pairs={{8,0},{0,8},{24,16},{16,24},{9,1},{1,9},{25,17},{17,25},{10,2},{2,... | collective-permute-start | bytes 589832 | tf_op jit(solution)/shard_map/ppermute | solution.py:57
  57.5 3.8 %collective-permute-start.24 = (bf16[2,2,192,128]{3,2,1,0:T(8,128)(2,1)S(1)}, bf16[2,2,192,128]{3,2,1,0:T(8,128)(2,1)S(1)}, u32[]{:S(2)}, u32[]{:S(2)}) collective-permute-start(bf16[2,2,192,128]{3,2,1,0:T(8,128)(2,1)S(1)} %collective-permute-done.23.refs_2_), channel_id=1, source_target_pairs={{8,0},{0,8},{24,16},{16,24},{9,1},{1,9},{25,17},{17,25},{10,2},{2,... | collective-permute-start | bytes 589832 | tf_op jit(solution)/shard_map/ppermute | solution.py:57
  61.3 2.5 %collective-permute-start.5 = (bf16[1,64,128]{2,1,0:T(8,128)(2,1)S(1)}, bf16[1,64,128]{2,1,0:T(8,128)(2,1)S(1)}, u32[]{:S(2)}, u32[]{:S(2)}) collective-permute-start(bf16[1,64,128]{2,1,0:T(8,128)(2,1)S(1)} %get-tuple-element.39), channel_id=1, source_target_pairs={{0,8},{4,12},{8,16},{12,20},{16,24},{20,28},{1,9},{5,13},{9,17},{1... | collective-permute-start | bytes 49160 | tf_op jit(solution)/shard_map/ppermute | solution.py:52
  63.8 1.9 %collective-permute-start.6 = (bf16[1,64,128]{2,1,0:T(8,128)(2,1)S(1)}, bf16[1,64,128]{2,1,0:T(8,128)(2,1)S(1)}, u32[]{:S(2)}, u32[]{:S(2)}) collective-permute-start(bf16[1,64,128]{2,1,0:T(8,128)(2,1)S(1)} %get-tuple-element.40), channel_id=1, source_target_pairs={{8,0},{12,4},{16,8},{20,12},{24,16},{28,20},{9,1},{13,5},{17,9},{2... | collective-permute-start | bytes 49160 | tf_op jit(solution)/shard_map/ppermute | solution.py:52
  65.8 3.1 %collective-permute-done.6.below_ref = bf16[1,64,128]{2,1,0:T(8,128)(2,1)S(1)} collective-permute-done((bf16[1,64,128]{2,1,0:T(8,128)(2,1)S(1)}, bf16[1,64,128]{2,1,0:T(8,128)(2,1)S(1)}, u32[]{:S(2)}, u32[]{:S(2)}) %collective-permute-start.6) | collective-permute-done | bytes 16416 | tf_op jit(solution)/shard_map/ppermute | solution.py:52
  68.9 2.2 %shard_map.133 = bf16[16,64,128]{2,1,0:T(8,128)(2,1)} custom-call(bf16[16,64,128]{2,1,0:T(8,128)(2,1)S(1)} %get-tuple-element.37.mid_ref, bf16[16,64,128]{2,1,0:T(8,128)(2,1)S(1)} %get-tuple-element.38.gpre_ref, bf16[1,64,128]{2,1,0:T(8,128)(2,1)S(1)} %collective-permute-done.5.above_ref, bf16[1,64,128]{2,1,0:T(8,128)(2,1)S(1)} %collective-permute-done.6.below_ref, ...), custom_call_target="tpu_custom_call" | custom-call | flops 301989888 | bytes 1114112 | tf_op jit(solution)/shard_map/pallas_call | solution.py:30
  71.1 1.3 %shard_map.141 = (f32[3,384,128]{2,1,0:T(8,128)}, f32[384,128]{1,0:T(8,128)}, f32[3,384,128]{2,1,0:T(8,128)}, f32[384,128]{1,0:T(8,128)}) custom-call(bf16[2,2,192,128]{3,2,1,0:T(8,128)(2,1)S(1)} %shard_map.140.refs_0_, bf16[2,2,192,128]{3,2,1,0:T(8,128)(2,1)S(1)} %collective-permute-done.22.refs_1_, ...), custom_call_target="tpu_custom_call" | custom-call | flops 98304 | bytes 2359296 | tf_op jit(solution)/shard_map/pallas_call | solution.py:30
  (58 shorter events, 4.2 us)
Async XLA Ops:
  0.6 19.7 %collective-permute-start.2 = (bf16[16,64,128]{2,1,0:T(8,128)(2,1)}, bf16[16,64,128]{2,1,0:T(8,128)(2,1)S(1)}, u32[]{:S(2)}, u32[]{:S(2)}) collective-permute-start(bf16[16,64,128]{2,1,0:T(8,128)(2,1)} %bitcast.10), channel_id=1, source_target_pairs={{4,0},{12,8},{20,16},{28,24},{5,1},{13,9},{21,17},{29,25},{6,2},{1... | collective-permute-start | bytes 786440 | tf_op jit(solution)/shard_map/ppermute | solution.py:52
  5.7 20.9 %collective-permute-start.3 = (bf16[14,64,128]{2,1,0:T(8,128)(2,1)S(1)}, bf16[14,64,128]{2,1,0:T(8,128)(2,1)S(1)}, u32[]{:S(2)}, u32[]{:S(2)}) collective-permute-start(bf16[14,64,128]{2,1,0:T(8,128)(2,1)S(1)} %get-tuple-element.33.refs_5_), channel_id=1, source_target_pairs={{4,0},{12,8},{20,16},{28,24},{5,1},{13,9},{21,17},{29,25},{6,2},{1... | collective-permute-start | bytes 688136 | tf_op jit(solution)/shard_map/ppermute | solution.py:52
  7.0 11.9 %copy-start.1 = (bf16[1,1,16,64,128]{4,3,2,1,0:T(8,128)(2,1)S(1)}, bf16[1,1,16,64,128]{4,3,2,1,0:T(8,128)(2,1)}, u32[]{:S(2)}) copy-start(bf16[1,1,16,64,128]{4,3,2,1,0:T(8,128)(2,1)} %param.9) | copy-start | bytes 786436
  7.0 11.9 %copy-start.5 = (bf16[3,3,128,128]{3,2,1,0:T(8,128)(2,1)S(1)}, bf16[3,3,128,128]{3,2,1,0:T(8,128)(2,1)}, u32[]{:S(2)}) copy-start(bf16[3,3,128,128]{3,2,1,0:T(8,128)(2,1)} %refs_8_.1) | copy-start | bytes 884740
  7.0 11.9 %copy-start.9 = (bf16[3,128,128]{2,1,0:T(8,128)(2,1)S(1)}, bf16[3,128,128]{2,1,0:T(8,128)(2,1)}, u32[]{:S(2)}) copy-start(bf16[3,128,128]{2,1,0:T(8,128)(2,1)} %refs_7_.1) | copy-start | bytes 294916
  8.6 6.5 %collective-permute-start = (bf16[4,64,128]{2,1,0:T(8,128)(2,1)}, bf16[4,64,128]{2,1,0:T(8,128)(2,1)S(1)}, u32[]{:S(2)}, u32[]{:S(2)}) collective-permute-start(bf16[4,64,128]{2,1,0:T(8,128)(2,1)} %get-tuple-element.31), channel_id=1, source_target_pairs={{0,8},{4,12},{8,16},{12,20},{16,24},{20,28},{1,9},{5,13},{9,17},{1... | collective-permute-start | bytes 196616 | tf_op jit(solution)/shard_map/ppermute | solution.py:52
  13.1 5.8 %collective-permute-start.1 = (bf16[4,64,128]{2,1,0:T(8,128)(2,1)}, bf16[4,64,128]{2,1,0:T(8,128)(2,1)S(1)}, u32[]{:S(2)}, u32[]{:S(2)}) collective-permute-start(bf16[4,64,128]{2,1,0:T(8,128)(2,1)} %get-tuple-element.32), channel_id=1, source_target_pairs={{8,0},{12,4},{16,8},{20,12},{24,16},{28,20},{9,1},{13,5},{17,9},{2... | collective-permute-start | bytes 196616 | tf_op jit(solution)/shard_map/ppermute | solution.py:52
  18.9 7.7 %collective-permute-start.4 = (bf16[4,64,128]{2,1,0:T(8,128)(2,1)S(1)}, bf16[4,64,128]{2,1,0:T(8,128)(2,1)S(1)}, u32[]{:S(2)}, u32[]{:S(2)}) collective-permute-start(bf16[4,64,128]{2,1,0:T(8,128)(2,1)S(1)} %shard_map.131), channel_id=1, source_target_pairs={{4,0},{12,8},{20,16},{28,24},{5,1},{13,9},{21,17},{29,25},{6,2},{1... | collective-permute-start | bytes 196616 | tf_op jit(solution)/shard_map/ppermute | solution.py:52
  22.2 4.4 %copy-start.6 = (bf16[1,1,16,64,128]{4,3,2,1,0:T(8,128)(2,1)S(1)}, bf16[1,1,16,64,128]{4,3,2,1,0:T(8,128)(2,1)}, u32[]{:S(2)}) copy-start(bf16[1,1,16,64,128]{4,3,2,1,0:T(8,128)(2,1)} %param.10) | copy-start | bytes 786436
  22.2 4.4 %copy-start.10 = (bf16[1,1,16,64,128]{4,3,2,1,0:T(8,128)(2,1)S(1)}, bf16[1,1,16,64,128]{4,3,2,1,0:T(8,128)(2,1)}, u32[]{:S(2)}) copy-start(bf16[1,1,16,64,128]{4,3,2,1,0:T(8,128)(2,1)} %param.11) | copy-start | bytes 786436
  22.2 4.4 %copy-start.11 = (bf16[3,128,128]{2,1,0:T(8,128)(2,1)S(1)}, bf16[3,128,128]{2,1,0:T(8,128)(2,1)}, u32[]{:S(2)}) copy-start(bf16[3,128,128]{2,1,0:T(8,128)(2,1)} %refs_11_.1) | copy-start | bytes 294916
  23.3 6.5 %collective-permute-start.14 = (bf16[384,128]{1,0:T(8,128)(2,1)S(1)}, bf16[384,128]{1,0:T(8,128)(2,1)S(1)}, u32[]{:S(2)}, u32[]{:S(2)}) collective-permute-start(bf16[384,128]{1,0:T(8,128)(2,1)S(1)} %get-tuple-element.48), channel_id=1, source_target_pairs={{8,0},{0,8},{24,16},{16,24},{9,1},{1,9},{25,17},{17,25},{10,2},{2,... | collective-permute-start | bytes 294920 | tf_op jit(solution)/shard_map/ppermute | solution.py:57
  23.4 7.5 %collective-permute-start.15 = (bf16[384,128]{1,0:T(8,128)(2,1)S(1)}, bf16[384,128]{1,0:T(8,128)(2,1)S(1)}, u32[]{:S(2)}, u32[]{:S(2)}) collective-permute-start(bf16[384,128]{1,0:T(8,128)(2,1)S(1)} %get-tuple-element.49), channel_id=1, source_target_pairs={{16,0},{24,8},{0,16},{8,24},{17,1},{25,9},{1,17},{9,25},{18,2},{26... | collective-permute-start | bytes 294920 | tf_op jit(solution)/shard_map/ppermute | solution.py:57
  23.6 7.4 %collective-permute-start.16 = (bf16[384,128]{1,0:T(8,128)(2,1)S(1)}, bf16[384,128]{1,0:T(8,128)(2,1)S(1)}, u32[]{:S(2)}, u32[]{:S(2)}) collective-permute-start(bf16[384,128]{1,0:T(8,128)(2,1)S(1)} %get-tuple-element.50), channel_id=1, source_target_pairs={{24,0},{16,8},{8,16},{0,24},{25,1},{17,9},{9,17},{1,25},{26,2},{18... | collective-permute-start | bytes 294920 | tf_op jit(solution)/shard_map/ppermute | solution.py:57
  28.7 4.4 %collective-permute-start.7 = (bf16[384,128]{1,0:T(8,128)(2,1)S(1)}, bf16[384,128]{1,0:T(8,128)(2,1)S(1)}, u32[]{:S(2)}, u32[]{:S(2)}) collective-permute-start(bf16[384,128]{1,0:T(8,128)(2,1)S(1)} %get-tuple-element.42), channel_id=1, source_target_pairs={{8,0},{0,8},{24,16},{16,24},{9,1},{1,9},{25,17},{17,25},{10,2},{2,... | collective-permute-start | bytes 294920 | tf_op jit(solution)/shard_map/ppermute | solution.py:57
  28.8 4.3 %collective-permute-start.8 = (bf16[384,128]{1,0:T(8,128)(2,1)S(1)}, bf16[384,128]{1,0:T(8,128)(2,1)S(1)}, u32[]{:S(2)}, u32[]{:S(2)}) collective-permute-start(bf16[384,128]{1,0:T(8,128)(2,1)S(1)} %get-tuple-element.43), channel_id=1, source_target_pairs={{16,0},{24,8},{0,16},{8,24},{17,1},{25,9},{1,17},{9,25},{18,2},{26... | collective-permute-start | bytes 294920 | tf_op jit(solution)/shard_map/ppermute | solution.py:57
  29.8 5.6 %collective-permute-start.9 = (bf16[384,128]{1,0:T(8,128)(2,1)S(1)}, bf16[384,128]{1,0:T(8,128)(2,1)S(1)}, u32[]{:S(2)}, u32[]{:S(2)}) collective-permute-start(bf16[384,128]{1,0:T(8,128)(2,1)S(1)} %get-tuple-element.44), channel_id=1, source_target_pairs={{24,0},{16,8},{8,16},{0,24},{25,1},{17,9},{9,17},{1,25},{26,2},{18... | collective-permute-start | bytes 294920 | tf_op jit(solution)/shard_map/ppermute | solution.py:57
  31.0 6.4 %collective-permute-start.17 = (bf16[192,128]{1,0:T(8,128)(2,1)S(1)}, bf16[192,128]{1,0:T(8,128)(2,1)S(1)}, u32[]{:S(2)}, u32[]{:S(2)}) collective-permute-start(bf16[192,128]{1,0:T(8,128)(2,1)S(1)} %get-tuple-element.52), channel_id=1, source_target_pairs={{4,0},{0,4},{5,1},{1,5},{6,2},{2,6},{7,3},{3,7},{12,8},{8,12},{13,... | collective-permute-start | bytes 147464 | tf_op jit(solution)/shard_map/ppermute | solution.py:57
  35.5 5.6 %collective-permute-start.10 = (bf16[192,128]{1,0:T(8,128)(2,1)S(1)}, bf16[192,128]{1,0:T(8,128)(2,1)S(1)}, u32[]{:S(2)}, u32[]{:S(2)}) collective-permute-start(bf16[192,128]{1,0:T(8,128)(2,1)S(1)} %get-tuple-element.46), channel_id=1, source_target_pairs={{4,0},{0,4},{5,1},{1,5},{6,2},{2,6},{7,3},{3,7},{12,8},{8,12},{13,... | collective-permute-start | bytes 147464 | tf_op jit(solution)/shard_map/ppermute | solution.py:57
  37.4 7.0 %collective-permute-start.20 = (bf16[192,128]{1,0:T(8,128)(2,1)S(1)}, bf16[192,128]{1,0:T(8,128)(2,1)S(1)}, u32[]{:S(2)}, u32[]{:S(2)}) collective-permute-start(bf16[192,128]{1,0:T(8,128)(2,1)S(1)} %shard_map.138.refs_4_), channel_id=1, source_target_pairs={{3,0},{2,1},{1,2},{0,3},{7,4},{6,5},{5,6},{4,7},{11,8},{10,9},{9,1... | collective-permute-start | bytes 147464 | tf_op jit(solution)/shard_map/ppermute | solution.py:57
  40.8 4.5 %collective-permute-start.19 = (bf16[192,128]{1,0:T(8,128)(2,1)S(1)}, bf16[192,128]{1,0:T(8,128)(2,1)S(1)}, u32[]{:S(2)}, u32[]{:S(2)}) collective-permute-start(bf16[192,128]{1,0:T(8,128)(2,1)S(1)} %shard_map.138.refs_4_), channel_id=1, source_target_pairs={{2,0},{3,1},{0,2},{1,3},{6,4},{7,5},{4,6},{5,7},{10,8},{11,9},{8,1... | collective-permute-start | bytes 147464 | tf_op jit(solution)/shard_map/ppermute | solution.py:57
  40.8 4.5 %collective-permute-start.18 = (bf16[192,128]{1,0:T(8,128)(2,1)S(1)}, bf16[192,128]{1,0:T(8,128)(2,1)S(1)}, u32[]{:S(2)}, u32[]{:S(2)}) collective-permute-start(bf16[192,128]{1,0:T(8,128)(2,1)S(1)} %shard_map.138.refs_4_), channel_id=1, source_target_pairs={{1,0},{0,1},{3,2},{2,3},{5,4},{4,5},{7,6},{6,7},{9,8},{8,9},{11,10... | collective-permute-start | bytes 147464 | tf_op jit(solution)/shard_map/ppermute | solution.py:57
  41.2 5.3 %collective-permute-start.13 = (bf16[192,128]{1,0:T(8,128)(2,1)S(1)}, bf16[192,128]{1,0:T(8,128)(2,1)S(1)}, u32[]{:S(2)}, u32[]{:S(2)}) collective-permute-start(bf16[192,128]{1,0:T(8,128)(2,1)S(1)} %shard_map.135.refs_0_), channel_id=1, source_target_pairs={{3,0},{2,1},{1,2},{0,3},{7,4},{6,5},{5,6},{4,7},{11,8},{10,9},{9,1... | collective-permute-start | bytes 147464 | tf_op jit(solution)/shard_map/ppermute | solution.py:57
  44.4 4.9 %collective-permute-start.12 = (bf16[192,128]{1,0:T(8,128)(2,1)S(1)}, bf16[192,128]{1,0:T(8,128)(2,1)S(1)}, u32[]{:S(2)}, u32[]{:S(2)}) collective-permute-start(bf16[192,128]{1,0:T(8,128)(2,1)S(1)} %shard_map.135.refs_0_), channel_id=1, source_target_pairs={{2,0},{3,1},{0,2},{1,3},{6,4},{7,5},{4,6},{5,7},{10,8},{11,9},{8,1... | collective-permute-start | bytes 147464 | tf_op jit(solution)/shard_map/ppermute | solution.py:57
  44.5 4.9 %collective-permute-start.11 = (bf16[192,128]{1,0:T(8,128)(2,1)S(1)}, bf16[192,128]{1,0:T(8,128)(2,1)S(1)}, u32[]{:S(2)}, u32[]{:S(2)}) collective-permute-start(bf16[192,128]{1,0:T(8,128)(2,1)S(1)} %shard_map.135.refs_0_), channel_id=1, source_target_pairs={{1,0},{0,1},{3,2},{2,3},{5,4},{4,5},{7,6},{6,7},{9,8},{8,9},{11,10... | collective-permute-start | bytes 147464 | tf_op jit(solution)/shard_map/ppermute | solution.py:57
  49.4 19.5 %copy-start.12 = (bf16[3,3,128,128]{3,2,1,0:T(8,128)(2,1)S(1)}, bf16[3,3,128,128]{3,2,1,0:T(8,128)(2,1)}, u32[]{:S(2)}) copy-start(bf16[3,3,128,128]{3,2,1,0:T(8,128)(2,1)} %spatial_ref.5) | copy-start | bytes 884740
  49.4 3.5 %collective-permute-start.21 = (bf16[2,192,128]{2,1,0:T(8,128)(2,1)S(1)}, bf16[2,192,128]{2,1,0:T(8,128)(2,1)S(1)}, u32[]{:S(2)}, u32[]{:S(2)}) collective-permute-start(bf16[2,192,128]{2,1,0:T(8,128)(2,1)S(1)} %shard_map.139.own_ref), channel_id=1, source_target_pairs={{4,0},{0,4},{5,1},{1,5},{6,2},{2,6},{7,3},{3,7},{12,8},{8,12},{13,... | collective-permute-start | bytes 294920 | tf_op jit(solution)/shard_map/ppermute | solution.py:57
  52.9 4.6 %collective-permute-start.23 = (bf16[2,2,192,128]{3,2,1,0:T(8,128)(2,1)S(1)}, bf16[2,2,192,128]{3,2,1,0:T(8,128)(2,1)S(1)}, u32[]{:S(2)}, u32[]{:S(2)}) collective-permute-start(bf16[2,2,192,128]{3,2,1,0:T(8,128)(2,1)S(1)} %shard_map.140.refs_0_), channel_id=1, source_target_pairs={{16,0},{24,8},{0,16},{8,24},{17,1},{25,9},{1,17},{9,25},{18,2},{26... | collective-permute-start | bytes 589832 | tf_op jit(solution)/shard_map/ppermute | solution.py:57
  53.4 17.7 %collective-permute-start.22 = (bf16[2,2,192,128]{3,2,1,0:T(8,128)(2,1)S(1)}, bf16[2,2,192,128]{3,2,1,0:T(8,128)(2,1)S(1)}, u32[]{:S(2)}, u32[]{:S(2)}) collective-permute-start(bf16[2,2,192,128]{3,2,1,0:T(8,128)(2,1)S(1)} %shard_map.140.refs_0_), channel_id=1, source_target_pairs={{8,0},{0,8},{24,16},{16,24},{9,1},{1,9},{25,17},{17,25},{10,2},{2,... | collective-permute-start | bytes 589832 | tf_op jit(solution)/shard_map/ppermute | solution.py:57
  57.5 13.6 %collective-permute-start.24 = (bf16[2,2,192,128]{3,2,1,0:T(8,128)(2,1)S(1)}, bf16[2,2,192,128]{3,2,1,0:T(8,128)(2,1)S(1)}, u32[]{:S(2)}, u32[]{:S(2)}) collective-permute-start(bf16[2,2,192,128]{3,2,1,0:T(8,128)(2,1)S(1)} %collective-permute-done.23.refs_2_), channel_id=1, source_target_pairs={{8,0},{0,8},{24,16},{16,24},{9,1},{1,9},{25,17},{17,25},{10,2},{2,... | collective-permute-start | bytes 589832 | tf_op jit(solution)/shard_map/ppermute | solution.py:57
  61.3 4.5 %collective-permute-start.5 = (bf16[1,64,128]{2,1,0:T(8,128)(2,1)S(1)}, bf16[1,64,128]{2,1,0:T(8,128)(2,1)S(1)}, u32[]{:S(2)}, u32[]{:S(2)}) collective-permute-start(bf16[1,64,128]{2,1,0:T(8,128)(2,1)S(1)} %get-tuple-element.39), channel_id=1, source_target_pairs={{0,8},{4,12},{8,16},{12,20},{16,24},{20,28},{1,9},{5,13},{9,17},{1... | collective-permute-start | bytes 49160 | tf_op jit(solution)/shard_map/ppermute | solution.py:52
  63.8 5.1 %collective-permute-start.6 = (bf16[1,64,128]{2,1,0:T(8,128)(2,1)S(1)}, bf16[1,64,128]{2,1,0:T(8,128)(2,1)S(1)}, u32[]{:S(2)}, u32[]{:S(2)}) collective-permute-start(bf16[1,64,128]{2,1,0:T(8,128)(2,1)S(1)} %get-tuple-element.40), channel_id=1, source_target_pairs={{8,0},{12,4},{16,8},{20,12},{24,16},{28,20},{9,1},{13,5},{17,9},{2... | collective-permute-start | bytes 49160 | tf_op jit(solution)/shard_map/ppermute | solution.py:52
  (6 other events, 8.5 us)

commit v4 on v3

--- a/solution.py
+++ b/solution.py
@@ -23,16 +23,23 @@
     return jax.ShapeDtypeStruct(shape, jnp.float32)
 
 
-def call(kernel, outs, scratch, flops, *operands, grid=(), in_specs=None, limit=24):
+def call(kernel, outs, scratch, flops, *operands, after=(), whole=False, limit=24):
     single = len(outs) == 1
     moved = sum(math.prod(x.shape) * x.dtype.itemsize for x in (*operands, *outs))
     vmem = pl.BlockSpec(memory_space=pltpu.VMEM)
+    spare = pl.BlockSpec(memory_space=pl.ANY)
+    spec = spare if whole else vmem
+    count = len(operands)
+    operands = (*operands, *after)
+
+    def body(*refs):
+        kernel(*refs[:count], *refs[len(operands) :])
+
     return pl.pallas_call(
-        kernel,
+        body,
         out_shape=outs[0] if single else tuple(outs),
-        grid=grid,
-        in_specs=in_specs or [vmem] * len(operands),
-        out_specs=vmem if single else (vmem,) * len(outs),
+        in_specs=[spec] * count + [spare] * len(after),
+        out_specs=spec if single else (spec,) * len(outs),
         scratch_shapes=scratch,
         compiler_params=pltpu.CompilerParams(vmem_limit_bytes=limit * MIB),
         cost_estimate=pl.CostEstimate(
@@ -50,6 +57,18 @@
         if 0 <= band + band_step < bands and frame + frame_step < frames
     ]
     return lax.ppermute(block, ("section", "video"), pairs)
+
+
+def paired(block, start):
+    bands = lax.axis_size("section")
+    pairs = [(band, band + 1) for band in range(start, bands - 1, 2)]
+    return lax.ppermute(block, "section", pairs + [(right, left) for left, right in pairs])
+
+
+def beside_band(pair_refs, row):
+    odd = lax.rem(lax.axis_index("section"), 2) == 1
+    first, second = (ref[row : row + 1] for ref in pair_refs)
+    return jnp.where(odd, first, second), jnp.where(odd, second, first)
 
 
 def flipped(block, axis, flip):
@@ -127,10 +146,20 @@
 
 
 def pack_kernel(*refs):
-    parts, (up_ref, down_ref) = refs[:8], refs[8:]
-    for n in range(4):
-        up_ref[n : n + 1] = parts[n][...]
-        down_ref[n : n + 1] = parts[n + 4][...]
+    parts, outs, sems = refs[:4], refs[4:6], refs[6]
+    last = parts[0].shape[0] - 1
+    odd = lax.rem(lax.axis_index("section"), 2)
+    copies = []
+    for n, part in enumerate(parts):
+        for out, row in zip(outs, ((1 - odd) * last, odd * last)):
+            sem = sems.at[len(copies)]
+            copies.append(
+                pltpu.make_async_copy(part.at[pl.ds(row, 1)], out.at[pl.ds(n, 1)], sem)
+            )
+    for copy in copies:
+        copy.start()
+    for copy in copies:
+        copy.wait()
 
 
 def interior(grad_ref, preact_ref, wholes, temporal_ref, spatial_ref, inner_ref, gpre_ref, views_ref):
@@ -153,14 +182,15 @@
         inner_ref[pl.ds(n * half, half)] = convolved(views_ref, spatial_ref, n * half, first)
 
 
-def edge_rows(grad_ref, low_ref, high_ref, afters, gpre_ref, temporal_ref, spatial_ref, views_ref):
+def edge_rows(grad_ref, pair_refs, afters, gpre_ref, temporal_ref, spatial_ref, views_ref):
     rows, cols, ch = grad_ref.shape
-    above = [low_ref[0:1]] + [ref[2:3] for ref in afters]
-    below = [high_ref[0:1]] + [ref[3:4] for ref in afters]
-    beside(pre_gradient(above, low_ref[1:2], temporal_ref), views_ref, 0)
+    (grad_above, grad_below), (above_pre, below_pre) = (beside_band(pair_refs, n) for n in (0, 1))
+    above = [grad_above] + [ref[2:3] for ref in afters]
+    below = [grad_below] + [ref[3:4] for ref in afters]
+    beside(pre_gradient(above, above_pre, temporal_ref), views_ref, 0)
     beside(gpre_ref[0:2].astype(jnp.float32), views_ref, 1)
     beside(gpre_ref[rows - 2 : rows].astype(jnp.float32), views_ref, 3)
-    beside(pre_gradient(below, high_ref[1:2], temporal_ref), views_ref, 5)
+    beside(pre_gradient(below, below_pre, temporal_ref), views_ref, 5)
     return (
         convolved(views_ref, spatial_ref, 0, grad_ref[0:1]),
         convolved(views_ref, spatial_ref, 3, grad_ref[rows - 1 : rows]),
@@ -179,13 +209,12 @@
     )
 
 
-def last_edge_kernel(grad_ref, low_ref, high_ref, gpre_ref, temporal_ref, spatial_ref, edge_ref, views_ref):
+def last_edge_kernel(grad_ref, one_ref, two_ref, gpre_ref, temporal_ref, spatial_ref, edge_ref, views_ref):
     def body():
         edge_ref[0:1], edge_ref[1:2] = edge_rows(
-            grad_ref, low_ref, high_ref, [], gpre_ref, temporal_ref, spatial_ref, views_ref
-        )
-        edge_ref[2:3] = low_ref[0:1]
-        edge_ref[3:4] = high_ref[0:1]
+            grad_ref, (one_ref, two_ref), [], gpre_ref, temporal_ref, spatial_ref, views_ref
+        )
+        edge_ref[2:3], edge_ref[3:4] = beside_band((one_ref, two_ref), 0)
 
     on_last(body)
 
@@ -209,18 +238,19 @@
 
 
 def mid_kernel(later, *refs):
-    grad_ref, low_ref, high_ref, inner_ref, gpre_ref = refs[:5]
+    grad_ref, inner_ref, gpre_ref = refs[0], refs[3], refs[4]
     afters, (temporal_ref, spatial_ref, mid_ref, views_ref) = refs[5 : 5 + later], refs[5 + later :]
     rows = grad_ref.shape[0]
     first, last = edge_rows(
-        grad_ref, low_ref, high_ref, afters, gpre_ref, temporal_ref, spatial_ref, views_ref
+        grad_ref, refs[1:3], afters, gpre_ref, temporal_ref, spatial_ref, views_ref
     )
     mid_ref[0:1], mid_ref[rows - 1 : rows] = first, last
     mid_ref[1 : rows - 1] = inner_ref[...]
 
 
 def two_kernel(later, *refs):
-    saved_ref, preact_ref, gpre_ref, low_ref, high_ref, grad_ref = refs[:6]
+    saved_ref, preact_ref, gpre_ref = refs[:3]
+    pair_refs, grad_ref = refs[3:5], refs[5]
     wholes, outs = refs[6 : 6 + later], refs[6 + later : 10 + later]
     views_ref, act_ref, sums_ref = refs[10 + later :]
     rows, cols, ch = saved_ref.shape
@@ -235,12 +265,13 @@
 
     views = views_ref[...].reshape(rows * cols, 3 * ch)
     grads = [ref[...] for ref in (grad_ref, *wholes)]
-    kernel_sums(saved_ref, low_ref[2:3], high_ref[2:3], act_ref[...], grads, views, sums_ref)
+    above, below = beside_band(pair_refs, 2)
+    kernel_sums(saved_ref, above, below, act_ref[...], grads, views, sums_ref)
     hand_out(sums_ref, outs)
 
 
-def block_one(saved_ref, preact_ref, low_ref, high_ref, mids, temporal_ref, outs, scratch):
-    gpre_ref, first_ref, last_ref = outs[:3]
+def block_one(saved_ref, preact_ref, pair_refs, mids, temporal_ref, outs, scratch):
+    gpre_ref, edge_refs = outs[0], outs[1:3]
     views_ref, act_ref, sums_ref = scratch
     rows, cols, ch = saved_ref.shape
     step = 4
@@ -254,36 +285,32 @@
         hval = preact_ref[here].astype(jnp.float32)
         act_ref[here] = (hval * sigmoid(hval)).astype(jnp.bfloat16)
 
-    first_ref[...] = gpre_ref[0:1]
-    last_ref[...] = gpre_ref[rows - 1 : rows]
+    odd = lax.rem(lax.axis_index("section"), 2)
+    edge_refs[0][...] = gpre_ref[pl.ds((1 - odd) * (rows - 1), 1)]
+    edge_refs[1][...] = gpre_ref[pl.ds(odd * (rows - 1), 1)]
     views = views_ref[...].reshape(rows * cols, 3 * ch)
     grads = [ref[...] for ref in mids]
-    kernel_sums(saved_ref, low_ref[3:4], high_ref[3:4], act_ref[...], grads, views, sums_ref)
+    above, below = beside_band(pair_refs, 3)
+    kernel_sums(saved_ref, above, below, act_ref[...], grads, views, sums_ref)
     hand_out(sums_ref, outs[3:])
 
 
 def one_kernel(later, *refs):
-    saved_ref, preact_ref, low_ref, high_ref, mid_ref = refs[:5]
+    saved_ref, preact_ref, mid_ref = refs[0], refs[1], refs[4]
     nexts, temporal_ref = refs[5 : 5 + later], refs[5 + later]
     outs, scratch = refs[6 + later : 13 + later], refs[13 + later :]
-    block_one(
-        saved_ref, preact_ref, low_ref, high_ref, [mid_ref, *nexts], temporal_ref, outs, scratch
-    )
+    block_one(saved_ref, preact_ref, refs[2:4], [mid_ref, *nexts], temporal_ref, outs, scratch)
 
 
 def mid_one_kernel(*refs):
-    grad_ref, low_ref, high_ref, inner_ref, gpre_two_ref, after_inner_ref, after_edge_ref = refs[:7]
+    grad_ref, pair_refs, (after_inner_ref, after_edge_ref) = refs[0], refs[1:3], refs[5:7]
     temporal_two_ref, spatial_two_ref, saved_ref, preact_ref, temporal_ref = refs[7:12]
     mid_ref, outs, scratch = refs[12], refs[13:20], refs[20:23]
     next_ref, edge_views_ref = refs[23:]
     rows = grad_ref.shape[0]
     mid_kernel(
         1,
-        grad_ref,
-        low_ref,
-        high_ref,
-        inner_ref,
-        gpre_two_ref,
+        *refs[:5],
         after_edge_ref,
         temporal_two_ref,
         spatial_two_ref,
@@ -293,16 +320,15 @@
     next_ref[0:1] = after_edge_ref[0:1]
     next_ref[1 : rows - 1] = after_inner_ref[...]
     next_ref[rows - 1 : rows] = after_edge_ref[1:2]
-    block_one(
-        saved_ref, preact_ref, low_ref, high_ref, [mid_ref, next_ref], temporal_ref, outs, scratch
-    )
-
-
-def input_kernel(mid_ref, gpre_ref, above_ref, below_ref, spatial_ref, out_ref, views_ref):
+    block_one(saved_ref, preact_ref, pair_refs, [mid_ref, next_ref], temporal_ref, outs, scratch)
+
+
+def input_kernel(mid_ref, gpre_ref, one_ref, two_ref, spatial_ref, out_ref, views_ref):
     rows, cols, ch = out_ref.shape
     step = 4
-    beside(above_ref[...].astype(jnp.float32), views_ref, 0)
-    beside(below_ref[...].astype(jnp.float32), views_ref, rows + 1)
+    above, below = beside_band((one_ref, two_ref), 0)
+    beside(above.astype(jnp.float32), views_ref, 0)
+    beside(below.astype(jnp.float32), views_ref, rows + 1)
 
     @pl.loop(0, rows // step)
     def _(n):
@@ -371,22 +397,25 @@
                     outs[2 * block + 1][here] = share[n, block].astype(jnp.float32)
 
 
-def frames_summed(own, *parts):
+def frames_summed(own, *parts, after=()):
     height, ch = own.shape
     half = height // 2
-    keep, send = call(band_kernel, [f32(half, ch), bf16(half, ch)], [], own.size, own, *parts)
+    outs = [f32(half, ch), bf16(half, ch)]
+    keep, send = call(band_kernel, outs, [], own.size, own, *parts, after=after)
     other = flipped(send, "video", 1)
     return call(frame_kernel, [bf16(half, ch)], [], half * ch, keep, other)
 
 
-def totals(one, two, factor):
+def totals(one, two, factor, meanwhile):
     height, ch = one[0].shape
     one, two = (
         [own] + [flipped(part, "section", flip + 1) for flip, part in enumerate(parts)]
         for own, *parts in (one, two)
     )
     if lax.axis_size("video") == 2 and lax.axis_size("dp") == 4:
-        two, one = frames_summed(*two), frames_summed(*one)
+        two = frames_summed(*two)
+        one = frames_summed(*one, after=(two,))
+        done = meanwhile((one,))
         parts = [
             x
             for own in (one, two)
@@ -394,11 +423,17 @@
         ]
         half = height // 2
         own = call(
-            functools.partial(clip_kernel, factor), [bf16(2, half, ch)], [], 8 * height * ch, *parts
+            functools.partial(clip_kernel, factor),
+            [bf16(2, half, ch)],
+            [],
+            8 * height * ch,
+            *parts,
+            after=(done,),
         )
         other = flipped(own, "video", 1)
         share = call(join_kernel, [bf16(2, 2, half, ch)], [], 1, own, other)
     else:
+        done = meanwhile(())
         own = [sum(x.astype(jnp.float32) for x in parts) for parts in (one, two)]
         share = lax.psum(jnp.stack(own), ("video", "dp")) * factor
         share = share.astype(jnp.bfloat16)[None]
@@ -413,7 +448,8 @@
         across,
         flipped(across, "section", 1),
     )
-    return [x.reshape(3, 3, ch, ch) if x.ndim == 3 else x.reshape(3, ch, ch) for x in outs]
+    outs = [x.reshape(3, 3, ch, ch) if x.ndim == 3 else x.reshape(3, ch, ch) for x in outs]
+    return done, outs
 
 
 def on_device(
@@ -447,23 +483,32 @@
     kernels = (temporal_two, spatial_two)
 
     wholes = [from_ahead(grad, 0, n + 1) for n in range(later)]
-    edges = [pl.BlockSpec((1, cols, ch), lambda _, at=at: (at, 0, 0)) for at in (0, rows - 1)]
-    up, down = call(
+    packs = call(
         pack_kernel,
         [bf16(4, cols, ch)] * 2,
-        [],
+        [pltpu.SemaphoreType.DMA((8,))],
         1,
-        *(grad, pre_two, saved_two, saved_one) * 2,
-        grid=(1,),
-        in_specs=[edges[0]] * 4 + [edges[1]] * 4,
-        limit=56,
-    )
-    low = from_ahead(down, -1, 0)
-    high = from_ahead(up, 1, 0)
+        grad,
+        pre_two,
+        saved_two,
+        saved_one,
+        whole=True,
+        limit=58,
+    )
+    pairs = [paired(pack, start) for start, pack in enumerate(packs)]
 
     known = ()
     if frames == 2:
-        known = call(last_inner_kernel, inner_outs, [views], 1.2 * conv, grad, pre_two, *kernels)
+        known = call(
+            last_inner_kernel,
+            inner_outs,
+            [views],
+            1.2 * conv,
+            grad,
+            pre_two,
+            *kernels,
+            after=pairs[:1],
+        )
         after_inner = from_ahead(known[0], 0, 1)
         edge = call(
             last_edge_kernel,
@@ -471,13 +516,15 @@
             [edge_views],
             conv // 8,
             grad,
-            low,
-            high,
+            *pairs,
             known[1],
             *kernels,
         )
     else:
-        edge = jnp.concatenate([grad[:1], grad[rows - 1 :], low[:1], high[:1]])
+        odd = lax.rem(lax.axis_index("section"), 2) == 1
+        one, two = (pair[:1] for pair in pairs)
+        above, below = jnp.where(odd, one, two), jnp.where(odd, two, one)
+        edge = jnp.concatenate([grad[:1], grad[rows - 1 :], above, below])
     after_edges = [from_ahead(edge, 0, n + 1) for n in range(later)]
     inner, gpre_two = call(
         functools.partial(inner_kernel, later),
@@ -498,17 +545,16 @@
         saved_two,
         pre_two,
         gpre_two,
-        low,
-        high,
+        *pairs,
         grad,
         *wholes,
     )
-    mid_inputs = (grad, low, high, inner, gpre_two)
+    mid_inputs = (grad, *pairs, inner, gpre_two)
     one_inputs = (saved_one, pre_one)
     mid_outs = [bf16(rows, cols, ch)]
     one_outs = [bf16(rows, cols, ch)] + [bf16(1, cols, ch)] * 2 + handed
     if frames == 2:
-        mid, gpre_one, first, last, *parts_one = call(
+        mid, gpre_one, *tail = call(
             mid_one_kernel,
             mid_outs + one_outs,
             [views, act, sums, act, edge_views],
@@ -530,30 +576,33 @@
             *after_edges,
             *kernels,
         )
-        gpre_one, first, last, *parts_one = call(
+        gpre_one, *tail = call(
             functools.partial(one_kernel, later),
             one_outs,
             [views, act, sums],
             1.2 * conv,
             *one_inputs,
-            low,
-            high,
+            *pairs,
             mid,
             *[from_ahead(mid, 0, n + 1) for n in range(later)],
             temporal_one,
         )
-    sums = totals(parts_one, parts_two, factor)
-    grad_in = call(
-        input_kernel,
-        [bf16(rows, cols, ch)],
-        [pltpu.VMEM((rows + 2, cols, 3 * ch), jnp.bfloat16)],
-        conv,
-        mid,
-        gpre_one,
-        from_ahead(last, -1, 0),
-        from_ahead(first, 1, 0),
-        spatial_one,
-    )
+    edges_one, parts_one = tail[:2], tail[2:]
+
+    def input_gradient(after):
+        return call(
+            input_kernel,
+            [bf16(rows, cols, ch)],
+            [pltpu.VMEM((rows + 2, cols, 3 * ch), jnp.bfloat16)],
+            conv,
+            mid,
+            gpre_one,
+            *[paired(edge, start) for start, edge in enumerate(edges_one)],
+            spatial_one,
+            after=after,
+        )
+
+    grad_in, sums = totals(parts_one, parts_two, factor, input_gradient)
     return (grad_in.reshape(shape), *sums)
 
 

time: 72.8 us -> 66.1 us (0.908)
  starting transfers between devices: 38.2 us -> 33.2 us
  Pallas kernels: 10.2 us -> 13.8 us
  local copies, waits for them, and re-layouts: 3.8 us -> 1 us
  waiting for transfers between devices: 19.3 us -> 16.6 us
    ppermute x7 -> x3, starting transfers between devices: 14.9 us -> 4 us  [from_ahead(): return lax.ppermute(block, ('section', 'video'), pairs)]
    ppermute x0 -> x4, starting transfers between devices: none -> 8.75 us  [paired(): lax.ppermute(block, 'section', pairs + [(right, left) for left, right in...]
    ppermute x7 -> x3, waiting for transfers between devices: 8.08 us -> 0.8 us  [from_ahead(): return lax.ppermute(block, ('section', 'video'), pairs)]
    ppermute x0 -> x4, waiting for transfers between devices: none -> 3.64 us  [paired(): lax.ppermute(block, 'section', pairs + [(right, left) for left, right in...]
    pallas_call x14, Pallas kernels: 10.2 us -> 13.8 us  [call(): pl.pallas_call(body, out_shape=outs[0] if single else tuple(outs), in_spe...]
    ppermute x18, starting transfers between devices: 23.3 us -> 20.5 us  [flipped(): lax.ppermute(block, axis, [(place ^ flip, place) for place in range(count)])]
    unnamed x26 -> x22, local copies, waits for them, and re-layouts: 3.8 us -> 1 us
    ppermute x18, waiting for transfers between devices: 11.3 us -> 12.2 us  [flipped(): lax.ppermute(block, axis, [(place ^ flip, place) for place in range(count)])]
  transfers between devices with their start and end apart: 25 -> 25, of which waited for: 9 -> 10; matrix products, arithmetic and copies ran while one was open for 0% -> 0% of each run, Pallas kernels for 12% -> 19%
where the time goes in v4:
time: 66.1 us; the launch traced here: 65.5 us
  starting transfers between devices  33.2 us (50%)
  waiting for transfers between devices  16.6 us (25%)
  Pallas kernels  13.8 us (21%)
  local copies, waits for them, and re-layouts  1 us (2%)
  between operations  0.93 us (1%)
    ppermute x18, starting transfers between devices, flipped(): lax.ppermute(block, axis, [(place ^ flip, place) for place in range(count)])  20.5 us
    pallas_call x14, Pallas kernels, call(): pl.pallas_call(body, out_shape=outs[0] if single else tuple(outs), in_spe...  13.8 us
    ppermute x18, waiting for transfers between devices, flipped(): lax.ppermute(block, axis, [(place ^ flip, place) for place in range(count)])  12.2 us
    ppermute x4, starting transfers between devices, paired(): lax.ppermute(block, 'section', pairs + [(right, left) for left, right in...  8.75 us
    ppermute x3, starting transfers between devices, from_ahead(): return lax.ppermute(block, ('section', 'video'), pairs)  4 us
    ppermute x4, waiting for transfers between devices, paired(): lax.ppermute(block, 'section', pairs + [(right, left) for left, right in...  3.64 us
  transfers between devices with their start and end apart: 25, of which 10 were waited for; matrix products, arithmetic and copies ran while one was open for 0% of the time, Pallas kernels for 19%

profile of v4, /device:TPU:1, one launch (start us, length us, event | category | flops | bytes accessed | tf_op | source)
XLA Modules:
  0.0 65.5 jit_solution(16538482919880710398)
XLA Ops:
  0.6 1.3 %collective-permute-start.2 = (bf16[16,64,128]{2,1,0:T(8,128)(2,1)}, bf16[16,64,128]{2,1,0:T(8,128)(2,1)S(1)}, u32[]{:S(2)}, u32[]{:S(2)}) collective-permute-start(bf16[16,64,128]{2,1,0:T(8,128)(2,1)} %bitcast.10), channel_id=1, source_target_pairs={{4,0},{12,8},{20,16},{28,24},{5,1},{13,9},{21,17},{29,25},{6,2},{1... | collective-permute-start | bytes 786440 | tf_op jit(solution)/shard_map/ppermute | solution.py:59
  2.0 5.2 %shard_map.128 = (bf16[4,64,128]{2,1,0:T(8,128)(2,1)}, bf16[4,64,128]{2,1,0:T(8,128)(2,1)}) custom-call(bf16[16,64,128]{2,1,0:T(8,128)(2,1)} %bitcast.11, bf16[16,64,128]{2,1,0:T(8,128)(2,1)} %bitcast.17, bf16[16,64,128]{2,1,0:T(8,128)(2,1)} %bitcast.24, bf16[16,64,128]{2,1,0:T(8,128)(2,1)} %bitcast.21), custom_call_target="tpu_custom_call" | custom-call | flops 1 | bytes 1179648 | tf_op jit(solution)/shard_map/pallas_call | solution.py:38
  7.3 1.4 %collective-permute-done.refs_4_.refs_1_.refs_3_ = bf16[4,64,128]{2,1,0:T(8,128)(2,1)S(1)} collective-permute-done((bf16[4,64,128]{2,1,0:T(8,128)(2,1)}, bf16[4,64,128]{2,1,0:T(8,128)(2,1)S(1)}, u32[]{:S(2)}, u32[]{:S(2)}) %collective-permute-start) | collective-permute-done | bytes 65568 | tf_op jit(solution)/shard_map/ppermute | solution.py:65
  8.7 1.3 %collective-permute-start.3 = (bf16[14,64,128]{2,1,0:T(8,128)(2,1)S(1)}, bf16[14,64,128]{2,1,0:T(8,128)(2,1)S(1)}, u32[]{:S(2)}, u32[]{:S(2)}) collective-permute-start(bf16[14,64,128]{2,1,0:T(8,128)(2,1)S(1)} %get-tuple-element.33.refs_5_), channel_id=1, source_target_pairs={{4,0},{12,8},{20,16},{28,24},{5,1},{13,9},{21,17},{29,25},{6,2},{1... | collective-permute-start | bytes 688136 | tf_op jit(solution)/shard_map/ppermute | solution.py:59
  10.1 4.5 %collective-permute-start.1 = (bf16[4,64,128]{2,1,0:T(8,128)(2,1)S(1)}, bf16[4,64,128]{2,1,0:T(8,128)(2,1)S(1)}, u32[]{:S(2)}, u32[]{:S(2)}) collective-permute-start(bf16[4,64,128]{2,1,0:T(8,128)(2,1)S(1)} %copy-done.10), channel_id=1, source_target_pairs={{8,16},{16,8},{9,17},{17,9},{10,18},{18,10},{11,19},{19,11},{12,20... | collective-permute-start | bytes 196616 | tf_op jit(solution)/shard_map/ppermute | solution.py:65
  14.6 2.2 %collective-permute-done.1.refs_2_.refs_4_ = bf16[4,64,128]{2,1,0:T(8,128)(2,1)S(1)} collective-permute-done((bf16[4,64,128]{2,1,0:T(8,128)(2,1)S(1)}, bf16[4,64,128]{2,1,0:T(8,128)(2,1)S(1)}, u32[]{:S(2)}, u32[]{:S(2)}) %collective-permute-start.1) | collective-permute-done | bytes 65568 | tf_op jit(solution)/shard_map/ppermute | solution.py:65
  16.8 1.4 %collective-permute-start.4 = (bf16[4,64,128]{2,1,0:T(8,128)(2,1)S(1)}, bf16[4,64,128]{2,1,0:T(8,128)(2,1)S(1)}, u32[]{:S(2)}, u32[]{:S(2)}) collective-permute-start(bf16[4,64,128]{2,1,0:T(8,128)(2,1)S(1)} %shard_map.131), channel_id=1, source_target_pairs={{4,0},{12,8},{20,16},{28,24},{5,1},{13,9},{21,17},{29,25},{6,2},{1... | collective-permute-start | bytes 196616 | tf_op jit(solution)/shard_map/ppermute | solution.py:59
  18.3 1.8 %shard_map.130 = (bf16[14,64,128]{2,1,0:T(8,128)(2,1)S(1)}, bf16[16,64,128]{2,1,0:T(8,128)(2,1)S(1)}) custom-call(bf16[16,64,128]{2,1,0:T(8,128)(2,1)S(1)} %bitcast.14, bf16[16,64,128]{2,1,0:T(8,128)(2,1)S(1)} %bitcast.19, bf16[16,64,128]{2,1,0:T(8,128)(2,1)S(1)} %collective-permute-done.2.refs_2_.refs_6_, bf16[3,128,128]{2,1,0:T(8,128)(2,1)S(1)} %copy-done.6, ...), custom_call_target="tpu_custom_call" | custom-call | flops 362387872 | bytes 2162688 | tf_op jit(solution)/shard_map/pallas_call | solution.py:38
  20.1 1.1 %shard_map.133 = (f32[384,128]{1,0:T(8,128)S(1)}, bf16[384,128]{1,0:T(8,128)(2,1)S(1)}, bf16[384,128]{1,0:T(8,128)(2,1)S(1)}, bf16[384,128]{1,0:T(8,128)(2,1)S(1)}) custom-call(bf16[16,64,128]{2,1,0:T(8,128)(2,1)S(1)} %bitcast.25, bf16[16,64,128]{2,1,0:T(8,128)(2,1)S(1)} %bitcast.20, bf16[16,64,128]{2,1,0:T(8,128)(2,1)S(1)} %get-tuple-element.36.refs_4_.refs_2_, ...), custom_call_target="tpu_custom_call" | custom-call | flops 362387872 | bytes 1933312 | tf_op jit(solution)/shard_map/pallas_call | solution.py:38
  21.2 1.6 %collective-permute-start.11 = (bf16[384,128]{1,0:T(8,128)(2,1)S(1)}, bf16[384,128]{1,0:T(8,128)(2,1)S(1)}, u32[]{:S(2)}, u32[]{:S(2)}) collective-permute-start(bf16[384,128]{1,0:T(8,128)(2,1)S(1)} %get-tuple-element.47), channel_id=1, source_target_pairs={{16,0},{24,8},{0,16},{8,24},{17,1},{25,9},{1,17},{9,25},{18,2},{26... | collective-permute-start | bytes 294920 | tf_op jit(solution)/shard_map/ppermute | solution.py:76
  22.8 0.6 collective-permute-start.12
  23.4 0.8 %collective-permute-done.4.refs_6_ = bf16[4,64,128]{2,1,0:T(8,128)(2,1)S(1)} collective-permute-done((bf16[4,64,128]{2,1,0:T(8,128)(2,1)S(1)}, bf16[4,64,128]{2,1,0:T(8,128)(2,1)S(1)}, u32[]{:S(2)}, u32[]{:S(2)}) %collective-permute-start.4) | collective-permute-done | bytes 65568 | tf_op jit(solution)/shard_map/ppermute | solution.py:59
  24.2 2.1 %shard_map.132 = (bf16[16,64,128]{2,1,0:T(8,128)(2,1)S(1)}, bf16[16,64,128]{2,1,0:T(8,128)(2,1)S(1)}, bf16[1,64,128]{2,1,0:T(8,128)(2,1)S(1)}, bf16[1,64,128]{2,...) custom-call(bf16[16,64,128]{2,1,0:T(8,128)(2,1)S(1)} %bitcast.16, ...), custom_call_target="tpu_custom_call" | custom-call | flops 452984832 | bytes 3244032 | tf_op jit(solution)/shard_map/pallas_call | solution.py:38
  26.3 2.7 %collective-permute-start.8 = (bf16[384,128]{1,0:T(8,128)(2,1)S(1)}, bf16[384,128]{1,0:T(8,128)(2,1)S(1)}, u32[]{:S(2)}, u32[]{:S(2)}) collective-permute-start(bf16[384,128]{1,0:T(8,128)(2,1)S(1)} %get-tuple-element.43), channel_id=1, source_target_pairs={{16,0},{24,8},{0,16},{8,24},{17,1},{25,9},{1,17},{9,25},{18,2},{26... | collective-permute-start | bytes 294920 | tf_op jit(solution)/shard_map/ppermute | solution.py:76
  29.2 1.8 %collective-permute-start.13 = (bf16[192,128]{1,0:T(8,128)(2,1)S(1)}, bf16[192,128]{1,0:T(8,128)(2,1)S(1)}, u32[]{:S(2)}, u32[]{:S(2)}) collective-permute-start(bf16[192,128]{1,0:T(8,128)(2,1)S(1)} %get-tuple-element.50), channel_id=1, source_target_pairs={{4,0},{0,4},{5,1},{1,5},{6,2},{2,6},{7,3},{3,7},{12,8},{8,12},{13,... | collective-permute-start | bytes 147464 | tf_op jit(solution)/shard_map/ppermute | solution.py:76
  31.0 1.8 %collective-permute-done.13.refs_1_ = bf16[192,128]{1,0:T(8,128)(2,1)S(1)} collective-permute-done((bf16[192,128]{1,0:T(8,128)(2,1)S(1)}, bf16[192,128]{1,0:T(8,128)(2,1)S(1)}, u32[]{:S(2)}, u32[]{:S(2)}) %collective-permute-start.13) | collective-permute-done | bytes 49184 | tf_op jit(solution)/shard_map/ppermute | solution.py:76
  32.8 1.5 %collective-permute-done.9.refs_3_ = bf16[384,128]{1,0:T(8,128)(2,1)S(1)} collective-permute-done((bf16[384,128]{1,0:T(8,128)(2,1)S(1)}, bf16[384,128]{1,0:T(8,128)(2,1)S(1)}, u32[]{:S(2)}, u32[]{:S(2)}) %collective-permute-start.9) | collective-permute-done | bytes 98336 | tf_op jit(solution)/shard_map/ppermute | solution.py:76
  34.3 0.9 %collective-permute-start.14 = (bf16[192,128]{1,0:T(8,128)(2,1)S(1)}, bf16[192,128]{1,0:T(8,128)(2,1)S(1)}, u32[]{:S(2)}, u32[]{:S(2)}) collective-permute-start(bf16[192,128]{1,0:T(8,128)(2,1)S(1)} %get-tuple-element.52), channel_id=1, source_target_pairs={{4,0},{0,4},{5,1},{1,5},{6,2},{2,6},{7,3},{3,7},{12,8},{8,12},{13,... | collective-permute-start | bytes 147464 | tf_op jit(solution)/shard_map/ppermute | solution.py:76
  35.2 3.3 %collective-permute-start.20 = (bf16[192,128]{1,0:T(8,128)(2,1)S(1)}, bf16[192,128]{1,0:T(8,128)(2,1)S(1)}, u32[]{:S(2)}, u32[]{:S(2)}) collective-permute-start(bf16[192,128]{1,0:T(8,128)(2,1)S(1)} %shard_map.135.refs_4_), channel_id=1, source_target_pairs={{3,0},{2,1},{1,2},{0,3},{7,4},{6,5},{5,6},{4,7},{11,8},{10,9},{9,1... | collective-permute-start | bytes 147464 | tf_op jit(solution)/shard_map/ppermute | solution.py:76
  38.5 0.9 %collective-permute-start.5 = (bf16[1,64,128]{2,1,0:T(8,128)(2,1)S(1)}, bf16[1,64,128]{2,1,0:T(8,128)(2,1)S(1)}, u32[]{:S(2)}, u32[]{:S(2)}) collective-permute-start(bf16[1,64,128]{2,1,0:T(8,128)(2,1)S(1)} %get-tuple-element.39), channel_id=1, source_target_pairs={{0,8},{16,24},{8,0},{24,16},{1,9},{17,25},{9,1},{25,17},{2,10},{18... | collective-permute-start | bytes 49160 | tf_op jit(solution)/shard_map/ppermute | solution.py:65
  39.4 3.2 %collective-permute-start.6 = (bf16[1,64,128]{2,1,0:T(8,128)(2,1)S(1)}, bf16[1,64,128]{2,1,0:T(8,128)(2,1)S(1)}, u32[]{:S(2)}, u32[]{:S(2)}) collective-permute-start(bf16[1,64,128]{2,1,0:T(8,128)(2,1)S(1)} %get-tuple-element.40), channel_id=1, source_target_pairs={{8,16},{16,8},{9,17},{17,9},{10,18},{18,10},{11,19},{19,11},{12,20... | collective-permute-start | bytes 49160 | tf_op jit(solution)/shard_map/ppermute | solution.py:65
  42.9 3.4 %collective-permute-start.17 = (bf16[192,128]{1,0:T(8,128)(2,1)S(1)}, bf16[192,128]{1,0:T(8,128)(2,1)S(1)}, u32[]{:S(2)}, u32[]{:S(2)}) collective-permute-start(bf16[192,128]{1,0:T(8,128)(2,1)S(1)} %shard_map.137.refs_5_.refs_0_), channel_id=1, source_target_pairs={{3,0},{2,1},{1,2},{0,3},{7,4},{6,5},{5,6},{4,7},{11,8},{10,9},{9,1... | collective-permute-start | bytes 147464 | tf_op jit(solution)/shard_map/ppermute | solution.py:76
  46.7 2.2 %shard_map.138.refs_8_ = bf16[16,64,128]{2,1,0:T(8,128)(2,1)} custom-call(bf16[16,64,128]{2,1,0:T(8,128)(2,1)S(1)} %get-tuple-element.37.refs_0_, bf16[16,64,128]{2,1,0:T(8,128)(2,1)S(1)} %get-tuple-element.38.refs_1_, bf16[1,64,128]{2,1,0:T(8,128)(2,1)S(1)} %collective-permute-done.5.refs_2_, bf16[1,64,128]{2,1,0:T(8,128)(2,1)S(1)} %collective-permute-done.6.refs_3_, ...), custom_call_target="tpu_custom_call" | custom-call | flops 301989888 | bytes 1114112 | tf_op jit(solution)/shard_map/pallas_call | solution.py:38
  48.9 1.4 %collective-permute-done.16.refs_2_ = bf16[192,128]{1,0:T(8,128)(2,1)S(1)} collective-permute-done((bf16[192,128]{1,0:T(8,128)(2,1)S(1)}, bf16[192,128]{1,0:T(8,128)(2,1)S(1)}, u32[]{:S(2)}, u32[]{:S(2)}) %collective-permute-start.16) | collective-permute-done | bytes 49184 | tf_op jit(solution)/shard_map/ppermute | solution.py:76
  50.4 0.9 %copy-done.4 = bf16[16,64,128]{2,1,0:T(8,128)(2,1)S(1)} copy-done((bf16[16,64,128]{2,1,0:T(8,128)(2,1)S(1)}, bf16[16,64,128]{2,1,0:T(8,128)(2,1)}, u32[]{:S(2)}) %copy-start.4) | copy-done | bytes 262168
  51.4 0.6 collective-permute-start.21
  52.0 3.8 %collective-permute-done.21.refs_1_ = bf16[2,192,128]{2,1,0:T(8,128)(2,1)S(1)} collective-permute-done((bf16[2,192,128]{2,1,0:T(8,128)(2,1)S(1)}, bf16[2,192,128]{2,1,0:T(8,128)(2,1)S(1)}, u32[]{:S(2)}, u32[]{:S(2)}) %collective-permute-start.21) | collective-permute-done | bytes 98336 | tf_op jit(solution)/shard_map/ppermute | solution.py:76
  55.9 2.9 %collective-permute-start.22 = (bf16[2,2,192,128]{3,2,1,0:T(8,128)(2,1)S(1)}, bf16[2,2,192,128]{3,2,1,0:T(8,128)(2,1)S(1)}, u32[]{:S(2)}, u32[]{:S(2)}) collective-permute-start(bf16[2,2,192,128]{3,2,1,0:T(8,128)(2,1)S(1)} %shard_map.140.refs_0_), channel_id=1, source_target_pairs={{8,0},{0,8},{24,16},{16,24},{9,1},{1,9},{25,17},{17,25},{10,2},{2,... | collective-permute-start | bytes 589832 | tf_op jit(solution)/shard_map/ppermute | solution.py:76
  58.8 2.6 %collective-permute-done.23.refs_2_ = bf16[2,2,192,128]{3,2,1,0:T(8,128)(2,1)S(1)} collective-permute-done((bf16[2,2,192,128]{3,2,1,0:T(8,128)(2,1)S(1)}, bf16[2,2,192,128]{3,2,1,0:T(8,128)(2,1)S(1)}, u32[]{:S(2)}, u32[]{:S(2)}) %collective-permute-start.23) | collective-permute-done | bytes 196640 | tf_op jit(solution)/shard_map/ppermute | solution.py:76
  61.4 1.8 %collective-permute-start.24 = (bf16[2,2,192,128]{3,2,1,0:T(8,128)(2,1)S(1)}, bf16[2,2,192,128]{3,2,1,0:T(8,128)(2,1)S(1)}, u32[]{:S(2)}, u32[]{:S(2)}) collective-permute-start(bf16[2,2,192,128]{3,2,1,0:T(8,128)(2,1)S(1)} %collective-permute-done.23.refs_2_), channel_id=1, source_target_pairs={{8,0},{0,8},{24,16},{16,24},{9,1},{1,9},{25,17},{17,25},{10,2},{2,... | collective-permute-start | bytes 589832 | tf_op jit(solution)/shard_map/ppermute | solution.py:76
  63.2 1.1 %collective-permute-done.24.refs_3_ = bf16[2,2,192,128]{3,2,1,0:T(8,128)(2,1)S(1)} collective-permute-done((bf16[2,2,192,128]{3,2,1,0:T(8,128)(2,1)S(1)}, bf16[2,2,192,128]{3,2,1,0:T(8,128)(2,1)S(1)}, u32[]{:S(2)}, u32[]{:S(2)}) %collective-permute-start.24) | collective-permute-done | bytes 196640 | tf_op jit(solution)/shard_map/ppermute | solution.py:76
  64.3 1.3 %shard_map.141 = (f32[3,384,128]{2,1,0:T(8,128)}, f32[384,128]{1,0:T(8,128)}, f32[3,384,128]{2,1,0:T(8,128)}, f32[384,128]{1,0:T(8,128)}) custom-call(bf16[2,2,192,128]{3,2,1,0:T(8,128)(2,1)S(1)} %shard_map.140.refs_0_, bf16[2,2,192,128]{3,2,1,0:T(8,128)(2,1)S(1)} %collective-permute-done.22.refs_1_, ...), custom_call_target="tpu_custom_call" | custom-call | flops 98304 | bytes 2359296 | tf_op jit(solution)/shard_map/pallas_call | solution.py:38
  (54 shorter events, 1.4 us)
Async XLA Ops:
  0.6 17.6 %collective-permute-start.2 = (bf16[16,64,128]{2,1,0:T(8,128)(2,1)}, bf16[16,64,128]{2,1,0:T(8,128)(2,1)S(1)}, u32[]{:S(2)}, u32[]{:S(2)}) collective-permute-start(bf16[16,64,128]{2,1,0:T(8,128)(2,1)} %bitcast.10), channel_id=1, source_target_pairs={{4,0},{12,8},{20,16},{28,24},{5,1},{13,9},{21,17},{29,25},{6,2},{1... | collective-permute-start | bytes 786440 | tf_op jit(solution)/shard_map/ppermute | solution.py:59
  1.9 6.8 %copy-start = (bf16[1,1,16,64,128]{4,3,2,1,0:T(8,128)(2,1)S(1)}, bf16[1,1,16,64,128]{4,3,2,1,0:T(8,128)(2,1)}, u32[]{:S(2)}) copy-start(bf16[1,1,16,64,128]{4,3,2,1,0:T(8,128)(2,1)} %param.9) | copy-start | bytes 786436
  1.9 6.8 %copy-start.1 = (bf16[3,3,128,128]{3,2,1,0:T(8,128)(2,1)S(1)}, bf16[3,3,128,128]{3,2,1,0:T(8,128)(2,1)}, u32[]{:S(2)}) copy-start(bf16[3,3,128,128]{3,2,1,0:T(8,128)(2,1)} %refs_8_.1) | copy-start | bytes 884740
  2.0 6.8 %copy-start.2 = (bf16[1,1,16,64,128]{4,3,2,1,0:T(8,128)(2,1)S(1)}, bf16[1,1,16,64,128]{4,3,2,1,0:T(8,128)(2,1)}, u32[]{:S(2)}) copy-start(bf16[1,1,16,64,128]{4,3,2,1,0:T(8,128)(2,1)} %param.13) | copy-start | bytes 786436
  2.0 6.8 %copy-start.6 = (bf16[3,128,128]{2,1,0:T(8,128)(2,1)S(1)}, bf16[3,128,128]{2,1,0:T(8,128)(2,1)}, u32[]{:S(2)}) copy-start(bf16[3,128,128]{2,1,0:T(8,128)(2,1)} %refs_7_.1) | copy-start | bytes 294916
  7.2 1.5 %collective-permute-start = (bf16[4,64,128]{2,1,0:T(8,128)(2,1)}, bf16[4,64,128]{2,1,0:T(8,128)(2,1)S(1)}, u32[]{:S(2)}, u32[]{:S(2)}) collective-permute-start(bf16[4,64,128]{2,1,0:T(8,128)(2,1)} %get-tuple-element.31), channel_id=1, source_target_pairs={{0,8},{16,24},{8,0},{24,16},{1,9},{17,25},{9,1},{25,17},{2,10},{18... | collective-permute-start | bytes 196616 | tf_op jit(solution)/shard_map/ppermute | solution.py:65
  8.7 15.4 %collective-permute-start.3 = (bf16[14,64,128]{2,1,0:T(8,128)(2,1)S(1)}, bf16[14,64,128]{2,1,0:T(8,128)(2,1)S(1)}, u32[]{:S(2)}, u32[]{:S(2)}) collective-permute-start(bf16[14,64,128]{2,1,0:T(8,128)(2,1)S(1)} %get-tuple-element.33.refs_5_), channel_id=1, source_target_pairs={{4,0},{12,8},{20,16},{28,24},{5,1},{13,9},{21,17},{29,25},{6,2},{1... | collective-permute-start | bytes 688136 | tf_op jit(solution)/shard_map/ppermute | solution.py:59
  10.1 6.8 %collective-permute-start.1 = (bf16[4,64,128]{2,1,0:T(8,128)(2,1)S(1)}, bf16[4,64,128]{2,1,0:T(8,128)(2,1)S(1)}, u32[]{:S(2)}, u32[]{:S(2)}) collective-permute-start(bf16[4,64,128]{2,1,0:T(8,128)(2,1)S(1)} %copy-done.10), channel_id=1, source_target_pairs={{8,16},{16,8},{9,17},{17,9},{10,18},{18,10},{11,19},{19,11},{12,20... | collective-permute-start | bytes 196616 | tf_op jit(solution)/shard_map/ppermute | solution.py:65
  16.8 7.3 %collective-permute-start.4 = (bf16[4,64,128]{2,1,0:T(8,128)(2,1)S(1)}, bf16[4,64,128]{2,1,0:T(8,128)(2,1)S(1)}, u32[]{:S(2)}, u32[]{:S(2)}) collective-permute-start(bf16[4,64,128]{2,1,0:T(8,128)(2,1)S(1)} %shard_map.131), channel_id=1, source_target_pairs={{4,0},{12,8},{20,16},{28,24},{5,1},{13,9},{21,17},{29,25},{6,2},{1... | collective-permute-start | bytes 196616 | tf_op jit(solution)/shard_map/ppermute | solution.py:59
  20.0 4.1 %copy-start.3 = (bf16[1,1,16,64,128]{4,3,2,1,0:T(8,128)(2,1)S(1)}, bf16[1,1,16,64,128]{4,3,2,1,0:T(8,128)(2,1)}, u32[]{:S(2)}) copy-start(bf16[1,1,16,64,128]{4,3,2,1,0:T(8,128)(2,1)} %param.10) | copy-start | bytes 786436
  20.1 4.1 %copy-start.8 = (bf16[1,1,16,64,128]{4,3,2,1,0:T(8,128)(2,1)S(1)}, bf16[1,1,16,64,128]{4,3,2,1,0:T(8,128)(2,1)}, u32[]{:S(2)}) copy-start(bf16[1,1,16,64,128]{4,3,2,1,0:T(8,128)(2,1)} %param.11) | copy-start | bytes 786436
  21.2 7.9 %collective-permute-start.10 = (bf16[384,128]{1,0:T(8,128)(2,1)S(1)}, bf16[384,128]{1,0:T(8,128)(2,1)S(1)}, u32[]{:S(2)}, u32[]{:S(2)}) collective-permute-start(bf16[384,128]{1,0:T(8,128)(2,1)S(1)} %get-tuple-element.46), channel_id=1, source_target_pairs={{8,0},{0,8},{24,16},{16,24},{9,1},{1,9},{25,17},{17,25},{10,2},{2,... | collective-permute-start | bytes 294920 | tf_op jit(solution)/shard_map/ppermute | solution.py:76
  21.2 7.9 %collective-permute-start.11 = (bf16[384,128]{1,0:T(8,128)(2,1)S(1)}, bf16[384,128]{1,0:T(8,128)(2,1)S(1)}, u32[]{:S(2)}, u32[]{:S(2)}) collective-permute-start(bf16[384,128]{1,0:T(8,128)(2,1)S(1)} %get-tuple-element.47), channel_id=1, source_target_pairs={{16,0},{24,8},{0,16},{8,24},{17,1},{25,9},{1,17},{9,25},{18,2},{26... | collective-permute-start | bytes 294920 | tf_op jit(solution)/shard_map/ppermute | solution.py:76
  22.8 6.3 %collective-permute-start.12 = (bf16[384,128]{1,0:T(8,128)(2,1)S(1)}, bf16[384,128]{1,0:T(8,128)(2,1)S(1)}, u32[]{:S(2)}, u32[]{:S(2)}) collective-permute-start(bf16[384,128]{1,0:T(8,128)(2,1)S(1)} %get-tuple-element.48), channel_id=1, source_target_pairs={{24,0},{16,8},{8,16},{0,24},{25,1},{17,9},{9,17},{1,25},{26,2},{18... | collective-permute-start | bytes 294920 | tf_op jit(solution)/shard_map/ppermute | solution.py:76
  26.3 6.5 %collective-permute-start.7 = (bf16[384,128]{1,0:T(8,128)(2,1)S(1)}, bf16[384,128]{1,0:T(8,128)(2,1)S(1)}, u32[]{:S(2)}, u32[]{:S(2)}) collective-permute-start(bf16[384,128]{1,0:T(8,128)(2,1)S(1)} %get-tuple-element.42), channel_id=1, source_target_pairs={{8,0},{0,8},{24,16},{16,24},{9,1},{1,9},{25,17},{17,25},{10,2},{2,... | collective-permute-start | bytes 294920 | tf_op jit(solution)/shard_map/ppermute | solution.py:76
  26.3 6.4 %collective-permute-start.8 = (bf16[384,128]{1,0:T(8,128)(2,1)S(1)}, bf16[384,128]{1,0:T(8,128)(2,1)S(1)}, u32[]{:S(2)}, u32[]{:S(2)}) collective-permute-start(bf16[384,128]{1,0:T(8,128)(2,1)S(1)} %get-tuple-element.43), channel_id=1, source_target_pairs={{16,0},{24,8},{0,16},{8,24},{17,1},{25,9},{1,17},{9,25},{18,2},{26... | collective-permute-start | bytes 294920 | tf_op jit(solution)/shard_map/ppermute | solution.py:76
  29.1 5.2 %collective-permute-start.9 = (bf16[384,128]{1,0:T(8,128)(2,1)S(1)}, bf16[384,128]{1,0:T(8,128)(2,1)S(1)}, u32[]{:S(2)}, u32[]{:S(2)}) collective-permute-start(bf16[384,128]{1,0:T(8,128)(2,1)S(1)} %get-tuple-element.44), channel_id=1, source_target_pairs={{24,0},{16,8},{8,16},{0,24},{25,1},{17,9},{9,17},{1,25},{26,2},{18... | collective-permute-start | bytes 294920 | tf_op jit(solution)/shard_map/ppermute | solution.py:76
  29.2 3.6 %collective-permute-start.13 = (bf16[192,128]{1,0:T(8,128)(2,1)S(1)}, bf16[192,128]{1,0:T(8,128)(2,1)S(1)}, u32[]{:S(2)}, u32[]{:S(2)}) collective-permute-start(bf16[192,128]{1,0:T(8,128)(2,1)S(1)} %get-tuple-element.50), channel_id=1, source_target_pairs={{4,0},{0,4},{5,1},{1,5},{6,2},{2,6},{7,3},{3,7},{12,8},{8,12},{13,... | collective-permute-start | bytes 147464 | tf_op jit(solution)/shard_map/ppermute | solution.py:76
  34.2 12.4 %copy-start.7 = (bf16[3,3,128,128]{3,2,1,0:T(8,128)(2,1)S(1)}, bf16[3,3,128,128]{3,2,1,0:T(8,128)(2,1)}, u32[]{:S(2)}) copy-start(bf16[3,3,128,128]{3,2,1,0:T(8,128)(2,1)} %refs_4_.5) | copy-start | bytes 884740
  34.3 8.4 %collective-permute-start.14 = (bf16[192,128]{1,0:T(8,128)(2,1)S(1)}, bf16[192,128]{1,0:T(8,128)(2,1)S(1)}, u32[]{:S(2)}, u32[]{:S(2)}) collective-permute-start(bf16[192,128]{1,0:T(8,128)(2,1)S(1)} %get-tuple-element.52), channel_id=1, source_target_pairs={{4,0},{0,4},{5,1},{1,5},{6,2},{2,6},{7,3},{3,7},{12,8},{8,12},{13,... | collective-permute-start | bytes 147464 | tf_op jit(solution)/shard_map/ppermute | solution.py:76
  35.2 11.2 %collective-permute-start.20 = (bf16[192,128]{1,0:T(8,128)(2,1)S(1)}, bf16[192,128]{1,0:T(8,128)(2,1)S(1)}, u32[]{:S(2)}, u32[]{:S(2)}) collective-permute-start(bf16[192,128]{1,0:T(8,128)(2,1)S(1)} %shard_map.135.refs_4_), channel_id=1, source_target_pairs={{3,0},{2,1},{1,2},{0,3},{7,4},{6,5},{5,6},{4,7},{11,8},{10,9},{9,1... | collective-permute-start | bytes 147464 | tf_op jit(solution)/shard_map/ppermute | solution.py:76
  38.5 4.4 %collective-permute-start.5 = (bf16[1,64,128]{2,1,0:T(8,128)(2,1)S(1)}, bf16[1,64,128]{2,1,0:T(8,128)(2,1)S(1)}, u32[]{:S(2)}, u32[]{:S(2)}) collective-permute-start(bf16[1,64,128]{2,1,0:T(8,128)(2,1)S(1)} %get-tuple-element.39), channel_id=1, source_target_pairs={{0,8},{16,24},{8,0},{24,16},{1,9},{17,25},{9,1},{25,17},{2,10},{18... | collective-permute-start | bytes 49160 | tf_op jit(solution)/shard_map/ppermute | solution.py:65
  39.4 6.9 %collective-permute-start.6 = (bf16[1,64,128]{2,1,0:T(8,128)(2,1)S(1)}, bf16[1,64,128]{2,1,0:T(8,128)(2,1)S(1)}, u32[]{:S(2)}, u32[]{:S(2)}) collective-permute-start(bf16[1,64,128]{2,1,0:T(8,128)(2,1)S(1)} %get-tuple-element.40), channel_id=1, source_target_pairs={{8,16},{16,8},{9,17},{17,9},{10,18},{18,10},{11,19},{19,11},{12,20... | collective-permute-start | bytes 49160 | tf_op jit(solution)/shard_map/ppermute | solution.py:65
  42.6 6.3 %collective-permute-start.19 = (bf16[192,128]{1,0:T(8,128)(2,1)S(1)}, bf16[192,128]{1,0:T(8,128)(2,1)S(1)}, u32[]{:S(2)}, u32[]{:S(2)}) collective-permute-start(bf16[192,128]{1,0:T(8,128)(2,1)S(1)} %shard_map.135.refs_4_), channel_id=1, source_target_pairs={{2,0},{3,1},{0,2},{1,3},{6,4},{7,5},{4,6},{5,7},{10,8},{11,9},{8,1... | collective-permute-start | bytes 147464 | tf_op jit(solution)/shard_map/ppermute | solution.py:76
  42.7 6.2 %collective-permute-start.18 = (bf16[192,128]{1,0:T(8,128)(2,1)S(1)}, bf16[192,128]{1,0:T(8,128)(2,1)S(1)}, u32[]{:S(2)}, u32[]{:S(2)}) collective-permute-start(bf16[192,128]{1,0:T(8,128)(2,1)S(1)} %shard_map.135.refs_4_), channel_id=1, source_target_pairs={{1,0},{0,1},{3,2},{2,3},{5,4},{4,5},{7,6},{6,7},{9,8},{8,9},{11,10... | collective-permute-start | bytes 147464 | tf_op jit(solution)/shard_map/ppermute | solution.py:76
  42.9 6.0 %collective-permute-start.17 = (bf16[192,128]{1,0:T(8,128)(2,1)S(1)}, bf16[192,128]{1,0:T(8,128)(2,1)S(1)}, u32[]{:S(2)}, u32[]{:S(2)}) collective-permute-start(bf16[192,128]{1,0:T(8,128)(2,1)S(1)} %shard_map.137.refs_5_.refs_0_), channel_id=1, source_target_pairs={{3,0},{2,1},{1,2},{0,3},{7,4},{6,5},{5,6},{4,7},{11,8},{10,9},{9,1... | collective-permute-start | bytes 147464 | tf_op jit(solution)/shard_map/ppermute | solution.py:76
  46.3 4.0 %collective-permute-start.16 = (bf16[192,128]{1,0:T(8,128)(2,1)S(1)}, bf16[192,128]{1,0:T(8,128)(2,1)S(1)}, u32[]{:S(2)}, u32[]{:S(2)}) collective-permute-start(bf16[192,128]{1,0:T(8,128)(2,1)S(1)} %shard_map.137.refs_5_.refs_0_), channel_id=1, source_target_pairs={{2,0},{3,1},{0,2},{1,3},{6,4},{7,5},{4,6},{5,7},{10,8},{11,9},{8,1... | collective-permute-start | bytes 147464 | tf_op jit(solution)/shard_map/ppermute | solution.py:76
  46.3 4.1 %collective-permute-start.15 = (bf16[192,128]{1,0:T(8,128)(2,1)S(1)}, bf16[192,128]{1,0:T(8,128)(2,1)S(1)}, u32[]{:S(2)}, u32[]{:S(2)}) collective-permute-start(bf16[192,128]{1,0:T(8,128)(2,1)S(1)} %shard_map.137.refs_5_.refs_0_), channel_id=1, source_target_pairs={{1,0},{0,1},{3,2},{2,3},{5,4},{4,5},{7,6},{6,7},{9,8},{8,9},{11,10... | collective-permute-start | bytes 147464 | tf_op jit(solution)/shard_map/ppermute | solution.py:76
  51.4 4.4 %collective-permute-start.21 = (bf16[2,192,128]{2,1,0:T(8,128)(2,1)S(1)}, bf16[2,192,128]{2,1,0:T(8,128)(2,1)S(1)}, u32[]{:S(2)}, u32[]{:S(2)}) collective-permute-start(bf16[2,192,128]{2,1,0:T(8,128)(2,1)S(1)} %shard_map.139.refs_0_), channel_id=1, source_target_pairs={{4,0},{0,4},{5,1},{1,5},{6,2},{2,6},{7,3},{3,7},{12,8},{8,12},{13,... | collective-permute-start | bytes 294920 | tf_op jit(solution)/shard_map/ppermute | solution.py:76
  55.8 5.6 %collective-permute-start.23 = (bf16[2,2,192,128]{3,2,1,0:T(8,128)(2,1)S(1)}, bf16[2,2,192,128]{3,2,1,0:T(8,128)(2,1)S(1)}, u32[]{:S(2)}, u32[]{:S(2)}) collective-permute-start(bf16[2,2,192,128]{3,2,1,0:T(8,128)(2,1)S(1)} %shard_map.140.refs_0_), channel_id=1, source_target_pairs={{16,0},{24,8},{0,16},{8,24},{17,1},{25,9},{1,17},{9,25},{18,2},{26... | collective-permute-start | bytes 589832 | tf_op jit(solution)/shard_map/ppermute | solution.py:76
  55.9 7.3 %collective-permute-start.22 = (bf16[2,2,192,128]{3,2,1,0:T(8,128)(2,1)S(1)}, bf16[2,2,192,128]{3,2,1,0:T(8,128)(2,1)S(1)}, u32[]{:S(2)}, u32[]{:S(2)}) collective-permute-start(bf16[2,2,192,128]{3,2,1,0:T(8,128)(2,1)S(1)} %shard_map.140.refs_0_), channel_id=1, source_target_pairs={{8,0},{0,8},{24,16},{16,24},{9,1},{1,9},{25,17},{17,25},{10,2},{2,... | collective-permute-start | bytes 589832 | tf_op jit(solution)/shard_map/ppermute | solution.py:76
  61.4 2.8 %collective-permute-start.24 = (bf16[2,2,192,128]{3,2,1,0:T(8,128)(2,1)S(1)}, bf16[2,2,192,128]{3,2,1,0:T(8,128)(2,1)S(1)}, u32[]{:S(2)}, u32[]{:S(2)}) collective-permute-start(bf16[2,2,192,128]{3,2,1,0:T(8,128)(2,1)S(1)} %collective-permute-done.23.refs_2_), channel_id=1, source_target_pairs={{8,0},{0,8},{24,16},{16,24},{9,1},{1,9},{25,17},{17,25},{10,2},{2,... | collective-permute-start | bytes 589832 | tf_op jit(solution)/shard_map/ppermute | solution.py:76
  (4 other events, 11.1 us)

commit v5 on v4

--- a/solution.py
+++ b/solution.py
@@ -23,12 +23,12 @@
     return jax.ShapeDtypeStruct(shape, jnp.float32)
 
 
-def call(kernel, outs, scratch, flops, *operands, after=(), whole=False, limit=24):
+def call(kernel, outs, scratch, flops, *operands, after=(), spare_inputs=False, limit=24):
     single = len(outs) == 1
     moved = sum(math.prod(x.shape) * x.dtype.itemsize for x in (*operands, *outs))
     vmem = pl.BlockSpec(memory_space=pltpu.VMEM)
     spare = pl.BlockSpec(memory_space=pl.ANY)
-    spec = spare if whole else vmem
+    spec = spare if spare_inputs else vmem
     count = len(operands)
     operands = (*operands, *after)
 
@@ -39,7 +39,7 @@
         body,
         out_shape=outs[0] if single else tuple(outs),
         in_specs=[spec] * count + [spare] * len(after),
-        out_specs=spec if single else (spec,) * len(outs),
+        out_specs=vmem if single else (vmem,) * len(outs),
         scratch_shapes=scratch,
         compiler_params=pltpu.CompilerParams(vmem_limit_bytes=limit * MIB),
         cost_estimate=pl.CostEstimate(
@@ -110,6 +110,10 @@
             view, kernel, (((1,), (1,)), ((), ())), preferred_element_type=jnp.float32
         )
     return total.astype(jnp.bfloat16).reshape(first.shape)
+
+
+def is_last():
+    return lax.axis_index("video") == lax.axis_size("video") - 1
 
 
 def kernel_sums(saved_ref, above, below, act, grads, views, sums_ref):
@@ -129,20 +133,18 @@
         jnp.concatenate([grad.reshape(flat) for grad in grads], axis=1),
         preferred_element_type=jnp.float32,
     )
+    zeros = jnp.zeros((ch, ch), jnp.float32)
     for k in range(3):
         step = 2 - k
-        here = slice(k * ch, (k + 1) * ch)
-        if step < len(grads):
-            sums_ref[3, here] = sums[:, step * ch : (step + 1) * ch]
-        else:
-            sums_ref[3, here] = jnp.zeros((ch, ch), jnp.float32)
-
-
-def hand_out(sums_ref, outs):
-    band = lax.axis_index("section")
-    outs[0][...] = sums_ref[band]
-    for flip in range(1, 4):
-        outs[flip][...] = sums_ref[jnp.bitwise_xor(band, flip)].astype(jnp.bfloat16)
+        value = sums[:, step * ch : (step + 1) * ch] if step < len(grads) else zeros
+        sums_ref[3, k * ch : (k + 1) * ch] = jnp.where(is_last(), zeros, value) if step else value
+
+
+def hand_out(sums_ref, keep_ref, send_ref):
+    odd = lax.rem(lax.axis_index("section"), 2)
+    for n in range(2):
+        keep_ref[n] = sums_ref[2 * n + odd]
+        send_ref[n] = sums_ref[2 * n + 1 - odd].astype(jnp.bfloat16)
 
 
 def pack_kernel(*refs):
@@ -197,26 +199,21 @@
     )
 
 
-def on_last(body):
-    pl.when(lax.axis_index("video") == lax.axis_size("video") - 1)(body)
-
-
 def last_inner_kernel(grad_ref, preact_ref, temporal_ref, spatial_ref, inner_ref, gpre_ref, views_ref):
-    on_last(
-        lambda: interior(
+    @pl.when(is_last())
+    def _():
+        interior(
             grad_ref, preact_ref, [], temporal_ref, spatial_ref, inner_ref, gpre_ref, views_ref
         )
-    )
 
 
 def last_edge_kernel(grad_ref, one_ref, two_ref, gpre_ref, temporal_ref, spatial_ref, edge_ref, views_ref):
-    def body():
+    @pl.when(is_last())
+    def _():
         edge_ref[0:1], edge_ref[1:2] = edge_rows(
             grad_ref, (one_ref, two_ref), [], gpre_ref, temporal_ref, spatial_ref, views_ref
         )
         edge_ref[2:3], edge_ref[3:4] = beside_band((one_ref, two_ref), 0)
-
-    on_last(body)
 
 
 def inner_kernel(later, *refs):
@@ -226,13 +223,12 @@
         interior(*inputs, wholes, *kernels, *outs)
         return
 
-    def copied():
+    @pl.when(is_last())
+    def _():
         outs[0][...] = known[0][...]
         outs[1][...] = known[1][...]
 
-    on_last(copied)
-
-    @pl.when(lax.axis_index("video") < lax.axis_size("video") - 1)
+    @pl.when(jnp.logical_not(is_last()))
     def _():
         interior(*inputs, wholes, *kernels, *outs)
 
@@ -251,8 +247,8 @@
 def two_kernel(later, *refs):
     saved_ref, preact_ref, gpre_ref = refs[:3]
     pair_refs, grad_ref = refs[3:5], refs[5]
-    wholes, outs = refs[6 : 6 + later], refs[6 + later : 10 + later]
-    views_ref, act_ref, sums_ref = refs[10 + later :]
+    wholes, outs = refs[6 : 6 + later], refs[6 + later : 8 + later]
+    views_ref, act_ref, sums_ref = refs[8 + later :]
     rows, cols, ch = saved_ref.shape
     step = 4
 
@@ -267,7 +263,7 @@
     grads = [ref[...] for ref in (grad_ref, *wholes)]
     above, below = beside_band(pair_refs, 2)
     kernel_sums(saved_ref, above, below, act_ref[...], grads, views, sums_ref)
-    hand_out(sums_ref, outs)
+    hand_out(sums_ref, *outs)
 
 
 def block_one(saved_ref, preact_ref, pair_refs, mids, temporal_ref, outs, scratch):
@@ -292,39 +288,44 @@
     grads = [ref[...] for ref in mids]
     above, below = beside_band(pair_refs, 3)
     kernel_sums(saved_ref, above, below, act_ref[...], grads, views, sums_ref)
-    hand_out(sums_ref, outs[3:])
+    hand_out(sums_ref, *outs[3:])
 
 
 def one_kernel(later, *refs):
     saved_ref, preact_ref, mid_ref = refs[0], refs[1], refs[4]
     nexts, temporal_ref = refs[5 : 5 + later], refs[5 + later]
-    outs, scratch = refs[6 + later : 13 + later], refs[13 + later :]
+    outs, scratch = refs[6 + later : 11 + later], refs[11 + later :]
     block_one(saved_ref, preact_ref, refs[2:4], [mid_ref, *nexts], temporal_ref, outs, scratch)
 
 
 def mid_one_kernel(*refs):
     grad_ref, pair_refs, (after_inner_ref, after_edge_ref) = refs[0], refs[1:3], refs[5:7]
     temporal_two_ref, spatial_two_ref, saved_ref, preact_ref, temporal_ref = refs[7:12]
-    mid_ref, outs, scratch = refs[12], refs[13:20], refs[20:23]
-    next_ref, edge_views_ref = refs[23:]
+    mid_ref, outs, scratch = refs[12], refs[13:18], refs[18:21]
+    next_ref, edge_ref, edge_views_ref = refs[21:]
     rows = grad_ref.shape[0]
+
+    @pl.when(is_last())
+    def _():
+        edge_ref[...] = jnp.zeros(edge_ref.shape, edge_ref.dtype)
+        next_ref[...] = jnp.zeros(next_ref.shape, next_ref.dtype)
+
+    @pl.when(jnp.logical_not(is_last()))
+    def _():
+        edge_ref[...] = after_edge_ref[...]
+        next_ref[0:1] = after_edge_ref[0:1]
+        next_ref[1 : rows - 1] = after_inner_ref[...]
+        next_ref[rows - 1 : rows] = after_edge_ref[1:2]
+
     mid_kernel(
-        1,
-        *refs[:5],
-        after_edge_ref,
-        temporal_two_ref,
-        spatial_two_ref,
-        mid_ref,
-        edge_views_ref,
-    )
-    next_ref[0:1] = after_edge_ref[0:1]
-    next_ref[1 : rows - 1] = after_inner_ref[...]
-    next_ref[rows - 1 : rows] = after_edge_ref[1:2]
+        1, *refs[:5], edge_ref, temporal_two_ref, spatial_two_ref, mid_ref, edge_views_ref
+    )
     block_one(saved_ref, preact_ref, pair_refs, [mid_ref, next_ref], temporal_ref, outs, scratch)
 
 
-def input_kernel(mid_ref, gpre_ref, one_ref, two_ref, spatial_ref, out_ref, views_ref):
+def input_kernel(mid_ref, gpre_ref, one_ref, two_ref, spatial_ref, out_ref, token_ref, views_ref):
     rows, cols, ch = out_ref.shape
+    token_ref[...] = jnp.zeros(token_ref.shape, token_ref.dtype)
     step = 4
     above, below = beside_band((one_ref, two_ref), 0)
     beside(above.astype(jnp.float32), views_ref, 0)
@@ -341,32 +342,31 @@
         out_ref[here] = convolved(views_ref, spatial_ref, n * step, mid_ref[here])
 
 
-def added(refs, rows):
-    total = refs[0][rows].astype(jnp.float32)
-    for ref in refs[1:]:
-        total = total + ref[rows].astype(jnp.float32)
-    return total
-
-
-def band_kernel(own_ref, *refs):
-    parts, (keep_ref, send_ref) = refs[:3], refs[3:]
-    half = keep_ref.shape[0]
+def pair_kernel(keep_ref, part_ref, own_ref, send_ref):
+    across = lax.axis_index("section") // 2
+    own_ref[...] = keep_ref[across] + part_ref[across].astype(jnp.float32)
+    other = keep_ref[1 - across] + part_ref[1 - across].astype(jnp.float32)
+    send_ref[...] = other.astype(jnp.bfloat16)
+
+
+def band_kernel(one_ref, one_part_ref, two_ref, two_part_ref, keep_ref, send_ref):
+    half = keep_ref.shape[1]
     frame = lax.axis_index("video")
     mine = pl.ds(pl.multiple_of(frame * half, half), half)
     other = pl.ds(pl.multiple_of((1 - frame) * half, half), half)
-    keep_ref[...] = added((own_ref, *parts), mine)
-    send_ref[...] = added((own_ref, *parts), other).astype(jnp.bfloat16)
-
-
-def frame_kernel(keep_ref, part_ref, out_ref):
-    out_ref[...] = (keep_ref[...] + part_ref[...].astype(jnp.float32)).astype(jnp.bfloat16)
-
-
-def clip_kernel(factor, *refs):
-    out_ref = refs[-1]
-    for block in range(2):
-        a, b, c, d = (ref[...].astype(jnp.float32) for ref in refs[4 * block : 4 * block + 4])
-        out_ref[block] = (((a + b) + (c + d)) * factor).astype(jnp.bfloat16)
+    for block, (own, part) in enumerate(((one_ref, one_part_ref), (two_ref, two_part_ref))):
+        keep_ref[block] = own[mine] + part[mine].astype(jnp.float32)
+        send_ref[block] = (own[other] + part[other].astype(jnp.float32)).astype(jnp.bfloat16)
+
+
+def add_kernel(one_ref, two_ref, out_ref):
+    total = one_ref[...].astype(jnp.float32) + two_ref[...].astype(jnp.float32)
+    out_ref[...] = total.astype(jnp.bfloat16)
+
+
+def scaled_kernel(factor, one_ref, two_ref, out_ref):
+    total = one_ref[...].astype(jnp.float32) + two_ref[...].astype(jnp.float32)
+    out_ref[...] = (total * factor).astype(jnp.bfloat16)
 
 
 def join_kernel(own_ref, other_ref, out_ref):
@@ -397,43 +397,36 @@
                     outs[2 * block + 1][here] = share[n, block].astype(jnp.float32)
 
 
-def frames_summed(own, *parts, after=()):
-    height, ch = own.shape
-    half = height // 2
-    outs = [f32(half, ch), bf16(half, ch)]
-    keep, send = call(band_kernel, outs, [], own.size, own, *parts, after=after)
-    other = flipped(send, "video", 1)
-    return call(frame_kernel, [bf16(half, ch)], [], half * ch, keep, other)
+def bands_summed(keep, send):
+    _, height, ch = keep.shape
+    part = flipped(send, "section", 1)
+    outs = [f32(height, ch), bf16(height, ch)]
+    own, across = call(pair_kernel, outs, [], keep.size, keep, part)
+    return own, flipped(across, "section", 2)
 
 
 def totals(one, two, factor, meanwhile):
     height, ch = one[0].shape
-    one, two = (
-        [own] + [flipped(part, "section", flip + 1) for flip, part in enumerate(parts)]
-        for own, *parts in (one, two)
-    )
     if lax.axis_size("video") == 2 and lax.axis_size("dp") == 4:
-        two = frames_summed(*two)
-        one = frames_summed(*one, after=(two,))
-        done = meanwhile((one,))
-        parts = [
-            x
-            for own in (one, two)
-            for x in [own] + [flipped(own, "dp", flip) for flip in range(1, 4)]
-        ]
-        half = height // 2
+        cut = (2, height // 2, ch)
+        size = height * ch
+        keep, send = call(band_kernel, [f32(*cut), bf16(*cut)], [], 2 * size, *one, *two)
+        own = call(add_kernel, [bf16(*cut)], [], size, keep, flipped(send, "video", 1))
+        done, token = meanwhile((own,))
+        own = call(add_kernel, [bf16(*cut)], [], size, own, flipped(own, "dp", 1))
         own = call(
-            functools.partial(clip_kernel, factor),
-            [bf16(2, half, ch)],
+            functools.partial(scaled_kernel, factor),
+            [bf16(*cut)],
             [],
-            8 * height * ch,
-            *parts,
-            after=(done,),
+            size,
+            own,
+            flipped(own, "dp", 2),
+            after=(token,),
         )
         other = flipped(own, "video", 1)
-        share = call(join_kernel, [bf16(2, 2, half, ch)], [], 1, own, other)
+        share = call(join_kernel, [bf16(2, *cut)], [], 1, own, other)
     else:
-        done = meanwhile(())
+        done, _ = meanwhile(())
         own = [sum(x.astype(jnp.float32) for x in parts) for parts in (one, two)]
         share = lax.psum(jnp.stack(own), ("video", "dp")) * factor
         share = share.astype(jnp.bfloat16)[None]
@@ -478,11 +471,16 @@
     edge_views = pltpu.VMEM((6, cols, 3 * ch), jnp.bfloat16)
     act = pltpu.VMEM((rows, cols, ch), jnp.bfloat16)
     sums = pltpu.VMEM((4, 3 * ch, ch), jnp.float32)
-    handed = [f32(3 * ch, ch)] + [bf16(3 * ch, ch)] * 3
+    handed = [f32(2, 3 * ch, ch), bf16(2, 3 * ch, ch)]
     inner_outs = [bf16(rows - 2, cols, ch), bf16(rows, cols, ch)]
     kernels = (temporal_two, spatial_two)
 
-    wholes = [from_ahead(grad, 0, n + 1) for n in range(later)]
+    def from_later(x):
+        if frames == 2:
+            return [flipped(x, "video", 1)]
+        return [from_ahead(x, 0, n + 1) for n in range(later)]
+
+    wholes = from_later(grad)
     packs = call(
         pack_kernel,
         [bf16(4, cols, ch)] * 2,
@@ -492,7 +490,7 @@
         pre_two,
         saved_two,
         saved_one,
-        whole=True,
+        spare_inputs=True,
         limit=58,
     )
     pairs = [paired(pack, start) for start, pack in enumerate(packs)]
@@ -509,7 +507,7 @@
             *kernels,
             after=pairs[:1],
         )
-        after_inner = from_ahead(known[0], 0, 1)
+        (after_inner,) = from_later(known[0])
         edge = call(
             last_edge_kernel,
             [bf16(4, cols, ch)],
@@ -525,7 +523,7 @@
         one, two = (pair[:1] for pair in pairs)
         above, below = jnp.where(odd, one, two), jnp.where(odd, two, one)
         edge = jnp.concatenate([grad[:1], grad[rows - 1 :], above, below])
-    after_edges = [from_ahead(edge, 0, n + 1) for n in range(later)]
+    after_edges = from_later(edge)
     inner, gpre_two = call(
         functools.partial(inner_kernel, later),
         inner_outs,
@@ -549,6 +547,7 @@
         grad,
         *wholes,
     )
+    sums_two = bands_summed(*parts_two)
     mid_inputs = (grad, *pairs, inner, gpre_two)
     one_inputs = (saved_one, pre_one)
     mid_outs = [bf16(rows, cols, ch)]
@@ -557,7 +556,7 @@
         mid, gpre_one, *tail = call(
             mid_one_kernel,
             mid_outs + one_outs,
-            [views, act, sums, act, edge_views],
+            [views, act, sums, act, pltpu.VMEM((4, cols, ch), jnp.bfloat16), edge_views],
             1.5 * conv,
             *mid_inputs,
             after_inner,
@@ -565,6 +564,7 @@
             *kernels,
             *one_inputs,
             temporal_one,
+            after=sums_two[:1],
         )
     else:
         mid = call(
@@ -584,7 +584,7 @@
             *one_inputs,
             *pairs,
             mid,
-            *[from_ahead(mid, 0, n + 1) for n in range(later)],
+            *from_later(mid),
             temporal_one,
         )
     edges_one, parts_one = tail[:2], tail[2:]
@@ -592,7 +592,7 @@
     def input_gradient(after):
         return call(
             input_kernel,
-            [bf16(rows, cols, ch)],
+            [bf16(rows, cols, ch), f32(8, 128)],
             [pltpu.VMEM((rows + 2, cols, 3 * ch), jnp.bfloat16)],
             conv,
             mid,
@@ -602,7 +602,7 @@
             after=after,
         )
 
-    grad_in, sums = totals(parts_one, parts_two, factor, input_gradient)
+    grad_in, sums = totals(bands_summed(*parts_one), sums_two, factor, input_gradient)
     return (grad_in.reshape(shape), *sums)
 
 

time: 66.1 us -> 61.3 us (0.927)
  starting transfers between devices: 33.2 us -> 28.2 us
  waiting for transfers between devices: 16.6 us -> 21.3 us
  Pallas kernels: 13.8 us -> 10.4 us
  local copies, waits for them, and re-layouts: 1 us -> 0.04 us
    ppermute x18 -> x14, waiting for transfers between devices: 12.2 us -> 19.1 us  [flipped(): lax.ppermute(block, axis, [(place ^ flip, place) for place in range(count)])]
    ppermute x3 -> x0, starting transfers between devices: 4 us -> none  [from_ahead(): return lax.ppermute(block, ('section', 'video'), pairs)]
    pallas_call x14 -> x15, Pallas kernels: 13.8 us -> 10.4 us  [call(): pl.pallas_call(body, out_shape=outs[0] if single else tuple(outs), in_spe...]
    ppermute x18 -> x14, starting transfers between devices: 20.5 us -> 17.7 us  [flipped(): lax.ppermute(block, axis, [(place ^ flip, place) for place in range(count)])]
    ppermute x4, starting transfers between devices: 8.75 us -> 10.5 us  [paired(): lax.ppermute(block, 'section', pairs + [(right, left) for left, right in...]
    ppermute x4, waiting for transfers between devices: 3.64 us -> 2.15 us  [paired(): lax.ppermute(block, 'section', pairs + [(right, left) for left, right in...]
    unnamed x22 -> x18, local copies, waits for them, and re-layouts: 1 us -> 0.04 us
    ppermute x3 -> x0, waiting for transfers between devices: 0.8 us -> none  [from_ahead(): return lax.ppermute(block, ('section', 'video'), pairs)]
  transfers between devices with their start and end apart: 25 -> 18, of which waited for: 10 -> 10; matrix products, arithmetic and copies ran while one was open for 0% -> 0% of each run, Pallas kernels for 19% -> 11%
where the time goes in v5:
time: 61.3 us; the launch traced here: 60.7 us
  starting transfers between devices  28.2 us (46%)
  waiting for transfers between devices  21.3 us (35%)
  Pallas kernels  10.4 us (17%)
  between operations  0.84 us (1%)
    ppermute x14, waiting for transfers between devices, flipped(): lax.ppermute(block, axis, [(place ^ flip, place) for place in range(count)])  19.1 us
    ppermute x14, starting transfers between devices, flipped(): lax.ppermute(block, axis, [(place ^ flip, place) for place in range(count)])  17.7 us
    ppermute x4, starting transfers between devices, paired(): lax.ppermute(block, 'section', pairs + [(right, left) for left, right in...  10.5 us
    pallas_call x15, Pallas kernels, call(): pl.pallas_call(body, out_shape=outs[0] if single else tuple(outs), in_spe...  10.4 us
    ppermute x4, waiting for transfers between devices, paired(): lax.ppermute(block, 'section', pairs + [(right, left) for left, right in...  2.15 us
  transfers between devices with their start and end apart: 18, of which 10 were waited for; matrix products, arithmetic and copies ran while one was open for 0% of the time, Pallas kernels for 11%

profile of v5, /device:TPU:1, one launch (start us, length us, event | category | flops | bytes accessed | tf_op | source)
XLA Modules:
  0.0 60.7 jit_solution(5010240958900444501)
XLA Ops:
  0.6 2.1 %collective-permute-start.2 = (bf16[16,64,128]{2,1,0:T(8,128)(2,1)}, bf16[16,64,128]{2,1,0:T(8,128)(2,1)S(1)}, u32[]{:S(2)}, u32[]{:S(2)}) collective-permute-start(bf16[16,64,128]{2,1,0:T(8,128)(2,1)} %bitcast.10), channel_id=1, source_target_pairs={{4,0},{0,4},{5,1},{1,5},{6,2},{2,6},{7,3},{3,7},{12,8},{8,12},{13,... | collective-permute-start | bytes 786440 | tf_op jit(solution)/shard_map/ppermute | solution.py:76
  2.7 1.6 %shard_map.128 = (bf16[4,64,128]{2,1,0:T(8,128)(2,1)}, bf16[4,64,128]{2,1,0:T(8,128)(2,1)}) custom-call(bf16[16,64,128]{2,1,0:T(8,128)(2,1)} %bitcast.11, bf16[16,64,128]{2,1,0:T(8,128)(2,1)} %bitcast.17, bf16[16,64,128]{2,1,0:T(8,128)(2,1)} %bitcast.23, bf16[16,64,128]{2,1,0:T(8,128)(2,1)} %bitcast.21), custom_call_target="tpu_custom_call" | custom-call | flops 1 | bytes 1179648 | tf_op jit(solution)/shard_map/pallas_call | solution.py:38
  4.4 1.0 %collective-permute-start = (bf16[4,64,128]{2,1,0:T(8,128)(2,1)}, bf16[4,64,128]{2,1,0:T(8,128)(2,1)S(1)}, u32[]{:S(2)}, u32[]{:S(2)}) collective-permute-start(bf16[4,64,128]{2,1,0:T(8,128)(2,1)} %get-tuple-element.31), channel_id=1, source_target_pairs={{0,8},{16,24},{8,0},{24,16},{1,9},{17,25},{9,1},{25,17},{2,10},{18... | collective-permute-start | bytes 196616 | tf_op jit(solution)/shard_map/ppermute | solution.py:65
  5.4 3.0 %collective-permute-start.1 = (bf16[4,64,128]{2,1,0:T(8,128)(2,1)}, bf16[4,64,128]{2,1,0:T(8,128)(2,1)S(1)}, u32[]{:S(2)}, u32[]{:S(2)}) collective-permute-start(bf16[4,64,128]{2,1,0:T(8,128)(2,1)} %get-tuple-element.32), channel_id=1, source_target_pairs={{8,16},{16,8},{9,17},{17,9},{10,18},{18,10},{11,19},{19,11},{12,20... | collective-permute-start | bytes 196616 | tf_op jit(solution)/shard_map/ppermute | solution.py:65
  8.5 2.0 %collective-permute-start.3 = (bf16[14,64,128]{2,1,0:T(8,128)(2,1)S(1)}, bf16[14,64,128]{2,1,0:T(8,128)(2,1)S(1)}, u32[]{:S(2)}, u32[]{:S(2)}) collective-permute-start(bf16[14,64,128]{2,1,0:T(8,128)(2,1)S(1)} %get-tuple-element.33.refs_5_), channel_id=1, source_target_pairs={{4,0},{0,4},{5,1},{1,5},{6,2},{2,6},{7,3},{3,7},{12,8},{8,12},{13,... | collective-permute-start | bytes 688136 | tf_op jit(solution)/shard_map/ppermute | solution.py:76
  10.6 1.7 %shard_map.130 = (bf16[14,64,128]{2,1,0:T(8,128)(2,1)S(1)}, bf16[16,64,128]{2,1,0:T(8,128)(2,1)S(1)}) custom-call(bf16[16,64,128]{2,1,0:T(8,128)(2,1)S(1)} %bitcast.13, bf16[16,64,128]{2,1,0:T(8,128)(2,1)S(1)} %bitcast.19, bf16[16,64,128]{2,1,0:T(8,128)(2,1)S(1)} %collective-permute-done.2.refs_2_.refs_6_, bf16[3,128,128]{2,1,0:T(8,128)(2,1)S(1)} %copy-done.5, ...), custom_call_target="tpu_custom_call" | custom-call | flops 362387872 | bytes 2162688 | tf_op jit(solution)/shard_map/pallas_call | solution.py:38
  12.3 1.1 %shard_map.132 = (f32[2,384,128]{2,1,0:T(8,128)S(1)}, bf16[2,384,128]{2,1,0:T(8,128)(2,1)S(1)}) custom-call(bf16[16,64,128]{2,1,0:T(8,128)(2,1)S(1)} %bitcast.24, bf16[16,64,128]{2,1,0:T(8,128)(2,1)S(1)} %bitcast.20, bf16[16,64,128]{2,1,0:T(8,128)(2,1)S(1)} %get-tuple-element.36.refs_2_.refs_4_, ...), custom_call_target="tpu_custom_call" | custom-call | flops 362387872 | bytes 2031616 | tf_op jit(solution)/shard_map/pallas_call | solution.py:38
  13.6 0.8 %collective-permute-start.4 = (bf16[4,64,128]{2,1,0:T(8,128)(2,1)S(1)}, bf16[4,64,128]{2,1,0:T(8,128)(2,1)S(1)}, u32[]{:S(2)}, u32[]{:S(2)}) collective-permute-start(bf16[4,64,128]{2,1,0:T(8,128)(2,1)S(1)} %shard_map.131), channel_id=1, source_target_pairs={{4,0},{0,4},{5,1},{1,5},{6,2},{2,6},{7,3},{3,7},{12,8},{8,12},{13,... | collective-permute-start | bytes 196616 | tf_op jit(solution)/shard_map/ppermute | solution.py:76
  14.4 0.6 %collective-permute-done.5.refs_1_ = bf16[2,384,128]{2,1,0:T(8,128)(2,1)S(1)} collective-permute-done((bf16[2,384,128]{2,1,0:T(8,128)(2,1)S(1)}, bf16[2,384,128]{2,1,0:T(8,128)(2,1)S(1)}, u32[]{:S(2)}, u32[]{:S(2)}) %collective-permute-start.5) | collective-permute-done | bytes 196640 | tf_op jit(solution)/shard_map/ppermute | solution.py:76
  15.0 1.7 %collective-permute-done.4.refs_6_ = bf16[4,64,128]{2,1,0:T(8,128)(2,1)S(1)} collective-permute-done((bf16[4,64,128]{2,1,0:T(8,128)(2,1)S(1)}, bf16[4,64,128]{2,1,0:T(8,128)(2,1)S(1)}, u32[]{:S(2)}, u32[]{:S(2)}) %collective-permute-start.4) | collective-permute-done | bytes 65568 | tf_op jit(solution)/shard_map/ppermute | solution.py:76
  16.8 2.2 %shard_map.134 = (bf16[16,64,128]{2,1,0:T(8,128)(2,1)S(1)}, bf16[16,64,128]{2,1,0:T(8,128)(2,1)S(1)}, bf16[1,64,128]{2,1,0:T(8,128)(2,1)S(1)}, bf16[1,64,128]{2,...) custom-call(bf16[16,64,128]{2,1,0:T(8,128)(2,1)S(1)} %bitcast.16, ...), custom_call_target="tpu_custom_call" | custom-call | flops 452984832 | bytes 3342336 | tf_op jit(solution)/shard_map/pallas_call | solution.py:38
  19.0 1.6 %collective-permute-start.8 = (bf16[2,384,128]{2,1,0:T(8,128)(2,1)S(1)}, bf16[2,384,128]{2,1,0:T(8,128)(2,1)S(1)}, u32[]{:S(2)}, u32[]{:S(2)}) collective-permute-start(bf16[2,384,128]{2,1,0:T(8,128)(2,1)S(1)} %get-tuple-element.45), channel_id=1, source_target_pairs={{8,0},{0,8},{24,16},{16,24},{9,1},{1,9},{25,17},{17,25},{10,2},{2,... | collective-permute-start | bytes 589832 | tf_op jit(solution)/shard_map/ppermute | solution.py:76
  20.6 1.1 %collective-permute-start.10 = (bf16[384,128]{1,0:T(8,128)(2,1)S(1)}, bf16[384,128]{1,0:T(8,128)(2,1)S(1)}, u32[]{:S(2)}, u32[]{:S(2)}) collective-permute-start(bf16[384,128]{1,0:T(8,128)(2,1)S(1)} %get-tuple-element.48), channel_id=1, source_target_pairs={{16,0},{24,8},{0,16},{8,24},{17,1},{25,9},{1,17},{9,25},{18,2},{26... | collective-permute-start | bytes 294920 | tf_op jit(solution)/shard_map/ppermute | solution.py:76
  21.7 1.1 %collective-permute-start.9 = (bf16[384,128]{1,0:T(8,128)(2,1)S(1)}, bf16[384,128]{1,0:T(8,128)(2,1)S(1)}, u32[]{:S(2)}, u32[]{:S(2)}) collective-permute-start(bf16[384,128]{1,0:T(8,128)(2,1)S(1)} %get-tuple-element.47), channel_id=1, source_target_pairs={{16,0},{24,8},{0,16},{8,24},{17,1},{25,9},{1,17},{9,25},{18,2},{26... | collective-permute-start | bytes 294920 | tf_op jit(solution)/shard_map/ppermute | solution.py:76
  22.9 2.1 %collective-permute-done.10.refs_3_ = bf16[384,128]{1,0:T(8,128)(2,1)S(1)} collective-permute-done((bf16[384,128]{1,0:T(8,128)(2,1)S(1)}, bf16[384,128]{1,0:T(8,128)(2,1)S(1)}, u32[]{:S(2)}, u32[]{:S(2)}) %collective-permute-start.10) | collective-permute-done | bytes 98336 | tf_op jit(solution)/shard_map/ppermute | solution.py:76
  25.0 2.1 %collective-permute-done.9.refs_1_ = bf16[384,128]{1,0:T(8,128)(2,1)S(1)} collective-permute-done((bf16[384,128]{1,0:T(8,128)(2,1)S(1)}, bf16[384,128]{1,0:T(8,128)(2,1)S(1)}, u32[]{:S(2)}, u32[]{:S(2)}) %collective-permute-start.9) | collective-permute-done | bytes 98336 | tf_op jit(solution)/shard_map/ppermute | solution.py:76
  27.1 0.6 %collective-permute-start.11 = (bf16[2,192,128]{2,1,0:T(8,128)(2,1)S(1)}, bf16[2,192,128]{2,1,0:T(8,128)(2,1)S(1)}, u32[]{:S(2)}, u32[]{:S(2)}) collective-permute-start(bf16[2,192,128]{2,1,0:T(8,128)(2,1)S(1)} %get-tuple-element.50), channel_id=1, source_target_pairs={{4,0},{0,4},{5,1},{1,5},{6,2},{2,6},{7,3},{3,7},{12,8},{8,12},{13,... | collective-permute-start | bytes 294920 | tf_op jit(solution)/shard_map/ppermute | solution.py:76
  27.7 2.9 %collective-permute-done.11.refs_1_ = bf16[2,192,128]{2,1,0:T(8,128)(2,1)S(1)} collective-permute-done((bf16[2,192,128]{2,1,0:T(8,128)(2,1)S(1)}, bf16[2,192,128]{2,1,0:T(8,128)(2,1)S(1)}, u32[]{:S(2)}, u32[]{:S(2)}) %collective-permute-start.11) | collective-permute-done | bytes 98336 | tf_op jit(solution)/shard_map/ppermute | solution.py:76
  30.7 1.4 %collective-permute-start.12 = (bf16[2,192,128]{2,1,0:T(8,128)(2,1)S(1)}, bf16[2,192,128]{2,1,0:T(8,128)(2,1)S(1)}, u32[]{:S(2)}, u32[]{:S(2)}) collective-permute-start(bf16[2,192,128]{2,1,0:T(8,128)(2,1)S(1)} %shard_map.137.refs_5_.refs_0_), channel_id=1, source_target_pairs={{1,0},{0,1},{3,2},{2,3},{5,4},{4,5},{7,6},{6,7},{9,8},{8,9},{11,10... | collective-permute-start | bytes 294920 | tf_op jit(solution)/shard_map/ppermute | solution.py:76
  32.0 2.2 %collective-permute-done.12.refs_1_ = bf16[2,192,128]{2,1,0:T(8,128)(2,1)S(1)} collective-permute-done((bf16[2,192,128]{2,1,0:T(8,128)(2,1)S(1)}, bf16[2,192,128]{2,1,0:T(8,128)(2,1)S(1)}, u32[]{:S(2)}, u32[]{:S(2)}) %collective-permute-start.12) | collective-permute-done | bytes 98336 | tf_op jit(solution)/shard_map/ppermute | solution.py:76
  34.2 2.4 %collective-permute-start.13 = (bf16[2,192,128]{2,1,0:T(8,128)(2,1)S(1)}, bf16[2,192,128]{2,1,0:T(8,128)(2,1)S(1)}, u32[]{:S(2)}, u32[]{:S(2)}) collective-permute-start(bf16[2,192,128]{2,1,0:T(8,128)(2,1)S(1)} %shard_map.139.refs_0_), channel_id=1, source_target_pairs={{2,0},{3,1},{0,2},{1,3},{6,4},{7,5},{4,6},{5,7},{10,8},{11,9},{8,1... | collective-permute-start | bytes 294920 | tf_op jit(solution)/shard_map/ppermute | solution.py:76
  36.6 3.5 %collective-permute-start.6 = (bf16[1,64,128]{2,1,0:T(8,128)(2,1)S(1)}, bf16[1,64,128]{2,1,0:T(8,128)(2,1)S(1)}, u32[]{:S(2)}, u32[]{:S(2)}) collective-permute-start(bf16[1,64,128]{2,1,0:T(8,128)(2,1)S(1)} %get-tuple-element.42), channel_id=1, source_target_pairs={{0,8},{16,24},{8,0},{24,16},{1,9},{17,25},{9,1},{25,17},{2,10},{18... | collective-permute-start | bytes 49160 | tf_op jit(solution)/shard_map/ppermute | solution.py:65
  40.1 2.9 %collective-permute-start.7 = (bf16[1,64,128]{2,1,0:T(8,128)(2,1)S(1)}, bf16[1,64,128]{2,1,0:T(8,128)(2,1)S(1)}, u32[]{:S(2)}, u32[]{:S(2)}) collective-permute-start(bf16[1,64,128]{2,1,0:T(8,128)(2,1)S(1)} %get-tuple-element.43), channel_id=1, source_target_pairs={{8,16},{16,8},{9,17},{17,9},{10,18},{18,10},{11,19},{19,11},{12,20... | collective-permute-start | bytes 49160 | tf_op jit(solution)/shard_map/ppermute | solution.py:65
  43.0 2.1 %collective-permute-done.7.refs_3_ = bf16[1,64,128]{2,1,0:T(8,128)(2,1)S(1)} collective-permute-done((bf16[1,64,128]{2,1,0:T(8,128)(2,1)S(1)}, bf16[1,64,128]{2,1,0:T(8,128)(2,1)S(1)}, u32[]{:S(2)}, u32[]{:S(2)}) %collective-permute-start.7) | collective-permute-done | bytes 16416 | tf_op jit(solution)/shard_map/ppermute | solution.py:65
  45.1 2.2 %shard_map.138 = (bf16[16,64,128]{2,1,0:T(8,128)(2,1)}, f32[8,128]{1,0:T(8,128)S(1)}) custom-call(bf16[16,64,128]{2,1,0:T(8,128)(2,1)S(1)} %get-tuple-element.40.refs_0_, bf16[16,64,128]{2,1,0:T(8,128)(2,1)S(1)} %get-tuple-element.41.refs_1_, bf16[1,64,128]{2,1,0:T(8,128)(2,1)S(1)} %collective-permute-done.6.refs_2_, ...), custom_call_target="tpu_custom_call" | custom-call | flops 301989888 | bytes 1118208 | tf_op jit(solution)/shard_map/pallas_call | solution.py:38
  47.4 0.6 %collective-permute-start.14 = (bf16[2,192,128]{2,1,0:T(8,128)(2,1)S(1)}, bf16[2,192,128]{2,1,0:T(8,128)(2,1)S(1)}, u32[]{:S(2)}, u32[]{:S(2)}) collective-permute-start(bf16[2,192,128]{2,1,0:T(8,128)(2,1)S(1)} %shard_map.140.refs_0_), channel_id=1, source_target_pairs={{4,0},{0,4},{5,1},{1,5},{6,2},{2,6},{7,3},{3,7},{12,8},{8,12},{13,... | collective-permute-start | bytes 294920 | tf_op jit(solution)/shard_map/ppermute | solution.py:76
  48.0 2.9 %collective-permute-done.14.refs_1_ = bf16[2,192,128]{2,1,0:T(8,128)(2,1)S(1)} collective-permute-done((bf16[2,192,128]{2,1,0:T(8,128)(2,1)S(1)}, bf16[2,192,128]{2,1,0:T(8,128)(2,1)S(1)}, u32[]{:S(2)}, u32[]{:S(2)}) %collective-permute-start.14) | collective-permute-done | bytes 98336 | tf_op jit(solution)/shard_map/ppermute | solution.py:76
  51.1 2.5 %collective-permute-start.15 = (bf16[2,2,192,128]{3,2,1,0:T(8,128)(2,1)S(1)}, bf16[2,2,192,128]{3,2,1,0:T(8,128)(2,1)S(1)}, u32[]{:S(2)}, u32[]{:S(2)}) collective-permute-start(bf16[2,2,192,128]{3,2,1,0:T(8,128)(2,1)S(1)} %shard_map.141.refs_0_), channel_id=1, source_target_pairs={{8,0},{0,8},{24,16},{16,24},{9,1},{1,9},{25,17},{17,25},{10,2},{2,... | collective-permute-start | bytes 589832 | tf_op jit(solution)/shard_map/ppermute | solution.py:76
  53.6 3.4 %collective-permute-done.16.refs_2_ = bf16[2,2,192,128]{3,2,1,0:T(8,128)(2,1)S(1)} collective-permute-done((bf16[2,2,192,128]{3,2,1,0:T(8,128)(2,1)S(1)}, bf16[2,2,192,128]{3,2,1,0:T(8,128)(2,1)S(1)}, u32[]{:S(2)}, u32[]{:S(2)}) %collective-permute-start.16) | collective-permute-done | bytes 196640 | tf_op jit(solution)/shard_map/ppermute | solution.py:76
  57.0 1.4 %collective-permute-start.17 = (bf16[2,2,192,128]{3,2,1,0:T(8,128)(2,1)S(1)}, bf16[2,2,192,128]{3,2,1,0:T(8,128)(2,1)S(1)}, u32[]{:S(2)}, u32[]{:S(2)}) collective-permute-start(bf16[2,2,192,128]{3,2,1,0:T(8,128)(2,1)S(1)} %collective-permute-done.16.refs_2_), channel_id=1, source_target_pairs={{8,0},{0,8},{24,16},{16,24},{9,1},{1,9},{25,17},{17,25},{10,2},{2,... | collective-permute-start | bytes 589832 | tf_op jit(solution)/shard_map/ppermute | solution.py:76
  58.4 1.1 %collective-permute-done.17.refs_3_ = bf16[2,2,192,128]{3,2,1,0:T(8,128)(2,1)S(1)} collective-permute-done((bf16[2,2,192,128]{3,2,1,0:T(8,128)(2,1)S(1)}, bf16[2,2,192,128]{3,2,1,0:T(8,128)(2,1)S(1)}, u32[]{:S(2)}, u32[]{:S(2)}) %collective-permute-start.17) | collective-permute-done | bytes 196640 | tf_op jit(solution)/shard_map/ppermute | solution.py:76
  59.4 1.3 %shard_map.142 = (f32[3,384,128]{2,1,0:T(8,128)}, f32[384,128]{1,0:T(8,128)}, f32[3,384,128]{2,1,0:T(8,128)}, f32[384,128]{1,0:T(8,128)}) custom-call(bf16[2,2,192,128]{3,2,1,0:T(8,128)(2,1)S(1)} %shard_map.141.refs_0_, bf16[2,2,192,128]{3,2,1,0:T(8,128)(2,1)S(1)} %collective-permute-done.15.refs_1_, ...), custom_call_target="tpu_custom_call" | custom-call | flops 98304 | bytes 2359296 | tf_op jit(solution)/shard_map/pallas_call | solution.py:38
  (37 shorter events, 0.4 us)
Async XLA Ops:
  0.6 9.9 %collective-permute-start.2 = (bf16[16,64,128]{2,1,0:T(8,128)(2,1)}, bf16[16,64,128]{2,1,0:T(8,128)(2,1)S(1)}, u32[]{:S(2)}, u32[]{:S(2)}) collective-permute-start(bf16[16,64,128]{2,1,0:T(8,128)(2,1)} %bitcast.10), channel_id=1, source_target_pairs={{4,0},{0,4},{5,1},{1,5},{6,2},{2,6},{7,3},{3,7},{12,8},{8,12},{13,... | collective-permute-start | bytes 786440 | tf_op jit(solution)/shard_map/ppermute | solution.py:76
  2.7 5.7 %copy-start = (bf16[1,1,16,64,128]{4,3,2,1,0:T(8,128)(2,1)S(1)}, bf16[1,1,16,64,128]{4,3,2,1,0:T(8,128)(2,1)}, u32[]{:S(2)}) copy-start(bf16[1,1,16,64,128]{4,3,2,1,0:T(8,128)(2,1)} %param.9) | copy-start | bytes 786436
  2.7 5.7 %copy-start.1 = (bf16[3,3,128,128]{3,2,1,0:T(8,128)(2,1)S(1)}, bf16[3,3,128,128]{3,2,1,0:T(8,128)(2,1)}, u32[]{:S(2)}) copy-start(bf16[3,3,128,128]{3,2,1,0:T(8,128)(2,1)} %refs_8_.1) | copy-start | bytes 884740
  2.7 5.7 %copy-start.2 = (bf16[1,1,16,64,128]{4,3,2,1,0:T(8,128)(2,1)S(1)}, bf16[1,1,16,64,128]{4,3,2,1,0:T(8,128)(2,1)}, u32[]{:S(2)}) copy-start(bf16[1,1,16,64,128]{4,3,2,1,0:T(8,128)(2,1)} %param.13) | copy-start | bytes 786436
  2.7 5.7 %copy-start.5 = (bf16[3,128,128]{2,1,0:T(8,128)(2,1)S(1)}, bf16[3,128,128]{2,1,0:T(8,128)(2,1)}, u32[]{:S(2)}) copy-start(bf16[3,128,128]{2,1,0:T(8,128)(2,1)} %refs_7_.1) | copy-start | bytes 294916
  4.4 4.1 %collective-permute-start = (bf16[4,64,128]{2,1,0:T(8,128)(2,1)}, bf16[4,64,128]{2,1,0:T(8,128)(2,1)S(1)}, u32[]{:S(2)}, u32[]{:S(2)}) collective-permute-start(bf16[4,64,128]{2,1,0:T(8,128)(2,1)} %get-tuple-element.31), channel_id=1, source_target_pairs={{0,8},{16,24},{8,0},{24,16},{1,9},{17,25},{9,1},{25,17},{2,10},{18... | collective-permute-start | bytes 196616 | tf_op jit(solution)/shard_map/ppermute | solution.py:65
  5.4 6.9 %collective-permute-start.1 = (bf16[4,64,128]{2,1,0:T(8,128)(2,1)}, bf16[4,64,128]{2,1,0:T(8,128)(2,1)S(1)}, u32[]{:S(2)}, u32[]{:S(2)}) collective-permute-start(bf16[4,64,128]{2,1,0:T(8,128)(2,1)} %get-tuple-element.32), channel_id=1, source_target_pairs={{8,16},{16,8},{9,17},{17,9},{10,18},{18,10},{11,19},{19,11},{12,20... | collective-permute-start | bytes 196616 | tf_op jit(solution)/shard_map/ppermute | solution.py:65
  8.5 8.3 %collective-permute-start.3 = (bf16[14,64,128]{2,1,0:T(8,128)(2,1)S(1)}, bf16[14,64,128]{2,1,0:T(8,128)(2,1)S(1)}, u32[]{:S(2)}, u32[]{:S(2)}) collective-permute-start(bf16[14,64,128]{2,1,0:T(8,128)(2,1)S(1)} %get-tuple-element.33.refs_5_), channel_id=1, source_target_pairs={{4,0},{0,4},{5,1},{1,5},{6,2},{2,6},{7,3},{3,7},{12,8},{8,12},{13,... | collective-permute-start | bytes 688136 | tf_op jit(solution)/shard_map/ppermute | solution.py:76
  10.5 1.8 %copy-start.4 = (bf16[1,1,16,64,128]{4,3,2,1,0:T(8,128)(2,1)S(1)}, bf16[1,1,16,64,128]{4,3,2,1,0:T(8,128)(2,1)}, u32[]{:S(2)}) copy-start(bf16[1,1,16,64,128]{4,3,2,1,0:T(8,128)(2,1)} %param.12) | copy-start | bytes 786436
  13.5 1.5 %collective-permute-start.5 = (bf16[2,384,128]{2,1,0:T(8,128)(2,1)S(1)}, bf16[2,384,128]{2,1,0:T(8,128)(2,1)S(1)}, u32[]{:S(2)}, u32[]{:S(2)}) collective-permute-start(bf16[2,384,128]{2,1,0:T(8,128)(2,1)S(1)} %get-tuple-element.38), channel_id=1, source_target_pairs={{8,0},{0,8},{24,16},{16,24},{9,1},{1,9},{25,17},{17,25},{10,2},{2,... | collective-permute-start | bytes 589832 | tf_op jit(solution)/shard_map/ppermute | solution.py:76
  13.6 3.2 %copy-start.7 = (bf16[3,128,128]{2,1,0:T(8,128)(2,1)S(1)}, bf16[3,128,128]{2,1,0:T(8,128)(2,1)}, u32[]{:S(2)}) copy-start(bf16[3,128,128]{2,1,0:T(8,128)(2,1)} %refs_11_.1) | copy-start | bytes 294916
  13.6 3.2 %collective-permute-start.4 = (bf16[4,64,128]{2,1,0:T(8,128)(2,1)S(1)}, bf16[4,64,128]{2,1,0:T(8,128)(2,1)S(1)}, u32[]{:S(2)}, u32[]{:S(2)}) collective-permute-start(bf16[4,64,128]{2,1,0:T(8,128)(2,1)S(1)} %shard_map.131), channel_id=1, source_target_pairs={{4,0},{0,4},{5,1},{1,5},{6,2},{2,6},{7,3},{3,7},{12,8},{8,12},{13,... | collective-permute-start | bytes 196616 | tf_op jit(solution)/shard_map/ppermute | solution.py:76
  15.0 1.8 %copy-start.3 = (bf16[1,1,16,64,128]{4,3,2,1,0:T(8,128)(2,1)S(1)}, bf16[1,1,16,64,128]{4,3,2,1,0:T(8,128)(2,1)}, u32[]{:S(2)}) copy-start(bf16[1,1,16,64,128]{4,3,2,1,0:T(8,128)(2,1)} %param.10) | copy-start | bytes 786436
  15.0 1.8 %copy-start.6 = (bf16[1,1,16,64,128]{4,3,2,1,0:T(8,128)(2,1)S(1)}, bf16[1,1,16,64,128]{4,3,2,1,0:T(8,128)(2,1)}, u32[]{:S(2)}) copy-start(bf16[1,1,16,64,128]{4,3,2,1,0:T(8,128)(2,1)} %param.11) | copy-start | bytes 786436
  19.0 2.7 %collective-permute-start.8 = (bf16[2,384,128]{2,1,0:T(8,128)(2,1)S(1)}, bf16[2,384,128]{2,1,0:T(8,128)(2,1)S(1)}, u32[]{:S(2)}, u32[]{:S(2)}) collective-permute-start(bf16[2,384,128]{2,1,0:T(8,128)(2,1)S(1)} %get-tuple-element.45), channel_id=1, source_target_pairs={{8,0},{0,8},{24,16},{16,24},{9,1},{1,9},{25,17},{17,25},{10,2},{2,... | collective-permute-start | bytes 589832 | tf_op jit(solution)/shard_map/ppermute | solution.py:76
  20.6 4.4 %collective-permute-start.10 = (bf16[384,128]{1,0:T(8,128)(2,1)S(1)}, bf16[384,128]{1,0:T(8,128)(2,1)S(1)}, u32[]{:S(2)}, u32[]{:S(2)}) collective-permute-start(bf16[384,128]{1,0:T(8,128)(2,1)S(1)} %get-tuple-element.48), channel_id=1, source_target_pairs={{16,0},{24,8},{0,16},{8,24},{17,1},{25,9},{1,17},{9,25},{18,2},{26... | collective-permute-start | bytes 294920 | tf_op jit(solution)/shard_map/ppermute | solution.py:76
  21.7 5.3 %collective-permute-start.9 = (bf16[384,128]{1,0:T(8,128)(2,1)S(1)}, bf16[384,128]{1,0:T(8,128)(2,1)S(1)}, u32[]{:S(2)}, u32[]{:S(2)}) collective-permute-start(bf16[384,128]{1,0:T(8,128)(2,1)S(1)} %get-tuple-element.47), channel_id=1, source_target_pairs={{16,0},{24,8},{0,16},{8,24},{17,1},{25,9},{1,17},{9,25},{18,2},{26... | collective-permute-start | bytes 294920 | tf_op jit(solution)/shard_map/ppermute | solution.py:76
  27.1 3.5 %collective-permute-start.11 = (bf16[2,192,128]{2,1,0:T(8,128)(2,1)S(1)}, bf16[2,192,128]{2,1,0:T(8,128)(2,1)S(1)}, u32[]{:S(2)}, u32[]{:S(2)}) collective-permute-start(bf16[2,192,128]{2,1,0:T(8,128)(2,1)S(1)} %get-tuple-element.50), channel_id=1, source_target_pairs={{4,0},{0,4},{5,1},{1,5},{6,2},{2,6},{7,3},{3,7},{12,8},{8,12},{13,... | collective-permute-start | bytes 294920 | tf_op jit(solution)/shard_map/ppermute | solution.py:76
  30.6 14.5 %copy-start.8 = (bf16[3,3,128,128]{3,2,1,0:T(8,128)(2,1)S(1)}, bf16[3,3,128,128]{3,2,1,0:T(8,128)(2,1)}, u32[]{:S(2)}) copy-start(bf16[3,3,128,128]{3,2,1,0:T(8,128)(2,1)} %refs_4_.5) | copy-start | bytes 884740
  30.7 3.5 %collective-permute-start.12 = (bf16[2,192,128]{2,1,0:T(8,128)(2,1)S(1)}, bf16[2,192,128]{2,1,0:T(8,128)(2,1)S(1)}, u32[]{:S(2)}, u32[]{:S(2)}) collective-permute-start(bf16[2,192,128]{2,1,0:T(8,128)(2,1)S(1)} %shard_map.137.refs_5_.refs_0_), channel_id=1, source_target_pairs={{1,0},{0,1},{3,2},{2,3},{5,4},{4,5},{7,6},{6,7},{9,8},{8,9},{11,10... | collective-permute-start | bytes 294920 | tf_op jit(solution)/shard_map/ppermute | solution.py:76
  34.2 13.2 %collective-permute-start.13 = (bf16[2,192,128]{2,1,0:T(8,128)(2,1)S(1)}, bf16[2,192,128]{2,1,0:T(8,128)(2,1)S(1)}, u32[]{:S(2)}, u32[]{:S(2)}) collective-permute-start(bf16[2,192,128]{2,1,0:T(8,128)(2,1)S(1)} %shard_map.139.refs_0_), channel_id=1, source_target_pairs={{2,0},{3,1},{0,2},{1,3},{6,4},{7,5},{4,6},{5,7},{10,8},{11,9},{8,1... | collective-permute-start | bytes 294920 | tf_op jit(solution)/shard_map/ppermute | solution.py:76
  36.6 6.4 %collective-permute-start.6 = (bf16[1,64,128]{2,1,0:T(8,128)(2,1)S(1)}, bf16[1,64,128]{2,1,0:T(8,128)(2,1)S(1)}, u32[]{:S(2)}, u32[]{:S(2)}) collective-permute-start(bf16[1,64,128]{2,1,0:T(8,128)(2,1)S(1)} %get-tuple-element.42), channel_id=1, source_target_pairs={{0,8},{16,24},{8,0},{24,16},{1,9},{17,25},{9,1},{25,17},{2,10},{18... | collective-permute-start | bytes 49160 | tf_op jit(solution)/shard_map/ppermute | solution.py:65
  40.1 5.0 %collective-permute-start.7 = (bf16[1,64,128]{2,1,0:T(8,128)(2,1)S(1)}, bf16[1,64,128]{2,1,0:T(8,128)(2,1)S(1)}, u32[]{:S(2)}, u32[]{:S(2)}) collective-permute-start(bf16[1,64,128]{2,1,0:T(8,128)(2,1)S(1)} %get-tuple-element.43), channel_id=1, source_target_pairs={{8,16},{16,8},{9,17},{17,9},{10,18},{18,10},{11,19},{19,11},{12,20... | collective-permute-start | bytes 49160 | tf_op jit(solution)/shard_map/ppermute | solution.py:65
  47.4 3.5 %collective-permute-start.14 = (bf16[2,192,128]{2,1,0:T(8,128)(2,1)S(1)}, bf16[2,192,128]{2,1,0:T(8,128)(2,1)S(1)}, u32[]{:S(2)}, u32[]{:S(2)}) collective-permute-start(bf16[2,192,128]{2,1,0:T(8,128)(2,1)S(1)} %shard_map.140.refs_0_), channel_id=1, source_target_pairs={{4,0},{0,4},{5,1},{1,5},{6,2},{2,6},{7,3},{3,7},{12,8},{8,12},{13,... | collective-permute-start | bytes 294920 | tf_op jit(solution)/shard_map/ppermute | solution.py:76
  51.0 6.0 %collective-permute-start.16 = (bf16[2,2,192,128]{3,2,1,0:T(8,128)(2,1)S(1)}, bf16[2,2,192,128]{3,2,1,0:T(8,128)(2,1)S(1)}, u32[]{:S(2)}, u32[]{:S(2)}) collective-permute-start(bf16[2,2,192,128]{3,2,1,0:T(8,128)(2,1)S(1)} %shard_map.141.refs_0_), channel_id=1, source_target_pairs={{16,0},{24,8},{0,16},{8,24},{17,1},{25,9},{1,17},{9,25},{18,2},{26... | collective-permute-start | bytes 589832 | tf_op jit(solution)/shard_map/ppermute | solution.py:76
  51.1 7.3 %collective-permute-start.15 = (bf16[2,2,192,128]{3,2,1,0:T(8,128)(2,1)S(1)}, bf16[2,2,192,128]{3,2,1,0:T(8,128)(2,1)S(1)}, u32[]{:S(2)}, u32[]{:S(2)}) collective-permute-start(bf16[2,2,192,128]{3,2,1,0:T(8,128)(2,1)S(1)} %shard_map.141.refs_0_), channel_id=1, source_target_pairs={{8,0},{0,8},{24,16},{16,24},{9,1},{1,9},{25,17},{17,25},{10,2},{2,... | collective-permute-start | bytes 589832 | tf_op jit(solution)/shard_map/ppermute | solution.py:76
  57.0 2.4 %collective-permute-start.17 = (bf16[2,2,192,128]{3,2,1,0:T(8,128)(2,1)S(1)}, bf16[2,2,192,128]{3,2,1,0:T(8,128)(2,1)S(1)}, u32[]{:S(2)}, u32[]{:S(2)}) collective-permute-start(bf16[2,2,192,128]{3,2,1,0:T(8,128)(2,1)S(1)} %collective-permute-done.16.refs_2_), channel_id=1, source_target_pairs={{8,0},{0,8},{24,16},{16,24},{9,1},{1,9},{25,17},{17,25},{10,2},{2,... | collective-permute-start | bytes 589832 | tf_op jit(solution)/shard_map/ppermute | solution.py:76

commit v6 on v5

--- a/solution.py
+++ b/solution.py
@@ -142,9 +142,10 @@
 
 def hand_out(sums_ref, keep_ref, send_ref):
     odd = lax.rem(lax.axis_index("section"), 2)
+    height = sums_ref.shape[1]
     for n in range(2):
         keep_ref[n] = sums_ref[2 * n + odd]
-        send_ref[n] = sums_ref[2 * n + 1 - odd].astype(jnp.bfloat16)
+        send_ref[n * height : (n + 1) * height] = sums_ref[2 * n + 1 - odd].astype(jnp.bfloat16)
 
 
 def pack_kernel(*refs):
@@ -187,8 +188,8 @@
 def edge_rows(grad_ref, pair_refs, afters, gpre_ref, temporal_ref, spatial_ref, views_ref):
     rows, cols, ch = grad_ref.shape
     (grad_above, grad_below), (above_pre, below_pre) = (beside_band(pair_refs, n) for n in (0, 1))
-    above = [grad_above] + [ref[2:3] for ref in afters]
-    below = [grad_below] + [ref[3:4] for ref in afters]
+    above = [grad_above] + [ref[0:1] for ref in afters]
+    below = [grad_below] + [ref[1:2] for ref in afters]
     beside(pre_gradient(above, above_pre, temporal_ref), views_ref, 0)
     beside(gpre_ref[0:2].astype(jnp.float32), views_ref, 1)
     beside(gpre_ref[rows - 2 : rows].astype(jnp.float32), views_ref, 3)
@@ -207,13 +208,18 @@
         )
 
 
-def last_edge_kernel(grad_ref, one_ref, two_ref, gpre_ref, temporal_ref, spatial_ref, edge_ref, views_ref):
+def last_mid_kernel(grad_ref, one_ref, two_ref, inner_ref, gpre_ref, temporal_ref, spatial_ref, sent_ref, views_ref):
+    rows = grad_ref.shape[0]
+
     @pl.when(is_last())
     def _():
-        edge_ref[0:1], edge_ref[1:2] = edge_rows(
+        sent_ref[0:1], sent_ref[rows - 1 : rows] = edge_rows(
             grad_ref, (one_ref, two_ref), [], gpre_ref, temporal_ref, spatial_ref, views_ref
         )
-        edge_ref[2:3], edge_ref[3:4] = beside_band((one_ref, two_ref), 0)
+        sent_ref[1 : rows - 1] = inner_ref[...]
+        sent_ref[rows : rows + 1], sent_ref[rows + 1 : rows + 2] = beside_band(
+            (one_ref, two_ref), 0
+        )
 
 
 def inner_kernel(later, *refs):
@@ -267,7 +273,7 @@
 
 
 def block_one(saved_ref, preact_ref, pair_refs, mids, temporal_ref, outs, scratch):
-    gpre_ref, edge_refs = outs[0], outs[1:3]
+    gpre_ref, keep_ref, send_ref = outs
     views_ref, act_ref, sums_ref = scratch
     rows, cols, ch = saved_ref.shape
     step = 4
@@ -282,28 +288,29 @@
         act_ref[here] = (hval * sigmoid(hval)).astype(jnp.bfloat16)
 
     odd = lax.rem(lax.axis_index("section"), 2)
-    edge_refs[0][...] = gpre_ref[pl.ds((1 - odd) * (rows - 1), 1)]
-    edge_refs[1][...] = gpre_ref[pl.ds(odd * (rows - 1), 1)]
+    size = send_ref.shape[0] - 2 * cols
+    send_ref[size : size + cols] = gpre_ref[(1 - odd) * (rows - 1)]
+    send_ref[size + cols : size + 2 * cols] = gpre_ref[odd * (rows - 1)]
     views = views_ref[...].reshape(rows * cols, 3 * ch)
     grads = [ref[...] for ref in mids]
     above, below = beside_band(pair_refs, 3)
     kernel_sums(saved_ref, above, below, act_ref[...], grads, views, sums_ref)
-    hand_out(sums_ref, *outs[3:])
+    hand_out(sums_ref, keep_ref, send_ref)
 
 
 def one_kernel(later, *refs):
     saved_ref, preact_ref, mid_ref = refs[0], refs[1], refs[4]
     nexts, temporal_ref = refs[5 : 5 + later], refs[5 + later]
-    outs, scratch = refs[6 + later : 11 + later], refs[11 + later :]
+    outs, scratch = refs[6 + later : 9 + later], refs[9 + later :]
     block_one(saved_ref, preact_ref, refs[2:4], [mid_ref, *nexts], temporal_ref, outs, scratch)
 
 
 def mid_one_kernel(*refs):
-    grad_ref, pair_refs, (after_inner_ref, after_edge_ref) = refs[0], refs[1:3], refs[5:7]
-    temporal_two_ref, spatial_two_ref, saved_ref, preact_ref, temporal_ref = refs[7:12]
-    mid_ref, outs, scratch = refs[12], refs[13:18], refs[18:21]
-    next_ref, edge_ref, edge_views_ref = refs[21:]
-    rows = grad_ref.shape[0]
+    pair_refs, after_ref = refs[1:3], refs[5]
+    temporal_two_ref, spatial_two_ref, saved_ref, preact_ref, temporal_ref = refs[6:11]
+    mid_ref, outs, scratch = refs[11], refs[12:15], refs[15:18]
+    next_ref, edge_ref, edge_views_ref = refs[18:]
+    rows = next_ref.shape[0]
 
     @pl.when(is_last())
     def _():
@@ -312,10 +319,8 @@
 
     @pl.when(jnp.logical_not(is_last()))
     def _():
-        edge_ref[...] = after_edge_ref[...]
-        next_ref[0:1] = after_edge_ref[0:1]
-        next_ref[1 : rows - 1] = after_inner_ref[...]
-        next_ref[rows - 1 : rows] = after_edge_ref[1:2]
+        next_ref[...] = after_ref[:rows]
+        edge_ref[...] = after_ref[rows:]
 
     mid_kernel(
         1, *refs[:5], edge_ref, temporal_two_ref, spatial_two_ref, mid_ref, edge_views_ref
@@ -323,13 +328,18 @@
     block_one(saved_ref, preact_ref, pair_refs, [mid_ref, next_ref], temporal_ref, outs, scratch)
 
 
-def input_kernel(mid_ref, gpre_ref, one_ref, two_ref, spatial_ref, out_ref, token_ref, views_ref):
+def input_kernel(mid_ref, gpre_ref, pair_ref, across_ref, spatial_ref, out_ref, token_ref, views_ref):
     rows, cols, ch = out_ref.shape
+    band, bands = lax.axis_index("section"), lax.axis_size("section")
+    first = pair_ref[pair_ref.shape[0] - 2 * cols : pair_ref.shape[0] - cols]
+    second = across_ref[across_ref.shape[0] - cols :]
+    second = jnp.where((band > 0) & (band < bands - 1), second, jnp.zeros_like(second))
+    odd = lax.rem(band, 2) == 1
+    above, below = jnp.where(odd, first, second), jnp.where(odd, second, first)
     token_ref[...] = jnp.zeros(token_ref.shape, token_ref.dtype)
     step = 4
-    above, below = beside_band((one_ref, two_ref), 0)
-    beside(above.astype(jnp.float32), views_ref, 0)
-    beside(below.astype(jnp.float32), views_ref, rows + 1)
+    beside(above.astype(jnp.float32)[None], views_ref, 0)
+    beside(below.astype(jnp.float32)[None], views_ref, rows + 1)
 
     @pl.loop(0, rows // step)
     def _(n):
@@ -343,10 +353,16 @@
 
 
 def pair_kernel(keep_ref, part_ref, own_ref, send_ref):
+    _, height, _ = keep_ref.shape
     across = lax.axis_index("section") // 2
-    own_ref[...] = keep_ref[across] + part_ref[across].astype(jnp.float32)
-    other = keep_ref[1 - across] + part_ref[1 - across].astype(jnp.float32)
-    send_ref[...] = other.astype(jnp.bfloat16)
+    other = 1 - across
+    part = part_ref[pl.ds(pl.multiple_of(across * height, height), height)]
+    own_ref[...] = keep_ref[across] + part.astype(jnp.float32)
+    part = part_ref[pl.ds(pl.multiple_of(other * height, height), height)]
+    send_ref[:height] = (keep_ref[other] + part.astype(jnp.float32)).astype(jnp.bfloat16)
+    rest = send_ref.shape[0] - height
+    if rest:
+        send_ref[height:] = part_ref[2 * height + rest :]
 
 
 def band_kernel(one_ref, one_part_ref, two_ref, two_part_ref, keep_ref, send_ref):
@@ -369,40 +385,34 @@
     out_ref[...] = (total * factor).astype(jnp.bfloat16)
 
 
-def join_kernel(own_ref, other_ref, out_ref):
-    frame = lax.axis_index("video")
-    out_ref[frame] = own_ref[...]
-    out_ref[1 - frame] = other_ref[...]
-
-
 def place_kernel(*refs):
-    shares, outs = refs[:4], refs[4:]
-    band = lax.axis_index("section")
-    parts, _, height, _ = shares[0].shape
-    for flip, share in enumerate(shares):
-        place = jnp.bitwise_xor(band, flip)
+    shares, outs = refs[:-4], refs[-4:]
+    band, frame = lax.axis_index("section"), lax.axis_index("video")
+    halves = len(shares) // 4
+    height = shares[0].shape[1]
+    for n, share in enumerate(shares):
+        place = jnp.bitwise_xor(band, n // halves)
+        half = jnp.bitwise_xor(frame, n % halves) if halves == 2 else 0
+        here = pl.ds(pl.multiple_of(half * height, height), height)
 
         @pl.when(place < 3)
         def _():
             for block in range(2):
-                for n in range(parts):
-                    here = slice(n * height, (n + 1) * height)
-                    outs[2 * block][place, here] = share[n, block].astype(jnp.float32)
+                outs[2 * block][place, here] = share[block].astype(jnp.float32)
 
         @pl.when(place == 3)
         def _():
             for block in range(2):
-                for n in range(parts):
-                    here = slice(n * height, (n + 1) * height)
-                    outs[2 * block + 1][here] = share[n, block].astype(jnp.float32)
-
-
-def bands_summed(keep, send):
+                outs[2 * block + 1][here] = share[block].astype(jnp.float32)
+
+
+def bands_summed(keep, send, after=()):
     _, height, ch = keep.shape
-    part = flipped(send, "section", 1)
-    outs = [f32(height, ch), bf16(height, ch)]
-    own, across = call(pair_kernel, outs, [], keep.size, keep, part)
-    return own, flipped(across, "section", 2)
+    rest = (send.shape[0] - 2 * height) // 2
+    pair = flipped(send, "section", 1)
+    outs = [f32(height, ch), bf16(height + rest, ch)]
+    own, across = call(pair_kernel, outs, [], keep.size, keep, pair, after=after)
+    return own, flipped(across, "section", 2), pair
 
 
 def totals(one, two, factor, meanwhile):
@@ -410,7 +420,8 @@
     if lax.axis_size("video") == 2 and lax.axis_size("dp") == 4:
         cut = (2, height // 2, ch)
         size = height * ch
-        keep, send = call(band_kernel, [f32(*cut), bf16(*cut)], [], 2 * size, *one, *two)
+        operands = (*one[:2], *two[:2])
+        keep, send = call(band_kernel, [f32(*cut), bf16(*cut)], [], 2 * size, *operands)
         own = call(add_kernel, [bf16(*cut)], [], size, keep, flipped(send, "video", 1))
         done, token = meanwhile((own,))
         own = call(add_kernel, [bf16(*cut)], [], size, own, flipped(own, "dp", 1))
@@ -423,23 +434,22 @@
             flipped(own, "dp", 2),
             after=(token,),
         )
-        other = flipped(own, "video", 1)
-        share = call(join_kernel, [bf16(2, *cut)], [], 1, own, other)
+        shares = [own, flipped(own, "video", 1)]
     else:
         done, _ = meanwhile(())
-        own = [sum(x.astype(jnp.float32) for x in parts) for parts in (one, two)]
+        own = [x[0] + x[1][:height].astype(jnp.float32) for x in (one, two)]
         share = lax.psum(jnp.stack(own), ("video", "dp")) * factor
-        share = share.astype(jnp.bfloat16)[None]
-    across = flipped(share, "section", 2)
+        shares = [share.astype(jnp.bfloat16)]
+    across = [flipped(share, "section", 2) for share in shares]
     outs = call(
         place_kernel,
         [f32(3, height, ch), f32(height, ch)] * 2,
         [],
-        share.size,
-        share,
-        flipped(share, "section", 1),
-        across,
-        flipped(across, "section", 1),
+        4 * height * ch,
+        *shares,
+        *[flipped(share, "section", 1) for share in shares],
+        *across,
+        *[flipped(share, "section", 1) for share in across],
     )
     outs = [x.reshape(3, 3, ch, ch) if x.ndim == 3 else x.reshape(3, ch, ch) for x in outs]
     return done, outs
@@ -471,7 +481,7 @@
     edge_views = pltpu.VMEM((6, cols, 3 * ch), jnp.bfloat16)
     act = pltpu.VMEM((rows, cols, ch), jnp.bfloat16)
     sums = pltpu.VMEM((4, 3 * ch, ch), jnp.float32)
-    handed = [f32(2, 3 * ch, ch), bf16(2, 3 * ch, ch)]
+    handed = [f32(2, 3 * ch, ch), bf16(6 * ch, ch)]
     inner_outs = [bf16(rows - 2, cols, ch), bf16(rows, cols, ch)]
     kernels = (temporal_two, spatial_two)
 
@@ -507,23 +517,22 @@
             *kernels,
             after=pairs[:1],
         )
-        (after_inner,) = from_later(known[0])
-        edge = call(
-            last_edge_kernel,
-            [bf16(4, cols, ch)],
+        sent = call(
+            last_mid_kernel,
+            [bf16(rows + 2, cols, ch)],
             [edge_views],
             conv // 8,
             grad,
             *pairs,
-            known[1],
+            *known,
             *kernels,
         )
+        afters = from_later(sent)
     else:
         odd = lax.rem(lax.axis_index("section"), 2) == 1
         one, two = (pair[:1] for pair in pairs)
         above, below = jnp.where(odd, one, two), jnp.where(odd, two, one)
-        edge = jnp.concatenate([grad[:1], grad[rows - 1 :], above, below])
-    after_edges = from_later(edge)
+        afters = from_later(jnp.concatenate([above, below]))
     inner, gpre_two = call(
         functools.partial(inner_kernel, later),
         inner_outs,
@@ -534,6 +543,7 @@
         *wholes,
         *kernels,
         *known,
+        after=(sent,) if frames == 2 else (),
     )
     parts_two = call(
         functools.partial(two_kernel, later),
@@ -551,16 +561,15 @@
     mid_inputs = (grad, *pairs, inner, gpre_two)
     one_inputs = (saved_one, pre_one)
     mid_outs = [bf16(rows, cols, ch)]
-    one_outs = [bf16(rows, cols, ch)] + [bf16(1, cols, ch)] * 2 + handed
+    one_outs = [bf16(rows, cols, ch), f32(2, 3 * ch, ch), bf16(6 * ch + 2 * cols, ch)]
     if frames == 2:
-        mid, gpre_one, *tail = call(
+        mid, gpre_one, *parts_one = call(
             mid_one_kernel,
             mid_outs + one_outs,
-            [views, act, sums, act, pltpu.VMEM((4, cols, ch), jnp.bfloat16), edge_views],
+            [views, act, sums, act, pltpu.VMEM((2, cols, ch), jnp.bfloat16), edge_views],
             1.5 * conv,
             *mid_inputs,
-            after_inner,
-            *after_edges,
+            *afters,
             *kernels,
             *one_inputs,
             temporal_one,
@@ -573,10 +582,10 @@
             [edge_views],
             conv // 8,
             *mid_inputs,
-            *after_edges,
+            *afters,
             *kernels,
         )
-        gpre_one, *tail = call(
+        gpre_one, *parts_one = call(
             functools.partial(one_kernel, later),
             one_outs,
             [views, act, sums],
@@ -587,7 +596,10 @@
             *from_later(mid),
             temporal_one,
         )
-    edges_one, parts_one = tail[:2], tail[2:]
+    keep, send = parts_one
+    send, across = lax.optimization_barrier((send, sums_two[1]))
+    sums_two = (sums_two[0], across)
+    sums_one = bands_summed(keep, send)
 
     def input_gradient(after):
         return call(
@@ -597,12 +609,13 @@
             conv,
             mid,
             gpre_one,
-            *[paired(edge, start) for start, edge in enumerate(edges_one)],
+            sums_one[2],
+            sums_one[1],
             spatial_one,
             after=after,
         )
 
-    grad_in, sums = totals(bands_summed(*parts_one), sums_two, factor, input_gradient)
+    grad_in, sums = totals(sums_one, sums_two, factor, input_gradient)
     return (grad_in.reshape(shape), *sums)
 
 

time: 61.3 us -> 56.9 us (0.928)
  waiting for transfers between devices: 21.3 us -> 18.1 us
  starting transfers between devices: 28.2 us -> 27 us
    ppermute x4 -> x2, starting transfers between devices: 10.5 us -> 4.07 us  [paired(): lax.ppermute(block, 'section', pairs + [(right, left) for left, right in...]
    ppermute x14 -> x16, starting transfers between devices: 17.7 us -> 22.9 us  [flipped(): lax.ppermute(block, axis, [(place ^ flip, place) for place in range(count)])]
    ppermute x14 -> x16, waiting for transfers between devices: 19.1 us -> 15.1 us  [flipped(): lax.ppermute(block, axis, [(place ^ flip, place) for place in range(count)])]
    ppermute x4 -> x2, waiting for transfers between devices: 2.15 us -> 2.95 us  [paired(): lax.ppermute(block, 'section', pairs + [(right, left) for left, right in...]
    pallas_call x15 -> x14, Pallas kernels: 10.4 us -> 10.4 us  [call(): pl.pallas_call(body, out_shape=outs[0] if single else tuple(outs), in_spe...]
  transfers between devices with their start and end apart: 18 -> 18, of which waited for: 10 -> 9; matrix products, arithmetic and copies ran while one was open for 0% -> 0% of each run, Pallas kernels for 11% -> 16%
where the time goes in v6:
time: 56.9 us; the launch traced here: 56.3 us
  starting transfers between devices  27 us (47%)
  waiting for transfers between devices  18.1 us (32%)
  Pallas kernels  10.4 us (18%)
  between operations  0.81 us (1%)
    ppermute x16, starting transfers between devices, flipped(): lax.ppermute(block, axis, [(place ^ flip, place) for place in range(count)])  22.9 us
    ppermute x16, waiting for transfers between devices, flipped(): lax.ppermute(block, axis, [(place ^ flip, place) for place in range(count)])  15.1 us
    pallas_call x14, Pallas kernels, call(): pl.pallas_call(body, out_shape=outs[0] if single else tuple(outs), in_spe...  10.4 us
    ppermute x2, starting transfers between devices, paired(): lax.ppermute(block, 'section', pairs + [(right, left) for left, right in...  4.07 us
    ppermute x2, waiting for transfers between devices, paired(): lax.ppermute(block, 'section', pairs + [(right, left) for left, right in...  2.95 us
  transfers between devices with their start and end apart: 18, of which 9 were waited for; matrix products, arithmetic and copies ran while one was open for 0% of the time, Pallas kernels for 16%

profile of v6, /device:TPU:1, one launch (start us, length us, event | category | flops | bytes accessed | tf_op | source)
XLA Modules:
  0.0 56.3 jit_solution(3063303980717634656)
XLA Ops:
  0.6 2.1 %collective-permute-start.2 = (bf16[16,64,128]{2,1,0:T(8,128)(2,1)}, bf16[16,64,128]{2,1,0:T(8,128)(2,1)S(1)}, u32[]{:S(2)}, u32[]{:S(2)}) collective-permute-start(bf16[16,64,128]{2,1,0:T(8,128)(2,1)} %bitcast.10), channel_id=1, source_target_pairs={{4,0},{0,4},{5,1},{1,5},{6,2},{2,6},{7,3},{3,7},{12,8},{8,12},{13,... | collective-permute-start | bytes 786440 | tf_op jit(solution)/shard_map/ppermute | solution.py:76
  2.7 1.6 %shard_map.128 = (bf16[4,64,128]{2,1,0:T(8,128)(2,1)}, bf16[4,64,128]{2,1,0:T(8,128)(2,1)}) custom-call(bf16[16,64,128]{2,1,0:T(8,128)(2,1)} %bitcast.11, bf16[16,64,128]{2,1,0:T(8,128)(2,1)} %bitcast.17, bf16[16,64,128]{2,1,0:T(8,128)(2,1)} %bitcast.23, bf16[16,64,128]{2,1,0:T(8,128)(2,1)} %bitcast.21), custom_call_target="tpu_custom_call" | custom-call | flops 1 | bytes 1179648 | tf_op jit(solution)/shard_map/pallas_call | solution.py:38
  4.4 1.0 %collective-permute-start = (bf16[4,64,128]{2,1,0:T(8,128)(2,1)}, bf16[4,64,128]{2,1,0:T(8,128)(2,1)S(1)}, u32[]{:S(2)}, u32[]{:S(2)}) collective-permute-start(bf16[4,64,128]{2,1,0:T(8,128)(2,1)} %get-tuple-element.31), channel_id=1, source_target_pairs={{0,8},{16,24},{8,0},{24,16},{1,9},{17,25},{9,1},{25,17},{2,10},{18... | collective-permute-start | bytes 196616 | tf_op jit(solution)/shard_map/ppermute | solution.py:65
  5.4 3.0 %collective-permute-start.1 = (bf16[4,64,128]{2,1,0:T(8,128)(2,1)}, bf16[4,64,128]{2,1,0:T(8,128)(2,1)S(1)}, u32[]{:S(2)}, u32[]{:S(2)}) collective-permute-start(bf16[4,64,128]{2,1,0:T(8,128)(2,1)} %get-tuple-element.32), channel_id=1, source_target_pairs={{8,16},{16,8},{9,17},{17,9},{10,18},{18,10},{11,19},{19,11},{12,20... | collective-permute-start | bytes 196616 | tf_op jit(solution)/shard_map/ppermute | solution.py:65
  8.5 2.9 %collective-permute-done.1.refs_2_.refs_4_ = bf16[4,64,128]{2,1,0:T(8,128)(2,1)S(1)} collective-permute-done((bf16[4,64,128]{2,1,0:T(8,128)(2,1)}, bf16[4,64,128]{2,1,0:T(8,128)(2,1)S(1)}, u32[]{:S(2)}, u32[]{:S(2)}) %collective-permute-start.1) | collective-permute-done | bytes 65568 | tf_op jit(solution)/shard_map/ppermute | solution.py:65
  11.5 0.3 collective-permute-start.3
  11.8 1.7 %shard_map.131 = (bf16[14,64,128]{2,1,0:T(8,128)(2,1)S(1)}, bf16[16,64,128]{2,1,0:T(8,128)(2,1)S(1)}) custom-call(bf16[16,64,128]{2,1,0:T(8,128)(2,1)S(1)} %bitcast.14, bf16[16,64,128]{2,1,0:T(8,128)(2,1)S(1)} %bitcast.19, bf16[16,64,128]{2,1,0:T(8,128)(2,1)S(1)} %collective-permute-done.2.refs_2_.refs_6_, bf16[3,128,128]{2,1,0:T(8,128)(2,1)S(1)} %copy-done.5, ...), custom_call_target="tpu_custom_call" | custom-call | flops 362387872 | bytes 2162688 | tf_op jit(solution)/shard_map/pallas_call | solution.py:38
  13.5 1.1 %shard_map.132 = (f32[2,384,128]{2,1,0:T(8,128)S(1)}, bf16[768,128]{1,0:T(8,128)(2,1)S(1)}) custom-call(bf16[16,64,128]{2,1,0:T(8,128)(2,1)S(1)} %bitcast.24, bf16[16,64,128]{2,1,0:T(8,128)(2,1)S(1)} %bitcast.20, bf16[16,64,128]{2,1,0:T(8,128)(2,1)S(1)} %get-tuple-element.36.refs_2_.refs_4_, ...), custom_call_target="tpu_custom_call" | custom-call | flops 362387872 | bytes 2031616 | tf_op jit(solution)/shard_map/pallas_call | solution.py:38
  14.7 0.1 collective-permute-start.4
  14.8 1.4 %collective-permute-done.4.refs_1_ = bf16[768,128]{1,0:T(8,128)(2,1)S(1)} collective-permute-done((bf16[768,128]{1,0:T(8,128)(2,1)S(1)}, bf16[768,128]{1,0:T(8,128)(2,1)S(1)}, u32[]{:S(2)}, u32[]{:S(2)}) %collective-permute-start.4) | collective-permute-done | bytes 196640 | tf_op jit(solution)/shard_map/ppermute | solution.py:76
  16.2 1.4 %collective-permute-start.5 = (bf16[384,128]{1,0:T(8,128)(2,1)S(1)}, bf16[384,128]{1,0:T(8,128)(2,1)S(1)}, u32[]{:S(2)}, u32[]{:S(2)}) collective-permute-start(bf16[384,128]{1,0:T(8,128)(2,1)S(1)} %get-tuple-element.43), channel_id=1, source_target_pairs={{16,0},{24,8},{0,16},{8,24},{17,1},{25,9},{1,17},{9,25},{18,2},{26... | collective-permute-start | bytes 294920 | tf_op jit(solution)/shard_map/ppermute | solution.py:76
  17.7 2.2 %shard_map.134 = (bf16[16,64,128]{2,1,0:T(8,128)(2,1)S(1)}, bf16[16,64,128]{2,1,0:T(8,128)(2,1)S(1)}, f32[2,384,128]{2,1,0:T(8,128)S(1)}, bf16[896,128]{1,0:T(8,128)(2,1)S(1)}) custom-call(bf16[16,64,128]{2,1,0:T(8,128)(2,1)S(1)} %bitcast.16, bf16[4,64,128]{2,1,0:T(8,128)(2,1)S(1)} %collective-permute-done.refs_4_.refs_1_.refs_3_, ...), custom_call_target="tpu_custom_call" | custom-call | flops 452984832 | bytes 3342336 | tf_op jit(solution)/shard_map/pallas_call | solution.py:38
  19.9 0.7 %collective-permute-done.5.refs_3_ = bf16[384,128]{1,0:T(8,128)(2,1)S(1)} collective-permute-done((bf16[384,128]{1,0:T(8,128)(2,1)S(1)}, bf16[384,128]{1,0:T(8,128)(2,1)S(1)}, u32[]{:S(2)}, u32[]{:S(2)}) %collective-permute-start.5) | collective-permute-done | bytes 98336 | tf_op jit(solution)/shard_map/ppermute | solution.py:76
  20.6 1.0 %collective-permute-start.6 = (bf16[896,128]{1,0:T(8,128)(2,1)S(1)}, bf16[896,128]{1,0:T(8,128)(2,1)S(1)}, u32[]{:S(2)}, u32[]{:S(2)}) collective-permute-start(bf16[896,128]{1,0:T(8,128)(2,1)S(1)} %get-tuple-element.44), channel_id=1, source_target_pairs={{8,0},{0,8},{24,16},{16,24},{9,1},{1,9},{25,17},{17,25},{10,2},{2,... | collective-permute-start | bytes 688136 | tf_op jit(solution)/shard_map/ppermute | solution.py:76
  21.5 1.1 %collective-permute-done.6.refs_1_.refs_2_ = bf16[896,128]{1,0:T(8,128)(2,1)S(1)} collective-permute-done((bf16[896,128]{1,0:T(8,128)(2,1)S(1)}, bf16[896,128]{1,0:T(8,128)(2,1)S(1)}, u32[]{:S(2)}, u32[]{:S(2)}) %collective-permute-start.6) | collective-permute-done | bytes 229408 | tf_op jit(solution)/shard_map/ppermute | solution.py:76
  22.7 1.4 %collective-permute-start.7 = (bf16[448,128]{1,0:T(8,128)(2,1)S(1)}, bf16[448,128]{1,0:T(8,128)(2,1)S(1)}, u32[]{:S(2)}, u32[]{:S(2)}) collective-permute-start(bf16[448,128]{1,0:T(8,128)(2,1)S(1)} %get-tuple-element.46), channel_id=1, source_target_pairs={{16,0},{24,8},{0,16},{8,24},{17,1},{25,9},{1,17},{9,25},{18,2},{26... | collective-permute-start | bytes 344072 | tf_op jit(solution)/shard_map/ppermute | solution.py:76
  24.1 3.0 %collective-permute-done.7.refs_1_.refs_3_ = bf16[448,128]{1,0:T(8,128)(2,1)S(1)} collective-permute-done((bf16[448,128]{1,0:T(8,128)(2,1)S(1)}, bf16[448,128]{1,0:T(8,128)(2,1)S(1)}, u32[]{:S(2)}, u32[]{:S(2)}) %collective-permute-start.7) | collective-permute-done | bytes 114720 | tf_op jit(solution)/shard_map/ppermute | solution.py:76
  27.1 0.1 collective-permute-start.8
  27.2 3.5 %collective-permute-done.8.refs_1_ = bf16[2,192,128]{2,1,0:T(8,128)(2,1)S(1)} collective-permute-done((bf16[2,192,128]{2,1,0:T(8,128)(2,1)S(1)}, bf16[2,192,128]{2,1,0:T(8,128)(2,1)S(1)}, u32[]{:S(2)}, u32[]{:S(2)}) %collective-permute-start.8) | collective-permute-done | bytes 98336 | tf_op jit(solution)/shard_map/ppermute | solution.py:76
  30.7 1.6 %collective-permute-start.9 = (bf16[2,192,128]{2,1,0:T(8,128)(2,1)S(1)}, bf16[2,192,128]{2,1,0:T(8,128)(2,1)S(1)}, u32[]{:S(2)}, u32[]{:S(2)}) collective-permute-start(bf16[2,192,128]{2,1,0:T(8,128)(2,1)S(1)} %shard_map.137.refs_5_.refs_0_), channel_id=1, source_target_pairs={{1,0},{0,1},{3,2},{2,3},{5,4},{4,5},{7,6},{6,7},{9,8},{8,9},{11,10... | collective-permute-start | bytes 294920 | tf_op jit(solution)/shard_map/ppermute | solution.py:76
  32.3 2.0 %collective-permute-done.9.refs_1_ = bf16[2,192,128]{2,1,0:T(8,128)(2,1)S(1)} collective-permute-done((bf16[2,192,128]{2,1,0:T(8,128)(2,1)S(1)}, bf16[2,192,128]{2,1,0:T(8,128)(2,1)S(1)}, u32[]{:S(2)}, u32[]{:S(2)}) %collective-permute-start.9) | collective-permute-done | bytes 98336 | tf_op jit(solution)/shard_map/ppermute | solution.py:76
  34.3 2.5 %collective-permute-start.10 = (bf16[2,192,128]{2,1,0:T(8,128)(2,1)S(1)}, bf16[2,192,128]{2,1,0:T(8,128)(2,1)S(1)}, u32[]{:S(2)}, u32[]{:S(2)}) collective-permute-start(bf16[2,192,128]{2,1,0:T(8,128)(2,1)S(1)} %shard_map.139.refs_0_), channel_id=1, source_target_pairs={{2,0},{3,1},{0,2},{1,3},{6,4},{7,5},{4,6},{5,7},{10,8},{11,9},{8,1... | collective-permute-start | bytes 294920 | tf_op jit(solution)/shard_map/ppermute | solution.py:76
  36.8 2.2 %shard_map.138 = (bf16[16,64,128]{2,1,0:T(8,128)(2,1)}, f32[8,128]{1,0:T(8,128)S(1)}) custom-call(bf16[16,64,128]{2,1,0:T(8,128)(2,1)S(1)} %get-tuple-element.40.refs_0_, bf16[16,64,128]{2,1,0:T(8,128)(2,1)S(1)} %get-tuple-element.41.refs_1_, bf16[896,128]{1,0:T(8,128)(2,1)S(1)} %collective-permute-done.6.refs_1_.refs_2_, ...), custom_call_target="tpu_custom_call" | custom-call | flops 301989888 | bytes 1429504 | tf_op jit(solution)/shard_map/pallas_call | solution.py:38
  39.1 0.1 collective-permute-start.11
  39.2 1.2 %collective-permute-start.14 = (bf16[2,192,128]{2,1,0:T(8,128)(2,1)S(1)}, bf16[2,192,128]{2,1,0:T(8,128)(2,1)S(1)}, u32[]{:S(2)}, u32[]{:S(2)}) collective-permute-start(bf16[2,192,128]{2,1,0:T(8,128)(2,1)S(1)} %shard_map.140.refs_0_), channel_id=1, source_target_pairs={{16,0},{24,8},{0,16},{8,24},{17,1},{25,9},{1,17},{9,25},{18,2},{26... | collective-permute-start | bytes 294920 | tf_op jit(solution)/shard_map/ppermute | solution.py:76
  40.4 2.5 %collective-permute-done.11.refs_1_ = bf16[2,192,128]{2,1,0:T(8,128)(2,1)S(1)} collective-permute-done((bf16[2,192,128]{2,1,0:T(8,128)(2,1)S(1)}, bf16[2,192,128]{2,1,0:T(8,128)(2,1)S(1)}, u32[]{:S(2)}, u32[]{:S(2)}) %collective-permute-start.11) | collective-permute-done | bytes 98336 | tf_op jit(solution)/shard_map/ppermute | solution.py:76
  43.0 1.2 %collective-permute-start.15 = (bf16[2,192,128]{2,1,0:T(8,128)(2,1)S(1)}, bf16[2,192,128]{2,1,0:T(8,128)(2,1)S(1)}, u32[]{:S(2)}, u32[]{:S(2)}) collective-permute-start(bf16[2,192,128]{2,1,0:T(8,128)(2,1)S(1)} %collective-permute-done.11.refs_1_), channel_id=1, source_target_pairs={{16,0},{24,8},{0,16},{8,24},{17,1},{25,9},{1,17},{9,25},{18,2},{26... | collective-permute-start | bytes 294920 | tf_op jit(solution)/shard_map/ppermute | solution.py:76
  44.1 6.8 %collective-permute-start.12 = (bf16[2,192,128]{2,1,0:T(8,128)(2,1)S(1)}, bf16[2,192,128]{2,1,0:T(8,128)(2,1)S(1)}, u32[]{:S(2)}, u32[]{:S(2)}) collective-permute-start(bf16[2,192,128]{2,1,0:T(8,128)(2,1)S(1)} %shard_map.140.refs_0_), channel_id=1, source_target_pairs={{8,0},{0,8},{24,16},{16,24},{9,1},{1,9},{25,17},{17,25},{10,2},{2,... | collective-permute-start | bytes 294920 | tf_op jit(solution)/shard_map/ppermute | solution.py:76
  50.9 0.5 collective-permute-start.16
  51.4 2.6 %collective-permute-start.17 = (bf16[2,192,128]{2,1,0:T(8,128)(2,1)S(1)}, bf16[2,192,128]{2,1,0:T(8,128)(2,1)S(1)}, u32[]{:S(2)}, u32[]{:S(2)}) collective-permute-start(bf16[2,192,128]{2,1,0:T(8,128)(2,1)S(1)} %collective-permute-done.15.refs_5_), channel_id=1, source_target_pairs={{8,0},{0,8},{24,16},{16,24},{9,1},{1,9},{25,17},{17,25},{10,2},{2,... | collective-permute-start | bytes 294920 | tf_op jit(solution)/shard_map/ppermute | solution.py:76
  54.1 0.9 %collective-permute-done.17.refs_7_ = bf16[2,192,128]{2,1,0:T(8,128)(2,1)S(1)} collective-permute-done((bf16[2,192,128]{2,1,0:T(8,128)(2,1)S(1)}, bf16[2,192,128]{2,1,0:T(8,128)(2,1)S(1)}, u32[]{:S(2)}, u32[]{:S(2)}) %collective-permute-start.17) | collective-permute-done | bytes 98336 | tf_op jit(solution)/shard_map/ppermute | solution.py:76
  55.0 1.3 %shard_map.141 = (f32[3,384,128]{2,1,0:T(8,128)}, f32[384,128]{1,0:T(8,128)}, f32[3,384,128]{2,1,0:T(8,128)}, f32[384,128]{1,0:T(8,128)}) custom-call(bf16[2,192,128]{2,1,0:T(8,128)(2,1)S(1)} %shard_map.140.refs_0_, bf16[2,192,128]{2,1,0:T(8,128)(2,1)S(1)} %collective-permute-done.11.refs_1_, bf16[2,192,128]{2,1,0:T(8,128)(2,1)S(1)} %collective-permute-done.12.refs_2_, ...), custom_call_target="tpu_custom_call" | custom-call | flops 196608 | bytes 2359296 | tf_op jit(solution)/shard_map/pallas_call | solution.py:38
  (36 shorter events, 0.3 us)
Async XLA Ops:
  0.6 11.1 %collective-permute-start.2 = (bf16[16,64,128]{2,1,0:T(8,128)(2,1)}, bf16[16,64,128]{2,1,0:T(8,128)(2,1)S(1)}, u32[]{:S(2)}, u32[]{:S(2)}) collective-permute-start(bf16[16,64,128]{2,1,0:T(8,128)(2,1)} %bitcast.10), channel_id=1, source_target_pairs={{4,0},{0,4},{5,1},{1,5},{6,2},{2,6},{7,3},{3,7},{12,8},{8,12},{13,... | collective-permute-start | bytes 786440 | tf_op jit(solution)/shard_map/ppermute | solution.py:76
  2.7 5.7 %copy-start = (bf16[1,1,16,64,128]{4,3,2,1,0:T(8,128)(2,1)S(1)}, bf16[1,1,16,64,128]{4,3,2,1,0:T(8,128)(2,1)}, u32[]{:S(2)}) copy-start(bf16[1,1,16,64,128]{4,3,2,1,0:T(8,128)(2,1)} %param.9) | copy-start | bytes 786436
  2.7 5.7 %copy-start.1 = (bf16[3,3,128,128]{3,2,1,0:T(8,128)(2,1)S(1)}, bf16[3,3,128,128]{3,2,1,0:T(8,128)(2,1)}, u32[]{:S(2)}) copy-start(bf16[3,3,128,128]{3,2,1,0:T(8,128)(2,1)} %refs_7_.1) | copy-start | bytes 884740
  2.7 5.7 %copy-start.2 = (bf16[1,1,16,64,128]{4,3,2,1,0:T(8,128)(2,1)S(1)}, bf16[1,1,16,64,128]{4,3,2,1,0:T(8,128)(2,1)}, u32[]{:S(2)}) copy-start(bf16[1,1,16,64,128]{4,3,2,1,0:T(8,128)(2,1)} %param.13) | copy-start | bytes 786436
  2.7 5.7 %copy-start.5 = (bf16[3,128,128]{2,1,0:T(8,128)(2,1)S(1)}, bf16[3,128,128]{2,1,0:T(8,128)(2,1)}, u32[]{:S(2)}) copy-start(bf16[3,128,128]{2,1,0:T(8,128)(2,1)} %refs_6_.3) | copy-start | bytes 294916
  4.4 4.1 %collective-permute-start = (bf16[4,64,128]{2,1,0:T(8,128)(2,1)}, bf16[4,64,128]{2,1,0:T(8,128)(2,1)S(1)}, u32[]{:S(2)}, u32[]{:S(2)}) collective-permute-start(bf16[4,64,128]{2,1,0:T(8,128)(2,1)} %get-tuple-element.31), channel_id=1, source_target_pairs={{0,8},{16,24},{8,0},{24,16},{1,9},{17,25},{9,1},{25,17},{2,10},{18... | collective-permute-start | bytes 196616 | tf_op jit(solution)/shard_map/ppermute | solution.py:65
  5.4 6.1 %collective-permute-start.1 = (bf16[4,64,128]{2,1,0:T(8,128)(2,1)}, bf16[4,64,128]{2,1,0:T(8,128)(2,1)S(1)}, u32[]{:S(2)}, u32[]{:S(2)}) collective-permute-start(bf16[4,64,128]{2,1,0:T(8,128)(2,1)} %get-tuple-element.32), channel_id=1, source_target_pairs={{8,16},{16,8},{9,17},{17,9},{10,18},{18,10},{11,19},{19,11},{12,20... | collective-permute-start | bytes 196616 | tf_op jit(solution)/shard_map/ppermute | solution.py:65
  11.5 2.0 %copy-start.4 = (bf16[1,1,16,64,128]{4,3,2,1,0:T(8,128)(2,1)S(1)}, bf16[1,1,16,64,128]{4,3,2,1,0:T(8,128)(2,1)}, u32[]{:S(2)}) copy-start(bf16[1,1,16,64,128]{4,3,2,1,0:T(8,128)(2,1)} %param.12) | copy-start | bytes 786436
  11.5 6.2 %collective-permute-start.3 = (bf16[18,64,128]{2,1,0:T(8,128)(2,1)S(1)}, bf16[18,64,128]{2,1,0:T(8,128)(2,1)S(1)}, u32[]{:S(2)}, u32[]{:S(2)}) collective-permute-start(bf16[18,64,128]{2,1,0:T(8,128)(2,1)S(1)} %shard_map.130.refs_7_), channel_id=1, source_target_pairs={{4,0},{0,4},{5,1},{1,5},{6,2},{2,6},{7,3},{3,7},{12,8},{8,12},{13,... | collective-permute-start | bytes 884744 | tf_op jit(solution)/shard_map/ppermute | solution.py:76
  13.5 4.2 %copy-start.8 = (bf16[3,128,128]{2,1,0:T(8,128)(2,1)S(1)}, bf16[3,128,128]{2,1,0:T(8,128)(2,1)}, u32[]{:S(2)}) copy-start(bf16[3,128,128]{2,1,0:T(8,128)(2,1)} %refs_10_.1) | copy-start | bytes 294916
  14.7 1.5 %collective-permute-start.4 = (bf16[768,128]{1,0:T(8,128)(2,1)S(1)}, bf16[768,128]{1,0:T(8,128)(2,1)S(1)}, u32[]{:S(2)}, u32[]{:S(2)}) collective-permute-start(bf16[768,128]{1,0:T(8,128)(2,1)S(1)} %get-tuple-element.38), channel_id=1, source_target_pairs={{8,0},{0,8},{24,16},{16,24},{9,1},{1,9},{25,17},{17,25},{10,2},{2,... | collective-permute-start | bytes 589832 | tf_op jit(solution)/shard_map/ppermute | solution.py:76
  16.2 1.5 %copy-start.3 = (bf16[1,1,16,64,128]{4,3,2,1,0:T(8,128)(2,1)S(1)}, bf16[1,1,16,64,128]{4,3,2,1,0:T(8,128)(2,1)}, u32[]{:S(2)}) copy-start(bf16[1,1,16,64,128]{4,3,2,1,0:T(8,128)(2,1)} %param.10) | copy-start | bytes 786436
  16.2 1.5 %copy-start.7 = (bf16[1,1,16,64,128]{4,3,2,1,0:T(8,128)(2,1)S(1)}, bf16[1,1,16,64,128]{4,3,2,1,0:T(8,128)(2,1)}, u32[]{:S(2)}) copy-start(bf16[1,1,16,64,128]{4,3,2,1,0:T(8,128)(2,1)} %param.11) | copy-start | bytes 786436
  16.2 4.3 %collective-permute-start.5 = (bf16[384,128]{1,0:T(8,128)(2,1)S(1)}, bf16[384,128]{1,0:T(8,128)(2,1)S(1)}, u32[]{:S(2)}, u32[]{:S(2)}) collective-permute-start(bf16[384,128]{1,0:T(8,128)(2,1)S(1)} %get-tuple-element.43), channel_id=1, source_target_pairs={{16,0},{24,8},{0,16},{8,24},{17,1},{25,9},{1,17},{9,25},{18,2},{26... | collective-permute-start | bytes 294920 | tf_op jit(solution)/shard_map/ppermute | solution.py:76
  20.6 2.1 %collective-permute-start.6 = (bf16[896,128]{1,0:T(8,128)(2,1)S(1)}, bf16[896,128]{1,0:T(8,128)(2,1)S(1)}, u32[]{:S(2)}, u32[]{:S(2)}) collective-permute-start(bf16[896,128]{1,0:T(8,128)(2,1)S(1)} %get-tuple-element.44), channel_id=1, source_target_pairs={{8,0},{0,8},{24,16},{16,24},{9,1},{1,9},{25,17},{17,25},{10,2},{2,... | collective-permute-start | bytes 688136 | tf_op jit(solution)/shard_map/ppermute | solution.py:76
  22.7 4.4 %collective-permute-start.7 = (bf16[448,128]{1,0:T(8,128)(2,1)S(1)}, bf16[448,128]{1,0:T(8,128)(2,1)S(1)}, u32[]{:S(2)}, u32[]{:S(2)}) collective-permute-start(bf16[448,128]{1,0:T(8,128)(2,1)S(1)} %get-tuple-element.46), channel_id=1, source_target_pairs={{16,0},{24,8},{0,16},{8,24},{17,1},{25,9},{1,17},{9,25},{18,2},{26... | collective-permute-start | bytes 344072 | tf_op jit(solution)/shard_map/ppermute | solution.py:76
  27.1 3.5 %collective-permute-start.8 = (bf16[2,192,128]{2,1,0:T(8,128)(2,1)S(1)}, bf16[2,192,128]{2,1,0:T(8,128)(2,1)S(1)}, u32[]{:S(2)}, u32[]{:S(2)}) collective-permute-start(bf16[2,192,128]{2,1,0:T(8,128)(2,1)S(1)} %get-tuple-element.50), channel_id=1, source_target_pairs={{4,0},{0,4},{5,1},{1,5},{6,2},{2,6},{7,3},{3,7},{12,8},{8,12},{13,... | collective-permute-start | bytes 294920 | tf_op jit(solution)/shard_map/ppermute | solution.py:76
  30.7 6.2 %copy-start.6 = (bf16[3,3,128,128]{3,2,1,0:T(8,128)(2,1)S(1)}, bf16[3,3,128,128]{3,2,1,0:T(8,128)(2,1)}, u32[]{:S(2)}) copy-start(bf16[3,3,128,128]{3,2,1,0:T(8,128)(2,1)} %refs_4_.3) | copy-start | bytes 884740
  30.7 3.6 %collective-permute-start.9 = (bf16[2,192,128]{2,1,0:T(8,128)(2,1)S(1)}, bf16[2,192,128]{2,1,0:T(8,128)(2,1)S(1)}, u32[]{:S(2)}, u32[]{:S(2)}) collective-permute-start(bf16[2,192,128]{2,1,0:T(8,128)(2,1)S(1)} %shard_map.137.refs_5_.refs_0_), channel_id=1, source_target_pairs={{1,0},{0,1},{3,2},{2,3},{5,4},{4,5},{7,6},{6,7},{9,8},{8,9},{11,10... | collective-permute-start | bytes 294920 | tf_op jit(solution)/shard_map/ppermute | solution.py:76
  34.3 4.8 %collective-permute-start.10 = (bf16[2,192,128]{2,1,0:T(8,128)(2,1)S(1)}, bf16[2,192,128]{2,1,0:T(8,128)(2,1)S(1)}, u32[]{:S(2)}, u32[]{:S(2)}) collective-permute-start(bf16[2,192,128]{2,1,0:T(8,128)(2,1)S(1)} %shard_map.139.refs_0_), channel_id=1, source_target_pairs={{2,0},{3,1},{0,2},{1,3},{6,4},{7,5},{4,6},{5,7},{10,8},{11,9},{8,1... | collective-permute-start | bytes 294920 | tf_op jit(solution)/shard_map/ppermute | solution.py:76
  39.1 3.8 %collective-permute-start.11 = (bf16[2,192,128]{2,1,0:T(8,128)(2,1)S(1)}, bf16[2,192,128]{2,1,0:T(8,128)(2,1)S(1)}, u32[]{:S(2)}, u32[]{:S(2)}) collective-permute-start(bf16[2,192,128]{2,1,0:T(8,128)(2,1)S(1)} %shard_map.140.refs_0_), channel_id=1, source_target_pairs={{4,0},{0,4},{5,1},{1,5},{6,2},{2,6},{7,3},{3,7},{12,8},{8,12},{13,... | collective-permute-start | bytes 294920 | tf_op jit(solution)/shard_map/ppermute | solution.py:76
  39.2 11.7 %collective-permute-start.14 = (bf16[2,192,128]{2,1,0:T(8,128)(2,1)S(1)}, bf16[2,192,128]{2,1,0:T(8,128)(2,1)S(1)}, u32[]{:S(2)}, u32[]{:S(2)}) collective-permute-start(bf16[2,192,128]{2,1,0:T(8,128)(2,1)S(1)} %shard_map.140.refs_0_), channel_id=1, source_target_pairs={{16,0},{24,8},{0,16},{8,24},{17,1},{25,9},{1,17},{9,25},{18,2},{26... | collective-permute-start | bytes 294920 | tf_op jit(solution)/shard_map/ppermute | solution.py:76
  43.0 8.5 %collective-permute-start.15 = (bf16[2,192,128]{2,1,0:T(8,128)(2,1)S(1)}, bf16[2,192,128]{2,1,0:T(8,128)(2,1)S(1)}, u32[]{:S(2)}, u32[]{:S(2)}) collective-permute-start(bf16[2,192,128]{2,1,0:T(8,128)(2,1)S(1)} %collective-permute-done.11.refs_1_), channel_id=1, source_target_pairs={{16,0},{24,8},{0,16},{8,24},{17,1},{25,9},{1,17},{9,25},{18,2},{26... | collective-permute-start | bytes 294920 | tf_op jit(solution)/shard_map/ppermute | solution.py:76
  44.1 10.0 %collective-permute-start.12 = (bf16[2,192,128]{2,1,0:T(8,128)(2,1)S(1)}, bf16[2,192,128]{2,1,0:T(8,128)(2,1)S(1)}, u32[]{:S(2)}, u32[]{:S(2)}) collective-permute-start(bf16[2,192,128]{2,1,0:T(8,128)(2,1)S(1)} %shard_map.140.refs_0_), channel_id=1, source_target_pairs={{8,0},{0,8},{24,16},{16,24},{9,1},{1,9},{25,17},{17,25},{10,2},{2,... | collective-permute-start | bytes 294920 | tf_op jit(solution)/shard_map/ppermute | solution.py:76
  50.9 3.2 %collective-permute-start.13 = (bf16[2,192,128]{2,1,0:T(8,128)(2,1)S(1)}, bf16[2,192,128]{2,1,0:T(8,128)(2,1)S(1)}, u32[]{:S(2)}, u32[]{:S(2)}) collective-permute-start(bf16[2,192,128]{2,1,0:T(8,128)(2,1)S(1)} %collective-permute-done.11.refs_1_), channel_id=1, source_target_pairs={{8,0},{0,8},{24,16},{16,24},{9,1},{1,9},{25,17},{17,25},{10,2},{2,... | collective-permute-start | bytes 294920 | tf_op jit(solution)/shard_map/ppermute | solution.py:76
  50.9 3.2 %collective-permute-start.16 = (bf16[2,192,128]{2,1,0:T(8,128)(2,1)S(1)}, bf16[2,192,128]{2,1,0:T(8,128)(2,1)S(1)}, u32[]{:S(2)}, u32[]{:S(2)}) collective-permute-start(bf16[2,192,128]{2,1,0:T(8,128)(2,1)S(1)} %collective-permute-done.14.refs_4_), channel_id=1, source_target_pairs={{8,0},{0,8},{24,16},{16,24},{9,1},{1,9},{25,17},{17,25},{10,2},{2,... | collective-permute-start | bytes 294920 | tf_op jit(solution)/shard_map/ppermute | solution.py:76
  51.4 3.6 %collective-permute-start.17 = (bf16[2,192,128]{2,1,0:T(8,128)(2,1)S(1)}, bf16[2,192,128]{2,1,0:T(8,128)(2,1)S(1)}, u32[]{:S(2)}, u32[]{:S(2)}) collective-permute-start(bf16[2,192,128]{2,1,0:T(8,128)(2,1)S(1)} %collective-permute-done.15.refs_5_), channel_id=1, source_target_pairs={{8,0},{0,8},{24,16},{16,24},{9,1},{1,9},{25,17},{17,25},{10,2},{2,... | collective-permute-start | bytes 294920 | tf_op jit(solution)/shard_map/ppermute | solution.py:76

commit v7 on v6

--- a/solution.py
+++ b/solution.py
@@ -59,21 +59,30 @@
     return lax.ppermute(block, ("section", "video"), pairs)
 
 
-def paired(block, start):
-    bands = lax.axis_size("section")
-    pairs = [(band, band + 1) for band in range(start, bands - 1, 2)]
-    return lax.ppermute(block, "section", pairs + [(right, left) for left, right in pairs])
-
-
 def beside_band(pair_refs, row):
-    odd = lax.rem(lax.axis_index("section"), 2) == 1
+    band = lax.axis_index("section")
+    odd = lax.rem(band, 2) == 1
+    inside = (band > 0) & (band < lax.axis_size("section") - 1)
     first, second = (ref[row : row + 1] for ref in pair_refs)
+    second = jnp.where(inside, second, jnp.zeros_like(second))
     return jnp.where(odd, first, second), jnp.where(odd, second, first)
 
 
 def flipped(block, axis, flip):
     count = lax.axis_size(axis)
     return lax.ppermute(block, axis, [(place ^ flip, place) for place in range(count)])
+
+
+def flipped_both(block):
+    bands = lax.axis_size("section")
+    pairs = [
+        (2 * (band ^ 2) + 1 - frame, 2 * band + frame) for band in range(bands) for frame in range(2)
+    ]
+    return lax.ppermute(block, ("section", "video"), pairs)
+
+
+def later_than(block, *others):
+    return lax.optimization_barrier((block, *others))[0]
 
 
 def beside(gpre, views_ref, start):
@@ -330,16 +339,12 @@
 
 def input_kernel(mid_ref, gpre_ref, pair_ref, across_ref, spatial_ref, out_ref, token_ref, views_ref):
     rows, cols, ch = out_ref.shape
-    band, bands = lax.axis_index("section"), lax.axis_size("section")
-    first = pair_ref[pair_ref.shape[0] - 2 * cols : pair_ref.shape[0] - cols]
-    second = across_ref[across_ref.shape[0] - cols :]
-    second = jnp.where((band > 0) & (band < bands - 1), second, jnp.zeros_like(second))
-    odd = lax.rem(band, 2) == 1
-    above, below = jnp.where(odd, first, second), jnp.where(odd, second, first)
+    pair = pair_ref[pair_ref.shape[0] - 2 * cols : pair_ref.shape[0] - cols]
+    above, below = beside_band((pair[None], across_ref[across_ref.shape[0] - cols :][None]), 0)
     token_ref[...] = jnp.zeros(token_ref.shape, token_ref.dtype)
     step = 4
-    beside(above.astype(jnp.float32)[None], views_ref, 0)
-    beside(below.astype(jnp.float32)[None], views_ref, rows + 1)
+    beside(above.astype(jnp.float32), views_ref, 0)
+    beside(below.astype(jnp.float32), views_ref, rows + 1)
 
     @pl.loop(0, rows // step)
     def _(n):
@@ -352,27 +357,49 @@
         out_ref[here] = convolved(views_ref, spatial_ref, n * step, mid_ref[here])
 
 
+def halves(count, index):
+    return [pl.ds(pl.multiple_of(n * count, count), count) for n in (index, 1 - index)]
+
+
 def pair_kernel(keep_ref, part_ref, own_ref, send_ref):
+    across = lax.axis_index("section") // 2
+    mine, other = halves(own_ref.shape[0], across)
+    own_ref[...] = keep_ref[across] + part_ref[mine].astype(jnp.float32)
+    total = keep_ref[1 - across] + part_ref[other].astype(jnp.float32)
+    send_ref[...] = total.astype(jnp.bfloat16)
+
+
+def band_kernel(own_ref, part_ref, keep_ref, send_ref):
+    mine, other = halves(keep_ref.shape[0], lax.axis_index("video"))
+    keep_ref[...] = own_ref[mine] + part_ref[mine].astype(jnp.float32)
+    send_ref[...] = (own_ref[other] + part_ref[other].astype(jnp.float32)).astype(jnp.bfloat16)
+
+
+def pair_quarter_kernel(keep_ref, part_ref, own_ref, across_ref, frame_ref, both_ref):
     _, height, _ = keep_ref.shape
-    across = lax.axis_index("section") // 2
-    other = 1 - across
-    part = part_ref[pl.ds(pl.multiple_of(across * height, height), height)]
-    own_ref[...] = keep_ref[across] + part.astype(jnp.float32)
-    part = part_ref[pl.ds(pl.multiple_of(other * height, height), height)]
-    send_ref[:height] = (keep_ref[other] + part.astype(jnp.float32)).astype(jnp.bfloat16)
-    rest = send_ref.shape[0] - height
-    if rest:
-        send_ref[height:] = part_ref[2 * height + rest :]
-
-
-def band_kernel(one_ref, one_part_ref, two_ref, two_part_ref, keep_ref, send_ref):
-    half = keep_ref.shape[1]
-    frame = lax.axis_index("video")
-    mine = pl.ds(pl.multiple_of(frame * half, half), half)
-    other = pl.ds(pl.multiple_of((1 - frame) * half, half), half)
-    for block, (own, part) in enumerate(((one_ref, one_part_ref), (two_ref, two_part_ref))):
-        keep_ref[block] = own[mine] + part[mine].astype(jnp.float32)
-        send_ref[block] = (own[other] + part[other].astype(jnp.float32)).astype(jnp.bfloat16)
+    half = own_ref.shape[0]
+    band = lax.axis_index("section") // 2
+    frames = halves(half, lax.axis_index("video"))
+
+    def quarter(band, rows):
+        start = pl.multiple_of(band * height, height)
+        part = part_ref.at[pl.ds(start, height)][rows]
+        return keep_ref[band, rows] + part.astype(jnp.float32)
+
+    own_ref[...] = quarter(band, frames[0])
+    across_ref[:half] = quarter(1 - band, frames[0]).astype(jnp.bfloat16)
+    rest = across_ref.shape[0] - half
+    across_ref[half:] = part_ref[2 * height + rest :]
+    frame_ref[...] = quarter(band, frames[1]).astype(jnp.bfloat16)
+    both_ref[...] = quarter(1 - band, frames[1]).astype(jnp.bfloat16)
+
+
+def plane_kernel(own_ref, *refs):
+    parts, out_ref = refs[:-1], refs[-1]
+    total = own_ref[...]
+    for part in parts:
+        total = total + part[: out_ref.shape[0]].astype(jnp.float32)
+    out_ref[...] = total.astype(jnp.bfloat16)
 
 
 def add_kernel(one_ref, two_ref, out_ref):
@@ -380,9 +407,11 @@
     out_ref[...] = total.astype(jnp.bfloat16)
 
 
-def scaled_kernel(factor, one_ref, two_ref, out_ref):
-    total = one_ref[...].astype(jnp.float32) + two_ref[...].astype(jnp.float32)
-    out_ref[...] = (total * factor).astype(jnp.bfloat16)
+def scaled_kernel(factor, *refs):
+    out_ref = refs[-1]
+    for block in range(2):
+        one, two = (ref[...].astype(jnp.float32) for ref in refs[2 * block : 2 * block + 2])
+        out_ref[block] = ((one + two) * factor).astype(jnp.bfloat16)
 
 
 def place_kernel(*refs):
@@ -406,53 +435,20 @@
                 outs[2 * block + 1][here] = share[block].astype(jnp.float32)
 
 
-def bands_summed(keep, send, after=()):
-    _, height, ch = keep.shape
-    rest = (send.shape[0] - 2 * height) // 2
-    pair = flipped(send, "section", 1)
-    outs = [f32(height, ch), bf16(height + rest, ch)]
-    own, across = call(pair_kernel, outs, [], keep.size, keep, pair, after=after)
-    return own, flipped(across, "section", 2), pair
-
-
-def totals(one, two, factor, meanwhile):
-    height, ch = one[0].shape
-    if lax.axis_size("video") == 2 and lax.axis_size("dp") == 4:
-        cut = (2, height // 2, ch)
-        size = height * ch
-        operands = (*one[:2], *two[:2])
-        keep, send = call(band_kernel, [f32(*cut), bf16(*cut)], [], 2 * size, *operands)
-        own = call(add_kernel, [bf16(*cut)], [], size, keep, flipped(send, "video", 1))
-        done, token = meanwhile((own,))
-        own = call(add_kernel, [bf16(*cut)], [], size, own, flipped(own, "dp", 1))
-        own = call(
-            functools.partial(scaled_kernel, factor),
-            [bf16(*cut)],
-            [],
-            size,
-            own,
-            flipped(own, "dp", 2),
-            after=(token,),
-        )
-        shares = [own, flipped(own, "video", 1)]
-    else:
-        done, _ = meanwhile(())
-        own = [x[0] + x[1][:height].astype(jnp.float32) for x in (one, two)]
-        share = lax.psum(jnp.stack(own), ("video", "dp")) * factor
-        shares = [share.astype(jnp.bfloat16)]
+def place(shares):
     across = [flipped(share, "section", 2) for share in shares]
+    ch = shares[0].shape[2]
     outs = call(
         place_kernel,
-        [f32(3, height, ch), f32(height, ch)] * 2,
+        [f32(3, 3 * ch, ch), f32(3 * ch, ch)] * 2,
         [],
-        4 * height * ch,
+        12 * ch * ch,
         *shares,
         *[flipped(share, "section", 1) for share in shares],
         *across,
         *[flipped(share, "section", 1) for share in across],
     )
-    outs = [x.reshape(3, 3, ch, ch) if x.ndim == 3 else x.reshape(3, ch, ch) for x in outs]
-    return done, outs
+    return [x.reshape(3, 3, ch, ch) if x.ndim == 3 else x.reshape(3, ch, ch) for x in outs]
 
 
 def on_device(
@@ -503,7 +499,8 @@
         spare_inputs=True,
         limit=58,
     )
-    pairs = [paired(pack, start) for start, pack in enumerate(packs)]
+    first, second = (flipped(pack, "section", 1) for pack in packs)
+    pairs = [first, flipped(second, "section", 2)]
 
     known = ()
     if frames == 2:
@@ -515,7 +512,7 @@
             grad,
             pre_two,
             *kernels,
-            after=pairs[:1],
+            after=(first, second),
         )
         sent = call(
             last_mid_kernel,
@@ -529,10 +526,7 @@
         )
         afters = from_later(sent)
     else:
-        odd = lax.rem(lax.axis_index("section"), 2) == 1
-        one, two = (pair[:1] for pair in pairs)
-        above, below = jnp.where(odd, one, two), jnp.where(odd, two, one)
-        afters = from_later(jnp.concatenate([above, below]))
+        afters = from_later(jnp.concatenate(beside_band(pairs, 0)))
     inner, gpre_two = call(
         functools.partial(inner_kernel, later),
         inner_outs,
@@ -557,7 +551,17 @@
         grad,
         *wholes,
     )
-    sums_two = bands_summed(*parts_two)
+    height, half = 3 * ch, 3 * ch // 2
+    keep_two, send_two = parts_two
+    own_two, send_two = call(
+        pair_kernel,
+        [f32(height, ch), bf16(height, ch)],
+        [],
+        height * ch,
+        keep_two,
+        flipped(send_two, "section", 1),
+    )
+    across_two = flipped(send_two, "section", 2)
     mid_inputs = (grad, *pairs, inner, gpre_two)
     one_inputs = (saved_one, pre_one)
     mid_outs = [bf16(rows, cols, ch)]
@@ -573,7 +577,7 @@
             *kernels,
             *one_inputs,
             temporal_one,
-            after=sums_two[:1],
+            after=(own_two,),
         )
     else:
         mid = call(
@@ -596,12 +600,13 @@
             *from_later(mid),
             temporal_one,
         )
-    keep, send = parts_one
-    send, across = lax.optimization_barrier((send, sums_two[1]))
-    sums_two = (sums_two[0], across)
-    sums_one = bands_summed(keep, send)
-
-    def input_gradient(after):
+    keep_one, send_one = parts_one
+    split = frames == 2 and lax.axis_size("dp") == 4
+    if split:
+        send_one = later_than(send_one, across_two)
+    pair_one = flipped(send_one, "section", 1)
+
+    def input_gradient(edge, after):
         return call(
             input_kernel,
             [bf16(rows, cols, ch), f32(8, 128)],
@@ -609,13 +614,62 @@
             conv,
             mid,
             gpre_one,
-            sums_one[2],
-            sums_one[1],
+            pair_one,
+            edge,
             spatial_one,
             after=after,
         )
 
-    grad_in, sums = totals(sums_one, sums_two, factor, input_gradient)
+    if split:
+
+        def added(one, two):
+            return call(add_kernel, [bf16(half, ch)], [], half * ch, one, two)
+
+        keep_two, send_two = call(
+            band_kernel,
+            [f32(half, ch), bf16(half, ch)],
+            [],
+            height * ch,
+            own_two,
+            across_two,
+        )
+        sum_two = added(keep_two, flipped(send_two, "video", 1))
+        quarters = [f32(half, ch), bf16(half + cols, ch)] + [bf16(half, ch)] * 2
+        own_one, *sends = call(
+            pair_quarter_kernel, quarters, [], height * ch, keep_one, pair_one, after=(send_two,)
+        )
+        across = flipped(sends[0], "section", 2)
+        parts = [across, flipped(sends[1], "video", 1), flipped_both(sends[2])]
+        sum_one = call(plane_kernel, [bf16(half, ch)], [], 4 * half * ch, own_one, *parts)
+        part_two = flipped(sum_two, "dp", 1)
+        part_one = flipped(later_than(sum_one, sum_two), "dp", 1)
+        sum_two = added(sum_two, part_two)
+        sum_one = added(sum_one, part_one)
+        last_two = flipped(sum_two, "dp", 2)
+        last_one = flipped(later_than(sum_one, sum_two), "dp", 2)
+        grad_in, token = input_gradient(across, (sum_one,))
+        own = call(
+            functools.partial(scaled_kernel, factor),
+            [bf16(2, half, ch)],
+            [],
+            height * ch,
+            sum_one,
+            last_one,
+            sum_two,
+            last_two,
+            after=(token,),
+        )
+        sums = place([own, flipped(own, "video", 1)])
+    else:
+        own_one, send_one = call(
+            pair_kernel, [f32(height, ch), bf16(height, ch)], [], height * ch, keep_one, pair_one
+        )
+        edge = flipped(pair_one[pair_one.shape[0] - cols :], "section", 2)
+        grad_in, _ = input_gradient(edge, ())
+        own_one = own_one + flipped(send_one, "section", 2).astype(jnp.float32)
+        own_two = own_two + across_two.astype(jnp.float32)
+        share = lax.psum(jnp.stack((own_one, own_two)), ("video", "dp")) * factor
+        sums = place([share.astype(jnp.bfloat16)])
     return (grad_in.reshape(shape), *sums)
 
 

time: 56.9 us -> 53.9 us (0.947)
  waiting for transfers between devices: 18.1 us -> 9.93 us
  starting transfers between devices: 27 us -> 32.2 us
    ppermute x16 -> x22, starting transfers between devices: 22.9 us -> 31.4 us  [flipped(): lax.ppermute(block, axis, [(place ^ flip, place) for place in range(count)])]
    ppermute x16 -> x22, waiting for transfers between devices: 15.1 us -> 8.7 us  [flipped(): lax.ppermute(block, axis, [(place ^ flip, place) for place in range(count)])]
    ppermute x2 -> x1, starting transfers between devices: 4.07 us -> 0.75 us  [flipped_both(): return lax.ppermute(block, ('section', 'video'), pairs)]
    ppermute x2 -> x1, waiting for transfers between devices: 2.95 us -> 1.23 us  [flipped_both(): return lax.ppermute(block, ('section', 'video'), pairs)]
    pallas_call x14 -> x16, Pallas kernels: 10.4 us -> 10.4 us  [call(): pl.pallas_call(body, out_shape=outs[0] if single else tuple(outs), in_spe...]
  transfers between devices with their start and end apart: 18 -> 23, of which waited for: 9 -> 9; matrix products, arithmetic and copies ran while one was open for 0% -> 0% of each run, Pallas kernels for 16% -> 17%
where the time goes in v7:
time: 53.9 us; the launch traced here: 53.3 us
  starting transfers between devices  32.2 us (60%)
  Pallas kernels  10.4 us (19%)
  waiting for transfers between devices  9.93 us (18%)
  between operations  0.78 us (1%)
    ppermute x22, starting transfers between devices, flipped(): lax.ppermute(block, axis, [(place ^ flip, place) for place in range(count)])  31.4 us
    pallas_call x16, Pallas kernels, call(): pl.pallas_call(body, out_shape=outs[0] if single else tuple(outs), in_spe...  10.4 us
    ppermute x22, waiting for transfers between devices, flipped(): lax.ppermute(block, axis, [(place ^ flip, place) for place in range(count)])  8.7 us
    ppermute x1, waiting for transfers between devices, flipped_both(): return lax.ppermute(block, ('section', 'video'), pairs)  1.23 us
  transfers between devices with their start and end apart: 23, of which 9 were waited for; matrix products, arithmetic and copies ran while one was open for 0% of the time, Pallas kernels for 17%

profile of v7, /device:TPU:1, one launch (start us, length us, event | category | flops | bytes accessed | tf_op | source)
XLA Modules:
  0.0 53.3 jit_solution(9492897019806635676)
XLA Ops:
  0.6 2.1 %collective-permute-start.3 = (bf16[16,64,128]{2,1,0:T(8,128)(2,1)}, bf16[16,64,128]{2,1,0:T(8,128)(2,1)S(1)}, u32[]{:S(2)}, u32[]{:S(2)}) collective-permute-start(bf16[16,64,128]{2,1,0:T(8,128)(2,1)} %bitcast.10), channel_id=1, source_target_pairs={{4,0},{0,4},{5,1},{1,5},{6,2},{2,6},{7,3},{3,7},{12,8},{8,12},{13,... | collective-permute-start | bytes 786440 | tf_op jit(solution)/shard_map/ppermute | solution.py:73
  2.7 1.6 %shard_map.128 = (bf16[4,64,128]{2,1,0:T(8,128)(2,1)}, bf16[4,64,128]{2,1,0:T(8,128)(2,1)}) custom-call(bf16[16,64,128]{2,1,0:T(8,128)(2,1)} %bitcast.11, bf16[16,64,128]{2,1,0:T(8,128)(2,1)} %bitcast.17, bf16[16,64,128]{2,1,0:T(8,128)(2,1)} %bitcast.23, bf16[16,64,128]{2,1,0:T(8,128)(2,1)} %bitcast.21), custom_call_target="tpu_custom_call" | custom-call | flops 1 | bytes 1179648 | tf_op jit(solution)/shard_map/pallas_call | solution.py:38
  4.4 1.0 %collective-permute-start.1 = (bf16[4,64,128]{2,1,0:T(8,128)(2,1)}, bf16[4,64,128]{2,1,0:T(8,128)(2,1)S(1)}, u32[]{:S(2)}, u32[]{:S(2)}) collective-permute-start(bf16[4,64,128]{2,1,0:T(8,128)(2,1)} %get-tuple-element.35), channel_id=1, source_target_pairs={{8,0},{0,8},{24,16},{16,24},{9,1},{1,9},{25,17},{17,25},{10,2},{2,... | collective-permute-start | bytes 196616 | tf_op jit(solution)/shard_map/ppermute | solution.py:73
  5.5 1.0 %collective-permute-done.1.refs_5_ = bf16[4,64,128]{2,1,0:T(8,128)(2,1)S(1)} collective-permute-done((bf16[4,64,128]{2,1,0:T(8,128)(2,1)}, bf16[4,64,128]{2,1,0:T(8,128)(2,1)S(1)}, u32[]{:S(2)}, u32[]{:S(2)}) %collective-permute-start.1) | collective-permute-done | bytes 65568 | tf_op jit(solution)/shard_map/ppermute | solution.py:73
  6.5 1.2 %collective-permute-start.2 = (bf16[4,64,128]{2,1,0:T(8,128)(2,1)S(1)}, bf16[4,64,128]{2,1,0:T(8,128)(2,1)S(1)}, u32[]{:S(2)}, u32[]{:S(2)}) collective-permute-start(bf16[4,64,128]{2,1,0:T(8,128)(2,1)S(1)} %collective-permute-done.1.refs_5_), channel_id=1, source_target_pairs={{16,0},{24,8},{0,16},{8,24},{17,1},{25,9},{1,17},{9,25},{18,2},{26... | collective-permute-start | bytes 196616 | tf_op jit(solution)/shard_map/ppermute | solution.py:73
  7.8 2.0 %collective-permute-done.2.refs_2_.refs_4_ = bf16[4,64,128]{2,1,0:T(8,128)(2,1)S(1)} collective-permute-done((bf16[4,64,128]{2,1,0:T(8,128)(2,1)S(1)}, bf16[4,64,128]{2,1,0:T(8,128)(2,1)S(1)}, u32[]{:S(2)}, u32[]{:S(2)}) %collective-permute-start.2) | collective-permute-done | bytes 65568 | tf_op jit(solution)/shard_map/ppermute | solution.py:73
  9.8 0.9 %collective-permute-start.4 = (bf16[18,64,128]{2,1,0:T(8,128)(2,1)S(1)}, bf16[18,64,128]{2,1,0:T(8,128)(2,1)S(1)}, u32[]{:S(2)}, u32[]{:S(2)}) collective-permute-start(bf16[18,64,128]{2,1,0:T(8,128)(2,1)S(1)} %shard_map.130.refs_7_), channel_id=1, source_target_pairs={{4,0},{0,4},{5,1},{1,5},{6,2},{2,6},{7,3},{3,7},{12,8},{8,12},{13,... | collective-permute-start | bytes 884744 | tf_op jit(solution)/shard_map/ppermute | solution.py:73
  10.7 1.7 %shard_map.131 = (bf16[14,64,128]{2,1,0:T(8,128)(2,1)S(1)}, bf16[16,64,128]{2,1,0:T(8,128)(2,1)S(1)}) custom-call(bf16[16,64,128]{2,1,0:T(8,128)(2,1)S(1)} %bitcast.14, bf16[16,64,128]{2,1,0:T(8,128)(2,1)S(1)} %bitcast.19, bf16[16,64,128]{2,1,0:T(8,128)(2,1)S(1)} %collective-permute-done.3.refs_2_.refs_6_, bf16[3,128,128]{2,1,0:T(8,128)(2,1)S(1)} %copy-done.5, ...), custom_call_target="tpu_custom_call" | custom-call | flops 362387872 | bytes 2162688 | tf_op jit(solution)/shard_map/pallas_call | solution.py:38
  12.5 1.1 %shard_map.132 = (f32[2,384,128]{2,1,0:T(8,128)S(1)}, bf16[768,128]{1,0:T(8,128)(2,1)S(1)}) custom-call(bf16[16,64,128]{2,1,0:T(8,128)(2,1)S(1)} %bitcast.24, bf16[16,64,128]{2,1,0:T(8,128)(2,1)S(1)} %bitcast.20, bf16[16,64,128]{2,1,0:T(8,128)(2,1)S(1)} %get-tuple-element.39.refs_2_.refs_4_, ...), custom_call_target="tpu_custom_call" | custom-call | flops 362387872 | bytes 2031616 | tf_op jit(solution)/shard_map/pallas_call | solution.py:38
  13.6 1.2 %collective-permute-start.5 = (bf16[768,128]{1,0:T(8,128)(2,1)S(1)}, bf16[768,128]{1,0:T(8,128)(2,1)S(1)}, u32[]{:S(2)}, u32[]{:S(2)}) collective-permute-start(bf16[768,128]{1,0:T(8,128)(2,1)S(1)} %get-tuple-element.41), channel_id=1, source_target_pairs={{8,0},{0,8},{24,16},{16,24},{9,1},{1,9},{25,17},{17,25},{10,2},{2,... | collective-permute-start | bytes 589832 | tf_op jit(solution)/shard_map/ppermute | solution.py:73
  14.9 1.1 %collective-permute-done.5.refs_1_ = bf16[768,128]{1,0:T(8,128)(2,1)S(1)} collective-permute-done((bf16[768,128]{1,0:T(8,128)(2,1)S(1)}, bf16[768,128]{1,0:T(8,128)(2,1)S(1)}, u32[]{:S(2)}, u32[]{:S(2)}) %collective-permute-start.5) | collective-permute-done | bytes 196640 | tf_op jit(solution)/shard_map/ppermute | solution.py:73
  16.0 1.6 %collective-permute-start.6 = (bf16[384,128]{1,0:T(8,128)(2,1)S(1)}, bf16[384,128]{1,0:T(8,128)(2,1)S(1)}, u32[]{:S(2)}, u32[]{:S(2)}) collective-permute-start(bf16[384,128]{1,0:T(8,128)(2,1)S(1)} %get-tuple-element.46), channel_id=1, source_target_pairs={{16,0},{24,8},{0,16},{8,24},{17,1},{25,9},{1,17},{9,25},{18,2},{26... | collective-permute-start | bytes 294920 | tf_op jit(solution)/shard_map/ppermute | solution.py:73
  17.6 2.2 %shard_map.134 = (bf16[16,64,128]{2,1,0:T(8,128)(2,1)S(1)}, bf16[16,64,128]{2,1,0:T(8,128)(2,1)S(1)}, f32[2,384,128]{2,1,0:T(8,128)S(1)}, bf16[896,128]{1,0:T(8,128)(2,1)S(1)}) custom-call(bf16[16,64,128]{2,1,0:T(8,128)(2,1)S(1)} %bitcast.16, bf16[4,64,128]{2,1,0:T(8,128)(2,1)S(1)} %collective-permute-done.refs_4_.refs_1_.refs_3_, ...), custom_call_target="tpu_custom_call" | custom-call | flops 452984832 | bytes 3342336 | tf_op jit(solution)/shard_map/pallas_call | solution.py:38
  20.3 1.2 %collective-permute-start.7 = (bf16[896,128]{1,0:T(8,128)(2,1)S(1)}, bf16[896,128]{1,0:T(8,128)(2,1)S(1)}, u32[]{:S(2)}, u32[]{:S(2)}) collective-permute-start(bf16[896,128]{1,0:T(8,128)(2,1)S(1)} %get-tuple-element.47), channel_id=1, source_target_pairs={{8,0},{0,8},{24,16},{16,24},{9,1},{1,9},{25,17},{17,25},{10,2},{2,... | collective-permute-start | bytes 688136 | tf_op jit(solution)/shard_map/ppermute | solution.py:73
  21.5 1.1 %collective-permute-done.7.refs_1_.refs_2_ = bf16[896,128]{1,0:T(8,128)(2,1)S(1)} collective-permute-done((bf16[896,128]{1,0:T(8,128)(2,1)S(1)}, bf16[896,128]{1,0:T(8,128)(2,1)S(1)}, u32[]{:S(2)}, u32[]{:S(2)}) %collective-permute-start.7) | collective-permute-done | bytes 229408 | tf_op jit(solution)/shard_map/ppermute | solution.py:73
  22.7 1.4 %collective-permute-start.8 = (bf16[256,128]{1,0:T(8,128)(2,1)S(1)}, bf16[256,128]{1,0:T(8,128)(2,1)S(1)}, u32[]{:S(2)}, u32[]{:S(2)}) collective-permute-start(bf16[256,128]{1,0:T(8,128)(2,1)S(1)} %get-tuple-element.50), channel_id=1, source_target_pairs={{16,0},{24,8},{0,16},{8,24},{17,1},{25,9},{1,17},{9,25},{18,2},{26... | collective-permute-start | bytes 196616 | tf_op jit(solution)/shard_map/ppermute | solution.py:73
  24.1 0.8 %collective-permute-start.11 = (bf16[192,128]{1,0:T(8,128)(2,1)S(1)}, bf16[192,128]{1,0:T(8,128)(2,1)S(1)}, u32[]{:S(2)}, u32[]{:S(2)}) collective-permute-start(bf16[192,128]{1,0:T(8,128)(2,1)S(1)} %get-tuple-element.49.refs_2_), channel_id=1, source_target_pairs={{4,0},{0,4},{5,1},{1,5},{6,2},{2,6},{7,3},{3,7},{12,8},{8,12},{13,... | collective-permute-start | bytes 147464 | tf_op jit(solution)/shard_map/ppermute | solution.py:73
  25.5 0.7 %collective-permute-start.10 = (bf16[192,128]{1,0:T(8,128)(2,1)S(1)}, bf16[192,128]{1,0:T(8,128)(2,1)S(1)}, u32[]{:S(2)}, u32[]{:S(2)}) collective-permute-start(bf16[192,128]{1,0:T(8,128)(2,1)S(1)} %get-tuple-element.53), channel_id=1, source_target_pairs={{20,0},{16,4},{28,8},{24,12},{4,16},{0,20},{12,24},{8,28},{21,1},{... | collective-permute-start | bytes 147464 | tf_op jit(solution)/shard_map/ppermute | solution.py:81
  27.0 1.4 %collective-permute-start.13 = (bf16[192,128]{1,0:T(8,128)(2,1)S(1)}, bf16[192,128]{1,0:T(8,128)(2,1)S(1)}, u32[]{:S(2)}, u32[]{:S(2)}) collective-permute-start(bf16[192,128]{1,0:T(8,128)(2,1)S(1)} %shard_map.138.refs_0_), channel_id=1, source_target_pairs={{1,0},{0,1},{3,2},{2,3},{5,4},{4,5},{7,6},{6,7},{9,8},{8,9},{11,10... | collective-permute-start | bytes 147464 | tf_op jit(solution)/shard_map/ppermute | solution.py:73
  28.4 1.2 %collective-permute-done.10.refs_3_ = bf16[192,128]{1,0:T(8,128)(2,1)S(1)} collective-permute-done((bf16[192,128]{1,0:T(8,128)(2,1)S(1)}, bf16[192,128]{1,0:T(8,128)(2,1)S(1)}, u32[]{:S(2)}, u32[]{:S(2)}) %collective-permute-start.10) | collective-permute-done | bytes 49184 | tf_op jit(solution)/shard_map/ppermute | solution.py:81
  29.7 1.4 %collective-permute-start.12 = (bf16[192,128]{1,0:T(8,128)(2,1)S(1)}, bf16[192,128]{1,0:T(8,128)(2,1)S(1)}, u32[]{:S(2)}, u32[]{:S(2)}) collective-permute-start(bf16[192,128]{1,0:T(8,128)(2,1)S(1)} %shard_map.137.refs_0_), channel_id=1, source_target_pairs={{1,0},{0,1},{3,2},{2,3},{5,4},{4,5},{7,6},{6,7},{9,8},{8,9},{11,10... | collective-permute-start | bytes 147464 | tf_op jit(solution)/shard_map/ppermute | solution.py:73
  31.1 2.4 %collective-permute-start.15 = (bf16[192,128]{1,0:T(8,128)(2,1)S(1)}, bf16[192,128]{1,0:T(8,128)(2,1)S(1)}, u32[]{:S(2)}, u32[]{:S(2)}) collective-permute-start(bf16[192,128]{1,0:T(8,128)(2,1)S(1)} %shard_map.141.refs_2_), channel_id=1, source_target_pairs={{2,0},{3,1},{0,2},{1,3},{6,4},{7,5},{4,6},{5,7},{10,8},{11,9},{8,1... | collective-permute-start | bytes 147464 | tf_op jit(solution)/shard_map/ppermute | solution.py:73
  33.5 2.3 %collective-permute-start.14 = (bf16[192,128]{1,0:T(8,128)(2,1)S(1)}, bf16[192,128]{1,0:T(8,128)(2,1)S(1)}, u32[]{:S(2)}, u32[]{:S(2)}) collective-permute-start(bf16[192,128]{1,0:T(8,128)(2,1)S(1)} %shard_map.139.refs_5_.refs_0_), channel_id=1, source_target_pairs={{2,0},{3,1},{0,2},{1,3},{6,4},{7,5},{4,6},{5,7},{10,8},{11,9},{8,1... | collective-permute-start | bytes 147464 | tf_op jit(solution)/shard_map/ppermute | solution.py:73
  35.8 2.2 %shard_map.140 = (bf16[16,64,128]{2,1,0:T(8,128)(2,1)}, f32[8,128]{1,0:T(8,128)S(1)}) custom-call(bf16[16,64,128]{2,1,0:T(8,128)(2,1)S(1)} %get-tuple-element.43.refs_0_, bf16[16,64,128]{2,1,0:T(8,128)(2,1)S(1)} %get-tuple-element.44.refs_1_, bf16[896,128]{1,0:T(8,128)(2,1)S(1)} %collective-permute-done.7.refs_1_.refs_2_, ...), custom_call_target="tpu_custom_call" | custom-call | flops 301989888 | bytes 1380352 | tf_op jit(solution)/shard_map/pallas_call | solution.py:38
  38.8 1.5 %collective-permute-start.19 = (bf16[2,192,128]{2,1,0:T(8,128)(2,1)S(1)}, bf16[2,192,128]{2,1,0:T(8,128)(2,1)S(1)}, u32[]{:S(2)}, u32[]{:S(2)}) collective-permute-start(bf16[2,192,128]{2,1,0:T(8,128)(2,1)S(1)} %shard_map.142.refs_0_), channel_id=1, source_target_pairs={{16,0},{24,8},{0,16},{8,24},{17,1},{25,9},{1,17},{9,25},{18,2},{26... | collective-permute-start | bytes 294920 | tf_op jit(solution)/shard_map/ppermute | solution.py:73
  40.4 1.3 %collective-permute-done.16.refs_1_ = bf16[2,192,128]{2,1,0:T(8,128)(2,1)S(1)} collective-permute-done((bf16[2,192,128]{2,1,0:T(8,128)(2,1)S(1)}, bf16[2,192,128]{2,1,0:T(8,128)(2,1)S(1)}, u32[]{:S(2)}, u32[]{:S(2)}) %collective-permute-start.16) | collective-permute-done | bytes 98336 | tf_op jit(solution)/shard_map/ppermute | solution.py:73
  41.6 1.5 %collective-permute-start.20 = (bf16[2,192,128]{2,1,0:T(8,128)(2,1)S(1)}, bf16[2,192,128]{2,1,0:T(8,128)(2,1)S(1)}, u32[]{:S(2)}, u32[]{:S(2)}) collective-permute-start(bf16[2,192,128]{2,1,0:T(8,128)(2,1)S(1)} %collective-permute-done.16.refs_1_), channel_id=1, source_target_pairs={{16,0},{24,8},{0,16},{8,24},{17,1},{25,9},{1,17},{9,25},{18,2},{26... | collective-permute-start | bytes 294920 | tf_op jit(solution)/shard_map/ppermute | solution.py:73
  43.2 3.3 %collective-permute-start.17 = (bf16[2,192,128]{2,1,0:T(8,128)(2,1)S(1)}, bf16[2,192,128]{2,1,0:T(8,128)(2,1)S(1)}, u32[]{:S(2)}, u32[]{:S(2)}) collective-permute-start(bf16[2,192,128]{2,1,0:T(8,128)(2,1)S(1)} %shard_map.142.refs_0_), channel_id=1, source_target_pairs={{8,0},{0,8},{24,16},{16,24},{9,1},{1,9},{25,17},{17,25},{10,2},{2,... | collective-permute-start | bytes 294920 | tf_op jit(solution)/shard_map/ppermute | solution.py:73
  46.5 0.9 %collective-permute-start.21 = (bf16[2,192,128]{2,1,0:T(8,128)(2,1)S(1)}, bf16[2,192,128]{2,1,0:T(8,128)(2,1)S(1)}, u32[]{:S(2)}, u32[]{:S(2)}) collective-permute-start(bf16[2,192,128]{2,1,0:T(8,128)(2,1)S(1)} %collective-permute-done.19.refs_4_), channel_id=1, source_target_pairs={{8,0},{0,8},{24,16},{16,24},{9,1},{1,9},{25,17},{17,25},{10,2},{2,... | collective-permute-start | bytes 294920 | tf_op jit(solution)/shard_map/ppermute | solution.py:73
  47.4 3.7 %collective-permute-start.22 = (bf16[2,192,128]{2,1,0:T(8,128)(2,1)S(1)}, bf16[2,192,128]{2,1,0:T(8,128)(2,1)S(1)}, u32[]{:S(2)}, u32[]{:S(2)}) collective-permute-start(bf16[2,192,128]{2,1,0:T(8,128)(2,1)S(1)} %collective-permute-done.20.refs_5_), channel_id=1, source_target_pairs={{8,0},{0,8},{24,16},{16,24},{9,1},{1,9},{25,17},{17,25},{10,2},{2,... | collective-permute-start | bytes 294920 | tf_op jit(solution)/shard_map/ppermute | solution.py:73
  51.1 0.9 %collective-permute-done.22.refs_7_ = bf16[2,192,128]{2,1,0:T(8,128)(2,1)S(1)} collective-permute-done((bf16[2,192,128]{2,1,0:T(8,128)(2,1)S(1)}, bf16[2,192,128]{2,1,0:T(8,128)(2,1)S(1)}, u32[]{:S(2)}, u32[]{:S(2)}) %collective-permute-start.22) | collective-permute-done | bytes 98336 | tf_op jit(solution)/shard_map/ppermute | solution.py:73
  52.0 1.3 %shard_map.143 = (f32[3,384,128]{2,1,0:T(8,128)}, f32[384,128]{1,0:T(8,128)}, f32[3,384,128]{2,1,0:T(8,128)}, f32[384,128]{1,0:T(8,128)}) custom-call(bf16[2,192,128]{2,1,0:T(8,128)(2,1)S(1)} %shard_map.142.refs_0_, bf16[2,192,128]{2,1,0:T(8,128)(2,1)S(1)} %collective-permute-done.16.refs_1_, bf16[2,192,128]{2,1,0:T(8,128)(2,1)S(1)} %collective-permute-done.17.refs_2_, ...), custom_call_target="tpu_custom_call" | custom-call | flops 196608 | bytes 2359296 | tf_op jit(solution)/shard_map/pallas_call | solution.py:38
  (48 shorter events, 3.0 us)
Async XLA Ops:
  0.6 10.1 %collective-permute-start.3 = (bf16[16,64,128]{2,1,0:T(8,128)(2,1)}, bf16[16,64,128]{2,1,0:T(8,128)(2,1)S(1)}, u32[]{:S(2)}, u32[]{:S(2)}) collective-permute-start(bf16[16,64,128]{2,1,0:T(8,128)(2,1)} %bitcast.10), channel_id=1, source_target_pairs={{4,0},{0,4},{5,1},{1,5},{6,2},{2,6},{7,3},{3,7},{12,8},{8,12},{13,... | collective-permute-start | bytes 786440 | tf_op jit(solution)/shard_map/ppermute | solution.py:73
  2.7 5.0 %copy-start = (bf16[1,1,16,64,128]{4,3,2,1,0:T(8,128)(2,1)S(1)}, bf16[1,1,16,64,128]{4,3,2,1,0:T(8,128)(2,1)}, u32[]{:S(2)}) copy-start(bf16[1,1,16,64,128]{4,3,2,1,0:T(8,128)(2,1)} %param.9) | copy-start | bytes 786436
  2.7 5.0 %copy-start.1 = (bf16[3,3,128,128]{3,2,1,0:T(8,128)(2,1)S(1)}, bf16[3,3,128,128]{3,2,1,0:T(8,128)(2,1)}, u32[]{:S(2)}) copy-start(bf16[3,3,128,128]{3,2,1,0:T(8,128)(2,1)} %refs_7_.1) | copy-start | bytes 884740
  2.7 5.0 %copy-start.2 = (bf16[1,1,16,64,128]{4,3,2,1,0:T(8,128)(2,1)S(1)}, bf16[1,1,16,64,128]{4,3,2,1,0:T(8,128)(2,1)}, u32[]{:S(2)}) copy-start(bf16[1,1,16,64,128]{4,3,2,1,0:T(8,128)(2,1)} %param.13) | copy-start | bytes 786436
  2.7 5.0 %copy-start.5 = (bf16[3,128,128]{2,1,0:T(8,128)(2,1)S(1)}, bf16[3,128,128]{2,1,0:T(8,128)(2,1)}, u32[]{:S(2)}) copy-start(bf16[3,128,128]{2,1,0:T(8,128)(2,1)} %refs_6_.3) | copy-start | bytes 294916
  4.4 2.1 %collective-permute-start.1 = (bf16[4,64,128]{2,1,0:T(8,128)(2,1)}, bf16[4,64,128]{2,1,0:T(8,128)(2,1)S(1)}, u32[]{:S(2)}, u32[]{:S(2)}) collective-permute-start(bf16[4,64,128]{2,1,0:T(8,128)(2,1)} %get-tuple-element.35), channel_id=1, source_target_pairs={{8,0},{0,8},{24,16},{16,24},{9,1},{1,9},{25,17},{17,25},{10,2},{2,... | collective-permute-start | bytes 196616 | tf_op jit(solution)/shard_map/ppermute | solution.py:73
  5.4 2.4 %collective-permute-start = (bf16[4,64,128]{2,1,0:T(8,128)(2,1)}, bf16[4,64,128]{2,1,0:T(8,128)(2,1)S(1)}, u32[]{:S(2)}, u32[]{:S(2)}) collective-permute-start(bf16[4,64,128]{2,1,0:T(8,128)(2,1)} %get-tuple-element.34), channel_id=1, source_target_pairs={{8,0},{0,8},{24,16},{16,24},{9,1},{1,9},{25,17},{17,25},{10,2},{2,... | collective-permute-start | bytes 196616 | tf_op jit(solution)/shard_map/ppermute | solution.py:73
  6.5 3.3 %collective-permute-start.2 = (bf16[4,64,128]{2,1,0:T(8,128)(2,1)S(1)}, bf16[4,64,128]{2,1,0:T(8,128)(2,1)S(1)}, u32[]{:S(2)}, u32[]{:S(2)}) collective-permute-start(bf16[4,64,128]{2,1,0:T(8,128)(2,1)S(1)} %collective-permute-done.1.refs_5_), channel_id=1, source_target_pairs={{16,0},{24,8},{0,16},{8,24},{17,1},{25,9},{1,17},{9,25},{18,2},{26... | collective-permute-start | bytes 196616 | tf_op jit(solution)/shard_map/ppermute | solution.py:73
  9.8 2.6 %copy-start.4 = (bf16[1,1,16,64,128]{4,3,2,1,0:T(8,128)(2,1)S(1)}, bf16[1,1,16,64,128]{4,3,2,1,0:T(8,128)(2,1)}, u32[]{:S(2)}) copy-start(bf16[1,1,16,64,128]{4,3,2,1,0:T(8,128)(2,1)} %param.12) | copy-start | bytes 786436
  9.8 7.8 %collective-permute-start.4 = (bf16[18,64,128]{2,1,0:T(8,128)(2,1)S(1)}, bf16[18,64,128]{2,1,0:T(8,128)(2,1)S(1)}, u32[]{:S(2)}, u32[]{:S(2)}) collective-permute-start(bf16[18,64,128]{2,1,0:T(8,128)(2,1)S(1)} %shard_map.130.refs_7_), channel_id=1, source_target_pairs={{4,0},{0,4},{5,1},{1,5},{6,2},{2,6},{7,3},{3,7},{12,8},{8,12},{13,... | collective-permute-start | bytes 884744 | tf_op jit(solution)/shard_map/ppermute | solution.py:73
  12.5 5.1 %copy-start.8 = (bf16[3,128,128]{2,1,0:T(8,128)(2,1)S(1)}, bf16[3,128,128]{2,1,0:T(8,128)(2,1)}, u32[]{:S(2)}) copy-start(bf16[3,128,128]{2,1,0:T(8,128)(2,1)} %refs_10_.1) | copy-start | bytes 294916
  13.6 2.3 %collective-permute-start.5 = (bf16[768,128]{1,0:T(8,128)(2,1)S(1)}, bf16[768,128]{1,0:T(8,128)(2,1)S(1)}, u32[]{:S(2)}, u32[]{:S(2)}) collective-permute-start(bf16[768,128]{1,0:T(8,128)(2,1)S(1)} %get-tuple-element.41), channel_id=1, source_target_pairs={{8,0},{0,8},{24,16},{16,24},{9,1},{1,9},{25,17},{17,25},{10,2},{2,... | collective-permute-start | bytes 589832 | tf_op jit(solution)/shard_map/ppermute | solution.py:73
  15.9 1.7 %copy-start.3 = (bf16[1,1,16,64,128]{4,3,2,1,0:T(8,128)(2,1)S(1)}, bf16[1,1,16,64,128]{4,3,2,1,0:T(8,128)(2,1)}, u32[]{:S(2)}) copy-start(bf16[1,1,16,64,128]{4,3,2,1,0:T(8,128)(2,1)} %param.10) | copy-start | bytes 786436
  15.9 1.7 %copy-start.7 = (bf16[1,1,16,64,128]{4,3,2,1,0:T(8,128)(2,1)S(1)}, bf16[1,1,16,64,128]{4,3,2,1,0:T(8,128)(2,1)}, u32[]{:S(2)}) copy-start(bf16[1,1,16,64,128]{4,3,2,1,0:T(8,128)(2,1)} %param.11) | copy-start | bytes 786436
  16.0 4.3 %collective-permute-start.6 = (bf16[384,128]{1,0:T(8,128)(2,1)S(1)}, bf16[384,128]{1,0:T(8,128)(2,1)S(1)}, u32[]{:S(2)}, u32[]{:S(2)}) collective-permute-start(bf16[384,128]{1,0:T(8,128)(2,1)S(1)} %get-tuple-element.46), channel_id=1, source_target_pairs={{16,0},{24,8},{0,16},{8,24},{17,1},{25,9},{1,17},{9,25},{18,2},{26... | collective-permute-start | bytes 294920 | tf_op jit(solution)/shard_map/ppermute | solution.py:73
  20.3 2.3 %collective-permute-start.7 = (bf16[896,128]{1,0:T(8,128)(2,1)S(1)}, bf16[896,128]{1,0:T(8,128)(2,1)S(1)}, u32[]{:S(2)}, u32[]{:S(2)}) collective-permute-start(bf16[896,128]{1,0:T(8,128)(2,1)S(1)} %get-tuple-element.47), channel_id=1, source_target_pairs={{8,0},{0,8},{24,16},{16,24},{9,1},{1,9},{25,17},{17,25},{10,2},{2,... | collective-permute-start | bytes 688136 | tf_op jit(solution)/shard_map/ppermute | solution.py:73
  22.7 7.0 %collective-permute-start.8 = (bf16[256,128]{1,0:T(8,128)(2,1)S(1)}, bf16[256,128]{1,0:T(8,128)(2,1)S(1)}, u32[]{:S(2)}, u32[]{:S(2)}) collective-permute-start(bf16[256,128]{1,0:T(8,128)(2,1)S(1)} %get-tuple-element.50), channel_id=1, source_target_pairs={{16,0},{24,8},{0,16},{8,24},{17,1},{25,9},{1,17},{9,25},{18,2},{26... | collective-permute-start | bytes 196616 | tf_op jit(solution)/shard_map/ppermute | solution.py:73
  24.1 2.9 %collective-permute-start.11 = (bf16[192,128]{1,0:T(8,128)(2,1)S(1)}, bf16[192,128]{1,0:T(8,128)(2,1)S(1)}, u32[]{:S(2)}, u32[]{:S(2)}) collective-permute-start(bf16[192,128]{1,0:T(8,128)(2,1)S(1)} %get-tuple-element.49.refs_2_), channel_id=1, source_target_pairs={{4,0},{0,4},{5,1},{1,5},{6,2},{2,6},{7,3},{3,7},{12,8},{8,12},{13,... | collective-permute-start | bytes 147464 | tf_op jit(solution)/shard_map/ppermute | solution.py:73
  24.9 3.6 %collective-permute-start.9 = (bf16[192,128]{1,0:T(8,128)(2,1)S(1)}, bf16[192,128]{1,0:T(8,128)(2,1)S(1)}, u32[]{:S(2)}, u32[]{:S(2)}) collective-permute-start(bf16[192,128]{1,0:T(8,128)(2,1)S(1)} %get-tuple-element.52), channel_id=1, source_target_pairs={{4,0},{0,4},{5,1},{1,5},{6,2},{2,6},{7,3},{3,7},{12,8},{8,12},{13,... | collective-permute-start | bytes 147464 | tf_op jit(solution)/shard_map/ppermute | solution.py:73
  25.5 4.1 %collective-permute-start.10 = (bf16[192,128]{1,0:T(8,128)(2,1)S(1)}, bf16[192,128]{1,0:T(8,128)(2,1)S(1)}, u32[]{:S(2)}, u32[]{:S(2)}) collective-permute-start(bf16[192,128]{1,0:T(8,128)(2,1)S(1)} %get-tuple-element.53), channel_id=1, source_target_pairs={{20,0},{16,4},{28,8},{24,12},{4,16},{0,20},{12,24},{8,28},{21,1},{... | collective-permute-start | bytes 147464 | tf_op jit(solution)/shard_map/ppermute | solution.py:81
  27.0 4.0 %collective-permute-start.13 = (bf16[192,128]{1,0:T(8,128)(2,1)S(1)}, bf16[192,128]{1,0:T(8,128)(2,1)S(1)}, u32[]{:S(2)}, u32[]{:S(2)}) collective-permute-start(bf16[192,128]{1,0:T(8,128)(2,1)S(1)} %shard_map.138.refs_0_), channel_id=1, source_target_pairs={{1,0},{0,1},{3,2},{2,3},{5,4},{4,5},{7,6},{6,7},{9,8},{8,9},{11,10... | collective-permute-start | bytes 147464 | tf_op jit(solution)/shard_map/ppermute | solution.py:73
  29.7 6.1 %copy-start.6 = (bf16[3,3,128,128]{3,2,1,0:T(8,128)(2,1)S(1)}, bf16[3,3,128,128]{3,2,1,0:T(8,128)(2,1)}, u32[]{:S(2)}) copy-start(bf16[3,3,128,128]{3,2,1,0:T(8,128)(2,1)} %refs_4_.3) | copy-start | bytes 884740
  29.7 3.8 %collective-permute-start.12 = (bf16[192,128]{1,0:T(8,128)(2,1)S(1)}, bf16[192,128]{1,0:T(8,128)(2,1)S(1)}, u32[]{:S(2)}, u32[]{:S(2)}) collective-permute-start(bf16[192,128]{1,0:T(8,128)(2,1)S(1)} %shard_map.137.refs_0_), channel_id=1, source_target_pairs={{1,0},{0,1},{3,2},{2,3},{5,4},{4,5},{7,6},{6,7},{9,8},{8,9},{11,10... | collective-permute-start | bytes 147464 | tf_op jit(solution)/shard_map/ppermute | solution.py:73
  31.1 7.0 %collective-permute-start.15 = (bf16[192,128]{1,0:T(8,128)(2,1)S(1)}, bf16[192,128]{1,0:T(8,128)(2,1)S(1)}, u32[]{:S(2)}, u32[]{:S(2)}) collective-permute-start(bf16[192,128]{1,0:T(8,128)(2,1)S(1)} %shard_map.141.refs_2_), channel_id=1, source_target_pairs={{2,0},{3,1},{0,2},{1,3},{6,4},{7,5},{4,6},{5,7},{10,8},{11,9},{8,1... | collective-permute-start | bytes 147464 | tf_op jit(solution)/shard_map/ppermute | solution.py:73
  33.5 4.6 %collective-permute-start.14 = (bf16[192,128]{1,0:T(8,128)(2,1)S(1)}, bf16[192,128]{1,0:T(8,128)(2,1)S(1)}, u32[]{:S(2)}, u32[]{:S(2)}) collective-permute-start(bf16[192,128]{1,0:T(8,128)(2,1)S(1)} %shard_map.139.refs_5_.refs_0_), channel_id=1, source_target_pairs={{2,0},{3,1},{0,2},{1,3},{6,4},{7,5},{4,6},{5,7},{10,8},{11,9},{8,1... | collective-permute-start | bytes 147464 | tf_op jit(solution)/shard_map/ppermute | solution.py:73
  38.1 3.5 %collective-permute-start.16 = (bf16[2,192,128]{2,1,0:T(8,128)(2,1)S(1)}, bf16[2,192,128]{2,1,0:T(8,128)(2,1)S(1)}, u32[]{:S(2)}, u32[]{:S(2)}) collective-permute-start(bf16[2,192,128]{2,1,0:T(8,128)(2,1)S(1)} %shard_map.142.refs_0_), channel_id=1, source_target_pairs={{4,0},{0,4},{5,1},{1,5},{6,2},{2,6},{7,3},{3,7},{12,8},{8,12},{13,... | collective-permute-start | bytes 294920 | tf_op jit(solution)/shard_map/ppermute | solution.py:73
  38.8 7.7 %collective-permute-start.19 = (bf16[2,192,128]{2,1,0:T(8,128)(2,1)S(1)}, bf16[2,192,128]{2,1,0:T(8,128)(2,1)S(1)}, u32[]{:S(2)}, u32[]{:S(2)}) collective-permute-start(bf16[2,192,128]{2,1,0:T(8,128)(2,1)S(1)} %shard_map.142.refs_0_), channel_id=1, source_target_pairs={{16,0},{24,8},{0,16},{8,24},{17,1},{25,9},{1,17},{9,25},{18,2},{26... | collective-permute-start | bytes 294920 | tf_op jit(solution)/shard_map/ppermute | solution.py:73
  41.6 5.8 %collective-permute-start.20 = (bf16[2,192,128]{2,1,0:T(8,128)(2,1)S(1)}, bf16[2,192,128]{2,1,0:T(8,128)(2,1)S(1)}, u32[]{:S(2)}, u32[]{:S(2)}) collective-permute-start(bf16[2,192,128]{2,1,0:T(8,128)(2,1)S(1)} %collective-permute-done.16.refs_1_), channel_id=1, source_target_pairs={{16,0},{24,8},{0,16},{8,24},{17,1},{25,9},{1,17},{9,25},{18,2},{26... | collective-permute-start | bytes 294920 | tf_op jit(solution)/shard_map/ppermute | solution.py:73
  43.2 7.9 %collective-permute-start.17 = (bf16[2,192,128]{2,1,0:T(8,128)(2,1)S(1)}, bf16[2,192,128]{2,1,0:T(8,128)(2,1)S(1)}, u32[]{:S(2)}, u32[]{:S(2)}) collective-permute-start(bf16[2,192,128]{2,1,0:T(8,128)(2,1)S(1)} %shard_map.142.refs_0_), channel_id=1, source_target_pairs={{8,0},{0,8},{24,16},{16,24},{9,1},{1,9},{25,17},{17,25},{10,2},{2,... | collective-permute-start | bytes 294920 | tf_op jit(solution)/shard_map/ppermute | solution.py:73
  46.5 4.6 %collective-permute-start.18 = (bf16[2,192,128]{2,1,0:T(8,128)(2,1)S(1)}, bf16[2,192,128]{2,1,0:T(8,128)(2,1)S(1)}, u32[]{:S(2)}, u32[]{:S(2)}) collective-permute-start(bf16[2,192,128]{2,1,0:T(8,128)(2,1)S(1)} %collective-permute-done.16.refs_1_), channel_id=1, source_target_pairs={{8,0},{0,8},{24,16},{16,24},{9,1},{1,9},{25,17},{17,25},{10,2},{2,... | collective-permute-start | bytes 294920 | tf_op jit(solution)/shard_map/ppermute | solution.py:73
  46.5 4.6 %collective-permute-start.21 = (bf16[2,192,128]{2,1,0:T(8,128)(2,1)S(1)}, bf16[2,192,128]{2,1,0:T(8,128)(2,1)S(1)}, u32[]{:S(2)}, u32[]{:S(2)}) collective-permute-start(bf16[2,192,128]{2,1,0:T(8,128)(2,1)S(1)} %collective-permute-done.19.refs_4_), channel_id=1, source_target_pairs={{8,0},{0,8},{24,16},{16,24},{9,1},{1,9},{25,17},{17,25},{10,2},{2,... | collective-permute-start | bytes 294920 | tf_op jit(solution)/shard_map/ppermute | solution.py:73
  47.4 4.6 %collective-permute-start.22 = (bf16[2,192,128]{2,1,0:T(8,128)(2,1)S(1)}, bf16[2,192,128]{2,1,0:T(8,128)(2,1)S(1)}, u32[]{:S(2)}, u32[]{:S(2)}) collective-permute-start(bf16[2,192,128]{2,1,0:T(8,128)(2,1)S(1)} %collective-permute-done.20.refs_5_), channel_id=1, source_target_pairs={{8,0},{0,8},{24,16},{16,24},{9,1},{1,9},{25,17},{17,25},{10,2},{2,... | collective-permute-start | bytes 294920 | tf_op jit(solution)/shard_map/ppermute | solution.py:73

commit v8 on v7

--- a/solution.py
+++ b/solution.py
@@ -23,12 +23,15 @@
     return jax.ShapeDtypeStruct(shape, jnp.float32)
 
 
-def call(kernel, outs, scratch, flops, *operands, after=(), spare_inputs=False, limit=24):
+def call(
+    kernel, outs, scratch, flops, *operands, after=(), spare_inputs=False, outs_where=pltpu.VMEM, limit=24
+):
     single = len(outs) == 1
     moved = sum(math.prod(x.shape) * x.dtype.itemsize for x in (*operands, *outs))
     vmem = pl.BlockSpec(memory_space=pltpu.VMEM)
     spare = pl.BlockSpec(memory_space=pl.ANY)
     spec = spare if spare_inputs else vmem
+    out_spec = pl.BlockSpec(memory_space=outs_where)
     count = len(operands)
     operands = (*operands, *after)
 
@@ -39,7 +42,7 @@
         body,
         out_shape=outs[0] if single else tuple(outs),
         in_specs=[spec] * count + [spare] * len(after),
-        out_specs=vmem if single else (vmem,) * len(outs),
+        out_specs=out_spec if single else (out_spec,) * len(outs),
         scratch_shapes=scratch,
         compiler_params=pltpu.CompilerParams(vmem_limit_bytes=limit * MIB),
         cost_estimate=pl.CostEstimate(
@@ -407,48 +410,48 @@
     out_ref[...] = total.astype(jnp.bfloat16)
 
 
-def scaled_kernel(factor, *refs):
-    out_ref = refs[-1]
-    for block in range(2):
-        one, two = (ref[...].astype(jnp.float32) for ref in refs[2 * block : 2 * block + 2])
-        out_ref[block] = ((one + two) * factor).astype(jnp.bfloat16)
+def scaled_kernel(factor, one_ref, two_ref, out_ref):
+    total = one_ref[...].astype(jnp.float32) + two_ref[...].astype(jnp.float32)
+    out_ref[...] = (total * factor).astype(jnp.bfloat16)
 
 
 def place_kernel(*refs):
-    shares, outs = refs[:-4], refs[-4:]
+    shares, (spatial_ref, temporal_ref, sums_ref, sems) = refs[:-4], refs[-4:]
     band, frame = lax.axis_index("section"), lax.axis_index("video")
-    halves = len(shares) // 4
-    height = shares[0].shape[1]
+    parts = len(shares) // 4
+    height = shares[0].shape[0]
     for n, share in enumerate(shares):
-        place = jnp.bitwise_xor(band, n // halves)
-        half = jnp.bitwise_xor(frame, n % halves) if halves == 2 else 0
+        place = jnp.bitwise_xor(band, n // parts)
+        half = jnp.bitwise_xor(frame, n % parts) if parts == 2 else 0
         here = pl.ds(pl.multiple_of(half * height, height), height)
 
-        @pl.when(place < 3)
-        def _():
-            for block in range(2):
-                outs[2 * block][place, here] = share[block].astype(jnp.float32)
-
-        @pl.when(place == 3)
-        def _():
-            for block in range(2):
-                outs[2 * block + 1][here] = share[block].astype(jnp.float32)
-
-
-def place(shares):
-    across = [flipped(share, "section", 2) for share in shares]
-    ch = shares[0].shape[2]
-    outs = call(
+        sums_ref[place, here] = share[...].astype(jnp.float32)
+
+    copies = [
+        pltpu.make_async_copy(sums_ref.at[pl.ds(0, 3)], spatial_ref, sems.at[0]),
+        pltpu.make_async_copy(sums_ref.at[3], temporal_ref, sems.at[1]),
+    ]
+    for copy in copies:
+        copy.start()
+    for copy in copies:
+        copy.wait()
+
+
+def placed(shares, across, after=()):
+    ch = shares[0].shape[1]
+    spatial, temporal = call(
         place_kernel,
-        [f32(3, 3 * ch, ch), f32(3 * ch, ch)] * 2,
-        [],
+        [f32(3, 3 * ch, ch), f32(3 * ch, ch)],
+        [pltpu.VMEM((4, 3 * ch, ch), jnp.float32), pltpu.SemaphoreType.DMA((2,))],
         12 * ch * ch,
         *shares,
         *[flipped(share, "section", 1) for share in shares],
         *across,
         *[flipped(share, "section", 1) for share in across],
-    )
-    return [x.reshape(3, 3, ch, ch) if x.ndim == 3 else x.reshape(3, ch, ch) for x in outs]
+        after=after,
+        outs_where=pltpu.HBM,
+    )
+    return spatial.reshape(3, 3, ch, ch), temporal.reshape(3, ch, ch)
 
 
 def on_device(
@@ -622,8 +625,8 @@
 
     if split:
 
-        def added(one, two):
-            return call(add_kernel, [bf16(half, ch)], [], half * ch, one, two)
+        def added(one, two, after=()):
+            return call(add_kernel, [bf16(half, ch)], [], half * ch, one, two, after=after)
 
         keep_two, send_two = call(
             band_kernel,
@@ -643,23 +646,27 @@
         sum_one = call(plane_kernel, [bf16(half, ch)], [], 4 * half * ch, own_one, *parts)
         part_two = flipped(sum_two, "dp", 1)
         part_one = flipped(later_than(sum_one, sum_two), "dp", 1)
-        sum_two = added(sum_two, part_two)
+        sum_two = added(sum_two, part_two, after=(sum_one,))
         sum_one = added(sum_one, part_one)
         last_two = flipped(sum_two, "dp", 2)
         last_one = flipped(later_than(sum_one, sum_two), "dp", 2)
-        grad_in, token = input_gradient(across, (sum_one,))
-        own = call(
-            functools.partial(scaled_kernel, factor),
-            [bf16(2, half, ch)],
-            [],
-            height * ch,
-            sum_one,
-            last_one,
-            sum_two,
-            last_two,
-            after=(token,),
-        )
-        sums = place([own, flipped(own, "video", 1)])
+
+        def scaled(one, two, after=()):
+            kernel = functools.partial(scaled_kernel, factor)
+            return call(kernel, [bf16(half, ch)], [], half * ch, one, two, after=after)
+
+        def gathered(own):
+            shares = [own, flipped(own, "video", 1)]
+            return shares, [flipped(own, "section", 2), flipped_both(own)]
+
+        own_two = scaled(sum_two, last_two, after=(sum_one,))
+        own_one = scaled(sum_one, last_one, after=(own_two,))
+        parts_one, parts_two = gathered(own_one), gathered(own_two)
+        sums_two = placed(*parts_two)
+        grad_in, token = input_gradient(across, (own_one,))
+        *parts_one, token = lax.optimization_barrier((*parts_one, token))
+        sums_one = placed(*parts_one, after=(token,))
+        sums = (*sums_one, *sums_two)
     else:
         own_one, send_one = call(
             pair_kernel, [f32(height, ch), bf16(height, ch)], [], height * ch, keep_one, pair_one
@@ -668,8 +675,11 @@
         grad_in, _ = input_gradient(edge, ())
         own_one = own_one + flipped(send_one, "section", 2).astype(jnp.float32)
         own_two = own_two + across_two.astype(jnp.float32)
-        share = lax.psum(jnp.stack((own_one, own_two)), ("video", "dp")) * factor
-        sums = place([share.astype(jnp.bfloat16)])
+        both = lax.psum((own_one, own_two), ("video", "dp"))
+        sums = []
+        for share in both:
+            share = (share * factor).astype(jnp.bfloat16)
+            sums += placed([share], [flipped(share, "section", 2)])
     return (grad_in.reshape(shape), *sums)
 
 

time: 53.9 us -> 53.7 us (level)
  waiting for transfers between devices: 9.93 us -> 7.89 us
  starting transfers between devices: 32.2 us -> 33.5 us
  Pallas kernels: 10.4 us -> 11 us
    ppermute x1 -> x3, starting transfers between devices: 0.75 us -> 3.41 us  [flipped_both(): return lax.ppermute(block, ('section', 'video'), pairs)]
    ppermute x22 -> x27, waiting for transfers between devices: 8.7 us -> 6.66 us  [flipped(): lax.ppermute(block, axis, [(place ^ flip, place) for place in range(count)])]
    ppermute x22 -> x27, starting transfers between devices: 31.4 us -> 30.1 us  [flipped(): lax.ppermute(block, axis, [(place ^ flip, place) for place in range(count)])]
    pallas_call x16 -> x18, Pallas kernels: 10.4 us -> 11 us  [call(): pl.pallas_call(body, out_shape=outs[0] if single else tuple(outs), in_spe...]
    ppermute x1 -> x3, waiting for transfers between devices: 1.23 us -> 1.23 us  [flipped_both(): return lax.ppermute(block, ('section', 'video'), pairs)]
  transfers between devices with their start and end apart: 23 -> 30, of which waited for: 9 -> 8; matrix products, arithmetic and copies ran while one was open for 0% -> 0% of each run, Pallas kernels for 17% -> 19%
where the time goes in v8:
time: 53.7 us; the launch traced here: 53.3 us
  starting transfers between devices  33.5 us (62%)
  Pallas kernels  11 us (20%)
  waiting for transfers between devices  7.89 us (15%)
  between operations  0.82 us (2%)
    ppermute x27, starting transfers between devices, flipped(): lax.ppermute(block, axis, [(place ^ flip, place) for place in range(count)])  30.1 us
    pallas_call x18, Pallas kernels, call(): pl.pallas_call(body, out_shape=outs[0] if single else tuple(outs), in_spe...  11 us
    ppermute x27, waiting for transfers between devices, flipped(): lax.ppermute(block, axis, [(place ^ flip, place) for place in range(count)])  6.66 us
    ppermute x3, starting transfers between devices, flipped_both(): return lax.ppermute(block, ('section', 'video'), pairs)  3.41 us
    ppermute x3, waiting for transfers between devices, flipped_both(): return lax.ppermute(block, ('section', 'video'), pairs)  1.23 us
  transfers between devices with their start and end apart: 30, of which 8 were waited for; matrix products, arithmetic and copies ran while one was open for 0% of the time, Pallas kernels for 19%

profile of v8, /device:TPU:1, one launch (start us, length us, event | category | flops | bytes accessed | tf_op | source)
XLA Modules:
  0.0 53.3 jit_solution(8539493750744765026)
XLA Ops:
  0.6 2.1 %collective-permute-start.3 = (bf16[16,64,128]{2,1,0:T(8,128)(2,1)}, bf16[16,64,128]{2,1,0:T(8,128)(2,1)S(1)}, u32[]{:S(2)}, u32[]{:S(2)}) collective-permute-start(bf16[16,64,128]{2,1,0:T(8,128)(2,1)} %bitcast.10), channel_id=1, source_target_pairs={{4,0},{0,4},{5,1},{1,5},{6,2},{2,6},{7,3},{3,7},{12,8},{8,12},{13,... | collective-permute-start | bytes 786440 | tf_op jit(solution)/shard_map/ppermute | solution.py:76
  2.7 1.6 %shard_map.128 = (bf16[4,64,128]{2,1,0:T(8,128)(2,1)}, bf16[4,64,128]{2,1,0:T(8,128)(2,1)}) custom-call(bf16[16,64,128]{2,1,0:T(8,128)(2,1)} %bitcast.11, bf16[16,64,128]{2,1,0:T(8,128)(2,1)} %bitcast.17, bf16[16,64,128]{2,1,0:T(8,128)(2,1)} %bitcast.23, bf16[16,64,128]{2,1,0:T(8,128)(2,1)} %bitcast.21), custom_call_target="tpu_custom_call" | custom-call | flops 1 | bytes 1179648 | tf_op jit(solution)/shard_map/pallas_call | solution.py:41
  4.4 1.0 %collective-permute-start.1 = (bf16[4,64,128]{2,1,0:T(8,128)(2,1)}, bf16[4,64,128]{2,1,0:T(8,128)(2,1)S(1)}, u32[]{:S(2)}, u32[]{:S(2)}) collective-permute-start(bf16[4,64,128]{2,1,0:T(8,128)(2,1)} %get-tuple-element.40), channel_id=1, source_target_pairs={{8,0},{0,8},{24,16},{16,24},{9,1},{1,9},{25,17},{17,25},{10,2},{2,... | collective-permute-start | bytes 196616 | tf_op jit(solution)/shard_map/ppermute | solution.py:76
  5.5 1.0 %collective-permute-done.1.refs_5_ = bf16[4,64,128]{2,1,0:T(8,128)(2,1)S(1)} collective-permute-done((bf16[4,64,128]{2,1,0:T(8,128)(2,1)}, bf16[4,64,128]{2,1,0:T(8,128)(2,1)S(1)}, u32[]{:S(2)}, u32[]{:S(2)}) %collective-permute-start.1) | collective-permute-done | bytes 65568 | tf_op jit(solution)/shard_map/ppermute | solution.py:76
  6.5 1.2 %collective-permute-start.2 = (bf16[4,64,128]{2,1,0:T(8,128)(2,1)S(1)}, bf16[4,64,128]{2,1,0:T(8,128)(2,1)S(1)}, u32[]{:S(2)}, u32[]{:S(2)}) collective-permute-start(bf16[4,64,128]{2,1,0:T(8,128)(2,1)S(1)} %collective-permute-done.1.refs_5_), channel_id=1, source_target_pairs={{16,0},{24,8},{0,16},{8,24},{17,1},{25,9},{1,17},{9,25},{18,2},{26... | collective-permute-start | bytes 196616 | tf_op jit(solution)/shard_map/ppermute | solution.py:76
  7.8 2.0 %collective-permute-done.2.refs_2_.refs_4_ = bf16[4,64,128]{2,1,0:T(8,128)(2,1)S(1)} collective-permute-done((bf16[4,64,128]{2,1,0:T(8,128)(2,1)S(1)}, bf16[4,64,128]{2,1,0:T(8,128)(2,1)S(1)}, u32[]{:S(2)}, u32[]{:S(2)}) %collective-permute-start.2) | collective-permute-done | bytes 65568 | tf_op jit(solution)/shard_map/ppermute | solution.py:76
  9.8 0.9 %collective-permute-start.4 = (bf16[18,64,128]{2,1,0:T(8,128)(2,1)S(1)}, bf16[18,64,128]{2,1,0:T(8,128)(2,1)S(1)}, u32[]{:S(2)}, u32[]{:S(2)}) collective-permute-start(bf16[18,64,128]{2,1,0:T(8,128)(2,1)S(1)} %shard_map.130.refs_7_), channel_id=1, source_target_pairs={{4,0},{0,4},{5,1},{1,5},{6,2},{2,6},{7,3},{3,7},{12,8},{8,12},{13,... | collective-permute-start | bytes 884744 | tf_op jit(solution)/shard_map/ppermute | solution.py:76
  10.7 1.7 %shard_map.131 = (bf16[14,64,128]{2,1,0:T(8,128)(2,1)S(1)}, bf16[16,64,128]{2,1,0:T(8,128)(2,1)S(1)}) custom-call(bf16[16,64,128]{2,1,0:T(8,128)(2,1)S(1)} %bitcast.14, bf16[16,64,128]{2,1,0:T(8,128)(2,1)S(1)} %bitcast.19, bf16[16,64,128]{2,1,0:T(8,128)(2,1)S(1)} %collective-permute-done.3.refs_2_.refs_6_, bf16[3,128,128]{2,1,0:T(8,128)(2,1)S(1)} %copy-done.5, ...), custom_call_target="tpu_custom_call" | custom-call | flops 362387872 | bytes 2162688 | tf_op jit(solution)/shard_map/pallas_call | solution.py:41
  12.5 1.1 %shard_map.132 = (f32[2,384,128]{2,1,0:T(8,128)S(1)}, bf16[768,128]{1,0:T(8,128)(2,1)S(1)}) custom-call(bf16[16,64,128]{2,1,0:T(8,128)(2,1)S(1)} %bitcast.24, bf16[16,64,128]{2,1,0:T(8,128)(2,1)S(1)} %bitcast.20, bf16[16,64,128]{2,1,0:T(8,128)(2,1)S(1)} %get-tuple-element.44.refs_2_.refs_4_, ...), custom_call_target="tpu_custom_call" | custom-call | flops 362387872 | bytes 2031616 | tf_op jit(solution)/shard_map/pallas_call | solution.py:41
  13.6 1.2 %collective-permute-start.5 = (bf16[768,128]{1,0:T(8,128)(2,1)S(1)}, bf16[768,128]{1,0:T(8,128)(2,1)S(1)}, u32[]{:S(2)}, u32[]{:S(2)}) collective-permute-start(bf16[768,128]{1,0:T(8,128)(2,1)S(1)} %get-tuple-element.46), channel_id=1, source_target_pairs={{8,0},{0,8},{24,16},{16,24},{9,1},{1,9},{25,17},{17,25},{10,2},{2,... | collective-permute-start | bytes 589832 | tf_op jit(solution)/shard_map/ppermute | solution.py:76
  14.9 1.1 %collective-permute-done.5.refs_1_ = bf16[768,128]{1,0:T(8,128)(2,1)S(1)} collective-permute-done((bf16[768,128]{1,0:T(8,128)(2,1)S(1)}, bf16[768,128]{1,0:T(8,128)(2,1)S(1)}, u32[]{:S(2)}, u32[]{:S(2)}) %collective-permute-start.5) | collective-permute-done | bytes 196640 | tf_op jit(solution)/shard_map/ppermute | solution.py:76
  16.0 1.6 %collective-permute-start.6 = (bf16[384,128]{1,0:T(8,128)(2,1)S(1)}, bf16[384,128]{1,0:T(8,128)(2,1)S(1)}, u32[]{:S(2)}, u32[]{:S(2)}) collective-permute-start(bf16[384,128]{1,0:T(8,128)(2,1)S(1)} %get-tuple-element.51), channel_id=1, source_target_pairs={{16,0},{24,8},{0,16},{8,24},{17,1},{25,9},{1,17},{9,25},{18,2},{26... | collective-permute-start | bytes 294920 | tf_op jit(solution)/shard_map/ppermute | solution.py:76
  17.6 2.2 %shard_map.134 = (bf16[16,64,128]{2,1,0:T(8,128)(2,1)S(1)}, bf16[16,64,128]{2,1,0:T(8,128)(2,1)S(1)}, f32[2,384,128]{2,1,0:T(8,128)S(1)}, bf16[896,128]{1,0:T(8,128)(2,1)S(1)}) custom-call(bf16[16,64,128]{2,1,0:T(8,128)(2,1)S(1)} %bitcast.16, bf16[4,64,128]{2,1,0:T(8,128)(2,1)S(1)} %collective-permute-done.refs_4_.refs_1_.refs_3_, ...), custom_call_target="tpu_custom_call" | custom-call | flops 452984832 | bytes 3342336 | tf_op jit(solution)/shard_map/pallas_call | solution.py:41
  20.3 1.2 %collective-permute-start.7 = (bf16[896,128]{1,0:T(8,128)(2,1)S(1)}, bf16[896,128]{1,0:T(8,128)(2,1)S(1)}, u32[]{:S(2)}, u32[]{:S(2)}) collective-permute-start(bf16[896,128]{1,0:T(8,128)(2,1)S(1)} %get-tuple-element.52), channel_id=1, source_target_pairs={{8,0},{0,8},{24,16},{16,24},{9,1},{1,9},{25,17},{17,25},{10,2},{2,... | collective-permute-start | bytes 688136 | tf_op jit(solution)/shard_map/ppermute | solution.py:76
  21.5 1.1 %collective-permute-done.7.refs_1_.refs_2_ = bf16[896,128]{1,0:T(8,128)(2,1)S(1)} collective-permute-done((bf16[896,128]{1,0:T(8,128)(2,1)S(1)}, bf16[896,128]{1,0:T(8,128)(2,1)S(1)}, u32[]{:S(2)}, u32[]{:S(2)}) %collective-permute-start.7) | collective-permute-done | bytes 229408 | tf_op jit(solution)/shard_map/ppermute | solution.py:76
  22.7 1.4 %collective-permute-start.8 = (bf16[256,128]{1,0:T(8,128)(2,1)S(1)}, bf16[256,128]{1,0:T(8,128)(2,1)S(1)}, u32[]{:S(2)}, u32[]{:S(2)}) collective-permute-start(bf16[256,128]{1,0:T(8,128)(2,1)S(1)} %get-tuple-element.55), channel_id=1, source_target_pairs={{16,0},{24,8},{0,16},{8,24},{17,1},{25,9},{1,17},{9,25},{18,2},{26... | collective-permute-start | bytes 196616 | tf_op jit(solution)/shard_map/ppermute | solution.py:76
  24.1 0.8 %collective-permute-start.11 = (bf16[192,128]{1,0:T(8,128)(2,1)S(1)}, bf16[192,128]{1,0:T(8,128)(2,1)S(1)}, u32[]{:S(2)}, u32[]{:S(2)}) collective-permute-start(bf16[192,128]{1,0:T(8,128)(2,1)S(1)} %get-tuple-element.54.refs_2_), channel_id=1, source_target_pairs={{4,0},{0,4},{5,1},{1,5},{6,2},{2,6},{7,3},{3,7},{12,8},{8,12},{13,... | collective-permute-start | bytes 147464 | tf_op jit(solution)/shard_map/ppermute | solution.py:76
  25.5 0.7 %collective-permute-start.10 = (bf16[192,128]{1,0:T(8,128)(2,1)S(1)}, bf16[192,128]{1,0:T(8,128)(2,1)S(1)}, u32[]{:S(2)}, u32[]{:S(2)}) collective-permute-start(bf16[192,128]{1,0:T(8,128)(2,1)S(1)} %get-tuple-element.58), channel_id=1, source_target_pairs={{20,0},{16,4},{28,8},{24,12},{4,16},{0,20},{12,24},{8,28},{21,1},{... | collective-permute-start | bytes 147464 | tf_op jit(solution)/shard_map/ppermute | solution.py:84
  27.0 1.4 %collective-permute-start.13 = (bf16[192,128]{1,0:T(8,128)(2,1)S(1)}, bf16[192,128]{1,0:T(8,128)(2,1)S(1)}, u32[]{:S(2)}, u32[]{:S(2)}) collective-permute-start(bf16[192,128]{1,0:T(8,128)(2,1)S(1)} %shard_map.138.refs_0_), channel_id=1, source_target_pairs={{1,0},{0,1},{3,2},{2,3},{5,4},{4,5},{7,6},{6,7},{9,8},{8,9},{11,10... | collective-permute-start | bytes 147464 | tf_op jit(solution)/shard_map/ppermute | solution.py:76
  28.4 1.2 %collective-permute-done.10.refs_3_ = bf16[192,128]{1,0:T(8,128)(2,1)S(1)} collective-permute-done((bf16[192,128]{1,0:T(8,128)(2,1)S(1)}, bf16[192,128]{1,0:T(8,128)(2,1)S(1)}, u32[]{:S(2)}, u32[]{:S(2)}) %collective-permute-start.10) | collective-permute-done | bytes 49184 | tf_op jit(solution)/shard_map/ppermute | solution.py:84
  29.7 1.4 %collective-permute-start.12 = (bf16[192,128]{1,0:T(8,128)(2,1)S(1)}, bf16[192,128]{1,0:T(8,128)(2,1)S(1)}, u32[]{:S(2)}, u32[]{:S(2)}) collective-permute-start(bf16[192,128]{1,0:T(8,128)(2,1)S(1)} %shard_map.137.refs_0_.refs_2_), channel_id=1, source_target_pairs={{1,0},{0,1},{3,2},{2,3},{5,4},{4,5},{7,6},{6,7},{9,8},{8,9},{11,10... | collective-permute-start | bytes 147464 | tf_op jit(solution)/shard_map/ppermute | solution.py:76
  31.1 2.4 %collective-permute-start.15 = (bf16[192,128]{1,0:T(8,128)(2,1)S(1)}, bf16[192,128]{1,0:T(8,128)(2,1)S(1)}, u32[]{:S(2)}, u32[]{:S(2)}) collective-permute-start(bf16[192,128]{1,0:T(8,128)(2,1)S(1)} %shard_map.140.refs_0_), channel_id=1, source_target_pairs={{2,0},{3,1},{0,2},{1,3},{6,4},{7,5},{4,6},{5,7},{10,8},{11,9},{8,1... | collective-permute-start | bytes 147464 | tf_op jit(solution)/shard_map/ppermute | solution.py:76
  33.5 2.3 %collective-permute-start.14 = (bf16[192,128]{1,0:T(8,128)(2,1)S(1)}, bf16[192,128]{1,0:T(8,128)(2,1)S(1)}, u32[]{:S(2)}, u32[]{:S(2)}) collective-permute-start(bf16[192,128]{1,0:T(8,128)(2,1)S(1)} %shard_map.139.refs_2_.refs_0_), channel_id=1, source_target_pairs={{2,0},{3,1},{0,2},{1,3},{6,4},{7,5},{4,6},{5,7},{10,8},{11,9},{8,1... | collective-permute-start | bytes 147464 | tf_op jit(solution)/shard_map/ppermute | solution.py:76
  35.8 0.7 %collective-permute-start.23 = (bf16[192,128]{1,0:T(8,128)(2,1)S(1)}, bf16[192,128]{1,0:T(8,128)(2,1)S(1)}, u32[]{:S(2)}, u32[]{:S(2)}) collective-permute-start(bf16[192,128]{1,0:T(8,128)(2,1)S(1)} %shard_map.141.refs_2_.refs_0_), channel_id=1, source_target_pairs={{4,0},{0,4},{5,1},{1,5},{6,2},{2,6},{7,3},{3,7},{12,8},{8,12},{13,... | collective-permute-start | bytes 147464 | tf_op jit(solution)/shard_map/ppermute | solution.py:76
  36.8 1.7 %collective-permute-start.27 = (bf16[192,128]{1,0:T(8,128)(2,1)S(1)}, bf16[192,128]{1,0:T(8,128)(2,1)S(1)}, u32[]{:S(2)}, u32[]{:S(2)}) collective-permute-start(bf16[192,128]{1,0:T(8,128)(2,1)S(1)} %shard_map.141.refs_2_.refs_0_), channel_id=1, source_target_pairs={{20,0},{16,4},{28,8},{24,12},{4,16},{0,20},{12,24},{8,28},{21,1},{... | collective-permute-start | bytes 147464 | tf_op jit(solution)/shard_map/ppermute | solution.py:84
  38.6 0.7 %collective-permute-start.16 = (bf16[192,128]{1,0:T(8,128)(2,1)S(1)}, bf16[192,128]{1,0:T(8,128)(2,1)S(1)}, u32[]{:S(2)}, u32[]{:S(2)}) collective-permute-start(bf16[192,128]{1,0:T(8,128)(2,1)S(1)} %shard_map.142.refs_5_.refs_0_), channel_id=1, source_target_pairs={{4,0},{0,4},{5,1},{1,5},{6,2},{2,6},{7,3},{3,7},{12,8},{8,12},{13,... | collective-permute-start | bytes 147464 | tf_op jit(solution)/shard_map/ppermute | solution.py:76
  39.3 1.0 %collective-permute-start.17 = (bf16[192,128]{1,0:T(8,128)(2,1)S(1)}, bf16[192,128]{1,0:T(8,128)(2,1)S(1)}, u32[]{:S(2)}, u32[]{:S(2)}) collective-permute-start(bf16[192,128]{1,0:T(8,128)(2,1)S(1)} %shard_map.142.refs_5_.refs_0_), channel_id=1, source_target_pairs={{16,0},{24,8},{0,16},{8,24},{17,1},{25,9},{1,17},{9,25},{18,2},{26... | collective-permute-start | bytes 147464 | tf_op jit(solution)/shard_map/ppermute | solution.py:76
  40.3 0.9 %collective-permute-start.18 = (bf16[192,128]{1,0:T(8,128)(2,1)S(1)}, bf16[192,128]{1,0:T(8,128)(2,1)S(1)}, u32[]{:S(2)}, u32[]{:S(2)}) collective-permute-start(bf16[192,128]{1,0:T(8,128)(2,1)S(1)} %shard_map.142.refs_5_.refs_0_), channel_id=1, source_target_pairs={{20,0},{16,4},{28,8},{24,12},{4,16},{0,20},{12,24},{8,28},{21,1},{... | collective-permute-start | bytes 147464 | tf_op jit(solution)/shard_map/ppermute | solution.py:84
  41.3 5.9 %collective-permute-start.24 = (bf16[192,128]{1,0:T(8,128)(2,1)S(1)}, bf16[192,128]{1,0:T(8,128)(2,1)S(1)}, u32[]{:S(2)}, u32[]{:S(2)}) collective-permute-start(bf16[192,128]{1,0:T(8,128)(2,1)S(1)} %shard_map.141.refs_2_.refs_0_), channel_id=1, source_target_pairs={{8,0},{0,8},{24,16},{16,24},{9,1},{1,9},{25,17},{17,25},{10,2},{2,... | collective-permute-start | bytes 147464 | tf_op jit(solution)/shard_map/ppermute | solution.py:76
  47.8 2.2 %shard_map.143 = (bf16[16,64,128]{2,1,0:T(8,128)(2,1)}, f32[8,128]{1,0:T(8,128)S(1)}) custom-call(bf16[16,64,128]{2,1,0:T(8,128)(2,1)S(1)} %get-tuple-element.48.refs_0_, bf16[16,64,128]{2,1,0:T(8,128)(2,1)S(1)} %get-tuple-element.49.refs_1_, bf16[896,128]{1,0:T(8,128)(2,1)S(1)} %collective-permute-done.7.refs_1_.refs_2_, ...), custom_call_target="tpu_custom_call" | custom-call | flops 301989888 | bytes 1380352 | tf_op jit(solution)/shard_map/pallas_call | solution.py:41
  51.3 0.9 %shard_map.145 = (f32[3,384,128]{2,1,0:T(8,128)}, f32[384,128]{1,0:T(8,128)}) custom-call(bf16[192,128]{1,0:T(8,128)(2,1)S(1)} %shard_map.141.refs_2_.refs_0_, bf16[192,128]{1,0:T(8,128)(2,1)S(1)} %collective-permute-done.23.refs_1_, bf16[192,128]{1,0:T(8,128)(2,1)S(1)} %collective-permute-done.24.refs_2_, ...), custom_call_target="tpu_custom_call" | custom-call | flops 196608 | bytes 1179648 | tf_op jit(solution)/shard_map/pallas_call | solution.py:41
  52.3 0.9 %shard_map.144 = (f32[3,384,128]{2,1,0:T(8,128)}, f32[384,128]{1,0:T(8,128)}) custom-call(bf16[192,128]{1,0:T(8,128)(2,1)S(1)} %shard_map.142.refs_5_.refs_0_, bf16[192,128]{1,0:T(8,128)(2,1)S(1)} %collective-permute-done.16.refs_1_, bf16[192,128]{1,0:T(8,128)(2,1)S(1)} %collective-permute-done.19.refs_2_, ...), custom_call_target="tpu_custom_call" | custom-call | flops 196608 | bytes 1179648 | tf_op jit(solution)/shard_map/pallas_call | solution.py:41
  (64 shorter events, 4.4 us)
Async XLA Ops:
  0.6 10.1 %collective-permute-start.3 = (bf16[16,64,128]{2,1,0:T(8,128)(2,1)}, bf16[16,64,128]{2,1,0:T(8,128)(2,1)S(1)}, u32[]{:S(2)}, u32[]{:S(2)}) collective-permute-start(bf16[16,64,128]{2,1,0:T(8,128)(2,1)} %bitcast.10), channel_id=1, source_target_pairs={{4,0},{0,4},{5,1},{1,5},{6,2},{2,6},{7,3},{3,7},{12,8},{8,12},{13,... | collective-permute-start | bytes 786440 | tf_op jit(solution)/shard_map/ppermute | solution.py:76
  4.4 2.1 %collective-permute-start.1 = (bf16[4,64,128]{2,1,0:T(8,128)(2,1)}, bf16[4,64,128]{2,1,0:T(8,128)(2,1)S(1)}, u32[]{:S(2)}, u32[]{:S(2)}) collective-permute-start(bf16[4,64,128]{2,1,0:T(8,128)(2,1)} %get-tuple-element.40), channel_id=1, source_target_pairs={{8,0},{0,8},{24,16},{16,24},{9,1},{1,9},{25,17},{17,25},{10,2},{2,... | collective-permute-start | bytes 196616 | tf_op jit(solution)/shard_map/ppermute | solution.py:76
  5.4 2.4 %collective-permute-start = (bf16[4,64,128]{2,1,0:T(8,128)(2,1)}, bf16[4,64,128]{2,1,0:T(8,128)(2,1)S(1)}, u32[]{:S(2)}, u32[]{:S(2)}) collective-permute-start(bf16[4,64,128]{2,1,0:T(8,128)(2,1)} %get-tuple-element.39), channel_id=1, source_target_pairs={{8,0},{0,8},{24,16},{16,24},{9,1},{1,9},{25,17},{17,25},{10,2},{2,... | collective-permute-start | bytes 196616 | tf_op jit(solution)/shard_map/ppermute | solution.py:76
  6.5 3.3 %collective-permute-start.2 = (bf16[4,64,128]{2,1,0:T(8,128)(2,1)S(1)}, bf16[4,64,128]{2,1,0:T(8,128)(2,1)S(1)}, u32[]{:S(2)}, u32[]{:S(2)}) collective-permute-start(bf16[4,64,128]{2,1,0:T(8,128)(2,1)S(1)} %collective-permute-done.1.refs_5_), channel_id=1, source_target_pairs={{16,0},{24,8},{0,16},{8,24},{17,1},{25,9},{1,17},{9,25},{18,2},{26... | collective-permute-start | bytes 196616 | tf_op jit(solution)/shard_map/ppermute | solution.py:76
  9.8 7.8 %collective-permute-start.4 = (bf16[18,64,128]{2,1,0:T(8,128)(2,1)S(1)}, bf16[18,64,128]{2,1,0:T(8,128)(2,1)S(1)}, u32[]{:S(2)}, u32[]{:S(2)}) collective-permute-start(bf16[18,64,128]{2,1,0:T(8,128)(2,1)S(1)} %shard_map.130.refs_7_), channel_id=1, source_target_pairs={{4,0},{0,4},{5,1},{1,5},{6,2},{2,6},{7,3},{3,7},{12,8},{8,12},{13,... | collective-permute-start | bytes 884744 | tf_op jit(solution)/shard_map/ppermute | solution.py:76
  12.5 5.1 %copy-start.8 = (bf16[3,128,128]{2,1,0:T(8,128)(2,1)S(1)}, bf16[3,128,128]{2,1,0:T(8,128)(2,1)}, u32[]{:S(2)}) copy-start(bf16[3,128,128]{2,1,0:T(8,128)(2,1)} %refs_10_.1) | copy-start | bytes 294916
  13.6 2.3 %collective-permute-start.5 = (bf16[768,128]{1,0:T(8,128)(2,1)S(1)}, bf16[768,128]{1,0:T(8,128)(2,1)S(1)}, u32[]{:S(2)}, u32[]{:S(2)}) collective-permute-start(bf16[768,128]{1,0:T(8,128)(2,1)S(1)} %get-tuple-element.46), channel_id=1, source_target_pairs={{8,0},{0,8},{24,16},{16,24},{9,1},{1,9},{25,17},{17,25},{10,2},{2,... | collective-permute-start | bytes 589832 | tf_op jit(solution)/shard_map/ppermute | solution.py:76
  16.0 4.3 %collective-permute-start.6 = (bf16[384,128]{1,0:T(8,128)(2,1)S(1)}, bf16[384,128]{1,0:T(8,128)(2,1)S(1)}, u32[]{:S(2)}, u32[]{:S(2)}) collective-permute-start(bf16[384,128]{1,0:T(8,128)(2,1)S(1)} %get-tuple-element.51), channel_id=1, source_target_pairs={{16,0},{24,8},{0,16},{8,24},{17,1},{25,9},{1,17},{9,25},{18,2},{26... | collective-permute-start | bytes 294920 | tf_op jit(solution)/shard_map/ppermute | solution.py:76
  20.3 2.3 %collective-permute-start.7 = (bf16[896,128]{1,0:T(8,128)(2,1)S(1)}, bf16[896,128]{1,0:T(8,128)(2,1)S(1)}, u32[]{:S(2)}, u32[]{:S(2)}) collective-permute-start(bf16[896,128]{1,0:T(8,128)(2,1)S(1)} %get-tuple-element.52), channel_id=1, source_target_pairs={{8,0},{0,8},{24,16},{16,24},{9,1},{1,9},{25,17},{17,25},{10,2},{2,... | collective-permute-start | bytes 688136 | tf_op jit(solution)/shard_map/ppermute | solution.py:76
  22.7 7.0 %collective-permute-start.8 = (bf16[256,128]{1,0:T(8,128)(2,1)S(1)}, bf16[256,128]{1,0:T(8,128)(2,1)S(1)}, u32[]{:S(2)}, u32[]{:S(2)}) collective-permute-start(bf16[256,128]{1,0:T(8,128)(2,1)S(1)} %get-tuple-element.55), channel_id=1, source_target_pairs={{16,0},{24,8},{0,16},{8,24},{17,1},{25,9},{1,17},{9,25},{18,2},{26... | collective-permute-start | bytes 196616 | tf_op jit(solution)/shard_map/ppermute | solution.py:76
  24.1 2.9 %collective-permute-start.11 = (bf16[192,128]{1,0:T(8,128)(2,1)S(1)}, bf16[192,128]{1,0:T(8,128)(2,1)S(1)}, u32[]{:S(2)}, u32[]{:S(2)}) collective-permute-start(bf16[192,128]{1,0:T(8,128)(2,1)S(1)} %get-tuple-element.54.refs_2_), channel_id=1, source_target_pairs={{4,0},{0,4},{5,1},{1,5},{6,2},{2,6},{7,3},{3,7},{12,8},{8,12},{13,... | collective-permute-start | bytes 147464 | tf_op jit(solution)/shard_map/ppermute | solution.py:76
  24.9 3.6 %collective-permute-start.9 = (bf16[192,128]{1,0:T(8,128)(2,1)S(1)}, bf16[192,128]{1,0:T(8,128)(2,1)S(1)}, u32[]{:S(2)}, u32[]{:S(2)}) collective-permute-start(bf16[192,128]{1,0:T(8,128)(2,1)S(1)} %get-tuple-element.57), channel_id=1, source_target_pairs={{4,0},{0,4},{5,1},{1,5},{6,2},{2,6},{7,3},{3,7},{12,8},{8,12},{13,... | collective-permute-start | bytes 147464 | tf_op jit(solution)/shard_map/ppermute | solution.py:76
  25.5 4.1 %collective-permute-start.10 = (bf16[192,128]{1,0:T(8,128)(2,1)S(1)}, bf16[192,128]{1,0:T(8,128)(2,1)S(1)}, u32[]{:S(2)}, u32[]{:S(2)}) collective-permute-start(bf16[192,128]{1,0:T(8,128)(2,1)S(1)} %get-tuple-element.58), channel_id=1, source_target_pairs={{20,0},{16,4},{28,8},{24,12},{4,16},{0,20},{12,24},{8,28},{21,1},{... | collective-permute-start | bytes 147464 | tf_op jit(solution)/shard_map/ppermute | solution.py:84
  27.0 4.0 %collective-permute-start.13 = (bf16[192,128]{1,0:T(8,128)(2,1)S(1)}, bf16[192,128]{1,0:T(8,128)(2,1)S(1)}, u32[]{:S(2)}, u32[]{:S(2)}) collective-permute-start(bf16[192,128]{1,0:T(8,128)(2,1)S(1)} %shard_map.138.refs_0_), channel_id=1, source_target_pairs={{1,0},{0,1},{3,2},{2,3},{5,4},{4,5},{7,6},{6,7},{9,8},{8,9},{11,10... | collective-permute-start | bytes 147464 | tf_op jit(solution)/shard_map/ppermute | solution.py:76
  29.7 3.8 %collective-permute-start.12 = (bf16[192,128]{1,0:T(8,128)(2,1)S(1)}, bf16[192,128]{1,0:T(8,128)(2,1)S(1)}, u32[]{:S(2)}, u32[]{:S(2)}) collective-permute-start(bf16[192,128]{1,0:T(8,128)(2,1)S(1)} %shard_map.137.refs_0_.refs_2_), channel_id=1, source_target_pairs={{1,0},{0,1},{3,2},{2,3},{5,4},{4,5},{7,6},{6,7},{9,8},{8,9},{11,10... | collective-permute-start | bytes 147464 | tf_op jit(solution)/shard_map/ppermute | solution.py:76
  31.1 16.7 %copy-start.6 = (bf16[3,3,128,128]{3,2,1,0:T(8,128)(2,1)S(1)}, bf16[3,3,128,128]{3,2,1,0:T(8,128)(2,1)}, u32[]{:S(2)}) copy-start(bf16[3,3,128,128]{3,2,1,0:T(8,128)(2,1)} %refs_4_.3) | copy-start | bytes 884740
  31.1 4.7 %collective-permute-start.15 = (bf16[192,128]{1,0:T(8,128)(2,1)S(1)}, bf16[192,128]{1,0:T(8,128)(2,1)S(1)}, u32[]{:S(2)}, u32[]{:S(2)}) collective-permute-start(bf16[192,128]{1,0:T(8,128)(2,1)S(1)} %shard_map.140.refs_0_), channel_id=1, source_target_pairs={{2,0},{3,1},{0,2},{1,3},{6,4},{7,5},{4,6},{5,7},{10,8},{11,9},{8,1... | collective-permute-start | bytes 147464 | tf_op jit(solution)/shard_map/ppermute | solution.py:76
  33.5 5.1 %collective-permute-start.14 = (bf16[192,128]{1,0:T(8,128)(2,1)S(1)}, bf16[192,128]{1,0:T(8,128)(2,1)S(1)}, u32[]{:S(2)}, u32[]{:S(2)}) collective-permute-start(bf16[192,128]{1,0:T(8,128)(2,1)S(1)} %shard_map.139.refs_2_.refs_0_), channel_id=1, source_target_pairs={{2,0},{3,1},{0,2},{1,3},{6,4},{7,5},{4,6},{5,7},{10,8},{11,9},{8,1... | collective-permute-start | bytes 147464 | tf_op jit(solution)/shard_map/ppermute | solution.py:76
  35.8 4.5 %collective-permute-start.23 = (bf16[192,128]{1,0:T(8,128)(2,1)S(1)}, bf16[192,128]{1,0:T(8,128)(2,1)S(1)}, u32[]{:S(2)}, u32[]{:S(2)}) collective-permute-start(bf16[192,128]{1,0:T(8,128)(2,1)S(1)} %shard_map.141.refs_2_.refs_0_), channel_id=1, source_target_pairs={{4,0},{0,4},{5,1},{1,5},{6,2},{2,6},{7,3},{3,7},{12,8},{8,12},{13,... | collective-permute-start | bytes 147464 | tf_op jit(solution)/shard_map/ppermute | solution.py:76
  36.6 4.7 %collective-permute-start.26 = (bf16[192,128]{1,0:T(8,128)(2,1)S(1)}, bf16[192,128]{1,0:T(8,128)(2,1)S(1)}, u32[]{:S(2)}, u32[]{:S(2)}) collective-permute-start(bf16[192,128]{1,0:T(8,128)(2,1)S(1)} %shard_map.141.refs_2_.refs_0_), channel_id=1, source_target_pairs={{16,0},{24,8},{0,16},{8,24},{17,1},{25,9},{1,17},{9,25},{18,2},{26... | collective-permute-start | bytes 147464 | tf_op jit(solution)/shard_map/ppermute | solution.py:76
  36.8 10.4 %collective-permute-start.27 = (bf16[192,128]{1,0:T(8,128)(2,1)S(1)}, bf16[192,128]{1,0:T(8,128)(2,1)S(1)}, u32[]{:S(2)}, u32[]{:S(2)}) collective-permute-start(bf16[192,128]{1,0:T(8,128)(2,1)S(1)} %shard_map.141.refs_2_.refs_0_), channel_id=1, source_target_pairs={{20,0},{16,4},{28,8},{24,12},{4,16},{0,20},{12,24},{8,28},{21,1},{... | collective-permute-start | bytes 147464 | tf_op jit(solution)/shard_map/ppermute | solution.py:84
  38.6 8.7 %collective-permute-start.16 = (bf16[192,128]{1,0:T(8,128)(2,1)S(1)}, bf16[192,128]{1,0:T(8,128)(2,1)S(1)}, u32[]{:S(2)}, u32[]{:S(2)}) collective-permute-start(bf16[192,128]{1,0:T(8,128)(2,1)S(1)} %shard_map.142.refs_5_.refs_0_), channel_id=1, source_target_pairs={{4,0},{0,4},{5,1},{1,5},{6,2},{2,6},{7,3},{3,7},{12,8},{8,12},{13,... | collective-permute-start | bytes 147464 | tf_op jit(solution)/shard_map/ppermute | solution.py:76
  39.3 10.8 %collective-permute-start.17 = (bf16[192,128]{1,0:T(8,128)(2,1)S(1)}, bf16[192,128]{1,0:T(8,128)(2,1)S(1)}, u32[]{:S(2)}, u32[]{:S(2)}) collective-permute-start(bf16[192,128]{1,0:T(8,128)(2,1)S(1)} %shard_map.142.refs_5_.refs_0_), channel_id=1, source_target_pairs={{16,0},{24,8},{0,16},{8,24},{17,1},{25,9},{1,17},{9,25},{18,2},{26... | collective-permute-start | bytes 147464 | tf_op jit(solution)/shard_map/ppermute | solution.py:76
  40.3 9.7 %collective-permute-start.18 = (bf16[192,128]{1,0:T(8,128)(2,1)S(1)}, bf16[192,128]{1,0:T(8,128)(2,1)S(1)}, u32[]{:S(2)}, u32[]{:S(2)}) collective-permute-start(bf16[192,128]{1,0:T(8,128)(2,1)S(1)} %shard_map.142.refs_5_.refs_0_), channel_id=1, source_target_pairs={{20,0},{16,4},{28,8},{24,12},{4,16},{0,20},{12,24},{8,28},{21,1},{... | collective-permute-start | bytes 147464 | tf_op jit(solution)/shard_map/ppermute | solution.py:84
  41.3 9.3 %collective-permute-start.24 = (bf16[192,128]{1,0:T(8,128)(2,1)S(1)}, bf16[192,128]{1,0:T(8,128)(2,1)S(1)}, u32[]{:S(2)}, u32[]{:S(2)}) collective-permute-start(bf16[192,128]{1,0:T(8,128)(2,1)S(1)} %shard_map.141.refs_2_.refs_0_), channel_id=1, source_target_pairs={{8,0},{0,8},{24,16},{16,24},{9,1},{1,9},{25,17},{17,25},{10,2},{2,... | collective-permute-start | bytes 147464 | tf_op jit(solution)/shard_map/ppermute | solution.py:76
  47.2 3.4 %collective-permute-start.25 = (bf16[192,128]{1,0:T(8,128)(2,1)S(1)}, bf16[192,128]{1,0:T(8,128)(2,1)S(1)}, u32[]{:S(2)}, u32[]{:S(2)}) collective-permute-start(bf16[192,128]{1,0:T(8,128)(2,1)S(1)} %collective-permute-done.23.refs_1_), channel_id=1, source_target_pairs={{8,0},{0,8},{24,16},{16,24},{9,1},{1,9},{25,17},{17,25},{10,2},{2,... | collective-permute-start | bytes 147464 | tf_op jit(solution)/shard_map/ppermute | solution.py:76
  47.3 3.8 %collective-permute-start.28 = (bf16[192,128]{1,0:T(8,128)(2,1)S(1)}, bf16[192,128]{1,0:T(8,128)(2,1)S(1)}, u32[]{:S(2)}, u32[]{:S(2)}) collective-permute-start(bf16[192,128]{1,0:T(8,128)(2,1)S(1)} %collective-permute-done.26.refs_4_), channel_id=1, source_target_pairs={{8,0},{0,8},{24,16},{16,24},{9,1},{1,9},{25,17},{17,25},{10,2},{2,... | collective-permute-start | bytes 147464 | tf_op jit(solution)/shard_map/ppermute | solution.py:76
  50.1 1.2 %collective-permute-start.29 = (bf16[192,128]{1,0:T(8,128)(2,1)S(1)}, bf16[192,128]{1,0:T(8,128)(2,1)S(1)}, u32[]{:S(2)}, u32[]{:S(2)}) collective-permute-start(bf16[192,128]{1,0:T(8,128)(2,1)S(1)} %collective-permute-done.27.refs_5_), channel_id=1, source_target_pairs={{8,0},{0,8},{24,16},{16,24},{9,1},{1,9},{25,17},{17,25},{10,2},{2,... | collective-permute-start | bytes 147464 | tf_op jit(solution)/shard_map/ppermute | solution.py:76
  50.1 2.2 %collective-permute-start.19 = (bf16[192,128]{1,0:T(8,128)(2,1)S(1)}, bf16[192,128]{1,0:T(8,128)(2,1)S(1)}, u32[]{:S(2)}, u32[]{:S(2)}) collective-permute-start(bf16[192,128]{1,0:T(8,128)(2,1)S(1)} %shard_map.142.refs_5_.refs_0_), channel_id=1, source_target_pairs={{8,0},{0,8},{24,16},{16,24},{9,1},{1,9},{25,17},{17,25},{10,2},{2,... | collective-permute-start | bytes 147464 | tf_op jit(solution)/shard_map/ppermute | solution.py:76
  50.6 1.7 %collective-permute-start.20 = (bf16[192,128]{1,0:T(8,128)(2,1)S(1)}, bf16[192,128]{1,0:T(8,128)(2,1)S(1)}, u32[]{:S(2)}, u32[]{:S(2)}) collective-permute-start(bf16[192,128]{1,0:T(8,128)(2,1)S(1)} %collective-permute-done.16.refs_1_), channel_id=1, source_target_pairs={{8,0},{0,8},{24,16},{16,24},{9,1},{1,9},{25,17},{17,25},{10,2},{2,... | collective-permute-start | bytes 147464 | tf_op jit(solution)/shard_map/ppermute | solution.py:76
  50.7 1.6 %collective-permute-start.21 = (bf16[192,128]{1,0:T(8,128)(2,1)S(1)}, bf16[192,128]{1,0:T(8,128)(2,1)S(1)}, u32[]{:S(2)}, u32[]{:S(2)}) collective-permute-start(bf16[192,128]{1,0:T(8,128)(2,1)S(1)} %collective-permute-done.17.refs_4_), channel_id=1, source_target_pairs={{8,0},{0,8},{24,16},{16,24},{9,1},{1,9},{25,17},{17,25},{10,2},{2,... | collective-permute-start | bytes 147464 | tf_op jit(solution)/shard_map/ppermute | solution.py:76
  51.1 1.2 %collective-permute-start.22 = (bf16[192,128]{1,0:T(8,128)(2,1)S(1)}, bf16[192,128]{1,0:T(8,128)(2,1)S(1)}, u32[]{:S(2)}, u32[]{:S(2)}) collective-permute-start(bf16[192,128]{1,0:T(8,128)(2,1)S(1)} %collective-permute-done.18.refs_5_), channel_id=1, source_target_pairs={{8,0},{0,8},{24,16},{16,24},{9,1},{1,9},{25,17},{17,25},{10,2},{2,... | collective-permute-start | bytes 147464 | tf_op jit(solution)/shard_map/ppermute | solution.py:76
  (7 other events, 26.1 us)

commit v9 on v7

--- a/solution.py
+++ b/solution.py
@@ -125,27 +125,34 @@
     return lax.axis_index("video") == lax.axis_size("video") - 1
 
 
-def kernel_sums(saved_ref, above, below, act, grads, views, sums_ref):
+def left_sides(saved_ref, preact_ref, above, below, sides_ref):
     rows, cols, ch = saved_ref.shape
     flat = (rows * cols, ch)
-    saved = [
+    shifts = [
         jnp.concatenate([above, saved_ref[: rows - 1]], axis=0),
         saved_ref[...],
         jnp.concatenate([saved_ref[1:], below], axis=0),
     ]
+    for n, shift in enumerate(shifts):
+        sides_ref[n] = shift.reshape(flat).T
+    hval = preact_ref[...].astype(jnp.float32)
+    sides_ref[3] = (hval * sigmoid(hval)).astype(jnp.bfloat16).reshape(flat).T
+
+
+def kernel_sums(sides_ref, grads, views, sums_ref):
+    _, ch, pixels = sides_ref.shape
+    shifts = sides_ref[0:3].reshape(3 * ch, pixels)
+    sums = jnp.dot(shifts, views, preferred_element_type=jnp.float32)
     for ky in range(3):
-        sums = jnp.dot(saved[ky].reshape(flat).T, views, preferred_element_type=jnp.float32)
         for kx in range(3):
-            sums_ref[ky, kx * ch : (kx + 1) * ch] = sums[:, kx * ch : (kx + 1) * ch]
-    sums = jnp.dot(
-        act.reshape(flat).T,
-        jnp.concatenate([grad.reshape(flat) for grad in grads], axis=1),
-        preferred_element_type=jnp.float32,
-    )
+            here = slice(kx * ch, (kx + 1) * ch)
+            sums_ref[ky, here] = sums[ky * ch : (ky + 1) * ch, here]
+    grads = jnp.concatenate([grad.reshape(pixels, ch) for grad in grads], axis=1)
+    sums = jnp.dot(sides_ref[3], grads, preferred_element_type=jnp.float32)
     zeros = jnp.zeros((ch, ch), jnp.float32)
     for k in range(3):
         step = 2 - k
-        value = sums[:, step * ch : (step + 1) * ch] if step < len(grads) else zeros
+        value = sums[:, step * ch : (step + 1) * ch] if step * ch < grads.shape[1] else zeros
         sums_ref[3, k * ch : (k + 1) * ch] = jnp.where(is_last(), zeros, value) if step else value
 
 
@@ -217,18 +224,14 @@
         )
 
 
-def last_mid_kernel(grad_ref, one_ref, two_ref, inner_ref, gpre_ref, temporal_ref, spatial_ref, sent_ref, views_ref):
-    rows = grad_ref.shape[0]
-
+def last_edge_kernel(grad_ref, one_ref, two_ref, gpre_ref, temporal_ref, spatial_ref, edge_ref, views_ref):
     @pl.when(is_last())
     def _():
-        sent_ref[0:1], sent_ref[rows - 1 : rows] = edge_rows(
-            grad_ref, (one_ref, two_ref), [], gpre_ref, temporal_ref, spatial_ref, views_ref
-        )
-        sent_ref[1 : rows - 1] = inner_ref[...]
-        sent_ref[rows : rows + 1], sent_ref[rows + 1 : rows + 2] = beside_band(
-            (one_ref, two_ref), 0
-        )
+        pair_refs = (one_ref, two_ref)
+        edge_ref[0:1], edge_ref[1:2] = edge_rows(
+            grad_ref, pair_refs, [], gpre_ref, temporal_ref, spatial_ref, views_ref
+        )
+        edge_ref[2:3], edge_ref[3:4] = beside_band(pair_refs, 0)
 
 
 def inner_kernel(later, *refs):
@@ -263,7 +266,7 @@
     saved_ref, preact_ref, gpre_ref = refs[:3]
     pair_refs, grad_ref = refs[3:5], refs[5]
     wholes, outs = refs[6 : 6 + later], refs[6 + later : 8 + later]
-    views_ref, act_ref, sums_ref = refs[8 + later :]
+    views_ref, sides_ref, sums_ref = refs[8 + later :]
     rows, cols, ch = saved_ref.shape
     step = 4
 
@@ -271,20 +274,22 @@
     def _(n):
         here = pl.ds(n * step, step)
         beside(gpre_ref[here].astype(jnp.float32), views_ref, n * step)
-        hval = preact_ref[here].astype(jnp.float32)
-        act_ref[here] = (hval * sigmoid(hval)).astype(jnp.bfloat16)
 
     views = views_ref[...].reshape(rows * cols, 3 * ch)
     grads = [ref[...] for ref in (grad_ref, *wholes)]
-    above, below = beside_band(pair_refs, 2)
-    kernel_sums(saved_ref, above, below, act_ref[...], grads, views, sums_ref)
+    left_sides(saved_ref, preact_ref, *beside_band(pair_refs, 2), sides_ref)
+    kernel_sums(sides_ref, grads, views, sums_ref)
     hand_out(sums_ref, *outs)
 
 
-def block_one(saved_ref, preact_ref, pair_refs, mids, temporal_ref, outs, scratch):
+def sides_kernel(saved_ref, preact_ref, one_ref, two_ref, sides_ref):
+    left_sides(saved_ref, preact_ref, *beside_band((one_ref, two_ref), 3), sides_ref)
+
+
+def block_one(sides_ref, preact_ref, mids, temporal_ref, outs, scratch):
     gpre_ref, keep_ref, send_ref = outs
-    views_ref, act_ref, sums_ref = scratch
-    rows, cols, ch = saved_ref.shape
+    views_ref, sums_ref = scratch
+    rows, cols, ch = preact_ref.shape
     step = 4
 
     @pl.loop(0, rows // step)
@@ -293,31 +298,26 @@
         gpre = pre_gradient([ref[here] for ref in mids], preact_ref[here], temporal_ref)
         gpre_ref[here] = gpre.astype(jnp.bfloat16)
         beside(gpre, views_ref, n * step)
-        hval = preact_ref[here].astype(jnp.float32)
-        act_ref[here] = (hval * sigmoid(hval)).astype(jnp.bfloat16)
 
     odd = lax.rem(lax.axis_index("section"), 2)
     size = send_ref.shape[0] - 2 * cols
     send_ref[size : size + cols] = gpre_ref[(1 - odd) * (rows - 1)]
     send_ref[size + cols : size + 2 * cols] = gpre_ref[odd * (rows - 1)]
     views = views_ref[...].reshape(rows * cols, 3 * ch)
-    grads = [ref[...] for ref in mids]
-    above, below = beside_band(pair_refs, 3)
-    kernel_sums(saved_ref, above, below, act_ref[...], grads, views, sums_ref)
+    kernel_sums(sides_ref, [ref[...] for ref in mids], views, sums_ref)
     hand_out(sums_ref, keep_ref, send_ref)
 
 
 def one_kernel(later, *refs):
-    saved_ref, preact_ref, mid_ref = refs[0], refs[1], refs[4]
-    nexts, temporal_ref = refs[5 : 5 + later], refs[5 + later]
-    outs, scratch = refs[6 + later : 9 + later], refs[9 + later :]
-    block_one(saved_ref, preact_ref, refs[2:4], [mid_ref, *nexts], temporal_ref, outs, scratch)
+    sides_ref, preact_ref, mids = refs[0], refs[1], refs[2 : 3 + later]
+    temporal_ref, outs, scratch = refs[3 + later], refs[4 + later : 7 + later], refs[7 + later :]
+    block_one(sides_ref, preact_ref, mids, temporal_ref, outs, scratch)
 
 
 def mid_one_kernel(*refs):
-    pair_refs, after_ref = refs[1:3], refs[5]
-    temporal_two_ref, spatial_two_ref, saved_ref, preact_ref, temporal_ref = refs[6:11]
-    mid_ref, outs, scratch = refs[11], refs[12:15], refs[15:18]
+    after_inner_ref, after_edge_ref = refs[5:7]
+    temporal_two_ref, spatial_two_ref, sides_ref, preact_ref, temporal_ref = refs[7:12]
+    mid_ref, outs, scratch = refs[12], refs[13:16], refs[16:18]
     next_ref, edge_ref, edge_views_ref = refs[18:]
     rows = next_ref.shape[0]
 
@@ -328,13 +328,15 @@
 
     @pl.when(jnp.logical_not(is_last()))
     def _():
-        next_ref[...] = after_ref[:rows]
-        edge_ref[...] = after_ref[rows:]
+        edge_ref[...] = after_edge_ref[2:4]
+        next_ref[0:1] = after_edge_ref[0:1]
+        next_ref[1 : rows - 1] = after_inner_ref[...]
+        next_ref[rows - 1 : rows] = after_edge_ref[1:2]
 
     mid_kernel(
         1, *refs[:5], edge_ref, temporal_two_ref, spatial_two_ref, mid_ref, edge_views_ref
     )
-    block_one(saved_ref, preact_ref, pair_refs, [mid_ref, next_ref], temporal_ref, outs, scratch)
+    block_one(sides_ref, preact_ref, [mid_ref, next_ref], temporal_ref, outs, scratch)
 
 
 def input_kernel(mid_ref, gpre_ref, pair_ref, across_ref, spatial_ref, out_ref, token_ref, views_ref):
@@ -435,8 +437,7 @@
                 outs[2 * block + 1][here] = share[block].astype(jnp.float32)
 
 
-def place(shares):
-    across = [flipped(share, "section", 2) for share in shares]
+def placed(shares, across):
     ch = shares[0].shape[2]
     outs = call(
         place_kernel,
@@ -476,6 +477,7 @@
     views = pltpu.VMEM((rows, cols, 3 * ch), jnp.bfloat16)
     edge_views = pltpu.VMEM((6, cols, 3 * ch), jnp.bfloat16)
     act = pltpu.VMEM((rows, cols, ch), jnp.bfloat16)
+    sides = bf16(4, ch, rows * cols)
     sums = pltpu.VMEM((4, 3 * ch, ch), jnp.float32)
     handed = [f32(2, 3 * ch, ch), bf16(6 * ch, ch)]
     inner_outs = [bf16(rows - 2, cols, ch), bf16(rows, cols, ch)]
@@ -514,17 +516,7 @@
             *kernels,
             after=(first, second),
         )
-        sent = call(
-            last_mid_kernel,
-            [bf16(rows + 2, cols, ch)],
-            [edge_views],
-            conv // 8,
-            grad,
-            *pairs,
-            *known,
-            *kernels,
-        )
-        afters = from_later(sent)
+        afters = from_later(known[0])
     else:
         afters = from_later(jnp.concatenate(beside_band(pairs, 0)))
     inner, gpre_two = call(
@@ -537,12 +529,24 @@
         *wholes,
         *kernels,
         *known,
-        after=(sent,) if frames == 2 else (),
-    )
+    )
+    if frames == 2:
+        edge = call(
+            last_edge_kernel,
+            [bf16(4, cols, ch)],
+            [edge_views],
+            conv // 8,
+            grad,
+            *pairs,
+            known[1],
+            *kernels,
+            after=(gpre_two,),
+        )
+        afters += from_later(edge)
     parts_two = call(
         functools.partial(two_kernel, later),
         handed,
-        [views, act, sums],
+        [views, pltpu.VMEM(sides.shape, sides.dtype), sums],
         1.2 * conv,
         saved_two,
         pre_two,
@@ -550,6 +554,10 @@
         *pairs,
         grad,
         *wholes,
+        after=(edge,) if frames == 2 else (),
+    )
+    sides_one = call(
+        sides_kernel, [sides], [], conv // 8, saved_one, pre_one, *pairs, after=parts_two[:1]
     )
     height, half = 3 * ch, 3 * ch // 2
     keep_two, send_two = parts_two
@@ -560,17 +568,18 @@
         height * ch,
         keep_two,
         flipped(send_two, "section", 1),
+        after=afters[:1] if frames == 2 else (),
     )
     across_two = flipped(send_two, "section", 2)
     mid_inputs = (grad, *pairs, inner, gpre_two)
-    one_inputs = (saved_one, pre_one)
+    one_inputs = (sides_one, pre_one)
     mid_outs = [bf16(rows, cols, ch)]
     one_outs = [bf16(rows, cols, ch), f32(2, 3 * ch, ch), bf16(6 * ch + 2 * cols, ch)]
     if frames == 2:
         mid, gpre_one, *parts_one = call(
             mid_one_kernel,
             mid_outs + one_outs,
-            [views, act, sums, act, pltpu.VMEM((2, cols, ch), jnp.bfloat16), edge_views],
+            [views, sums, act, pltpu.VMEM((2, cols, ch), jnp.bfloat16), edge_views],
             1.5 * conv,
             *mid_inputs,
             *afters,
@@ -592,10 +601,9 @@
         gpre_one, *parts_one = call(
             functools.partial(one_kernel, later),
             one_outs,
-            [views, act, sums],
+            [views, sums],
             1.2 * conv,
             *one_inputs,
-            *pairs,
             mid,
             *from_later(mid),
             temporal_one,
@@ -659,7 +667,8 @@
             last_two,
             after=(token,),
         )
-        sums = place([own, flipped(own, "video", 1)])
+        shares = [own, flipped(own, "video", 1)]
+        sums = placed(shares, [flipped(own, "section", 2), flipped_both(own)])
     else:
         own_one, send_one = call(
             pair_kernel, [f32(height, ch), bf16(height, ch)], [], height * ch, keep_one, pair_one
@@ -669,7 +678,8 @@
         own_one = own_one + flipped(send_one, "section", 2).astype(jnp.float32)
         own_two = own_two + across_two.astype(jnp.float32)
         share = lax.psum(jnp.stack((own_one, own_two)), ("video", "dp")) * factor
-        sums = place([share.astype(jnp.bfloat16)])
+        share = share.astype(jnp.bfloat16)
+        sums = placed([share], [flipped(share, "section", 2)])
     return (grad_in.reshape(shape), *sums)
 
 

time: 53.9 us -> 51.7 us (0.959)
  waiting for transfers between devices: 9.93 us -> 6.07 us
  local copies, waits for them, and re-layouts: 0.04 us -> 0.95 us
  starting transfers between devices: 32.2 us -> 32.8 us
    ppermute x22, waiting for transfers between devices: 8.7 us -> 5.37 us  [flipped(): lax.ppermute(block, axis, [(place ^ flip, place) for place in range(count)])]
    ppermute x1 -> x2, starting transfers between devices: 0.75 us -> 3 us  [flipped_both(): return lax.ppermute(block, ('section', 'video'), pairs)]
    ppermute x22, starting transfers between devices: 31.4 us -> 29.8 us  [flipped(): lax.ppermute(block, axis, [(place ^ flip, place) for place in range(count)])]
    unnamed x18, local copies, waits for them, and re-layouts: 0.04 us -> 0.95 us
    ppermute x1 -> x2, waiting for transfers between devices: 1.23 us -> 0.7 us  [flipped_both(): return lax.ppermute(block, ('section', 'video'), pairs)]
    pallas_call x16 -> x17, Pallas kernels: 10.4 us -> 10.6 us  [call(): pl.pallas_call(body, out_shape=outs[0] if single else tuple(outs), in_spe...]
  transfers between devices with their start and end apart: 23 -> 24, of which waited for: 9 -> 7; matrix products, arithmetic and copies ran while one was open for 0% -> 0% of each run, Pallas kernels for 17% -> 18%
where the time goes in v9:
time: 51.7 us; the launch traced here: 51.2 us
  starting transfers between devices  32.8 us (63%)
  Pallas kernels  10.6 us (21%)
  waiting for transfers between devices  6.07 us (12%)
  local copies, waits for them, and re-layouts  0.95 us (2%)
  between operations  0.79 us (2%)
    ppermute x22, starting transfers between devices, flipped(): lax.ppermute(block, axis, [(place ^ flip, place) for place in range(count)])  29.8 us
    pallas_call x17, Pallas kernels, call(): pl.pallas_call(body, out_shape=outs[0] if single else tuple(outs), in_spe...  10.6 us
    ppermute x22, waiting for transfers between devices, flipped(): lax.ppermute(block, axis, [(place ^ flip, place) for place in range(count)])  5.37 us
    ppermute x2, starting transfers between devices, flipped_both(): return lax.ppermute(block, ('section', 'video'), pairs)  3 us
  transfers between devices with their start and end apart: 24, of which 7 were waited for; matrix products, arithmetic and copies ran while one was open for 0% of the time, Pallas kernels for 18%

profile of v9, /device:TPU:1, one launch (start us, length us, event | category | flops | bytes accessed | tf_op | source)
XLA Modules:
  0.0 51.2 jit_solution(10471916687471248676)
XLA Ops:
  0.6 2.1 %collective-permute-start.3 = (bf16[16,64,128]{2,1,0:T(8,128)(2,1)}, bf16[16,64,128]{2,1,0:T(8,128)(2,1)S(1)}, u32[]{:S(2)}, u32[]{:S(2)}) collective-permute-start(bf16[16,64,128]{2,1,0:T(8,128)(2,1)} %bitcast.10), channel_id=1, source_target_pairs={{4,0},{0,4},{5,1},{1,5},{6,2},{2,6},{7,3},{3,7},{12,8},{8,12},{13,... | collective-permute-start | bytes 786440 | tf_op jit(solution)/shard_map/ppermute | solution.py:73
  2.7 1.6 %shard_map.128 = (bf16[4,64,128]{2,1,0:T(8,128)(2,1)}, bf16[4,64,128]{2,1,0:T(8,128)(2,1)}) custom-call(bf16[16,64,128]{2,1,0:T(8,128)(2,1)} %bitcast.11, bf16[16,64,128]{2,1,0:T(8,128)(2,1)} %bitcast.17, bf16[16,64,128]{2,1,0:T(8,128)(2,1)} %bitcast.21, bf16[16,64,128]{2,1,0:T(8,128)(2,1)} %bitcast.25), custom_call_target="tpu_custom_call" | custom-call | flops 1 | bytes 1179648 | tf_op jit(solution)/shard_map/pallas_call | solution.py:38
  4.4 1.0 %collective-permute-start.1 = (bf16[4,64,128]{2,1,0:T(8,128)(2,1)}, bf16[4,64,128]{2,1,0:T(8,128)(2,1)S(1)}, u32[]{:S(2)}, u32[]{:S(2)}) collective-permute-start(bf16[4,64,128]{2,1,0:T(8,128)(2,1)} %get-tuple-element.35), channel_id=1, source_target_pairs={{8,0},{0,8},{24,16},{16,24},{9,1},{1,9},{25,17},{17,25},{10,2},{2,... | collective-permute-start | bytes 196616 | tf_op jit(solution)/shard_map/ppermute | solution.py:73
  5.5 1.0 %collective-permute-done.1.refs_5_ = bf16[4,64,128]{2,1,0:T(8,128)(2,1)S(1)} collective-permute-done((bf16[4,64,128]{2,1,0:T(8,128)(2,1)}, bf16[4,64,128]{2,1,0:T(8,128)(2,1)S(1)}, u32[]{:S(2)}, u32[]{:S(2)}) %collective-permute-start.1) | collective-permute-done | bytes 65568 | tf_op jit(solution)/shard_map/ppermute | solution.py:73
  6.5 1.2 %collective-permute-start.2 = (bf16[4,64,128]{2,1,0:T(8,128)(2,1)S(1)}, bf16[4,64,128]{2,1,0:T(8,128)(2,1)S(1)}, u32[]{:S(2)}, u32[]{:S(2)}) collective-permute-start(bf16[4,64,128]{2,1,0:T(8,128)(2,1)S(1)} %collective-permute-done.1.refs_5_), channel_id=1, source_target_pairs={{16,0},{24,8},{0,16},{8,24},{17,1},{25,9},{1,17},{9,25},{18,2},{26... | collective-permute-start | bytes 196616 | tf_op jit(solution)/shard_map/ppermute | solution.py:73
  7.8 2.0 %collective-permute-start.4 = (bf16[14,64,128]{2,1,0:T(8,128)(2,1)S(1)}, bf16[14,64,128]{2,1,0:T(8,128)(2,1)S(1)}, u32[]{:S(2)}, u32[]{:S(2)}) collective-permute-start(bf16[14,64,128]{2,1,0:T(8,128)(2,1)S(1)} %get-tuple-element.36.refs_5_), channel_id=1, source_target_pairs={{4,0},{0,4},{5,1},{1,5},{6,2},{2,6},{7,3},{3,7},{12,8},{8,12},{13,... | collective-permute-start | bytes 688136 | tf_op jit(solution)/shard_map/ppermute | solution.py:73
  9.8 1.7 %shard_map.130 = (bf16[14,64,128]{2,1,0:T(8,128)(2,1)S(1)}, bf16[16,64,128]{2,1,0:T(8,128)(2,1)S(1)}) custom-call(bf16[16,64,128]{2,1,0:T(8,128)(2,1)S(1)} %bitcast.13, bf16[16,64,128]{2,1,0:T(8,128)(2,1)S(1)} %bitcast.19, bf16[16,64,128]{2,1,0:T(8,128)(2,1)S(1)} %collective-permute-done.3.refs_2_.refs_6_, bf16[3,128,128]{2,1,0:T(8,128)(2,1)S(1)} %copy-done.6, ...), custom_call_target="tpu_custom_call" | custom-call | flops 362387872 | bytes 2162688 | tf_op jit(solution)/shard_map/pallas_call | solution.py:38
  11.6 0.9 %copy-done.3 = bf16[1,1,16,64,128]{4,3,2,1,0:T(8,128)(2,1)S(1)} copy-done((bf16[1,1,16,64,128]{4,3,2,1,0:T(8,128)(2,1)S(1)}, bf16[1,1,16,64,128]{4,3,2,1,0:T(8,128)(2,1)}, u32[]{:S(2)}) %copy-start.3) | copy-done | bytes 262168
  12.5 1.0 %shard_map.132 = (f32[2,384,128]{2,1,0:T(8,128)S(1)}, bf16[768,128]{1,0:T(8,128)(2,1)S(1)}) custom-call(bf16[16,64,128]{2,1,0:T(8,128)(2,1)S(1)} %bitcast.22, bf16[16,64,128]{2,1,0:T(8,128)(2,1)S(1)} %bitcast.20, bf16[16,64,128]{2,1,0:T(8,128)(2,1)S(1)} %get-tuple-element.39.refs_6_.refs_2_.refs_4_, ...), custom_call_target="tpu_custom_call" | custom-call | flops 362387872 | bytes 2031616 | tf_op jit(solution)/shard_map/pallas_call | solution.py:38
  13.5 1.0 %collective-permute-start.6 = (bf16[768,128]{1,0:T(8,128)(2,1)S(1)}, bf16[768,128]{1,0:T(8,128)(2,1)S(1)}, u32[]{:S(2)}, u32[]{:S(2)}) collective-permute-start(bf16[768,128]{1,0:T(8,128)(2,1)S(1)} %get-tuple-element.41), channel_id=1, source_target_pairs={{8,0},{0,8},{24,16},{16,24},{9,1},{1,9},{25,17},{17,25},{10,2},{2,... | collective-permute-start | bytes 589832 | tf_op jit(solution)/shard_map/ppermute | solution.py:73
  14.5 0.7 %collective-permute-done.4.refs_2_.refs_5_ = bf16[14,64,128]{2,1,0:T(8,128)(2,1)S(1)} collective-permute-done((bf16[14,64,128]{2,1,0:T(8,128)(2,1)S(1)}, bf16[14,64,128]{2,1,0:T(8,128)(2,1)S(1)}, u32[]{:S(2)}, u32[]{:S(2)}) %collective-permute-start.4) | collective-permute-done | bytes 229408 | tf_op jit(solution)/shard_map/ppermute | solution.py:73
  15.6 1.0 %collective-permute-start.7 = (bf16[384,128]{1,0:T(8,128)(2,1)S(1)}, bf16[384,128]{1,0:T(8,128)(2,1)S(1)}, u32[]{:S(2)}, u32[]{:S(2)}) collective-permute-start(bf16[384,128]{1,0:T(8,128)(2,1)S(1)} %get-tuple-element.46), channel_id=1, source_target_pairs={{16,0},{24,8},{0,16},{8,24},{17,1},{25,9},{1,17},{9,25},{18,2},{26... | collective-permute-start | bytes 294920 | tf_op jit(solution)/shard_map/ppermute | solution.py:73
  17.0 1.2 %collective-permute-done.5.refs_6_ = bf16[4,64,128]{2,1,0:T(8,128)(2,1)S(1)} collective-permute-done((bf16[4,64,128]{2,1,0:T(8,128)(2,1)S(1)}, bf16[4,64,128]{2,1,0:T(8,128)(2,1)S(1)}, u32[]{:S(2)}, u32[]{:S(2)}) %collective-permute-start.5) | collective-permute-done | bytes 65568 | tf_op jit(solution)/shard_map/ppermute | solution.py:73
  18.2 2.1 %shard_map.135 = (bf16[16,64,128]{2,1,0:T(8,128)(2,1)S(1)}, bf16[16,64,128]{2,1,0:T(8,128)(2,1)S(1)}, f32[2,384,128]{2,1,0:T(8,128)S(1)}, bf16[896,128]{1,0:T(8,128)(2,1)S(1)}) custom-call(bf16[16,64,128]{2,1,0:T(8,128)(2,1)S(1)} %bitcast.16, bf16[4,64,128]{2,1,0:T(8,128)(2,1)S(1)} %collective-permute-done.refs_4_.refs_1_.refs_3_.refs_2_, ...), custom_call_target="tpu_custom_call" | custom-call | flops 452984832 | bytes 4128768 | tf_op jit(solution)/shard_map/pallas_call | solution.py:38
  20.3 0.9 %collective-permute-start.8 = (bf16[896,128]{1,0:T(8,128)(2,1)S(1)}, bf16[896,128]{1,0:T(8,128)(2,1)S(1)}, u32[]{:S(2)}, u32[]{:S(2)}) collective-permute-start(bf16[896,128]{1,0:T(8,128)(2,1)S(1)} %get-tuple-element.47), channel_id=1, source_target_pairs={{8,0},{0,8},{24,16},{16,24},{9,1},{1,9},{25,17},{17,25},{10,2},{2,... | collective-permute-start | bytes 688136 | tf_op jit(solution)/shard_map/ppermute | solution.py:73
  21.3 1.1 %collective-permute-done.8.refs_1_.refs_2_ = bf16[896,128]{1,0:T(8,128)(2,1)S(1)} collective-permute-done((bf16[896,128]{1,0:T(8,128)(2,1)S(1)}, bf16[896,128]{1,0:T(8,128)(2,1)S(1)}, u32[]{:S(2)}, u32[]{:S(2)}) %collective-permute-start.8) | collective-permute-done | bytes 229408 | tf_op jit(solution)/shard_map/ppermute | solution.py:73
  22.4 1.0 %collective-permute-start.9 = (bf16[256,128]{1,0:T(8,128)(2,1)S(1)}, bf16[256,128]{1,0:T(8,128)(2,1)S(1)}, u32[]{:S(2)}, u32[]{:S(2)}) collective-permute-start(bf16[256,128]{1,0:T(8,128)(2,1)S(1)} %get-tuple-element.50), channel_id=1, source_target_pairs={{16,0},{24,8},{0,16},{8,24},{17,1},{25,9},{1,17},{9,25},{18,2},{26... | collective-permute-start | bytes 196616 | tf_op jit(solution)/shard_map/ppermute | solution.py:73
  23.4 0.8 %collective-permute-start.12 = (bf16[192,128]{1,0:T(8,128)(2,1)S(1)}, bf16[192,128]{1,0:T(8,128)(2,1)S(1)}, u32[]{:S(2)}, u32[]{:S(2)}) collective-permute-start(bf16[192,128]{1,0:T(8,128)(2,1)S(1)} %get-tuple-element.49.refs_2_), channel_id=1, source_target_pairs={{4,0},{0,4},{5,1},{1,5},{6,2},{2,6},{7,3},{3,7},{12,8},{8,12},{13,... | collective-permute-start | bytes 147464 | tf_op jit(solution)/shard_map/ppermute | solution.py:73
  24.9 1.7 %collective-permute-start.11 = (bf16[192,128]{1,0:T(8,128)(2,1)S(1)}, bf16[192,128]{1,0:T(8,128)(2,1)S(1)}, u32[]{:S(2)}, u32[]{:S(2)}) collective-permute-start(bf16[192,128]{1,0:T(8,128)(2,1)S(1)} %get-tuple-element.53), channel_id=1, source_target_pairs={{20,0},{16,4},{28,8},{24,12},{4,16},{0,20},{12,24},{8,28},{21,1},{... | collective-permute-start | bytes 147464 | tf_op jit(solution)/shard_map/ppermute | solution.py:81
  26.7 1.4 %collective-permute-start.14 = (bf16[192,128]{1,0:T(8,128)(2,1)S(1)}, bf16[192,128]{1,0:T(8,128)(2,1)S(1)}, u32[]{:S(2)}, u32[]{:S(2)}) collective-permute-start(bf16[192,128]{1,0:T(8,128)(2,1)S(1)} %shard_map.139.refs_0_), channel_id=1, source_target_pairs={{1,0},{0,1},{3,2},{2,3},{5,4},{4,5},{7,6},{6,7},{9,8},{8,9},{11,10... | collective-permute-start | bytes 147464 | tf_op jit(solution)/shard_map/ppermute | solution.py:73
  28.0 0.7 %collective-permute-done.11.refs_3_ = bf16[192,128]{1,0:T(8,128)(2,1)S(1)} collective-permute-done((bf16[192,128]{1,0:T(8,128)(2,1)S(1)}, bf16[192,128]{1,0:T(8,128)(2,1)S(1)}, u32[]{:S(2)}, u32[]{:S(2)}) %collective-permute-start.11) | collective-permute-done | bytes 49184 | tf_op jit(solution)/shard_map/ppermute | solution.py:81
  28.8 1.4 %collective-permute-start.13 = (bf16[192,128]{1,0:T(8,128)(2,1)S(1)}, bf16[192,128]{1,0:T(8,128)(2,1)S(1)}, u32[]{:S(2)}, u32[]{:S(2)}) collective-permute-start(bf16[192,128]{1,0:T(8,128)(2,1)S(1)} %shard_map.138.refs_0_), channel_id=1, source_target_pairs={{1,0},{0,1},{3,2},{2,3},{5,4},{4,5},{7,6},{6,7},{9,8},{8,9},{11,10... | collective-permute-start | bytes 147464 | tf_op jit(solution)/shard_map/ppermute | solution.py:73
  30.2 2.4 %collective-permute-start.16 = (bf16[192,128]{1,0:T(8,128)(2,1)S(1)}, bf16[192,128]{1,0:T(8,128)(2,1)S(1)}, u32[]{:S(2)}, u32[]{:S(2)}) collective-permute-start(bf16[192,128]{1,0:T(8,128)(2,1)S(1)} %shard_map.142.refs_2_), channel_id=1, source_target_pairs={{2,0},{3,1},{0,2},{1,3},{6,4},{7,5},{4,6},{5,7},{10,8},{11,9},{8,1... | collective-permute-start | bytes 147464 | tf_op jit(solution)/shard_map/ppermute | solution.py:73
  32.6 2.2 %collective-permute-start.15 = (bf16[192,128]{1,0:T(8,128)(2,1)S(1)}, bf16[192,128]{1,0:T(8,128)(2,1)S(1)}, u32[]{:S(2)}, u32[]{:S(2)}) collective-permute-start(bf16[192,128]{1,0:T(8,128)(2,1)S(1)} %shard_map.140.refs_5_.refs_0_), channel_id=1, source_target_pairs={{2,0},{3,1},{0,2},{1,3},{6,4},{7,5},{4,6},{5,7},{10,8},{11,9},{8,1... | collective-permute-start | bytes 147464 | tf_op jit(solution)/shard_map/ppermute | solution.py:73
  34.8 2.2 %shard_map.141 = (bf16[16,64,128]{2,1,0:T(8,128)(2,1)}, f32[8,128]{1,0:T(8,128)S(1)}) custom-call(bf16[16,64,128]{2,1,0:T(8,128)(2,1)S(1)} %get-tuple-element.43.refs_0_, bf16[16,64,128]{2,1,0:T(8,128)(2,1)S(1)} %get-tuple-element.44.refs_1_, bf16[896,128]{1,0:T(8,128)(2,1)S(1)} %collective-permute-done.8.refs_1_.refs_2_, ...), custom_call_target="tpu_custom_call" | custom-call | flops 301989888 | bytes 1380352 | tf_op jit(solution)/shard_map/pallas_call | solution.py:38
  37.1 2.5 %collective-permute-start.17 = (bf16[2,192,128]{2,1,0:T(8,128)(2,1)S(1)}, bf16[2,192,128]{2,1,0:T(8,128)(2,1)S(1)}, u32[]{:S(2)}, u32[]{:S(2)}) collective-permute-start(bf16[2,192,128]{2,1,0:T(8,128)(2,1)S(1)} %shard_map.143.refs_0_), channel_id=1, source_target_pairs={{4,0},{0,4},{5,1},{1,5},{6,2},{2,6},{7,3},{3,7},{12,8},{8,12},{13,... | collective-permute-start | bytes 294920 | tf_op jit(solution)/shard_map/ppermute | solution.py:73
  39.6 1.3 %collective-permute-start.21 = (bf16[2,192,128]{2,1,0:T(8,128)(2,1)S(1)}, bf16[2,192,128]{2,1,0:T(8,128)(2,1)S(1)}, u32[]{:S(2)}, u32[]{:S(2)}) collective-permute-start(bf16[2,192,128]{2,1,0:T(8,128)(2,1)S(1)} %shard_map.143.refs_0_), channel_id=1, source_target_pairs={{20,0},{16,4},{28,8},{24,12},{4,16},{0,20},{12,24},{8,28},{21,1},{... | collective-permute-start | bytes 294920 | tf_op jit(solution)/shard_map/ppermute | solution.py:81
  40.8 3.7 %collective-permute-start.18 = (bf16[2,192,128]{2,1,0:T(8,128)(2,1)S(1)}, bf16[2,192,128]{2,1,0:T(8,128)(2,1)S(1)}, u32[]{:S(2)}, u32[]{:S(2)}) collective-permute-start(bf16[2,192,128]{2,1,0:T(8,128)(2,1)S(1)} %shard_map.143.refs_0_), channel_id=1, source_target_pairs={{8,0},{0,8},{24,16},{16,24},{9,1},{1,9},{25,17},{17,25},{10,2},{2,... | collective-permute-start | bytes 294920 | tf_op jit(solution)/shard_map/ppermute | solution.py:73
  44.6 1.4 %collective-permute-start.19 = (bf16[2,192,128]{2,1,0:T(8,128)(2,1)S(1)}, bf16[2,192,128]{2,1,0:T(8,128)(2,1)S(1)}, u32[]{:S(2)}, u32[]{:S(2)}) collective-permute-start(bf16[2,192,128]{2,1,0:T(8,128)(2,1)S(1)} %collective-permute-done.17.refs_1_), channel_id=1, source_target_pairs={{8,0},{0,8},{24,16},{16,24},{9,1},{1,9},{25,17},{17,25},{10,2},{2,... | collective-permute-start | bytes 294920 | tf_op jit(solution)/shard_map/ppermute | solution.py:73
  46.5 2.4 %collective-permute-start.23 = (bf16[2,192,128]{2,1,0:T(8,128)(2,1)S(1)}, bf16[2,192,128]{2,1,0:T(8,128)(2,1)S(1)}, u32[]{:S(2)}, u32[]{:S(2)}) collective-permute-start(bf16[2,192,128]{2,1,0:T(8,128)(2,1)S(1)} %collective-permute-done.21.refs_5_), channel_id=1, source_target_pairs={{8,0},{0,8},{24,16},{16,24},{9,1},{1,9},{25,17},{17,25},{10,2},{2,... | collective-permute-start | bytes 294920 | tf_op jit(solution)/shard_map/ppermute | solution.py:73
  48.9 0.9 %collective-permute-done.23.refs_7_ = bf16[2,192,128]{2,1,0:T(8,128)(2,1)S(1)} collective-permute-done((bf16[2,192,128]{2,1,0:T(8,128)(2,1)S(1)}, bf16[2,192,128]{2,1,0:T(8,128)(2,1)S(1)}, u32[]{:S(2)}, u32[]{:S(2)}) %collective-permute-start.23) | collective-permute-done | bytes 98336 | tf_op jit(solution)/shard_map/ppermute | solution.py:73
  49.9 1.3 %shard_map.144 = (f32[3,384,128]{2,1,0:T(8,128)}, f32[384,128]{1,0:T(8,128)}, f32[3,384,128]{2,1,0:T(8,128)}, f32[384,128]{1,0:T(8,128)}) custom-call(bf16[2,192,128]{2,1,0:T(8,128)(2,1)S(1)} %shard_map.143.refs_0_, bf16[2,192,128]{2,1,0:T(8,128)(2,1)S(1)} %collective-permute-done.17.refs_1_, bf16[2,192,128]{2,1,0:T(8,128)(2,1)S(1)} %collective-permute-done.18.refs_2_, ...), custom_call_target="tpu_custom_call" | custom-call | flops 196608 | bytes 2359296 | tf_op jit(solution)/shard_map/pallas_call | solution.py:38
  (51 shorter events, 2.4 us)
Async XLA Ops:
  0.6 9.2 %collective-permute-start.3 = (bf16[16,64,128]{2,1,0:T(8,128)(2,1)}, bf16[16,64,128]{2,1,0:T(8,128)(2,1)S(1)}, u32[]{:S(2)}, u32[]{:S(2)}) collective-permute-start(bf16[16,64,128]{2,1,0:T(8,128)(2,1)} %bitcast.10), channel_id=1, source_target_pairs={{4,0},{0,4},{5,1},{1,5},{6,2},{2,6},{7,3},{3,7},{12,8},{8,12},{13,... | collective-permute-start | bytes 786440 | tf_op jit(solution)/shard_map/ppermute | solution.py:73
  2.7 5.0 %copy-start = (bf16[1,1,16,64,128]{4,3,2,1,0:T(8,128)(2,1)S(1)}, bf16[1,1,16,64,128]{4,3,2,1,0:T(8,128)(2,1)}, u32[]{:S(2)}) copy-start(bf16[1,1,16,64,128]{4,3,2,1,0:T(8,128)(2,1)} %param.9) | copy-start | bytes 786436
  2.7 5.0 %copy-start.1 = (bf16[3,3,128,128]{3,2,1,0:T(8,128)(2,1)S(1)}, bf16[3,3,128,128]{3,2,1,0:T(8,128)(2,1)}, u32[]{:S(2)}) copy-start(bf16[3,3,128,128]{3,2,1,0:T(8,128)(2,1)} %refs_8_.1) | copy-start | bytes 884740
  2.7 5.0 %copy-start.2 = (bf16[1,1,16,64,128]{4,3,2,1,0:T(8,128)(2,1)S(1)}, bf16[1,1,16,64,128]{4,3,2,1,0:T(8,128)(2,1)}, u32[]{:S(2)}) copy-start(bf16[1,1,16,64,128]{4,3,2,1,0:T(8,128)(2,1)} %param.13) | copy-start | bytes 786436
  2.7 5.0 %copy-start.6 = (bf16[3,128,128]{2,1,0:T(8,128)(2,1)S(1)}, bf16[3,128,128]{2,1,0:T(8,128)(2,1)}, u32[]{:S(2)}) copy-start(bf16[3,128,128]{2,1,0:T(8,128)(2,1)} %refs_7_.1) | copy-start | bytes 294916
  4.4 2.1 %collective-permute-start.1 = (bf16[4,64,128]{2,1,0:T(8,128)(2,1)}, bf16[4,64,128]{2,1,0:T(8,128)(2,1)S(1)}, u32[]{:S(2)}, u32[]{:S(2)}) collective-permute-start(bf16[4,64,128]{2,1,0:T(8,128)(2,1)} %get-tuple-element.35), channel_id=1, source_target_pairs={{8,0},{0,8},{24,16},{16,24},{9,1},{1,9},{25,17},{17,25},{10,2},{2,... | collective-permute-start | bytes 196616 | tf_op jit(solution)/shard_map/ppermute | solution.py:73
  5.4 2.4 %collective-permute-start = (bf16[4,64,128]{2,1,0:T(8,128)(2,1)}, bf16[4,64,128]{2,1,0:T(8,128)(2,1)S(1)}, u32[]{:S(2)}, u32[]{:S(2)}) collective-permute-start(bf16[4,64,128]{2,1,0:T(8,128)(2,1)} %get-tuple-element.34), channel_id=1, source_target_pairs={{8,0},{0,8},{24,16},{16,24},{9,1},{1,9},{25,17},{17,25},{10,2},{2,... | collective-permute-start | bytes 196616 | tf_op jit(solution)/shard_map/ppermute | solution.py:73
  6.5 5.1 %collective-permute-start.2 = (bf16[4,64,128]{2,1,0:T(8,128)(2,1)S(1)}, bf16[4,64,128]{2,1,0:T(8,128)(2,1)S(1)}, u32[]{:S(2)}, u32[]{:S(2)}) collective-permute-start(bf16[4,64,128]{2,1,0:T(8,128)(2,1)S(1)} %collective-permute-done.1.refs_5_), channel_id=1, source_target_pairs={{16,0},{24,8},{0,16},{8,24},{17,1},{25,9},{1,17},{9,25},{18,2},{26... | collective-permute-start | bytes 196616 | tf_op jit(solution)/shard_map/ppermute | solution.py:73
  7.8 7.4 %collective-permute-start.4 = (bf16[14,64,128]{2,1,0:T(8,128)(2,1)S(1)}, bf16[14,64,128]{2,1,0:T(8,128)(2,1)S(1)}, u32[]{:S(2)}, u32[]{:S(2)}) collective-permute-start(bf16[14,64,128]{2,1,0:T(8,128)(2,1)S(1)} %get-tuple-element.36.refs_5_), channel_id=1, source_target_pairs={{4,0},{0,4},{5,1},{1,5},{6,2},{2,6},{7,3},{3,7},{12,8},{8,12},{13,... | collective-permute-start | bytes 688136 | tf_op jit(solution)/shard_map/ppermute | solution.py:73
  13.5 2.0 %collective-permute-start.6 = (bf16[768,128]{1,0:T(8,128)(2,1)S(1)}, bf16[768,128]{1,0:T(8,128)(2,1)S(1)}, u32[]{:S(2)}, u32[]{:S(2)}) collective-permute-start(bf16[768,128]{1,0:T(8,128)(2,1)S(1)} %get-tuple-element.41), channel_id=1, source_target_pairs={{8,0},{0,8},{24,16},{16,24},{9,1},{1,9},{25,17},{17,25},{10,2},{2,... | collective-permute-start | bytes 589832 | tf_op jit(solution)/shard_map/ppermute | solution.py:73
  14.5 3.7 %collective-permute-start.5 = (bf16[4,64,128]{2,1,0:T(8,128)(2,1)S(1)}, bf16[4,64,128]{2,1,0:T(8,128)(2,1)S(1)}, u32[]{:S(2)}, u32[]{:S(2)}) collective-permute-start(bf16[4,64,128]{2,1,0:T(8,128)(2,1)S(1)} %shard_map.131.refs_7_), channel_id=1, source_target_pairs={{4,0},{0,4},{5,1},{1,5},{6,2},{2,6},{7,3},{3,7},{12,8},{8,12},{13,... | collective-permute-start | bytes 196616 | tf_op jit(solution)/shard_map/ppermute | solution.py:73
  15.6 1.1 %copy-start.4 = (bf16[1,1,16,64,128]{4,3,2,1,0:T(8,128)(2,1)S(1)}, bf16[1,1,16,64,128]{4,3,2,1,0:T(8,128)(2,1)}, u32[]{:S(2)}) copy-start(bf16[1,1,16,64,128]{4,3,2,1,0:T(8,128)(2,1)} %param.11) | copy-start | bytes 786436
  15.6 1.1 %copy-start.5 = (bf16[1,1,16,64,128]{4,3,2,1,0:T(8,128)(2,1)S(1)}, bf16[1,1,16,64,128]{4,3,2,1,0:T(8,128)(2,1)}, u32[]{:S(2)}) copy-start(bf16[1,1,16,64,128]{4,3,2,1,0:T(8,128)(2,1)} %param.10) | copy-start | bytes 786436
  15.6 4.7 %collective-permute-start.7 = (bf16[384,128]{1,0:T(8,128)(2,1)S(1)}, bf16[384,128]{1,0:T(8,128)(2,1)S(1)}, u32[]{:S(2)}, u32[]{:S(2)}) collective-permute-start(bf16[384,128]{1,0:T(8,128)(2,1)S(1)} %get-tuple-element.46), channel_id=1, source_target_pairs={{16,0},{24,8},{0,16},{8,24},{17,1},{25,9},{1,17},{9,25},{18,2},{26... | collective-permute-start | bytes 294920 | tf_op jit(solution)/shard_map/ppermute | solution.py:73
  16.7 1.5 %copy-start.8 = (bf16[3,128,128]{2,1,0:T(8,128)(2,1)S(1)}, bf16[3,128,128]{2,1,0:T(8,128)(2,1)}, u32[]{:S(2)}) copy-start(bf16[3,128,128]{2,1,0:T(8,128)(2,1)} %refs_11_.1) | copy-start | bytes 294916
  20.3 2.0 %collective-permute-start.8 = (bf16[896,128]{1,0:T(8,128)(2,1)S(1)}, bf16[896,128]{1,0:T(8,128)(2,1)S(1)}, u32[]{:S(2)}, u32[]{:S(2)}) collective-permute-start(bf16[896,128]{1,0:T(8,128)(2,1)S(1)} %get-tuple-element.47), channel_id=1, source_target_pairs={{8,0},{0,8},{24,16},{16,24},{9,1},{1,9},{25,17},{17,25},{10,2},{2,... | collective-permute-start | bytes 688136 | tf_op jit(solution)/shard_map/ppermute | solution.py:73
  22.4 6.4 %collective-permute-start.9 = (bf16[256,128]{1,0:T(8,128)(2,1)S(1)}, bf16[256,128]{1,0:T(8,128)(2,1)S(1)}, u32[]{:S(2)}, u32[]{:S(2)}) collective-permute-start(bf16[256,128]{1,0:T(8,128)(2,1)S(1)} %get-tuple-element.50), channel_id=1, source_target_pairs={{16,0},{24,8},{0,16},{8,24},{17,1},{25,9},{1,17},{9,25},{18,2},{26... | collective-permute-start | bytes 196616 | tf_op jit(solution)/shard_map/ppermute | solution.py:73
  23.4 3.2 %collective-permute-start.12 = (bf16[192,128]{1,0:T(8,128)(2,1)S(1)}, bf16[192,128]{1,0:T(8,128)(2,1)S(1)}, u32[]{:S(2)}, u32[]{:S(2)}) collective-permute-start(bf16[192,128]{1,0:T(8,128)(2,1)S(1)} %get-tuple-element.49.refs_2_), channel_id=1, source_target_pairs={{4,0},{0,4},{5,1},{1,5},{6,2},{2,6},{7,3},{3,7},{12,8},{8,12},{13,... | collective-permute-start | bytes 147464 | tf_op jit(solution)/shard_map/ppermute | solution.py:73
  24.2 3.8 %collective-permute-start.10 = (bf16[192,128]{1,0:T(8,128)(2,1)S(1)}, bf16[192,128]{1,0:T(8,128)(2,1)S(1)}, u32[]{:S(2)}, u32[]{:S(2)}) collective-permute-start(bf16[192,128]{1,0:T(8,128)(2,1)S(1)} %get-tuple-element.52), channel_id=1, source_target_pairs={{4,0},{0,4},{5,1},{1,5},{6,2},{2,6},{7,3},{3,7},{12,8},{8,12},{13,... | collective-permute-start | bytes 147464 | tf_op jit(solution)/shard_map/ppermute | solution.py:73
  24.9 3.9 %collective-permute-start.11 = (bf16[192,128]{1,0:T(8,128)(2,1)S(1)}, bf16[192,128]{1,0:T(8,128)(2,1)S(1)}, u32[]{:S(2)}, u32[]{:S(2)}) collective-permute-start(bf16[192,128]{1,0:T(8,128)(2,1)S(1)} %get-tuple-element.53), channel_id=1, source_target_pairs={{20,0},{16,4},{28,8},{24,12},{4,16},{0,20},{12,24},{8,28},{21,1},{... | collective-permute-start | bytes 147464 | tf_op jit(solution)/shard_map/ppermute | solution.py:81
  26.7 3.5 %collective-permute-start.14 = (bf16[192,128]{1,0:T(8,128)(2,1)S(1)}, bf16[192,128]{1,0:T(8,128)(2,1)S(1)}, u32[]{:S(2)}, u32[]{:S(2)}) collective-permute-start(bf16[192,128]{1,0:T(8,128)(2,1)S(1)} %shard_map.139.refs_0_), channel_id=1, source_target_pairs={{1,0},{0,1},{3,2},{2,3},{5,4},{4,5},{7,6},{6,7},{9,8},{8,9},{11,10... | collective-permute-start | bytes 147464 | tf_op jit(solution)/shard_map/ppermute | solution.py:73
  28.7 6.0 %copy-start.7 = (bf16[3,3,128,128]{3,2,1,0:T(8,128)(2,1)S(1)}, bf16[3,3,128,128]{3,2,1,0:T(8,128)(2,1)}, u32[]{:S(2)}) copy-start(bf16[3,3,128,128]{3,2,1,0:T(8,128)(2,1)} %refs_4_.5) | copy-start | bytes 884740
  28.8 3.8 %collective-permute-start.13 = (bf16[192,128]{1,0:T(8,128)(2,1)S(1)}, bf16[192,128]{1,0:T(8,128)(2,1)S(1)}, u32[]{:S(2)}, u32[]{:S(2)}) collective-permute-start(bf16[192,128]{1,0:T(8,128)(2,1)S(1)} %shard_map.138.refs_0_), channel_id=1, source_target_pairs={{1,0},{0,1},{3,2},{2,3},{5,4},{4,5},{7,6},{6,7},{9,8},{8,9},{11,10... | collective-permute-start | bytes 147464 | tf_op jit(solution)/shard_map/ppermute | solution.py:73
  30.2 6.9 %collective-permute-start.16 = (bf16[192,128]{1,0:T(8,128)(2,1)S(1)}, bf16[192,128]{1,0:T(8,128)(2,1)S(1)}, u32[]{:S(2)}, u32[]{:S(2)}) collective-permute-start(bf16[192,128]{1,0:T(8,128)(2,1)S(1)} %shard_map.142.refs_2_), channel_id=1, source_target_pairs={{2,0},{3,1},{0,2},{1,3},{6,4},{7,5},{4,6},{5,7},{10,8},{11,9},{8,1... | collective-permute-start | bytes 147464 | tf_op jit(solution)/shard_map/ppermute | solution.py:73
  32.6 4.5 %collective-permute-start.15 = (bf16[192,128]{1,0:T(8,128)(2,1)S(1)}, bf16[192,128]{1,0:T(8,128)(2,1)S(1)}, u32[]{:S(2)}, u32[]{:S(2)}) collective-permute-start(bf16[192,128]{1,0:T(8,128)(2,1)S(1)} %shard_map.140.refs_5_.refs_0_), channel_id=1, source_target_pairs={{2,0},{3,1},{0,2},{1,3},{6,4},{7,5},{4,6},{5,7},{10,8},{11,9},{8,1... | collective-permute-start | bytes 147464 | tf_op jit(solution)/shard_map/ppermute | solution.py:73
  37.1 7.5 %collective-permute-start.17 = (bf16[2,192,128]{2,1,0:T(8,128)(2,1)S(1)}, bf16[2,192,128]{2,1,0:T(8,128)(2,1)S(1)}, u32[]{:S(2)}, u32[]{:S(2)}) collective-permute-start(bf16[2,192,128]{2,1,0:T(8,128)(2,1)S(1)} %shard_map.143.refs_0_), channel_id=1, source_target_pairs={{4,0},{0,4},{5,1},{1,5},{6,2},{2,6},{7,3},{3,7},{12,8},{8,12},{13,... | collective-permute-start | bytes 294920 | tf_op jit(solution)/shard_map/ppermute | solution.py:73
  39.6 6.4 %collective-permute-start.20 = (bf16[2,192,128]{2,1,0:T(8,128)(2,1)S(1)}, bf16[2,192,128]{2,1,0:T(8,128)(2,1)S(1)}, u32[]{:S(2)}, u32[]{:S(2)}) collective-permute-start(bf16[2,192,128]{2,1,0:T(8,128)(2,1)S(1)} %shard_map.143.refs_0_), channel_id=1, source_target_pairs={{16,0},{24,8},{0,16},{8,24},{17,1},{25,9},{1,17},{9,25},{18,2},{26... | collective-permute-start | bytes 294920 | tf_op jit(solution)/shard_map/ppermute | solution.py:73
  39.6 6.9 %collective-permute-start.21 = (bf16[2,192,128]{2,1,0:T(8,128)(2,1)S(1)}, bf16[2,192,128]{2,1,0:T(8,128)(2,1)S(1)}, u32[]{:S(2)}, u32[]{:S(2)}) collective-permute-start(bf16[2,192,128]{2,1,0:T(8,128)(2,1)S(1)} %shard_map.143.refs_0_), channel_id=1, source_target_pairs={{20,0},{16,4},{28,8},{24,12},{4,16},{0,20},{12,24},{8,28},{21,1},{... | collective-permute-start | bytes 294920 | tf_op jit(solution)/shard_map/ppermute | solution.py:81
  40.8 8.1 %collective-permute-start.18 = (bf16[2,192,128]{2,1,0:T(8,128)(2,1)S(1)}, bf16[2,192,128]{2,1,0:T(8,128)(2,1)S(1)}, u32[]{:S(2)}, u32[]{:S(2)}) collective-permute-start(bf16[2,192,128]{2,1,0:T(8,128)(2,1)S(1)} %shard_map.143.refs_0_), channel_id=1, source_target_pairs={{8,0},{0,8},{24,16},{16,24},{9,1},{1,9},{25,17},{17,25},{10,2},{2,... | collective-permute-start | bytes 294920 | tf_op jit(solution)/shard_map/ppermute | solution.py:73
  44.6 4.4 %collective-permute-start.19 = (bf16[2,192,128]{2,1,0:T(8,128)(2,1)S(1)}, bf16[2,192,128]{2,1,0:T(8,128)(2,1)S(1)}, u32[]{:S(2)}, u32[]{:S(2)}) collective-permute-start(bf16[2,192,128]{2,1,0:T(8,128)(2,1)S(1)} %collective-permute-done.17.refs_1_), channel_id=1, source_target_pairs={{8,0},{0,8},{24,16},{16,24},{9,1},{1,9},{25,17},{17,25},{10,2},{2,... | collective-permute-start | bytes 294920 | tf_op jit(solution)/shard_map/ppermute | solution.py:73
  46.0 3.0 %collective-permute-start.22 = (bf16[2,192,128]{2,1,0:T(8,128)(2,1)S(1)}, bf16[2,192,128]{2,1,0:T(8,128)(2,1)S(1)}, u32[]{:S(2)}, u32[]{:S(2)}) collective-permute-start(bf16[2,192,128]{2,1,0:T(8,128)(2,1)S(1)} %collective-permute-done.20.refs_4_), channel_id=1, source_target_pairs={{8,0},{0,8},{24,16},{16,24},{9,1},{1,9},{25,17},{17,25},{10,2},{2,... | collective-permute-start | bytes 294920 | tf_op jit(solution)/shard_map/ppermute | solution.py:73
  46.5 3.4 %collective-permute-start.23 = (bf16[2,192,128]{2,1,0:T(8,128)(2,1)S(1)}, bf16[2,192,128]{2,1,0:T(8,128)(2,1)S(1)}, u32[]{:S(2)}, u32[]{:S(2)}) collective-permute-start(bf16[2,192,128]{2,1,0:T(8,128)(2,1)S(1)} %collective-permute-done.21.refs_5_), channel_id=1, source_target_pairs={{8,0},{0,8},{24,16},{16,24},{9,1},{1,9},{25,17},{17,25},{10,2},{2,... | collective-permute-start | bytes 294920 | tf_op jit(solution)/shard_map/ppermute | solution.py:73
  (1 other events, 1.0 us)

commit v10 on v9

--- a/solution.py
+++ b/solution.py
@@ -23,14 +23,14 @@
     return jax.ShapeDtypeStruct(shape, jnp.float32)
 
 
-def call(kernel, outs, scratch, flops, *operands, after=(), spare_inputs=False, limit=24):
+def call(kernel, outs, scratch, flops, *operands, after=(), early=(), spare_inputs=False, limit=24):
     single = len(outs) == 1
     moved = sum(math.prod(x.shape) * x.dtype.itemsize for x in (*operands, *outs))
     vmem = pl.BlockSpec(memory_space=pltpu.VMEM)
     spare = pl.BlockSpec(memory_space=pl.ANY)
     spec = spare if spare_inputs else vmem
     count = len(operands)
-    operands = (*operands, *after)
+    operands = (*operands, *early, *after)
 
     def body(*refs):
         kernel(*refs[:count], *refs[len(operands) :])
@@ -38,7 +38,7 @@
     return pl.pallas_call(
         body,
         out_shape=outs[0] if single else tuple(outs),
-        in_specs=[spec] * count + [spare] * len(after),
+        in_specs=[spec] * count + [vmem] * len(early) + [spare] * len(after),
         out_specs=vmem if single else (vmem,) * len(outs),
         scratch_shapes=scratch,
         compiler_params=pltpu.CompilerParams(vmem_limit_bytes=limit * MIB),
@@ -185,8 +185,7 @@
     rows, cols, ch = grad_ref.shape
     step = 4
 
-    @pl.loop(0, rows // step)
-    def _(n):
+    for n in range(rows // step):
         here = pl.ds(n * step, step)
         grads = [ref[here] for ref in (grad_ref, *wholes)]
         gpre = pre_gradient(grads, preact_ref[here], temporal_ref)
@@ -195,8 +194,7 @@
 
     half = rows // 2 - 1
 
-    @pl.loop(0, 2)
-    def _(n):
+    for n in range(2):
         first = grad_ref[pl.ds(n * half + 1, half)]
         inner_ref[pl.ds(n * half, half)] = convolved(views_ref, spatial_ref, n * half, first)
 
@@ -270,8 +268,7 @@
     rows, cols, ch = saved_ref.shape
     step = 4
 
-    @pl.loop(0, rows // step)
-    def _(n):
+    for n in range(rows // step):
         here = pl.ds(n * step, step)
         beside(gpre_ref[here].astype(jnp.float32), views_ref, n * step)
 
@@ -292,8 +289,7 @@
     rows, cols, ch = preact_ref.shape
     step = 4
 
-    @pl.loop(0, rows // step)
-    def _(n):
+    for n in range(rows // step):
         here = pl.ds(n * step, step)
         gpre = pre_gradient([ref[here] for ref in mids], preact_ref[here], temporal_ref)
         gpre_ref[here] = gpre.astype(jnp.bfloat16)
@@ -348,13 +344,11 @@
     beside(above.astype(jnp.float32), views_ref, 0)
     beside(below.astype(jnp.float32), views_ref, rows + 1)
 
-    @pl.loop(0, rows // step)
-    def _(n):
+    for n in range(rows // step):
         gpre = gpre_ref[pl.ds(n * step, step)].astype(jnp.float32)
         beside(gpre, views_ref, n * step + 1)
 
-    @pl.loop(0, rows // step)
-    def _(n):
+    for n in range(rows // step):
         here = pl.ds(n * step, step)
         out_ref[here] = convolved(views_ref, spatial_ref, n * step, mid_ref[here])
 
@@ -529,6 +523,7 @@
         *wholes,
         *kernels,
         *known,
+        early=(saved_two,),
     )
     if frames == 2:
         edge = call(
@@ -555,6 +550,7 @@
         grad,
         *wholes,
         after=(edge,) if frames == 2 else (),
+        early=(saved_one, pre_one, temporal_one),
     )
     sides_one = call(
         sides_kernel, [sides], [], conv // 8, saved_one, pre_one, *pairs, after=parts_two[:1]

time: 51.7 us -> 50.8 us (0.983)
  starting transfers between devices: 32.8 us -> 35.1 us
  Pallas kernels: 10.6 us -> 8.36 us
  waiting for transfers between devices: 6.07 us -> 4.98 us
    pallas_call x17, Pallas kernels: 10.6 us -> 8.36 us  [call(): pl.pallas_call(body, out_shape=outs[0] if single else tuple(outs), in_spe...]
    ppermute x22, starting transfers between devices: 29.8 us -> 32 us  [flipped(): lax.ppermute(block, axis, [(place ^ flip, place) for place in range(count)])]
    ppermute x22, waiting for transfers between devices: 5.37 us -> 4.32 us  [flipped(): lax.ppermute(block, axis, [(place ^ flip, place) for place in range(count)])]
  transfers between devices with their start and end apart: 24 -> 24, of which waited for: 7 -> 8; matrix products, arithmetic and copies ran while one was open for 0% -> 0% of each run, Pallas kernels for 18% -> 14%
where the time goes in v10:
time: 50.8 us; the launch traced here: 50.3 us
  starting transfers between devices  35.1 us (69%)
  Pallas kernels  8.36 us (16%)
  waiting for transfers between devices  4.98 us (10%)
  local copies, waits for them, and re-layouts  1.03 us (2%)
  between operations  0.8 us (2%)
    ppermute x22, starting transfers between devices, flipped(): lax.ppermute(block, axis, [(place ^ flip, place) for place in range(count)])  32 us
    pallas_call x17, Pallas kernels, call(): pl.pallas_call(body, out_shape=outs[0] if single else tuple(outs), in_spe...  8.36 us
    ppermute x22, waiting for transfers between devices, flipped(): lax.ppermute(block, axis, [(place ^ flip, place) for place in range(count)])  4.32 us
    ppermute x2, starting transfers between devices, flipped_both(): return lax.ppermute(block, ('section', 'video'), pairs)  3.11 us
    unnamed x18, local copies, waits for them, and re-layouts  1.03 us
  transfers between devices with their start and end apart: 24, of which 8 were waited for; matrix products, arithmetic and copies ran while one was open for 0% of the time, Pallas kernels for 14%

profile of v10, /device:TPU:1, one launch (start us, length us, event | category | flops | bytes accessed | tf_op | source)
XLA Modules:
  0.0 50.3 jit_solution(5003179669079127449)
XLA Ops:
  0.6 2.1 %collective-permute-start.3 = (bf16[16,64,128]{2,1,0:T(8,128)(2,1)}, bf16[16,64,128]{2,1,0:T(8,128)(2,1)S(1)}, u32[]{:S(2)}, u32[]{:S(2)}) collective-permute-start(bf16[16,64,128]{2,1,0:T(8,128)(2,1)} %bitcast.10), channel_id=1, source_target_pairs={{4,0},{0,4},{5,1},{1,5},{6,2},{2,6},{7,3},{3,7},{12,8},{8,12},{13,... | collective-permute-start | bytes 786440 | tf_op jit(solution)/shard_map/ppermute | solution.py:73
  2.7 1.6 %shard_map.128 = (bf16[4,64,128]{2,1,0:T(8,128)(2,1)}, bf16[4,64,128]{2,1,0:T(8,128)(2,1)}) custom-call(bf16[16,64,128]{2,1,0:T(8,128)(2,1)} %bitcast.11, bf16[16,64,128]{2,1,0:T(8,128)(2,1)} %bitcast.20, bf16[16,64,128]{2,1,0:T(8,128)(2,1)} %bitcast.24, bf16[16,64,128]{2,1,0:T(8,128)(2,1)} %bitcast.27), custom_call_target="tpu_custom_call" | custom-call | flops 1 | bytes 1179648 | tf_op jit(solution)/shard_map/pallas_call | solution.py:38
  4.4 1.0 %collective-permute-start.1 = (bf16[4,64,128]{2,1,0:T(8,128)(2,1)}, bf16[4,64,128]{2,1,0:T(8,128)(2,1)S(1)}, u32[]{:S(2)}, u32[]{:S(2)}) collective-permute-start(bf16[4,64,128]{2,1,0:T(8,128)(2,1)} %get-tuple-element.35), channel_id=1, source_target_pairs={{8,0},{0,8},{24,16},{16,24},{9,1},{1,9},{25,17},{17,25},{10,2},{2,... | collective-permute-start | bytes 196616 | tf_op jit(solution)/shard_map/ppermute | solution.py:73
  5.5 1.0 %collective-permute-done.1.refs_5_ = bf16[4,64,128]{2,1,0:T(8,128)(2,1)S(1)} collective-permute-done((bf16[4,64,128]{2,1,0:T(8,128)(2,1)}, bf16[4,64,128]{2,1,0:T(8,128)(2,1)S(1)}, u32[]{:S(2)}, u32[]{:S(2)}) %collective-permute-start.1) | collective-permute-done | bytes 65568 | tf_op jit(solution)/shard_map/ppermute | solution.py:73
  6.5 1.2 %collective-permute-start.2 = (bf16[4,64,128]{2,1,0:T(8,128)(2,1)S(1)}, bf16[4,64,128]{2,1,0:T(8,128)(2,1)S(1)}, u32[]{:S(2)}, u32[]{:S(2)}) collective-permute-start(bf16[4,64,128]{2,1,0:T(8,128)(2,1)S(1)} %collective-permute-done.1.refs_5_), channel_id=1, source_target_pairs={{16,0},{24,8},{0,16},{8,24},{17,1},{25,9},{1,17},{9,25},{18,2},{26... | collective-permute-start | bytes 196616 | tf_op jit(solution)/shard_map/ppermute | solution.py:73
  7.8 1.3 %collective-permute-start.4 = (bf16[14,64,128]{2,1,0:T(8,128)(2,1)S(1)}, bf16[14,64,128]{2,1,0:T(8,128)(2,1)S(1)}, u32[]{:S(2)}, u32[]{:S(2)}) collective-permute-start(bf16[14,64,128]{2,1,0:T(8,128)(2,1)S(1)} %get-tuple-element.36.refs_5_), channel_id=1, source_target_pairs={{4,0},{0,4},{5,1},{1,5},{6,2},{2,6},{7,3},{3,7},{12,8},{8,12},{13,... | collective-permute-start | bytes 688136 | tf_op jit(solution)/shard_map/ppermute | solution.py:73
  9.1 1.0 %shard_map.130 = (bf16[14,64,128]{2,1,0:T(8,128)(2,1)S(1)}, bf16[16,64,128]{2,1,0:T(8,128)(2,1)S(1)}) custom-call(bf16[16,64,128]{2,1,0:T(8,128)(2,1)S(1)} %bitcast.13, bf16[16,64,128]{2,1,0:T(8,128)(2,1)S(1)} %bitcast.22, bf16[16,64,128]{2,1,0:T(8,128)(2,1)S(1)} %collective-permute-done.3.refs_2_.refs_6_, bf16[3,128,128]{2,1,0:T(8,128)(2,1)S(1)} %copy-done.6, ...), custom_call_target="tpu_custom_call" | custom-call | flops 362387872 | bytes 2162688 | tf_op jit(solution)/shard_map/pallas_call | solution.py:38
  10.2 0.9 %copy-done.2 = bf16[1,1,16,64,128]{4,3,2,1,0:T(8,128)(2,1)S(1)} copy-done((bf16[1,1,16,64,128]{4,3,2,1,0:T(8,128)(2,1)S(1)}, bf16[1,1,16,64,128]{4,3,2,1,0:T(8,128)(2,1)}, u32[]{:S(2)}) %copy-start.2) | copy-done | bytes 262168
  11.2 0.8 %shard_map.132 = (f32[2,384,128]{2,1,0:T(8,128)S(1)}, bf16[768,128]{1,0:T(8,128)(2,1)S(1)}) custom-call(bf16[16,64,128]{2,1,0:T(8,128)(2,1)S(1)} %bitcast.26, bf16[16,64,128]{2,1,0:T(8,128)(2,1)S(1)} %bitcast.23, bf16[16,64,128]{2,1,0:T(8,128)(2,1)S(1)} %get-tuple-element.39.refs_6_.refs_2_.refs_4_, ...), custom_call_target="tpu_custom_call" | custom-call | flops 362387872 | bytes 2031616 | tf_op jit(solution)/shard_map/pallas_call | solution.py:38
  12.0 1.2 %collective-permute-start.6 = (bf16[768,128]{1,0:T(8,128)(2,1)S(1)}, bf16[768,128]{1,0:T(8,128)(2,1)S(1)}, u32[]{:S(2)}, u32[]{:S(2)}) collective-permute-start(bf16[768,128]{1,0:T(8,128)(2,1)S(1)} %get-tuple-element.41), channel_id=1, source_target_pairs={{8,0},{0,8},{24,16},{16,24},{9,1},{1,9},{25,17},{17,25},{10,2},{2,... | collective-permute-start | bytes 589832 | tf_op jit(solution)/shard_map/ppermute | solution.py:73
  13.7 0.7 %collective-permute-done.4.refs_2_.refs_5_ = bf16[14,64,128]{2,1,0:T(8,128)(2,1)S(1)} collective-permute-done((bf16[14,64,128]{2,1,0:T(8,128)(2,1)S(1)}, bf16[14,64,128]{2,1,0:T(8,128)(2,1)S(1)}, u32[]{:S(2)}, u32[]{:S(2)}) %collective-permute-start.4) | collective-permute-done | bytes 229408 | tf_op jit(solution)/shard_map/ppermute | solution.py:73
  14.4 1.8 %collective-permute-start.7 = (bf16[384,128]{1,0:T(8,128)(2,1)S(1)}, bf16[384,128]{1,0:T(8,128)(2,1)S(1)}, u32[]{:S(2)}, u32[]{:S(2)}) collective-permute-start(bf16[384,128]{1,0:T(8,128)(2,1)S(1)} %get-tuple-element.46), channel_id=1, source_target_pairs={{16,0},{24,8},{0,16},{8,24},{17,1},{25,9},{1,17},{9,25},{18,2},{26... | collective-permute-start | bytes 294920 | tf_op jit(solution)/shard_map/ppermute | solution.py:73
  16.9 1.5 %shard_map.135 = (bf16[16,64,128]{2,1,0:T(8,128)(2,1)S(1)}, bf16[16,64,128]{2,1,0:T(8,128)(2,1)S(1)}, f32[2,384,128]{2,1,0:T(8,128)S(1)}, bf16[896,128]{1,0:T(8,128)(2,1)S(1)}) custom-call(bf16[16,64,128]{2,1,0:T(8,128)(2,1)S(1)} %bitcast.16, bf16[4,64,128]{2,1,0:T(8,128)(2,1)S(1)} %collective-permute-done.refs_4_.refs_1_.refs_3_.refs_2_, ...), custom_call_target="tpu_custom_call" | custom-call | flops 452984832 | bytes 4128768 | tf_op jit(solution)/shard_map/pallas_call | solution.py:38
  18.4 2.2 %collective-permute-start.8 = (bf16[896,128]{1,0:T(8,128)(2,1)S(1)}, bf16[896,128]{1,0:T(8,128)(2,1)S(1)}, u32[]{:S(2)}, u32[]{:S(2)}) collective-permute-start(bf16[896,128]{1,0:T(8,128)(2,1)S(1)} %get-tuple-element.47), channel_id=1, source_target_pairs={{8,0},{0,8},{24,16},{16,24},{9,1},{1,9},{25,17},{17,25},{10,2},{2,... | collective-permute-start | bytes 688136 | tf_op jit(solution)/shard_map/ppermute | solution.py:73
  20.6 1.1 %collective-permute-done.8.refs_1_.refs_2_ = bf16[896,128]{1,0:T(8,128)(2,1)S(1)} collective-permute-done((bf16[896,128]{1,0:T(8,128)(2,1)S(1)}, bf16[896,128]{1,0:T(8,128)(2,1)S(1)}, u32[]{:S(2)}, u32[]{:S(2)}) %collective-permute-start.8) | collective-permute-done | bytes 229408 | tf_op jit(solution)/shard_map/ppermute | solution.py:73
  21.8 0.9 %collective-permute-start.9 = (bf16[256,128]{1,0:T(8,128)(2,1)S(1)}, bf16[256,128]{1,0:T(8,128)(2,1)S(1)}, u32[]{:S(2)}, u32[]{:S(2)}) collective-permute-start(bf16[256,128]{1,0:T(8,128)(2,1)S(1)} %get-tuple-element.50), channel_id=1, source_target_pairs={{16,0},{24,8},{0,16},{8,24},{17,1},{25,9},{1,17},{9,25},{18,2},{26... | collective-permute-start | bytes 196616 | tf_op jit(solution)/shard_map/ppermute | solution.py:73
  22.6 1.2 %collective-permute-start.12 = (bf16[192,128]{1,0:T(8,128)(2,1)S(1)}, bf16[192,128]{1,0:T(8,128)(2,1)S(1)}, u32[]{:S(2)}, u32[]{:S(2)}) collective-permute-start(bf16[192,128]{1,0:T(8,128)(2,1)S(1)} %get-tuple-element.49.refs_2_), channel_id=1, source_target_pairs={{4,0},{0,4},{5,1},{1,5},{6,2},{2,6},{7,3},{3,7},{12,8},{8,12},{13,... | collective-permute-start | bytes 147464 | tf_op jit(solution)/shard_map/ppermute | solution.py:73
  24.1 1.8 %collective-permute-start.11 = (bf16[192,128]{1,0:T(8,128)(2,1)S(1)}, bf16[192,128]{1,0:T(8,128)(2,1)S(1)}, u32[]{:S(2)}, u32[]{:S(2)}) collective-permute-start(bf16[192,128]{1,0:T(8,128)(2,1)S(1)} %get-tuple-element.53), channel_id=1, source_target_pairs={{20,0},{16,4},{28,8},{24,12},{4,16},{0,20},{12,24},{8,28},{21,1},{... | collective-permute-start | bytes 147464 | tf_op jit(solution)/shard_map/ppermute | solution.py:81
  26.0 1.4 %collective-permute-start.14 = (bf16[192,128]{1,0:T(8,128)(2,1)S(1)}, bf16[192,128]{1,0:T(8,128)(2,1)S(1)}, u32[]{:S(2)}, u32[]{:S(2)}) collective-permute-start(bf16[192,128]{1,0:T(8,128)(2,1)S(1)} %shard_map.139.refs_0_), channel_id=1, source_target_pairs={{1,0},{0,1},{3,2},{2,3},{5,4},{4,5},{7,6},{6,7},{9,8},{8,9},{11,10... | collective-permute-start | bytes 147464 | tf_op jit(solution)/shard_map/ppermute | solution.py:73
  27.5 0.7 %collective-permute-done.11.refs_3_ = bf16[192,128]{1,0:T(8,128)(2,1)S(1)} collective-permute-done((bf16[192,128]{1,0:T(8,128)(2,1)S(1)}, bf16[192,128]{1,0:T(8,128)(2,1)S(1)}, u32[]{:S(2)}, u32[]{:S(2)}) %collective-permute-start.11) | collective-permute-done | bytes 49184 | tf_op jit(solution)/shard_map/ppermute | solution.py:81
  28.2 1.4 %collective-permute-start.13 = (bf16[192,128]{1,0:T(8,128)(2,1)S(1)}, bf16[192,128]{1,0:T(8,128)(2,1)S(1)}, u32[]{:S(2)}, u32[]{:S(2)}) collective-permute-start(bf16[192,128]{1,0:T(8,128)(2,1)S(1)} %shard_map.138.refs_0_), channel_id=1, source_target_pairs={{1,0},{0,1},{3,2},{2,3},{5,4},{4,5},{7,6},{6,7},{9,8},{8,9},{11,10... | collective-permute-start | bytes 147464 | tf_op jit(solution)/shard_map/ppermute | solution.py:73
  29.5 2.4 %collective-permute-start.16 = (bf16[192,128]{1,0:T(8,128)(2,1)S(1)}, bf16[192,128]{1,0:T(8,128)(2,1)S(1)}, u32[]{:S(2)}, u32[]{:S(2)}) collective-permute-start(bf16[192,128]{1,0:T(8,128)(2,1)S(1)} %shard_map.142.refs_2_), channel_id=1, source_target_pairs={{2,0},{3,1},{0,2},{1,3},{6,4},{7,5},{4,6},{5,7},{10,8},{11,9},{8,1... | collective-permute-start | bytes 147464 | tf_op jit(solution)/shard_map/ppermute | solution.py:73
  31.9 2.3 %collective-permute-start.15 = (bf16[192,128]{1,0:T(8,128)(2,1)S(1)}, bf16[192,128]{1,0:T(8,128)(2,1)S(1)}, u32[]{:S(2)}, u32[]{:S(2)}) collective-permute-start(bf16[192,128]{1,0:T(8,128)(2,1)S(1)} %shard_map.140.refs_5_.refs_0_), channel_id=1, source_target_pairs={{2,0},{3,1},{0,2},{1,3},{6,4},{7,5},{4,6},{5,7},{10,8},{11,9},{8,1... | collective-permute-start | bytes 147464 | tf_op jit(solution)/shard_map/ppermute | solution.py:73
  34.2 1.5 %shard_map.141 = (bf16[16,64,128]{2,1,0:T(8,128)(2,1)}, f32[8,128]{1,0:T(8,128)S(1)}) custom-call(bf16[16,64,128]{2,1,0:T(8,128)(2,1)S(1)} %get-tuple-element.43.refs_0_, bf16[16,64,128]{2,1,0:T(8,128)(2,1)S(1)} %get-tuple-element.44.refs_1_, bf16[896,128]{1,0:T(8,128)(2,1)S(1)} %collective-permute-done.8.refs_1_.refs_2_, ...), custom_call_target="tpu_custom_call" | custom-call | flops 301989888 | bytes 1380352 | tf_op jit(solution)/shard_map/pallas_call | solution.py:38
  35.9 3.1 %collective-permute-start.17 = (bf16[2,192,128]{2,1,0:T(8,128)(2,1)S(1)}, bf16[2,192,128]{2,1,0:T(8,128)(2,1)S(1)}, u32[]{:S(2)}, u32[]{:S(2)}) collective-permute-start(bf16[2,192,128]{2,1,0:T(8,128)(2,1)S(1)} %shard_map.143.refs_0_), channel_id=1, source_target_pairs={{4,0},{0,4},{5,1},{1,5},{6,2},{2,6},{7,3},{3,7},{12,8},{8,12},{13,... | collective-permute-start | bytes 294920 | tf_op jit(solution)/shard_map/ppermute | solution.py:73
  39.0 1.3 %collective-permute-start.21 = (bf16[2,192,128]{2,1,0:T(8,128)(2,1)S(1)}, bf16[2,192,128]{2,1,0:T(8,128)(2,1)S(1)}, u32[]{:S(2)}, u32[]{:S(2)}) collective-permute-start(bf16[2,192,128]{2,1,0:T(8,128)(2,1)S(1)} %shard_map.143.refs_0_), channel_id=1, source_target_pairs={{20,0},{16,4},{28,8},{24,12},{4,16},{0,20},{12,24},{8,28},{21,1},{... | collective-permute-start | bytes 294920 | tf_op jit(solution)/shard_map/ppermute | solution.py:81
  40.2 3.6 %collective-permute-start.18 = (bf16[2,192,128]{2,1,0:T(8,128)(2,1)S(1)}, bf16[2,192,128]{2,1,0:T(8,128)(2,1)S(1)}, u32[]{:S(2)}, u32[]{:S(2)}) collective-permute-start(bf16[2,192,128]{2,1,0:T(8,128)(2,1)S(1)} %shard_map.143.refs_0_), channel_id=1, source_target_pairs={{8,0},{0,8},{24,16},{16,24},{9,1},{1,9},{25,17},{17,25},{10,2},{2,... | collective-permute-start | bytes 294920 | tf_op jit(solution)/shard_map/ppermute | solution.py:73
  43.9 1.5 %collective-permute-start.19 = (bf16[2,192,128]{2,1,0:T(8,128)(2,1)S(1)}, bf16[2,192,128]{2,1,0:T(8,128)(2,1)S(1)}, u32[]{:S(2)}, u32[]{:S(2)}) collective-permute-start(bf16[2,192,128]{2,1,0:T(8,128)(2,1)S(1)} %collective-permute-done.17.refs_1_), channel_id=1, source_target_pairs={{8,0},{0,8},{24,16},{16,24},{9,1},{1,9},{25,17},{17,25},{10,2},{2,... | collective-permute-start | bytes 294920 | tf_op jit(solution)/shard_map/ppermute | solution.py:73
  45.4 0.6 %collective-permute-start.22 = (bf16[2,192,128]{2,1,0:T(8,128)(2,1)S(1)}, bf16[2,192,128]{2,1,0:T(8,128)(2,1)S(1)}, u32[]{:S(2)}, u32[]{:S(2)}) collective-permute-start(bf16[2,192,128]{2,1,0:T(8,128)(2,1)S(1)} %collective-permute-done.20.refs_4_), channel_id=1, source_target_pairs={{8,0},{0,8},{24,16},{16,24},{9,1},{1,9},{25,17},{17,25},{10,2},{2,... | collective-permute-start | bytes 294920 | tf_op jit(solution)/shard_map/ppermute | solution.py:73
  46.0 2.0 %collective-permute-start.23 = (bf16[2,192,128]{2,1,0:T(8,128)(2,1)S(1)}, bf16[2,192,128]{2,1,0:T(8,128)(2,1)S(1)}, u32[]{:S(2)}, u32[]{:S(2)}) collective-permute-start(bf16[2,192,128]{2,1,0:T(8,128)(2,1)S(1)} %collective-permute-done.21.refs_5_), channel_id=1, source_target_pairs={{8,0},{0,8},{24,16},{16,24},{9,1},{1,9},{25,17},{17,25},{10,2},{2,... | collective-permute-start | bytes 294920 | tf_op jit(solution)/shard_map/ppermute | solution.py:73
  48.0 0.9 %collective-permute-done.23.refs_7_ = bf16[2,192,128]{2,1,0:T(8,128)(2,1)S(1)} collective-permute-done((bf16[2,192,128]{2,1,0:T(8,128)(2,1)S(1)}, bf16[2,192,128]{2,1,0:T(8,128)(2,1)S(1)}, u32[]{:S(2)}, u32[]{:S(2)}) %collective-permute-start.23) | collective-permute-done | bytes 98336 | tf_op jit(solution)/shard_map/ppermute | solution.py:73
  49.0 1.3 %shard_map.144 = (f32[3,384,128]{2,1,0:T(8,128)}, f32[384,128]{1,0:T(8,128)}, f32[3,384,128]{2,1,0:T(8,128)}, f32[384,128]{1,0:T(8,128)}) custom-call(bf16[2,192,128]{2,1,0:T(8,128)(2,1)S(1)} %shard_map.143.refs_0_, bf16[2,192,128]{2,1,0:T(8,128)(2,1)S(1)} %collective-permute-done.17.refs_1_, bf16[2,192,128]{2,1,0:T(8,128)(2,1)S(1)} %collective-permute-done.18.refs_2_, ...), custom_call_target="tpu_custom_call" | custom-call | flops 196608 | bytes 2359296 | tf_op jit(solution)/shard_map/pallas_call | solution.py:38
  (51 shorter events, 2.3 us)
Async XLA Ops:
  0.6 8.5 %collective-permute-start.3 = (bf16[16,64,128]{2,1,0:T(8,128)(2,1)}, bf16[16,64,128]{2,1,0:T(8,128)(2,1)S(1)}, u32[]{:S(2)}, u32[]{:S(2)}) collective-permute-start(bf16[16,64,128]{2,1,0:T(8,128)(2,1)} %bitcast.10), channel_id=1, source_target_pairs={{4,0},{0,4},{5,1},{1,5},{6,2},{2,6},{7,3},{3,7},{12,8},{8,12},{13,... | collective-permute-start | bytes 786440 | tf_op jit(solution)/shard_map/ppermute | solution.py:73
  2.7 5.0 %copy-start = (bf16[1,1,16,64,128]{4,3,2,1,0:T(8,128)(2,1)S(1)}, bf16[1,1,16,64,128]{4,3,2,1,0:T(8,128)(2,1)}, u32[]{:S(2)}) copy-start(bf16[1,1,16,64,128]{4,3,2,1,0:T(8,128)(2,1)} %param.9) | copy-start | bytes 786436
  2.7 5.0 %copy-start.1 = (bf16[3,3,128,128]{3,2,1,0:T(8,128)(2,1)S(1)}, bf16[3,3,128,128]{3,2,1,0:T(8,128)(2,1)}, u32[]{:S(2)}) copy-start(bf16[3,3,128,128]{3,2,1,0:T(8,128)(2,1)} %refs_8_.1) | copy-start | bytes 884740
  2.7 5.0 %copy-start.3 = (bf16[1,1,16,64,128]{4,3,2,1,0:T(8,128)(2,1)S(1)}, bf16[1,1,16,64,128]{4,3,2,1,0:T(8,128)(2,1)}, u32[]{:S(2)}) copy-start(bf16[1,1,16,64,128]{4,3,2,1,0:T(8,128)(2,1)} %param.13) | copy-start | bytes 786436
  2.7 5.0 %copy-start.6 = (bf16[3,128,128]{2,1,0:T(8,128)(2,1)S(1)}, bf16[3,128,128]{2,1,0:T(8,128)(2,1)}, u32[]{:S(2)}) copy-start(bf16[3,128,128]{2,1,0:T(8,128)(2,1)} %refs_7_.1) | copy-start | bytes 294916
  4.4 2.1 %collective-permute-start.1 = (bf16[4,64,128]{2,1,0:T(8,128)(2,1)}, bf16[4,64,128]{2,1,0:T(8,128)(2,1)S(1)}, u32[]{:S(2)}, u32[]{:S(2)}) collective-permute-start(bf16[4,64,128]{2,1,0:T(8,128)(2,1)} %get-tuple-element.35), channel_id=1, source_target_pairs={{8,0},{0,8},{24,16},{16,24},{9,1},{1,9},{25,17},{17,25},{10,2},{2,... | collective-permute-start | bytes 196616 | tf_op jit(solution)/shard_map/ppermute | solution.py:73
  5.4 3.7 %copy-start.4 = (bf16[1,1,16,64,128]{4,3,2,1,0:T(8,128)(2,1)S(1)}, bf16[1,1,16,64,128]{4,3,2,1,0:T(8,128)(2,1)}, u32[]{:S(2)}) copy-start(bf16[1,1,16,64,128]{4,3,2,1,0:T(8,128)(2,1)} %param.12) | copy-start | bytes 786436
  5.4 2.4 %collective-permute-start = (bf16[4,64,128]{2,1,0:T(8,128)(2,1)}, bf16[4,64,128]{2,1,0:T(8,128)(2,1)S(1)}, u32[]{:S(2)}, u32[]{:S(2)}) collective-permute-start(bf16[4,64,128]{2,1,0:T(8,128)(2,1)} %get-tuple-element.34), channel_id=1, source_target_pairs={{8,0},{0,8},{24,16},{16,24},{9,1},{1,9},{25,17},{17,25},{10,2},{2,... | collective-permute-start | bytes 196616 | tf_op jit(solution)/shard_map/ppermute | solution.py:73
  6.5 3.6 %collective-permute-start.2 = (bf16[4,64,128]{2,1,0:T(8,128)(2,1)S(1)}, bf16[4,64,128]{2,1,0:T(8,128)(2,1)S(1)}, u32[]{:S(2)}, u32[]{:S(2)}) collective-permute-start(bf16[4,64,128]{2,1,0:T(8,128)(2,1)S(1)} %collective-permute-done.1.refs_5_), channel_id=1, source_target_pairs={{16,0},{24,8},{0,16},{8,24},{17,1},{25,9},{1,17},{9,25},{18,2},{26... | collective-permute-start | bytes 196616 | tf_op jit(solution)/shard_map/ppermute | solution.py:73
  7.8 6.6 %collective-permute-start.4 = (bf16[14,64,128]{2,1,0:T(8,128)(2,1)S(1)}, bf16[14,64,128]{2,1,0:T(8,128)(2,1)S(1)}, u32[]{:S(2)}, u32[]{:S(2)}) collective-permute-start(bf16[14,64,128]{2,1,0:T(8,128)(2,1)S(1)} %get-tuple-element.36.refs_5_), channel_id=1, source_target_pairs={{4,0},{0,4},{5,1},{1,5},{6,2},{2,6},{7,3},{3,7},{12,8},{8,12},{13,... | collective-permute-start | bytes 688136 | tf_op jit(solution)/shard_map/ppermute | solution.py:73
  10.1 1.0 %copy-start.5 = (bf16[1,1,16,64,128]{4,3,2,1,0:T(8,128)(2,1)S(1)}, bf16[1,1,16,64,128]{4,3,2,1,0:T(8,128)(2,1)}, u32[]{:S(2)}) copy-start(bf16[1,1,16,64,128]{4,3,2,1,0:T(8,128)(2,1)} %param.10) | copy-start | bytes 786436
  10.1 1.0 %copy-start.7 = (bf16[3,128,128]{2,1,0:T(8,128)(2,1)S(1)}, bf16[3,128,128]{2,1,0:T(8,128)(2,1)}, u32[]{:S(2)}) copy-start(bf16[3,128,128]{2,1,0:T(8,128)(2,1)} %refs_11_.1) | copy-start | bytes 294916
  12.0 2.4 %collective-permute-start.6 = (bf16[768,128]{1,0:T(8,128)(2,1)S(1)}, bf16[768,128]{1,0:T(8,128)(2,1)S(1)}, u32[]{:S(2)}, u32[]{:S(2)}) collective-permute-start(bf16[768,128]{1,0:T(8,128)(2,1)S(1)} %get-tuple-element.41), channel_id=1, source_target_pairs={{8,0},{0,8},{24,16},{16,24},{9,1},{1,9},{25,17},{17,25},{10,2},{2,... | collective-permute-start | bytes 589832 | tf_op jit(solution)/shard_map/ppermute | solution.py:73
  13.2 3.7 %collective-permute-start.5 = (bf16[4,64,128]{2,1,0:T(8,128)(2,1)S(1)}, bf16[4,64,128]{2,1,0:T(8,128)(2,1)S(1)}, u32[]{:S(2)}, u32[]{:S(2)}) collective-permute-start(bf16[4,64,128]{2,1,0:T(8,128)(2,1)S(1)} %shard_map.131.refs_10_), channel_id=1, source_target_pairs={{4,0},{0,4},{5,1},{1,5},{6,2},{2,6},{7,3},{3,7},{12,8},{8,12},{13,... | collective-permute-start | bytes 196616 | tf_op jit(solution)/shard_map/ppermute | solution.py:73
  14.4 4.0 %collective-permute-start.7 = (bf16[384,128]{1,0:T(8,128)(2,1)S(1)}, bf16[384,128]{1,0:T(8,128)(2,1)S(1)}, u32[]{:S(2)}, u32[]{:S(2)}) collective-permute-start(bf16[384,128]{1,0:T(8,128)(2,1)S(1)} %get-tuple-element.46), channel_id=1, source_target_pairs={{16,0},{24,8},{0,16},{8,24},{17,1},{25,9},{1,17},{9,25},{18,2},{26... | collective-permute-start | bytes 294920 | tf_op jit(solution)/shard_map/ppermute | solution.py:73
  18.4 3.3 %collective-permute-start.8 = (bf16[896,128]{1,0:T(8,128)(2,1)S(1)}, bf16[896,128]{1,0:T(8,128)(2,1)S(1)}, u32[]{:S(2)}, u32[]{:S(2)}) collective-permute-start(bf16[896,128]{1,0:T(8,128)(2,1)S(1)} %get-tuple-element.47), channel_id=1, source_target_pairs={{8,0},{0,8},{24,16},{16,24},{9,1},{1,9},{25,17},{17,25},{10,2},{2,... | collective-permute-start | bytes 688136 | tf_op jit(solution)/shard_map/ppermute | solution.py:73
  21.8 6.4 %collective-permute-start.9 = (bf16[256,128]{1,0:T(8,128)(2,1)S(1)}, bf16[256,128]{1,0:T(8,128)(2,1)S(1)}, u32[]{:S(2)}, u32[]{:S(2)}) collective-permute-start(bf16[256,128]{1,0:T(8,128)(2,1)S(1)} %get-tuple-element.50), channel_id=1, source_target_pairs={{16,0},{24,8},{0,16},{8,24},{17,1},{25,9},{1,17},{9,25},{18,2},{26... | collective-permute-start | bytes 196616 | tf_op jit(solution)/shard_map/ppermute | solution.py:73
  22.6 3.3 %collective-permute-start.12 = (bf16[192,128]{1,0:T(8,128)(2,1)S(1)}, bf16[192,128]{1,0:T(8,128)(2,1)S(1)}, u32[]{:S(2)}, u32[]{:S(2)}) collective-permute-start(bf16[192,128]{1,0:T(8,128)(2,1)S(1)} %get-tuple-element.49.refs_2_), channel_id=1, source_target_pairs={{4,0},{0,4},{5,1},{1,5},{6,2},{2,6},{7,3},{3,7},{12,8},{8,12},{13,... | collective-permute-start | bytes 147464 | tf_op jit(solution)/shard_map/ppermute | solution.py:73
  23.8 3.7 %collective-permute-start.10 = (bf16[192,128]{1,0:T(8,128)(2,1)S(1)}, bf16[192,128]{1,0:T(8,128)(2,1)S(1)}, u32[]{:S(2)}, u32[]{:S(2)}) collective-permute-start(bf16[192,128]{1,0:T(8,128)(2,1)S(1)} %get-tuple-element.52), channel_id=1, source_target_pairs={{4,0},{0,4},{5,1},{1,5},{6,2},{2,6},{7,3},{3,7},{12,8},{8,12},{13,... | collective-permute-start | bytes 147464 | tf_op jit(solution)/shard_map/ppermute | solution.py:73
  24.1 4.0 %collective-permute-start.11 = (bf16[192,128]{1,0:T(8,128)(2,1)S(1)}, bf16[192,128]{1,0:T(8,128)(2,1)S(1)}, u32[]{:S(2)}, u32[]{:S(2)}) collective-permute-start(bf16[192,128]{1,0:T(8,128)(2,1)S(1)} %get-tuple-element.53), channel_id=1, source_target_pairs={{20,0},{16,4},{28,8},{24,12},{4,16},{0,20},{12,24},{8,28},{21,1},{... | collective-permute-start | bytes 147464 | tf_op jit(solution)/shard_map/ppermute | solution.py:81
  26.0 3.6 %collective-permute-start.14 = (bf16[192,128]{1,0:T(8,128)(2,1)S(1)}, bf16[192,128]{1,0:T(8,128)(2,1)S(1)}, u32[]{:S(2)}, u32[]{:S(2)}) collective-permute-start(bf16[192,128]{1,0:T(8,128)(2,1)S(1)} %shard_map.139.refs_0_), channel_id=1, source_target_pairs={{1,0},{0,1},{3,2},{2,3},{5,4},{4,5},{7,6},{6,7},{9,8},{8,9},{11,10... | collective-permute-start | bytes 147464 | tf_op jit(solution)/shard_map/ppermute | solution.py:73
  28.1 6.1 %copy-start.8 = (bf16[3,3,128,128]{3,2,1,0:T(8,128)(2,1)S(1)}, bf16[3,3,128,128]{3,2,1,0:T(8,128)(2,1)}, u32[]{:S(2)}) copy-start(bf16[3,3,128,128]{3,2,1,0:T(8,128)(2,1)} %refs_4_.5) | copy-start | bytes 884740
  28.2 3.8 %collective-permute-start.13 = (bf16[192,128]{1,0:T(8,128)(2,1)S(1)}, bf16[192,128]{1,0:T(8,128)(2,1)S(1)}, u32[]{:S(2)}, u32[]{:S(2)}) collective-permute-start(bf16[192,128]{1,0:T(8,128)(2,1)S(1)} %shard_map.138.refs_0_), channel_id=1, source_target_pairs={{1,0},{0,1},{3,2},{2,3},{5,4},{4,5},{7,6},{6,7},{9,8},{8,9},{11,10... | collective-permute-start | bytes 147464 | tf_op jit(solution)/shard_map/ppermute | solution.py:73
  29.5 6.2 %collective-permute-start.16 = (bf16[192,128]{1,0:T(8,128)(2,1)S(1)}, bf16[192,128]{1,0:T(8,128)(2,1)S(1)}, u32[]{:S(2)}, u32[]{:S(2)}) collective-permute-start(bf16[192,128]{1,0:T(8,128)(2,1)S(1)} %shard_map.142.refs_2_), channel_id=1, source_target_pairs={{2,0},{3,1},{0,2},{1,3},{6,4},{7,5},{4,6},{5,7},{10,8},{11,9},{8,1... | collective-permute-start | bytes 147464 | tf_op jit(solution)/shard_map/ppermute | solution.py:73
  31.9 3.9 %collective-permute-start.15 = (bf16[192,128]{1,0:T(8,128)(2,1)S(1)}, bf16[192,128]{1,0:T(8,128)(2,1)S(1)}, u32[]{:S(2)}, u32[]{:S(2)}) collective-permute-start(bf16[192,128]{1,0:T(8,128)(2,1)S(1)} %shard_map.140.refs_5_.refs_0_), channel_id=1, source_target_pairs={{2,0},{3,1},{0,2},{1,3},{6,4},{7,5},{4,6},{5,7},{10,8},{11,9},{8,1... | collective-permute-start | bytes 147464 | tf_op jit(solution)/shard_map/ppermute | solution.py:73
  35.9 8.0 %collective-permute-start.17 = (bf16[2,192,128]{2,1,0:T(8,128)(2,1)S(1)}, bf16[2,192,128]{2,1,0:T(8,128)(2,1)S(1)}, u32[]{:S(2)}, u32[]{:S(2)}) collective-permute-start(bf16[2,192,128]{2,1,0:T(8,128)(2,1)S(1)} %shard_map.143.refs_0_), channel_id=1, source_target_pairs={{4,0},{0,4},{5,1},{1,5},{6,2},{2,6},{7,3},{3,7},{12,8},{8,12},{13,... | collective-permute-start | bytes 294920 | tf_op jit(solution)/shard_map/ppermute | solution.py:73
  39.0 6.4 %collective-permute-start.20 = (bf16[2,192,128]{2,1,0:T(8,128)(2,1)S(1)}, bf16[2,192,128]{2,1,0:T(8,128)(2,1)S(1)}, u32[]{:S(2)}, u32[]{:S(2)}) collective-permute-start(bf16[2,192,128]{2,1,0:T(8,128)(2,1)S(1)} %shard_map.143.refs_0_), channel_id=1, source_target_pairs={{16,0},{24,8},{0,16},{8,24},{17,1},{25,9},{1,17},{9,25},{18,2},{26... | collective-permute-start | bytes 294920 | tf_op jit(solution)/shard_map/ppermute | solution.py:73
  39.0 7.0 %collective-permute-start.21 = (bf16[2,192,128]{2,1,0:T(8,128)(2,1)S(1)}, bf16[2,192,128]{2,1,0:T(8,128)(2,1)S(1)}, u32[]{:S(2)}, u32[]{:S(2)}) collective-permute-start(bf16[2,192,128]{2,1,0:T(8,128)(2,1)S(1)} %shard_map.143.refs_0_), channel_id=1, source_target_pairs={{20,0},{16,4},{28,8},{24,12},{4,16},{0,20},{12,24},{8,28},{21,1},{... | collective-permute-start | bytes 294920 | tf_op jit(solution)/shard_map/ppermute | solution.py:81
  40.2 7.8 %collective-permute-start.18 = (bf16[2,192,128]{2,1,0:T(8,128)(2,1)S(1)}, bf16[2,192,128]{2,1,0:T(8,128)(2,1)S(1)}, u32[]{:S(2)}, u32[]{:S(2)}) collective-permute-start(bf16[2,192,128]{2,1,0:T(8,128)(2,1)S(1)} %shard_map.143.refs_0_), channel_id=1, source_target_pairs={{8,0},{0,8},{24,16},{16,24},{9,1},{1,9},{25,17},{17,25},{10,2},{2,... | collective-permute-start | bytes 294920 | tf_op jit(solution)/shard_map/ppermute | solution.py:73
  43.9 4.2 %collective-permute-start.19 = (bf16[2,192,128]{2,1,0:T(8,128)(2,1)S(1)}, bf16[2,192,128]{2,1,0:T(8,128)(2,1)S(1)}, u32[]{:S(2)}, u32[]{:S(2)}) collective-permute-start(bf16[2,192,128]{2,1,0:T(8,128)(2,1)S(1)} %collective-permute-done.17.refs_1_), channel_id=1, source_target_pairs={{8,0},{0,8},{24,16},{16,24},{9,1},{1,9},{25,17},{17,25},{10,2},{2,... | collective-permute-start | bytes 294920 | tf_op jit(solution)/shard_map/ppermute | solution.py:73
  45.4 2.7 %collective-permute-start.22 = (bf16[2,192,128]{2,1,0:T(8,128)(2,1)S(1)}, bf16[2,192,128]{2,1,0:T(8,128)(2,1)S(1)}, u32[]{:S(2)}, u32[]{:S(2)}) collective-permute-start(bf16[2,192,128]{2,1,0:T(8,128)(2,1)S(1)} %collective-permute-done.20.refs_4_), channel_id=1, source_target_pairs={{8,0},{0,8},{24,16},{16,24},{9,1},{1,9},{25,17},{17,25},{10,2},{2,... | collective-permute-start | bytes 294920 | tf_op jit(solution)/shard_map/ppermute | solution.py:73
  46.0 3.0 %collective-permute-start.23 = (bf16[2,192,128]{2,1,0:T(8,128)(2,1)S(1)}, bf16[2,192,128]{2,1,0:T(8,128)(2,1)S(1)}, u32[]{:S(2)}, u32[]{:S(2)}) collective-permute-start(bf16[2,192,128]{2,1,0:T(8,128)(2,1)S(1)} %collective-permute-done.21.refs_5_), channel_id=1, source_target_pairs={{8,0},{0,8},{24,16},{16,24},{9,1},{1,9},{25,17},{17,25},{10,2},{2,... | collective-permute-start | bytes 294920 | tf_op jit(solution)/shard_map/ppermute | solution.py:73
  (1 other events, 1.0 us)

commit v11 on v10

--- a/solution.py
+++ b/solution.py
@@ -71,6 +71,25 @@
 def flipped(block, axis, flip):
     count = lax.axis_size(axis)
     return lax.ppermute(block, axis, [(place ^ flip, place) for place in range(count)])
+
+
+def flipped_odd(block, axis, flip):
+    names = ("section", "video", "dp")
+    counts = [lax.axis_size(name) for name in names]
+    pairs = []
+    for band in range(1, counts[0], 2):
+        for frame in range(counts[1]):
+            for clip in range(counts[2]):
+                place = {"section": band, "video": frame, "dp": clip}
+                source = dict(place)
+                source[axis] ^= flip
+                pairs.append(
+                    tuple(
+                        (at["section"] * counts[1] + at["video"]) * counts[2] + at["dp"]
+                        for at in (source, place)
+                    )
+                )
+    return lax.ppermute(block, names, pairs)
 
 
 def flipped_both(block):
@@ -263,8 +282,8 @@
 def two_kernel(later, *refs):
     saved_ref, preact_ref, gpre_ref = refs[:3]
     pair_refs, grad_ref = refs[3:5], refs[5]
-    wholes, outs = refs[6 : 6 + later], refs[6 + later : 8 + later]
-    views_ref, sides_ref, sums_ref = refs[8 + later :]
+    wholes, outs = refs[6 : 6 + later], refs[6 + later : 9 + later]
+    views_ref, sides_ref, sums_ref = refs[9 + later :]
     rows, cols, ch = saved_ref.shape
     step = 4
 
@@ -276,7 +295,7 @@
     grads = [ref[...] for ref in (grad_ref, *wholes)]
     left_sides(saved_ref, preact_ref, *beside_band(pair_refs, 2), sides_ref)
     kernel_sums(sides_ref, grads, views, sums_ref)
-    hand_out(sums_ref, *outs)
+    share_out(sums_ref, *outs)
 
 
 def sides_kernel(saved_ref, preact_ref, one_ref, two_ref, sides_ref):
@@ -357,6 +376,59 @@
     return [pl.ds(pl.multiple_of(n * count, count), count) for n in (index, 1 - index)]
 
 
+def is_odd():
+    return lax.rem(lax.axis_index("section"), 2) == 1
+
+
+def share_out(sums_ref, keep_ref, *send_refs):
+    height = sums_ref.shape[1]
+    for n in range(4):
+        keep_ref[n] = sums_ref[n]
+        start = n % 2 * height
+        send_refs[n // 2][start : start + height] = sums_ref[n].astype(jnp.bfloat16)
+
+
+def odd_pair_kernel(keep_ref, low_ref, high_ref, own_ref, send_ref):
+    height = keep_ref.shape[1]
+
+    @pl.when(is_odd())
+    def _():
+        across = lax.axis_index("section") // 2
+        for n in range(2):
+            here = slice(n * height, (n + 1) * height)
+            low, high = (ref[here].astype(jnp.float32) for ref in (low_ref, high_ref))
+            for where, ref in ((across, own_ref), (1 - across, send_ref)):
+                total = keep_ref[2 * where + n] + jnp.where(where == 0, low, high)
+                ref[here] = total.astype(ref.dtype)
+
+
+def odd_band_kernel(own_ref, part_ref, keep_ref, send_ref):
+    half = keep_ref.shape[1]
+
+    @pl.when(is_odd())
+    def _():
+        frame = lax.axis_index("video")
+        for n in range(2):
+            for where, ref in ((frame, keep_ref), (1 - frame, send_ref)):
+                rows = pl.ds(pl.multiple_of((2 * n + where) * half, half), half)
+                total = own_ref[rows] + part_ref[rows].astype(jnp.float32)
+                ref[n] = total.astype(ref.dtype)
+
+
+def odd_add_kernel(one_ref, two_ref, out_ref):
+    @pl.when(is_odd())
+    def _():
+        add_kernel(one_ref, two_ref, out_ref)
+
+
+def odd_scaled_kernel(factor, one_ref, two_ref, own_ref, send_ref):
+    @pl.when(is_odd())
+    def _():
+        total = one_ref[...].astype(jnp.float32) + two_ref[...].astype(jnp.float32)
+        total = (total * factor).astype(jnp.bfloat16)
+        send_ref[...], own_ref[...] = total[0], total[1]
+
+
 def pair_kernel(keep_ref, part_ref, own_ref, send_ref):
     across = lax.axis_index("section") // 2
     mine, other = halves(own_ref.shape[0], across)
@@ -365,12 +437,6 @@
     send_ref[...] = total.astype(jnp.bfloat16)
 
 
-def band_kernel(own_ref, part_ref, keep_ref, send_ref):
-    mine, other = halves(keep_ref.shape[0], lax.axis_index("video"))
-    keep_ref[...] = own_ref[mine] + part_ref[mine].astype(jnp.float32)
-    send_ref[...] = (own_ref[other] + part_ref[other].astype(jnp.float32)).astype(jnp.bfloat16)
-
-
 def pair_quarter_kernel(keep_ref, part_ref, own_ref, across_ref, frame_ref, both_ref):
     _, height, _ = keep_ref.shape
     half = own_ref.shape[0]
@@ -403,11 +469,10 @@
     out_ref[...] = total.astype(jnp.bfloat16)
 
 
-def scaled_kernel(factor, *refs):
-    out_ref = refs[-1]
-    for block in range(2):
-        one, two = (ref[...].astype(jnp.float32) for ref in refs[2 * block : 2 * block + 2])
-        out_ref[block] = ((one + two) * factor).astype(jnp.bfloat16)
+def scaled_kernel(factor, one_ref, two_ref, own_ref, given_ref, out_ref):
+    total = one_ref[...].astype(jnp.float32) + two_ref[...].astype(jnp.float32)
+    out_ref[0] = (total * factor).astype(jnp.bfloat16)
+    out_ref[1] = jnp.where(is_odd(), own_ref[...], given_ref[...])
 
 
 def place_kernel(*refs):
@@ -473,7 +538,7 @@
     act = pltpu.VMEM((rows, cols, ch), jnp.bfloat16)
     sides = bf16(4, ch, rows * cols)
     sums = pltpu.VMEM((4, 3 * ch, ch), jnp.float32)
-    handed = [f32(2, 3 * ch, ch), bf16(6 * ch, ch)]
+    handed = [f32(4, 3 * ch, ch)] + [bf16(6 * ch, ch)] * 2
     inner_outs = [bf16(rows - 2, cols, ch), bf16(rows, cols, ch)]
     kernels = (temporal_two, spatial_two)
 
@@ -523,7 +588,7 @@
         *wholes,
         *kernels,
         *known,
-        early=(saved_two,),
+        early=(saved_two, saved_one, pre_one, temporal_one),
     )
     if frames == 2:
         edge = call(
@@ -550,23 +615,22 @@
         grad,
         *wholes,
         after=(edge,) if frames == 2 else (),
-        early=(saved_one, pre_one, temporal_one),
     )
     sides_one = call(
         sides_kernel, [sides], [], conv // 8, saved_one, pre_one, *pairs, after=parts_two[:1]
     )
     height, half = 3 * ch, 3 * ch // 2
-    keep_two, send_two = parts_two
+    keep_two, *sends_two = parts_two
     own_two, send_two = call(
-        pair_kernel,
-        [f32(height, ch), bf16(height, ch)],
+        odd_pair_kernel,
+        [f32(2 * height, ch), bf16(2 * height, ch)],
         [],
-        height * ch,
+        2 * height * ch,
         keep_two,
-        flipped(send_two, "section", 1),
+        *[flipped(send, "section", 1) for send in sends_two],
         after=afters[:1] if frames == 2 else (),
     )
-    across_two = flipped(send_two, "section", 2)
+    across_two = flipped_odd(send_two, "section", 2)
     mid_inputs = (grad, *pairs, inner, gpre_two)
     one_inputs = (sides_one, pre_one)
     mid_outs = [bf16(rows, cols, ch)]
@@ -576,7 +640,7 @@
             mid_one_kernel,
             mid_outs + one_outs,
             [views, sums, act, pltpu.VMEM((2, cols, ch), jnp.bfloat16), edge_views],
-            1.5 * conv,
+            8 * conv,
             *mid_inputs,
             *afters,
             *kernels,
@@ -626,32 +690,46 @@
 
     if split:
 
+        odd_cut = (2, half, ch)
+        outs = [f32(*odd_cut), bf16(*odd_cut)]
+        def odd_added(one, two, after):
+            return call(odd_add_kernel, [bf16(*odd_cut)], [], height * ch, one, two, after=after)
+
         def added(one, two):
             return call(add_kernel, [bf16(half, ch)], [], half * ch, one, two)
 
+        quarters = [f32(half, ch), bf16(half + cols, ch)] + [bf16(half, ch)] * 2
+        own_one, *sends = call(
+            pair_quarter_kernel, quarters, [], height * ch, keep_one, pair_one
+        )
         keep_two, send_two = call(
-            band_kernel,
-            [f32(half, ch), bf16(half, ch)],
+            odd_band_kernel,
+            outs,
             [],
-            height * ch,
+            2 * height * ch,
             own_two,
             across_two,
-        )
-        sum_two = added(keep_two, flipped(send_two, "video", 1))
-        quarters = [f32(half, ch), bf16(half + cols, ch)] + [bf16(half, ch)] * 2
-        own_one, *sends = call(
-            pair_quarter_kernel, quarters, [], height * ch, keep_one, pair_one, after=(send_two,)
+            after=sends[2:],
         )
         across = flipped(sends[0], "section", 2)
         parts = [across, flipped(sends[1], "video", 1), flipped_both(sends[2])]
         sum_one = call(plane_kernel, [bf16(half, ch)], [], 4 * half * ch, own_one, *parts)
-        part_two = flipped(sum_two, "dp", 1)
-        part_one = flipped(later_than(sum_one, sum_two), "dp", 1)
-        sum_two = added(sum_two, part_two)
+        sum_two = odd_added(keep_two, flipped_odd(send_two, "video", 1), (sum_one,))
+        part_two = flipped_odd(sum_two, "dp", 1)
+        part_one = flipped(sum_one, "dp", 1)
         sum_one = added(sum_one, part_one)
-        last_two = flipped(sum_two, "dp", 2)
-        last_one = flipped(later_than(sum_one, sum_two), "dp", 2)
+        sum_two = odd_added(sum_two, part_two, (sum_one,))
+        last_two = flipped_odd(sum_two, "dp", 2)
+        last_one = flipped(sum_one, "dp", 2)
         grad_in, token = input_gradient(across, (sum_one,))
+        own_two, given_two = call(
+            functools.partial(odd_scaled_kernel, factor),
+            [bf16(half, ch)] * 2,
+            [],
+            height * ch,
+            sum_two,
+            last_two,
+        )
         own = call(
             functools.partial(scaled_kernel, factor),
             [bf16(2, half, ch)],
@@ -659,8 +737,8 @@
             height * ch,
             sum_one,
             last_one,
-            sum_two,
-            last_two,
+            own_two,
+            flipped(given_two, "section", 1),
             after=(token,),
         )
         shares = [own, flipped(own, "video", 1)]
@@ -673,6 +751,8 @@
         grad_in, _ = input_gradient(edge, ())
         own_one = own_one + flipped(send_one, "section", 2).astype(jnp.float32)
         own_two = own_two + across_two.astype(jnp.float32)
+        given_two = flipped(own_two[:height].astype(jnp.bfloat16), "section", 1)
+        own_two = jnp.where(is_odd(), own_two[height:], given_two.astype(jnp.float32))
         share = lax.psum(jnp.stack((own_one, own_two)), ("video", "dp")) * factor
         share = share.astype(jnp.bfloat16)
         sums = placed([share], [flipped(share, "section", 2)])

time: 50.8 us -> 58.1 us (1.14)
  waiting for transfers between devices: 4.98 us -> 16.3 us
  starting transfers between devices: 35.1 us -> 32.1 us
  local copies, waits for them, and re-layouts: 1.03 us -> 0.04 us
    ppermute x22 -> x20, starting transfers between devices: 32 us -> 16.9 us  [flipped(): lax.ppermute(block, axis, [(place ^ flip, place) for place in range(count)])]
    ppermute x0 -> x4, starting transfers between devices: none -> 13.2 us  [flipped_odd(): return lax.ppermute(block, names, pairs)]
    ppermute x22 -> x20, waiting for transfers between devices: 4.32 us -> 9.47 us  [flipped(): lax.ppermute(block, axis, [(place ^ flip, place) for place in range(count)])]
    ppermute x0 -> x4, waiting for transfers between devices: none -> 4.63 us  [flipped_odd(): return lax.ppermute(block, names, pairs)]
    ppermute x2, waiting for transfers between devices: 0.67 us -> 2.17 us  [flipped_both(): return lax.ppermute(block, ('section', 'video'), pairs)]
    ppermute x2, starting transfers between devices: 3.11 us -> 2.04 us  [flipped_both(): return lax.ppermute(block, ('section', 'video'), pairs)]
    unnamed x18, local copies, waits for them, and re-layouts: 1.03 us -> 0.04 us
    pallas_call x17 -> x18, Pallas kernels: 8.36 us -> 8.45 us  [call(): pl.pallas_call(body, out_shape=outs[0] if single else tuple(outs), in_spe...]
  transfers between devices with their start and end apart: 24 -> 26, of which waited for: 8 -> 12; matrix products, arithmetic and copies ran while one was open for 0% -> 0% of each run, Pallas kernels for 14% -> 12%
where the time goes in v11:
time: 58.1 us; the launch traced here: 57.7 us
  starting transfers between devices  32.1 us (55%)
  waiting for transfers between devices  16.3 us (28%)
  Pallas kernels  8.45 us (15%)
  between operations  0.89 us (2%)
    ppermute x20, starting transfers between devices, flipped(): lax.ppermute(block, axis, [(place ^ flip, place) for place in range(count)])  16.9 us
    ppermute x4, starting transfers between devices, flipped_odd(): return lax.ppermute(block, names, pairs)  13.2 us
    ppermute x20, waiting for transfers between devices, flipped(): lax.ppermute(block, axis, [(place ^ flip, place) for place in range(count)])  9.47 us
    pallas_call x18, Pallas kernels, call(): pl.pallas_call(body, out_shape=outs[0] if single else tuple(outs), in_spe...  8.45 us
    ppermute x4, waiting for transfers between devices, flipped_odd(): return lax.ppermute(block, names, pairs)  4.63 us
    ppermute x2, waiting for transfers between devices, flipped_both(): return lax.ppermute(block, ('section', 'video'), pairs)  2.17 us
    ppermute x2, starting transfers between devices, flipped_both(): return lax.ppermute(block, ('section', 'video'), pairs)  2.04 us
  transfers between devices with their start and end apart: 26, of which 12 were waited for; matrix products, arithmetic and copies ran while one was open for 0% of the time, Pallas kernels for 12%

profile of v11, /device:TPU:1, one launch (start us, length us, event | category | flops | bytes accessed | tf_op | source)
XLA Modules:
  0.0 57.7 jit_solution(2656895800768337334)
XLA Ops:
  0.6 2.1 %collective-permute-start.3 = (bf16[16,64,128]{2,1,0:T(8,128)(2,1)}, bf16[16,64,128]{2,1,0:T(8,128)(2,1)S(1)}, u32[]{:S(2)}, u32[]{:S(2)}) collective-permute-start(bf16[16,64,128]{2,1,0:T(8,128)(2,1)} %bitcast.10), channel_id=1, source_target_pairs={{4,0},{0,4},{5,1},{1,5},{6,2},{2,6},{7,3},{3,7},{12,8},{8,12},{13,... | collective-permute-start | bytes 786440 | tf_op jit(solution)/shard_map/ppermute | solution.py:73
  2.7 1.6 %shard_map.128 = (bf16[4,64,128]{2,1,0:T(8,128)(2,1)}, bf16[4,64,128]{2,1,0:T(8,128)(2,1)}) custom-call(bf16[16,64,128]{2,1,0:T(8,128)(2,1)} %bitcast.11, bf16[16,64,128]{2,1,0:T(8,128)(2,1)} %bitcast.20, bf16[16,64,128]{2,1,0:T(8,128)(2,1)} %bitcast.24, bf16[16,64,128]{2,1,0:T(8,128)(2,1)} %bitcast.17), custom_call_target="tpu_custom_call" | custom-call | flops 1 | bytes 1179648 | tf_op jit(solution)/shard_map/pallas_call | solution.py:38
  4.4 1.0 %collective-permute-start.1 = (bf16[4,64,128]{2,1,0:T(8,128)(2,1)}, bf16[4,64,128]{2,1,0:T(8,128)(2,1)S(1)}, u32[]{:S(2)}, u32[]{:S(2)}) collective-permute-start(bf16[4,64,128]{2,1,0:T(8,128)(2,1)} %get-tuple-element.36), channel_id=1, source_target_pairs={{8,0},{0,8},{24,16},{16,24},{9,1},{1,9},{25,17},{17,25},{10,2},{2,... | collective-permute-start | bytes 196616 | tf_op jit(solution)/shard_map/ppermute | solution.py:73
  5.5 1.0 %collective-permute-done.1.refs_5_ = bf16[4,64,128]{2,1,0:T(8,128)(2,1)S(1)} collective-permute-done((bf16[4,64,128]{2,1,0:T(8,128)(2,1)}, bf16[4,64,128]{2,1,0:T(8,128)(2,1)S(1)}, u32[]{:S(2)}, u32[]{:S(2)}) %collective-permute-start.1) | collective-permute-done | bytes 65568 | tf_op jit(solution)/shard_map/ppermute | solution.py:73
  6.5 1.2 %collective-permute-start.2 = (bf16[4,64,128]{2,1,0:T(8,128)(2,1)S(1)}, bf16[4,64,128]{2,1,0:T(8,128)(2,1)S(1)}, u32[]{:S(2)}, u32[]{:S(2)}) collective-permute-start(bf16[4,64,128]{2,1,0:T(8,128)(2,1)S(1)} %collective-permute-done.1.refs_5_), channel_id=1, source_target_pairs={{16,0},{24,8},{0,16},{8,24},{17,1},{25,9},{1,17},{9,25},{18,2},{26... | collective-permute-start | bytes 196616 | tf_op jit(solution)/shard_map/ppermute | solution.py:73
  7.8 1.3 %collective-permute-start.4 = (bf16[14,64,128]{2,1,0:T(8,128)(2,1)S(1)}, bf16[14,64,128]{2,1,0:T(8,128)(2,1)S(1)}, u32[]{:S(2)}, u32[]{:S(2)}) collective-permute-start(bf16[14,64,128]{2,1,0:T(8,128)(2,1)S(1)} %get-tuple-element.37.refs_5_), channel_id=1, source_target_pairs={{4,0},{0,4},{5,1},{1,5},{6,2},{2,6},{7,3},{3,7},{12,8},{8,12},{13,... | collective-permute-start | bytes 688136 | tf_op jit(solution)/shard_map/ppermute | solution.py:73
  9.1 1.0 %shard_map.130 = (bf16[14,64,128]{2,1,0:T(8,128)(2,1)S(1)}, bf16[16,64,128]{2,1,0:T(8,128)(2,1)S(1)}) custom-call(bf16[16,64,128]{2,1,0:T(8,128)(2,1)S(1)} %bitcast.13, bf16[16,64,128]{2,1,0:T(8,128)(2,1)S(1)} %bitcast.22, bf16[16,64,128]{2,1,0:T(8,128)(2,1)S(1)} %collective-permute-done.3.refs_2_.refs_6_, bf16[3,128,128]{2,1,0:T(8,128)(2,1)S(1)} %copy-done.6, ...), custom_call_target="tpu_custom_call" | custom-call | flops 362387872 | bytes 2162688 | tf_op jit(solution)/shard_map/pallas_call | solution.py:38
  10.2 0.7 %shard_map.132 = (f32[4,384,128]{2,1,0:T(8,128)S(1)}, bf16[768,128]{1,0:T(8,128)(2,1)S(1)}, bf16[768,128]{1,0:T(8,128)(2,1)S(1)}) custom-call(bf16[16,64,128]{2,1,0:T(8,128)(2,1)S(1)} %bitcast.26, bf16[16,64,128]{2,1,0:T(8,128)(2,1)S(1)} %bitcast.23, bf16[16,64,128]{2,1,0:T(8,128)(2,1)S(1)} %get-tuple-element.40.refs_6_.refs_2_.refs_4_, ...), custom_call_target="tpu_custom_call" | custom-call | flops 362387872 | bytes 2621440 | tf_op jit(solution)/shard_map/pallas_call | solution.py:38
  10.9 1.2 %collective-permute-start.6 = (bf16[768,128]{1,0:T(8,128)(2,1)S(1)}, bf16[768,128]{1,0:T(8,128)(2,1)S(1)}, u32[]{:S(2)}, u32[]{:S(2)}) collective-permute-start(bf16[768,128]{1,0:T(8,128)(2,1)S(1)} %get-tuple-element.42), channel_id=1, source_target_pairs={{8,0},{0,8},{24,16},{16,24},{9,1},{1,9},{25,17},{17,25},{10,2},{2,... | collective-permute-start | bytes 589832 | tf_op jit(solution)/shard_map/ppermute | solution.py:73
  12.2 0.9 %collective-permute-start.5 = (bf16[4,64,128]{2,1,0:T(8,128)(2,1)S(1)}, bf16[4,64,128]{2,1,0:T(8,128)(2,1)S(1)}, u32[]{:S(2)}, u32[]{:S(2)}) collective-permute-start(bf16[4,64,128]{2,1,0:T(8,128)(2,1)S(1)} %shard_map.131.refs_7_), channel_id=1, source_target_pairs={{4,0},{0,4},{5,1},{1,5},{6,2},{2,6},{7,3},{3,7},{12,8},{8,12},{13,... | collective-permute-start | bytes 196616 | tf_op jit(solution)/shard_map/ppermute | solution.py:73
  13.4 0.9 %collective-permute-done.4.refs_3_.refs_5_ = bf16[14,64,128]{2,1,0:T(8,128)(2,1)S(1)} collective-permute-done((bf16[14,64,128]{2,1,0:T(8,128)(2,1)S(1)}, bf16[14,64,128]{2,1,0:T(8,128)(2,1)S(1)}, u32[]{:S(2)}, u32[]{:S(2)}) %collective-permute-start.4) | collective-permute-done | bytes 229408 | tf_op jit(solution)/shard_map/ppermute | solution.py:73
  14.5 3.2 %collective-permute-start.8 = (bf16[768,128]{1,0:T(8,128)(2,1)S(1)}, bf16[768,128]{1,0:T(8,128)(2,1)S(1)}, u32[]{:S(2)}, u32[]{:S(2)}) collective-permute-start(bf16[768,128]{1,0:T(8,128)(2,1)S(1)} %get-tuple-element.48), channel_id=1, source_target_pairs={{24,8},{25,9},{26,10},{27,11},{28,12},{29,13},{30,14},{31,15},{8,2... | collective-permute-start | bytes 589832 | tf_op jit(solution)/shard_map/ppermute | solution.py:92
  17.7 1.6 %shard_map.135 = (bf16[16,64,128]{2,1,0:T(8,128)(2,1)S(1)}, bf16[16,64,128]{2,1,0:T(8,128)(2,1)S(1)}, f32[2,384,128]{2,1,0:T(8,128)S(1)}, bf16[896,128]{1,0:T(8,128)(2,1)S(1)}) custom-call(bf16[16,64,128]{2,1,0:T(8,128)(2,1)S(1)} %bitcast.16, bf16[4,64,128]{2,1,0:T(8,128)(2,1)S(1)} %collective-permute-done.refs_4_.refs_1_.refs_3_.refs_2_, ...), custom_call_target="tpu_custom_call" | custom-call | flops 2415919104 | bytes 4128768 | tf_op jit(solution)/shard_map/pallas_call | solution.py:38
  19.3 1.7 %collective-permute-done.8.refs_1_ = bf16[768,128]{1,0:T(8,128)(2,1)S(1)} collective-permute-done((bf16[768,128]{1,0:T(8,128)(2,1)S(1)}, bf16[768,128]{1,0:T(8,128)(2,1)S(1)}, u32[]{:S(2)}, u32[]{:S(2)}) %collective-permute-start.8) | collective-permute-done | bytes 196640 | tf_op jit(solution)/shard_map/ppermute | solution.py:92
  20.9 1.5 %collective-permute-done.9.refs_1_.refs_2_ = bf16[896,128]{1,0:T(8,128)(2,1)S(1)} collective-permute-done((bf16[896,128]{1,0:T(8,128)(2,1)S(1)}, bf16[896,128]{1,0:T(8,128)(2,1)S(1)}, u32[]{:S(2)}, u32[]{:S(2)}) %collective-permute-start.9) | collective-permute-done | bytes 229408 | tf_op jit(solution)/shard_map/ppermute | solution.py:73
  22.5 3.2 %collective-permute-start.15 = (bf16[2,192,128]{2,1,0:T(8,128)(2,1)S(1)}, bf16[2,192,128]{2,1,0:T(8,128)(2,1)S(1)}, u32[]{:S(2)}, u32[]{:S(2)}) collective-permute-start(bf16[2,192,128]{2,1,0:T(8,128)(2,1)S(1)} %get-tuple-element.57), channel_id=1, source_target_pairs={{12,8},{13,9},{14,10},{15,11},{8,12},{9,13},{10,14},{11,15},{28,24... | collective-permute-start | bytes 294920 | tf_op jit(solution)/shard_map/ppermute | solution.py:92
  25.7 1.5 %collective-permute-start.10 = (bf16[256,128]{1,0:T(8,128)(2,1)S(1)}, bf16[256,128]{1,0:T(8,128)(2,1)S(1)}, u32[]{:S(2)}, u32[]{:S(2)}) collective-permute-start(bf16[256,128]{1,0:T(8,128)(2,1)S(1)} %get-tuple-element.51), channel_id=1, source_target_pairs={{16,0},{24,8},{0,16},{8,24},{17,1},{25,9},{1,17},{9,25},{18,2},{26... | collective-permute-start | bytes 196616 | tf_op jit(solution)/shard_map/ppermute | solution.py:73
  27.2 1.2 %collective-permute-start.12 = (bf16[192,128]{1,0:T(8,128)(2,1)S(1)}, bf16[192,128]{1,0:T(8,128)(2,1)S(1)}, u32[]{:S(2)}, u32[]{:S(2)}) collective-permute-start(bf16[192,128]{1,0:T(8,128)(2,1)S(1)} %get-tuple-element.54.refs_2_), channel_id=1, source_target_pairs={{20,0},{16,4},{28,8},{24,12},{4,16},{0,20},{12,24},{8,28},{21,1},{... | collective-permute-start | bytes 147464 | tf_op jit(solution)/shard_map/ppermute | solution.py:100
  28.5 1.8 %collective-permute-done.11.refs_2_ = bf16[192,128]{1,0:T(8,128)(2,1)S(1)} collective-permute-done((bf16[192,128]{1,0:T(8,128)(2,1)S(1)}, bf16[192,128]{1,0:T(8,128)(2,1)S(1)}, u32[]{:S(2)}, u32[]{:S(2)}) %collective-permute-start.11) | collective-permute-done | bytes 49184 | tf_op jit(solution)/shard_map/ppermute | solution.py:73
  30.3 1.3 %collective-permute-done.12.refs_3_ = bf16[192,128]{1,0:T(8,128)(2,1)S(1)} collective-permute-done((bf16[192,128]{1,0:T(8,128)(2,1)S(1)}, bf16[192,128]{1,0:T(8,128)(2,1)S(1)}, u32[]{:S(2)}, u32[]{:S(2)}) %collective-permute-start.12) | collective-permute-done | bytes 49184 | tf_op jit(solution)/shard_map/ppermute | solution.py:100
  31.7 2.8 %collective-permute-start.16 = (bf16[2,192,128]{2,1,0:T(8,128)(2,1)S(1)}, bf16[2,192,128]{2,1,0:T(8,128)(2,1)S(1)}, u32[]{:S(2)}, u32[]{:S(2)}) collective-permute-start(bf16[2,192,128]{2,1,0:T(8,128)(2,1)S(1)} %shard_map.141.refs_0_), channel_id=1, source_target_pairs={{9,8},{8,9},{11,10},{10,11},{13,12},{12,13},{15,14},{14,15},{25,24... | collective-permute-start | bytes 294920 | tf_op jit(solution)/shard_map/ppermute | solution.py:92
  35.2 2.7 %collective-permute-done.13.refs_1_ = bf16[192,128]{1,0:T(8,128)(2,1)S(1)} collective-permute-done((bf16[192,128]{1,0:T(8,128)(2,1)S(1)}, bf16[192,128]{1,0:T(8,128)(2,1)S(1)}, u32[]{:S(2)}, u32[]{:S(2)}) %collective-permute-start.13) | collective-permute-done | bytes 49184 | tf_op jit(solution)/shard_map/ppermute | solution.py:73
  37.9 4.0 %collective-permute-start.17 = (bf16[2,192,128]{2,1,0:T(8,128)(2,1)S(1)}, bf16[2,192,128]{2,1,0:T(8,128)(2,1)S(1)}, u32[]{:S(2)}, u32[]{:S(2)}) collective-permute-start(bf16[2,192,128]{2,1,0:T(8,128)(2,1)S(1)} %shard_map.142.refs_0_), channel_id=1, source_target_pairs={{10,8},{11,9},{8,10},{9,11},{14,12},{15,13},{12,14},{13,15},{26,24... | collective-permute-start | bytes 294920 | tf_op jit(solution)/shard_map/ppermute | solution.py:92
  42.4 3.0 %collective-permute-done.17.refs_1_ = bf16[2,192,128]{2,1,0:T(8,128)(2,1)S(1)} collective-permute-done((bf16[2,192,128]{2,1,0:T(8,128)(2,1)S(1)}, bf16[2,192,128]{2,1,0:T(8,128)(2,1)S(1)}, u32[]{:S(2)}, u32[]{:S(2)}) %collective-permute-start.17) | collective-permute-done | bytes 98336 | tf_op jit(solution)/shard_map/ppermute | solution.py:92
  45.5 1.5 %shard_map.139 = (bf16[16,64,128]{2,1,0:T(8,128)(2,1)}, f32[8,128]{1,0:T(8,128)S(1)}) custom-call(bf16[16,64,128]{2,1,0:T(8,128)(2,1)S(1)} %get-tuple-element.45.refs_0_, bf16[16,64,128]{2,1,0:T(8,128)(2,1)S(1)} %get-tuple-element.46.refs_1_, bf16[896,128]{1,0:T(8,128)(2,1)S(1)} %collective-permute-done.9.refs_1_.refs_2_, ...), custom_call_target="tpu_custom_call" | custom-call | flops 301989888 | bytes 1380352 | tf_op jit(solution)/shard_map/pallas_call | solution.py:38
  47.0 0.8 %collective-permute-start.23 = (bf16[2,192,128]{2,1,0:T(8,128)(2,1)S(1)}, bf16[2,192,128]{2,1,0:T(8,128)(2,1)S(1)}, u32[]{:S(2)}, u32[]{:S(2)}) collective-permute-start(bf16[2,192,128]{2,1,0:T(8,128)(2,1)S(1)} %shard_map.144.refs_0_), channel_id=1, source_target_pairs={{20,0},{16,4},{28,8},{24,12},{4,16},{0,20},{12,24},{8,28},{21,1},{... | collective-permute-start | bytes 294920 | tf_op jit(solution)/shard_map/ppermute | solution.py:100
  47.8 1.2 %collective-permute-start.22 = (bf16[2,192,128]{2,1,0:T(8,128)(2,1)S(1)}, bf16[2,192,128]{2,1,0:T(8,128)(2,1)S(1)}, u32[]{:S(2)}, u32[]{:S(2)}) collective-permute-start(bf16[2,192,128]{2,1,0:T(8,128)(2,1)S(1)} %shard_map.144.refs_0_), channel_id=1, source_target_pairs={{16,0},{24,8},{0,16},{8,24},{17,1},{25,9},{1,17},{9,25},{18,2},{26... | collective-permute-start | bytes 294920 | tf_op jit(solution)/shard_map/ppermute | solution.py:73
  49.7 1.3 %collective-permute-start.20 = (bf16[2,192,128]{2,1,0:T(8,128)(2,1)S(1)}, bf16[2,192,128]{2,1,0:T(8,128)(2,1)S(1)}, u32[]{:S(2)}, u32[]{:S(2)}) collective-permute-start(bf16[2,192,128]{2,1,0:T(8,128)(2,1)S(1)} %shard_map.144.refs_0_), channel_id=1, source_target_pairs={{8,0},{0,8},{24,16},{16,24},{9,1},{1,9},{25,17},{17,25},{10,2},{2,... | collective-permute-start | bytes 294920 | tf_op jit(solution)/shard_map/ppermute | solution.py:73
  51.1 0.8 %collective-permute-done.23.refs_5_ = bf16[2,192,128]{2,1,0:T(8,128)(2,1)S(1)} collective-permute-done((bf16[2,192,128]{2,1,0:T(8,128)(2,1)S(1)}, bf16[2,192,128]{2,1,0:T(8,128)(2,1)S(1)}, u32[]{:S(2)}, u32[]{:S(2)}) %collective-permute-start.23) | collective-permute-done | bytes 98336 | tf_op jit(solution)/shard_map/ppermute | solution.py:100
  51.9 2.3 %collective-permute-start.25 = (bf16[2,192,128]{2,1,0:T(8,128)(2,1)S(1)}, bf16[2,192,128]{2,1,0:T(8,128)(2,1)S(1)}, u32[]{:S(2)}, u32[]{:S(2)}) collective-permute-start(bf16[2,192,128]{2,1,0:T(8,128)(2,1)S(1)} %collective-permute-done.23.refs_5_), channel_id=1, source_target_pairs={{8,0},{0,8},{24,16},{16,24},{9,1},{1,9},{25,17},{17,25},{10,2},{2,... | collective-permute-start | bytes 294920 | tf_op jit(solution)/shard_map/ppermute | solution.py:73
  55.1 0.9 %collective-permute-done.24.refs_6_ = bf16[2,192,128]{2,1,0:T(8,128)(2,1)S(1)} collective-permute-done((bf16[2,192,128]{2,1,0:T(8,128)(2,1)S(1)}, bf16[2,192,128]{2,1,0:T(8,128)(2,1)S(1)}, u32[]{:S(2)}, u32[]{:S(2)}) %collective-permute-start.24) | collective-permute-done | bytes 98336 | tf_op jit(solution)/shard_map/ppermute | solution.py:73
  56.4 1.3 %shard_map.145 = (f32[3,384,128]{2,1,0:T(8,128)}, f32[384,128]{1,0:T(8,128)}, f32[3,384,128]{2,1,0:T(8,128)}, f32[384,128]{1,0:T(8,128)}) custom-call(bf16[2,192,128]{2,1,0:T(8,128)(2,1)S(1)} %shard_map.144.refs_0_, bf16[2,192,128]{2,1,0:T(8,128)(2,1)S(1)} %collective-permute-done.19.refs_1_, bf16[2,192,128]{2,1,0:T(8,128)(2,1)S(1)} %collective-permute-done.20.refs_2_, ...), custom_call_target="tpu_custom_call" | custom-call | flops 196608 | bytes 2359296 | tf_op jit(solution)/shard_map/pallas_call | solution.py:38
  (56 shorter events, 4.2 us)
Async XLA Ops:
  0.6 8.5 %collective-permute-start.3 = (bf16[16,64,128]{2,1,0:T(8,128)(2,1)}, bf16[16,64,128]{2,1,0:T(8,128)(2,1)S(1)}, u32[]{:S(2)}, u32[]{:S(2)}) collective-permute-start(bf16[16,64,128]{2,1,0:T(8,128)(2,1)} %bitcast.10), channel_id=1, source_target_pairs={{4,0},{0,4},{5,1},{1,5},{6,2},{2,6},{7,3},{3,7},{12,8},{8,12},{13,... | collective-permute-start | bytes 786440 | tf_op jit(solution)/shard_map/ppermute | solution.py:73
  2.7 5.0 %copy-start = (bf16[1,1,16,64,128]{4,3,2,1,0:T(8,128)(2,1)S(1)}, bf16[1,1,16,64,128]{4,3,2,1,0:T(8,128)(2,1)}, u32[]{:S(2)}) copy-start(bf16[1,1,16,64,128]{4,3,2,1,0:T(8,128)(2,1)} %param.9) | copy-start | bytes 786436
  2.7 5.0 %copy-start.2 = (bf16[1,1,16,64,128]{4,3,2,1,0:T(8,128)(2,1)S(1)}, bf16[1,1,16,64,128]{4,3,2,1,0:T(8,128)(2,1)}, u32[]{:S(2)}) copy-start(bf16[1,1,16,64,128]{4,3,2,1,0:T(8,128)(2,1)} %param.13) | copy-start | bytes 786436
  2.7 5.0 %copy-start.4 = (bf16[3,3,128,128]{3,2,1,0:T(8,128)(2,1)S(1)}, bf16[3,3,128,128]{3,2,1,0:T(8,128)(2,1)}, u32[]{:S(2)}) copy-start(bf16[3,3,128,128]{3,2,1,0:T(8,128)(2,1)} %refs_8_.1) | copy-start | bytes 884740
  2.7 5.0 %copy-start.6 = (bf16[3,128,128]{2,1,0:T(8,128)(2,1)S(1)}, bf16[3,128,128]{2,1,0:T(8,128)(2,1)}, u32[]{:S(2)}) copy-start(bf16[3,128,128]{2,1,0:T(8,128)(2,1)} %refs_7_.1) | copy-start | bytes 294916
  4.4 2.1 %collective-permute-start.1 = (bf16[4,64,128]{2,1,0:T(8,128)(2,1)}, bf16[4,64,128]{2,1,0:T(8,128)(2,1)S(1)}, u32[]{:S(2)}, u32[]{:S(2)}) collective-permute-start(bf16[4,64,128]{2,1,0:T(8,128)(2,1)} %get-tuple-element.36), channel_id=1, source_target_pairs={{8,0},{0,8},{24,16},{16,24},{9,1},{1,9},{25,17},{17,25},{10,2},{2,... | collective-permute-start | bytes 196616 | tf_op jit(solution)/shard_map/ppermute | solution.py:73
  5.4 3.7 %copy-start.8 = (bf16[3,128,128]{2,1,0:T(8,128)(2,1)S(1)}, bf16[3,128,128]{2,1,0:T(8,128)(2,1)}, u32[]{:S(2)}) copy-start(bf16[3,128,128]{2,1,0:T(8,128)(2,1)} %refs_11_.1) | copy-start | bytes 294916
  5.4 2.3 %collective-permute-start = (bf16[4,64,128]{2,1,0:T(8,128)(2,1)}, bf16[4,64,128]{2,1,0:T(8,128)(2,1)S(1)}, u32[]{:S(2)}, u32[]{:S(2)}) collective-permute-start(bf16[4,64,128]{2,1,0:T(8,128)(2,1)} %get-tuple-element.35), channel_id=1, source_target_pairs={{8,0},{0,8},{24,16},{16,24},{9,1},{1,9},{25,17},{17,25},{10,2},{2,... | collective-permute-start | bytes 196616 | tf_op jit(solution)/shard_map/ppermute | solution.py:73
  6.5 3.6 %collective-permute-start.2 = (bf16[4,64,128]{2,1,0:T(8,128)(2,1)S(1)}, bf16[4,64,128]{2,1,0:T(8,128)(2,1)S(1)}, u32[]{:S(2)}, u32[]{:S(2)}) collective-permute-start(bf16[4,64,128]{2,1,0:T(8,128)(2,1)S(1)} %collective-permute-done.1.refs_5_), channel_id=1, source_target_pairs={{16,0},{24,8},{0,16},{8,24},{17,1},{25,9},{1,17},{9,25},{18,2},{26... | collective-permute-start | bytes 196616 | tf_op jit(solution)/shard_map/ppermute | solution.py:73
  7.8 6.6 %collective-permute-start.4 = (bf16[14,64,128]{2,1,0:T(8,128)(2,1)S(1)}, bf16[14,64,128]{2,1,0:T(8,128)(2,1)S(1)}, u32[]{:S(2)}, u32[]{:S(2)}) collective-permute-start(bf16[14,64,128]{2,1,0:T(8,128)(2,1)S(1)} %get-tuple-element.37.refs_5_), channel_id=1, source_target_pairs={{4,0},{0,4},{5,1},{1,5},{6,2},{2,6},{7,3},{3,7},{12,8},{8,12},{13,... | collective-permute-start | bytes 688136 | tf_op jit(solution)/shard_map/ppermute | solution.py:73
  10.9 3.5 %collective-permute-start.6 = (bf16[768,128]{1,0:T(8,128)(2,1)S(1)}, bf16[768,128]{1,0:T(8,128)(2,1)S(1)}, u32[]{:S(2)}, u32[]{:S(2)}) collective-permute-start(bf16[768,128]{1,0:T(8,128)(2,1)S(1)} %get-tuple-element.42), channel_id=1, source_target_pairs={{8,0},{0,8},{24,16},{16,24},{9,1},{1,9},{25,17},{17,25},{10,2},{2,... | collective-permute-start | bytes 589832 | tf_op jit(solution)/shard_map/ppermute | solution.py:73
  12.1 2.3 %collective-permute-start.7 = (bf16[768,128]{1,0:T(8,128)(2,1)S(1)}, bf16[768,128]{1,0:T(8,128)(2,1)S(1)}, u32[]{:S(2)}, u32[]{:S(2)}) collective-permute-start(bf16[768,128]{1,0:T(8,128)(2,1)S(1)} %get-tuple-element.43), channel_id=1, source_target_pairs={{8,0},{0,8},{24,16},{16,24},{9,1},{1,9},{25,17},{17,25},{10,2},{2,... | collective-permute-start | bytes 589832 | tf_op jit(solution)/shard_map/ppermute | solution.py:73
  12.2 5.5 %collective-permute-start.5 = (bf16[4,64,128]{2,1,0:T(8,128)(2,1)S(1)}, bf16[4,64,128]{2,1,0:T(8,128)(2,1)S(1)}, u32[]{:S(2)}, u32[]{:S(2)}) collective-permute-start(bf16[4,64,128]{2,1,0:T(8,128)(2,1)S(1)} %shard_map.131.refs_7_), channel_id=1, source_target_pairs={{4,0},{0,4},{5,1},{1,5},{6,2},{2,6},{7,3},{3,7},{12,8},{8,12},{13,... | collective-permute-start | bytes 196616 | tf_op jit(solution)/shard_map/ppermute | solution.py:73
  14.5 6.4 %collective-permute-start.8 = (bf16[768,128]{1,0:T(8,128)(2,1)S(1)}, bf16[768,128]{1,0:T(8,128)(2,1)S(1)}, u32[]{:S(2)}, u32[]{:S(2)}) collective-permute-start(bf16[768,128]{1,0:T(8,128)(2,1)S(1)} %get-tuple-element.48), channel_id=1, source_target_pairs={{24,8},{25,9},{26,10},{27,11},{28,12},{29,13},{30,14},{31,15},{8,2... | collective-permute-start | bytes 589832 | tf_op jit(solution)/shard_map/ppermute | solution.py:92
  20.9 1.5 %collective-permute-start.9 = (bf16[896,128]{1,0:T(8,128)(2,1)S(1)}, bf16[896,128]{1,0:T(8,128)(2,1)S(1)}, u32[]{:S(2)}, u32[]{:S(2)}) collective-permute-start(bf16[896,128]{1,0:T(8,128)(2,1)S(1)} %get-tuple-element.49), channel_id=1, source_target_pairs={{8,0},{0,8},{24,16},{16,24},{9,1},{1,9},{25,17},{17,25},{10,2},{2,... | collective-permute-start | bytes 688136 | tf_op jit(solution)/shard_map/ppermute | solution.py:73
  22.5 9.1 %collective-permute-start.15 = (bf16[2,192,128]{2,1,0:T(8,128)(2,1)S(1)}, bf16[2,192,128]{2,1,0:T(8,128)(2,1)S(1)}, u32[]{:S(2)}, u32[]{:S(2)}) collective-permute-start(bf16[2,192,128]{2,1,0:T(8,128)(2,1)S(1)} %get-tuple-element.57), channel_id=1, source_target_pairs={{12,8},{13,9},{14,10},{15,11},{8,12},{9,13},{10,14},{11,15},{28,24... | collective-permute-start | bytes 294920 | tf_op jit(solution)/shard_map/ppermute | solution.py:92
  25.7 5.9 %collective-permute-start.10 = (bf16[256,128]{1,0:T(8,128)(2,1)S(1)}, bf16[256,128]{1,0:T(8,128)(2,1)S(1)}, u32[]{:S(2)}, u32[]{:S(2)}) collective-permute-start(bf16[256,128]{1,0:T(8,128)(2,1)S(1)} %get-tuple-element.51), channel_id=1, source_target_pairs={{16,0},{24,8},{0,16},{8,24},{17,1},{25,9},{1,17},{9,25},{18,2},{26... | collective-permute-start | bytes 196616 | tf_op jit(solution)/shard_map/ppermute | solution.py:73
  27.2 3.1 %collective-permute-start.11 = (bf16[192,128]{1,0:T(8,128)(2,1)S(1)}, bf16[192,128]{1,0:T(8,128)(2,1)S(1)}, u32[]{:S(2)}, u32[]{:S(2)}) collective-permute-start(bf16[192,128]{1,0:T(8,128)(2,1)S(1)} %get-tuple-element.53), channel_id=1, source_target_pairs={{4,0},{0,4},{5,1},{1,5},{6,2},{2,6},{7,3},{3,7},{12,8},{8,12},{13,... | collective-permute-start | bytes 147464 | tf_op jit(solution)/shard_map/ppermute | solution.py:73
  27.2 4.4 %collective-permute-start.12 = (bf16[192,128]{1,0:T(8,128)(2,1)S(1)}, bf16[192,128]{1,0:T(8,128)(2,1)S(1)}, u32[]{:S(2)}, u32[]{:S(2)}) collective-permute-start(bf16[192,128]{1,0:T(8,128)(2,1)S(1)} %get-tuple-element.54.refs_2_), channel_id=1, source_target_pairs={{20,0},{16,4},{28,8},{24,12},{4,16},{0,20},{12,24},{8,28},{21,1},{... | collective-permute-start | bytes 147464 | tf_op jit(solution)/shard_map/ppermute | solution.py:100
  31.7 6.1 %collective-permute-start.16 = (bf16[2,192,128]{2,1,0:T(8,128)(2,1)S(1)}, bf16[2,192,128]{2,1,0:T(8,128)(2,1)S(1)}, u32[]{:S(2)}, u32[]{:S(2)}) collective-permute-start(bf16[2,192,128]{2,1,0:T(8,128)(2,1)S(1)} %shard_map.141.refs_0_), channel_id=1, source_target_pairs={{9,8},{8,9},{11,10},{10,11},{13,12},{12,13},{15,14},{14,15},{25,24... | collective-permute-start | bytes 294920 | tf_op jit(solution)/shard_map/ppermute | solution.py:92
  34.5 3.3 %collective-permute-start.13 = (bf16[192,128]{1,0:T(8,128)(2,1)S(1)}, bf16[192,128]{1,0:T(8,128)(2,1)S(1)}, u32[]{:S(2)}, u32[]{:S(2)}) collective-permute-start(bf16[192,128]{1,0:T(8,128)(2,1)S(1)} %shard_map.137.refs_0_.refs_2_), channel_id=1, source_target_pairs={{1,0},{0,1},{3,2},{2,3},{5,4},{4,5},{7,6},{6,7},{9,8},{8,9},{11,10... | collective-permute-start | bytes 147464 | tf_op jit(solution)/shard_map/ppermute | solution.py:73
  37.8 7.6 %copy-start.7 = (bf16[3,3,128,128]{3,2,1,0:T(8,128)(2,1)S(1)}, bf16[3,3,128,128]{3,2,1,0:T(8,128)(2,1)}, u32[]{:S(2)}) copy-start(bf16[3,3,128,128]{3,2,1,0:T(8,128)(2,1)} %refs_4_.5) | copy-start | bytes 884740
  37.9 7.4 %collective-permute-start.17 = (bf16[2,192,128]{2,1,0:T(8,128)(2,1)S(1)}, bf16[2,192,128]{2,1,0:T(8,128)(2,1)S(1)}, u32[]{:S(2)}, u32[]{:S(2)}) collective-permute-start(bf16[2,192,128]{2,1,0:T(8,128)(2,1)S(1)} %shard_map.142.refs_0_), channel_id=1, source_target_pairs={{10,8},{11,9},{8,10},{9,11},{14,12},{15,13},{12,14},{13,15},{26,24... | collective-permute-start | bytes 294920 | tf_op jit(solution)/shard_map/ppermute | solution.py:92
  41.9 5.0 %collective-permute-start.14 = (bf16[192,128]{1,0:T(8,128)(2,1)S(1)}, bf16[192,128]{1,0:T(8,128)(2,1)S(1)}, u32[]{:S(2)}, u32[]{:S(2)}) collective-permute-start(bf16[192,128]{1,0:T(8,128)(2,1)S(1)} %shard_map.138.refs_5_.refs_2_.refs_0_), channel_id=1, source_target_pairs={{2,0},{3,1},{0,2},{1,3},{6,4},{7,5},{4,6},{5,7},{10,8},{11,9},{8,1... | collective-permute-start | bytes 147464 | tf_op jit(solution)/shard_map/ppermute | solution.py:73
  45.4 1.6 %collective-permute-start.18 = (bf16[192,128]{1,0:T(8,128)(2,1)S(1)}, bf16[192,128]{1,0:T(8,128)(2,1)S(1)}, u32[]{:S(2)}, u32[]{:S(2)}) collective-permute-start(bf16[192,128]{1,0:T(8,128)(2,1)S(1)} %get-tuple-element.59), channel_id=1, source_target_pairs={{8,0},{0,8},{24,16},{16,24},{9,1},{1,9},{25,17},{17,25},{10,2},{2,... | collective-permute-start | bytes 147464 | tf_op jit(solution)/shard_map/ppermute | solution.py:73
  47.0 4.9 %collective-permute-start.23 = (bf16[2,192,128]{2,1,0:T(8,128)(2,1)S(1)}, bf16[2,192,128]{2,1,0:T(8,128)(2,1)S(1)}, u32[]{:S(2)}, u32[]{:S(2)}) collective-permute-start(bf16[2,192,128]{2,1,0:T(8,128)(2,1)S(1)} %shard_map.144.refs_0_), channel_id=1, source_target_pairs={{20,0},{16,4},{28,8},{24,12},{4,16},{0,20},{12,24},{8,28},{21,1},{... | collective-permute-start | bytes 294920 | tf_op jit(solution)/shard_map/ppermute | solution.py:100
  47.8 6.6 %collective-permute-start.22 = (bf16[2,192,128]{2,1,0:T(8,128)(2,1)S(1)}, bf16[2,192,128]{2,1,0:T(8,128)(2,1)S(1)}, u32[]{:S(2)}, u32[]{:S(2)}) collective-permute-start(bf16[2,192,128]{2,1,0:T(8,128)(2,1)S(1)} %shard_map.144.refs_0_), channel_id=1, source_target_pairs={{16,0},{24,8},{0,16},{8,24},{17,1},{25,9},{1,17},{9,25},{18,2},{26... | collective-permute-start | bytes 294920 | tf_op jit(solution)/shard_map/ppermute | solution.py:73
  49.0 6.1 %collective-permute-start.19 = (bf16[2,192,128]{2,1,0:T(8,128)(2,1)S(1)}, bf16[2,192,128]{2,1,0:T(8,128)(2,1)S(1)}, u32[]{:S(2)}, u32[]{:S(2)}) collective-permute-start(bf16[2,192,128]{2,1,0:T(8,128)(2,1)S(1)} %shard_map.144.refs_0_), channel_id=1, source_target_pairs={{4,0},{0,4},{5,1},{1,5},{6,2},{2,6},{7,3},{3,7},{12,8},{8,12},{13,... | collective-permute-start | bytes 294920 | tf_op jit(solution)/shard_map/ppermute | solution.py:73
  49.7 5.4 %collective-permute-start.20 = (bf16[2,192,128]{2,1,0:T(8,128)(2,1)S(1)}, bf16[2,192,128]{2,1,0:T(8,128)(2,1)S(1)}, u32[]{:S(2)}, u32[]{:S(2)}) collective-permute-start(bf16[2,192,128]{2,1,0:T(8,128)(2,1)S(1)} %shard_map.144.refs_0_), channel_id=1, source_target_pairs={{8,0},{0,8},{24,16},{16,24},{9,1},{1,9},{25,17},{17,25},{10,2},{2,... | collective-permute-start | bytes 294920 | tf_op jit(solution)/shard_map/ppermute | solution.py:73
  51.9 3.2 %collective-permute-start.25 = (bf16[2,192,128]{2,1,0:T(8,128)(2,1)S(1)}, bf16[2,192,128]{2,1,0:T(8,128)(2,1)S(1)}, u32[]{:S(2)}, u32[]{:S(2)}) collective-permute-start(bf16[2,192,128]{2,1,0:T(8,128)(2,1)S(1)} %collective-permute-done.23.refs_5_), channel_id=1, source_target_pairs={{8,0},{0,8},{24,16},{16,24},{9,1},{1,9},{25,17},{17,25},{10,2},{2,... | collective-permute-start | bytes 294920 | tf_op jit(solution)/shard_map/ppermute | solution.py:73
  54.5 1.6 %collective-permute-start.24 = (bf16[2,192,128]{2,1,0:T(8,128)(2,1)S(1)}, bf16[2,192,128]{2,1,0:T(8,128)(2,1)S(1)}, u32[]{:S(2)}, u32[]{:S(2)}) collective-permute-start(bf16[2,192,128]{2,1,0:T(8,128)(2,1)S(1)} %collective-permute-done.22.refs_4_), channel_id=1, source_target_pairs={{8,0},{0,8},{24,16},{16,24},{9,1},{1,9},{25,17},{17,25},{10,2},{2,... | collective-permute-start | bytes 294920 | tf_op jit(solution)/shard_map/ppermute | solution.py:73
  55.1 1.3 %collective-permute-start.21 = (bf16[2,192,128]{2,1,0:T(8,128)(2,1)S(1)}, bf16[2,192,128]{2,1,0:T(8,128)(2,1)S(1)}, u32[]{:S(2)}, u32[]{:S(2)}) collective-permute-start(bf16[2,192,128]{2,1,0:T(8,128)(2,1)S(1)} %collective-permute-done.19.refs_1_), channel_id=1, source_target_pairs={{8,0},{0,8},{24,16},{16,24},{9,1},{1,9},{25,17},{17,25},{10,2},{2,... | collective-permute-start | bytes 294920 | tf_op jit(solution)/shard_map/ppermute | solution.py:73
  (3 other events, 11.2 us)

commit v12 on v10

--- a/solution.py
+++ b/solution.py
@@ -156,12 +156,11 @@
         sums_ref[3, k * ch : (k + 1) * ch] = jnp.where(is_last(), zeros, value) if step else value
 
 
-def hand_out(sums_ref, keep_ref, send_ref):
+def hand_out(sums_ref, keep_ref, *send_refs):
     odd = lax.rem(lax.axis_index("section"), 2)
-    height = sums_ref.shape[1]
-    for n in range(2):
+    for n, send_ref in enumerate(send_refs):
         keep_ref[n] = sums_ref[2 * n + odd]
-        send_ref[n * height : (n + 1) * height] = sums_ref[2 * n + 1 - odd].astype(jnp.bfloat16)
+        send_ref[...] = sums_ref[2 * n + 1 - odd].astype(jnp.bfloat16)
 
 
 def pack_kernel(*refs):
@@ -263,8 +262,8 @@
 def two_kernel(later, *refs):
     saved_ref, preact_ref, gpre_ref = refs[:3]
     pair_refs, grad_ref = refs[3:5], refs[5]
-    wholes, outs = refs[6 : 6 + later], refs[6 + later : 8 + later]
-    views_ref, sides_ref, sums_ref = refs[8 + later :]
+    wholes, outs = refs[6 : 6 + later], refs[6 + later : 9 + later]
+    views_ref, sides_ref, sums_ref = refs[9 + later :]
     rows, cols, ch = saved_ref.shape
     step = 4
 
@@ -301,7 +300,8 @@
     send_ref[size + cols : size + 2 * cols] = gpre_ref[odd * (rows - 1)]
     views = views_ref[...].reshape(rows * cols, 3 * ch)
     kernel_sums(sides_ref, [ref[...] for ref in mids], views, sums_ref)
-    hand_out(sums_ref, keep_ref, send_ref)
+    height = sums_ref.shape[1]
+    hand_out(sums_ref, keep_ref, send_ref.at[:height], send_ref.at[height : 2 * height])
 
 
 def one_kernel(later, *refs):
@@ -357,11 +357,11 @@
     return [pl.ds(pl.multiple_of(n * count, count), count) for n in (index, 1 - index)]
 
 
-def pair_kernel(keep_ref, part_ref, own_ref, send_ref):
+def pair_kernel(keep_ref, low_ref, high_ref, own_ref, send_ref):
     across = lax.axis_index("section") // 2
-    mine, other = halves(own_ref.shape[0], across)
-    own_ref[...] = keep_ref[across] + part_ref[mine].astype(jnp.float32)
-    total = keep_ref[1 - across] + part_ref[other].astype(jnp.float32)
+    parts = [ref[...].astype(jnp.float32) for ref in (low_ref, high_ref)]
+    own_ref[...] = keep_ref[across] + jnp.where(across == 0, *parts)
+    total = keep_ref[1 - across] + jnp.where(across == 0, *parts[::-1])
     send_ref[...] = total.astype(jnp.bfloat16)
 
 
@@ -473,7 +473,7 @@
     act = pltpu.VMEM((rows, cols, ch), jnp.bfloat16)
     sides = bf16(4, ch, rows * cols)
     sums = pltpu.VMEM((4, 3 * ch, ch), jnp.float32)
-    handed = [f32(2, 3 * ch, ch), bf16(6 * ch, ch)]
+    handed = [f32(2, 3 * ch, ch)] + [bf16(3 * ch, ch)] * 2
     inner_outs = [bf16(rows - 2, cols, ch), bf16(rows, cols, ch)]
     kernels = (temporal_two, spatial_two)
 
@@ -504,7 +504,7 @@
             last_inner_kernel,
             inner_outs,
             [views],
-            1.2 * conv,
+            0.1 * conv,
             grad,
             pre_two,
             *kernels,
@@ -517,13 +517,13 @@
         functools.partial(inner_kernel, later),
         inner_outs,
         [views],
-        1.2 * conv,
+        0.1 * conv,
         grad,
         pre_two,
         *wholes,
         *kernels,
         *known,
-        early=(saved_two,),
+        early=(saved_two, saved_one, pre_one, temporal_one),
     )
     if frames == 2:
         edge = call(
@@ -550,21 +550,20 @@
         grad,
         *wholes,
         after=(edge,) if frames == 2 else (),
-        early=(saved_one, pre_one, temporal_one),
     )
     sides_one = call(
         sides_kernel, [sides], [], conv // 8, saved_one, pre_one, *pairs, after=parts_two[:1]
     )
     height, half = 3 * ch, 3 * ch // 2
-    keep_two, send_two = parts_two
+    keep_two, low_two, high_two = parts_two
     own_two, send_two = call(
         pair_kernel,
         [f32(height, ch), bf16(height, ch)],
         [],
         height * ch,
         keep_two,
-        flipped(send_two, "section", 1),
-        after=afters[:1] if frames == 2 else (),
+        flipped(low_two, "section", 1),
+        flipped(high_two, "section", 1),
     )
     across_two = flipped(send_two, "section", 2)
     mid_inputs = (grad, *pairs, inner, gpre_two)
@@ -576,7 +575,7 @@
             mid_one_kernel,
             mid_outs + one_outs,
             [views, sums, act, pltpu.VMEM((2, cols, ch), jnp.bfloat16), edge_views],
-            1.5 * conv,
+            8 * conv,
             *mid_inputs,
             *afters,
             *kernels,
@@ -667,7 +666,13 @@
         sums = placed(shares, [flipped(own, "section", 2), flipped_both(own)])
     else:
         own_one, send_one = call(
-            pair_kernel, [f32(height, ch), bf16(height, ch)], [], height * ch, keep_one, pair_one
+            pair_kernel,
+            [f32(height, ch), bf16(height, ch)],
+            [],
+            height * ch,
+            keep_one,
+            pair_one[:height],
+            pair_one[height : 2 * height],
         )
         edge = flipped(pair_one[pair_one.shape[0] - cols :], "section", 2)
         grad_in, _ = input_gradient(edge, ())

time: 50.8 us -> 50.2 us (0.988)
  waiting for transfers between devices: 4.98 us -> 7.01 us
  starting transfers between devices: 35.1 us -> 33.5 us
  local copies, waits for them, and re-layouts: 1.03 us -> 0.03 us
    ppermute x2, starting transfers between devices: 3.11 us -> 1.1 us  [flipped_both(): return lax.ppermute(block, ('section', 'video'), pairs)]
    ppermute x22 -> x23, waiting for transfers between devices: 4.32 us -> 5.9 us  [flipped(): lax.ppermute(block, axis, [(place ^ flip, place) for place in range(count)])]
    unnamed x18, local copies, waits for them, and re-layouts: 1.03 us -> 0.03 us
    ppermute x22 -> x23, starting transfers between devices: 32 us -> 32.4 us  [flipped(): lax.ppermute(block, axis, [(place ^ flip, place) for place in range(count)])]
  transfers between devices with their start and end apart: 24 -> 25, of which waited for: 8 -> 9; matrix products, arithmetic and copies ran while one was open for 0% -> 0% of each run, Pallas kernels for 14% -> 14%
where the time goes in v12:
time: 50.2 us; the launch traced here: 49.7 us
  starting transfers between devices  33.5 us (67%)
  Pallas kernels  8.42 us (17%)
  waiting for transfers between devices  7.01 us (14%)
  between operations  0.79 us (2%)
    ppermute x23, starting transfers between devices, flipped(): lax.ppermute(block, axis, [(place ^ flip, place) for place in range(count)])  32.4 us
    pallas_call x17, Pallas kernels, call(): pl.pallas_call(body, out_shape=outs[0] if single else tuple(outs), in_spe...  8.42 us
    ppermute x23, waiting for transfers between devices, flipped(): lax.ppermute(block, axis, [(place ^ flip, place) for place in range(count)])  5.9 us
    ppermute x2, waiting for transfers between devices, flipped_both(): return lax.ppermute(block, ('section', 'video'), pairs)  1.11 us
    ppermute x2, starting transfers between devices, flipped_both(): return lax.ppermute(block, ('section', 'video'), pairs)  1.1 us
  transfers between devices with their start and end apart: 25, of which 9 were waited for; matrix products, arithmetic and copies ran while one was open for 0% of the time, Pallas kernels for 14%

profile of v12, /device:TPU:1, one launch (start us, length us, event | category | flops | bytes accessed | tf_op | source)
XLA Modules:
  0.0 49.7 jit_solution(941422131515719237)
XLA Ops:
  0.6 2.1 %collective-permute-start.3 = (bf16[16,64,128]{2,1,0:T(8,128)(2,1)}, bf16[16,64,128]{2,1,0:T(8,128)(2,1)S(1)}, u32[]{:S(2)}, u32[]{:S(2)}) collective-permute-start(bf16[16,64,128]{2,1,0:T(8,128)(2,1)} %bitcast.10), channel_id=1, source_target_pairs={{4,0},{0,4},{5,1},{1,5},{6,2},{2,6},{7,3},{3,7},{12,8},{8,12},{13,... | collective-permute-start | bytes 786440 | tf_op jit(solution)/shard_map/ppermute | solution.py:73
  2.7 1.6 %shard_map.128 = (bf16[4,64,128]{2,1,0:T(8,128)(2,1)}, bf16[4,64,128]{2,1,0:T(8,128)(2,1)}) custom-call(bf16[16,64,128]{2,1,0:T(8,128)(2,1)} %bitcast.11, bf16[16,64,128]{2,1,0:T(8,128)(2,1)} %bitcast.17, bf16[16,64,128]{2,1,0:T(8,128)(2,1)} %bitcast.21, bf16[16,64,128]{2,1,0:T(8,128)(2,1)} %bitcast.24), custom_call_target="tpu_custom_call" | custom-call | flops 1 | bytes 1179648 | tf_op jit(solution)/shard_map/pallas_call | solution.py:38
  4.4 1.0 %collective-permute-start = (bf16[4,64,128]{2,1,0:T(8,128)(2,1)}, bf16[4,64,128]{2,1,0:T(8,128)(2,1)S(1)}, u32[]{:S(2)}, u32[]{:S(2)}) collective-permute-start(bf16[4,64,128]{2,1,0:T(8,128)(2,1)} %get-tuple-element.35), channel_id=1, source_target_pairs={{8,0},{0,8},{24,16},{16,24},{9,1},{1,9},{25,17},{17,25},{10,2},{2,... | collective-permute-start | bytes 196616 | tf_op jit(solution)/shard_map/ppermute | solution.py:73
  5.5 1.0 %collective-permute-done.refs_4_.refs_1_.refs_3_.refs_2_ = bf16[4,64,128]{2,1,0:T(8,128)(2,1)S(1)} collective-permute-done((bf16[4,64,128]{2,1,0:T(8,128)(2,1)}, bf16[4,64,128]{2,1,0:T(8,128)(2,1)S(1)}, u32[]{:S(2)}, u32[]{:S(2)}) %collective-permute-start) | collective-permute-done | bytes 65568 | tf_op jit(solution)/shard_map/ppermute | solution.py:73
  7.0 0.8 %collective-permute-start.4 = (bf16[14,64,128]{2,1,0:T(8,128)(2,1)S(1)}, bf16[14,64,128]{2,1,0:T(8,128)(2,1)S(1)}, u32[]{:S(2)}, u32[]{:S(2)}) collective-permute-start(bf16[14,64,128]{2,1,0:T(8,128)(2,1)S(1)} %get-tuple-element.37.refs_5_), channel_id=1, source_target_pairs={{4,0},{0,4},{5,1},{1,5},{6,2},{2,6},{7,3},{3,7},{12,8},{8,12},{13,... | collective-permute-start | bytes 688136 | tf_op jit(solution)/shard_map/ppermute | solution.py:73
  7.8 1.7 %collective-permute-start.2 = (bf16[4,64,128]{2,1,0:T(8,128)(2,1)S(1)}, bf16[4,64,128]{2,1,0:T(8,128)(2,1)S(1)}, u32[]{:S(2)}, u32[]{:S(2)}) collective-permute-start(bf16[4,64,128]{2,1,0:T(8,128)(2,1)S(1)} %collective-permute-done.1.refs_5_), channel_id=1, source_target_pairs={{16,0},{24,8},{0,16},{8,24},{17,1},{25,9},{1,17},{9,25},{18,2},{26... | collective-permute-start | bytes 196616 | tf_op jit(solution)/shard_map/ppermute | solution.py:73
  9.5 1.0 %shard_map.130 = (bf16[14,64,128]{2,1,0:T(8,128)(2,1)S(1)}, bf16[16,64,128]{2,1,0:T(8,128)(2,1)S(1)}) custom-call(bf16[16,64,128]{2,1,0:T(8,128)(2,1)S(1)} %bitcast.13, bf16[16,64,128]{2,1,0:T(8,128)(2,1)S(1)} %bitcast.19, bf16[16,64,128]{2,1,0:T(8,128)(2,1)S(1)} %collective-permute-done.3.refs_2_.refs_6_, bf16[3,128,128]{2,1,0:T(8,128)(2,1)S(1)} %copy-done.6, ...), custom_call_target="tpu_custom_call" | custom-call | flops 30198988 | bytes 2162688 | tf_op jit(solution)/shard_map/pallas_call | solution.py:38
  10.6 1.0 %collective-permute-done.2.refs_2_.refs_4_.refs_3_ = bf16[4,64,128]{2,1,0:T(8,128)(2,1)S(1)} collective-permute-done((bf16[4,64,128]{2,1,0:T(8,128)(2,1)S(1)}, bf16[4,64,128]{2,1,0:T(8,128)(2,1)S(1)}, u32[]{:S(2)}, u32[]{:S(2)}) %collective-permute-start.2) | collective-permute-done | bytes 65568 | tf_op jit(solution)/shard_map/ppermute | solution.py:73
  11.6 0.8 %shard_map.132 = (f32[2,384,128]{2,1,0:T(8,128)S(1)}, bf16[384,128]{1,0:T(8,128)(2,1)S(1)}, bf16[384,128]{1,0:T(8,128)(2,1)S(1)}) custom-call(bf16[16,64,128]{2,1,0:T(8,128)(2,1)S(1)} %bitcast.23, bf16[16,64,128]{2,1,0:T(8,128)(2,1)S(1)} %bitcast.20, bf16[16,64,128]{2,1,0:T(8,128)(2,1)S(1)} %get-tuple-element.40.refs_6_.refs_2_.refs_4_, ...), custom_call_target="tpu_custom_call" | custom-call | flops 362387872 | bytes 2031616 | tf_op jit(solution)/shard_map/pallas_call | solution.py:38
  12.4 1.0 %collective-permute-start.6 = (bf16[384,128]{1,0:T(8,128)(2,1)S(1)}, bf16[384,128]{1,0:T(8,128)(2,1)S(1)}, u32[]{:S(2)}, u32[]{:S(2)}) collective-permute-start(bf16[384,128]{1,0:T(8,128)(2,1)S(1)} %get-tuple-element.42), channel_id=1, source_target_pairs={{8,0},{0,8},{24,16},{16,24},{9,1},{1,9},{25,17},{17,25},{10,2},{2,... | collective-permute-start | bytes 294920 | tf_op jit(solution)/shard_map/ppermute | solution.py:73
  13.6 1.1 %collective-permute-start.5 = (bf16[4,64,128]{2,1,0:T(8,128)(2,1)S(1)}, bf16[4,64,128]{2,1,0:T(8,128)(2,1)S(1)}, u32[]{:S(2)}, u32[]{:S(2)}) collective-permute-start(bf16[4,64,128]{2,1,0:T(8,128)(2,1)S(1)} %shard_map.131.refs_7_), channel_id=1, source_target_pairs={{4,0},{0,4},{5,1},{1,5},{6,2},{2,6},{7,3},{3,7},{12,8},{8,12},{13,... | collective-permute-start | bytes 196616 | tf_op jit(solution)/shard_map/ppermute | solution.py:73
  15.1 1.5 %collective-permute-start.8 = (bf16[384,128]{1,0:T(8,128)(2,1)S(1)}, bf16[384,128]{1,0:T(8,128)(2,1)S(1)}, u32[]{:S(2)}, u32[]{:S(2)}) collective-permute-start(bf16[384,128]{1,0:T(8,128)(2,1)S(1)} %get-tuple-element.48), channel_id=1, source_target_pairs={{16,0},{24,8},{0,16},{8,24},{17,1},{25,9},{1,17},{9,25},{18,2},{26... | collective-permute-start | bytes 294920 | tf_op jit(solution)/shard_map/ppermute | solution.py:73
  16.7 1.5 %shard_map.135 = (bf16[16,64,128]{2,1,0:T(8,128)(2,1)S(1)}, bf16[16,64,128]{2,1,0:T(8,128)(2,1)S(1)}, f32[2,384,128]{2,1,0:T(8,128)S(1)}, bf16[896,128]{1,0:T(8,128)(2,1)S(1)}) custom-call(bf16[16,64,128]{2,1,0:T(8,128)(2,1)S(1)} %bitcast.16, bf16[4,64,128]{2,1,0:T(8,128)(2,1)S(1)} %collective-permute-done.refs_4_.refs_1_.refs_3_.refs_2_, ...), custom_call_target="tpu_custom_call" | custom-call | flops 2415919104 | bytes 4128768 | tf_op jit(solution)/shard_map/pallas_call | solution.py:38
  18.7 1.9 %collective-permute-start.9 = (bf16[896,128]{1,0:T(8,128)(2,1)S(1)}, bf16[896,128]{1,0:T(8,128)(2,1)S(1)}, u32[]{:S(2)}, u32[]{:S(2)}) collective-permute-start(bf16[896,128]{1,0:T(8,128)(2,1)S(1)} %get-tuple-element.49), channel_id=1, source_target_pairs={{8,0},{0,8},{24,16},{16,24},{9,1},{1,9},{25,17},{17,25},{10,2},{2,... | collective-permute-start | bytes 688136 | tf_op jit(solution)/shard_map/ppermute | solution.py:73
  20.5 1.1 %collective-permute-done.9.refs_1_.refs_2_ = bf16[896,128]{1,0:T(8,128)(2,1)S(1)} collective-permute-done((bf16[896,128]{1,0:T(8,128)(2,1)S(1)}, bf16[896,128]{1,0:T(8,128)(2,1)S(1)}, u32[]{:S(2)}, u32[]{:S(2)}) %collective-permute-start.9) | collective-permute-done | bytes 229408 | tf_op jit(solution)/shard_map/ppermute | solution.py:73
  21.7 1.3 %collective-permute-start.10 = (bf16[256,128]{1,0:T(8,128)(2,1)S(1)}, bf16[256,128]{1,0:T(8,128)(2,1)S(1)}, u32[]{:S(2)}, u32[]{:S(2)}) collective-permute-start(bf16[256,128]{1,0:T(8,128)(2,1)S(1)} %get-tuple-element.52), channel_id=1, source_target_pairs={{16,0},{24,8},{0,16},{8,24},{17,1},{25,9},{1,17},{9,25},{18,2},{26... | collective-permute-start | bytes 196616 | tf_op jit(solution)/shard_map/ppermute | solution.py:73
  23.0 0.7 %collective-permute-start.13 = (bf16[192,128]{1,0:T(8,128)(2,1)S(1)}, bf16[192,128]{1,0:T(8,128)(2,1)S(1)}, u32[]{:S(2)}, u32[]{:S(2)}) collective-permute-start(bf16[192,128]{1,0:T(8,128)(2,1)S(1)} %get-tuple-element.51.refs_2_), channel_id=1, source_target_pairs={{4,0},{0,4},{5,1},{1,5},{6,2},{2,6},{7,3},{3,7},{12,8},{8,12},{13,... | collective-permute-start | bytes 147464 | tf_op jit(solution)/shard_map/ppermute | solution.py:73
  25.1 0.9 %collective-permute-done.13.refs_1_ = bf16[192,128]{1,0:T(8,128)(2,1)S(1)} collective-permute-done((bf16[192,128]{1,0:T(8,128)(2,1)S(1)}, bf16[192,128]{1,0:T(8,128)(2,1)S(1)}, u32[]{:S(2)}, u32[]{:S(2)}) %collective-permute-start.13) | collective-permute-done | bytes 49184 | tf_op jit(solution)/shard_map/ppermute | solution.py:73
  26.0 1.4 %collective-permute-start.15 = (bf16[192,128]{1,0:T(8,128)(2,1)S(1)}, bf16[192,128]{1,0:T(8,128)(2,1)S(1)}, u32[]{:S(2)}, u32[]{:S(2)}) collective-permute-start(bf16[192,128]{1,0:T(8,128)(2,1)S(1)} %shard_map.139.refs_0_), channel_id=1, source_target_pairs={{1,0},{0,1},{3,2},{2,3},{5,4},{4,5},{7,6},{6,7},{9,8},{8,9},{11,10... | collective-permute-start | bytes 147464 | tf_op jit(solution)/shard_map/ppermute | solution.py:73
  27.4 1.1 %collective-permute-done.12.refs_3_ = bf16[192,128]{1,0:T(8,128)(2,1)S(1)} collective-permute-done((bf16[192,128]{1,0:T(8,128)(2,1)S(1)}, bf16[192,128]{1,0:T(8,128)(2,1)S(1)}, u32[]{:S(2)}, u32[]{:S(2)}) %collective-permute-start.12) | collective-permute-done | bytes 49184 | tf_op jit(solution)/shard_map/ppermute | solution.py:81
  28.6 1.4 %collective-permute-start.14 = (bf16[192,128]{1,0:T(8,128)(2,1)S(1)}, bf16[192,128]{1,0:T(8,128)(2,1)S(1)}, u32[]{:S(2)}, u32[]{:S(2)}) collective-permute-start(bf16[192,128]{1,0:T(8,128)(2,1)S(1)} %shard_map.138.refs_0_), channel_id=1, source_target_pairs={{1,0},{0,1},{3,2},{2,3},{5,4},{4,5},{7,6},{6,7},{9,8},{8,9},{11,10... | collective-permute-start | bytes 147464 | tf_op jit(solution)/shard_map/ppermute | solution.py:73
  30.0 2.4 %collective-permute-start.17 = (bf16[192,128]{1,0:T(8,128)(2,1)S(1)}, bf16[192,128]{1,0:T(8,128)(2,1)S(1)}, u32[]{:S(2)}, u32[]{:S(2)}) collective-permute-start(bf16[192,128]{1,0:T(8,128)(2,1)S(1)} %shard_map.142.refs_2_), channel_id=1, source_target_pairs={{2,0},{3,1},{0,2},{1,3},{6,4},{7,5},{4,6},{5,7},{10,8},{11,9},{8,1... | collective-permute-start | bytes 147464 | tf_op jit(solution)/shard_map/ppermute | solution.py:73
  32.4 2.4 %collective-permute-start.16 = (bf16[192,128]{1,0:T(8,128)(2,1)S(1)}, bf16[192,128]{1,0:T(8,128)(2,1)S(1)}, u32[]{:S(2)}, u32[]{:S(2)}) collective-permute-start(bf16[192,128]{1,0:T(8,128)(2,1)S(1)} %shard_map.140.refs_5_.refs_0_), channel_id=1, source_target_pairs={{2,0},{3,1},{0,2},{1,3},{6,4},{7,5},{4,6},{5,7},{10,8},{11,9},{8,1... | collective-permute-start | bytes 147464 | tf_op jit(solution)/shard_map/ppermute | solution.py:73
  34.8 1.5 %shard_map.141 = (bf16[16,64,128]{2,1,0:T(8,128)(2,1)}, f32[8,128]{1,0:T(8,128)S(1)}) custom-call(bf16[16,64,128]{2,1,0:T(8,128)(2,1)S(1)} %get-tuple-element.45.refs_0_, bf16[16,64,128]{2,1,0:T(8,128)(2,1)S(1)} %get-tuple-element.46.refs_1_, bf16[896,128]{1,0:T(8,128)(2,1)S(1)} %collective-permute-done.9.refs_1_.refs_2_, ...), custom_call_target="tpu_custom_call" | custom-call | flops 301989888 | bytes 1380352 | tf_op jit(solution)/shard_map/pallas_call | solution.py:38
  36.3 0.8 %collective-permute-start.18 = (bf16[2,192,128]{2,1,0:T(8,128)(2,1)S(1)}, bf16[2,192,128]{2,1,0:T(8,128)(2,1)S(1)}, u32[]{:S(2)}, u32[]{:S(2)}) collective-permute-start(bf16[2,192,128]{2,1,0:T(8,128)(2,1)S(1)} %shard_map.143.refs_0_), channel_id=1, source_target_pairs={{4,0},{0,4},{5,1},{1,5},{6,2},{2,6},{7,3},{3,7},{12,8},{8,12},{13,... | collective-permute-start | bytes 294920 | tf_op jit(solution)/shard_map/ppermute | solution.py:73
  37.1 2.2 %collective-permute-start.21 = (bf16[2,192,128]{2,1,0:T(8,128)(2,1)S(1)}, bf16[2,192,128]{2,1,0:T(8,128)(2,1)S(1)}, u32[]{:S(2)}, u32[]{:S(2)}) collective-permute-start(bf16[2,192,128]{2,1,0:T(8,128)(2,1)S(1)} %shard_map.143.refs_0_), channel_id=1, source_target_pairs={{16,0},{24,8},{0,16},{8,24},{17,1},{25,9},{1,17},{9,25},{18,2},{26... | collective-permute-start | bytes 294920 | tf_op jit(solution)/shard_map/ppermute | solution.py:73
  39.8 4.5 %collective-permute-start.19 = (bf16[2,192,128]{2,1,0:T(8,128)(2,1)S(1)}, bf16[2,192,128]{2,1,0:T(8,128)(2,1)S(1)}, u32[]{:S(2)}, u32[]{:S(2)}) collective-permute-start(bf16[2,192,128]{2,1,0:T(8,128)(2,1)S(1)} %shard_map.143.refs_0_), channel_id=1, source_target_pairs={{8,0},{0,8},{24,16},{16,24},{9,1},{1,9},{25,17},{17,25},{10,2},{2,... | collective-permute-start | bytes 294920 | tf_op jit(solution)/shard_map/ppermute | solution.py:73
  44.3 1.1 %collective-permute-start.20 = (bf16[2,192,128]{2,1,0:T(8,128)(2,1)S(1)}, bf16[2,192,128]{2,1,0:T(8,128)(2,1)S(1)}, u32[]{:S(2)}, u32[]{:S(2)}) collective-permute-start(bf16[2,192,128]{2,1,0:T(8,128)(2,1)S(1)} %collective-permute-done.18.refs_1_), channel_id=1, source_target_pairs={{8,0},{0,8},{24,16},{16,24},{9,1},{1,9},{25,17},{17,25},{10,2},{2,... | collective-permute-start | bytes 294920 | tf_op jit(solution)/shard_map/ppermute | solution.py:73
  45.4 1.0 %collective-permute-start.23 = (bf16[2,192,128]{2,1,0:T(8,128)(2,1)S(1)}, bf16[2,192,128]{2,1,0:T(8,128)(2,1)S(1)}, u32[]{:S(2)}, u32[]{:S(2)}) collective-permute-start(bf16[2,192,128]{2,1,0:T(8,128)(2,1)S(1)} %collective-permute-done.21.refs_4_), channel_id=1, source_target_pairs={{8,0},{0,8},{24,16},{16,24},{9,1},{1,9},{25,17},{17,25},{10,2},{2,... | collective-permute-start | bytes 294920 | tf_op jit(solution)/shard_map/ppermute | solution.py:73
  46.4 1.1 %collective-permute-start.24 = (bf16[2,192,128]{2,1,0:T(8,128)(2,1)S(1)}, bf16[2,192,128]{2,1,0:T(8,128)(2,1)S(1)}, u32[]{:S(2)}, u32[]{:S(2)}) collective-permute-start(bf16[2,192,128]{2,1,0:T(8,128)(2,1)S(1)} %collective-permute-done.22.refs_5_), channel_id=1, source_target_pairs={{8,0},{0,8},{24,16},{16,24},{9,1},{1,9},{25,17},{17,25},{10,2},{2,... | collective-permute-start | bytes 294920 | tf_op jit(solution)/shard_map/ppermute | solution.py:73
  47.5 0.9 %collective-permute-done.24.refs_7_ = bf16[2,192,128]{2,1,0:T(8,128)(2,1)S(1)} collective-permute-done((bf16[2,192,128]{2,1,0:T(8,128)(2,1)S(1)}, bf16[2,192,128]{2,1,0:T(8,128)(2,1)S(1)}, u32[]{:S(2)}, u32[]{:S(2)}) %collective-permute-start.24) | collective-permute-done | bytes 98336 | tf_op jit(solution)/shard_map/ppermute | solution.py:73
  48.4 1.3 %shard_map.144 = (f32[3,384,128]{2,1,0:T(8,128)}, f32[384,128]{1,0:T(8,128)}, f32[3,384,128]{2,1,0:T(8,128)}, f32[384,128]{1,0:T(8,128)}) custom-call(bf16[2,192,128]{2,1,0:T(8,128)(2,1)S(1)} %shard_map.143.refs_0_, bf16[2,192,128]{2,1,0:T(8,128)(2,1)S(1)} %collective-permute-done.18.refs_1_, bf16[2,192,128]{2,1,0:T(8,128)(2,1)S(1)} %collective-permute-done.19.refs_2_, ...), custom_call_target="tpu_custom_call" | custom-call | flops 196608 | bytes 2359296 | tf_op jit(solution)/shard_map/pallas_call | solution.py:38
  (53 shorter events, 3.7 us)
Async XLA Ops:
  0.6 8.9 %collective-permute-start.3 = (bf16[16,64,128]{2,1,0:T(8,128)(2,1)}, bf16[16,64,128]{2,1,0:T(8,128)(2,1)S(1)}, u32[]{:S(2)}, u32[]{:S(2)}) collective-permute-start(bf16[16,64,128]{2,1,0:T(8,128)(2,1)} %bitcast.10), channel_id=1, source_target_pairs={{4,0},{0,4},{5,1},{1,5},{6,2},{2,6},{7,3},{3,7},{12,8},{8,12},{13,... | collective-permute-start | bytes 786440 | tf_op jit(solution)/shard_map/ppermute | solution.py:73
  2.7 4.2 %copy-start = (bf16[1,1,16,64,128]{4,3,2,1,0:T(8,128)(2,1)S(1)}, bf16[1,1,16,64,128]{4,3,2,1,0:T(8,128)(2,1)}, u32[]{:S(2)}) copy-start(bf16[1,1,16,64,128]{4,3,2,1,0:T(8,128)(2,1)} %param.9) | copy-start | bytes 786436
  2.7 4.2 %copy-start.1 = (bf16[1,1,16,64,128]{4,3,2,1,0:T(8,128)(2,1)S(1)}, bf16[1,1,16,64,128]{4,3,2,1,0:T(8,128)(2,1)}, u32[]{:S(2)}) copy-start(bf16[1,1,16,64,128]{4,3,2,1,0:T(8,128)(2,1)} %param.13) | copy-start | bytes 786436
  2.7 4.2 %copy-start.2 = (bf16[3,3,128,128]{3,2,1,0:T(8,128)(2,1)S(1)}, bf16[3,3,128,128]{3,2,1,0:T(8,128)(2,1)}, u32[]{:S(2)}) copy-start(bf16[3,3,128,128]{3,2,1,0:T(8,128)(2,1)} %refs_8_.1) | copy-start | bytes 884740
  2.7 4.2 %copy-start.6 = (bf16[3,128,128]{2,1,0:T(8,128)(2,1)S(1)}, bf16[3,128,128]{2,1,0:T(8,128)(2,1)}, u32[]{:S(2)}) copy-start(bf16[3,128,128]{2,1,0:T(8,128)(2,1)} %refs_7_.1) | copy-start | bytes 294916
  4.4 2.1 %collective-permute-start = (bf16[4,64,128]{2,1,0:T(8,128)(2,1)}, bf16[4,64,128]{2,1,0:T(8,128)(2,1)S(1)}, u32[]{:S(2)}, u32[]{:S(2)}) collective-permute-start(bf16[4,64,128]{2,1,0:T(8,128)(2,1)} %get-tuple-element.35), channel_id=1, source_target_pairs={{8,0},{0,8},{24,16},{16,24},{9,1},{1,9},{25,17},{17,25},{10,2},{2,... | collective-permute-start | bytes 196616 | tf_op jit(solution)/shard_map/ppermute | solution.py:73
  5.4 4.1 %copy-start.5 = (bf16[1,1,16,64,128]{4,3,2,1,0:T(8,128)(2,1)S(1)}, bf16[1,1,16,64,128]{4,3,2,1,0:T(8,128)(2,1)}, u32[]{:S(2)}) copy-start(bf16[1,1,16,64,128]{4,3,2,1,0:T(8,128)(2,1)} %param.11) | copy-start | bytes 786436
  5.4 4.1 %copy-start.8 = (bf16[3,128,128]{2,1,0:T(8,128)(2,1)S(1)}, bf16[3,128,128]{2,1,0:T(8,128)(2,1)}, u32[]{:S(2)}) copy-start(bf16[3,128,128]{2,1,0:T(8,128)(2,1)} %refs_11_.1) | copy-start | bytes 294916
  5.4 1.5 %collective-permute-start.1 = (bf16[4,64,128]{2,1,0:T(8,128)(2,1)}, bf16[4,64,128]{2,1,0:T(8,128)(2,1)S(1)}, u32[]{:S(2)}, u32[]{:S(2)}) collective-permute-start(bf16[4,64,128]{2,1,0:T(8,128)(2,1)} %get-tuple-element.36), channel_id=1, source_target_pairs={{8,0},{0,8},{24,16},{16,24},{9,1},{1,9},{25,17},{17,25},{10,2},{2,... | collective-permute-start | bytes 196616 | tf_op jit(solution)/shard_map/ppermute | solution.py:73
  7.0 9.6 %collective-permute-start.4 = (bf16[14,64,128]{2,1,0:T(8,128)(2,1)S(1)}, bf16[14,64,128]{2,1,0:T(8,128)(2,1)S(1)}, u32[]{:S(2)}, u32[]{:S(2)}) collective-permute-start(bf16[14,64,128]{2,1,0:T(8,128)(2,1)S(1)} %get-tuple-element.37.refs_5_), channel_id=1, source_target_pairs={{4,0},{0,4},{5,1},{1,5},{6,2},{2,6},{7,3},{3,7},{12,8},{8,12},{13,... | collective-permute-start | bytes 688136 | tf_op jit(solution)/shard_map/ppermute | solution.py:73
  7.8 3.8 %collective-permute-start.2 = (bf16[4,64,128]{2,1,0:T(8,128)(2,1)S(1)}, bf16[4,64,128]{2,1,0:T(8,128)(2,1)S(1)}, u32[]{:S(2)}, u32[]{:S(2)}) collective-permute-start(bf16[4,64,128]{2,1,0:T(8,128)(2,1)S(1)} %collective-permute-done.1.refs_5_), channel_id=1, source_target_pairs={{16,0},{24,8},{0,16},{8,24},{17,1},{25,9},{1,17},{9,25},{18,2},{26... | collective-permute-start | bytes 196616 | tf_op jit(solution)/shard_map/ppermute | solution.py:73
  12.4 2.6 %collective-permute-start.6 = (bf16[384,128]{1,0:T(8,128)(2,1)S(1)}, bf16[384,128]{1,0:T(8,128)(2,1)S(1)}, u32[]{:S(2)}, u32[]{:S(2)}) collective-permute-start(bf16[384,128]{1,0:T(8,128)(2,1)S(1)} %get-tuple-element.42), channel_id=1, source_target_pairs={{8,0},{0,8},{24,16},{16,24},{9,1},{1,9},{25,17},{17,25},{10,2},{2,... | collective-permute-start | bytes 294920 | tf_op jit(solution)/shard_map/ppermute | solution.py:73
  13.5 1.6 %collective-permute-start.7 = (bf16[384,128]{1,0:T(8,128)(2,1)S(1)}, bf16[384,128]{1,0:T(8,128)(2,1)S(1)}, u32[]{:S(2)}, u32[]{:S(2)}) collective-permute-start(bf16[384,128]{1,0:T(8,128)(2,1)S(1)} %get-tuple-element.43), channel_id=1, source_target_pairs={{8,0},{0,8},{24,16},{16,24},{9,1},{1,9},{25,17},{17,25},{10,2},{2,... | collective-permute-start | bytes 294920 | tf_op jit(solution)/shard_map/ppermute | solution.py:73
  13.6 3.1 %collective-permute-start.5 = (bf16[4,64,128]{2,1,0:T(8,128)(2,1)S(1)}, bf16[4,64,128]{2,1,0:T(8,128)(2,1)S(1)}, u32[]{:S(2)}, u32[]{:S(2)}) collective-permute-start(bf16[4,64,128]{2,1,0:T(8,128)(2,1)S(1)} %shard_map.131.refs_7_), channel_id=1, source_target_pairs={{4,0},{0,4},{5,1},{1,5},{6,2},{2,6},{7,3},{3,7},{12,8},{8,12},{13,... | collective-permute-start | bytes 196616 | tf_op jit(solution)/shard_map/ppermute | solution.py:73
  15.1 3.5 %collective-permute-start.8 = (bf16[384,128]{1,0:T(8,128)(2,1)S(1)}, bf16[384,128]{1,0:T(8,128)(2,1)S(1)}, u32[]{:S(2)}, u32[]{:S(2)}) collective-permute-start(bf16[384,128]{1,0:T(8,128)(2,1)S(1)} %get-tuple-element.48), channel_id=1, source_target_pairs={{16,0},{24,8},{0,16},{8,24},{17,1},{25,9},{1,17},{9,25},{18,2},{26... | collective-permute-start | bytes 294920 | tf_op jit(solution)/shard_map/ppermute | solution.py:73
  18.7 3.0 %collective-permute-start.9 = (bf16[896,128]{1,0:T(8,128)(2,1)S(1)}, bf16[896,128]{1,0:T(8,128)(2,1)S(1)}, u32[]{:S(2)}, u32[]{:S(2)}) collective-permute-start(bf16[896,128]{1,0:T(8,128)(2,1)S(1)} %get-tuple-element.49), channel_id=1, source_target_pairs={{8,0},{0,8},{24,16},{16,24},{9,1},{1,9},{25,17},{17,25},{10,2},{2,... | collective-permute-start | bytes 688136 | tf_op jit(solution)/shard_map/ppermute | solution.py:73
  21.7 6.8 %collective-permute-start.10 = (bf16[256,128]{1,0:T(8,128)(2,1)S(1)}, bf16[256,128]{1,0:T(8,128)(2,1)S(1)}, u32[]{:S(2)}, u32[]{:S(2)}) collective-permute-start(bf16[256,128]{1,0:T(8,128)(2,1)S(1)} %get-tuple-element.52), channel_id=1, source_target_pairs={{16,0},{24,8},{0,16},{8,24},{17,1},{25,9},{1,17},{9,25},{18,2},{26... | collective-permute-start | bytes 196616 | tf_op jit(solution)/shard_map/ppermute | solution.py:73
  23.0 3.0 %collective-permute-start.13 = (bf16[192,128]{1,0:T(8,128)(2,1)S(1)}, bf16[192,128]{1,0:T(8,128)(2,1)S(1)}, u32[]{:S(2)}, u32[]{:S(2)}) collective-permute-start(bf16[192,128]{1,0:T(8,128)(2,1)S(1)} %get-tuple-element.51.refs_2_), channel_id=1, source_target_pairs={{4,0},{0,4},{5,1},{1,5},{6,2},{2,6},{7,3},{3,7},{12,8},{8,12},{13,... | collective-permute-start | bytes 147464 | tf_op jit(solution)/shard_map/ppermute | solution.py:73
  23.8 3.7 %collective-permute-start.11 = (bf16[192,128]{1,0:T(8,128)(2,1)S(1)}, bf16[192,128]{1,0:T(8,128)(2,1)S(1)}, u32[]{:S(2)}, u32[]{:S(2)}) collective-permute-start(bf16[192,128]{1,0:T(8,128)(2,1)S(1)} %get-tuple-element.54), channel_id=1, source_target_pairs={{4,0},{0,4},{5,1},{1,5},{6,2},{2,6},{7,3},{3,7},{12,8},{8,12},{13,... | collective-permute-start | bytes 147464 | tf_op jit(solution)/shard_map/ppermute | solution.py:73
  24.5 4.0 %collective-permute-start.12 = (bf16[192,128]{1,0:T(8,128)(2,1)S(1)}, bf16[192,128]{1,0:T(8,128)(2,1)S(1)}, u32[]{:S(2)}, u32[]{:S(2)}) collective-permute-start(bf16[192,128]{1,0:T(8,128)(2,1)S(1)} %get-tuple-element.55), channel_id=1, source_target_pairs={{20,0},{16,4},{28,8},{24,12},{4,16},{0,20},{12,24},{8,28},{21,1},{... | collective-permute-start | bytes 147464 | tf_op jit(solution)/shard_map/ppermute | solution.py:81
  26.0 4.0 %collective-permute-start.15 = (bf16[192,128]{1,0:T(8,128)(2,1)S(1)}, bf16[192,128]{1,0:T(8,128)(2,1)S(1)}, u32[]{:S(2)}, u32[]{:S(2)}) collective-permute-start(bf16[192,128]{1,0:T(8,128)(2,1)S(1)} %shard_map.139.refs_0_), channel_id=1, source_target_pairs={{1,0},{0,1},{3,2},{2,3},{5,4},{4,5},{7,6},{6,7},{9,8},{8,9},{11,10... | collective-permute-start | bytes 147464 | tf_op jit(solution)/shard_map/ppermute | solution.py:73
  28.5 6.2 %copy-start.7 = (bf16[3,3,128,128]{3,2,1,0:T(8,128)(2,1)S(1)}, bf16[3,3,128,128]{3,2,1,0:T(8,128)(2,1)}, u32[]{:S(2)}) copy-start(bf16[3,3,128,128]{3,2,1,0:T(8,128)(2,1)} %refs_4_.5) | copy-start | bytes 884740
  28.6 3.8 %collective-permute-start.14 = (bf16[192,128]{1,0:T(8,128)(2,1)S(1)}, bf16[192,128]{1,0:T(8,128)(2,1)S(1)}, u32[]{:S(2)}, u32[]{:S(2)}) collective-permute-start(bf16[192,128]{1,0:T(8,128)(2,1)S(1)} %shard_map.138.refs_0_), channel_id=1, source_target_pairs={{1,0},{0,1},{3,2},{2,3},{5,4},{4,5},{7,6},{6,7},{9,8},{8,9},{11,10... | collective-permute-start | bytes 147464 | tf_op jit(solution)/shard_map/ppermute | solution.py:73
  30.0 6.3 %collective-permute-start.17 = (bf16[192,128]{1,0:T(8,128)(2,1)S(1)}, bf16[192,128]{1,0:T(8,128)(2,1)S(1)}, u32[]{:S(2)}, u32[]{:S(2)}) collective-permute-start(bf16[192,128]{1,0:T(8,128)(2,1)S(1)} %shard_map.142.refs_2_), channel_id=1, source_target_pairs={{2,0},{3,1},{0,2},{1,3},{6,4},{7,5},{4,6},{5,7},{10,8},{11,9},{8,1... | collective-permute-start | bytes 147464 | tf_op jit(solution)/shard_map/ppermute | solution.py:73
  32.4 3.9 %collective-permute-start.16 = (bf16[192,128]{1,0:T(8,128)(2,1)S(1)}, bf16[192,128]{1,0:T(8,128)(2,1)S(1)}, u32[]{:S(2)}, u32[]{:S(2)}) collective-permute-start(bf16[192,128]{1,0:T(8,128)(2,1)S(1)} %shard_map.140.refs_5_.refs_0_), channel_id=1, source_target_pairs={{2,0},{3,1},{0,2},{1,3},{6,4},{7,5},{4,6},{5,7},{10,8},{11,9},{8,1... | collective-permute-start | bytes 147464 | tf_op jit(solution)/shard_map/ppermute | solution.py:73
  36.3 7.9 %collective-permute-start.18 = (bf16[2,192,128]{2,1,0:T(8,128)(2,1)S(1)}, bf16[2,192,128]{2,1,0:T(8,128)(2,1)S(1)}, u32[]{:S(2)}, u32[]{:S(2)}) collective-permute-start(bf16[2,192,128]{2,1,0:T(8,128)(2,1)S(1)} %shard_map.143.refs_0_), channel_id=1, source_target_pairs={{4,0},{0,4},{5,1},{1,5},{6,2},{2,6},{7,3},{3,7},{12,8},{8,12},{13,... | collective-permute-start | bytes 294920 | tf_op jit(solution)/shard_map/ppermute | solution.py:73
  37.1 8.3 %collective-permute-start.21 = (bf16[2,192,128]{2,1,0:T(8,128)(2,1)S(1)}, bf16[2,192,128]{2,1,0:T(8,128)(2,1)S(1)}, u32[]{:S(2)}, u32[]{:S(2)}) collective-permute-start(bf16[2,192,128]{2,1,0:T(8,128)(2,1)S(1)} %shard_map.143.refs_0_), channel_id=1, source_target_pairs={{16,0},{24,8},{0,16},{8,24},{17,1},{25,9},{1,17},{9,25},{18,2},{26... | collective-permute-start | bytes 294920 | tf_op jit(solution)/shard_map/ppermute | solution.py:73
  39.3 7.1 %collective-permute-start.22 = (bf16[2,192,128]{2,1,0:T(8,128)(2,1)S(1)}, bf16[2,192,128]{2,1,0:T(8,128)(2,1)S(1)}, u32[]{:S(2)}, u32[]{:S(2)}) collective-permute-start(bf16[2,192,128]{2,1,0:T(8,128)(2,1)S(1)} %shard_map.143.refs_0_), channel_id=1, source_target_pairs={{20,0},{16,4},{28,8},{24,12},{4,16},{0,20},{12,24},{8,28},{21,1},{... | collective-permute-start | bytes 294920 | tf_op jit(solution)/shard_map/ppermute | solution.py:81
  39.8 7.7 %collective-permute-start.19 = (bf16[2,192,128]{2,1,0:T(8,128)(2,1)S(1)}, bf16[2,192,128]{2,1,0:T(8,128)(2,1)S(1)}, u32[]{:S(2)}, u32[]{:S(2)}) collective-permute-start(bf16[2,192,128]{2,1,0:T(8,128)(2,1)S(1)} %shard_map.143.refs_0_), channel_id=1, source_target_pairs={{8,0},{0,8},{24,16},{16,24},{9,1},{1,9},{25,17},{17,25},{10,2},{2,... | collective-permute-start | bytes 294920 | tf_op jit(solution)/shard_map/ppermute | solution.py:73
  44.3 3.2 %collective-permute-start.20 = (bf16[2,192,128]{2,1,0:T(8,128)(2,1)S(1)}, bf16[2,192,128]{2,1,0:T(8,128)(2,1)S(1)}, u32[]{:S(2)}, u32[]{:S(2)}) collective-permute-start(bf16[2,192,128]{2,1,0:T(8,128)(2,1)S(1)} %collective-permute-done.18.refs_1_), channel_id=1, source_target_pairs={{8,0},{0,8},{24,16},{16,24},{9,1},{1,9},{25,17},{17,25},{10,2},{2,... | collective-permute-start | bytes 294920 | tf_op jit(solution)/shard_map/ppermute | solution.py:73
  45.4 2.1 %collective-permute-start.23 = (bf16[2,192,128]{2,1,0:T(8,128)(2,1)S(1)}, bf16[2,192,128]{2,1,0:T(8,128)(2,1)S(1)}, u32[]{:S(2)}, u32[]{:S(2)}) collective-permute-start(bf16[2,192,128]{2,1,0:T(8,128)(2,1)S(1)} %collective-permute-done.21.refs_4_), channel_id=1, source_target_pairs={{8,0},{0,8},{24,16},{16,24},{9,1},{1,9},{25,17},{17,25},{10,2},{2,... | collective-permute-start | bytes 294920 | tf_op jit(solution)/shard_map/ppermute | solution.py:73
  46.4 2.0 %collective-permute-start.24 = (bf16[2,192,128]{2,1,0:T(8,128)(2,1)S(1)}, bf16[2,192,128]{2,1,0:T(8,128)(2,1)S(1)}, u32[]{:S(2)}, u32[]{:S(2)}) collective-permute-start(bf16[2,192,128]{2,1,0:T(8,128)(2,1)S(1)} %collective-permute-done.22.refs_5_), channel_id=1, source_target_pairs={{8,0},{0,8},{24,16},{16,24},{9,1},{1,9},{25,17},{17,25},{10,2},{2,... | collective-permute-start | bytes 294920 | tf_op jit(solution)/shard_map/ppermute | solution.py:73
  (2 other events, 8.3 us)

commit v13 on v12

--- a/solution.py
+++ b/solution.py
@@ -43,7 +43,7 @@
         scratch_shapes=scratch,
         compiler_params=pltpu.CompilerParams(vmem_limit_bytes=limit * MIB),
         cost_estimate=pl.CostEstimate(
-            flops=int(flops), bytes_accessed=int(moved), transcendentals=0
+            flops=int(flops), bytes_accessed=int(moved) if flops else 0, transcendentals=0
         ),
     )(*operands)
 
@@ -410,40 +410,60 @@
         out_ref[block] = ((one + two) * factor).astype(jnp.bfloat16)
 
 
-def place_kernel(*refs):
-    shares, outs = refs[:-4], refs[-4:]
+def place_kernel(places, *refs):
+    shares, outs = refs[: len(places)], refs[-6:-2]
+    sums_ref, sems = refs[-2:]
     band, frame = lax.axis_index("section"), lax.axis_index("video")
-    halves = len(shares) // 4
     height = shares[0].shape[1]
+
+    def copies(n, block):
+        flip, other = places[n]
+        place = jnp.bitwise_xor(band, flip)
+        half = 0 if other is None else jnp.bitwise_xor(frame, int(other))
+        here = pl.ds(pl.multiple_of(half * height, height), height)
+        spatial, temporal = outs[2 * block : 2 * block + 2]
+        source, sem = sums_ref.at[n, block], sems.at[n, block]
+        return (
+            (place < 3, lambda: pltpu.make_async_copy(source, spatial.at[place, here], sem)),
+            (place == 3, lambda: pltpu.make_async_copy(source, temporal.at[here], sem)),
+        )
+
     for n, share in enumerate(shares):
-        place = jnp.bitwise_xor(band, n // halves)
-        half = jnp.bitwise_xor(frame, n % halves) if halves == 2 else 0
-        here = pl.ds(pl.multiple_of(half * height, height), height)
-
-        @pl.when(place < 3)
-        def _():
-            for block in range(2):
-                outs[2 * block][place, here] = share[block].astype(jnp.float32)
-
-        @pl.when(place == 3)
-        def _():
-            for block in range(2):
-                outs[2 * block + 1][here] = share[block].astype(jnp.float32)
-
-
-def placed(shares, across):
-    ch = shares[0].shape[2]
-    outs = call(
-        place_kernel,
-        [f32(3, 3 * ch, ch), f32(3 * ch, ch)] * 2,
-        [],
-        12 * ch * ch,
-        *shares,
-        *[flipped(share, "section", 1) for share in shares],
-        *across,
-        *[flipped(share, "section", 1) for share in across],
-    )
-    return [x.reshape(3, 3, ch, ch) if x.ndim == 3 else x.reshape(3, ch, ch) for x in outs]
+        for block in range(2):
+            sums_ref[n, block] = share[block].astype(jnp.float32)
+            for inside, copy in copies(n, block):
+                pl.when(inside)(lambda: copy().start())
+    for n in range(len(shares)):
+        for block in range(2):
+            for inside, copy in copies(n, block):
+                pl.when(inside)(lambda: copy().wait())
+
+
+def placed(shares, places, given=()):
+    _, height, ch = shares[0].shape
+    count = len(shares)
+    outs = (f32(3, 3 * ch, ch), f32(3 * ch, ch)) * 2
+    vmem, spare = (pl.BlockSpec(memory_space=space) for space in (pltpu.VMEM, pl.ANY))
+    return pl.pallas_call(
+        functools.partial(place_kernel, places),
+        out_shape=outs,
+        in_specs=[vmem] * count + [spare] * len(given),
+        out_specs=(spare,) * 4,
+        scratch_shapes=[
+            pltpu.VMEM((count, 2, height, ch), jnp.float32),
+            pltpu.SemaphoreType.DMA((count, 2)),
+        ],
+        input_output_aliases={count + n: n for n in range(len(given))},
+        compiler_params=pltpu.CompilerParams(vmem_limit_bytes=24 * MIB),
+        cost_estimate=pl.CostEstimate(
+            flops=0, bytes_accessed=6 * count * height * ch * 2, transcendentals=0
+        ),
+    )(*shares, *given)
+
+
+def unpacked(sums):
+    ch = sums[0].shape[-1]
+    return [x.reshape(3, 3, ch, ch) if x.ndim == 3 else x.reshape(3, ch, ch) for x in sums]
 
 
 def on_device(
@@ -495,7 +515,8 @@
         spare_inputs=True,
         limit=58,
     )
-    first, second = (flipped(pack, "section", 1) for pack in packs)
+    second = flipped(packs[1], "section", 1)
+    first = flipped(later_than(packs[0], second), "section", 1)
     pairs = [first, flipped(second, "section", 2)]
 
     known = ()
@@ -504,7 +525,7 @@
             last_inner_kernel,
             inner_outs,
             [views],
-            0.1 * conv,
+            0,
             grad,
             pre_two,
             *kernels,
@@ -517,7 +538,7 @@
         functools.partial(inner_kernel, later),
         inner_outs,
         [views],
-        0.1 * conv,
+        0,
         grad,
         pre_two,
         *wholes,
@@ -530,7 +551,7 @@
             last_edge_kernel,
             [bf16(4, cols, ch)],
             [edge_views],
-            conv // 8,
+            0,
             grad,
             *pairs,
             known[1],
@@ -542,7 +563,7 @@
         functools.partial(two_kernel, later),
         handed,
         [views, pltpu.VMEM(sides.shape, sides.dtype), sums],
-        1.2 * conv,
+        8 * conv,
         saved_two,
         pre_two,
         gpre_two,
@@ -662,8 +683,13 @@
             last_two,
             after=(token,),
         )
-        shares = [own, flipped(own, "video", 1)]
-        sums = placed(shares, [flipped(own, "section", 2), flipped_both(own)])
+        frame, across, both = flipped(own, "video", 1), flipped(own, "section", 2), flipped_both(own)
+        shares = [own, frame, across]
+        shares += [flipped(share, "section", 1) for share in shares]
+        last = [both, flipped(both, "section", 1)]
+        places = [(0, False), (0, True), (2, False), (1, False), (1, True), (3, False)]
+        sums = placed(shares, places)
+        sums = unpacked(placed(last, [(2, True), (3, True)], sums))
     else:
         own_one, send_one = call(
             pair_kernel,
@@ -680,7 +706,9 @@
         own_two = own_two + across_two.astype(jnp.float32)
         share = lax.psum(jnp.stack((own_one, own_two)), ("video", "dp")) * factor
         share = share.astype(jnp.bfloat16)
-        sums = placed([share], [flipped(share, "section", 2)])
+        shares = [share, flipped(share, "section", 2)]
+        shares += [flipped(share, "section", 1) for share in shares]
+        sums = unpacked(placed(shares, [(0, None), (2, None), (1, None), (3, None)]))
     return (grad_in.reshape(shape), *sums)
 
 

time: 50.2 us -> 48.9 us (0.974)
  waiting for transfers between devices: 7.01 us -> 5.26 us
  Pallas kernels: 8.42 us -> 9.03 us
    pallas_call x0 -> x2, Pallas kernels: none -> 1.91 us  [placed(): pl.pallas_call(functools.partial(place_kernel, places), out_shape=outs, i...]
    ppermute x23, waiting for transfers between devices: 5.9 us -> 4.43 us  [flipped(): lax.ppermute(block, axis, [(place ^ flip, place) for place in range(count)])]
    pallas_call x17 -> x16, Pallas kernels: 8.42 us -> 7.12 us  [call(): pl.pallas_call(body, out_shape=outs[0] if single else tuple(outs), in_spe...]
  transfers between devices with their start and end apart: 25 -> 25, of which waited for: 9 -> 8; matrix products, arithmetic and copies ran while one was open for 0% -> 0% of each run, Pallas kernels for 14% -> 17%
where the time goes in v13:
time: 48.9 us; the launch traced here: 48.6 us
  starting transfers between devices  33.5 us (69%)
  Pallas kernels  9.03 us (18%)
  waiting for transfers between devices  5.26 us (11%)
  between operations  0.82 us (2%)
    ppermute x23, starting transfers between devices, flipped(): lax.ppermute(block, axis, [(place ^ flip, place) for place in range(count)])  32.1 us
    pallas_call x16, Pallas kernels, call(): pl.pallas_call(body, out_shape=outs[0] if single else tuple(outs), in_spe...  7.12 us
    ppermute x23, waiting for transfers between devices, flipped(): lax.ppermute(block, axis, [(place ^ flip, place) for place in range(count)])  4.43 us
    pallas_call x2, Pallas kernels, placed(): pl.pallas_call(functools.partial(place_kernel, places), out_shape=outs, i...  1.91 us
    ppermute x2, starting transfers between devices, flipped_both(): return lax.ppermute(block, ('section', 'video'), pairs)  1.34 us
  transfers between devices with their start and end apart: 25, of which 8 were waited for; matrix products, arithmetic and copies ran while one was open for 0% of the time, Pallas kernels for 17%

profile of v13, /device:TPU:1, one launch (start us, length us, event | category | flops | bytes accessed | tf_op | source)
XLA Modules:
  0.0 48.6 jit_solution(7498931776410643883)
XLA Ops:
  0.6 2.1 %collective-permute-start.3 = (bf16[16,64,128]{2,1,0:T(8,128)(2,1)}, bf16[16,64,128]{2,1,0:T(8,128)(2,1)S(1)}, u32[]{:S(2)}, u32[]{:S(2)}) collective-permute-start(bf16[16,64,128]{2,1,0:T(8,128)(2,1)} %bitcast.10), channel_id=1, source_target_pairs={{4,0},{0,4},{5,1},{1,5},{6,2},{2,6},{7,3},{3,7},{12,8},{8,12},{13,... | collective-permute-start | bytes 786440 | tf_op jit(solution)/shard_map/ppermute | solution.py:73
  2.7 1.6 %shard_map.128 = (bf16[4,64,128]{2,1,0:T(8,128)(2,1)}, bf16[4,64,128]{2,1,0:T(8,128)(2,1)}) custom-call(bf16[16,64,128]{2,1,0:T(8,128)(2,1)} %bitcast.11, bf16[16,64,128]{2,1,0:T(8,128)(2,1)} %bitcast.17, bf16[16,64,128]{2,1,0:T(8,128)(2,1)} %bitcast.24, bf16[16,64,128]{2,1,0:T(8,128)(2,1)} %bitcast.21), custom_call_target="tpu_custom_call" | custom-call | flops 1 | bytes 1179648 | tf_op jit(solution)/shard_map/pallas_call | solution.py:38
  4.4 1.0 %collective-permute-start = (bf16[4,64,128]{2,1,0:T(8,128)(2,1)}, bf16[4,64,128]{2,1,0:T(8,128)(2,1)S(1)}, u32[]{:S(2)}, u32[]{:S(2)}) collective-permute-start(bf16[4,64,128]{2,1,0:T(8,128)(2,1)} %get-tuple-element.41), channel_id=1, source_target_pairs={{8,0},{0,8},{24,16},{16,24},{9,1},{1,9},{25,17},{17,25},{10,2},{2,... | collective-permute-start | bytes 196616 | tf_op jit(solution)/shard_map/ppermute | solution.py:73
  5.4 1.1 %collective-permute-done.refs_5_ = bf16[4,64,128]{2,1,0:T(8,128)(2,1)S(1)} collective-permute-done((bf16[4,64,128]{2,1,0:T(8,128)(2,1)}, bf16[4,64,128]{2,1,0:T(8,128)(2,1)S(1)}, u32[]{:S(2)}, u32[]{:S(2)}) %collective-permute-start) | collective-permute-done | bytes 65568 | tf_op jit(solution)/shard_map/ppermute | solution.py:73
  6.5 0.4 collective-permute-start.1
  6.9 1.2 %collective-permute-start.2 = (bf16[4,64,128]{2,1,0:T(8,128)(2,1)S(1)}, bf16[4,64,128]{2,1,0:T(8,128)(2,1)S(1)}, u32[]{:S(2)}, u32[]{:S(2)}) collective-permute-start(bf16[4,64,128]{2,1,0:T(8,128)(2,1)S(1)} %collective-permute-done.refs_5_), channel_id=1, source_target_pairs={{16,0},{24,8},{0,16},{8,24},{17,1},{25,9},{1,17},{9,25},{18,2},{26... | collective-permute-start | bytes 196616 | tf_op jit(solution)/shard_map/ppermute | solution.py:73
  8.2 1.3 %collective-permute-start.4 = (bf16[14,64,128]{2,1,0:T(8,128)(2,1)S(1)}, bf16[14,64,128]{2,1,0:T(8,128)(2,1)S(1)}, u32[]{:S(2)}, u32[]{:S(2)}) collective-permute-start(bf16[14,64,128]{2,1,0:T(8,128)(2,1)S(1)} %get-tuple-element.43.refs_5_), channel_id=1, source_target_pairs={{4,0},{0,4},{5,1},{1,5},{6,2},{2,6},{7,3},{3,7},{12,8},{8,12},{13,... | collective-permute-start | bytes 688136 | tf_op jit(solution)/shard_map/ppermute | solution.py:73
  9.6 1.0 %shard_map.130 = (bf16[14,64,128]{2,1,0:T(8,128)(2,1)S(1)}, bf16[16,64,128]{2,1,0:T(8,128)(2,1)S(1)}) custom-call(bf16[16,64,128]{2,1,0:T(8,128)(2,1)S(1)} %bitcast.13, bf16[16,64,128]{2,1,0:T(8,128)(2,1)S(1)} %bitcast.19, bf16[16,64,128]{2,1,0:T(8,128)(2,1)S(1)} %collective-permute-done.3.refs_2_.refs_6_, bf16[3,128,128]{2,1,0:T(8,128)(2,1)S(1)} %copy-done.6, ...), custom_call_target="tpu_custom_call" | custom-call | tf_op jit(solution)/shard_map/pallas_call | solution.py:38
  10.6 0.9 %shard_map.132 = (f32[2,384,128]{2,1,0:T(8,128)S(1)}, bf16[384,128]{1,0:T(8,128)(2,1)S(1)}, bf16[384,128]{1,0:T(8,128)(2,1)S(1)}) custom-call(bf16[16,64,128]{2,1,0:T(8,128)(2,1)S(1)} %bitcast.26, bf16[16,64,128]{2,1,0:T(8,128)(2,1)S(1)} %bitcast.20, bf16[16,64,128]{2,1,0:T(8,128)(2,1)S(1)} %get-tuple-element.46.refs_6_.refs_2_.refs_4_, ...), custom_call_target="tpu_custom_call" | custom-call | flops 2415919104 | bytes 2031616 | tf_op jit(solution)/shard_map/pallas_call | solution.py:38
  11.5 0.9 %collective-permute-start.6 = (bf16[384,128]{1,0:T(8,128)(2,1)S(1)}, bf16[384,128]{1,0:T(8,128)(2,1)S(1)}, u32[]{:S(2)}, u32[]{:S(2)}) collective-permute-start(bf16[384,128]{1,0:T(8,128)(2,1)S(1)} %get-tuple-element.48), channel_id=1, source_target_pairs={{8,0},{0,8},{24,16},{16,24},{9,1},{1,9},{25,17},{17,25},{10,2},{2,... | collective-permute-start | bytes 294920 | tf_op jit(solution)/shard_map/ppermute | solution.py:73
  12.4 0.8 %collective-permute-start.5 = (bf16[4,64,128]{2,1,0:T(8,128)(2,1)S(1)}, bf16[4,64,128]{2,1,0:T(8,128)(2,1)S(1)}, u32[]{:S(2)}, u32[]{:S(2)}) collective-permute-start(bf16[4,64,128]{2,1,0:T(8,128)(2,1)S(1)} %shard_map.131.refs_7_), channel_id=1, source_target_pairs={{4,0},{0,4},{5,1},{1,5},{6,2},{2,6},{7,3},{3,7},{12,8},{8,12},{13,... | collective-permute-start | bytes 196616 | tf_op jit(solution)/shard_map/ppermute | solution.py:73
  13.7 1.4 %collective-permute-start.8 = (bf16[384,128]{1,0:T(8,128)(2,1)S(1)}, bf16[384,128]{1,0:T(8,128)(2,1)S(1)}, u32[]{:S(2)}, u32[]{:S(2)}) collective-permute-start(bf16[384,128]{1,0:T(8,128)(2,1)S(1)} %get-tuple-element.54), channel_id=1, source_target_pairs={{16,0},{24,8},{0,16},{8,24},{17,1},{25,9},{1,17},{9,25},{18,2},{26... | collective-permute-start | bytes 294920 | tf_op jit(solution)/shard_map/ppermute | solution.py:73
  15.1 1.5 %collective-permute-done.5.refs_6_ = bf16[4,64,128]{2,1,0:T(8,128)(2,1)S(1)} collective-permute-done((bf16[4,64,128]{2,1,0:T(8,128)(2,1)S(1)}, bf16[4,64,128]{2,1,0:T(8,128)(2,1)S(1)}, u32[]{:S(2)}, u32[]{:S(2)}) %collective-permute-start.5) | collective-permute-done | bytes 65568 | tf_op jit(solution)/shard_map/ppermute | solution.py:73
  16.6 1.5 %shard_map.135 = (bf16[16,64,128]{2,1,0:T(8,128)(2,1)S(1)}, bf16[16,64,128]{2,1,0:T(8,128)(2,1)S(1)}, f32[2,384,128]{2,1,0:T(8,128)S(1)}, bf16[896,128]{1,0:T(8,128)(2,1)S(1)}) custom-call(bf16[16,64,128]{2,1,0:T(8,128)(2,1)S(1)} %bitcast.16, bf16[4,64,128]{2,1,0:T(8,128)(2,1)S(1)} %collective-permute-done.1.refs_4_.refs_1_.refs_3_.refs_2_, ...), custom_call_target="tpu_custom_call" | custom-call | flops 2415919104 | bytes 4128768 | tf_op jit(solution)/shard_map/pallas_call | solution.py:38
  18.2 1.2 %collective-permute-start.9 = (bf16[896,128]{1,0:T(8,128)(2,1)S(1)}, bf16[896,128]{1,0:T(8,128)(2,1)S(1)}, u32[]{:S(2)}, u32[]{:S(2)}) collective-permute-start(bf16[896,128]{1,0:T(8,128)(2,1)S(1)} %get-tuple-element.55), channel_id=1, source_target_pairs={{8,0},{0,8},{24,16},{16,24},{9,1},{1,9},{25,17},{17,25},{10,2},{2,... | collective-permute-start | bytes 688136 | tf_op jit(solution)/shard_map/ppermute | solution.py:73
  19.4 1.1 %collective-permute-done.9.refs_1_.refs_2_ = bf16[896,128]{1,0:T(8,128)(2,1)S(1)} collective-permute-done((bf16[896,128]{1,0:T(8,128)(2,1)S(1)}, bf16[896,128]{1,0:T(8,128)(2,1)S(1)}, u32[]{:S(2)}, u32[]{:S(2)}) %collective-permute-start.9) | collective-permute-done | bytes 229408 | tf_op jit(solution)/shard_map/ppermute | solution.py:73
  20.5 1.2 %collective-permute-start.10 = (bf16[256,128]{1,0:T(8,128)(2,1)S(1)}, bf16[256,128]{1,0:T(8,128)(2,1)S(1)}, u32[]{:S(2)}, u32[]{:S(2)}) collective-permute-start(bf16[256,128]{1,0:T(8,128)(2,1)S(1)} %get-tuple-element.58), channel_id=1, source_target_pairs={{16,0},{24,8},{0,16},{8,24},{17,1},{25,9},{1,17},{9,25},{18,2},{26... | collective-permute-start | bytes 196616 | tf_op jit(solution)/shard_map/ppermute | solution.py:73
  21.7 1.3 %collective-permute-start.13 = (bf16[192,128]{1,0:T(8,128)(2,1)S(1)}, bf16[192,128]{1,0:T(8,128)(2,1)S(1)}, u32[]{:S(2)}, u32[]{:S(2)}) collective-permute-start(bf16[192,128]{1,0:T(8,128)(2,1)S(1)} %get-tuple-element.57.refs_2_), channel_id=1, source_target_pairs={{4,0},{0,4},{5,1},{1,5},{6,2},{2,6},{7,3},{3,7},{12,8},{8,12},{13,... | collective-permute-start | bytes 147464 | tf_op jit(solution)/shard_map/ppermute | solution.py:73
  23.1 1.3 %collective-permute-start.12 = (bf16[192,128]{1,0:T(8,128)(2,1)S(1)}, bf16[192,128]{1,0:T(8,128)(2,1)S(1)}, u32[]{:S(2)}, u32[]{:S(2)}) collective-permute-start(bf16[192,128]{1,0:T(8,128)(2,1)S(1)} %get-tuple-element.61), channel_id=1, source_target_pairs={{20,0},{16,4},{28,8},{24,12},{4,16},{0,20},{12,24},{8,28},{21,1},{... | collective-permute-start | bytes 147464 | tf_op jit(solution)/shard_map/ppermute | solution.py:81
  24.8 1.4 %collective-permute-start.15 = (bf16[192,128]{1,0:T(8,128)(2,1)S(1)}, bf16[192,128]{1,0:T(8,128)(2,1)S(1)}, u32[]{:S(2)}, u32[]{:S(2)}) collective-permute-start(bf16[192,128]{1,0:T(8,128)(2,1)S(1)} %shard_map.139.refs_0_), channel_id=1, source_target_pairs={{1,0},{0,1},{3,2},{2,3},{5,4},{4,5},{7,6},{6,7},{9,8},{8,9},{11,10... | collective-permute-start | bytes 147464 | tf_op jit(solution)/shard_map/ppermute | solution.py:73
  26.4 0.8 %collective-permute-done.12.refs_3_ = bf16[192,128]{1,0:T(8,128)(2,1)S(1)} collective-permute-done((bf16[192,128]{1,0:T(8,128)(2,1)S(1)}, bf16[192,128]{1,0:T(8,128)(2,1)S(1)}, u32[]{:S(2)}, u32[]{:S(2)}) %collective-permute-start.12) | collective-permute-done | bytes 49184 | tf_op jit(solution)/shard_map/ppermute | solution.py:81
  27.3 1.4 %collective-permute-start.14 = (bf16[192,128]{1,0:T(8,128)(2,1)S(1)}, bf16[192,128]{1,0:T(8,128)(2,1)S(1)}, u32[]{:S(2)}, u32[]{:S(2)}) collective-permute-start(bf16[192,128]{1,0:T(8,128)(2,1)S(1)} %shard_map.138.refs_0_), channel_id=1, source_target_pairs={{1,0},{0,1},{3,2},{2,3},{5,4},{4,5},{7,6},{6,7},{9,8},{8,9},{11,10... | collective-permute-start | bytes 147464 | tf_op jit(solution)/shard_map/ppermute | solution.py:73
  28.6 2.4 %collective-permute-start.17 = (bf16[192,128]{1,0:T(8,128)(2,1)S(1)}, bf16[192,128]{1,0:T(8,128)(2,1)S(1)}, u32[]{:S(2)}, u32[]{:S(2)}) collective-permute-start(bf16[192,128]{1,0:T(8,128)(2,1)S(1)} %shard_map.142.refs_2_), channel_id=1, source_target_pairs={{2,0},{3,1},{0,2},{1,3},{6,4},{7,5},{4,6},{5,7},{10,8},{11,9},{8,1... | collective-permute-start | bytes 147464 | tf_op jit(solution)/shard_map/ppermute | solution.py:73
  31.1 2.4 %collective-permute-start.16 = (bf16[192,128]{1,0:T(8,128)(2,1)S(1)}, bf16[192,128]{1,0:T(8,128)(2,1)S(1)}, u32[]{:S(2)}, u32[]{:S(2)}) collective-permute-start(bf16[192,128]{1,0:T(8,128)(2,1)S(1)} %shard_map.140.refs_5_.refs_0_), channel_id=1, source_target_pairs={{2,0},{3,1},{0,2},{1,3},{6,4},{7,5},{4,6},{5,7},{10,8},{11,9},{8,1... | collective-permute-start | bytes 147464 | tf_op jit(solution)/shard_map/ppermute | solution.py:73
  33.5 1.5 %shard_map.141 = (bf16[16,64,128]{2,1,0:T(8,128)(2,1)}, f32[8,128]{1,0:T(8,128)S(1)}) custom-call(bf16[16,64,128]{2,1,0:T(8,128)(2,1)S(1)} %get-tuple-element.51.refs_0_, bf16[16,64,128]{2,1,0:T(8,128)(2,1)S(1)} %get-tuple-element.52.refs_1_, bf16[896,128]{1,0:T(8,128)(2,1)S(1)} %collective-permute-done.9.refs_1_.refs_2_, ...), custom_call_target="tpu_custom_call" | custom-call | flops 301989888 | bytes 1380352 | tf_op jit(solution)/shard_map/pallas_call | solution.py:38
  35.0 1.8 %collective-permute-start.21 = (bf16[2,192,128]{2,1,0:T(8,128)(2,1)S(1)}, bf16[2,192,128]{2,1,0:T(8,128)(2,1)S(1)}, u32[]{:S(2)}, u32[]{:S(2)}) collective-permute-start(bf16[2,192,128]{2,1,0:T(8,128)(2,1)S(1)} %shard_map.143.refs_0_), channel_id=1, source_target_pairs={{16,0},{24,8},{0,16},{8,24},{17,1},{25,9},{1,17},{9,25},{18,2},{26... | collective-permute-start | bytes 294920 | tf_op jit(solution)/shard_map/ppermute | solution.py:73
  36.8 1.7 %collective-permute-start.20 = (bf16[2,192,128]{2,1,0:T(8,128)(2,1)S(1)}, bf16[2,192,128]{2,1,0:T(8,128)(2,1)S(1)}, u32[]{:S(2)}, u32[]{:S(2)}) collective-permute-start(bf16[2,192,128]{2,1,0:T(8,128)(2,1)S(1)} %shard_map.143.refs_0_), channel_id=1, source_target_pairs={{4,0},{0,4},{5,1},{1,5},{6,2},{2,6},{7,3},{3,7},{12,8},{8,12},{13,... | collective-permute-start | bytes 294920 | tf_op jit(solution)/shard_map/ppermute | solution.py:73
  38.5 4.4 %collective-permute-start.22 = (bf16[2,192,128]{2,1,0:T(8,128)(2,1)S(1)}, bf16[2,192,128]{2,1,0:T(8,128)(2,1)S(1)}, u32[]{:S(2)}, u32[]{:S(2)}) collective-permute-start(bf16[2,192,128]{2,1,0:T(8,128)(2,1)S(1)} %shard_map.143.refs_0_), channel_id=1, source_target_pairs={{8,0},{0,8},{24,16},{16,24},{9,1},{1,9},{25,17},{17,25},{10,2},{2,... | collective-permute-start | bytes 294920 | tf_op jit(solution)/shard_map/ppermute | solution.py:73
  42.8 1.7 %collective-permute-start.24 = (bf16[2,192,128]{2,1,0:T(8,128)(2,1)S(1)}, bf16[2,192,128]{2,1,0:T(8,128)(2,1)S(1)}, u32[]{:S(2)}, u32[]{:S(2)}) collective-permute-start(bf16[2,192,128]{2,1,0:T(8,128)(2,1)S(1)} %collective-permute-done.21.refs_2_), channel_id=1, source_target_pairs={{8,0},{0,8},{24,16},{16,24},{9,1},{1,9},{25,17},{17,25},{10,2},{2,... | collective-permute-start | bytes 294920 | tf_op jit(solution)/shard_map/ppermute | solution.py:73
  44.6 2.1 %collective-permute-start.19 = (bf16[2,192,128]{2,1,0:T(8,128)(2,1)S(1)}, bf16[2,192,128]{2,1,0:T(8,128)(2,1)S(1)}, u32[]{:S(2)}, u32[]{:S(2)}) collective-permute-start(bf16[2,192,128]{2,1,0:T(8,128)(2,1)S(1)} %collective-permute-done.18.refs_0_), channel_id=1, source_target_pairs={{8,0},{0,8},{24,16},{16,24},{9,1},{1,9},{25,17},{17,25},{10,2},{2,... | collective-permute-start | bytes 294920 | tf_op jit(solution)/shard_map/ppermute | solution.py:73
  46.7 1.1 %shard_map.144 = (f32[3,384,128]{2,1,0:T(8,128)}, f32[384,128]{1,0:T(8,128)}, f32[3,384,128]{2,1,0:T(8,128)}, f32[384,128]{1,0:T(8,128)}) custom-call(bf16[2,192,128]{2,1,0:T(8,128)(2,1)S(1)} %shard_map.143.refs_0_, bf16[2,192,128]{2,1,0:T(8,128)(2,1)S(1)} %collective-permute-done.20.refs_1_, bf16[2,192,128]{2,1,0:T(8,128)(2,1)S(1)} %collective-permute-done.21.refs_2_, ...), custom_call_target="tpu_custom_call" | custom-call | bytes 1769472 | tf_op jit(solution)/shard_map/pallas_call | solution.py:447
  47.8 0.8 %shard_map.145 = (f32[3,384,128]{2,1,0:T(8,128)}, f32[384,128]{1,0:T(8,128)}, f32[3,384,128]{2,1,0:T(8,128)}, f32[384,128]{1,0:T(8,128)}) custom-call(bf16[2,192,128]{2,1,0:T(8,128)(2,1)S(1)} %collective-permute-done.18.refs_0_, ...), custom_call_target="tpu_custom_call", output_to_operand_aliasing={{0}: (2, {}), {1}: (3, {}), {2}: (4, {}), {3}: (5, {})} | custom-call | bytes 589824 | tf_op jit(solution)/shard_map/pallas_call | solution.py:447
  (54 shorter events, 1.7 us)
Async XLA Ops:
  0.6 8.9 %collective-permute-start.3 = (bf16[16,64,128]{2,1,0:T(8,128)(2,1)}, bf16[16,64,128]{2,1,0:T(8,128)(2,1)S(1)}, u32[]{:S(2)}, u32[]{:S(2)}) collective-permute-start(bf16[16,64,128]{2,1,0:T(8,128)(2,1)} %bitcast.10), channel_id=1, source_target_pairs={{4,0},{0,4},{5,1},{1,5},{6,2},{2,6},{7,3},{3,7},{12,8},{8,12},{13,... | collective-permute-start | bytes 786440 | tf_op jit(solution)/shard_map/ppermute | solution.py:73
  2.7 5.4 %copy-start = (bf16[1,1,16,64,128]{4,3,2,1,0:T(8,128)(2,1)S(1)}, bf16[1,1,16,64,128]{4,3,2,1,0:T(8,128)(2,1)}, u32[]{:S(2)}) copy-start(bf16[1,1,16,64,128]{4,3,2,1,0:T(8,128)(2,1)} %param.9) | copy-start | bytes 786436
  2.7 5.4 %copy-start.1 = (bf16[3,3,128,128]{3,2,1,0:T(8,128)(2,1)S(1)}, bf16[3,3,128,128]{3,2,1,0:T(8,128)(2,1)}, u32[]{:S(2)}) copy-start(bf16[3,3,128,128]{3,2,1,0:T(8,128)(2,1)} %refs_8_.1) | copy-start | bytes 884740
  2.7 5.4 %copy-start.2 = (bf16[1,1,16,64,128]{4,3,2,1,0:T(8,128)(2,1)S(1)}, bf16[1,1,16,64,128]{4,3,2,1,0:T(8,128)(2,1)}, u32[]{:S(2)}) copy-start(bf16[1,1,16,64,128]{4,3,2,1,0:T(8,128)(2,1)} %param.13) | copy-start | bytes 786436
  2.7 5.4 %copy-start.6 = (bf16[3,128,128]{2,1,0:T(8,128)(2,1)S(1)}, bf16[3,128,128]{2,1,0:T(8,128)(2,1)}, u32[]{:S(2)}) copy-start(bf16[3,128,128]{2,1,0:T(8,128)(2,1)} %refs_7_.1) | copy-start | bytes 294916
  4.4 2.1 %collective-permute-start = (bf16[4,64,128]{2,1,0:T(8,128)(2,1)}, bf16[4,64,128]{2,1,0:T(8,128)(2,1)S(1)}, u32[]{:S(2)}, u32[]{:S(2)}) collective-permute-start(bf16[4,64,128]{2,1,0:T(8,128)(2,1)} %get-tuple-element.41), channel_id=1, source_target_pairs={{8,0},{0,8},{24,16},{16,24},{9,1},{1,9},{25,17},{17,25},{10,2},{2,... | collective-permute-start | bytes 196616 | tf_op jit(solution)/shard_map/ppermute | solution.py:73
  6.5 3.0 %copy-start.5 = (bf16[1,1,16,64,128]{4,3,2,1,0:T(8,128)(2,1)S(1)}, bf16[1,1,16,64,128]{4,3,2,1,0:T(8,128)(2,1)}, u32[]{:S(2)}) copy-start(bf16[1,1,16,64,128]{4,3,2,1,0:T(8,128)(2,1)} %param.11) | copy-start | bytes 786436
  6.5 3.0 %copy-start.8 = (bf16[3,128,128]{2,1,0:T(8,128)(2,1)S(1)}, bf16[3,128,128]{2,1,0:T(8,128)(2,1)}, u32[]{:S(2)}) copy-start(bf16[3,128,128]{2,1,0:T(8,128)(2,1)} %refs_11_.1) | copy-start | bytes 294916
  6.5 1.7 %collective-permute-start.1 = (bf16[4,64,128]{2,1,0:T(8,128)(2,1)}, bf16[4,64,128]{2,1,0:T(8,128)(2,1)S(1)}, u32[]{:S(2)}, u32[]{:S(2)}) collective-permute-start(bf16[4,64,128]{2,1,0:T(8,128)(2,1)} %get-tuple-element.42), channel_id=1, source_target_pairs={{8,0},{0,8},{24,16},{16,24},{9,1},{1,9},{25,17},{17,25},{10,2},{2,... | collective-permute-start | bytes 196616 | tf_op jit(solution)/shard_map/ppermute | solution.py:73
  6.9 3.6 %collective-permute-start.2 = (bf16[4,64,128]{2,1,0:T(8,128)(2,1)S(1)}, bf16[4,64,128]{2,1,0:T(8,128)(2,1)S(1)}, u32[]{:S(2)}, u32[]{:S(2)}) collective-permute-start(bf16[4,64,128]{2,1,0:T(8,128)(2,1)S(1)} %collective-permute-done.refs_5_), channel_id=1, source_target_pairs={{16,0},{24,8},{0,16},{8,24},{17,1},{25,9},{1,17},{9,25},{18,2},{26... | collective-permute-start | bytes 196616 | tf_op jit(solution)/shard_map/ppermute | solution.py:73
  8.2 8.4 %collective-permute-start.4 = (bf16[14,64,128]{2,1,0:T(8,128)(2,1)S(1)}, bf16[14,64,128]{2,1,0:T(8,128)(2,1)S(1)}, u32[]{:S(2)}, u32[]{:S(2)}) collective-permute-start(bf16[14,64,128]{2,1,0:T(8,128)(2,1)S(1)} %get-tuple-element.43.refs_5_), channel_id=1, source_target_pairs={{4,0},{0,4},{5,1},{1,5},{6,2},{2,6},{7,3},{3,7},{12,8},{8,12},{13,... | collective-permute-start | bytes 688136 | tf_op jit(solution)/shard_map/ppermute | solution.py:73
  11.5 2.1 %collective-permute-start.6 = (bf16[384,128]{1,0:T(8,128)(2,1)S(1)}, bf16[384,128]{1,0:T(8,128)(2,1)S(1)}, u32[]{:S(2)}, u32[]{:S(2)}) collective-permute-start(bf16[384,128]{1,0:T(8,128)(2,1)S(1)} %get-tuple-element.48), channel_id=1, source_target_pairs={{8,0},{0,8},{24,16},{16,24},{9,1},{1,9},{25,17},{17,25},{10,2},{2,... | collective-permute-start | bytes 294920 | tf_op jit(solution)/shard_map/ppermute | solution.py:73
  12.4 1.3 %collective-permute-start.7 = (bf16[384,128]{1,0:T(8,128)(2,1)S(1)}, bf16[384,128]{1,0:T(8,128)(2,1)S(1)}, u32[]{:S(2)}, u32[]{:S(2)}) collective-permute-start(bf16[384,128]{1,0:T(8,128)(2,1)S(1)} %get-tuple-element.49), channel_id=1, source_target_pairs={{8,0},{0,8},{24,16},{16,24},{9,1},{1,9},{25,17},{17,25},{10,2},{2,... | collective-permute-start | bytes 294920 | tf_op jit(solution)/shard_map/ppermute | solution.py:73
  12.4 4.2 %collective-permute-start.5 = (bf16[4,64,128]{2,1,0:T(8,128)(2,1)S(1)}, bf16[4,64,128]{2,1,0:T(8,128)(2,1)S(1)}, u32[]{:S(2)}, u32[]{:S(2)}) collective-permute-start(bf16[4,64,128]{2,1,0:T(8,128)(2,1)S(1)} %shard_map.131.refs_7_), channel_id=1, source_target_pairs={{4,0},{0,4},{5,1},{1,5},{6,2},{2,6},{7,3},{3,7},{12,8},{8,12},{13,... | collective-permute-start | bytes 196616 | tf_op jit(solution)/shard_map/ppermute | solution.py:73
  13.7 4.4 %collective-permute-start.8 = (bf16[384,128]{1,0:T(8,128)(2,1)S(1)}, bf16[384,128]{1,0:T(8,128)(2,1)S(1)}, u32[]{:S(2)}, u32[]{:S(2)}) collective-permute-start(bf16[384,128]{1,0:T(8,128)(2,1)S(1)} %get-tuple-element.54), channel_id=1, source_target_pairs={{16,0},{24,8},{0,16},{8,24},{17,1},{25,9},{1,17},{9,25},{18,2},{26... | collective-permute-start | bytes 294920 | tf_op jit(solution)/shard_map/ppermute | solution.py:73
  18.2 2.3 %collective-permute-start.9 = (bf16[896,128]{1,0:T(8,128)(2,1)S(1)}, bf16[896,128]{1,0:T(8,128)(2,1)S(1)}, u32[]{:S(2)}, u32[]{:S(2)}) collective-permute-start(bf16[896,128]{1,0:T(8,128)(2,1)S(1)} %get-tuple-element.55), channel_id=1, source_target_pairs={{8,0},{0,8},{24,16},{16,24},{9,1},{1,9},{25,17},{17,25},{10,2},{2,... | collective-permute-start | bytes 688136 | tf_op jit(solution)/shard_map/ppermute | solution.py:73
  20.5 6.7 %collective-permute-start.10 = (bf16[256,128]{1,0:T(8,128)(2,1)S(1)}, bf16[256,128]{1,0:T(8,128)(2,1)S(1)}, u32[]{:S(2)}, u32[]{:S(2)}) collective-permute-start(bf16[256,128]{1,0:T(8,128)(2,1)S(1)} %get-tuple-element.58), channel_id=1, source_target_pairs={{16,0},{24,8},{0,16},{8,24},{17,1},{25,9},{1,17},{9,25},{18,2},{26... | collective-permute-start | bytes 196616 | tf_op jit(solution)/shard_map/ppermute | solution.py:73
  21.7 3.1 %collective-permute-start.13 = (bf16[192,128]{1,0:T(8,128)(2,1)S(1)}, bf16[192,128]{1,0:T(8,128)(2,1)S(1)}, u32[]{:S(2)}, u32[]{:S(2)}) collective-permute-start(bf16[192,128]{1,0:T(8,128)(2,1)S(1)} %get-tuple-element.57.refs_2_), channel_id=1, source_target_pairs={{4,0},{0,4},{5,1},{1,5},{6,2},{2,6},{7,3},{3,7},{12,8},{8,12},{13,... | collective-permute-start | bytes 147464 | tf_op jit(solution)/shard_map/ppermute | solution.py:73
  22.9 3.5 %collective-permute-start.11 = (bf16[192,128]{1,0:T(8,128)(2,1)S(1)}, bf16[192,128]{1,0:T(8,128)(2,1)S(1)}, u32[]{:S(2)}, u32[]{:S(2)}) collective-permute-start(bf16[192,128]{1,0:T(8,128)(2,1)S(1)} %get-tuple-element.60), channel_id=1, source_target_pairs={{4,0},{0,4},{5,1},{1,5},{6,2},{2,6},{7,3},{3,7},{12,8},{8,12},{13,... | collective-permute-start | bytes 147464 | tf_op jit(solution)/shard_map/ppermute | solution.py:73
  23.1 4.1 %collective-permute-start.12 = (bf16[192,128]{1,0:T(8,128)(2,1)S(1)}, bf16[192,128]{1,0:T(8,128)(2,1)S(1)}, u32[]{:S(2)}, u32[]{:S(2)}) collective-permute-start(bf16[192,128]{1,0:T(8,128)(2,1)S(1)} %get-tuple-element.61), channel_id=1, source_target_pairs={{20,0},{16,4},{28,8},{24,12},{4,16},{0,20},{12,24},{8,28},{21,1},{... | collective-permute-start | bytes 147464 | tf_op jit(solution)/shard_map/ppermute | solution.py:81
  24.8 3.8 %collective-permute-start.15 = (bf16[192,128]{1,0:T(8,128)(2,1)S(1)}, bf16[192,128]{1,0:T(8,128)(2,1)S(1)}, u32[]{:S(2)}, u32[]{:S(2)}) collective-permute-start(bf16[192,128]{1,0:T(8,128)(2,1)S(1)} %shard_map.139.refs_0_), channel_id=1, source_target_pairs={{1,0},{0,1},{3,2},{2,3},{5,4},{4,5},{7,6},{6,7},{9,8},{8,9},{11,10... | collective-permute-start | bytes 147464 | tf_op jit(solution)/shard_map/ppermute | solution.py:73
  27.2 6.2 %copy-start.7 = (bf16[3,3,128,128]{3,2,1,0:T(8,128)(2,1)S(1)}, bf16[3,3,128,128]{3,2,1,0:T(8,128)(2,1)}, u32[]{:S(2)}) copy-start(bf16[3,3,128,128]{3,2,1,0:T(8,128)(2,1)} %refs_4_.5) | copy-start | bytes 884740
  27.3 3.8 %collective-permute-start.14 = (bf16[192,128]{1,0:T(8,128)(2,1)S(1)}, bf16[192,128]{1,0:T(8,128)(2,1)S(1)}, u32[]{:S(2)}, u32[]{:S(2)}) collective-permute-start(bf16[192,128]{1,0:T(8,128)(2,1)S(1)} %shard_map.138.refs_0_), channel_id=1, source_target_pairs={{1,0},{0,1},{3,2},{2,3},{5,4},{4,5},{7,6},{6,7},{9,8},{8,9},{11,10... | collective-permute-start | bytes 147464 | tf_op jit(solution)/shard_map/ppermute | solution.py:73
  28.6 6.3 %collective-permute-start.17 = (bf16[192,128]{1,0:T(8,128)(2,1)S(1)}, bf16[192,128]{1,0:T(8,128)(2,1)S(1)}, u32[]{:S(2)}, u32[]{:S(2)}) collective-permute-start(bf16[192,128]{1,0:T(8,128)(2,1)S(1)} %shard_map.142.refs_2_), channel_id=1, source_target_pairs={{2,0},{3,1},{0,2},{1,3},{6,4},{7,5},{4,6},{5,7},{10,8},{11,9},{8,1... | collective-permute-start | bytes 147464 | tf_op jit(solution)/shard_map/ppermute | solution.py:73
  31.1 3.9 %collective-permute-start.16 = (bf16[192,128]{1,0:T(8,128)(2,1)S(1)}, bf16[192,128]{1,0:T(8,128)(2,1)S(1)}, u32[]{:S(2)}, u32[]{:S(2)}) collective-permute-start(bf16[192,128]{1,0:T(8,128)(2,1)S(1)} %shard_map.140.refs_5_.refs_0_), channel_id=1, source_target_pairs={{2,0},{3,1},{0,2},{1,3},{6,4},{7,5},{4,6},{5,7},{10,8},{11,9},{8,1... | collective-permute-start | bytes 147464 | tf_op jit(solution)/shard_map/ppermute | solution.py:73
  35.0 7.8 %collective-permute-start.21 = (bf16[2,192,128]{2,1,0:T(8,128)(2,1)S(1)}, bf16[2,192,128]{2,1,0:T(8,128)(2,1)S(1)}, u32[]{:S(2)}, u32[]{:S(2)}) collective-permute-start(bf16[2,192,128]{2,1,0:T(8,128)(2,1)S(1)} %shard_map.143.refs_0_), channel_id=1, source_target_pairs={{16,0},{24,8},{0,16},{8,24},{17,1},{25,9},{1,17},{9,25},{18,2},{26... | collective-permute-start | bytes 294920 | tf_op jit(solution)/shard_map/ppermute | solution.py:73
  36.8 7.8 %collective-permute-start.20 = (bf16[2,192,128]{2,1,0:T(8,128)(2,1)S(1)}, bf16[2,192,128]{2,1,0:T(8,128)(2,1)S(1)}, u32[]{:S(2)}, u32[]{:S(2)}) collective-permute-start(bf16[2,192,128]{2,1,0:T(8,128)(2,1)S(1)} %shard_map.143.refs_0_), channel_id=1, source_target_pairs={{4,0},{0,4},{5,1},{1,5},{6,2},{2,6},{7,3},{3,7},{12,8},{8,12},{13,... | collective-permute-start | bytes 294920 | tf_op jit(solution)/shard_map/ppermute | solution.py:73
  38.5 6.1 %collective-permute-start.18 = (bf16[2,192,128]{2,1,0:T(8,128)(2,1)S(1)}, bf16[2,192,128]{2,1,0:T(8,128)(2,1)S(1)}, u32[]{:S(2)}, u32[]{:S(2)}) collective-permute-start(bf16[2,192,128]{2,1,0:T(8,128)(2,1)S(1)} %shard_map.143.refs_0_), channel_id=1, source_target_pairs={{20,0},{16,4},{28,8},{24,12},{4,16},{0,20},{12,24},{8,28},{21,1},{... | collective-permute-start | bytes 294920 | tf_op jit(solution)/shard_map/ppermute | solution.py:81
  38.5 8.2 %collective-permute-start.22 = (bf16[2,192,128]{2,1,0:T(8,128)(2,1)S(1)}, bf16[2,192,128]{2,1,0:T(8,128)(2,1)S(1)}, u32[]{:S(2)}, u32[]{:S(2)}) collective-permute-start(bf16[2,192,128]{2,1,0:T(8,128)(2,1)S(1)} %shard_map.143.refs_0_), channel_id=1, source_target_pairs={{8,0},{0,8},{24,16},{16,24},{9,1},{1,9},{25,17},{17,25},{10,2},{2,... | collective-permute-start | bytes 294920 | tf_op jit(solution)/shard_map/ppermute | solution.py:73
  42.8 3.9 %collective-permute-start.24 = (bf16[2,192,128]{2,1,0:T(8,128)(2,1)S(1)}, bf16[2,192,128]{2,1,0:T(8,128)(2,1)S(1)}, u32[]{:S(2)}, u32[]{:S(2)}) collective-permute-start(bf16[2,192,128]{2,1,0:T(8,128)(2,1)S(1)} %collective-permute-done.21.refs_2_), channel_id=1, source_target_pairs={{8,0},{0,8},{24,16},{16,24},{9,1},{1,9},{25,17},{17,25},{10,2},{2,... | collective-permute-start | bytes 294920 | tf_op jit(solution)/shard_map/ppermute | solution.py:73
  44.6 2.1 %collective-permute-start.23 = (bf16[2,192,128]{2,1,0:T(8,128)(2,1)S(1)}, bf16[2,192,128]{2,1,0:T(8,128)(2,1)S(1)}, u32[]{:S(2)}, u32[]{:S(2)}) collective-permute-start(bf16[2,192,128]{2,1,0:T(8,128)(2,1)S(1)} %collective-permute-done.20.refs_1_), channel_id=1, source_target_pairs={{8,0},{0,8},{24,16},{16,24},{9,1},{1,9},{25,17},{17,25},{10,2},{2,... | collective-permute-start | bytes 294920 | tf_op jit(solution)/shard_map/ppermute | solution.py:73
  44.6 3.2 %collective-permute-start.19 = (bf16[2,192,128]{2,1,0:T(8,128)(2,1)S(1)}, bf16[2,192,128]{2,1,0:T(8,128)(2,1)S(1)}, u32[]{:S(2)}, u32[]{:S(2)}) collective-permute-start(bf16[2,192,128]{2,1,0:T(8,128)(2,1)S(1)} %collective-permute-done.18.refs_0_), channel_id=1, source_target_pairs={{8,0},{0,8},{24,16},{16,24},{9,1},{1,9},{25,17},{17,25},{10,2},{2,... | collective-permute-start | bytes 294920 | tf_op jit(solution)/shard_map/ppermute | solution.py:73
  (2 other events, 6.1 us)

commit v14 on v13

--- a/solution.py
+++ b/solution.py
@@ -282,18 +282,14 @@
     left_sides(saved_ref, preact_ref, *beside_band((one_ref, two_ref), 3), sides_ref)
 
 
-def block_one(sides_ref, preact_ref, mids, temporal_ref, outs, scratch):
-    gpre_ref, keep_ref, send_ref = outs
-    views_ref, sums_ref = scratch
-    rows, cols, ch = preact_ref.shape
-    step = 4
-
-    for n in range(rows // step):
-        here = pl.ds(n * step, step)
-        gpre = pre_gradient([ref[here] for ref in mids], preact_ref[here], temporal_ref)
-        gpre_ref[here] = gpre.astype(jnp.bfloat16)
-        beside(gpre, views_ref, n * step)
-
+def pre_rows(preact, mids, temporal_ref, gpre_ref, views_ref, start):
+    gpre = pre_gradient(mids, preact, temporal_ref)
+    gpre_ref[start : start + preact.shape[0]] = gpre.astype(jnp.bfloat16)
+    beside(gpre, views_ref, start)
+
+
+def block_sums(gpre_ref, sides_ref, mids, views_ref, sums_ref, keep_ref, send_ref):
+    rows, cols, ch = gpre_ref.shape
     odd = lax.rem(lax.axis_index("section"), 2)
     size = send_ref.shape[0] - 2 * cols
     send_ref[size : size + cols] = gpre_ref[(1 - odd) * (rows - 1)]
@@ -307,14 +303,31 @@
 def one_kernel(later, *refs):
     sides_ref, preact_ref, mids = refs[0], refs[1], refs[2 : 3 + later]
     temporal_ref, outs, scratch = refs[3 + later], refs[4 + later : 7 + later], refs[7 + later :]
-    block_one(sides_ref, preact_ref, mids, temporal_ref, outs, scratch)
+    gpre_ref, keep_ref, send_ref = outs
+    views_ref, sums_ref = scratch
+    for n in range(preact_ref.shape[0] // 4):
+        here = slice(4 * n, 4 * n + 4)
+        grads = [ref[here] for ref in mids]
+        pre_rows(preact_ref[here], grads, temporal_ref, gpre_ref, views_ref, 4 * n)
+    block_sums(gpre_ref, sides_ref, mids, views_ref, sums_ref, keep_ref, send_ref)
+
+
+def one_inner_kernel(preact_ref, inner_ref, after_ref, temporal_ref, gpre_ref, views_ref):
+    rows = inner_ref.shape[0]
+    for n in range(rows // 7):
+        here = slice(7 * n, 7 * n + 7)
+        after = after_ref[here]
+        after = jnp.where(is_last(), jnp.zeros_like(after), after)
+        preact = preact_ref[7 * n + 1 : 7 * n + 8]
+        pre_rows(preact, [inner_ref[here], after], temporal_ref, gpre_ref, views_ref, 7 * n)
 
 
 def mid_one_kernel(*refs):
     after_inner_ref, after_edge_ref = refs[5:7]
     temporal_two_ref, spatial_two_ref, sides_ref, preact_ref, temporal_ref = refs[7:12]
-    mid_ref, outs, scratch = refs[12], refs[13:16], refs[16:18]
-    next_ref, edge_ref, edge_views_ref = refs[18:]
+    inner_gpre_ref, inner_views_ref = refs[12:14]
+    mid_ref, gpre_ref, keep_ref, send_ref = refs[14:18]
+    views_ref, sums_ref, next_ref, edge_ref, edge_views_ref = refs[18:]
     rows = next_ref.shape[0]
 
     @pl.when(is_last())
@@ -332,7 +345,13 @@
     mid_kernel(
         1, *refs[:5], edge_ref, temporal_two_ref, spatial_two_ref, mid_ref, edge_views_ref
     )
-    block_one(sides_ref, preact_ref, [mid_ref, next_ref], temporal_ref, outs, scratch)
+    gpre_ref[1 : rows - 1] = inner_gpre_ref[...]
+    views_ref[1 : rows - 1] = inner_views_ref[...]
+    for row in (0, rows - 1):
+        here = slice(row, row + 1)
+        grads = [mid_ref[here], next_ref[here]]
+        pre_rows(preact_ref[here], grads, temporal_ref, gpre_ref, views_ref, row)
+    block_sums(gpre_ref, sides_ref, [mid_ref, next_ref], views_ref, sums_ref, keep_ref, send_ref)
 
 
 def input_kernel(mid_ref, gpre_ref, pair_ref, across_ref, spatial_ref, out_ref, token_ref, views_ref):
@@ -592,6 +611,16 @@
     mid_outs = [bf16(rows, cols, ch)]
     one_outs = [bf16(rows, cols, ch), f32(2, 3 * ch, ch), bf16(6 * ch + 2 * cols, ch)]
     if frames == 2:
+        inners_one = call(
+            one_inner_kernel,
+            [bf16(rows - 2, cols, ch), bf16(rows - 2, cols, 3 * ch)],
+            [],
+            conv // 8,
+            pre_one,
+            inner,
+            afters[0],
+            temporal_one,
+        )
         mid, gpre_one, *parts_one = call(
             mid_one_kernel,
             mid_outs + one_outs,
@@ -602,6 +631,7 @@
             *kernels,
             *one_inputs,
             temporal_one,
+            *inners_one,
             after=(own_two,),
         )
     else:
@@ -660,7 +690,7 @@
         sum_two = added(keep_two, flipped(send_two, "video", 1))
         quarters = [f32(half, ch), bf16(half + cols, ch)] + [bf16(half, ch)] * 2
         own_one, *sends = call(
-            pair_quarter_kernel, quarters, [], height * ch, keep_one, pair_one, after=(send_two,)
+            pair_quarter_kernel, quarters, [], 8 * conv, keep_one, pair_one, after=(send_two,)
         )
         across = flipped(sends[0], "section", 2)
         parts = [across, flipped(sends[1], "video", 1), flipped_both(sends[2])]

time: 48.9 us -> 48.7 us (level)
    ppermute x23, starting transfers between devices: 32.1 us -> 31.6 us  [flipped(): lax.ppermute(block, axis, [(place ^ flip, place) for place in range(count)])]
    pallas_call x16 -> x17, Pallas kernels: 7.12 us -> 7.36 us  [call(): pl.pallas_call(body, out_shape=outs[0] if single else tuple(outs), in_spe...]
  transfers between devices with their start and end apart: 25 -> 25, of which waited for: 8 -> 7; matrix products, arithmetic and copies ran while one was open for 0% -> 0% of each run, Pallas kernels for 17% -> 17%
where the time goes in v14:
time: 48.7 us; the launch traced here: 48.4 us
  starting transfers between devices  33.3 us (68%)
  Pallas kernels  9.27 us (19%)
  waiting for transfers between devices  4.93 us (10%)
  between operations  0.83 us (2%)
    ppermute x23, starting transfers between devices, flipped(): lax.ppermute(block, axis, [(place ^ flip, place) for place in range(count)])  31.6 us
    pallas_call x17, Pallas kernels, call(): pl.pallas_call(body, out_shape=outs[0] if single else tuple(outs), in_spe...  7.36 us
    ppermute x23, waiting for transfers between devices, flipped(): lax.ppermute(block, axis, [(place ^ flip, place) for place in range(count)])  4.17 us
    pallas_call x2, Pallas kernels, placed(): pl.pallas_call(functools.partial(place_kernel, places), out_shape=outs, i...  1.91 us
    ppermute x2, starting transfers between devices, flipped_both(): return lax.ppermute(block, ('section', 'video'), pairs)  1.75 us
  transfers between devices with their start and end apart: 25, of which 7 were waited for; matrix products, arithmetic and copies ran while one was open for 0% of the time, Pallas kernels for 17%

profile of v14, /device:TPU:1, one launch (start us, length us, event | category | flops | bytes accessed | tf_op | source)
XLA Modules:
  0.0 48.4 jit_solution(2247196730967597325)
XLA Ops:
  0.6 2.1 %collective-permute-start.3 = (bf16[16,64,128]{2,1,0:T(8,128)(2,1)}, bf16[16,64,128]{2,1,0:T(8,128)(2,1)S(1)}, u32[]{:S(2)}, u32[]{:S(2)}) collective-permute-start(bf16[16,64,128]{2,1,0:T(8,128)(2,1)} %bitcast.10), channel_id=1, source_target_pairs={{4,0},{0,4},{5,1},{1,5},{6,2},{2,6},{7,3},{3,7},{12,8},{8,12},{13,... | collective-permute-start | bytes 786440 | tf_op jit(solution)/shard_map/ppermute | solution.py:73
  2.7 1.6 %shard_map.128 = (bf16[4,64,128]{2,1,0:T(8,128)(2,1)}, bf16[4,64,128]{2,1,0:T(8,128)(2,1)}) custom-call(bf16[16,64,128]{2,1,0:T(8,128)(2,1)} %bitcast.11, bf16[16,64,128]{2,1,0:T(8,128)(2,1)} %bitcast.17, bf16[16,64,128]{2,1,0:T(8,128)(2,1)} %bitcast.28, bf16[16,64,128]{2,1,0:T(8,128)(2,1)} %bitcast.25), custom_call_target="tpu_custom_call" | custom-call | flops 1 | bytes 1179648 | tf_op jit(solution)/shard_map/pallas_call | solution.py:38
  4.4 1.0 %collective-permute-start = (bf16[4,64,128]{2,1,0:T(8,128)(2,1)}, bf16[4,64,128]{2,1,0:T(8,128)(2,1)S(1)}, u32[]{:S(2)}, u32[]{:S(2)}) collective-permute-start(bf16[4,64,128]{2,1,0:T(8,128)(2,1)} %get-tuple-element.43), channel_id=1, source_target_pairs={{8,0},{0,8},{24,16},{16,24},{9,1},{1,9},{25,17},{17,25},{10,2},{2,... | collective-permute-start | bytes 196616 | tf_op jit(solution)/shard_map/ppermute | solution.py:73
  5.4 1.1 %collective-permute-done.refs_5_ = bf16[4,64,128]{2,1,0:T(8,128)(2,1)S(1)} collective-permute-done((bf16[4,64,128]{2,1,0:T(8,128)(2,1)}, bf16[4,64,128]{2,1,0:T(8,128)(2,1)S(1)}, u32[]{:S(2)}, u32[]{:S(2)}) %collective-permute-start) | collective-permute-done | bytes 65568 | tf_op jit(solution)/shard_map/ppermute | solution.py:73
  6.9 1.2 %collective-permute-start.2 = (bf16[4,64,128]{2,1,0:T(8,128)(2,1)S(1)}, bf16[4,64,128]{2,1,0:T(8,128)(2,1)S(1)}, u32[]{:S(2)}, u32[]{:S(2)}) collective-permute-start(bf16[4,64,128]{2,1,0:T(8,128)(2,1)S(1)} %collective-permute-done.refs_5_), channel_id=1, source_target_pairs={{16,0},{24,8},{0,16},{8,24},{17,1},{25,9},{1,17},{9,25},{18,2},{26... | collective-permute-start | bytes 196616 | tf_op jit(solution)/shard_map/ppermute | solution.py:73
  8.2 1.3 %collective-permute-start.4 = (bf16[14,64,128]{2,1,0:T(8,128)(2,1)S(1)}, bf16[14,64,128]{2,1,0:T(8,128)(2,1)S(1)}, u32[]{:S(2)}, u32[]{:S(2)}) collective-permute-start(bf16[14,64,128]{2,1,0:T(8,128)(2,1)S(1)} %get-tuple-element.45.refs_5_), channel_id=1, source_target_pairs={{4,0},{0,4},{5,1},{1,5},{6,2},{2,6},{7,3},{3,7},{12,8},{8,12},{13,... | collective-permute-start | bytes 688136 | tf_op jit(solution)/shard_map/ppermute | solution.py:73
  9.6 1.0 %shard_map.130 = (bf16[14,64,128]{2,1,0:T(8,128)(2,1)S(1)}, bf16[16,64,128]{2,1,0:T(8,128)(2,1)S(1)}) custom-call(bf16[16,64,128]{2,1,0:T(8,128)(2,1)S(1)} %bitcast.13, bf16[16,64,128]{2,1,0:T(8,128)(2,1)S(1)} %bitcast.19, bf16[16,64,128]{2,1,0:T(8,128)(2,1)S(1)} %collective-permute-done.3.refs_2_.refs_6_, bf16[3,128,128]{2,1,0:T(8,128)(2,1)S(1)} %copy-done.6, ...), custom_call_target="tpu_custom_call" | custom-call | tf_op jit(solution)/shard_map/pallas_call | solution.py:38
  10.6 0.9 %shard_map.132 = (f32[2,384,128]{2,1,0:T(8,128)S(1)}, bf16[384,128]{1,0:T(8,128)(2,1)S(1)}, bf16[384,128]{1,0:T(8,128)(2,1)S(1)}) custom-call(bf16[16,64,128]{2,1,0:T(8,128)(2,1)S(1)} %bitcast.30, bf16[16,64,128]{2,1,0:T(8,128)(2,1)S(1)} %bitcast.20, bf16[16,64,128]{2,1,0:T(8,128)(2,1)S(1)} %get-tuple-element.48.refs_6_.refs_2_.refs_4_, ...), custom_call_target="tpu_custom_call" | custom-call | flops 2415919104 | bytes 2031616 | tf_op jit(solution)/shard_map/pallas_call | solution.py:38
  11.5 0.9 %collective-permute-start.6 = (bf16[384,128]{1,0:T(8,128)(2,1)S(1)}, bf16[384,128]{1,0:T(8,128)(2,1)S(1)}, u32[]{:S(2)}, u32[]{:S(2)}) collective-permute-start(bf16[384,128]{1,0:T(8,128)(2,1)S(1)} %get-tuple-element.52), channel_id=1, source_target_pairs={{8,0},{0,8},{24,16},{16,24},{9,1},{1,9},{25,17},{17,25},{10,2},{2,... | collective-permute-start | bytes 294920 | tf_op jit(solution)/shard_map/ppermute | solution.py:73
  12.4 0.8 %collective-permute-start.5 = (bf16[4,64,128]{2,1,0:T(8,128)(2,1)S(1)}, bf16[4,64,128]{2,1,0:T(8,128)(2,1)S(1)}, u32[]{:S(2)}, u32[]{:S(2)}) collective-permute-start(bf16[4,64,128]{2,1,0:T(8,128)(2,1)S(1)} %shard_map.131.refs_7_), channel_id=1, source_target_pairs={{4,0},{0,4},{5,1},{1,5},{6,2},{2,6},{7,3},{3,7},{12,8},{8,12},{13,... | collective-permute-start | bytes 196616 | tf_op jit(solution)/shard_map/ppermute | solution.py:73
  13.7 1.4 %collective-permute-start.8 = (bf16[384,128]{1,0:T(8,128)(2,1)S(1)}, bf16[384,128]{1,0:T(8,128)(2,1)S(1)}, u32[]{:S(2)}, u32[]{:S(2)}) collective-permute-start(bf16[384,128]{1,0:T(8,128)(2,1)S(1)} %get-tuple-element.58), channel_id=1, source_target_pairs={{16,0},{24,8},{0,16},{8,24},{17,1},{25,9},{1,17},{9,25},{18,2},{26... | collective-permute-start | bytes 294920 | tf_op jit(solution)/shard_map/ppermute | solution.py:73
  15.6 1.0 %collective-permute-done.5.refs_6_ = bf16[4,64,128]{2,1,0:T(8,128)(2,1)S(1)} collective-permute-done((bf16[4,64,128]{2,1,0:T(8,128)(2,1)S(1)}, bf16[4,64,128]{2,1,0:T(8,128)(2,1)S(1)}, u32[]{:S(2)}, u32[]{:S(2)}) %collective-permute-start.5) | collective-permute-done | bytes 65568 | tf_op jit(solution)/shard_map/ppermute | solution.py:73
  16.6 1.3 %shard_map.136 = (bf16[16,64,128]{2,1,0:T(8,128)(2,1)S(1)}, bf16[16,64,128]{2,1,0:T(8,128)(2,1)S(1)}, f32[2,384,128]{2,1,0:T(8,128)S(1)}, bf16[896,128]{1,0:T(8,128)(2,1)S(1)}) custom-call(bf16[16,64,128]{2,1,0:T(8,128)(2,1)S(1)} %bitcast.16, bf16[4,64,128]{2,1,0:T(8,128)(2,1)S(1)} %collective-permute-done.1.refs_4_.refs_1_.refs_3_.refs_2_, ...), custom_call_target="tpu_custom_call" | custom-call | flops 2415919104 | bytes 5046272 | tf_op jit(solution)/shard_map/pallas_call | solution.py:38
  17.9 1.2 %collective-permute-start.9 = (bf16[896,128]{1,0:T(8,128)(2,1)S(1)}, bf16[896,128]{1,0:T(8,128)(2,1)S(1)}, u32[]{:S(2)}, u32[]{:S(2)}) collective-permute-start(bf16[896,128]{1,0:T(8,128)(2,1)S(1)} %get-tuple-element.59), channel_id=1, source_target_pairs={{8,0},{0,8},{24,16},{16,24},{9,1},{1,9},{25,17},{17,25},{10,2},{2,... | collective-permute-start | bytes 688136 | tf_op jit(solution)/shard_map/ppermute | solution.py:73
  19.1 1.1 %collective-permute-done.9.refs_1_.refs_2_ = bf16[896,128]{1,0:T(8,128)(2,1)S(1)} collective-permute-done((bf16[896,128]{1,0:T(8,128)(2,1)S(1)}, bf16[896,128]{1,0:T(8,128)(2,1)S(1)}, u32[]{:S(2)}, u32[]{:S(2)}) %collective-permute-start.9) | collective-permute-done | bytes 229408 | tf_op jit(solution)/shard_map/ppermute | solution.py:73
  20.3 1.3 %collective-permute-start.10 = (bf16[256,128]{1,0:T(8,128)(2,1)S(1)}, bf16[256,128]{1,0:T(8,128)(2,1)S(1)}, u32[]{:S(2)}, u32[]{:S(2)}) collective-permute-start(bf16[256,128]{1,0:T(8,128)(2,1)S(1)} %get-tuple-element.62), channel_id=1, source_target_pairs={{16,0},{24,8},{0,16},{8,24},{17,1},{25,9},{1,17},{9,25},{18,2},{26... | collective-permute-start | bytes 196616 | tf_op jit(solution)/shard_map/ppermute | solution.py:73
  21.6 1.1 %collective-permute-start.13 = (bf16[192,128]{1,0:T(8,128)(2,1)S(1)}, bf16[192,128]{1,0:T(8,128)(2,1)S(1)}, u32[]{:S(2)}, u32[]{:S(2)}) collective-permute-start(bf16[192,128]{1,0:T(8,128)(2,1)S(1)} %get-tuple-element.61.refs_2_), channel_id=1, source_target_pairs={{4,0},{0,4},{5,1},{1,5},{6,2},{2,6},{7,3},{3,7},{12,8},{8,12},{13,... | collective-permute-start | bytes 147464 | tf_op jit(solution)/shard_map/ppermute | solution.py:73
  23.1 1.2 %collective-permute-start.12 = (bf16[192,128]{1,0:T(8,128)(2,1)S(1)}, bf16[192,128]{1,0:T(8,128)(2,1)S(1)}, u32[]{:S(2)}, u32[]{:S(2)}) collective-permute-start(bf16[192,128]{1,0:T(8,128)(2,1)S(1)} %get-tuple-element.65), channel_id=1, source_target_pairs={{20,0},{16,4},{28,8},{24,12},{4,16},{0,20},{12,24},{8,28},{21,1},{... | collective-permute-start | bytes 147464 | tf_op jit(solution)/shard_map/ppermute | solution.py:81
  24.6 1.4 %collective-permute-start.15 = (bf16[192,128]{1,0:T(8,128)(2,1)S(1)}, bf16[192,128]{1,0:T(8,128)(2,1)S(1)}, u32[]{:S(2)}, u32[]{:S(2)}) collective-permute-start(bf16[192,128]{1,0:T(8,128)(2,1)S(1)} %shard_map.140.refs_0_), channel_id=1, source_target_pairs={{1,0},{0,1},{3,2},{2,3},{5,4},{4,5},{7,6},{6,7},{9,8},{8,9},{11,10... | collective-permute-start | bytes 147464 | tf_op jit(solution)/shard_map/ppermute | solution.py:73
  26.4 0.8 %collective-permute-done.12.refs_3_ = bf16[192,128]{1,0:T(8,128)(2,1)S(1)} collective-permute-done((bf16[192,128]{1,0:T(8,128)(2,1)S(1)}, bf16[192,128]{1,0:T(8,128)(2,1)S(1)}, u32[]{:S(2)}, u32[]{:S(2)}) %collective-permute-start.12) | collective-permute-done | bytes 49184 | tf_op jit(solution)/shard_map/ppermute | solution.py:81
  27.2 1.3 %collective-permute-start.14 = (bf16[192,128]{1,0:T(8,128)(2,1)S(1)}, bf16[192,128]{1,0:T(8,128)(2,1)S(1)}, u32[]{:S(2)}, u32[]{:S(2)}) collective-permute-start(bf16[192,128]{1,0:T(8,128)(2,1)S(1)} %shard_map.139.refs_0_), channel_id=1, source_target_pairs={{1,0},{0,1},{3,2},{2,3},{5,4},{4,5},{7,6},{6,7},{9,8},{8,9},{11,10... | collective-permute-start | bytes 147464 | tf_op jit(solution)/shard_map/ppermute | solution.py:73
  28.6 2.4 %collective-permute-start.17 = (bf16[192,128]{1,0:T(8,128)(2,1)S(1)}, bf16[192,128]{1,0:T(8,128)(2,1)S(1)}, u32[]{:S(2)}, u32[]{:S(2)}) collective-permute-start(bf16[192,128]{1,0:T(8,128)(2,1)S(1)} %shard_map.143.refs_2_), channel_id=1, source_target_pairs={{2,0},{3,1},{0,2},{1,3},{6,4},{7,5},{4,6},{5,7},{10,8},{11,9},{8,1... | collective-permute-start | bytes 147464 | tf_op jit(solution)/shard_map/ppermute | solution.py:73
  31.0 2.3 %collective-permute-start.16 = (bf16[192,128]{1,0:T(8,128)(2,1)S(1)}, bf16[192,128]{1,0:T(8,128)(2,1)S(1)}, u32[]{:S(2)}, u32[]{:S(2)}) collective-permute-start(bf16[192,128]{1,0:T(8,128)(2,1)S(1)} %shard_map.141.refs_5_.refs_0_), channel_id=1, source_target_pairs={{2,0},{3,1},{0,2},{1,3},{6,4},{7,5},{4,6},{5,7},{10,8},{11,9},{8,1... | collective-permute-start | bytes 147464 | tf_op jit(solution)/shard_map/ppermute | solution.py:73
  33.3 1.5 %shard_map.142 = (bf16[16,64,128]{2,1,0:T(8,128)(2,1)}, f32[8,128]{1,0:T(8,128)S(1)}) custom-call(bf16[16,64,128]{2,1,0:T(8,128)(2,1)S(1)} %get-tuple-element.55.refs_0_, bf16[16,64,128]{2,1,0:T(8,128)(2,1)S(1)} %get-tuple-element.56.refs_1_, bf16[896,128]{1,0:T(8,128)(2,1)S(1)} %collective-permute-done.9.refs_1_.refs_2_, ...), custom_call_target="tpu_custom_call" | custom-call | flops 301989888 | bytes 1380352 | tf_op jit(solution)/shard_map/pallas_call | solution.py:38
  34.9 0.9 %collective-permute-start.20 = (bf16[2,192,128]{2,1,0:T(8,128)(2,1)S(1)}, bf16[2,192,128]{2,1,0:T(8,128)(2,1)S(1)}, u32[]{:S(2)}, u32[]{:S(2)}) collective-permute-start(bf16[2,192,128]{2,1,0:T(8,128)(2,1)S(1)} %shard_map.144.refs_0_), channel_id=1, source_target_pairs={{4,0},{0,4},{5,1},{1,5},{6,2},{2,6},{7,3},{3,7},{12,8},{8,12},{13,... | collective-permute-start | bytes 294920 | tf_op jit(solution)/shard_map/ppermute | solution.py:73
  35.8 2.4 %collective-permute-start.21 = (bf16[2,192,128]{2,1,0:T(8,128)(2,1)S(1)}, bf16[2,192,128]{2,1,0:T(8,128)(2,1)S(1)}, u32[]{:S(2)}, u32[]{:S(2)}) collective-permute-start(bf16[2,192,128]{2,1,0:T(8,128)(2,1)S(1)} %shard_map.144.refs_0_), channel_id=1, source_target_pairs={{16,0},{24,8},{0,16},{8,24},{17,1},{25,9},{1,17},{9,25},{18,2},{26... | collective-permute-start | bytes 294920 | tf_op jit(solution)/shard_map/ppermute | solution.py:73
  38.8 4.1 %collective-permute-start.22 = (bf16[2,192,128]{2,1,0:T(8,128)(2,1)S(1)}, bf16[2,192,128]{2,1,0:T(8,128)(2,1)S(1)}, u32[]{:S(2)}, u32[]{:S(2)}) collective-permute-start(bf16[2,192,128]{2,1,0:T(8,128)(2,1)S(1)} %shard_map.144.refs_0_), channel_id=1, source_target_pairs={{8,0},{0,8},{24,16},{16,24},{9,1},{1,9},{25,17},{17,25},{10,2},{2,... | collective-permute-start | bytes 294920 | tf_op jit(solution)/shard_map/ppermute | solution.py:73
  42.9 1.1 %collective-permute-start.23 = (bf16[2,192,128]{2,1,0:T(8,128)(2,1)S(1)}, bf16[2,192,128]{2,1,0:T(8,128)(2,1)S(1)}, u32[]{:S(2)}, u32[]{:S(2)}) collective-permute-start(bf16[2,192,128]{2,1,0:T(8,128)(2,1)S(1)} %collective-permute-done.20.refs_1_), channel_id=1, source_target_pairs={{8,0},{0,8},{24,16},{16,24},{9,1},{1,9},{25,17},{17,25},{10,2},{2,... | collective-permute-start | bytes 294920 | tf_op jit(solution)/shard_map/ppermute | solution.py:73
  44.0 1.1 %collective-permute-start.24 = (bf16[2,192,128]{2,1,0:T(8,128)(2,1)S(1)}, bf16[2,192,128]{2,1,0:T(8,128)(2,1)S(1)}, u32[]{:S(2)}, u32[]{:S(2)}) collective-permute-start(bf16[2,192,128]{2,1,0:T(8,128)(2,1)S(1)} %collective-permute-done.21.refs_2_), channel_id=1, source_target_pairs={{8,0},{0,8},{24,16},{16,24},{9,1},{1,9},{25,17},{17,25},{10,2},{2,... | collective-permute-start | bytes 294920 | tf_op jit(solution)/shard_map/ppermute | solution.py:73
  45.1 1.4 %collective-permute-start.19 = (bf16[2,192,128]{2,1,0:T(8,128)(2,1)S(1)}, bf16[2,192,128]{2,1,0:T(8,128)(2,1)S(1)}, u32[]{:S(2)}, u32[]{:S(2)}) collective-permute-start(bf16[2,192,128]{2,1,0:T(8,128)(2,1)S(1)} %collective-permute-done.18.refs_0_), channel_id=1, source_target_pairs={{8,0},{0,8},{24,16},{16,24},{9,1},{1,9},{25,17},{17,25},{10,2},{2,... | collective-permute-start | bytes 294920 | tf_op jit(solution)/shard_map/ppermute | solution.py:73
  46.5 1.1 %shard_map.145 = (f32[3,384,128]{2,1,0:T(8,128)}, f32[384,128]{1,0:T(8,128)}, f32[3,384,128]{2,1,0:T(8,128)}, f32[384,128]{1,0:T(8,128)}) custom-call(bf16[2,192,128]{2,1,0:T(8,128)(2,1)S(1)} %shard_map.144.refs_0_, bf16[2,192,128]{2,1,0:T(8,128)(2,1)S(1)} %collective-permute-done.20.refs_1_, bf16[2,192,128]{2,1,0:T(8,128)(2,1)S(1)} %collective-permute-done.21.refs_2_, ...), custom_call_target="tpu_custom_call" | custom-call | bytes 1769472 | tf_op jit(solution)/shard_map/pallas_call | solution.py:466
  47.6 0.8 %shard_map.146 = (f32[3,384,128]{2,1,0:T(8,128)}, f32[384,128]{1,0:T(8,128)}, f32[3,384,128]{2,1,0:T(8,128)}, f32[384,128]{1,0:T(8,128)}) custom-call(bf16[2,192,128]{2,1,0:T(8,128)(2,1)S(1)} %collective-permute-done.18.refs_0_, ...), custom_call_target="tpu_custom_call", output_to_operand_aliasing={{0}: (2, {}), {1}: (3, {}), {2}: (4, {}), {3}: (5, {})} | custom-call | bytes 589824 | tf_op jit(solution)/shard_map/pallas_call | solution.py:466
  (55 shorter events, 3.5 us)
Async XLA Ops:
  0.6 8.9 %collective-permute-start.3 = (bf16[16,64,128]{2,1,0:T(8,128)(2,1)}, bf16[16,64,128]{2,1,0:T(8,128)(2,1)S(1)}, u32[]{:S(2)}, u32[]{:S(2)}) collective-permute-start(bf16[16,64,128]{2,1,0:T(8,128)(2,1)} %bitcast.10), channel_id=1, source_target_pairs={{4,0},{0,4},{5,1},{1,5},{6,2},{2,6},{7,3},{3,7},{12,8},{8,12},{13,... | collective-permute-start | bytes 786440 | tf_op jit(solution)/shard_map/ppermute | solution.py:73
  2.7 5.4 %copy-start = (bf16[1,1,16,64,128]{4,3,2,1,0:T(8,128)(2,1)S(1)}, bf16[1,1,16,64,128]{4,3,2,1,0:T(8,128)(2,1)}, u32[]{:S(2)}) copy-start(bf16[1,1,16,64,128]{4,3,2,1,0:T(8,128)(2,1)} %param.9) | copy-start | bytes 786436
  2.7 5.4 %copy-start.1 = (bf16[3,3,128,128]{3,2,1,0:T(8,128)(2,1)S(1)}, bf16[3,3,128,128]{3,2,1,0:T(8,128)(2,1)}, u32[]{:S(2)}) copy-start(bf16[3,3,128,128]{3,2,1,0:T(8,128)(2,1)} %refs_8_.1) | copy-start | bytes 884740
  2.7 5.4 %copy-start.2 = (bf16[1,1,16,64,128]{4,3,2,1,0:T(8,128)(2,1)S(1)}, bf16[1,1,16,64,128]{4,3,2,1,0:T(8,128)(2,1)}, u32[]{:S(2)}) copy-start(bf16[1,1,16,64,128]{4,3,2,1,0:T(8,128)(2,1)} %param.13) | copy-start | bytes 786436
  2.7 5.4 %copy-start.6 = (bf16[3,128,128]{2,1,0:T(8,128)(2,1)S(1)}, bf16[3,128,128]{2,1,0:T(8,128)(2,1)}, u32[]{:S(2)}) copy-start(bf16[3,128,128]{2,1,0:T(8,128)(2,1)} %refs_7_.1) | copy-start | bytes 294916
  4.4 2.1 %collective-permute-start = (bf16[4,64,128]{2,1,0:T(8,128)(2,1)}, bf16[4,64,128]{2,1,0:T(8,128)(2,1)S(1)}, u32[]{:S(2)}, u32[]{:S(2)}) collective-permute-start(bf16[4,64,128]{2,1,0:T(8,128)(2,1)} %get-tuple-element.43), channel_id=1, source_target_pairs={{8,0},{0,8},{24,16},{16,24},{9,1},{1,9},{25,17},{17,25},{10,2},{2,... | collective-permute-start | bytes 196616 | tf_op jit(solution)/shard_map/ppermute | solution.py:73
  6.5 3.0 %copy-start.5 = (bf16[1,1,16,64,128]{4,3,2,1,0:T(8,128)(2,1)S(1)}, bf16[1,1,16,64,128]{4,3,2,1,0:T(8,128)(2,1)}, u32[]{:S(2)}) copy-start(bf16[1,1,16,64,128]{4,3,2,1,0:T(8,128)(2,1)} %param.12) | copy-start | bytes 786436
  6.5 3.0 %copy-start.7 = (bf16[3,128,128]{2,1,0:T(8,128)(2,1)S(1)}, bf16[3,128,128]{2,1,0:T(8,128)(2,1)}, u32[]{:S(2)}) copy-start(bf16[3,128,128]{2,1,0:T(8,128)(2,1)} %refs_11_.1) | copy-start | bytes 294916
  6.5 1.7 %collective-permute-start.1 = (bf16[4,64,128]{2,1,0:T(8,128)(2,1)}, bf16[4,64,128]{2,1,0:T(8,128)(2,1)S(1)}, u32[]{:S(2)}, u32[]{:S(2)}) collective-permute-start(bf16[4,64,128]{2,1,0:T(8,128)(2,1)} %get-tuple-element.44), channel_id=1, source_target_pairs={{8,0},{0,8},{24,16},{16,24},{9,1},{1,9},{25,17},{17,25},{10,2},{2,... | collective-permute-start | bytes 196616 | tf_op jit(solution)/shard_map/ppermute | solution.py:73
  6.9 3.6 %collective-permute-start.2 = (bf16[4,64,128]{2,1,0:T(8,128)(2,1)S(1)}, bf16[4,64,128]{2,1,0:T(8,128)(2,1)S(1)}, u32[]{:S(2)}, u32[]{:S(2)}) collective-permute-start(bf16[4,64,128]{2,1,0:T(8,128)(2,1)S(1)} %collective-permute-done.refs_5_), channel_id=1, source_target_pairs={{16,0},{24,8},{0,16},{8,24},{17,1},{25,9},{1,17},{9,25},{18,2},{26... | collective-permute-start | bytes 196616 | tf_op jit(solution)/shard_map/ppermute | solution.py:73
  8.2 6.9 %collective-permute-start.4 = (bf16[14,64,128]{2,1,0:T(8,128)(2,1)S(1)}, bf16[14,64,128]{2,1,0:T(8,128)(2,1)S(1)}, u32[]{:S(2)}, u32[]{:S(2)}) collective-permute-start(bf16[14,64,128]{2,1,0:T(8,128)(2,1)S(1)} %get-tuple-element.45.refs_5_), channel_id=1, source_target_pairs={{4,0},{0,4},{5,1},{1,5},{6,2},{2,6},{7,3},{3,7},{12,8},{8,12},{13,... | collective-permute-start | bytes 688136 | tf_op jit(solution)/shard_map/ppermute | solution.py:73
  11.5 2.1 %collective-permute-start.6 = (bf16[384,128]{1,0:T(8,128)(2,1)S(1)}, bf16[384,128]{1,0:T(8,128)(2,1)S(1)}, u32[]{:S(2)}, u32[]{:S(2)}) collective-permute-start(bf16[384,128]{1,0:T(8,128)(2,1)S(1)} %get-tuple-element.52), channel_id=1, source_target_pairs={{8,0},{0,8},{24,16},{16,24},{9,1},{1,9},{25,17},{17,25},{10,2},{2,... | collective-permute-start | bytes 294920 | tf_op jit(solution)/shard_map/ppermute | solution.py:73
  12.4 1.3 %collective-permute-start.7 = (bf16[384,128]{1,0:T(8,128)(2,1)S(1)}, bf16[384,128]{1,0:T(8,128)(2,1)S(1)}, u32[]{:S(2)}, u32[]{:S(2)}) collective-permute-start(bf16[384,128]{1,0:T(8,128)(2,1)S(1)} %get-tuple-element.53), channel_id=1, source_target_pairs={{8,0},{0,8},{24,16},{16,24},{9,1},{1,9},{25,17},{17,25},{10,2},{2,... | collective-permute-start | bytes 294920 | tf_op jit(solution)/shard_map/ppermute | solution.py:73
  12.4 4.2 %collective-permute-start.5 = (bf16[4,64,128]{2,1,0:T(8,128)(2,1)S(1)}, bf16[4,64,128]{2,1,0:T(8,128)(2,1)S(1)}, u32[]{:S(2)}, u32[]{:S(2)}) collective-permute-start(bf16[4,64,128]{2,1,0:T(8,128)(2,1)S(1)} %shard_map.131.refs_7_), channel_id=1, source_target_pairs={{4,0},{0,4},{5,1},{1,5},{6,2},{2,6},{7,3},{3,7},{12,8},{8,12},{13,... | collective-permute-start | bytes 196616 | tf_op jit(solution)/shard_map/ppermute | solution.py:73
  13.7 4.2 %collective-permute-start.8 = (bf16[384,128]{1,0:T(8,128)(2,1)S(1)}, bf16[384,128]{1,0:T(8,128)(2,1)S(1)}, u32[]{:S(2)}, u32[]{:S(2)}) collective-permute-start(bf16[384,128]{1,0:T(8,128)(2,1)S(1)} %get-tuple-element.58), channel_id=1, source_target_pairs={{16,0},{24,8},{0,16},{8,24},{17,1},{25,9},{1,17},{9,25},{18,2},{26... | collective-permute-start | bytes 294920 | tf_op jit(solution)/shard_map/ppermute | solution.py:73
  17.9 2.3 %collective-permute-start.9 = (bf16[896,128]{1,0:T(8,128)(2,1)S(1)}, bf16[896,128]{1,0:T(8,128)(2,1)S(1)}, u32[]{:S(2)}, u32[]{:S(2)}) collective-permute-start(bf16[896,128]{1,0:T(8,128)(2,1)S(1)} %get-tuple-element.59), channel_id=1, source_target_pairs={{8,0},{0,8},{24,16},{16,24},{9,1},{1,9},{25,17},{17,25},{10,2},{2,... | collective-permute-start | bytes 688136 | tf_op jit(solution)/shard_map/ppermute | solution.py:73
  20.3 6.9 %collective-permute-start.10 = (bf16[256,128]{1,0:T(8,128)(2,1)S(1)}, bf16[256,128]{1,0:T(8,128)(2,1)S(1)}, u32[]{:S(2)}, u32[]{:S(2)}) collective-permute-start(bf16[256,128]{1,0:T(8,128)(2,1)S(1)} %get-tuple-element.62), channel_id=1, source_target_pairs={{16,0},{24,8},{0,16},{8,24},{17,1},{25,9},{1,17},{9,25},{18,2},{26... | collective-permute-start | bytes 196616 | tf_op jit(solution)/shard_map/ppermute | solution.py:73
  21.6 3.0 %collective-permute-start.13 = (bf16[192,128]{1,0:T(8,128)(2,1)S(1)}, bf16[192,128]{1,0:T(8,128)(2,1)S(1)}, u32[]{:S(2)}, u32[]{:S(2)}) collective-permute-start(bf16[192,128]{1,0:T(8,128)(2,1)S(1)} %get-tuple-element.61.refs_2_), channel_id=1, source_target_pairs={{4,0},{0,4},{5,1},{1,5},{6,2},{2,6},{7,3},{3,7},{12,8},{8,12},{13,... | collective-permute-start | bytes 147464 | tf_op jit(solution)/shard_map/ppermute | solution.py:73
  22.7 3.8 %collective-permute-start.11 = (bf16[192,128]{1,0:T(8,128)(2,1)S(1)}, bf16[192,128]{1,0:T(8,128)(2,1)S(1)}, u32[]{:S(2)}, u32[]{:S(2)}) collective-permute-start(bf16[192,128]{1,0:T(8,128)(2,1)S(1)} %get-tuple-element.64), channel_id=1, source_target_pairs={{4,0},{0,4},{5,1},{1,5},{6,2},{2,6},{7,3},{3,7},{12,8},{8,12},{13,... | collective-permute-start | bytes 147464 | tf_op jit(solution)/shard_map/ppermute | solution.py:73
  23.1 4.1 %collective-permute-start.12 = (bf16[192,128]{1,0:T(8,128)(2,1)S(1)}, bf16[192,128]{1,0:T(8,128)(2,1)S(1)}, u32[]{:S(2)}, u32[]{:S(2)}) collective-permute-start(bf16[192,128]{1,0:T(8,128)(2,1)S(1)} %get-tuple-element.65), channel_id=1, source_target_pairs={{20,0},{16,4},{28,8},{24,12},{4,16},{0,20},{12,24},{8,28},{21,1},{... | collective-permute-start | bytes 147464 | tf_op jit(solution)/shard_map/ppermute | solution.py:81
  24.6 4.0 %collective-permute-start.15 = (bf16[192,128]{1,0:T(8,128)(2,1)S(1)}, bf16[192,128]{1,0:T(8,128)(2,1)S(1)}, u32[]{:S(2)}, u32[]{:S(2)}) collective-permute-start(bf16[192,128]{1,0:T(8,128)(2,1)S(1)} %shard_map.140.refs_0_), channel_id=1, source_target_pairs={{1,0},{0,1},{3,2},{2,3},{5,4},{4,5},{7,6},{6,7},{9,8},{8,9},{11,10... | collective-permute-start | bytes 147464 | tf_op jit(solution)/shard_map/ppermute | solution.py:73
  27.2 6.1 %copy-start.8 = (bf16[3,3,128,128]{3,2,1,0:T(8,128)(2,1)S(1)}, bf16[3,3,128,128]{3,2,1,0:T(8,128)(2,1)}, u32[]{:S(2)}) copy-start(bf16[3,3,128,128]{3,2,1,0:T(8,128)(2,1)} %refs_4_.5) | copy-start | bytes 884740
  27.2 3.7 %collective-permute-start.14 = (bf16[192,128]{1,0:T(8,128)(2,1)S(1)}, bf16[192,128]{1,0:T(8,128)(2,1)S(1)}, u32[]{:S(2)}, u32[]{:S(2)}) collective-permute-start(bf16[192,128]{1,0:T(8,128)(2,1)S(1)} %shard_map.139.refs_0_), channel_id=1, source_target_pairs={{1,0},{0,1},{3,2},{2,3},{5,4},{4,5},{7,6},{6,7},{9,8},{8,9},{11,10... | collective-permute-start | bytes 147464 | tf_op jit(solution)/shard_map/ppermute | solution.py:73
  28.6 6.3 %collective-permute-start.17 = (bf16[192,128]{1,0:T(8,128)(2,1)S(1)}, bf16[192,128]{1,0:T(8,128)(2,1)S(1)}, u32[]{:S(2)}, u32[]{:S(2)}) collective-permute-start(bf16[192,128]{1,0:T(8,128)(2,1)S(1)} %shard_map.143.refs_2_), channel_id=1, source_target_pairs={{2,0},{3,1},{0,2},{1,3},{6,4},{7,5},{4,6},{5,7},{10,8},{11,9},{8,1... | collective-permute-start | bytes 147464 | tf_op jit(solution)/shard_map/ppermute | solution.py:73
  31.0 3.9 %collective-permute-start.16 = (bf16[192,128]{1,0:T(8,128)(2,1)S(1)}, bf16[192,128]{1,0:T(8,128)(2,1)S(1)}, u32[]{:S(2)}, u32[]{:S(2)}) collective-permute-start(bf16[192,128]{1,0:T(8,128)(2,1)S(1)} %shard_map.141.refs_5_.refs_0_), channel_id=1, source_target_pairs={{2,0},{3,1},{0,2},{1,3},{6,4},{7,5},{4,6},{5,7},{10,8},{11,9},{8,1... | collective-permute-start | bytes 147464 | tf_op jit(solution)/shard_map/ppermute | solution.py:73
  34.9 7.9 %collective-permute-start.20 = (bf16[2,192,128]{2,1,0:T(8,128)(2,1)S(1)}, bf16[2,192,128]{2,1,0:T(8,128)(2,1)S(1)}, u32[]{:S(2)}, u32[]{:S(2)}) collective-permute-start(bf16[2,192,128]{2,1,0:T(8,128)(2,1)S(1)} %shard_map.144.refs_0_), channel_id=1, source_target_pairs={{4,0},{0,4},{5,1},{1,5},{6,2},{2,6},{7,3},{3,7},{12,8},{8,12},{13,... | collective-permute-start | bytes 294920 | tf_op jit(solution)/shard_map/ppermute | solution.py:73
  35.8 8.2 %collective-permute-start.21 = (bf16[2,192,128]{2,1,0:T(8,128)(2,1)S(1)}, bf16[2,192,128]{2,1,0:T(8,128)(2,1)S(1)}, u32[]{:S(2)}, u32[]{:S(2)}) collective-permute-start(bf16[2,192,128]{2,1,0:T(8,128)(2,1)S(1)} %shard_map.144.refs_0_), channel_id=1, source_target_pairs={{16,0},{24,8},{0,16},{8,24},{17,1},{25,9},{1,17},{9,25},{18,2},{26... | collective-permute-start | bytes 294920 | tf_op jit(solution)/shard_map/ppermute | solution.py:73
  38.2 6.8 %collective-permute-start.18 = (bf16[2,192,128]{2,1,0:T(8,128)(2,1)S(1)}, bf16[2,192,128]{2,1,0:T(8,128)(2,1)S(1)}, u32[]{:S(2)}, u32[]{:S(2)}) collective-permute-start(bf16[2,192,128]{2,1,0:T(8,128)(2,1)S(1)} %shard_map.144.refs_0_), channel_id=1, source_target_pairs={{20,0},{16,4},{28,8},{24,12},{4,16},{0,20},{12,24},{8,28},{21,1},{... | collective-permute-start | bytes 294920 | tf_op jit(solution)/shard_map/ppermute | solution.py:81
  38.8 7.6 %collective-permute-start.22 = (bf16[2,192,128]{2,1,0:T(8,128)(2,1)S(1)}, bf16[2,192,128]{2,1,0:T(8,128)(2,1)S(1)}, u32[]{:S(2)}, u32[]{:S(2)}) collective-permute-start(bf16[2,192,128]{2,1,0:T(8,128)(2,1)S(1)} %shard_map.144.refs_0_), channel_id=1, source_target_pairs={{8,0},{0,8},{24,16},{16,24},{9,1},{1,9},{25,17},{17,25},{10,2},{2,... | collective-permute-start | bytes 294920 | tf_op jit(solution)/shard_map/ppermute | solution.py:73
  42.9 3.6 %collective-permute-start.23 = (bf16[2,192,128]{2,1,0:T(8,128)(2,1)S(1)}, bf16[2,192,128]{2,1,0:T(8,128)(2,1)S(1)}, u32[]{:S(2)}, u32[]{:S(2)}) collective-permute-start(bf16[2,192,128]{2,1,0:T(8,128)(2,1)S(1)} %collective-permute-done.20.refs_1_), channel_id=1, source_target_pairs={{8,0},{0,8},{24,16},{16,24},{9,1},{1,9},{25,17},{17,25},{10,2},{2,... | collective-permute-start | bytes 294920 | tf_op jit(solution)/shard_map/ppermute | solution.py:73
  44.0 2.4 %collective-permute-start.24 = (bf16[2,192,128]{2,1,0:T(8,128)(2,1)S(1)}, bf16[2,192,128]{2,1,0:T(8,128)(2,1)S(1)}, u32[]{:S(2)}, u32[]{:S(2)}) collective-permute-start(bf16[2,192,128]{2,1,0:T(8,128)(2,1)S(1)} %collective-permute-done.21.refs_2_), channel_id=1, source_target_pairs={{8,0},{0,8},{24,16},{16,24},{9,1},{1,9},{25,17},{17,25},{10,2},{2,... | collective-permute-start | bytes 294920 | tf_op jit(solution)/shard_map/ppermute | solution.py:73
  45.1 2.5 %collective-permute-start.19 = (bf16[2,192,128]{2,1,0:T(8,128)(2,1)S(1)}, bf16[2,192,128]{2,1,0:T(8,128)(2,1)S(1)}, u32[]{:S(2)}, u32[]{:S(2)}) collective-permute-start(bf16[2,192,128]{2,1,0:T(8,128)(2,1)S(1)} %collective-permute-done.18.refs_0_), channel_id=1, source_target_pairs={{8,0},{0,8},{24,16},{16,24},{9,1},{1,9},{25,17},{17,25},{10,2},{2,... | collective-permute-start | bytes 294920 | tf_op jit(solution)/shard_map/ppermute | solution.py:73
  (2 other events, 6.1 us)

commit v15 on v14

--- a/solution.py
+++ b/solution.py
@@ -406,7 +406,7 @@
     rest = across_ref.shape[0] - half
     across_ref[half:] = part_ref[2 * height + rest :]
     frame_ref[...] = quarter(band, frames[1]).astype(jnp.bfloat16)
-    both_ref[...] = quarter(1 - band, frames[1]).astype(jnp.bfloat16)
+    both_ref[:half] = quarter(1 - band, frames[1]).astype(jnp.bfloat16)
 
 
 def plane_kernel(own_ref, *refs):
@@ -688,7 +688,7 @@
             across_two,
         )
         sum_two = added(keep_two, flipped(send_two, "video", 1))
-        quarters = [f32(half, ch), bf16(half + cols, ch)] + [bf16(half, ch)] * 2
+        quarters = [f32(half, ch)] + [bf16(half + more, ch) for more in (cols, 0, cols + 16)]
         own_one, *sends = call(
             pair_quarter_kernel, quarters, [], 8 * conv, keep_one, pair_one, after=(send_two,)
         )
@@ -716,10 +716,9 @@
         frame, across, both = flipped(own, "video", 1), flipped(own, "section", 2), flipped_both(own)
         shares = [own, frame, across]
         shares += [flipped(share, "section", 1) for share in shares]
-        last = [both, flipped(both, "section", 1)]
         places = [(0, False), (0, True), (2, False), (1, False), (1, True), (3, False)]
-        sums = placed(shares, places)
-        sums = unpacked(placed(last, [(2, True), (3, True)], sums))
+        sums = placed([*shares, both], [*places, (2, True)])
+        sums = unpacked(placed([flipped(both, "section", 1)], [(3, True)], sums))
     else:
         own_one, send_one = call(
             pair_kernel,

time: 48.7 us -> 49.8 us (1.023)
  waiting for transfers between devices: 4.93 us -> 6.69 us
  starting transfers between devices: 33.3 us -> 32.7 us
    ppermute x23, waiting for transfers between devices: 4.17 us -> 6.69 us  [flipped(): lax.ppermute(block, axis, [(place ^ flip, place) for place in range(count)])]
    ppermute x23, starting transfers between devices: 31.6 us -> 29.7 us  [flipped(): lax.ppermute(block, axis, [(place ^ flip, place) for place in range(count)])]
    ppermute x2, starting transfers between devices: 1.75 us -> 3.01 us  [flipped_both(): return lax.ppermute(block, ('section', 'video'), pairs)]
    ppermute x2, waiting for transfers between devices: 0.76 us -> 0.01 us  [flipped_both(): return lax.ppermute(block, ('section', 'video'), pairs)]
where the time goes in v15:
time: 49.8 us; the launch traced here: 49.5 us
  starting transfers between devices  32.7 us (66%)
  Pallas kernels  9.26 us (19%)
  waiting for transfers between devices  6.69 us (13%)
  between operations  0.84 us (2%)
    ppermute x23, starting transfers between devices, flipped(): lax.ppermute(block, axis, [(place ^ flip, place) for place in range(count)])  29.7 us
    pallas_call x17, Pallas kernels, call(): pl.pallas_call(body, out_shape=outs[0] if single else tuple(outs), in_spe...  7.35 us
    ppermute x23, waiting for transfers between devices, flipped(): lax.ppermute(block, axis, [(place ^ flip, place) for place in range(count)])  6.69 us
    ppermute x2, starting transfers between devices, flipped_both(): return lax.ppermute(block, ('section', 'video'), pairs)  3.01 us
    pallas_call x2, Pallas kernels, placed(): pl.pallas_call(functools.partial(place_kernel, places), out_shape=outs, i...  1.91 us
  transfers between devices with their start and end apart: 25, of which 7 were waited for; matrix products, arithmetic and copies ran while one was open for 0% of the time, Pallas kernels for 17%

profile of v15, /device:TPU:1, one launch (start us, length us, event | category | flops | bytes accessed | tf_op | source)
XLA Modules:
  0.0 49.5 jit_solution(9022749082708511744)
XLA Ops:
  0.6 2.1 %collective-permute-start.3 = (bf16[16,64,128]{2,1,0:T(8,128)(2,1)}, bf16[16,64,128]{2,1,0:T(8,128)(2,1)S(1)}, u32[]{:S(2)}, u32[]{:S(2)}) collective-permute-start(bf16[16,64,128]{2,1,0:T(8,128)(2,1)} %bitcast.10), channel_id=1, source_target_pairs={{4,0},{0,4},{5,1},{1,5},{6,2},{2,6},{7,3},{3,7},{12,8},{8,12},{13,... | collective-permute-start | bytes 786440 | tf_op jit(solution)/shard_map/ppermute | solution.py:73
  2.7 1.6 %shard_map.128 = (bf16[4,64,128]{2,1,0:T(8,128)(2,1)}, bf16[4,64,128]{2,1,0:T(8,128)(2,1)}) custom-call(bf16[16,64,128]{2,1,0:T(8,128)(2,1)} %bitcast.11, bf16[16,64,128]{2,1,0:T(8,128)(2,1)} %bitcast.17, bf16[16,64,128]{2,1,0:T(8,128)(2,1)} %bitcast.28, bf16[16,64,128]{2,1,0:T(8,128)(2,1)} %bitcast.25), custom_call_target="tpu_custom_call" | custom-call | flops 1 | bytes 1179648 | tf_op jit(solution)/shard_map/pallas_call | solution.py:38
  4.4 1.0 %collective-permute-start = (bf16[4,64,128]{2,1,0:T(8,128)(2,1)}, bf16[4,64,128]{2,1,0:T(8,128)(2,1)S(1)}, u32[]{:S(2)}, u32[]{:S(2)}) collective-permute-start(bf16[4,64,128]{2,1,0:T(8,128)(2,1)} %get-tuple-element.43), channel_id=1, source_target_pairs={{8,0},{0,8},{24,16},{16,24},{9,1},{1,9},{25,17},{17,25},{10,2},{2,... | collective-permute-start | bytes 196616 | tf_op jit(solution)/shard_map/ppermute | solution.py:73
  5.4 1.1 %collective-permute-done.refs_5_ = bf16[4,64,128]{2,1,0:T(8,128)(2,1)S(1)} collective-permute-done((bf16[4,64,128]{2,1,0:T(8,128)(2,1)}, bf16[4,64,128]{2,1,0:T(8,128)(2,1)S(1)}, u32[]{:S(2)}, u32[]{:S(2)}) %collective-permute-start) | collective-permute-done | bytes 65568 | tf_op jit(solution)/shard_map/ppermute | solution.py:73
  6.9 1.2 %collective-permute-start.2 = (bf16[4,64,128]{2,1,0:T(8,128)(2,1)S(1)}, bf16[4,64,128]{2,1,0:T(8,128)(2,1)S(1)}, u32[]{:S(2)}, u32[]{:S(2)}) collective-permute-start(bf16[4,64,128]{2,1,0:T(8,128)(2,1)S(1)} %collective-permute-done.refs_5_), channel_id=1, source_target_pairs={{16,0},{24,8},{0,16},{8,24},{17,1},{25,9},{1,17},{9,25},{18,2},{26... | collective-permute-start | bytes 196616 | tf_op jit(solution)/shard_map/ppermute | solution.py:73
  8.2 1.3 %collective-permute-start.4 = (bf16[14,64,128]{2,1,0:T(8,128)(2,1)S(1)}, bf16[14,64,128]{2,1,0:T(8,128)(2,1)S(1)}, u32[]{:S(2)}, u32[]{:S(2)}) collective-permute-start(bf16[14,64,128]{2,1,0:T(8,128)(2,1)S(1)} %get-tuple-element.45.refs_5_), channel_id=1, source_target_pairs={{4,0},{0,4},{5,1},{1,5},{6,2},{2,6},{7,3},{3,7},{12,8},{8,12},{13,... | collective-permute-start | bytes 688136 | tf_op jit(solution)/shard_map/ppermute | solution.py:73
  9.6 1.0 %shard_map.130 = (bf16[14,64,128]{2,1,0:T(8,128)(2,1)S(1)}, bf16[16,64,128]{2,1,0:T(8,128)(2,1)S(1)}) custom-call(bf16[16,64,128]{2,1,0:T(8,128)(2,1)S(1)} %bitcast.13, bf16[16,64,128]{2,1,0:T(8,128)(2,1)S(1)} %bitcast.19, bf16[16,64,128]{2,1,0:T(8,128)(2,1)S(1)} %collective-permute-done.3.refs_2_.refs_6_, bf16[3,128,128]{2,1,0:T(8,128)(2,1)S(1)} %copy-done.6, ...), custom_call_target="tpu_custom_call" | custom-call | tf_op jit(solution)/shard_map/pallas_call | solution.py:38
  10.6 0.9 %shard_map.132 = (f32[2,384,128]{2,1,0:T(8,128)S(1)}, bf16[384,128]{1,0:T(8,128)(2,1)S(1)}, bf16[384,128]{1,0:T(8,128)(2,1)S(1)}) custom-call(bf16[16,64,128]{2,1,0:T(8,128)(2,1)S(1)} %bitcast.30, bf16[16,64,128]{2,1,0:T(8,128)(2,1)S(1)} %bitcast.20, bf16[16,64,128]{2,1,0:T(8,128)(2,1)S(1)} %get-tuple-element.48.refs_6_.refs_2_.refs_4_, ...), custom_call_target="tpu_custom_call" | custom-call | flops 2415919104 | bytes 2031616 | tf_op jit(solution)/shard_map/pallas_call | solution.py:38
  11.5 0.9 %collective-permute-start.6 = (bf16[384,128]{1,0:T(8,128)(2,1)S(1)}, bf16[384,128]{1,0:T(8,128)(2,1)S(1)}, u32[]{:S(2)}, u32[]{:S(2)}) collective-permute-start(bf16[384,128]{1,0:T(8,128)(2,1)S(1)} %get-tuple-element.52), channel_id=1, source_target_pairs={{8,0},{0,8},{24,16},{16,24},{9,1},{1,9},{25,17},{17,25},{10,2},{2,... | collective-permute-start | bytes 294920 | tf_op jit(solution)/shard_map/ppermute | solution.py:73
  12.4 0.8 %collective-permute-start.5 = (bf16[4,64,128]{2,1,0:T(8,128)(2,1)S(1)}, bf16[4,64,128]{2,1,0:T(8,128)(2,1)S(1)}, u32[]{:S(2)}, u32[]{:S(2)}) collective-permute-start(bf16[4,64,128]{2,1,0:T(8,128)(2,1)S(1)} %shard_map.131.refs_7_), channel_id=1, source_target_pairs={{4,0},{0,4},{5,1},{1,5},{6,2},{2,6},{7,3},{3,7},{12,8},{8,12},{13,... | collective-permute-start | bytes 196616 | tf_op jit(solution)/shard_map/ppermute | solution.py:73
  13.7 1.4 %collective-permute-start.8 = (bf16[384,128]{1,0:T(8,128)(2,1)S(1)}, bf16[384,128]{1,0:T(8,128)(2,1)S(1)}, u32[]{:S(2)}, u32[]{:S(2)}) collective-permute-start(bf16[384,128]{1,0:T(8,128)(2,1)S(1)} %get-tuple-element.58), channel_id=1, source_target_pairs={{16,0},{24,8},{0,16},{8,24},{17,1},{25,9},{1,17},{9,25},{18,2},{26... | collective-permute-start | bytes 294920 | tf_op jit(solution)/shard_map/ppermute | solution.py:73
  15.6 1.0 %collective-permute-done.5.refs_6_ = bf16[4,64,128]{2,1,0:T(8,128)(2,1)S(1)} collective-permute-done((bf16[4,64,128]{2,1,0:T(8,128)(2,1)S(1)}, bf16[4,64,128]{2,1,0:T(8,128)(2,1)S(1)}, u32[]{:S(2)}, u32[]{:S(2)}) %collective-permute-start.5) | collective-permute-done | bytes 65568 | tf_op jit(solution)/shard_map/ppermute | solution.py:73
  16.6 1.3 %shard_map.136 = (bf16[16,64,128]{2,1,0:T(8,128)(2,1)S(1)}, bf16[16,64,128]{2,1,0:T(8,128)(2,1)S(1)}, f32[2,384,128]{2,1,0:T(8,128)S(1)}, bf16[896,128]{1,0:T(8,128)(2,1)S(1)}) custom-call(bf16[16,64,128]{2,1,0:T(8,128)(2,1)S(1)} %bitcast.16, bf16[4,64,128]{2,1,0:T(8,128)(2,1)S(1)} %collective-permute-done.1.refs_4_.refs_1_.refs_3_.refs_2_, ...), custom_call_target="tpu_custom_call" | custom-call | flops 2415919104 | bytes 5046272 | tf_op jit(solution)/shard_map/pallas_call | solution.py:38
  17.9 1.2 %collective-permute-start.9 = (bf16[896,128]{1,0:T(8,128)(2,1)S(1)}, bf16[896,128]{1,0:T(8,128)(2,1)S(1)}, u32[]{:S(2)}, u32[]{:S(2)}) collective-permute-start(bf16[896,128]{1,0:T(8,128)(2,1)S(1)} %get-tuple-element.59), channel_id=1, source_target_pairs={{8,0},{0,8},{24,16},{16,24},{9,1},{1,9},{25,17},{17,25},{10,2},{2,... | collective-permute-start | bytes 688136 | tf_op jit(solution)/shard_map/ppermute | solution.py:73
  19.1 1.1 %collective-permute-done.9.refs_1_.refs_2_ = bf16[896,128]{1,0:T(8,128)(2,1)S(1)} collective-permute-done((bf16[896,128]{1,0:T(8,128)(2,1)S(1)}, bf16[896,128]{1,0:T(8,128)(2,1)S(1)}, u32[]{:S(2)}, u32[]{:S(2)}) %collective-permute-start.9) | collective-permute-done | bytes 229408 | tf_op jit(solution)/shard_map/ppermute | solution.py:73
  20.3 2.1 %collective-permute-start.12 = (bf16[272,128]{1,0:T(8,128)(2,1)S(1)}, bf16[272,128]{1,0:T(8,128)(2,1)S(1)}, u32[]{:S(2)}, u32[]{:S(2)}) collective-permute-start(bf16[272,128]{1,0:T(8,128)(2,1)S(1)} %get-tuple-element.65), channel_id=1, source_target_pairs={{20,0},{16,4},{28,8},{24,12},{4,16},{0,20},{12,24},{8,28},{21,1},{... | collective-permute-start | bytes 208904 | tf_op jit(solution)/shard_map/ppermute | solution.py:81
  23.0 1.3 %collective-permute-start.11 = (bf16[192,128]{1,0:T(8,128)(2,1)S(1)}, bf16[192,128]{1,0:T(8,128)(2,1)S(1)}, u32[]{:S(2)}, u32[]{:S(2)}) collective-permute-start(bf16[192,128]{1,0:T(8,128)(2,1)S(1)} %get-tuple-element.64), channel_id=1, source_target_pairs={{4,0},{0,4},{5,1},{1,5},{6,2},{2,6},{7,3},{3,7},{12,8},{8,12},{13,... | collective-permute-start | bytes 147464 | tf_op jit(solution)/shard_map/ppermute | solution.py:73
  24.2 1.6 %collective-permute-done.13.refs_1_ = bf16[192,128]{1,0:T(8,128)(2,1)S(1)} collective-permute-done((bf16[192,128]{1,0:T(8,128)(2,1)S(1)}, bf16[192,128]{1,0:T(8,128)(2,1)S(1)}, u32[]{:S(2)}, u32[]{:S(2)}) %collective-permute-start.13) | collective-permute-done | bytes 49184 | tf_op jit(solution)/shard_map/ppermute | solution.py:73
  25.8 1.4 %collective-permute-start.15 = (bf16[192,128]{1,0:T(8,128)(2,1)S(1)}, bf16[192,128]{1,0:T(8,128)(2,1)S(1)}, u32[]{:S(2)}, u32[]{:S(2)}) collective-permute-start(bf16[192,128]{1,0:T(8,128)(2,1)S(1)} %shard_map.140.refs_0_), channel_id=1, source_target_pairs={{1,0},{0,1},{3,2},{2,3},{5,4},{4,5},{7,6},{6,7},{9,8},{8,9},{11,10... | collective-permute-start | bytes 147464 | tf_op jit(solution)/shard_map/ppermute | solution.py:73
  27.3 0.8 %collective-permute-start.14 = (bf16[192,128]{1,0:T(8,128)(2,1)S(1)}, bf16[192,128]{1,0:T(8,128)(2,1)S(1)}, u32[]{:S(2)}, u32[]{:S(2)}) collective-permute-start(bf16[192,128]{1,0:T(8,128)(2,1)S(1)} %shard_map.139.refs_0_), channel_id=1, source_target_pairs={{1,0},{0,1},{3,2},{2,3},{5,4},{4,5},{7,6},{6,7},{9,8},{8,9},{11,10... | collective-permute-start | bytes 147464 | tf_op jit(solution)/shard_map/ppermute | solution.py:73
  28.0 0.8 %collective-permute-done.15.refs_1_ = bf16[192,128]{1,0:T(8,128)(2,1)S(1)} collective-permute-done((bf16[192,128]{1,0:T(8,128)(2,1)S(1)}, bf16[192,128]{1,0:T(8,128)(2,1)S(1)}, u32[]{:S(2)}, u32[]{:S(2)}) %collective-permute-start.15) | collective-permute-done | bytes 49184 | tf_op jit(solution)/shard_map/ppermute | solution.py:73
  28.9 2.4 %collective-permute-start.17 = (bf16[192,128]{1,0:T(8,128)(2,1)S(1)}, bf16[192,128]{1,0:T(8,128)(2,1)S(1)}, u32[]{:S(2)}, u32[]{:S(2)}) collective-permute-start(bf16[192,128]{1,0:T(8,128)(2,1)S(1)} %shard_map.143.refs_2_), channel_id=1, source_target_pairs={{2,0},{3,1},{0,2},{1,3},{6,4},{7,5},{4,6},{5,7},{10,8},{11,9},{8,1... | collective-permute-start | bytes 147464 | tf_op jit(solution)/shard_map/ppermute | solution.py:73
  31.2 1.4 %collective-permute-start.16 = (bf16[192,128]{1,0:T(8,128)(2,1)S(1)}, bf16[192,128]{1,0:T(8,128)(2,1)S(1)}, u32[]{:S(2)}, u32[]{:S(2)}) collective-permute-start(bf16[192,128]{1,0:T(8,128)(2,1)S(1)} %shard_map.141.refs_5_.refs_0_), channel_id=1, source_target_pairs={{2,0},{3,1},{0,2},{1,3},{6,4},{7,5},{4,6},{5,7},{10,8},{11,9},{8,1... | collective-permute-start | bytes 147464 | tf_op jit(solution)/shard_map/ppermute | solution.py:73
  32.7 1.5 %shard_map.142 = (bf16[16,64,128]{2,1,0:T(8,128)(2,1)}, f32[8,128]{1,0:T(8,128)S(1)}) custom-call(bf16[16,64,128]{2,1,0:T(8,128)(2,1)S(1)} %get-tuple-element.55.refs_0_, bf16[16,64,128]{2,1,0:T(8,128)(2,1)S(1)} %get-tuple-element.56.refs_1_, bf16[896,128]{1,0:T(8,128)(2,1)S(1)} %collective-permute-done.9.refs_1_.refs_2_, ...), custom_call_target="tpu_custom_call" | custom-call | flops 301989888 | bytes 1380352 | tf_op jit(solution)/shard_map/pallas_call | solution.py:38
  34.2 1.0 %collective-permute-done.16.refs_1_ = bf16[192,128]{1,0:T(8,128)(2,1)S(1)} collective-permute-done((bf16[192,128]{1,0:T(8,128)(2,1)S(1)}, bf16[192,128]{1,0:T(8,128)(2,1)S(1)}, u32[]{:S(2)}, u32[]{:S(2)}) %collective-permute-start.16) | collective-permute-done | bytes 49184 | tf_op jit(solution)/shard_map/ppermute | solution.py:73
  35.2 1.1 %collective-permute-start.20 = (bf16[2,192,128]{2,1,0:T(8,128)(2,1)S(1)}, bf16[2,192,128]{2,1,0:T(8,128)(2,1)S(1)}, u32[]{:S(2)}, u32[]{:S(2)}) collective-permute-start(bf16[2,192,128]{2,1,0:T(8,128)(2,1)S(1)} %shard_map.144.refs_0_), channel_id=1, source_target_pairs={{4,0},{0,4},{5,1},{1,5},{6,2},{2,6},{7,3},{3,7},{12,8},{8,12},{13,... | collective-permute-start | bytes 294920 | tf_op jit(solution)/shard_map/ppermute | solution.py:73
  37.0 0.9 %collective-permute-start.18 = (bf16[2,192,128]{2,1,0:T(8,128)(2,1)S(1)}, bf16[2,192,128]{2,1,0:T(8,128)(2,1)S(1)}, u32[]{:S(2)}, u32[]{:S(2)}) collective-permute-start(bf16[2,192,128]{2,1,0:T(8,128)(2,1)S(1)} %shard_map.144.refs_0_), channel_id=1, source_target_pairs={{20,0},{16,4},{28,8},{24,12},{4,16},{0,20},{12,24},{8,28},{21,1},{... | collective-permute-start | bytes 294920 | tf_op jit(solution)/shard_map/ppermute | solution.py:81
  37.9 5.5 %collective-permute-start.22 = (bf16[2,192,128]{2,1,0:T(8,128)(2,1)S(1)}, bf16[2,192,128]{2,1,0:T(8,128)(2,1)S(1)}, u32[]{:S(2)}, u32[]{:S(2)}) collective-permute-start(bf16[2,192,128]{2,1,0:T(8,128)(2,1)S(1)} %shard_map.144.refs_0_), channel_id=1, source_target_pairs={{8,0},{0,8},{24,16},{16,24},{9,1},{1,9},{25,17},{17,25},{10,2},{2,... | collective-permute-start | bytes 294920 | tf_op jit(solution)/shard_map/ppermute | solution.py:73
  43.4 1.1 %collective-permute-start.23 = (bf16[2,192,128]{2,1,0:T(8,128)(2,1)S(1)}, bf16[2,192,128]{2,1,0:T(8,128)(2,1)S(1)}, u32[]{:S(2)}, u32[]{:S(2)}) collective-permute-start(bf16[2,192,128]{2,1,0:T(8,128)(2,1)S(1)} %collective-permute-done.20.refs_1_), channel_id=1, source_target_pairs={{8,0},{0,8},{24,16},{16,24},{9,1},{1,9},{25,17},{17,25},{10,2},{2,... | collective-permute-start | bytes 294920 | tf_op jit(solution)/shard_map/ppermute | solution.py:73
  44.6 0.9 %collective-permute-start.24 = (bf16[2,192,128]{2,1,0:T(8,128)(2,1)S(1)}, bf16[2,192,128]{2,1,0:T(8,128)(2,1)S(1)}, u32[]{:S(2)}, u32[]{:S(2)}) collective-permute-start(bf16[2,192,128]{2,1,0:T(8,128)(2,1)S(1)} %collective-permute-done.21.refs_2_), channel_id=1, source_target_pairs={{8,0},{0,8},{24,16},{16,24},{9,1},{1,9},{25,17},{17,25},{10,2},{2,... | collective-permute-start | bytes 294920 | tf_op jit(solution)/shard_map/ppermute | solution.py:73
  45.5 2.1 %collective-permute-start.19 = (bf16[2,192,128]{2,1,0:T(8,128)(2,1)S(1)}, bf16[2,192,128]{2,1,0:T(8,128)(2,1)S(1)}, u32[]{:S(2)}, u32[]{:S(2)}) collective-permute-start(bf16[2,192,128]{2,1,0:T(8,128)(2,1)S(1)} %collective-permute-done.18.refs_6_), channel_id=1, source_target_pairs={{8,0},{0,8},{24,16},{16,24},{9,1},{1,9},{25,17},{17,25},{10,2},{2,... | collective-permute-start | bytes 294920 | tf_op jit(solution)/shard_map/ppermute | solution.py:73
  47.6 1.2 %shard_map.145 = (f32[3,384,128]{2,1,0:T(8,128)}, f32[384,128]{1,0:T(8,128)}, f32[3,384,128]{2,1,0:T(8,128)}, f32[384,128]{1,0:T(8,128)}) custom-call(bf16[2,192,128]{2,1,0:T(8,128)(2,1)S(1)} %shard_map.144.refs_0_, bf16[2,192,128]{2,1,0:T(8,128)(2,1)S(1)} %collective-permute-done.20.refs_1_, bf16[2,192,128]{2,1,0:T(8,128)(2,1)S(1)} %collective-permute-done.21.refs_2_, ...), custom_call_target="tpu_custom_call" | custom-call | bytes 2064384 | tf_op jit(solution)/shard_map/pallas_call | solution.py:466
  (55 shorter events, 3.7 us)
Async XLA Ops:
  0.6 8.9 %collective-permute-start.3 = (bf16[16,64,128]{2,1,0:T(8,128)(2,1)}, bf16[16,64,128]{2,1,0:T(8,128)(2,1)S(1)}, u32[]{:S(2)}, u32[]{:S(2)}) collective-permute-start(bf16[16,64,128]{2,1,0:T(8,128)(2,1)} %bitcast.10), channel_id=1, source_target_pairs={{4,0},{0,4},{5,1},{1,5},{6,2},{2,6},{7,3},{3,7},{12,8},{8,12},{13,... | collective-permute-start | bytes 786440 | tf_op jit(solution)/shard_map/ppermute | solution.py:73
  2.7 5.4 %copy-start = (bf16[1,1,16,64,128]{4,3,2,1,0:T(8,128)(2,1)S(1)}, bf16[1,1,16,64,128]{4,3,2,1,0:T(8,128)(2,1)}, u32[]{:S(2)}) copy-start(bf16[1,1,16,64,128]{4,3,2,1,0:T(8,128)(2,1)} %param.9) | copy-start | bytes 786436
  2.7 5.4 %copy-start.1 = (bf16[3,3,128,128]{3,2,1,0:T(8,128)(2,1)S(1)}, bf16[3,3,128,128]{3,2,1,0:T(8,128)(2,1)}, u32[]{:S(2)}) copy-start(bf16[3,3,128,128]{3,2,1,0:T(8,128)(2,1)} %refs_8_.1) | copy-start | bytes 884740
  2.7 5.4 %copy-start.2 = (bf16[1,1,16,64,128]{4,3,2,1,0:T(8,128)(2,1)S(1)}, bf16[1,1,16,64,128]{4,3,2,1,0:T(8,128)(2,1)}, u32[]{:S(2)}) copy-start(bf16[1,1,16,64,128]{4,3,2,1,0:T(8,128)(2,1)} %param.13) | copy-start | bytes 786436
  2.7 5.4 %copy-start.6 = (bf16[3,128,128]{2,1,0:T(8,128)(2,1)S(1)}, bf16[3,128,128]{2,1,0:T(8,128)(2,1)}, u32[]{:S(2)}) copy-start(bf16[3,128,128]{2,1,0:T(8,128)(2,1)} %refs_7_.1) | copy-start | bytes 294916
  4.4 2.1 %collective-permute-start = (bf16[4,64,128]{2,1,0:T(8,128)(2,1)}, bf16[4,64,128]{2,1,0:T(8,128)(2,1)S(1)}, u32[]{:S(2)}, u32[]{:S(2)}) collective-permute-start(bf16[4,64,128]{2,1,0:T(8,128)(2,1)} %get-tuple-element.43), channel_id=1, source_target_pairs={{8,0},{0,8},{24,16},{16,24},{9,1},{1,9},{25,17},{17,25},{10,2},{2,... | collective-permute-start | bytes 196616 | tf_op jit(solution)/shard_map/ppermute | solution.py:73
  6.5 3.0 %copy-start.5 = (bf16[1,1,16,64,128]{4,3,2,1,0:T(8,128)(2,1)S(1)}, bf16[1,1,16,64,128]{4,3,2,1,0:T(8,128)(2,1)}, u32[]{:S(2)}) copy-start(bf16[1,1,16,64,128]{4,3,2,1,0:T(8,128)(2,1)} %param.12) | copy-start | bytes 786436
  6.5 3.0 %copy-start.7 = (bf16[3,128,128]{2,1,0:T(8,128)(2,1)S(1)}, bf16[3,128,128]{2,1,0:T(8,128)(2,1)}, u32[]{:S(2)}) copy-start(bf16[3,128,128]{2,1,0:T(8,128)(2,1)} %refs_11_.1) | copy-start | bytes 294916
  6.5 1.7 %collective-permute-start.1 = (bf16[4,64,128]{2,1,0:T(8,128)(2,1)}, bf16[4,64,128]{2,1,0:T(8,128)(2,1)S(1)}, u32[]{:S(2)}, u32[]{:S(2)}) collective-permute-start(bf16[4,64,128]{2,1,0:T(8,128)(2,1)} %get-tuple-element.44), channel_id=1, source_target_pairs={{8,0},{0,8},{24,16},{16,24},{9,1},{1,9},{25,17},{17,25},{10,2},{2,... | collective-permute-start | bytes 196616 | tf_op jit(solution)/shard_map/ppermute | solution.py:73
  6.9 3.6 %collective-permute-start.2 = (bf16[4,64,128]{2,1,0:T(8,128)(2,1)S(1)}, bf16[4,64,128]{2,1,0:T(8,128)(2,1)S(1)}, u32[]{:S(2)}, u32[]{:S(2)}) collective-permute-start(bf16[4,64,128]{2,1,0:T(8,128)(2,1)S(1)} %collective-permute-done.refs_5_), channel_id=1, source_target_pairs={{16,0},{24,8},{0,16},{8,24},{17,1},{25,9},{1,17},{9,25},{18,2},{26... | collective-permute-start | bytes 196616 | tf_op jit(solution)/shard_map/ppermute | solution.py:73
  8.2 6.9 %collective-permute-start.4 = (bf16[14,64,128]{2,1,0:T(8,128)(2,1)S(1)}, bf16[14,64,128]{2,1,0:T(8,128)(2,1)S(1)}, u32[]{:S(2)}, u32[]{:S(2)}) collective-permute-start(bf16[14,64,128]{2,1,0:T(8,128)(2,1)S(1)} %get-tuple-element.45.refs_5_), channel_id=1, source_target_pairs={{4,0},{0,4},{5,1},{1,5},{6,2},{2,6},{7,3},{3,7},{12,8},{8,12},{13,... | collective-permute-start | bytes 688136 | tf_op jit(solution)/shard_map/ppermute | solution.py:73
  11.5 2.1 %collective-permute-start.6 = (bf16[384,128]{1,0:T(8,128)(2,1)S(1)}, bf16[384,128]{1,0:T(8,128)(2,1)S(1)}, u32[]{:S(2)}, u32[]{:S(2)}) collective-permute-start(bf16[384,128]{1,0:T(8,128)(2,1)S(1)} %get-tuple-element.52), channel_id=1, source_target_pairs={{8,0},{0,8},{24,16},{16,24},{9,1},{1,9},{25,17},{17,25},{10,2},{2,... | collective-permute-start | bytes 294920 | tf_op jit(solution)/shard_map/ppermute | solution.py:73
  12.4 1.3 %collective-permute-start.7 = (bf16[384,128]{1,0:T(8,128)(2,1)S(1)}, bf16[384,128]{1,0:T(8,128)(2,1)S(1)}, u32[]{:S(2)}, u32[]{:S(2)}) collective-permute-start(bf16[384,128]{1,0:T(8,128)(2,1)S(1)} %get-tuple-element.53), channel_id=1, source_target_pairs={{8,0},{0,8},{24,16},{16,24},{9,1},{1,9},{25,17},{17,25},{10,2},{2,... | collective-permute-start | bytes 294920 | tf_op jit(solution)/shard_map/ppermute | solution.py:73
  12.4 4.2 %collective-permute-start.5 = (bf16[4,64,128]{2,1,0:T(8,128)(2,1)S(1)}, bf16[4,64,128]{2,1,0:T(8,128)(2,1)S(1)}, u32[]{:S(2)}, u32[]{:S(2)}) collective-permute-start(bf16[4,64,128]{2,1,0:T(8,128)(2,1)S(1)} %shard_map.131.refs_7_), channel_id=1, source_target_pairs={{4,0},{0,4},{5,1},{1,5},{6,2},{2,6},{7,3},{3,7},{12,8},{8,12},{13,... | collective-permute-start | bytes 196616 | tf_op jit(solution)/shard_map/ppermute | solution.py:73
  13.7 4.2 %collective-permute-start.8 = (bf16[384,128]{1,0:T(8,128)(2,1)S(1)}, bf16[384,128]{1,0:T(8,128)(2,1)S(1)}, u32[]{:S(2)}, u32[]{:S(2)}) collective-permute-start(bf16[384,128]{1,0:T(8,128)(2,1)S(1)} %get-tuple-element.58), channel_id=1, source_target_pairs={{16,0},{24,8},{0,16},{8,24},{17,1},{25,9},{1,17},{9,25},{18,2},{26... | collective-permute-start | bytes 294920 | tf_op jit(solution)/shard_map/ppermute | solution.py:73
  17.9 2.3 %collective-permute-start.9 = (bf16[896,128]{1,0:T(8,128)(2,1)S(1)}, bf16[896,128]{1,0:T(8,128)(2,1)S(1)}, u32[]{:S(2)}, u32[]{:S(2)}) collective-permute-start(bf16[896,128]{1,0:T(8,128)(2,1)S(1)} %get-tuple-element.59), channel_id=1, source_target_pairs={{8,0},{0,8},{24,16},{16,24},{9,1},{1,9},{25,17},{17,25},{10,2},{2,... | collective-permute-start | bytes 688136 | tf_op jit(solution)/shard_map/ppermute | solution.py:73
  20.3 6.9 %collective-permute-start.12 = (bf16[272,128]{1,0:T(8,128)(2,1)S(1)}, bf16[272,128]{1,0:T(8,128)(2,1)S(1)}, u32[]{:S(2)}, u32[]{:S(2)}) collective-permute-start(bf16[272,128]{1,0:T(8,128)(2,1)S(1)} %get-tuple-element.65), channel_id=1, source_target_pairs={{20,0},{16,4},{28,8},{24,12},{4,16},{0,20},{12,24},{8,28},{21,1},{... | collective-permute-start | bytes 208904 | tf_op jit(solution)/shard_map/ppermute | solution.py:81
  22.4 4.8 %collective-permute-start.10 = (bf16[256,128]{1,0:T(8,128)(2,1)S(1)}, bf16[256,128]{1,0:T(8,128)(2,1)S(1)}, u32[]{:S(2)}, u32[]{:S(2)}) collective-permute-start(bf16[256,128]{1,0:T(8,128)(2,1)S(1)} %get-tuple-element.62), channel_id=1, source_target_pairs={{16,0},{24,8},{0,16},{8,24},{17,1},{25,9},{1,17},{9,25},{18,2},{26... | collective-permute-start | bytes 196616 | tf_op jit(solution)/shard_map/ppermute | solution.py:73
  22.8 3.0 %collective-permute-start.13 = (bf16[192,128]{1,0:T(8,128)(2,1)S(1)}, bf16[192,128]{1,0:T(8,128)(2,1)S(1)}, u32[]{:S(2)}, u32[]{:S(2)}) collective-permute-start(bf16[192,128]{1,0:T(8,128)(2,1)S(1)} %get-tuple-element.61.refs_2_), channel_id=1, source_target_pairs={{4,0},{0,4},{5,1},{1,5},{6,2},{2,6},{7,3},{3,7},{12,8},{8,12},{13,... | collective-permute-start | bytes 147464 | tf_op jit(solution)/shard_map/ppermute | solution.py:73
  23.0 4.2 %collective-permute-start.11 = (bf16[192,128]{1,0:T(8,128)(2,1)S(1)}, bf16[192,128]{1,0:T(8,128)(2,1)S(1)}, u32[]{:S(2)}, u32[]{:S(2)}) collective-permute-start(bf16[192,128]{1,0:T(8,128)(2,1)S(1)} %get-tuple-element.64), channel_id=1, source_target_pairs={{4,0},{0,4},{5,1},{1,5},{6,2},{2,6},{7,3},{3,7},{12,8},{8,12},{13,... | collective-permute-start | bytes 147464 | tf_op jit(solution)/shard_map/ppermute | solution.py:73
  25.8 3.0 %collective-permute-start.15 = (bf16[192,128]{1,0:T(8,128)(2,1)S(1)}, bf16[192,128]{1,0:T(8,128)(2,1)S(1)}, u32[]{:S(2)}, u32[]{:S(2)}) collective-permute-start(bf16[192,128]{1,0:T(8,128)(2,1)S(1)} %shard_map.140.refs_0_), channel_id=1, source_target_pairs={{1,0},{0,1},{3,2},{2,3},{5,4},{4,5},{7,6},{6,7},{9,8},{8,9},{11,10... | collective-permute-start | bytes 147464 | tf_op jit(solution)/shard_map/ppermute | solution.py:73
  27.2 5.4 %copy-start.8 = (bf16[3,3,128,128]{3,2,1,0:T(8,128)(2,1)S(1)}, bf16[3,3,128,128]{3,2,1,0:T(8,128)(2,1)}, u32[]{:S(2)}) copy-start(bf16[3,3,128,128]{3,2,1,0:T(8,128)(2,1)} %refs_4_.5) | copy-start | bytes 884740
  27.3 4.0 %collective-permute-start.14 = (bf16[192,128]{1,0:T(8,128)(2,1)S(1)}, bf16[192,128]{1,0:T(8,128)(2,1)S(1)}, u32[]{:S(2)}, u32[]{:S(2)}) collective-permute-start(bf16[192,128]{1,0:T(8,128)(2,1)S(1)} %shard_map.139.refs_0_), channel_id=1, source_target_pairs={{1,0},{0,1},{3,2},{2,3},{5,4},{4,5},{7,6},{6,7},{9,8},{8,9},{11,10... | collective-permute-start | bytes 147464 | tf_op jit(solution)/shard_map/ppermute | solution.py:73
  28.9 5.3 %collective-permute-start.17 = (bf16[192,128]{1,0:T(8,128)(2,1)S(1)}, bf16[192,128]{1,0:T(8,128)(2,1)S(1)}, u32[]{:S(2)}, u32[]{:S(2)}) collective-permute-start(bf16[192,128]{1,0:T(8,128)(2,1)S(1)} %shard_map.143.refs_2_), channel_id=1, source_target_pairs={{2,0},{3,1},{0,2},{1,3},{6,4},{7,5},{4,6},{5,7},{10,8},{11,9},{8,1... | collective-permute-start | bytes 147464 | tf_op jit(solution)/shard_map/ppermute | solution.py:73
  31.2 3.9 %collective-permute-start.16 = (bf16[192,128]{1,0:T(8,128)(2,1)S(1)}, bf16[192,128]{1,0:T(8,128)(2,1)S(1)}, u32[]{:S(2)}, u32[]{:S(2)}) collective-permute-start(bf16[192,128]{1,0:T(8,128)(2,1)S(1)} %shard_map.141.refs_5_.refs_0_), channel_id=1, source_target_pairs={{2,0},{3,1},{0,2},{1,3},{6,4},{7,5},{4,6},{5,7},{10,8},{11,9},{8,1... | collective-permute-start | bytes 147464 | tf_op jit(solution)/shard_map/ppermute | solution.py:73
  35.2 8.2 %collective-permute-start.20 = (bf16[2,192,128]{2,1,0:T(8,128)(2,1)S(1)}, bf16[2,192,128]{2,1,0:T(8,128)(2,1)S(1)}, u32[]{:S(2)}, u32[]{:S(2)}) collective-permute-start(bf16[2,192,128]{2,1,0:T(8,128)(2,1)S(1)} %shard_map.144.refs_0_), channel_id=1, source_target_pairs={{4,0},{0,4},{5,1},{1,5},{6,2},{2,6},{7,3},{3,7},{12,8},{8,12},{13,... | collective-permute-start | bytes 294920 | tf_op jit(solution)/shard_map/ppermute | solution.py:73
  36.3 8.3 %collective-permute-start.21 = (bf16[2,192,128]{2,1,0:T(8,128)(2,1)S(1)}, bf16[2,192,128]{2,1,0:T(8,128)(2,1)S(1)}, u32[]{:S(2)}, u32[]{:S(2)}) collective-permute-start(bf16[2,192,128]{2,1,0:T(8,128)(2,1)S(1)} %shard_map.144.refs_0_), channel_id=1, source_target_pairs={{16,0},{24,8},{0,16},{8,24},{17,1},{25,9},{1,17},{9,25},{18,2},{26... | collective-permute-start | bytes 294920 | tf_op jit(solution)/shard_map/ppermute | solution.py:73
  37.0 8.5 %collective-permute-start.18 = (bf16[2,192,128]{2,1,0:T(8,128)(2,1)S(1)}, bf16[2,192,128]{2,1,0:T(8,128)(2,1)S(1)}, u32[]{:S(2)}, u32[]{:S(2)}) collective-permute-start(bf16[2,192,128]{2,1,0:T(8,128)(2,1)S(1)} %shard_map.144.refs_0_), channel_id=1, source_target_pairs={{20,0},{16,4},{28,8},{24,12},{4,16},{0,20},{12,24},{8,28},{21,1},{... | collective-permute-start | bytes 294920 | tf_op jit(solution)/shard_map/ppermute | solution.py:81
  37.9 9.7 %collective-permute-start.22 = (bf16[2,192,128]{2,1,0:T(8,128)(2,1)S(1)}, bf16[2,192,128]{2,1,0:T(8,128)(2,1)S(1)}, u32[]{:S(2)}, u32[]{:S(2)}) collective-permute-start(bf16[2,192,128]{2,1,0:T(8,128)(2,1)S(1)} %shard_map.144.refs_0_), channel_id=1, source_target_pairs={{8,0},{0,8},{24,16},{16,24},{9,1},{1,9},{25,17},{17,25},{10,2},{2,... | collective-permute-start | bytes 294920 | tf_op jit(solution)/shard_map/ppermute | solution.py:73
  43.4 4.2 %collective-permute-start.23 = (bf16[2,192,128]{2,1,0:T(8,128)(2,1)S(1)}, bf16[2,192,128]{2,1,0:T(8,128)(2,1)S(1)}, u32[]{:S(2)}, u32[]{:S(2)}) collective-permute-start(bf16[2,192,128]{2,1,0:T(8,128)(2,1)S(1)} %collective-permute-done.20.refs_1_), channel_id=1, source_target_pairs={{8,0},{0,8},{24,16},{16,24},{9,1},{1,9},{25,17},{17,25},{10,2},{2,... | collective-permute-start | bytes 294920 | tf_op jit(solution)/shard_map/ppermute | solution.py:73
  44.6 3.0 %collective-permute-start.24 = (bf16[2,192,128]{2,1,0:T(8,128)(2,1)S(1)}, bf16[2,192,128]{2,1,0:T(8,128)(2,1)S(1)}, u32[]{:S(2)}, u32[]{:S(2)}) collective-permute-start(bf16[2,192,128]{2,1,0:T(8,128)(2,1)S(1)} %collective-permute-done.21.refs_2_), channel_id=1, source_target_pairs={{8,0},{0,8},{24,16},{16,24},{9,1},{1,9},{25,17},{17,25},{10,2},{2,... | collective-permute-start | bytes 294920 | tf_op jit(solution)/shard_map/ppermute | solution.py:73
  45.5 3.3 %collective-permute-start.19 = (bf16[2,192,128]{2,1,0:T(8,128)(2,1)S(1)}, bf16[2,192,128]{2,1,0:T(8,128)(2,1)S(1)}, u32[]{:S(2)}, u32[]{:S(2)}) collective-permute-start(bf16[2,192,128]{2,1,0:T(8,128)(2,1)S(1)} %collective-permute-done.18.refs_6_), channel_id=1, source_target_pairs={{8,0},{0,8},{24,16},{16,24},{9,1},{1,9},{25,17},{17,25},{10,2},{2,... | collective-permute-start | bytes 294920 | tf_op jit(solution)/shard_map/ppermute | solution.py:73
  (2 other events, 6.1 us)

commit v16 on v15

--- a/solution.py
+++ b/solution.py
@@ -386,8 +386,9 @@
 
 def band_kernel(own_ref, part_ref, keep_ref, send_ref):
     mine, other = halves(keep_ref.shape[0], lax.axis_index("video"))
+    half = keep_ref.shape[0]
     keep_ref[...] = own_ref[mine] + part_ref[mine].astype(jnp.float32)
-    send_ref[...] = (own_ref[other] + part_ref[other].astype(jnp.float32)).astype(jnp.bfloat16)
+    send_ref[:half] = (own_ref[other] + part_ref[other].astype(jnp.float32)).astype(jnp.bfloat16)
 
 
 def pair_quarter_kernel(keep_ref, part_ref, own_ref, across_ref, frame_ref, both_ref):
@@ -406,7 +407,7 @@
     rest = across_ref.shape[0] - half
     across_ref[half:] = part_ref[2 * height + rest :]
     frame_ref[...] = quarter(band, frames[1]).astype(jnp.bfloat16)
-    both_ref[:half] = quarter(1 - band, frames[1]).astype(jnp.bfloat16)
+    both_ref[...] = quarter(1 - band, frames[1]).astype(jnp.bfloat16)
 
 
 def plane_kernel(own_ref, *refs):
@@ -418,7 +419,7 @@
 
 
 def add_kernel(one_ref, two_ref, out_ref):
-    total = one_ref[...].astype(jnp.float32) + two_ref[...].astype(jnp.float32)
+    total = one_ref[...].astype(jnp.float32) + two_ref[: one_ref.shape[0]].astype(jnp.float32)
     out_ref[...] = total.astype(jnp.bfloat16)
 
 
@@ -681,16 +682,16 @@
 
         keep_two, send_two = call(
             band_kernel,
-            [f32(half, ch), bf16(half, ch)],
+            [f32(half, ch), bf16(half + cols + 16, ch)],
             [],
-            height * ch,
+            0,
             own_two,
             across_two,
         )
         sum_two = added(keep_two, flipped(send_two, "video", 1))
-        quarters = [f32(half, ch)] + [bf16(half + more, ch) for more in (cols, 0, cols + 16)]
+        quarters = [f32(half, ch), bf16(half + cols, ch)] + [bf16(half, ch)] * 2
         own_one, *sends = call(
-            pair_quarter_kernel, quarters, [], 8 * conv, keep_one, pair_one, after=(send_two,)
+            pair_quarter_kernel, quarters, [], 0, keep_one, pair_one, after=(send_two,)
         )
         across = flipped(sends[0], "section", 2)
         parts = [across, flipped(sends[1], "video", 1), flipped_both(sends[2])]

time: 49.8 us -> 47.3 us (0.950)
  starting transfers between devices: 32.7 us -> 30.4 us
    ppermute x23, waiting for transfers between devices: 6.69 us -> 4.72 us  [flipped(): lax.ppermute(block, axis, [(place ^ flip, place) for place in range(count)])]
    ppermute x2, waiting for transfers between devices: 0.01 us -> 1.78 us  [flipped_both(): return lax.ppermute(block, ('section', 'video'), pairs)]
    ppermute x23, starting transfers between devices: 29.7 us -> 28.4 us  [flipped(): lax.ppermute(block, axis, [(place ^ flip, place) for place in range(count)])]
    ppermute x2, starting transfers between devices: 3.01 us -> 2.03 us  [flipped_both(): return lax.ppermute(block, ('section', 'video'), pairs)]
  transfers between devices with their start and end apart: 25 -> 25, of which waited for: 7 -> 6; matrix products, arithmetic and copies ran while one was open for 0% -> 0% of each run, Pallas kernels for 17% -> 18%
where the time goes in v16:
time: 47.3 us; the launch traced here: 47.1 us
  starting transfers between devices  30.4 us (64%)
  Pallas kernels  9.27 us (20%)
  waiting for transfers between devices  6.51 us (14%)
  between operations  0.83 us (2%)
    ppermute x23, starting transfers between devices, flipped(): lax.ppermute(block, axis, [(place ^ flip, place) for place in range(count)])  28.4 us
    pallas_call x17, Pallas kernels, call(): pl.pallas_call(body, out_shape=outs[0] if single else tuple(outs), in_spe...  7.36 us
    ppermute x23, waiting for transfers between devices, flipped(): lax.ppermute(block, axis, [(place ^ flip, place) for place in range(count)])  4.72 us
    ppermute x2, starting transfers between devices, flipped_both(): return lax.ppermute(block, ('section', 'video'), pairs)  2.03 us
    pallas_call x2, Pallas kernels, placed(): pl.pallas_call(functools.partial(place_kernel, places), out_shape=outs, i...  1.91 us
    ppermute x2, waiting for transfers between devices, flipped_both(): return lax.ppermute(block, ('section', 'video'), pairs)  1.78 us
  transfers between devices with their start and end apart: 25, of which 6 were waited for; matrix products, arithmetic and copies ran while one was open for 0% of the time, Pallas kernels for 18%

profile of v16, /device:TPU:1, one launch (start us, length us, event | category | flops | bytes accessed | tf_op | source)
XLA Modules:
  0.0 47.1 jit_solution(13954324980758293609)
XLA Ops:
  0.6 2.1 %collective-permute-start.3 = (bf16[16,64,128]{2,1,0:T(8,128)(2,1)}, bf16[16,64,128]{2,1,0:T(8,128)(2,1)S(1)}, u32[]{:S(2)}, u32[]{:S(2)}) collective-permute-start(bf16[16,64,128]{2,1,0:T(8,128)(2,1)} %bitcast.10), channel_id=1, source_target_pairs={{4,0},{0,4},{5,1},{1,5},{6,2},{2,6},{7,3},{3,7},{12,8},{8,12},{13,... | collective-permute-start | bytes 786440 | tf_op jit(solution)/shard_map/ppermute | solution.py:73
  2.7 1.6 %shard_map.128 = (bf16[4,64,128]{2,1,0:T(8,128)(2,1)}, bf16[4,64,128]{2,1,0:T(8,128)(2,1)}) custom-call(bf16[16,64,128]{2,1,0:T(8,128)(2,1)} %bitcast.11, bf16[16,64,128]{2,1,0:T(8,128)(2,1)} %bitcast.17, bf16[16,64,128]{2,1,0:T(8,128)(2,1)} %bitcast.28, bf16[16,64,128]{2,1,0:T(8,128)(2,1)} %bitcast.25), custom_call_target="tpu_custom_call" | custom-call | flops 1 | bytes 1179648 | tf_op jit(solution)/shard_map/pallas_call | solution.py:38
  4.4 1.0 %collective-permute-start = (bf16[4,64,128]{2,1,0:T(8,128)(2,1)}, bf16[4,64,128]{2,1,0:T(8,128)(2,1)S(1)}, u32[]{:S(2)}, u32[]{:S(2)}) collective-permute-start(bf16[4,64,128]{2,1,0:T(8,128)(2,1)} %get-tuple-element.43), channel_id=1, source_target_pairs={{8,0},{0,8},{24,16},{16,24},{9,1},{1,9},{25,17},{17,25},{10,2},{2,... | collective-permute-start | bytes 196616 | tf_op jit(solution)/shard_map/ppermute | solution.py:73
  5.4 1.1 %collective-permute-done.refs_5_ = bf16[4,64,128]{2,1,0:T(8,128)(2,1)S(1)} collective-permute-done((bf16[4,64,128]{2,1,0:T(8,128)(2,1)}, bf16[4,64,128]{2,1,0:T(8,128)(2,1)S(1)}, u32[]{:S(2)}, u32[]{:S(2)}) %collective-permute-start) | collective-permute-done | bytes 65568 | tf_op jit(solution)/shard_map/ppermute | solution.py:73
  6.9 1.2 %collective-permute-start.2 = (bf16[4,64,128]{2,1,0:T(8,128)(2,1)S(1)}, bf16[4,64,128]{2,1,0:T(8,128)(2,1)S(1)}, u32[]{:S(2)}, u32[]{:S(2)}) collective-permute-start(bf16[4,64,128]{2,1,0:T(8,128)(2,1)S(1)} %collective-permute-done.refs_5_), channel_id=1, source_target_pairs={{16,0},{24,8},{0,16},{8,24},{17,1},{25,9},{1,17},{9,25},{18,2},{26... | collective-permute-start | bytes 196616 | tf_op jit(solution)/shard_map/ppermute | solution.py:73
  8.2 1.3 %collective-permute-start.4 = (bf16[14,64,128]{2,1,0:T(8,128)(2,1)S(1)}, bf16[14,64,128]{2,1,0:T(8,128)(2,1)S(1)}, u32[]{:S(2)}, u32[]{:S(2)}) collective-permute-start(bf16[14,64,128]{2,1,0:T(8,128)(2,1)S(1)} %get-tuple-element.45.refs_5_), channel_id=1, source_target_pairs={{4,0},{0,4},{5,1},{1,5},{6,2},{2,6},{7,3},{3,7},{12,8},{8,12},{13,... | collective-permute-start | bytes 688136 | tf_op jit(solution)/shard_map/ppermute | solution.py:73
  9.6 1.0 %shard_map.130 = (bf16[14,64,128]{2,1,0:T(8,128)(2,1)S(1)}, bf16[16,64,128]{2,1,0:T(8,128)(2,1)S(1)}) custom-call(bf16[16,64,128]{2,1,0:T(8,128)(2,1)S(1)} %bitcast.13, bf16[16,64,128]{2,1,0:T(8,128)(2,1)S(1)} %bitcast.19, bf16[16,64,128]{2,1,0:T(8,128)(2,1)S(1)} %collective-permute-done.3.refs_2_.refs_6_, bf16[3,128,128]{2,1,0:T(8,128)(2,1)S(1)} %copy-done.6, ...), custom_call_target="tpu_custom_call" | custom-call | tf_op jit(solution)/shard_map/pallas_call | solution.py:38
  10.6 0.9 %shard_map.132 = (f32[2,384,128]{2,1,0:T(8,128)S(1)}, bf16[384,128]{1,0:T(8,128)(2,1)S(1)}, bf16[384,128]{1,0:T(8,128)(2,1)S(1)}) custom-call(bf16[16,64,128]{2,1,0:T(8,128)(2,1)S(1)} %bitcast.30, bf16[16,64,128]{2,1,0:T(8,128)(2,1)S(1)} %bitcast.20, bf16[16,64,128]{2,1,0:T(8,128)(2,1)S(1)} %get-tuple-element.48.refs_6_.refs_2_.refs_4_, ...), custom_call_target="tpu_custom_call" | custom-call | flops 2415919104 | bytes 2031616 | tf_op jit(solution)/shard_map/pallas_call | solution.py:38
  11.5 0.9 %collective-permute-start.6 = (bf16[384,128]{1,0:T(8,128)(2,1)S(1)}, bf16[384,128]{1,0:T(8,128)(2,1)S(1)}, u32[]{:S(2)}, u32[]{:S(2)}) collective-permute-start(bf16[384,128]{1,0:T(8,128)(2,1)S(1)} %get-tuple-element.52), channel_id=1, source_target_pairs={{8,0},{0,8},{24,16},{16,24},{9,1},{1,9},{25,17},{17,25},{10,2},{2,... | collective-permute-start | bytes 294920 | tf_op jit(solution)/shard_map/ppermute | solution.py:73
  12.4 0.8 %collective-permute-start.5 = (bf16[4,64,128]{2,1,0:T(8,128)(2,1)S(1)}, bf16[4,64,128]{2,1,0:T(8,128)(2,1)S(1)}, u32[]{:S(2)}, u32[]{:S(2)}) collective-permute-start(bf16[4,64,128]{2,1,0:T(8,128)(2,1)S(1)} %shard_map.131.refs_7_), channel_id=1, source_target_pairs={{4,0},{0,4},{5,1},{1,5},{6,2},{2,6},{7,3},{3,7},{12,8},{8,12},{13,... | collective-permute-start | bytes 196616 | tf_op jit(solution)/shard_map/ppermute | solution.py:73
  13.7 1.4 %collective-permute-start.8 = (bf16[384,128]{1,0:T(8,128)(2,1)S(1)}, bf16[384,128]{1,0:T(8,128)(2,1)S(1)}, u32[]{:S(2)}, u32[]{:S(2)}) collective-permute-start(bf16[384,128]{1,0:T(8,128)(2,1)S(1)} %get-tuple-element.58), channel_id=1, source_target_pairs={{16,0},{24,8},{0,16},{8,24},{17,1},{25,9},{1,17},{9,25},{18,2},{26... | collective-permute-start | bytes 294920 | tf_op jit(solution)/shard_map/ppermute | solution.py:73
  15.6 1.0 %collective-permute-done.5.refs_6_ = bf16[4,64,128]{2,1,0:T(8,128)(2,1)S(1)} collective-permute-done((bf16[4,64,128]{2,1,0:T(8,128)(2,1)S(1)}, bf16[4,64,128]{2,1,0:T(8,128)(2,1)S(1)}, u32[]{:S(2)}, u32[]{:S(2)}) %collective-permute-start.5) | collective-permute-done | bytes 65568 | tf_op jit(solution)/shard_map/ppermute | solution.py:73
  16.6 1.3 %shard_map.136 = (bf16[16,64,128]{2,1,0:T(8,128)(2,1)S(1)}, bf16[16,64,128]{2,1,0:T(8,128)(2,1)S(1)}, f32[2,384,128]{2,1,0:T(8,128)S(1)}, bf16[896,128]{1,0:T(8,128)(2,1)S(1)}) custom-call(bf16[16,64,128]{2,1,0:T(8,128)(2,1)S(1)} %bitcast.16, bf16[4,64,128]{2,1,0:T(8,128)(2,1)S(1)} %collective-permute-done.1.refs_4_.refs_1_.refs_3_.refs_2_, ...), custom_call_target="tpu_custom_call" | custom-call | flops 2415919104 | bytes 5046272 | tf_op jit(solution)/shard_map/pallas_call | solution.py:38
  17.9 1.2 %collective-permute-start.9 = (bf16[896,128]{1,0:T(8,128)(2,1)S(1)}, bf16[896,128]{1,0:T(8,128)(2,1)S(1)}, u32[]{:S(2)}, u32[]{:S(2)}) collective-permute-start(bf16[896,128]{1,0:T(8,128)(2,1)S(1)} %get-tuple-element.59), channel_id=1, source_target_pairs={{8,0},{0,8},{24,16},{16,24},{9,1},{1,9},{25,17},{17,25},{10,2},{2,... | collective-permute-start | bytes 688136 | tf_op jit(solution)/shard_map/ppermute | solution.py:73
  19.1 1.3 %collective-permute-start.13 = (bf16[272,128]{1,0:T(8,128)(2,1)S(1)}, bf16[272,128]{1,0:T(8,128)(2,1)S(1)}, u32[]{:S(2)}, u32[]{:S(2)}) collective-permute-start(bf16[272,128]{1,0:T(8,128)(2,1)S(1)} %get-tuple-element.61.refs_2_), channel_id=1, source_target_pairs={{4,0},{0,4},{5,1},{1,5},{6,2},{2,6},{7,3},{3,7},{12,8},{8,12},{13,... | collective-permute-start | bytes 208904 | tf_op jit(solution)/shard_map/ppermute | solution.py:73
  20.5 1.2 %collective-permute-start.10 = (bf16[256,128]{1,0:T(8,128)(2,1)S(1)}, bf16[256,128]{1,0:T(8,128)(2,1)S(1)}, u32[]{:S(2)}, u32[]{:S(2)}) collective-permute-start(bf16[256,128]{1,0:T(8,128)(2,1)S(1)} %get-tuple-element.62), channel_id=1, source_target_pairs={{16,0},{24,8},{0,16},{8,24},{17,1},{25,9},{1,17},{9,25},{18,2},{26... | collective-permute-start | bytes 196616 | tf_op jit(solution)/shard_map/ppermute | solution.py:73
  21.7 1.0 %collective-permute-start.11 = (bf16[192,128]{1,0:T(8,128)(2,1)S(1)}, bf16[192,128]{1,0:T(8,128)(2,1)S(1)}, u32[]{:S(2)}, u32[]{:S(2)}) collective-permute-start(bf16[192,128]{1,0:T(8,128)(2,1)S(1)} %get-tuple-element.64), channel_id=1, source_target_pairs={{4,0},{0,4},{5,1},{1,5},{6,2},{2,6},{7,3},{3,7},{12,8},{8,12},{13,... | collective-permute-start | bytes 147464 | tf_op jit(solution)/shard_map/ppermute | solution.py:73
  22.7 0.5 %collective-permute-start.12 = (bf16[192,128]{1,0:T(8,128)(2,1)S(1)}, bf16[192,128]{1,0:T(8,128)(2,1)S(1)}, u32[]{:S(2)}, u32[]{:S(2)}) collective-permute-start(bf16[192,128]{1,0:T(8,128)(2,1)S(1)} %get-tuple-element.65), channel_id=1, source_target_pairs={{20,0},{16,4},{28,8},{24,12},{4,16},{0,20},{12,24},{8,28},{21,1},{... | collective-permute-start | bytes 147464 | tf_op jit(solution)/shard_map/ppermute | solution.py:81
  23.2 1.4 %collective-permute-start.15 = (bf16[192,128]{1,0:T(8,128)(2,1)S(1)}, bf16[192,128]{1,0:T(8,128)(2,1)S(1)}, u32[]{:S(2)}, u32[]{:S(2)}) collective-permute-start(bf16[192,128]{1,0:T(8,128)(2,1)S(1)} %shard_map.140.refs_0_), channel_id=1, source_target_pairs={{1,0},{0,1},{3,2},{2,3},{5,4},{4,5},{7,6},{6,7},{9,8},{8,9},{11,10... | collective-permute-start | bytes 147464 | tf_op jit(solution)/shard_map/ppermute | solution.py:73
  24.8 1.8 %collective-permute-done.12.refs_3_ = bf16[192,128]{1,0:T(8,128)(2,1)S(1)} collective-permute-done((bf16[192,128]{1,0:T(8,128)(2,1)S(1)}, bf16[192,128]{1,0:T(8,128)(2,1)S(1)}, u32[]{:S(2)}, u32[]{:S(2)}) %collective-permute-start.12) | collective-permute-done | bytes 49184 | tf_op jit(solution)/shard_map/ppermute | solution.py:81
  26.6 1.4 %collective-permute-start.14 = (bf16[192,128]{1,0:T(8,128)(2,1)S(1)}, bf16[192,128]{1,0:T(8,128)(2,1)S(1)}, u32[]{:S(2)}, u32[]{:S(2)}) collective-permute-start(bf16[192,128]{1,0:T(8,128)(2,1)S(1)} %shard_map.139.refs_0_), channel_id=1, source_target_pairs={{1,0},{0,1},{3,2},{2,3},{5,4},{4,5},{7,6},{6,7},{9,8},{8,9},{11,10... | collective-permute-start | bytes 147464 | tf_op jit(solution)/shard_map/ppermute | solution.py:73
  28.0 2.4 %collective-permute-start.17 = (bf16[192,128]{1,0:T(8,128)(2,1)S(1)}, bf16[192,128]{1,0:T(8,128)(2,1)S(1)}, u32[]{:S(2)}, u32[]{:S(2)}) collective-permute-start(bf16[192,128]{1,0:T(8,128)(2,1)S(1)} %shard_map.143.refs_2_), channel_id=1, source_target_pairs={{2,0},{3,1},{0,2},{1,3},{6,4},{7,5},{4,6},{5,7},{10,8},{11,9},{8,1... | collective-permute-start | bytes 147464 | tf_op jit(solution)/shard_map/ppermute | solution.py:73
  30.3 1.6 %collective-permute-start.16 = (bf16[192,128]{1,0:T(8,128)(2,1)S(1)}, bf16[192,128]{1,0:T(8,128)(2,1)S(1)}, u32[]{:S(2)}, u32[]{:S(2)}) collective-permute-start(bf16[192,128]{1,0:T(8,128)(2,1)S(1)} %shard_map.141.refs_5_.refs_0_), channel_id=1, source_target_pairs={{2,0},{3,1},{0,2},{1,3},{6,4},{7,5},{4,6},{5,7},{10,8},{11,9},{8,1... | collective-permute-start | bytes 147464 | tf_op jit(solution)/shard_map/ppermute | solution.py:73
  32.0 1.5 %shard_map.142 = (bf16[16,64,128]{2,1,0:T(8,128)(2,1)}, f32[8,128]{1,0:T(8,128)S(1)}) custom-call(bf16[16,64,128]{2,1,0:T(8,128)(2,1)S(1)} %get-tuple-element.55.refs_0_, bf16[16,64,128]{2,1,0:T(8,128)(2,1)S(1)} %get-tuple-element.56.refs_1_, bf16[896,128]{1,0:T(8,128)(2,1)S(1)} %collective-permute-done.9.refs_1_.refs_2_, ...), custom_call_target="tpu_custom_call" | custom-call | flops 301989888 | bytes 1380352 | tf_op jit(solution)/shard_map/pallas_call | solution.py:38
  33.5 2.4 %collective-permute-done.16.refs_1_ = bf16[192,128]{1,0:T(8,128)(2,1)S(1)} collective-permute-done((bf16[192,128]{1,0:T(8,128)(2,1)S(1)}, bf16[192,128]{1,0:T(8,128)(2,1)S(1)}, u32[]{:S(2)}, u32[]{:S(2)}) %collective-permute-start.16) | collective-permute-done | bytes 49184 | tf_op jit(solution)/shard_map/ppermute | solution.py:73
  35.9 1.1 %collective-permute-start.20 = (bf16[2,192,128]{2,1,0:T(8,128)(2,1)S(1)}, bf16[2,192,128]{2,1,0:T(8,128)(2,1)S(1)}, u32[]{:S(2)}, u32[]{:S(2)}) collective-permute-start(bf16[2,192,128]{2,1,0:T(8,128)(2,1)S(1)} %shard_map.144.refs_0_), channel_id=1, source_target_pairs={{4,0},{0,4},{5,1},{1,5},{6,2},{2,6},{7,3},{3,7},{12,8},{8,12},{13,... | collective-permute-start | bytes 294920 | tf_op jit(solution)/shard_map/ppermute | solution.py:73
  37.1 1.5 %collective-permute-start.18 = (bf16[2,192,128]{2,1,0:T(8,128)(2,1)S(1)}, bf16[2,192,128]{2,1,0:T(8,128)(2,1)S(1)}, u32[]{:S(2)}, u32[]{:S(2)}) collective-permute-start(bf16[2,192,128]{2,1,0:T(8,128)(2,1)S(1)} %shard_map.144.refs_0_), channel_id=1, source_target_pairs={{20,0},{16,4},{28,8},{24,12},{4,16},{0,20},{12,24},{8,28},{21,1},{... | collective-permute-start | bytes 294920 | tf_op jit(solution)/shard_map/ppermute | solution.py:81
  38.6 3.0 %collective-permute-start.22 = (bf16[2,192,128]{2,1,0:T(8,128)(2,1)S(1)}, bf16[2,192,128]{2,1,0:T(8,128)(2,1)S(1)}, u32[]{:S(2)}, u32[]{:S(2)}) collective-permute-start(bf16[2,192,128]{2,1,0:T(8,128)(2,1)S(1)} %shard_map.144.refs_0_), channel_id=1, source_target_pairs={{8,0},{0,8},{24,16},{16,24},{9,1},{1,9},{25,17},{17,25},{10,2},{2,... | collective-permute-start | bytes 294920 | tf_op jit(solution)/shard_map/ppermute | solution.py:73
  41.6 1.8 %collective-permute-start.23 = (bf16[2,192,128]{2,1,0:T(8,128)(2,1)S(1)}, bf16[2,192,128]{2,1,0:T(8,128)(2,1)S(1)}, u32[]{:S(2)}, u32[]{:S(2)}) collective-permute-start(bf16[2,192,128]{2,1,0:T(8,128)(2,1)S(1)} %collective-permute-done.20.refs_1_), channel_id=1, source_target_pairs={{8,0},{0,8},{24,16},{16,24},{9,1},{1,9},{25,17},{17,25},{10,2},{2,... | collective-permute-start | bytes 294920 | tf_op jit(solution)/shard_map/ppermute | solution.py:73
  43.6 1.5 %collective-permute-start.19 = (bf16[2,192,128]{2,1,0:T(8,128)(2,1)S(1)}, bf16[2,192,128]{2,1,0:T(8,128)(2,1)S(1)}, u32[]{:S(2)}, u32[]{:S(2)}) collective-permute-start(bf16[2,192,128]{2,1,0:T(8,128)(2,1)S(1)} %collective-permute-done.18.refs_6_), channel_id=1, source_target_pairs={{8,0},{0,8},{24,16},{16,24},{9,1},{1,9},{25,17},{17,25},{10,2},{2,... | collective-permute-start | bytes 294920 | tf_op jit(solution)/shard_map/ppermute | solution.py:73
  45.2 1.2 %shard_map.145 = (f32[3,384,128]{2,1,0:T(8,128)}, f32[384,128]{1,0:T(8,128)}, f32[3,384,128]{2,1,0:T(8,128)}, f32[384,128]{1,0:T(8,128)}) custom-call(bf16[2,192,128]{2,1,0:T(8,128)(2,1)S(1)} %shard_map.144.refs_0_, bf16[2,192,128]{2,1,0:T(8,128)(2,1)S(1)} %collective-permute-done.20.refs_1_, bf16[2,192,128]{2,1,0:T(8,128)(2,1)S(1)} %collective-permute-done.21.refs_2_, ...), custom_call_target="tpu_custom_call" | custom-call | bytes 2064384 | tf_op jit(solution)/shard_map/pallas_call | solution.py:467
  46.4 0.7 %shard_map.146 = (f32[3,384,128]{2,1,0:T(8,128)}, f32[384,128]{1,0:T(8,128)}, f32[3,384,128]{2,1,0:T(8,128)}, f32[384,128]{1,0:T(8,128)}) custom-call(bf16[2,192,128]{2,1,0:T(8,128)(2,1)S(1)} %collective-permute-done.19.refs_0_, f32[3,384,128]{2,1,0:T(8,128)} %get-tuple-element.71.refs_1_, ...), custom_call_target="tpu_custom_call", output_to_operand_aliasing={{0}: (1, {}), {1}: (2, {}), {2}: (3, {}), {3}: (4, {})} | custom-call | bytes 294912 | tf_op jit(solution)/shard_map/pallas_call | solution.py:467
  (55 shorter events, 2.1 us)
Async XLA Ops:
  0.6 8.9 %collective-permute-start.3 = (bf16[16,64,128]{2,1,0:T(8,128)(2,1)}, bf16[16,64,128]{2,1,0:T(8,128)(2,1)S(1)}, u32[]{:S(2)}, u32[]{:S(2)}) collective-permute-start(bf16[16,64,128]{2,1,0:T(8,128)(2,1)} %bitcast.10), channel_id=1, source_target_pairs={{4,0},{0,4},{5,1},{1,5},{6,2},{2,6},{7,3},{3,7},{12,8},{8,12},{13,... | collective-permute-start | bytes 786440 | tf_op jit(solution)/shard_map/ppermute | solution.py:73
  2.7 5.4 %copy-start = (bf16[1,1,16,64,128]{4,3,2,1,0:T(8,128)(2,1)S(1)}, bf16[1,1,16,64,128]{4,3,2,1,0:T(8,128)(2,1)}, u32[]{:S(2)}) copy-start(bf16[1,1,16,64,128]{4,3,2,1,0:T(8,128)(2,1)} %param.9) | copy-start | bytes 786436
  2.7 5.4 %copy-start.1 = (bf16[3,3,128,128]{3,2,1,0:T(8,128)(2,1)S(1)}, bf16[3,3,128,128]{3,2,1,0:T(8,128)(2,1)}, u32[]{:S(2)}) copy-start(bf16[3,3,128,128]{3,2,1,0:T(8,128)(2,1)} %refs_8_.1) | copy-start | bytes 884740
  2.7 5.4 %copy-start.2 = (bf16[1,1,16,64,128]{4,3,2,1,0:T(8,128)(2,1)S(1)}, bf16[1,1,16,64,128]{4,3,2,1,0:T(8,128)(2,1)}, u32[]{:S(2)}) copy-start(bf16[1,1,16,64,128]{4,3,2,1,0:T(8,128)(2,1)} %param.13) | copy-start | bytes 786436
  2.7 5.4 %copy-start.6 = (bf16[3,128,128]{2,1,0:T(8,128)(2,1)S(1)}, bf16[3,128,128]{2,1,0:T(8,128)(2,1)}, u32[]{:S(2)}) copy-start(bf16[3,128,128]{2,1,0:T(8,128)(2,1)} %refs_7_.1) | copy-start | bytes 294916
  4.4 2.1 %collective-permute-start = (bf16[4,64,128]{2,1,0:T(8,128)(2,1)}, bf16[4,64,128]{2,1,0:T(8,128)(2,1)S(1)}, u32[]{:S(2)}, u32[]{:S(2)}) collective-permute-start(bf16[4,64,128]{2,1,0:T(8,128)(2,1)} %get-tuple-element.43), channel_id=1, source_target_pairs={{8,0},{0,8},{24,16},{16,24},{9,1},{1,9},{25,17},{17,25},{10,2},{2,... | collective-permute-start | bytes 196616 | tf_op jit(solution)/shard_map/ppermute | solution.py:73
  6.5 3.0 %copy-start.5 = (bf16[1,1,16,64,128]{4,3,2,1,0:T(8,128)(2,1)S(1)}, bf16[1,1,16,64,128]{4,3,2,1,0:T(8,128)(2,1)}, u32[]{:S(2)}) copy-start(bf16[1,1,16,64,128]{4,3,2,1,0:T(8,128)(2,1)} %param.12) | copy-start | bytes 786436
  6.5 3.0 %copy-start.7 = (bf16[3,128,128]{2,1,0:T(8,128)(2,1)S(1)}, bf16[3,128,128]{2,1,0:T(8,128)(2,1)}, u32[]{:S(2)}) copy-start(bf16[3,128,128]{2,1,0:T(8,128)(2,1)} %refs_11_.1) | copy-start | bytes 294916
  6.5 1.7 %collective-permute-start.1 = (bf16[4,64,128]{2,1,0:T(8,128)(2,1)}, bf16[4,64,128]{2,1,0:T(8,128)(2,1)S(1)}, u32[]{:S(2)}, u32[]{:S(2)}) collective-permute-start(bf16[4,64,128]{2,1,0:T(8,128)(2,1)} %get-tuple-element.44), channel_id=1, source_target_pairs={{8,0},{0,8},{24,16},{16,24},{9,1},{1,9},{25,17},{17,25},{10,2},{2,... | collective-permute-start | bytes 196616 | tf_op jit(solution)/shard_map/ppermute | solution.py:73
  6.9 3.6 %collective-permute-start.2 = (bf16[4,64,128]{2,1,0:T(8,128)(2,1)S(1)}, bf16[4,64,128]{2,1,0:T(8,128)(2,1)S(1)}, u32[]{:S(2)}, u32[]{:S(2)}) collective-permute-start(bf16[4,64,128]{2,1,0:T(8,128)(2,1)S(1)} %collective-permute-done.refs_5_), channel_id=1, source_target_pairs={{16,0},{24,8},{0,16},{8,24},{17,1},{25,9},{1,17},{9,25},{18,2},{26... | collective-permute-start | bytes 196616 | tf_op jit(solution)/shard_map/ppermute | solution.py:73
  8.2 6.9 %collective-permute-start.4 = (bf16[14,64,128]{2,1,0:T(8,128)(2,1)S(1)}, bf16[14,64,128]{2,1,0:T(8,128)(2,1)S(1)}, u32[]{:S(2)}, u32[]{:S(2)}) collective-permute-start(bf16[14,64,128]{2,1,0:T(8,128)(2,1)S(1)} %get-tuple-element.45.refs_5_), channel_id=1, source_target_pairs={{4,0},{0,4},{5,1},{1,5},{6,2},{2,6},{7,3},{3,7},{12,8},{8,12},{13,... | collective-permute-start | bytes 688136 | tf_op jit(solution)/shard_map/ppermute | solution.py:73
  11.5 2.1 %collective-permute-start.6 = (bf16[384,128]{1,0:T(8,128)(2,1)S(1)}, bf16[384,128]{1,0:T(8,128)(2,1)S(1)}, u32[]{:S(2)}, u32[]{:S(2)}) collective-permute-start(bf16[384,128]{1,0:T(8,128)(2,1)S(1)} %get-tuple-element.52), channel_id=1, source_target_pairs={{8,0},{0,8},{24,16},{16,24},{9,1},{1,9},{25,17},{17,25},{10,2},{2,... | collective-permute-start | bytes 294920 | tf_op jit(solution)/shard_map/ppermute | solution.py:73
  12.4 1.3 %collective-permute-start.7 = (bf16[384,128]{1,0:T(8,128)(2,1)S(1)}, bf16[384,128]{1,0:T(8,128)(2,1)S(1)}, u32[]{:S(2)}, u32[]{:S(2)}) collective-permute-start(bf16[384,128]{1,0:T(8,128)(2,1)S(1)} %get-tuple-element.53), channel_id=1, source_target_pairs={{8,0},{0,8},{24,16},{16,24},{9,1},{1,9},{25,17},{17,25},{10,2},{2,... | collective-permute-start | bytes 294920 | tf_op jit(solution)/shard_map/ppermute | solution.py:73
  12.4 4.2 %collective-permute-start.5 = (bf16[4,64,128]{2,1,0:T(8,128)(2,1)S(1)}, bf16[4,64,128]{2,1,0:T(8,128)(2,1)S(1)}, u32[]{:S(2)}, u32[]{:S(2)}) collective-permute-start(bf16[4,64,128]{2,1,0:T(8,128)(2,1)S(1)} %shard_map.131.refs_7_), channel_id=1, source_target_pairs={{4,0},{0,4},{5,1},{1,5},{6,2},{2,6},{7,3},{3,7},{12,8},{8,12},{13,... | collective-permute-start | bytes 196616 | tf_op jit(solution)/shard_map/ppermute | solution.py:73
  13.7 4.2 %collective-permute-start.8 = (bf16[384,128]{1,0:T(8,128)(2,1)S(1)}, bf16[384,128]{1,0:T(8,128)(2,1)S(1)}, u32[]{:S(2)}, u32[]{:S(2)}) collective-permute-start(bf16[384,128]{1,0:T(8,128)(2,1)S(1)} %get-tuple-element.58), channel_id=1, source_target_pairs={{16,0},{24,8},{0,16},{8,24},{17,1},{25,9},{1,17},{9,25},{18,2},{26... | collective-permute-start | bytes 294920 | tf_op jit(solution)/shard_map/ppermute | solution.py:73
  17.9 2.5 %collective-permute-start.9 = (bf16[896,128]{1,0:T(8,128)(2,1)S(1)}, bf16[896,128]{1,0:T(8,128)(2,1)S(1)}, u32[]{:S(2)}, u32[]{:S(2)}) collective-permute-start(bf16[896,128]{1,0:T(8,128)(2,1)S(1)} %get-tuple-element.59), channel_id=1, source_target_pairs={{8,0},{0,8},{24,16},{16,24},{9,1},{1,9},{25,17},{17,25},{10,2},{2,... | collective-permute-start | bytes 688136 | tf_op jit(solution)/shard_map/ppermute | solution.py:73
  19.1 4.1 %collective-permute-start.13 = (bf16[272,128]{1,0:T(8,128)(2,1)S(1)}, bf16[272,128]{1,0:T(8,128)(2,1)S(1)}, u32[]{:S(2)}, u32[]{:S(2)}) collective-permute-start(bf16[272,128]{1,0:T(8,128)(2,1)S(1)} %get-tuple-element.61.refs_2_), channel_id=1, source_target_pairs={{4,0},{0,4},{5,1},{1,5},{6,2},{2,6},{7,3},{3,7},{12,8},{8,12},{13,... | collective-permute-start | bytes 208904 | tf_op jit(solution)/shard_map/ppermute | solution.py:73
  20.5 6.0 %collective-permute-start.10 = (bf16[256,128]{1,0:T(8,128)(2,1)S(1)}, bf16[256,128]{1,0:T(8,128)(2,1)S(1)}, u32[]{:S(2)}, u32[]{:S(2)}) collective-permute-start(bf16[256,128]{1,0:T(8,128)(2,1)S(1)} %get-tuple-element.62), channel_id=1, source_target_pairs={{16,0},{24,8},{0,16},{8,24},{17,1},{25,9},{1,17},{9,25},{18,2},{26... | collective-permute-start | bytes 196616 | tf_op jit(solution)/shard_map/ppermute | solution.py:73
  21.7 3.1 %collective-permute-start.11 = (bf16[192,128]{1,0:T(8,128)(2,1)S(1)}, bf16[192,128]{1,0:T(8,128)(2,1)S(1)}, u32[]{:S(2)}, u32[]{:S(2)}) collective-permute-start(bf16[192,128]{1,0:T(8,128)(2,1)S(1)} %get-tuple-element.64), channel_id=1, source_target_pairs={{4,0},{0,4},{5,1},{1,5},{6,2},{2,6},{7,3},{3,7},{12,8},{8,12},{13,... | collective-permute-start | bytes 147464 | tf_op jit(solution)/shard_map/ppermute | solution.py:73
  22.7 3.8 %collective-permute-start.12 = (bf16[192,128]{1,0:T(8,128)(2,1)S(1)}, bf16[192,128]{1,0:T(8,128)(2,1)S(1)}, u32[]{:S(2)}, u32[]{:S(2)}) collective-permute-start(bf16[192,128]{1,0:T(8,128)(2,1)S(1)} %get-tuple-element.65), channel_id=1, source_target_pairs={{20,0},{16,4},{28,8},{24,12},{4,16},{0,20},{12,24},{8,28},{21,1},{... | collective-permute-start | bytes 147464 | tf_op jit(solution)/shard_map/ppermute | solution.py:81
  23.2 4.7 %collective-permute-start.15 = (bf16[192,128]{1,0:T(8,128)(2,1)S(1)}, bf16[192,128]{1,0:T(8,128)(2,1)S(1)}, u32[]{:S(2)}, u32[]{:S(2)}) collective-permute-start(bf16[192,128]{1,0:T(8,128)(2,1)S(1)} %shard_map.140.refs_0_), channel_id=1, source_target_pairs={{1,0},{0,1},{3,2},{2,3},{5,4},{4,5},{7,6},{6,7},{9,8},{8,9},{11,10... | collective-permute-start | bytes 147464 | tf_op jit(solution)/shard_map/ppermute | solution.py:73
  26.5 5.4 %copy-start.8 = (bf16[3,3,128,128]{3,2,1,0:T(8,128)(2,1)S(1)}, bf16[3,3,128,128]{3,2,1,0:T(8,128)(2,1)}, u32[]{:S(2)}) copy-start(bf16[3,3,128,128]{3,2,1,0:T(8,128)(2,1)} %refs_4_.5) | copy-start | bytes 884740
  26.6 3.8 %collective-permute-start.14 = (bf16[192,128]{1,0:T(8,128)(2,1)S(1)}, bf16[192,128]{1,0:T(8,128)(2,1)S(1)}, u32[]{:S(2)}, u32[]{:S(2)}) collective-permute-start(bf16[192,128]{1,0:T(8,128)(2,1)S(1)} %shard_map.139.refs_0_), channel_id=1, source_target_pairs={{1,0},{0,1},{3,2},{2,3},{5,4},{4,5},{7,6},{6,7},{9,8},{8,9},{11,10... | collective-permute-start | bytes 147464 | tf_op jit(solution)/shard_map/ppermute | solution.py:73
  28.0 5.5 %collective-permute-start.17 = (bf16[192,128]{1,0:T(8,128)(2,1)S(1)}, bf16[192,128]{1,0:T(8,128)(2,1)S(1)}, u32[]{:S(2)}, u32[]{:S(2)}) collective-permute-start(bf16[192,128]{1,0:T(8,128)(2,1)S(1)} %shard_map.143.refs_2_), channel_id=1, source_target_pairs={{2,0},{3,1},{0,2},{1,3},{6,4},{7,5},{4,6},{5,7},{10,8},{11,9},{8,1... | collective-permute-start | bytes 147464 | tf_op jit(solution)/shard_map/ppermute | solution.py:73
  30.3 5.5 %collective-permute-start.16 = (bf16[192,128]{1,0:T(8,128)(2,1)S(1)}, bf16[192,128]{1,0:T(8,128)(2,1)S(1)}, u32[]{:S(2)}, u32[]{:S(2)}) collective-permute-start(bf16[192,128]{1,0:T(8,128)(2,1)S(1)} %shard_map.141.refs_5_.refs_0_), channel_id=1, source_target_pairs={{2,0},{3,1},{0,2},{1,3},{6,4},{7,5},{4,6},{5,7},{10,8},{11,9},{8,1... | collective-permute-start | bytes 147464 | tf_op jit(solution)/shard_map/ppermute | solution.py:73
  35.9 5.8 %collective-permute-start.20 = (bf16[2,192,128]{2,1,0:T(8,128)(2,1)S(1)}, bf16[2,192,128]{2,1,0:T(8,128)(2,1)S(1)}, u32[]{:S(2)}, u32[]{:S(2)}) collective-permute-start(bf16[2,192,128]{2,1,0:T(8,128)(2,1)S(1)} %shard_map.144.refs_0_), channel_id=1, source_target_pairs={{4,0},{0,4},{5,1},{1,5},{6,2},{2,6},{7,3},{3,7},{12,8},{8,12},{13,... | collective-permute-start | bytes 294920 | tf_op jit(solution)/shard_map/ppermute | solution.py:73
  37.0 6.4 %collective-permute-start.21 = (bf16[2,192,128]{2,1,0:T(8,128)(2,1)S(1)}, bf16[2,192,128]{2,1,0:T(8,128)(2,1)S(1)}, u32[]{:S(2)}, u32[]{:S(2)}) collective-permute-start(bf16[2,192,128]{2,1,0:T(8,128)(2,1)S(1)} %shard_map.144.refs_0_), channel_id=1, source_target_pairs={{16,0},{24,8},{0,16},{8,24},{17,1},{25,9},{1,17},{9,25},{18,2},{26... | collective-permute-start | bytes 294920 | tf_op jit(solution)/shard_map/ppermute | solution.py:73
  37.1 6.5 %collective-permute-start.18 = (bf16[2,192,128]{2,1,0:T(8,128)(2,1)S(1)}, bf16[2,192,128]{2,1,0:T(8,128)(2,1)S(1)}, u32[]{:S(2)}, u32[]{:S(2)}) collective-permute-start(bf16[2,192,128]{2,1,0:T(8,128)(2,1)S(1)} %shard_map.144.refs_0_), channel_id=1, source_target_pairs={{20,0},{16,4},{28,8},{24,12},{4,16},{0,20},{12,24},{8,28},{21,1},{... | collective-permute-start | bytes 294920 | tf_op jit(solution)/shard_map/ppermute | solution.py:81
  38.6 6.6 %collective-permute-start.22 = (bf16[2,192,128]{2,1,0:T(8,128)(2,1)S(1)}, bf16[2,192,128]{2,1,0:T(8,128)(2,1)S(1)}, u32[]{:S(2)}, u32[]{:S(2)}) collective-permute-start(bf16[2,192,128]{2,1,0:T(8,128)(2,1)S(1)} %shard_map.144.refs_0_), channel_id=1, source_target_pairs={{8,0},{0,8},{24,16},{16,24},{9,1},{1,9},{25,17},{17,25},{10,2},{2,... | collective-permute-start | bytes 294920 | tf_op jit(solution)/shard_map/ppermute | solution.py:73
  41.6 3.5 %collective-permute-start.23 = (bf16[2,192,128]{2,1,0:T(8,128)(2,1)S(1)}, bf16[2,192,128]{2,1,0:T(8,128)(2,1)S(1)}, u32[]{:S(2)}, u32[]{:S(2)}) collective-permute-start(bf16[2,192,128]{2,1,0:T(8,128)(2,1)S(1)} %collective-permute-done.20.refs_1_), channel_id=1, source_target_pairs={{8,0},{0,8},{24,16},{16,24},{9,1},{1,9},{25,17},{17,25},{10,2},{2,... | collective-permute-start | bytes 294920 | tf_op jit(solution)/shard_map/ppermute | solution.py:73
  43.4 1.7 %collective-permute-start.24 = (bf16[2,192,128]{2,1,0:T(8,128)(2,1)S(1)}, bf16[2,192,128]{2,1,0:T(8,128)(2,1)S(1)}, u32[]{:S(2)}, u32[]{:S(2)}) collective-permute-start(bf16[2,192,128]{2,1,0:T(8,128)(2,1)S(1)} %collective-permute-done.21.refs_2_), channel_id=1, source_target_pairs={{8,0},{0,8},{24,16},{16,24},{9,1},{1,9},{25,17},{17,25},{10,2},{2,... | collective-permute-start | bytes 294920 | tf_op jit(solution)/shard_map/ppermute | solution.py:73
  43.6 2.7 %collective-permute-start.19 = (bf16[2,192,128]{2,1,0:T(8,128)(2,1)S(1)}, bf16[2,192,128]{2,1,0:T(8,128)(2,1)S(1)}, u32[]{:S(2)}, u32[]{:S(2)}) collective-permute-start(bf16[2,192,128]{2,1,0:T(8,128)(2,1)S(1)} %collective-permute-done.18.refs_6_), channel_id=1, source_target_pairs={{8,0},{0,8},{24,16},{16,24},{9,1},{1,9},{25,17},{17,25},{10,2},{2,... | collective-permute-start | bytes 294920 | tf_op jit(solution)/shard_map/ppermute | solution.py:73
  (2 other events, 6.1 us)

commit v17 on v16

--- a/solution.py
+++ b/solution.py
@@ -407,7 +407,7 @@
     rest = across_ref.shape[0] - half
     across_ref[half:] = part_ref[2 * height + rest :]
     frame_ref[...] = quarter(band, frames[1]).astype(jnp.bfloat16)
-    both_ref[...] = quarter(1 - band, frames[1]).astype(jnp.bfloat16)
+    both_ref[:half] = quarter(1 - band, frames[1]).astype(jnp.bfloat16)
 
 
 def plane_kernel(own_ref, *refs):
@@ -682,14 +682,14 @@
 
         keep_two, send_two = call(
             band_kernel,
-            [f32(half, ch), bf16(half + cols + 16, ch)],
+            [f32(half, ch), bf16(half + 2 * cols, ch)],
             [],
             0,
             own_two,
             across_two,
         )
         sum_two = added(keep_two, flipped(send_two, "video", 1))
-        quarters = [f32(half, ch), bf16(half + cols, ch)] + [bf16(half, ch)] * 2
+        quarters = [f32(half, ch)] + [bf16(half + more, ch) for more in (cols, 0, cols + 16)]
         own_one, *sends = call(
             pair_quarter_kernel, quarters, [], 0, keep_one, pair_one, after=(send_two,)
         )

time: 47.3 us -> 47.1 us (level)
    ppermute x2, waiting for transfers between devices: 1.78 us -> 0.01 us  [flipped_both(): return lax.ppermute(block, ('section', 'video'), pairs)]
    ppermute x23, waiting for transfers between devices: 4.72 us -> 6.33 us  [flipped(): lax.ppermute(block, axis, [(place ^ flip, place) for place in range(count)])]
    ppermute x23, starting transfers between devices: 28.4 us -> 27.2 us  [flipped(): lax.ppermute(block, axis, [(place ^ flip, place) for place in range(count)])]
    ppermute x2, starting transfers between devices: 2.03 us -> 3.23 us  [flipped_both(): return lax.ppermute(block, ('section', 'video'), pairs)]
where the time goes in v17:
time: 47.1 us; the launch traced here: 46.9 us
  starting transfers between devices  30.4 us (65%)
  Pallas kernels  9.27 us (20%)
  waiting for transfers between devices  6.33 us (13%)
  between operations  0.83 us (2%)
    ppermute x23, starting transfers between devices, flipped(): lax.ppermute(block, axis, [(place ^ flip, place) for place in range(count)])  27.2 us
    pallas_call x17, Pallas kernels, call(): pl.pallas_call(body, out_shape=outs[0] if single else tuple(outs), in_spe...  7.36 us
    ppermute x23, waiting for transfers between devices, flipped(): lax.ppermute(block, axis, [(place ^ flip, place) for place in range(count)])  6.33 us
    ppermute x2, starting transfers between devices, flipped_both(): return lax.ppermute(block, ('section', 'video'), pairs)  3.23 us
    pallas_call x2, Pallas kernels, placed(): pl.pallas_call(functools.partial(place_kernel, places), out_shape=outs, i...  1.91 us
  transfers between devices with their start and end apart: 25, of which 6 were waited for; matrix products, arithmetic and copies ran while one was open for 0% of the time, Pallas kernels for 18%

profile of v17, /device:TPU:1, one launch (start us, length us, event | category | flops | bytes accessed | tf_op | source)
XLA Modules:
  0.0 46.9 jit_solution(1667463345393292371)
XLA Ops:
  0.6 2.1 %collective-permute-start.3 = (bf16[16,64,128]{2,1,0:T(8,128)(2,1)}, bf16[16,64,128]{2,1,0:T(8,128)(2,1)S(1)}, u32[]{:S(2)}, u32[]{:S(2)}) collective-permute-start(bf16[16,64,128]{2,1,0:T(8,128)(2,1)} %bitcast.10), channel_id=1, source_target_pairs={{4,0},{0,4},{5,1},{1,5},{6,2},{2,6},{7,3},{3,7},{12,8},{8,12},{13,... | collective-permute-start | bytes 786440 | tf_op jit(solution)/shard_map/ppermute | solution.py:73
  2.7 1.6 %shard_map.128 = (bf16[4,64,128]{2,1,0:T(8,128)(2,1)}, bf16[4,64,128]{2,1,0:T(8,128)(2,1)}) custom-call(bf16[16,64,128]{2,1,0:T(8,128)(2,1)} %bitcast.11, bf16[16,64,128]{2,1,0:T(8,128)(2,1)} %bitcast.17, bf16[16,64,128]{2,1,0:T(8,128)(2,1)} %bitcast.28, bf16[16,64,128]{2,1,0:T(8,128)(2,1)} %bitcast.25), custom_call_target="tpu_custom_call" | custom-call | flops 1 | bytes 1179648 | tf_op jit(solution)/shard_map/pallas_call | solution.py:38
  4.4 1.0 %collective-permute-start = (bf16[4,64,128]{2,1,0:T(8,128)(2,1)}, bf16[4,64,128]{2,1,0:T(8,128)(2,1)S(1)}, u32[]{:S(2)}, u32[]{:S(2)}) collective-permute-start(bf16[4,64,128]{2,1,0:T(8,128)(2,1)} %get-tuple-element.43), channel_id=1, source_target_pairs={{8,0},{0,8},{24,16},{16,24},{9,1},{1,9},{25,17},{17,25},{10,2},{2,... | collective-permute-start | bytes 196616 | tf_op jit(solution)/shard_map/ppermute | solution.py:73
  5.4 1.1 %collective-permute-done.refs_5_ = bf16[4,64,128]{2,1,0:T(8,128)(2,1)S(1)} collective-permute-done((bf16[4,64,128]{2,1,0:T(8,128)(2,1)}, bf16[4,64,128]{2,1,0:T(8,128)(2,1)S(1)}, u32[]{:S(2)}, u32[]{:S(2)}) %collective-permute-start) | collective-permute-done | bytes 65568 | tf_op jit(solution)/shard_map/ppermute | solution.py:73
  6.9 1.2 %collective-permute-start.2 = (bf16[4,64,128]{2,1,0:T(8,128)(2,1)S(1)}, bf16[4,64,128]{2,1,0:T(8,128)(2,1)S(1)}, u32[]{:S(2)}, u32[]{:S(2)}) collective-permute-start(bf16[4,64,128]{2,1,0:T(8,128)(2,1)S(1)} %collective-permute-done.refs_5_), channel_id=1, source_target_pairs={{16,0},{24,8},{0,16},{8,24},{17,1},{25,9},{1,17},{9,25},{18,2},{26... | collective-permute-start | bytes 196616 | tf_op jit(solution)/shard_map/ppermute | solution.py:73
  8.2 1.3 %collective-permute-start.4 = (bf16[14,64,128]{2,1,0:T(8,128)(2,1)S(1)}, bf16[14,64,128]{2,1,0:T(8,128)(2,1)S(1)}, u32[]{:S(2)}, u32[]{:S(2)}) collective-permute-start(bf16[14,64,128]{2,1,0:T(8,128)(2,1)S(1)} %get-tuple-element.45.refs_5_), channel_id=1, source_target_pairs={{4,0},{0,4},{5,1},{1,5},{6,2},{2,6},{7,3},{3,7},{12,8},{8,12},{13,... | collective-permute-start | bytes 688136 | tf_op jit(solution)/shard_map/ppermute | solution.py:73
  9.6 1.0 %shard_map.130 = (bf16[14,64,128]{2,1,0:T(8,128)(2,1)S(1)}, bf16[16,64,128]{2,1,0:T(8,128)(2,1)S(1)}) custom-call(bf16[16,64,128]{2,1,0:T(8,128)(2,1)S(1)} %bitcast.13, bf16[16,64,128]{2,1,0:T(8,128)(2,1)S(1)} %bitcast.19, bf16[16,64,128]{2,1,0:T(8,128)(2,1)S(1)} %collective-permute-done.3.refs_2_.refs_6_, bf16[3,128,128]{2,1,0:T(8,128)(2,1)S(1)} %copy-done.6, ...), custom_call_target="tpu_custom_call" | custom-call | tf_op jit(solution)/shard_map/pallas_call | solution.py:38
  10.6 0.9 %shard_map.132 = (f32[2,384,128]{2,1,0:T(8,128)S(1)}, bf16[384,128]{1,0:T(8,128)(2,1)S(1)}, bf16[384,128]{1,0:T(8,128)(2,1)S(1)}) custom-call(bf16[16,64,128]{2,1,0:T(8,128)(2,1)S(1)} %bitcast.30, bf16[16,64,128]{2,1,0:T(8,128)(2,1)S(1)} %bitcast.20, bf16[16,64,128]{2,1,0:T(8,128)(2,1)S(1)} %get-tuple-element.48.refs_6_.refs_2_.refs_4_, ...), custom_call_target="tpu_custom_call" | custom-call | flops 2415919104 | bytes 2031616 | tf_op jit(solution)/shard_map/pallas_call | solution.py:38
  11.5 0.9 %collective-permute-start.6 = (bf16[384,128]{1,0:T(8,128)(2,1)S(1)}, bf16[384,128]{1,0:T(8,128)(2,1)S(1)}, u32[]{:S(2)}, u32[]{:S(2)}) collective-permute-start(bf16[384,128]{1,0:T(8,128)(2,1)S(1)} %get-tuple-element.52), channel_id=1, source_target_pairs={{8,0},{0,8},{24,16},{16,24},{9,1},{1,9},{25,17},{17,25},{10,2},{2,... | collective-permute-start | bytes 294920 | tf_op jit(solution)/shard_map/ppermute | solution.py:73
  12.4 0.8 %collective-permute-start.5 = (bf16[4,64,128]{2,1,0:T(8,128)(2,1)S(1)}, bf16[4,64,128]{2,1,0:T(8,128)(2,1)S(1)}, u32[]{:S(2)}, u32[]{:S(2)}) collective-permute-start(bf16[4,64,128]{2,1,0:T(8,128)(2,1)S(1)} %shard_map.131.refs_7_), channel_id=1, source_target_pairs={{4,0},{0,4},{5,1},{1,5},{6,2},{2,6},{7,3},{3,7},{12,8},{8,12},{13,... | collective-permute-start | bytes 196616 | tf_op jit(solution)/shard_map/ppermute | solution.py:73
  13.7 1.4 %collective-permute-start.8 = (bf16[384,128]{1,0:T(8,128)(2,1)S(1)}, bf16[384,128]{1,0:T(8,128)(2,1)S(1)}, u32[]{:S(2)}, u32[]{:S(2)}) collective-permute-start(bf16[384,128]{1,0:T(8,128)(2,1)S(1)} %get-tuple-element.58), channel_id=1, source_target_pairs={{16,0},{24,8},{0,16},{8,24},{17,1},{25,9},{1,17},{9,25},{18,2},{26... | collective-permute-start | bytes 294920 | tf_op jit(solution)/shard_map/ppermute | solution.py:73
  15.6 1.0 %collective-permute-done.5.refs_6_ = bf16[4,64,128]{2,1,0:T(8,128)(2,1)S(1)} collective-permute-done((bf16[4,64,128]{2,1,0:T(8,128)(2,1)S(1)}, bf16[4,64,128]{2,1,0:T(8,128)(2,1)S(1)}, u32[]{:S(2)}, u32[]{:S(2)}) %collective-permute-start.5) | collective-permute-done | bytes 65568 | tf_op jit(solution)/shard_map/ppermute | solution.py:73
  16.6 1.3 %shard_map.136 = (bf16[16,64,128]{2,1,0:T(8,128)(2,1)S(1)}, bf16[16,64,128]{2,1,0:T(8,128)(2,1)S(1)}, f32[2,384,128]{2,1,0:T(8,128)S(1)}, bf16[896,128]{1,0:T(8,128)(2,1)S(1)}) custom-call(bf16[16,64,128]{2,1,0:T(8,128)(2,1)S(1)} %bitcast.16, bf16[4,64,128]{2,1,0:T(8,128)(2,1)S(1)} %collective-permute-done.1.refs_4_.refs_1_.refs_3_.refs_2_, ...), custom_call_target="tpu_custom_call" | custom-call | flops 2415919104 | bytes 5046272 | tf_op jit(solution)/shard_map/pallas_call | solution.py:38
  17.9 1.2 %collective-permute-start.9 = (bf16[896,128]{1,0:T(8,128)(2,1)S(1)}, bf16[896,128]{1,0:T(8,128)(2,1)S(1)}, u32[]{:S(2)}, u32[]{:S(2)}) collective-permute-start(bf16[896,128]{1,0:T(8,128)(2,1)S(1)} %get-tuple-element.59), channel_id=1, source_target_pairs={{8,0},{0,8},{24,16},{16,24},{9,1},{1,9},{25,17},{17,25},{10,2},{2,... | collective-permute-start | bytes 688136 | tf_op jit(solution)/shard_map/ppermute | solution.py:73
  19.1 1.3 %collective-permute-start.13 = (bf16[320,128]{1,0:T(8,128)(2,1)S(1)}, bf16[320,128]{1,0:T(8,128)(2,1)S(1)}, u32[]{:S(2)}, u32[]{:S(2)}) collective-permute-start(bf16[320,128]{1,0:T(8,128)(2,1)S(1)} %get-tuple-element.61.refs_2_), channel_id=1, source_target_pairs={{4,0},{0,4},{5,1},{1,5},{6,2},{2,6},{7,3},{3,7},{12,8},{8,12},{13,... | collective-permute-start | bytes 245768 | tf_op jit(solution)/shard_map/ppermute | solution.py:73
  20.5 1.9 %collective-permute-start.12 = (bf16[272,128]{1,0:T(8,128)(2,1)S(1)}, bf16[272,128]{1,0:T(8,128)(2,1)S(1)}, u32[]{:S(2)}, u32[]{:S(2)}) collective-permute-start(bf16[272,128]{1,0:T(8,128)(2,1)S(1)} %get-tuple-element.65), channel_id=1, source_target_pairs={{20,0},{16,4},{28,8},{24,12},{4,16},{0,20},{12,24},{8,28},{21,1},{... | collective-permute-start | bytes 208904 | tf_op jit(solution)/shard_map/ppermute | solution.py:81
  23.3 1.4 %collective-permute-start.15 = (bf16[192,128]{1,0:T(8,128)(2,1)S(1)}, bf16[192,128]{1,0:T(8,128)(2,1)S(1)}, u32[]{:S(2)}, u32[]{:S(2)}) collective-permute-start(bf16[192,128]{1,0:T(8,128)(2,1)S(1)} %shard_map.140.refs_0_), channel_id=1, source_target_pairs={{1,0},{0,1},{3,2},{2,3},{5,4},{4,5},{7,6},{6,7},{9,8},{8,9},{11,10... | collective-permute-start | bytes 147464 | tf_op jit(solution)/shard_map/ppermute | solution.py:73
  24.6 1.5 %collective-permute-done.11.refs_2_ = bf16[192,128]{1,0:T(8,128)(2,1)S(1)} collective-permute-done((bf16[192,128]{1,0:T(8,128)(2,1)S(1)}, bf16[192,128]{1,0:T(8,128)(2,1)S(1)}, u32[]{:S(2)}, u32[]{:S(2)}) %collective-permute-start.11) | collective-permute-done | bytes 49184 | tf_op jit(solution)/shard_map/ppermute | solution.py:73
  26.1 1.3 %collective-permute-done.10.refs_1_.refs_3_ = bf16[256,128]{1,0:T(8,128)(2,1)S(1)} collective-permute-done((bf16[256,128]{1,0:T(8,128)(2,1)S(1)}, bf16[256,128]{1,0:T(8,128)(2,1)S(1)}, u32[]{:S(2)}, u32[]{:S(2)}) %collective-permute-start.10) | collective-permute-done | bytes 65568 | tf_op jit(solution)/shard_map/ppermute | solution.py:73
  27.4 1.3 %collective-permute-start.14 = (bf16[192,128]{1,0:T(8,128)(2,1)S(1)}, bf16[192,128]{1,0:T(8,128)(2,1)S(1)}, u32[]{:S(2)}, u32[]{:S(2)}) collective-permute-start(bf16[192,128]{1,0:T(8,128)(2,1)S(1)} %shard_map.139.refs_0_), channel_id=1, source_target_pairs={{1,0},{0,1},{3,2},{2,3},{5,4},{4,5},{7,6},{6,7},{9,8},{8,9},{11,10... | collective-permute-start | bytes 147464 | tf_op jit(solution)/shard_map/ppermute | solution.py:73
  28.8 2.4 %collective-permute-start.17 = (bf16[192,128]{1,0:T(8,128)(2,1)S(1)}, bf16[192,128]{1,0:T(8,128)(2,1)S(1)}, u32[]{:S(2)}, u32[]{:S(2)}) collective-permute-start(bf16[192,128]{1,0:T(8,128)(2,1)S(1)} %shard_map.143.refs_2_), channel_id=1, source_target_pairs={{2,0},{3,1},{0,2},{1,3},{6,4},{7,5},{4,6},{5,7},{10,8},{11,9},{8,1... | collective-permute-start | bytes 147464 | tf_op jit(solution)/shard_map/ppermute | solution.py:73
  31.2 1.6 %collective-permute-start.16 = (bf16[192,128]{1,0:T(8,128)(2,1)S(1)}, bf16[192,128]{1,0:T(8,128)(2,1)S(1)}, u32[]{:S(2)}, u32[]{:S(2)}) collective-permute-start(bf16[192,128]{1,0:T(8,128)(2,1)S(1)} %shard_map.141.refs_5_.refs_0_), channel_id=1, source_target_pairs={{2,0},{3,1},{0,2},{1,3},{6,4},{7,5},{4,6},{5,7},{10,8},{11,9},{8,1... | collective-permute-start | bytes 147464 | tf_op jit(solution)/shard_map/ppermute | solution.py:73
  32.8 1.5 %shard_map.142 = (bf16[16,64,128]{2,1,0:T(8,128)(2,1)}, f32[8,128]{1,0:T(8,128)S(1)}) custom-call(bf16[16,64,128]{2,1,0:T(8,128)(2,1)S(1)} %get-tuple-element.55.refs_0_, bf16[16,64,128]{2,1,0:T(8,128)(2,1)S(1)} %get-tuple-element.56.refs_1_, bf16[896,128]{1,0:T(8,128)(2,1)S(1)} %collective-permute-done.9.refs_1_.refs_2_, ...), custom_call_target="tpu_custom_call" | custom-call | flops 301989888 | bytes 1380352 | tf_op jit(solution)/shard_map/pallas_call | solution.py:38
  34.3 1.3 %collective-permute-done.16.refs_1_ = bf16[192,128]{1,0:T(8,128)(2,1)S(1)} collective-permute-done((bf16[192,128]{1,0:T(8,128)(2,1)S(1)}, bf16[192,128]{1,0:T(8,128)(2,1)S(1)}, u32[]{:S(2)}, u32[]{:S(2)}) %collective-permute-start.16) | collective-permute-done | bytes 49184 | tf_op jit(solution)/shard_map/ppermute | solution.py:73
  35.7 0.8 %collective-permute-start.20 = (bf16[2,192,128]{2,1,0:T(8,128)(2,1)S(1)}, bf16[2,192,128]{2,1,0:T(8,128)(2,1)S(1)}, u32[]{:S(2)}, u32[]{:S(2)}) collective-permute-start(bf16[2,192,128]{2,1,0:T(8,128)(2,1)S(1)} %shard_map.144.refs_0_), channel_id=1, source_target_pairs={{4,0},{0,4},{5,1},{1,5},{6,2},{2,6},{7,3},{3,7},{12,8},{8,12},{13,... | collective-permute-start | bytes 294920 | tf_op jit(solution)/shard_map/ppermute | solution.py:73
  36.5 0.6 %collective-permute-start.21 = (bf16[2,192,128]{2,1,0:T(8,128)(2,1)S(1)}, bf16[2,192,128]{2,1,0:T(8,128)(2,1)S(1)}, u32[]{:S(2)}, u32[]{:S(2)}) collective-permute-start(bf16[2,192,128]{2,1,0:T(8,128)(2,1)S(1)} %shard_map.144.refs_0_), channel_id=1, source_target_pairs={{16,0},{24,8},{0,16},{8,24},{17,1},{25,9},{1,17},{9,25},{18,2},{26... | collective-permute-start | bytes 294920 | tf_op jit(solution)/shard_map/ppermute | solution.py:73
  37.1 1.3 %collective-permute-start.18 = (bf16[2,192,128]{2,1,0:T(8,128)(2,1)S(1)}, bf16[2,192,128]{2,1,0:T(8,128)(2,1)S(1)}, u32[]{:S(2)}, u32[]{:S(2)}) collective-permute-start(bf16[2,192,128]{2,1,0:T(8,128)(2,1)S(1)} %shard_map.144.refs_0_), channel_id=1, source_target_pairs={{20,0},{16,4},{28,8},{24,12},{4,16},{0,20},{12,24},{8,28},{21,1},{... | collective-permute-start | bytes 294920 | tf_op jit(solution)/shard_map/ppermute | solution.py:81
  38.4 2.5 %collective-permute-start.22 = (bf16[2,192,128]{2,1,0:T(8,128)(2,1)S(1)}, bf16[2,192,128]{2,1,0:T(8,128)(2,1)S(1)}, u32[]{:S(2)}, u32[]{:S(2)}) collective-permute-start(bf16[2,192,128]{2,1,0:T(8,128)(2,1)S(1)} %shard_map.144.refs_0_), channel_id=1, source_target_pairs={{8,0},{0,8},{24,16},{16,24},{9,1},{1,9},{25,17},{17,25},{10,2},{2,... | collective-permute-start | bytes 294920 | tf_op jit(solution)/shard_map/ppermute | solution.py:73
  40.9 1.9 %collective-permute-start.23 = (bf16[2,192,128]{2,1,0:T(8,128)(2,1)S(1)}, bf16[2,192,128]{2,1,0:T(8,128)(2,1)S(1)}, u32[]{:S(2)}, u32[]{:S(2)}) collective-permute-start(bf16[2,192,128]{2,1,0:T(8,128)(2,1)S(1)} %collective-permute-done.20.refs_1_), channel_id=1, source_target_pairs={{8,0},{0,8},{24,16},{16,24},{9,1},{1,9},{25,17},{17,25},{10,2},{2,... | collective-permute-start | bytes 294920 | tf_op jit(solution)/shard_map/ppermute | solution.py:73
  43.4 1.5 %collective-permute-start.19 = (bf16[2,192,128]{2,1,0:T(8,128)(2,1)S(1)}, bf16[2,192,128]{2,1,0:T(8,128)(2,1)S(1)}, u32[]{:S(2)}, u32[]{:S(2)}) collective-permute-start(bf16[2,192,128]{2,1,0:T(8,128)(2,1)S(1)} %collective-permute-done.18.refs_6_), channel_id=1, source_target_pairs={{8,0},{0,8},{24,16},{16,24},{9,1},{1,9},{25,17},{17,25},{10,2},{2,... | collective-permute-start | bytes 294920 | tf_op jit(solution)/shard_map/ppermute | solution.py:73
  44.9 1.2 %shard_map.145 = (f32[3,384,128]{2,1,0:T(8,128)}, f32[384,128]{1,0:T(8,128)}, f32[3,384,128]{2,1,0:T(8,128)}, f32[384,128]{1,0:T(8,128)}) custom-call(bf16[2,192,128]{2,1,0:T(8,128)(2,1)S(1)} %shard_map.144.refs_0_, bf16[2,192,128]{2,1,0:T(8,128)(2,1)S(1)} %collective-permute-done.20.refs_1_, bf16[2,192,128]{2,1,0:T(8,128)(2,1)S(1)} %collective-permute-done.21.refs_2_, ...), custom_call_target="tpu_custom_call" | custom-call | bytes 2064384 | tf_op jit(solution)/shard_map/pallas_call | solution.py:467
  46.2 0.7 %shard_map.146 = (f32[3,384,128]{2,1,0:T(8,128)}, f32[384,128]{1,0:T(8,128)}, f32[3,384,128]{2,1,0:T(8,128)}, f32[384,128]{1,0:T(8,128)}) custom-call(bf16[2,192,128]{2,1,0:T(8,128)(2,1)S(1)} %collective-permute-done.19.refs_0_, f32[3,384,128]{2,1,0:T(8,128)} %get-tuple-element.71.refs_1_, ...), custom_call_target="tpu_custom_call", output_to_operand_aliasing={{0}: (1, {}), {1}: (2, {}), {2}: (3, {}), {3}: (4, {})} | custom-call | bytes 294912 | tf_op jit(solution)/shard_map/pallas_call | solution.py:467
  (55 shorter events, 3.1 us)
Async XLA Ops:
  0.6 8.9 %collective-permute-start.3 = (bf16[16,64,128]{2,1,0:T(8,128)(2,1)}, bf16[16,64,128]{2,1,0:T(8,128)(2,1)S(1)}, u32[]{:S(2)}, u32[]{:S(2)}) collective-permute-start(bf16[16,64,128]{2,1,0:T(8,128)(2,1)} %bitcast.10), channel_id=1, source_target_pairs={{4,0},{0,4},{5,1},{1,5},{6,2},{2,6},{7,3},{3,7},{12,8},{8,12},{13,... | collective-permute-start | bytes 786440 | tf_op jit(solution)/shard_map/ppermute | solution.py:73
  2.7 5.4 %copy-start = (bf16[1,1,16,64,128]{4,3,2,1,0:T(8,128)(2,1)S(1)}, bf16[1,1,16,64,128]{4,3,2,1,0:T(8,128)(2,1)}, u32[]{:S(2)}) copy-start(bf16[1,1,16,64,128]{4,3,2,1,0:T(8,128)(2,1)} %param.9) | copy-start | bytes 786436
  2.7 5.4 %copy-start.1 = (bf16[3,3,128,128]{3,2,1,0:T(8,128)(2,1)S(1)}, bf16[3,3,128,128]{3,2,1,0:T(8,128)(2,1)}, u32[]{:S(2)}) copy-start(bf16[3,3,128,128]{3,2,1,0:T(8,128)(2,1)} %refs_8_.1) | copy-start | bytes 884740
  2.7 5.4 %copy-start.2 = (bf16[1,1,16,64,128]{4,3,2,1,0:T(8,128)(2,1)S(1)}, bf16[1,1,16,64,128]{4,3,2,1,0:T(8,128)(2,1)}, u32[]{:S(2)}) copy-start(bf16[1,1,16,64,128]{4,3,2,1,0:T(8,128)(2,1)} %param.13) | copy-start | bytes 786436
  2.7 5.4 %copy-start.6 = (bf16[3,128,128]{2,1,0:T(8,128)(2,1)S(1)}, bf16[3,128,128]{2,1,0:T(8,128)(2,1)}, u32[]{:S(2)}) copy-start(bf16[3,128,128]{2,1,0:T(8,128)(2,1)} %refs_7_.1) | copy-start | bytes 294916
  4.4 2.1 %collective-permute-start = (bf16[4,64,128]{2,1,0:T(8,128)(2,1)}, bf16[4,64,128]{2,1,0:T(8,128)(2,1)S(1)}, u32[]{:S(2)}, u32[]{:S(2)}) collective-permute-start(bf16[4,64,128]{2,1,0:T(8,128)(2,1)} %get-tuple-element.43), channel_id=1, source_target_pairs={{8,0},{0,8},{24,16},{16,24},{9,1},{1,9},{25,17},{17,25},{10,2},{2,... | collective-permute-start | bytes 196616 | tf_op jit(solution)/shard_map/ppermute | solution.py:73
  6.5 3.0 %copy-start.5 = (bf16[1,1,16,64,128]{4,3,2,1,0:T(8,128)(2,1)S(1)}, bf16[1,1,16,64,128]{4,3,2,1,0:T(8,128)(2,1)}, u32[]{:S(2)}) copy-start(bf16[1,1,16,64,128]{4,3,2,1,0:T(8,128)(2,1)} %param.12) | copy-start | bytes 786436
  6.5 3.0 %copy-start.7 = (bf16[3,128,128]{2,1,0:T(8,128)(2,1)S(1)}, bf16[3,128,128]{2,1,0:T(8,128)(2,1)}, u32[]{:S(2)}) copy-start(bf16[3,128,128]{2,1,0:T(8,128)(2,1)} %refs_11_.1) | copy-start | bytes 294916
  6.5 1.7 %collective-permute-start.1 = (bf16[4,64,128]{2,1,0:T(8,128)(2,1)}, bf16[4,64,128]{2,1,0:T(8,128)(2,1)S(1)}, u32[]{:S(2)}, u32[]{:S(2)}) collective-permute-start(bf16[4,64,128]{2,1,0:T(8,128)(2,1)} %get-tuple-element.44), channel_id=1, source_target_pairs={{8,0},{0,8},{24,16},{16,24},{9,1},{1,9},{25,17},{17,25},{10,2},{2,... | collective-permute-start | bytes 196616 | tf_op jit(solution)/shard_map/ppermute | solution.py:73
  6.9 3.6 %collective-permute-start.2 = (bf16[4,64,128]{2,1,0:T(8,128)(2,1)S(1)}, bf16[4,64,128]{2,1,0:T(8,128)(2,1)S(1)}, u32[]{:S(2)}, u32[]{:S(2)}) collective-permute-start(bf16[4,64,128]{2,1,0:T(8,128)(2,1)S(1)} %collective-permute-done.refs_5_), channel_id=1, source_target_pairs={{16,0},{24,8},{0,16},{8,24},{17,1},{25,9},{1,17},{9,25},{18,2},{26... | collective-permute-start | bytes 196616 | tf_op jit(solution)/shard_map/ppermute | solution.py:73
  8.2 6.9 %collective-permute-start.4 = (bf16[14,64,128]{2,1,0:T(8,128)(2,1)S(1)}, bf16[14,64,128]{2,1,0:T(8,128)(2,1)S(1)}, u32[]{:S(2)}, u32[]{:S(2)}) collective-permute-start(bf16[14,64,128]{2,1,0:T(8,128)(2,1)S(1)} %get-tuple-element.45.refs_5_), channel_id=1, source_target_pairs={{4,0},{0,4},{5,1},{1,5},{6,2},{2,6},{7,3},{3,7},{12,8},{8,12},{13,... | collective-permute-start | bytes 688136 | tf_op jit(solution)/shard_map/ppermute | solution.py:73
  11.5 2.1 %collective-permute-start.6 = (bf16[384,128]{1,0:T(8,128)(2,1)S(1)}, bf16[384,128]{1,0:T(8,128)(2,1)S(1)}, u32[]{:S(2)}, u32[]{:S(2)}) collective-permute-start(bf16[384,128]{1,0:T(8,128)(2,1)S(1)} %get-tuple-element.52), channel_id=1, source_target_pairs={{8,0},{0,8},{24,16},{16,24},{9,1},{1,9},{25,17},{17,25},{10,2},{2,... | collective-permute-start | bytes 294920 | tf_op jit(solution)/shard_map/ppermute | solution.py:73
  12.4 1.3 %collective-permute-start.7 = (bf16[384,128]{1,0:T(8,128)(2,1)S(1)}, bf16[384,128]{1,0:T(8,128)(2,1)S(1)}, u32[]{:S(2)}, u32[]{:S(2)}) collective-permute-start(bf16[384,128]{1,0:T(8,128)(2,1)S(1)} %get-tuple-element.53), channel_id=1, source_target_pairs={{8,0},{0,8},{24,16},{16,24},{9,1},{1,9},{25,17},{17,25},{10,2},{2,... | collective-permute-start | bytes 294920 | tf_op jit(solution)/shard_map/ppermute | solution.py:73
  12.4 4.2 %collective-permute-start.5 = (bf16[4,64,128]{2,1,0:T(8,128)(2,1)S(1)}, bf16[4,64,128]{2,1,0:T(8,128)(2,1)S(1)}, u32[]{:S(2)}, u32[]{:S(2)}) collective-permute-start(bf16[4,64,128]{2,1,0:T(8,128)(2,1)S(1)} %shard_map.131.refs_7_), channel_id=1, source_target_pairs={{4,0},{0,4},{5,1},{1,5},{6,2},{2,6},{7,3},{3,7},{12,8},{8,12},{13,... | collective-permute-start | bytes 196616 | tf_op jit(solution)/shard_map/ppermute | solution.py:73
  13.7 4.2 %collective-permute-start.8 = (bf16[384,128]{1,0:T(8,128)(2,1)S(1)}, bf16[384,128]{1,0:T(8,128)(2,1)S(1)}, u32[]{:S(2)}, u32[]{:S(2)}) collective-permute-start(bf16[384,128]{1,0:T(8,128)(2,1)S(1)} %get-tuple-element.58), channel_id=1, source_target_pairs={{16,0},{24,8},{0,16},{8,24},{17,1},{25,9},{1,17},{9,25},{18,2},{26... | collective-permute-start | bytes 294920 | tf_op jit(solution)/shard_map/ppermute | solution.py:73
  17.9 2.5 %collective-permute-start.9 = (bf16[896,128]{1,0:T(8,128)(2,1)S(1)}, bf16[896,128]{1,0:T(8,128)(2,1)S(1)}, u32[]{:S(2)}, u32[]{:S(2)}) collective-permute-start(bf16[896,128]{1,0:T(8,128)(2,1)S(1)} %get-tuple-element.59), channel_id=1, source_target_pairs={{8,0},{0,8},{24,16},{16,24},{9,1},{1,9},{25,17},{17,25},{10,2},{2,... | collective-permute-start | bytes 688136 | tf_op jit(solution)/shard_map/ppermute | solution.py:73
  19.1 4.1 %collective-permute-start.13 = (bf16[320,128]{1,0:T(8,128)(2,1)S(1)}, bf16[320,128]{1,0:T(8,128)(2,1)S(1)}, u32[]{:S(2)}, u32[]{:S(2)}) collective-permute-start(bf16[320,128]{1,0:T(8,128)(2,1)S(1)} %get-tuple-element.61.refs_2_), channel_id=1, source_target_pairs={{4,0},{0,4},{5,1},{1,5},{6,2},{2,6},{7,3},{3,7},{12,8},{8,12},{13,... | collective-permute-start | bytes 245768 | tf_op jit(solution)/shard_map/ppermute | solution.py:73
  20.5 6.9 %collective-permute-start.12 = (bf16[272,128]{1,0:T(8,128)(2,1)S(1)}, bf16[272,128]{1,0:T(8,128)(2,1)S(1)}, u32[]{:S(2)}, u32[]{:S(2)}) collective-permute-start(bf16[272,128]{1,0:T(8,128)(2,1)S(1)} %get-tuple-element.65), channel_id=1, source_target_pairs={{20,0},{16,4},{28,8},{24,12},{4,16},{0,20},{12,24},{8,28},{21,1},{... | collective-permute-start | bytes 208904 | tf_op jit(solution)/shard_map/ppermute | solution.py:81
  22.4 5.0 %collective-permute-start.10 = (bf16[256,128]{1,0:T(8,128)(2,1)S(1)}, bf16[256,128]{1,0:T(8,128)(2,1)S(1)}, u32[]{:S(2)}, u32[]{:S(2)}) collective-permute-start(bf16[256,128]{1,0:T(8,128)(2,1)S(1)} %get-tuple-element.62), channel_id=1, source_target_pairs={{16,0},{24,8},{0,16},{8,24},{17,1},{25,9},{1,17},{9,25},{18,2},{26... | collective-permute-start | bytes 196616 | tf_op jit(solution)/shard_map/ppermute | solution.py:73
  22.8 3.3 %collective-permute-start.11 = (bf16[192,128]{1,0:T(8,128)(2,1)S(1)}, bf16[192,128]{1,0:T(8,128)(2,1)S(1)}, u32[]{:S(2)}, u32[]{:S(2)}) collective-permute-start(bf16[192,128]{1,0:T(8,128)(2,1)S(1)} %get-tuple-element.64), channel_id=1, source_target_pairs={{4,0},{0,4},{5,1},{1,5},{6,2},{2,6},{7,3},{3,7},{12,8},{8,12},{13,... | collective-permute-start | bytes 147464 | tf_op jit(solution)/shard_map/ppermute | solution.py:73
  23.3 5.5 %collective-permute-start.15 = (bf16[192,128]{1,0:T(8,128)(2,1)S(1)}, bf16[192,128]{1,0:T(8,128)(2,1)S(1)}, u32[]{:S(2)}, u32[]{:S(2)}) collective-permute-start(bf16[192,128]{1,0:T(8,128)(2,1)S(1)} %shard_map.140.refs_0_), channel_id=1, source_target_pairs={{1,0},{0,1},{3,2},{2,3},{5,4},{4,5},{7,6},{6,7},{9,8},{8,9},{11,10... | collective-permute-start | bytes 147464 | tf_op jit(solution)/shard_map/ppermute | solution.py:73
  27.4 5.4 %copy-start.8 = (bf16[3,3,128,128]{3,2,1,0:T(8,128)(2,1)S(1)}, bf16[3,3,128,128]{3,2,1,0:T(8,128)(2,1)}, u32[]{:S(2)}) copy-start(bf16[3,3,128,128]{3,2,1,0:T(8,128)(2,1)} %refs_4_.5) | copy-start | bytes 884740
  27.4 3.7 %collective-permute-start.14 = (bf16[192,128]{1,0:T(8,128)(2,1)S(1)}, bf16[192,128]{1,0:T(8,128)(2,1)S(1)}, u32[]{:S(2)}, u32[]{:S(2)}) collective-permute-start(bf16[192,128]{1,0:T(8,128)(2,1)S(1)} %shard_map.139.refs_0_), channel_id=1, source_target_pairs={{1,0},{0,1},{3,2},{2,3},{5,4},{4,5},{7,6},{6,7},{9,8},{8,9},{11,10... | collective-permute-start | bytes 147464 | tf_op jit(solution)/shard_map/ppermute | solution.py:73
  28.8 5.5 %collective-permute-start.17 = (bf16[192,128]{1,0:T(8,128)(2,1)S(1)}, bf16[192,128]{1,0:T(8,128)(2,1)S(1)}, u32[]{:S(2)}, u32[]{:S(2)}) collective-permute-start(bf16[192,128]{1,0:T(8,128)(2,1)S(1)} %shard_map.143.refs_2_), channel_id=1, source_target_pairs={{2,0},{3,1},{0,2},{1,3},{6,4},{7,5},{4,6},{5,7},{10,8},{11,9},{8,1... | collective-permute-start | bytes 147464 | tf_op jit(solution)/shard_map/ppermute | solution.py:73
  31.2 4.4 %collective-permute-start.16 = (bf16[192,128]{1,0:T(8,128)(2,1)S(1)}, bf16[192,128]{1,0:T(8,128)(2,1)S(1)}, u32[]{:S(2)}, u32[]{:S(2)}) collective-permute-start(bf16[192,128]{1,0:T(8,128)(2,1)S(1)} %shard_map.141.refs_5_.refs_0_), channel_id=1, source_target_pairs={{2,0},{3,1},{0,2},{1,3},{6,4},{7,5},{4,6},{5,7},{10,8},{11,9},{8,1... | collective-permute-start | bytes 147464 | tf_op jit(solution)/shard_map/ppermute | solution.py:73
  35.7 5.3 %collective-permute-start.20 = (bf16[2,192,128]{2,1,0:T(8,128)(2,1)S(1)}, bf16[2,192,128]{2,1,0:T(8,128)(2,1)S(1)}, u32[]{:S(2)}, u32[]{:S(2)}) collective-permute-start(bf16[2,192,128]{2,1,0:T(8,128)(2,1)S(1)} %shard_map.144.refs_0_), channel_id=1, source_target_pairs={{4,0},{0,4},{5,1},{1,5},{6,2},{2,6},{7,3},{3,7},{12,8},{8,12},{13,... | collective-permute-start | bytes 294920 | tf_op jit(solution)/shard_map/ppermute | solution.py:73
  36.5 6.4 %collective-permute-start.21 = (bf16[2,192,128]{2,1,0:T(8,128)(2,1)S(1)}, bf16[2,192,128]{2,1,0:T(8,128)(2,1)S(1)}, u32[]{:S(2)}, u32[]{:S(2)}) collective-permute-start(bf16[2,192,128]{2,1,0:T(8,128)(2,1)S(1)} %shard_map.144.refs_0_), channel_id=1, source_target_pairs={{16,0},{24,8},{0,16},{8,24},{17,1},{25,9},{1,17},{9,25},{18,2},{26... | collective-permute-start | bytes 294920 | tf_op jit(solution)/shard_map/ppermute | solution.py:73
  37.1 6.3 %collective-permute-start.18 = (bf16[2,192,128]{2,1,0:T(8,128)(2,1)S(1)}, bf16[2,192,128]{2,1,0:T(8,128)(2,1)S(1)}, u32[]{:S(2)}, u32[]{:S(2)}) collective-permute-start(bf16[2,192,128]{2,1,0:T(8,128)(2,1)S(1)} %shard_map.144.refs_0_), channel_id=1, source_target_pairs={{20,0},{16,4},{28,8},{24,12},{4,16},{0,20},{12,24},{8,28},{21,1},{... | collective-permute-start | bytes 294920 | tf_op jit(solution)/shard_map/ppermute | solution.py:81
  38.4 6.5 %collective-permute-start.22 = (bf16[2,192,128]{2,1,0:T(8,128)(2,1)S(1)}, bf16[2,192,128]{2,1,0:T(8,128)(2,1)S(1)}, u32[]{:S(2)}, u32[]{:S(2)}) collective-permute-start(bf16[2,192,128]{2,1,0:T(8,128)(2,1)S(1)} %shard_map.144.refs_0_), channel_id=1, source_target_pairs={{8,0},{0,8},{24,16},{16,24},{9,1},{1,9},{25,17},{17,25},{10,2},{2,... | collective-permute-start | bytes 294920 | tf_op jit(solution)/shard_map/ppermute | solution.py:73
  40.9 4.0 %collective-permute-start.23 = (bf16[2,192,128]{2,1,0:T(8,128)(2,1)S(1)}, bf16[2,192,128]{2,1,0:T(8,128)(2,1)S(1)}, u32[]{:S(2)}, u32[]{:S(2)}) collective-permute-start(bf16[2,192,128]{2,1,0:T(8,128)(2,1)S(1)} %collective-permute-done.20.refs_1_), channel_id=1, source_target_pairs={{8,0},{0,8},{24,16},{16,24},{9,1},{1,9},{25,17},{17,25},{10,2},{2,... | collective-permute-start | bytes 294920 | tf_op jit(solution)/shard_map/ppermute | solution.py:73
  42.9 2.1 %collective-permute-start.24 = (bf16[2,192,128]{2,1,0:T(8,128)(2,1)S(1)}, bf16[2,192,128]{2,1,0:T(8,128)(2,1)S(1)}, u32[]{:S(2)}, u32[]{:S(2)}) collective-permute-start(bf16[2,192,128]{2,1,0:T(8,128)(2,1)S(1)} %collective-permute-done.21.refs_2_), channel_id=1, source_target_pairs={{8,0},{0,8},{24,16},{16,24},{9,1},{1,9},{25,17},{17,25},{10,2},{2,... | collective-permute-start | bytes 294920 | tf_op jit(solution)/shard_map/ppermute | solution.py:73
  43.4 2.8 %collective-permute-start.19 = (bf16[2,192,128]{2,1,0:T(8,128)(2,1)S(1)}, bf16[2,192,128]{2,1,0:T(8,128)(2,1)S(1)}, u32[]{:S(2)}, u32[]{:S(2)}) collective-permute-start(bf16[2,192,128]{2,1,0:T(8,128)(2,1)S(1)} %collective-permute-done.18.refs_6_), channel_id=1, source_target_pairs={{8,0},{0,8},{24,16},{16,24},{9,1},{1,9},{25,17},{17,25},{10,2},{2,... | collective-permute-start | bytes 294920 | tf_op jit(solution)/shard_map/ppermute | solution.py:73
  (2 other events, 6.1 us)

commit v18 on v17

--- a/solution.py
+++ b/solution.py
@@ -125,18 +125,30 @@
     return lax.axis_index("video") == lax.axis_size("video") - 1
 
 
-def left_sides(saved_ref, preact_ref, above, below, sides_ref):
+def moved_rows(rows):
+    count = min(4, (rows - 4) // 3)
+    return slice(rows - 1 - count, rows - 1)
+
+
+def left_sides(saved_ref, preact_ref, above, below, sides_ref, moved=None):
     rows, cols, ch = saved_ref.shape
     flat = (rows * cols, ch)
+
+    def flipped_over(x):
+        if moved is not None:
+            kept = jnp.where(is_last(), x[moved], jnp.zeros_like(x[moved]))
+            x = jnp.concatenate([x[: moved.start], kept, x[moved.stop :]], axis=0)
+        return x.reshape(flat).T
+
     shifts = [
         jnp.concatenate([above, saved_ref[: rows - 1]], axis=0),
         saved_ref[...],
         jnp.concatenate([saved_ref[1:], below], axis=0),
     ]
     for n, shift in enumerate(shifts):
-        sides_ref[n] = shift.reshape(flat).T
+        sides_ref[n] = flipped_over(shift)
     hval = preact_ref[...].astype(jnp.float32)
-    sides_ref[3] = (hval * sigmoid(hval)).astype(jnp.bfloat16).reshape(flat).T
+    sides_ref[3] = flipped_over((hval * sigmoid(hval)).astype(jnp.bfloat16))
 
 
 def kernel_sums(sides_ref, grads, views, sums_ref):
@@ -163,17 +175,30 @@
         send_ref[...] = sums_ref[2 * n + 1 - odd].astype(jnp.bfloat16)
 
 
-def pack_kernel(*refs):
-    parts, outs, sems = refs[:4], refs[4:6], refs[6]
+def pack_kernel(moved, *refs):
+    parts, refs = refs[:4], refs[4:]
+    outs, sems = refs[-3:-1] if moved is None else refs[-4:-2], refs[-1]
     last = parts[0].shape[0] - 1
     odd = lax.rem(lax.axis_index("section"), 2)
-    copies = []
-    for n, part in enumerate(parts):
-        for out, row in zip(outs, ((1 - odd) * last, odd * last)):
-            sem = sems.at[len(copies)]
-            copies.append(
-                pltpu.make_async_copy(part.at[pl.ds(row, 1)], out.at[pl.ds(n, 1)], sem)
-            )
+    moves = [
+        (part.at[pl.ds(row, 1)], out.at[pl.ds(n, 1)])
+        for n, part in enumerate(parts)
+        for out, row in zip(outs, ((1 - odd) * last, odd * last))
+    ]
+    if moved is not None:
+        count = moved.stop - moved.start
+        sent_ref = refs[-2]
+        moves += [
+            (refs[0].at[pl.ds(moved.start, count)], sent_ref.at[pl.ds(0, count)]),
+            (
+                parts[3].at[pl.ds(moved.start - 1, count + 2)],
+                sent_ref.at[pl.ds(count, count + 2)],
+            ),
+        ]
+    copies = [
+        pltpu.make_async_copy(source, target, sems.at[n])
+        for n, (source, target) in enumerate(moves)
+    ]
     for copy in copies:
         copy.start()
     for copy in copies:
@@ -213,22 +238,34 @@
     )
 
 
-def last_inner_kernel(grad_ref, preact_ref, temporal_ref, spatial_ref, inner_ref, gpre_ref, views_ref):
+def last_inner_kernel(*refs):
+    grad_ref, preact_ref, kernels = refs[0], refs[1], refs[2:4]
+    sent_ref, outs, sem = refs[7], refs[8:11], refs[11]
+
     @pl.when(is_last())
     def _():
-        interior(
-            grad_ref, preact_ref, [], temporal_ref, spatial_ref, inner_ref, gpre_ref, views_ref
-        )
-
-
-def last_edge_kernel(grad_ref, one_ref, two_ref, gpre_ref, temporal_ref, spatial_ref, edge_ref, views_ref):
+        interior(grad_ref, preact_ref, [], *kernels, *outs)
+        count = sent_ref.shape[0]
+        copy = pltpu.make_async_copy(outs[0].at[pl.ds(0, count)], sent_ref, sem)
+        copy.start()
+        copy.wait()
+
+
+def last_edge_kernel(*refs):
+    grad_ref, pair_refs, gpre_ref, inner_ref = refs[0], refs[1:3], refs[3], refs[4]
+    temporal_ref, spatial_ref, edge_ref, views_ref = refs[5:]
+
     @pl.when(is_last())
     def _():
-        pair_refs = (one_ref, two_ref)
         edge_ref[0:1], edge_ref[1:2] = edge_rows(
             grad_ref, pair_refs, [], gpre_ref, temporal_ref, spatial_ref, views_ref
         )
         edge_ref[2:3], edge_ref[3:4] = beside_band(pair_refs, 0)
+
+    @pl.when(jnp.logical_not(is_last()))
+    def _():
+        moved = moved_rows(grad_ref.shape[0])
+        edge_ref[: moved.stop - moved.start] = inner_ref[moved.start - 1 : moved.stop - 1]
 
 
 def inner_kernel(later, *refs):
@@ -278,8 +315,8 @@
     hand_out(sums_ref, *outs)
 
 
-def sides_kernel(saved_ref, preact_ref, one_ref, two_ref, sides_ref):
-    left_sides(saved_ref, preact_ref, *beside_band((one_ref, two_ref), 3), sides_ref)
+def sides_kernel(moved, saved_ref, preact_ref, one_ref, two_ref, sides_ref):
+    left_sides(saved_ref, preact_ref, *beside_band((one_ref, two_ref), 3), sides_ref, moved)
 
 
 def pre_rows(preact, mids, temporal_ref, gpre_ref, views_ref, start):
@@ -288,7 +325,7 @@
     beside(gpre, views_ref, start)
 
 
-def block_sums(gpre_ref, sides_ref, mids, views_ref, sums_ref, keep_ref, send_ref):
+def block_sums(gpre_ref, sides_ref, mids, views_ref, sums_ref, keep_ref, send_ref, more=None):
     rows, cols, ch = gpre_ref.shape
     odd = lax.rem(lax.axis_index("section"), 2)
     size = send_ref.shape[0] - 2 * cols
@@ -296,6 +333,8 @@
     send_ref[size + cols : size + 2 * cols] = gpre_ref[odd * (rows - 1)]
     views = views_ref[...].reshape(rows * cols, 3 * ch)
     kernel_sums(sides_ref, [ref[...] for ref in mids], views, sums_ref)
+    if more is not None:
+        more()
     height = sums_ref.shape[1]
     hand_out(sums_ref, keep_ref, send_ref.at[:height], send_ref.at[height : 2 * height])
 
@@ -313,33 +352,63 @@
 
 
 def one_inner_kernel(preact_ref, inner_ref, after_ref, temporal_ref, gpre_ref, views_ref):
-    rows = inner_ref.shape[0]
-    for n in range(rows // 7):
-        here = slice(7 * n, 7 * n + 7)
-        after = after_ref[here]
-        after = jnp.where(is_last(), jnp.zeros_like(after), after)
-        preact = preact_ref[7 * n + 1 : 7 * n + 8]
-        pre_rows(preact, [inner_ref[here], after], temporal_ref, gpre_ref, views_ref, 7 * n)
+    known = after_ref.shape[0]
+    for rows in (slice(0, known // 2), slice(known // 2, known), slice(known, inner_ref.shape[0])):
+        grads = [inner_ref[rows]]
+        if rows.start < known:
+            after = after_ref[rows]
+            grads.append(jnp.where(is_last(), jnp.zeros_like(after), after))
+        preact = preact_ref[rows.start + 1 : rows.stop + 1]
+        pre_rows(preact, grads, temporal_ref, gpre_ref, views_ref, rows.start)
+
+
+def moved_sums(given_ref, moved_ref, mid, temporal_ref, extra_ref, views_ref, sums_ref):
+    count, cols, ch = mid.shape
+    flat = (count * cols, ch)
+    preact = given_ref[:count]
+    before = moved_ref[:count]
+    gpre = pre_gradient([before, mid], preact, temporal_ref)
+    extra_ref[...] = gpre.astype(jnp.bfloat16).reshape(flat)
+    beside(gpre, views_ref, 0)
+    sides = [given_ref[count + ky : 2 * count + ky].reshape(flat).T for ky in range(3)]
+    views = views_ref[...].reshape(count * cols, 3 * ch)
+    for ky in range(3):
+        sums_ref[ky] += jnp.concatenate(
+            [
+                jnp.dot(sides[ky], views[:, kx * ch : (kx + 1) * ch], preferred_element_type=jnp.float32)
+                for kx in range(3)
+            ],
+            axis=0,
+        )
+    hval = preact.astype(jnp.float32)
+    act = (hval * sigmoid(hval)).astype(jnp.bfloat16).reshape(flat).T
+    for k, grad in ((1, mid), (2, before)):
+        sums_ref[3, k * ch : (k + 1) * ch] += jnp.dot(
+            act, grad.reshape(flat), preferred_element_type=jnp.float32
+        )
 
 
 def mid_one_kernel(*refs):
     after_inner_ref, after_edge_ref = refs[5:7]
     temporal_two_ref, spatial_two_ref, sides_ref, preact_ref, temporal_ref = refs[7:12]
     inner_gpre_ref, inner_views_ref = refs[12:14]
-    mid_ref, gpre_ref, keep_ref, send_ref = refs[14:18]
-    views_ref, sums_ref, next_ref, edge_ref, edge_views_ref = refs[18:]
-    rows = next_ref.shape[0]
+    mid_ref, gpre_ref, keep_ref, send_ref, extra_ref = refs[14:19]
+    views_ref, sums_ref, next_ref, edge_ref, edge_views_ref, extra_views_ref = refs[19:]
+    rows, cols, ch = next_ref.shape
+    moved = moved_rows(rows)
+    next_ref[moved] = jnp.zeros((moved.stop - moved.start, cols, ch), next_ref.dtype)
 
     @pl.when(is_last())
     def _():
         edge_ref[...] = jnp.zeros(edge_ref.shape, edge_ref.dtype)
-        next_ref[...] = jnp.zeros(next_ref.shape, next_ref.dtype)
+        next_ref[: moved.start] = jnp.zeros((moved.start, cols, ch), next_ref.dtype)
+        next_ref[rows - 1 : rows] = jnp.zeros((1, cols, ch), next_ref.dtype)
 
     @pl.when(jnp.logical_not(is_last()))
     def _():
         edge_ref[...] = after_edge_ref[2:4]
         next_ref[0:1] = after_edge_ref[0:1]
-        next_ref[1 : rows - 1] = after_inner_ref[...]
+        next_ref[1 : moved.start] = after_inner_ref[...]
         next_ref[rows - 1 : rows] = after_edge_ref[1:2]
 
     mid_kernel(
@@ -351,10 +420,27 @@
         here = slice(row, row + 1)
         grads = [mid_ref[here], next_ref[here]]
         pre_rows(preact_ref[here], grads, temporal_ref, gpre_ref, views_ref, row)
-    block_sums(gpre_ref, sides_ref, [mid_ref, next_ref], views_ref, sums_ref, keep_ref, send_ref)
-
-
-def input_kernel(mid_ref, gpre_ref, pair_ref, across_ref, spatial_ref, out_ref, token_ref, views_ref):
+
+    def more():
+        @pl.when(is_last())
+        def _():
+            moved_sums(
+                after_inner_ref,
+                after_edge_ref,
+                mid_ref[moved],
+                temporal_ref,
+                extra_ref,
+                extra_views_ref,
+                sums_ref,
+            )
+
+    mids = [mid_ref, next_ref]
+    block_sums(gpre_ref, sides_ref, mids, views_ref, sums_ref, keep_ref, send_ref, more)
+
+
+def input_kernel(*refs):
+    mid_ref, gpre_ref, pair_ref, across_ref, spatial_ref = refs[:5]
+    given, (out_ref, token_ref, views_ref) = refs[5:-3], refs[-3:]
     rows, cols, ch = out_ref.shape
     pair = pair_ref[pair_ref.shape[0] - 2 * cols : pair_ref.shape[0] - cols]
     above, below = beside_band((pair[None], across_ref[across_ref.shape[0] - cols :][None]), 0)
@@ -367,6 +453,16 @@
         gpre = gpre_ref[pl.ds(n * step, step)].astype(jnp.float32)
         beside(gpre, views_ref, n * step + 1)
 
+    if given:
+
+        @pl.when(jnp.logical_not(is_last()))
+        def _():
+            moved = moved_rows(rows)
+            count = moved.stop - moved.start
+            size = given[0].shape[0] - count * cols
+            gpre = given[0][size:].reshape(count, cols, ch)
+            beside(gpre.astype(jnp.float32), views_ref, moved.start + 1)
+
     for n in range(rows // step):
         here = pl.ds(n * step, step)
         out_ref[here] = convolved(views_ref, spatial_ref, n * step, mid_ref[here])
@@ -384,11 +480,12 @@
     send_ref[...] = total.astype(jnp.bfloat16)
 
 
-def band_kernel(own_ref, part_ref, keep_ref, send_ref):
+def band_kernel(own_ref, part_ref, extra_ref, keep_ref, send_ref):
     mine, other = halves(keep_ref.shape[0], lax.axis_index("video"))
     half = keep_ref.shape[0]
     keep_ref[...] = own_ref[mine] + part_ref[mine].astype(jnp.float32)
     send_ref[:half] = (own_ref[other] + part_ref[other].astype(jnp.float32)).astype(jnp.bfloat16)
+    send_ref[half:] = extra_ref[...]
 
 
 def pair_quarter_kernel(keep_ref, part_ref, own_ref, across_ref, frame_ref, both_ref):
@@ -523,15 +620,18 @@
         return [from_ahead(x, 0, n + 1) for n in range(later)]
 
     wholes = from_later(grad)
+    moved = moved_rows(rows) if frames == 2 else None
+    count = moved.stop - moved.start if moved else 0
     packs = call(
-        pack_kernel,
-        [bf16(4, cols, ch)] * 2,
-        [pltpu.SemaphoreType.DMA((8,))],
+        functools.partial(pack_kernel, moved),
+        [bf16(4, cols, ch)] * 2 + ([bf16(rows - 2 - count, cols, ch)] if moved else []),
+        [pltpu.SemaphoreType.DMA((10,))],
         1,
         grad,
         pre_two,
         saved_two,
         saved_one,
+        *([pre_one] if moved else []),
         spare_inputs=True,
         limit=58,
     )
@@ -541,17 +641,18 @@
 
     known = ()
     if frames == 2:
-        known = call(
+        vmem, spare = (pl.BlockSpec(memory_space=space) for space in (pltpu.VMEM, pl.ANY))
+        sent, *known = pl.pallas_call(
             last_inner_kernel,
-            inner_outs,
-            [views],
-            0,
-            grad,
-            pre_two,
-            *kernels,
-            after=(first, second),
-        )
-        afters = from_later(known[0])
+            out_shape=(bf16(*packs[2].shape), *inner_outs),
+            in_specs=[vmem] * 4 + [spare] * 3,
+            out_specs=(spare, vmem, vmem),
+            scratch_shapes=[views, pltpu.SemaphoreType.DMA],
+            input_output_aliases={4: 0},
+            compiler_params=pltpu.CompilerParams(vmem_limit_bytes=24 * MIB),
+            cost_estimate=pl.CostEstimate(flops=0, bytes_accessed=0, transcendentals=0),
+        )(grad, pre_two, *kernels, packs[2], first, second)
+        afters = from_later(sent)
     else:
         afters = from_later(jnp.concatenate(beside_band(pairs, 0)))
     inner, gpre_two = call(
@@ -564,7 +665,7 @@
         *wholes,
         *kernels,
         *known,
-        early=(saved_two, saved_one, pre_one, temporal_one),
+        early=(saved_two, temporal_one),
     )
     if frames == 2:
         edge = call(
@@ -575,8 +676,8 @@
             grad,
             *pairs,
             known[1],
+            inner,
             *kernels,
-            after=(gpre_two,),
         )
         afters += from_later(edge)
     parts_two = call(
@@ -593,7 +694,14 @@
         after=(edge,) if frames == 2 else (),
     )
     sides_one = call(
-        sides_kernel, [sides], [], conv // 8, saved_one, pre_one, *pairs, after=parts_two[:1]
+        functools.partial(sides_kernel, moved),
+        [sides],
+        [],
+        conv // 8,
+        saved_one,
+        pre_one,
+        *pairs,
+        after=parts_two[:1],
     )
     height, half = 3 * ch, 3 * ch // 2
     keep_two, low_two, high_two = parts_two
@@ -621,11 +729,14 @@
             inner,
             afters[0],
             temporal_one,
-        )
-        mid, gpre_one, *parts_one = call(
+            after=(own_two,),
+        )
+        more_views = pltpu.VMEM((count, cols, 3 * ch), jnp.bfloat16)
+        edge_pair = pltpu.VMEM((2, cols, ch), jnp.bfloat16)
+        mid, gpre_one, *parts_one, extra = call(
             mid_one_kernel,
-            mid_outs + one_outs,
-            [views, sums, act, pltpu.VMEM((2, cols, ch), jnp.bfloat16), edge_views],
+            mid_outs + one_outs + [bf16(count * cols, ch)],
+            [views, sums, act, edge_pair, edge_views, more_views],
             8 * conv,
             *mid_inputs,
             *afters,
@@ -661,7 +772,7 @@
         send_one = later_than(send_one, across_two)
     pair_one = flipped(send_one, "section", 1)
 
-    def input_gradient(edge, after):
+    def input_gradient(edge, after, *given):
         return call(
             input_kernel,
             [bf16(rows, cols, ch), f32(8, 128)],
@@ -672,6 +783,7 @@
             pair_one,
             edge,
             spatial_one,
+            *given,
             after=after,
         )
 
@@ -682,13 +794,15 @@
 
         keep_two, send_two = call(
             band_kernel,
-            [f32(half, ch), bf16(half + 2 * cols, ch)],
+            [f32(half, ch), bf16(half + extra.shape[0], ch)],
             [],
             0,
             own_two,
             across_two,
-        )
-        sum_two = added(keep_two, flipped(send_two, "video", 1))
+            extra,
+        )
+        given_two = flipped(send_two, "video", 1)
+        sum_two = added(keep_two, given_two)
         quarters = [f32(half, ch)] + [bf16(half + more, ch) for more in (cols, 0, cols + 16)]
         own_one, *sends = call(
             pair_quarter_kernel, quarters, [], 0, keep_one, pair_one, after=(send_two,)
@@ -702,7 +816,7 @@
         sum_one = added(sum_one, part_one)
         last_two = flipped(sum_two, "dp", 2)
         last_one = flipped(later_than(sum_one, sum_two), "dp", 2)
-        grad_in, token = input_gradient(across, (sum_one,))
+        grad_in, token = input_gradient(across, (sum_one,), given_two)
         own = call(
             functools.partial(scaled_kernel, factor),
             [bf16(2, half, ch)],
@@ -731,7 +845,7 @@
             pair_one[height : 2 * height],
         )
         edge = flipped(pair_one[pair_one.shape[0] - cols :], "section", 2)
-        grad_in, _ = input_gradient(edge, ())
+        grad_in, _ = input_gradient(edge, (), *(from_later(extra) if frames == 2 else []))
         own_one = own_one + flipped(send_one, "section", 2).astype(jnp.float32)
         own_two = own_two + across_two.astype(jnp.float32)
         share = lax.psum(jnp.stack((own_one, own_two)), ("video", "dp")) * factor

time: 47.1 us -> 48 us (1.019)
  waiting for transfers between devices: 6.33 us -> 7.99 us
  starting transfers between devices: 30.4 us -> 29.3 us
    ppermute x23, waiting for transfers between devices: 6.33 us -> 7.98 us  [flipped(): lax.ppermute(block, axis, [(place ^ flip, place) for place in range(count)])]
    ppermute x23, starting transfers between devices: 27.2 us -> 26.4 us  [flipped(): lax.ppermute(block, axis, [(place ^ flip, place) for place in range(count)])]
    pallas_call x17 -> x16, Pallas kernels: 7.36 us -> 7.75 us  [call(): pl.pallas_call(body, out_shape=outs[0] if single else tuple(outs), in_spe...]
  transfers between devices with their start and end apart: 25 -> 25, of which waited for: 6 -> 10; matrix products, arithmetic and copies ran while one was open for 0% -> 0% of each run, Pallas kernels for 18% -> 19%
where the time goes in v18:
time: 48 us; the launch traced here: 47.8 us
  starting transfers between devices  29.3 us (61%)
  Pallas kernels  9.69 us (20%)
  waiting for transfers between devices  7.99 us (17%)
  between operations  0.84 us (2%)
    ppermute x23, starting transfers between devices, flipped(): lax.ppermute(block, axis, [(place ^ flip, place) for place in range(count)])  26.4 us
    ppermute x23, waiting for transfers between devices, flipped(): lax.ppermute(block, axis, [(place ^ flip, place) for place in range(count)])  7.98 us
    pallas_call x16, Pallas kernels, call(): pl.pallas_call(body, out_shape=outs[0] if single else tuple(outs), in_spe...  7.75 us
    ppermute x2, starting transfers between devices, flipped_both(): return lax.ppermute(block, ('section', 'video'), pairs)  2.84 us
    pallas_call x2, Pallas kernels, placed(): pl.pallas_call(functools.partial(place_kernel, places), out_shape=outs, i...  1.91 us
  transfers between devices with their start and end apart: 25, of which 10 were waited for; matrix products, arithmetic and copies ran while one was open for 0% of the time, Pallas kernels for 19%

profile of v18, /device:TPU:1, one launch (start us, length us, event | category | flops | bytes accessed | tf_op | source)
XLA Modules:
  0.0 47.8 jit_solution(18092516681143188428)
XLA Ops:
  0.6 2.1 %collective-permute-start.3 = (bf16[16,64,128]{2,1,0:T(8,128)(2,1)}, bf16[16,64,128]{2,1,0:T(8,128)(2,1)S(1)}, u32[]{:S(2)}, u32[]{:S(2)}) collective-permute-start(bf16[16,64,128]{2,1,0:T(8,128)(2,1)} %bitcast.10), channel_id=1, source_target_pairs={{4,0},{0,4},{5,1},{1,5},{6,2},{2,6},{7,3},{3,7},{12,8},{8,12},{13,... | collective-permute-start | bytes 786440 | tf_op jit(solution)/shard_map/ppermute | solution.py:73
  2.7 1.9 %shard_map.128 = (bf16[4,64,128]{2,1,0:T(8,128)(2,1)}, bf16[4,64,128]{2,1,0:T(8,128)(2,1)}, bf16[10,64,128]{2,1,0:T(8,128)(2,1)}) custom-call(bf16[16,64,128]{2,1,0:T(8,128)(2,1)} %bitcast.11, bf16[16,64,128]{2,1,0:T(8,128)(2,1)} %bitcast.17, bf16[16,64,128]{2,1,0:T(8,128)(2,1)} %bitcast.25, bf16[16,64,128]{2,1,0:T(8,128)(2,1)} %bitcast.28, ...), custom_call_target="tpu_custom_call" | custom-call | flops 1 | bytes 1605632 | tf_op jit(solution)/shard_map/pallas_call | solution.py:38
  4.7 1.0 %collective-permute-start = (bf16[4,64,128]{2,1,0:T(8,128)(2,1)}, bf16[4,64,128]{2,1,0:T(8,128)(2,1)S(1)}, u32[]{:S(2)}, u32[]{:S(2)}) collective-permute-start(bf16[4,64,128]{2,1,0:T(8,128)(2,1)} %get-tuple-element.46), channel_id=1, source_target_pairs={{8,0},{0,8},{24,16},{16,24},{9,1},{1,9},{25,17},{17,25},{10,2},{2,... | collective-permute-start | bytes 196616 | tf_op jit(solution)/shard_map/ppermute | solution.py:73
  5.7 1.1 %collective-permute-done.refs_6_ = bf16[4,64,128]{2,1,0:T(8,128)(2,1)S(1)} collective-permute-done((bf16[4,64,128]{2,1,0:T(8,128)(2,1)}, bf16[4,64,128]{2,1,0:T(8,128)(2,1)S(1)}, u32[]{:S(2)}, u32[]{:S(2)}) %collective-permute-start) | collective-permute-done | bytes 65568 | tf_op jit(solution)/shard_map/ppermute | solution.py:73
  7.1 1.2 %collective-permute-start.2 = (bf16[4,64,128]{2,1,0:T(8,128)(2,1)S(1)}, bf16[4,64,128]{2,1,0:T(8,128)(2,1)S(1)}, u32[]{:S(2)}, u32[]{:S(2)}) collective-permute-start(bf16[4,64,128]{2,1,0:T(8,128)(2,1)S(1)} %collective-permute-done.refs_6_), channel_id=1, source_target_pairs={{16,0},{24,8},{0,16},{8,24},{17,1},{25,9},{1,17},{9,25},{18,2},{26... | collective-permute-start | bytes 196616 | tf_op jit(solution)/shard_map/ppermute | solution.py:73
  8.5 2.0 %collective-permute-start.4 = (bf16[10,64,128]{2,1,0:T(8,128)(2,1)}, bf16[10,64,128]{2,1,0:T(8,128)(2,1)S(1)}, u32[]{:S(2)}, u32[]{:S(2)}) collective-permute-start(bf16[10,64,128]{2,1,0:T(8,128)(2,1)} %get-tuple-element.53), channel_id=1, source_target_pairs={{4,0},{0,4},{5,1},{1,5},{6,2},{2,6},{7,3},{3,7},{12,8},{8,12},{13,... | collective-permute-start | bytes 491528 | tf_op jit(solution)/shard_map/ppermute | solution.py:73
  10.5 1.0 %shard_map.130 = (bf16[14,64,128]{2,1,0:T(8,128)(2,1)S(1)}, bf16[16,64,128]{2,1,0:T(8,128)(2,1)S(1)}) custom-call(bf16[16,64,128]{2,1,0:T(8,128)(2,1)S(1)} %bitcast.13, bf16[16,64,128]{2,1,0:T(8,128)(2,1)S(1)} %bitcast.19, bf16[16,64,128]{2,1,0:T(8,128)(2,1)S(1)} %collective-permute-done.3.refs_2_.refs_6_, bf16[3,128,128]{2,1,0:T(8,128)(2,1)S(1)} %copy-done.6, ...), custom_call_target="tpu_custom_call" | custom-call | tf_op jit(solution)/shard_map/pallas_call | solution.py:38
  11.5 0.9 %shard_map.132 = (f32[2,384,128]{2,1,0:T(8,128)S(1)}, bf16[384,128]{1,0:T(8,128)(2,1)S(1)}, bf16[384,128]{1,0:T(8,128)(2,1)S(1)}) custom-call(bf16[16,64,128]{2,1,0:T(8,128)(2,1)S(1)} %bitcast.27, bf16[16,64,128]{2,1,0:T(8,128)(2,1)S(1)} %bitcast.20, bf16[16,64,128]{2,1,0:T(8,128)(2,1)S(1)} %get-tuple-element.52.refs_2_.refs_4_, ...), custom_call_target="tpu_custom_call" | custom-call | flops 2415919104 | bytes 2031616 | tf_op jit(solution)/shard_map/pallas_call | solution.py:38
  12.4 0.8 %collective-permute-start.6 = (bf16[384,128]{1,0:T(8,128)(2,1)S(1)}, bf16[384,128]{1,0:T(8,128)(2,1)S(1)}, u32[]{:S(2)}, u32[]{:S(2)}) collective-permute-start(bf16[384,128]{1,0:T(8,128)(2,1)S(1)} %get-tuple-element.55), channel_id=1, source_target_pairs={{8,0},{0,8},{24,16},{16,24},{9,1},{1,9},{25,17},{17,25},{10,2},{2,... | collective-permute-start | bytes 294920 | tf_op jit(solution)/shard_map/ppermute | solution.py:73
  14.6 1.1 %collective-permute-start.8 = (bf16[384,128]{1,0:T(8,128)(2,1)S(1)}, bf16[384,128]{1,0:T(8,128)(2,1)S(1)}, u32[]{:S(2)}, u32[]{:S(2)}) collective-permute-start(bf16[384,128]{1,0:T(8,128)(2,1)S(1)} %get-tuple-element.63), channel_id=1, source_target_pairs={{16,0},{24,8},{0,16},{8,24},{17,1},{25,9},{1,17},{9,25},{18,2},{26... | collective-permute-start | bytes 294920 | tf_op jit(solution)/shard_map/ppermute | solution.py:73
  16.4 1.2 %shard_map.136 = (bf16[16,64,128]{2,1,0:T(8,128)(2,1)S(1)}, bf16[16,64,128]{2,1,0:T(8,128)(2,1)S(1)}, f32[2,384,128]{2,1,0:T(8,128)S(1)}, bf16[896,128]{1,0:T(8,128)(2,1)S(1)}, bf16[256,128]{1,0:T(8,128)(2,1)S(1)}) custom-call(bf16[16,64,128]{2,1,0:T(8,128)(2,1)S(1)} %bitcast.16, ...), custom_call_target="tpu_custom_call" | custom-call | flops 2415919104 | bytes 5046272 | tf_op jit(solution)/shard_map/pallas_call | solution.py:38
  17.6 1.2 %collective-permute-done.8.refs_1_ = bf16[384,128]{1,0:T(8,128)(2,1)S(1)} collective-permute-done((bf16[384,128]{1,0:T(8,128)(2,1)S(1)}, bf16[384,128]{1,0:T(8,128)(2,1)S(1)}, u32[]{:S(2)}, u32[]{:S(2)}) %collective-permute-start.8) | collective-permute-done | bytes 98336 | tf_op jit(solution)/shard_map/ppermute | solution.py:73
  18.9 1.0 %collective-permute-start.9 = (bf16[896,128]{1,0:T(8,128)(2,1)S(1)}, bf16[896,128]{1,0:T(8,128)(2,1)S(1)}, u32[]{:S(2)}, u32[]{:S(2)}) collective-permute-start(bf16[896,128]{1,0:T(8,128)(2,1)S(1)} %get-tuple-element.64), channel_id=1, source_target_pairs={{8,0},{0,8},{24,16},{16,24},{9,1},{1,9},{25,17},{17,25},{10,2},{2,... | collective-permute-start | bytes 688136 | tf_op jit(solution)/shard_map/ppermute | solution.py:73
  19.9 0.9 %collective-permute-start.11 = (bf16[448,128]{1,0:T(8,128)(2,1)S(1)}, bf16[448,128]{1,0:T(8,128)(2,1)S(1)}, u32[]{:S(2)}, u32[]{:S(2)}) collective-permute-start(bf16[448,128]{1,0:T(8,128)(2,1)S(1)} %get-tuple-element.67.refs_2_), channel_id=1, source_target_pairs={{4,0},{0,4},{5,1},{1,5},{6,2},{2,6},{7,3},{3,7},{12,8},{8,12},{13,... | collective-permute-start | bytes 344072 | tf_op jit(solution)/shard_map/ppermute | solution.py:73
  21.0 1.7 %collective-permute-start.13 = (bf16[272,128]{1,0:T(8,128)(2,1)S(1)}, bf16[272,128]{1,0:T(8,128)(2,1)S(1)}, u32[]{:S(2)}, u32[]{:S(2)}) collective-permute-start(bf16[272,128]{1,0:T(8,128)(2,1)S(1)} %get-tuple-element.71), channel_id=1, source_target_pairs={{20,0},{16,4},{28,8},{24,12},{4,16},{0,20},{12,24},{8,28},{21,1},{... | collective-permute-start | bytes 208904 | tf_op jit(solution)/shard_map/ppermute | solution.py:81
  23.0 0.7 %collective-permute-start.12 = (bf16[192,128]{1,0:T(8,128)(2,1)S(1)}, bf16[192,128]{1,0:T(8,128)(2,1)S(1)}, u32[]{:S(2)}, u32[]{:S(2)}) collective-permute-start(bf16[192,128]{1,0:T(8,128)(2,1)S(1)} %get-tuple-element.70), channel_id=1, source_target_pairs={{4,0},{0,4},{5,1},{1,5},{6,2},{2,6},{7,3},{3,7},{12,8},{8,12},{13,... | collective-permute-start | bytes 147464 | tf_op jit(solution)/shard_map/ppermute | solution.py:73
  23.7 1.0 %collective-permute-done.11.refs_1_.refs_5_ = bf16[448,128]{1,0:T(8,128)(2,1)S(1)} collective-permute-done((bf16[448,128]{1,0:T(8,128)(2,1)S(1)}, bf16[448,128]{1,0:T(8,128)(2,1)S(1)}, u32[]{:S(2)}, u32[]{:S(2)}) %collective-permute-start.11) | collective-permute-done | bytes 114720 | tf_op jit(solution)/shard_map/ppermute | solution.py:73
  24.7 1.4 %collective-permute-start.15 = (bf16[192,128]{1,0:T(8,128)(2,1)S(1)}, bf16[192,128]{1,0:T(8,128)(2,1)S(1)}, u32[]{:S(2)}, u32[]{:S(2)}) collective-permute-start(bf16[192,128]{1,0:T(8,128)(2,1)S(1)} %shard_map.140.refs_0_), channel_id=1, source_target_pairs={{1,0},{0,1},{3,2},{2,3},{5,4},{4,5},{7,6},{6,7},{9,8},{8,9},{11,10... | collective-permute-start | bytes 147464 | tf_op jit(solution)/shard_map/ppermute | solution.py:73
  26.1 1.0 %collective-permute-done.12.refs_2_ = bf16[192,128]{1,0:T(8,128)(2,1)S(1)} collective-permute-done((bf16[192,128]{1,0:T(8,128)(2,1)S(1)}, bf16[192,128]{1,0:T(8,128)(2,1)S(1)}, u32[]{:S(2)}, u32[]{:S(2)}) %collective-permute-start.12) | collective-permute-done | bytes 49184 | tf_op jit(solution)/shard_map/ppermute | solution.py:73
  27.8 1.4 %collective-permute-start.14 = (bf16[192,128]{1,0:T(8,128)(2,1)S(1)}, bf16[192,128]{1,0:T(8,128)(2,1)S(1)}, u32[]{:S(2)}, u32[]{:S(2)}) collective-permute-start(bf16[192,128]{1,0:T(8,128)(2,1)S(1)} %shard_map.139.refs_0_), channel_id=1, source_target_pairs={{1,0},{0,1},{3,2},{2,3},{5,4},{4,5},{7,6},{6,7},{9,8},{8,9},{11,10... | collective-permute-start | bytes 147464 | tf_op jit(solution)/shard_map/ppermute | solution.py:73
  29.1 2.3 %collective-permute-start.17 = (bf16[192,128]{1,0:T(8,128)(2,1)S(1)}, bf16[192,128]{1,0:T(8,128)(2,1)S(1)}, u32[]{:S(2)}, u32[]{:S(2)}) collective-permute-start(bf16[192,128]{1,0:T(8,128)(2,1)S(1)} %shard_map.143.refs_2_), channel_id=1, source_target_pairs={{2,0},{3,1},{0,2},{1,3},{6,4},{7,5},{4,6},{5,7},{10,8},{11,9},{8,1... | collective-permute-start | bytes 147464 | tf_op jit(solution)/shard_map/ppermute | solution.py:73
  31.5 1.7 %collective-permute-start.16 = (bf16[192,128]{1,0:T(8,128)(2,1)S(1)}, bf16[192,128]{1,0:T(8,128)(2,1)S(1)}, u32[]{:S(2)}, u32[]{:S(2)}) collective-permute-start(bf16[192,128]{1,0:T(8,128)(2,1)S(1)} %shard_map.141.refs_6_.refs_0_), channel_id=1, source_target_pairs={{2,0},{3,1},{0,2},{1,3},{6,4},{7,5},{4,6},{5,7},{10,8},{11,9},{8,1... | collective-permute-start | bytes 147464 | tf_op jit(solution)/shard_map/ppermute | solution.py:73
  33.1 1.7 %shard_map.142 = (bf16[16,64,128]{2,1,0:T(8,128)(2,1)}, f32[8,128]{1,0:T(8,128)S(1)}) custom-call(bf16[16,64,128]{2,1,0:T(8,128)(2,1)S(1)} %get-tuple-element.60.refs_0_, bf16[16,64,128]{2,1,0:T(8,128)(2,1)S(1)} %get-tuple-element.61.refs_1_, bf16[896,128]{1,0:T(8,128)(2,1)S(1)} %collective-permute-done.9.refs_1_.refs_2_, ...), custom_call_target="tpu_custom_call" | custom-call | flops 301989888 | bytes 1495040 | tf_op jit(solution)/shard_map/pallas_call | solution.py:38
  34.8 1.6 %collective-permute-done.16.refs_1_ = bf16[192,128]{1,0:T(8,128)(2,1)S(1)} collective-permute-done((bf16[192,128]{1,0:T(8,128)(2,1)S(1)}, bf16[192,128]{1,0:T(8,128)(2,1)S(1)}, u32[]{:S(2)}, u32[]{:S(2)}) %collective-permute-start.16) | collective-permute-done | bytes 49184 | tf_op jit(solution)/shard_map/ppermute | solution.py:73
  36.5 0.7 %collective-permute-start.21 = (bf16[2,192,128]{2,1,0:T(8,128)(2,1)S(1)}, bf16[2,192,128]{2,1,0:T(8,128)(2,1)S(1)}, u32[]{:S(2)}, u32[]{:S(2)}) collective-permute-start(bf16[2,192,128]{2,1,0:T(8,128)(2,1)S(1)} %shard_map.144.refs_0_), channel_id=1, source_target_pairs={{16,0},{24,8},{0,16},{8,24},{17,1},{25,9},{1,17},{9,25},{18,2},{26... | collective-permute-start | bytes 294920 | tf_op jit(solution)/shard_map/ppermute | solution.py:73
  37.1 0.9 %collective-permute-start.20 = (bf16[2,192,128]{2,1,0:T(8,128)(2,1)S(1)}, bf16[2,192,128]{2,1,0:T(8,128)(2,1)S(1)}, u32[]{:S(2)}, u32[]{:S(2)}) collective-permute-start(bf16[2,192,128]{2,1,0:T(8,128)(2,1)S(1)} %shard_map.144.refs_0_), channel_id=1, source_target_pairs={{4,0},{0,4},{5,1},{1,5},{6,2},{2,6},{7,3},{3,7},{12,8},{8,12},{13,... | collective-permute-start | bytes 294920 | tf_op jit(solution)/shard_map/ppermute | solution.py:73
  38.0 1.2 %collective-permute-start.18 = (bf16[2,192,128]{2,1,0:T(8,128)(2,1)S(1)}, bf16[2,192,128]{2,1,0:T(8,128)(2,1)S(1)}, u32[]{:S(2)}, u32[]{:S(2)}) collective-permute-start(bf16[2,192,128]{2,1,0:T(8,128)(2,1)S(1)} %shard_map.144.refs_0_), channel_id=1, source_target_pairs={{20,0},{16,4},{28,8},{24,12},{4,16},{0,20},{12,24},{8,28},{21,1},{... | collective-permute-start | bytes 294920 | tf_op jit(solution)/shard_map/ppermute | solution.py:81
  39.2 2.5 %collective-permute-start.22 = (bf16[2,192,128]{2,1,0:T(8,128)(2,1)S(1)}, bf16[2,192,128]{2,1,0:T(8,128)(2,1)S(1)}, u32[]{:S(2)}, u32[]{:S(2)}) collective-permute-start(bf16[2,192,128]{2,1,0:T(8,128)(2,1)S(1)} %shard_map.144.refs_0_), channel_id=1, source_target_pairs={{8,0},{0,8},{24,16},{16,24},{9,1},{1,9},{25,17},{17,25},{10,2},{2,... | collective-permute-start | bytes 294920 | tf_op jit(solution)/shard_map/ppermute | solution.py:73
  41.7 2.2 %collective-permute-start.24 = (bf16[2,192,128]{2,1,0:T(8,128)(2,1)S(1)}, bf16[2,192,128]{2,1,0:T(8,128)(2,1)S(1)}, u32[]{:S(2)}, u32[]{:S(2)}) collective-permute-start(bf16[2,192,128]{2,1,0:T(8,128)(2,1)S(1)} %collective-permute-done.21.refs_2_), channel_id=1, source_target_pairs={{8,0},{0,8},{24,16},{16,24},{9,1},{1,9},{25,17},{17,25},{10,2},{2,... | collective-permute-start | bytes 294920 | tf_op jit(solution)/shard_map/ppermute | solution.py:73
  43.9 2.0 %collective-permute-start.19 = (bf16[2,192,128]{2,1,0:T(8,128)(2,1)S(1)}, bf16[2,192,128]{2,1,0:T(8,128)(2,1)S(1)}, u32[]{:S(2)}, u32[]{:S(2)}) collective-permute-start(bf16[2,192,128]{2,1,0:T(8,128)(2,1)S(1)} %collective-permute-done.18.refs_6_), channel_id=1, source_target_pairs={{8,0},{0,8},{24,16},{16,24},{9,1},{1,9},{25,17},{17,25},{10,2},{2,... | collective-permute-start | bytes 294920 | tf_op jit(solution)/shard_map/ppermute | solution.py:73
  45.9 1.2 %shard_map.145 = (f32[3,384,128]{2,1,0:T(8,128)}, f32[384,128]{1,0:T(8,128)}, f32[3,384,128]{2,1,0:T(8,128)}, f32[384,128]{1,0:T(8,128)}) custom-call(bf16[2,192,128]{2,1,0:T(8,128)(2,1)S(1)} %shard_map.144.refs_0_, bf16[2,192,128]{2,1,0:T(8,128)(2,1)S(1)} %collective-permute-done.20.refs_1_, bf16[2,192,128]{2,1,0:T(8,128)(2,1)S(1)} %collective-permute-done.21.refs_2_, ...), custom_call_target="tpu_custom_call" | custom-call | bytes 2064384 | tf_op jit(solution)/shard_map/pallas_call | solution.py:564
  47.1 0.7 %shard_map.146 = (f32[3,384,128]{2,1,0:T(8,128)}, f32[384,128]{1,0:T(8,128)}, f32[3,384,128]{2,1,0:T(8,128)}, f32[384,128]{1,0:T(8,128)}) custom-call(bf16[2,192,128]{2,1,0:T(8,128)(2,1)S(1)} %collective-permute-done.19.refs_0_, f32[3,384,128]{2,1,0:T(8,128)} %get-tuple-element.77.refs_1_, ...), custom_call_target="tpu_custom_call", output_to_operand_aliasing={{0}: (1, {}), {1}: (2, {}), {2}: (3, {}), {3}: (4, {})} | custom-call | bytes 294912 | tf_op jit(solution)/shard_map/pallas_call | solution.py:564
  (55 shorter events, 3.9 us)
Async XLA Ops:
  0.6 9.8 %collective-permute-start.3 = (bf16[16,64,128]{2,1,0:T(8,128)(2,1)}, bf16[16,64,128]{2,1,0:T(8,128)(2,1)S(1)}, u32[]{:S(2)}, u32[]{:S(2)}) collective-permute-start(bf16[16,64,128]{2,1,0:T(8,128)(2,1)} %bitcast.10), channel_id=1, source_target_pairs={{4,0},{0,4},{5,1},{1,5},{6,2},{2,6},{7,3},{3,7},{12,8},{8,12},{13,... | collective-permute-start | bytes 786440 | tf_op jit(solution)/shard_map/ppermute | solution.py:73
  2.7 5.7 %copy-start = (bf16[1,1,16,64,128]{4,3,2,1,0:T(8,128)(2,1)S(1)}, bf16[1,1,16,64,128]{4,3,2,1,0:T(8,128)(2,1)}, u32[]{:S(2)}) copy-start(bf16[1,1,16,64,128]{4,3,2,1,0:T(8,128)(2,1)} %param.9) | copy-start | bytes 786436
  2.7 5.7 %copy-start.1 = (bf16[3,3,128,128]{3,2,1,0:T(8,128)(2,1)S(1)}, bf16[3,3,128,128]{3,2,1,0:T(8,128)(2,1)}, u32[]{:S(2)}) copy-start(bf16[3,3,128,128]{3,2,1,0:T(8,128)(2,1)} %refs_8_.3) | copy-start | bytes 884740
  2.7 5.7 %copy-start.2 = (bf16[1,1,16,64,128]{4,3,2,1,0:T(8,128)(2,1)S(1)}, bf16[1,1,16,64,128]{4,3,2,1,0:T(8,128)(2,1)}, u32[]{:S(2)}) copy-start(bf16[1,1,16,64,128]{4,3,2,1,0:T(8,128)(2,1)} %param.13) | copy-start | bytes 786436
  2.7 5.7 %copy-start.6 = (bf16[3,128,128]{2,1,0:T(8,128)(2,1)S(1)}, bf16[3,128,128]{2,1,0:T(8,128)(2,1)}, u32[]{:S(2)}) copy-start(bf16[3,128,128]{2,1,0:T(8,128)(2,1)} %refs_7_.1) | copy-start | bytes 294916
  4.7 2.1 %collective-permute-start = (bf16[4,64,128]{2,1,0:T(8,128)(2,1)}, bf16[4,64,128]{2,1,0:T(8,128)(2,1)S(1)}, u32[]{:S(2)}, u32[]{:S(2)}) collective-permute-start(bf16[4,64,128]{2,1,0:T(8,128)(2,1)} %get-tuple-element.46), channel_id=1, source_target_pairs={{8,0},{0,8},{24,16},{16,24},{9,1},{1,9},{25,17},{17,25},{10,2},{2,... | collective-permute-start | bytes 196616 | tf_op jit(solution)/shard_map/ppermute | solution.py:73
  6.8 1.6 %collective-permute-start.1 = (bf16[4,64,128]{2,1,0:T(8,128)(2,1)}, bf16[4,64,128]{2,1,0:T(8,128)(2,1)S(1)}, u32[]{:S(2)}, u32[]{:S(2)}) collective-permute-start(bf16[4,64,128]{2,1,0:T(8,128)(2,1)} %get-tuple-element.47), channel_id=1, source_target_pairs={{8,0},{0,8},{24,16},{16,24},{9,1},{1,9},{25,17},{17,25},{10,2},{2,... | collective-permute-start | bytes 196616 | tf_op jit(solution)/shard_map/ppermute | solution.py:73
  7.1 4.3 %collective-permute-start.2 = (bf16[4,64,128]{2,1,0:T(8,128)(2,1)S(1)}, bf16[4,64,128]{2,1,0:T(8,128)(2,1)S(1)}, u32[]{:S(2)}, u32[]{:S(2)}) collective-permute-start(bf16[4,64,128]{2,1,0:T(8,128)(2,1)S(1)} %collective-permute-done.refs_6_), channel_id=1, source_target_pairs={{16,0},{24,8},{0,16},{8,24},{17,1},{25,9},{1,17},{9,25},{18,2},{26... | collective-permute-start | bytes 196616 | tf_op jit(solution)/shard_map/ppermute | solution.py:73
  8.4 2.0 %copy-start.4 = (bf16[1,1,16,64,128]{4,3,2,1,0:T(8,128)(2,1)S(1)}, bf16[1,1,16,64,128]{4,3,2,1,0:T(8,128)(2,1)}, u32[]{:S(2)}) copy-start(bf16[1,1,16,64,128]{4,3,2,1,0:T(8,128)(2,1)} %param.12) | copy-start | bytes 786436
  8.4 2.0 %copy-start.7 = (bf16[3,128,128]{2,1,0:T(8,128)(2,1)S(1)}, bf16[3,128,128]{2,1,0:T(8,128)(2,1)}, u32[]{:S(2)}) copy-start(bf16[3,128,128]{2,1,0:T(8,128)(2,1)} %refs_11_.1) | copy-start | bytes 294916
  8.5 7.2 %collective-permute-start.4 = (bf16[10,64,128]{2,1,0:T(8,128)(2,1)}, bf16[10,64,128]{2,1,0:T(8,128)(2,1)S(1)}, u32[]{:S(2)}, u32[]{:S(2)}) collective-permute-start(bf16[10,64,128]{2,1,0:T(8,128)(2,1)} %get-tuple-element.53), channel_id=1, source_target_pairs={{4,0},{0,4},{5,1},{1,5},{6,2},{2,6},{7,3},{3,7},{12,8},{8,12},{13,... | collective-permute-start | bytes 491528 | tf_op jit(solution)/shard_map/ppermute | solution.py:73
  12.4 1.7 %collective-permute-start.6 = (bf16[384,128]{1,0:T(8,128)(2,1)S(1)}, bf16[384,128]{1,0:T(8,128)(2,1)S(1)}, u32[]{:S(2)}, u32[]{:S(2)}) collective-permute-start(bf16[384,128]{1,0:T(8,128)(2,1)S(1)} %get-tuple-element.55), channel_id=1, source_target_pairs={{8,0},{0,8},{24,16},{16,24},{9,1},{1,9},{25,17},{17,25},{10,2},{2,... | collective-permute-start | bytes 294920 | tf_op jit(solution)/shard_map/ppermute | solution.py:73
  13.2 1.3 %collective-permute-start.7 = (bf16[384,128]{1,0:T(8,128)(2,1)S(1)}, bf16[384,128]{1,0:T(8,128)(2,1)S(1)}, u32[]{:S(2)}, u32[]{:S(2)}) collective-permute-start(bf16[384,128]{1,0:T(8,128)(2,1)S(1)} %get-tuple-element.56), channel_id=1, source_target_pairs={{8,0},{0,8},{24,16},{16,24},{9,1},{1,9},{25,17},{17,25},{10,2},{2,... | collective-permute-start | bytes 294920 | tf_op jit(solution)/shard_map/ppermute | solution.py:73
  13.3 3.1 %collective-permute-start.5 = (bf16[4,64,128]{2,1,0:T(8,128)(2,1)S(1)}, bf16[4,64,128]{2,1,0:T(8,128)(2,1)S(1)}, u32[]{:S(2)}, u32[]{:S(2)}) collective-permute-start(bf16[4,64,128]{2,1,0:T(8,128)(2,1)S(1)} %shard_map.131.refs_7_), channel_id=1, source_target_pairs={{4,0},{0,4},{5,1},{1,5},{6,2},{2,6},{7,3},{3,7},{12,8},{8,12},{13,... | collective-permute-start | bytes 196616 | tf_op jit(solution)/shard_map/ppermute | solution.py:73
  14.6 4.3 %collective-permute-start.8 = (bf16[384,128]{1,0:T(8,128)(2,1)S(1)}, bf16[384,128]{1,0:T(8,128)(2,1)S(1)}, u32[]{:S(2)}, u32[]{:S(2)}) collective-permute-start(bf16[384,128]{1,0:T(8,128)(2,1)S(1)} %get-tuple-element.63), channel_id=1, source_target_pairs={{16,0},{24,8},{0,16},{8,24},{17,1},{25,9},{1,17},{9,25},{18,2},{26... | collective-permute-start | bytes 294920 | tf_op jit(solution)/shard_map/ppermute | solution.py:73
  18.9 2.1 %collective-permute-start.9 = (bf16[896,128]{1,0:T(8,128)(2,1)S(1)}, bf16[896,128]{1,0:T(8,128)(2,1)S(1)}, u32[]{:S(2)}, u32[]{:S(2)}) collective-permute-start(bf16[896,128]{1,0:T(8,128)(2,1)S(1)} %get-tuple-element.64), channel_id=1, source_target_pairs={{8,0},{0,8},{24,16},{16,24},{9,1},{1,9},{25,17},{17,25},{10,2},{2,... | collective-permute-start | bytes 688136 | tf_op jit(solution)/shard_map/ppermute | solution.py:73
  19.9 4.8 %collective-permute-start.11 = (bf16[448,128]{1,0:T(8,128)(2,1)S(1)}, bf16[448,128]{1,0:T(8,128)(2,1)S(1)}, u32[]{:S(2)}, u32[]{:S(2)}) collective-permute-start(bf16[448,128]{1,0:T(8,128)(2,1)S(1)} %get-tuple-element.67.refs_2_), channel_id=1, source_target_pairs={{4,0},{0,4},{5,1},{1,5},{6,2},{2,6},{7,3},{3,7},{12,8},{8,12},{13,... | collective-permute-start | bytes 344072 | tf_op jit(solution)/shard_map/ppermute | solution.py:73
  21.0 6.7 %collective-permute-start.13 = (bf16[272,128]{1,0:T(8,128)(2,1)S(1)}, bf16[272,128]{1,0:T(8,128)(2,1)S(1)}, u32[]{:S(2)}, u32[]{:S(2)}) collective-permute-start(bf16[272,128]{1,0:T(8,128)(2,1)S(1)} %get-tuple-element.71), channel_id=1, source_target_pairs={{20,0},{16,4},{28,8},{24,12},{4,16},{0,20},{12,24},{8,28},{21,1},{... | collective-permute-start | bytes 208904 | tf_op jit(solution)/shard_map/ppermute | solution.py:81
  22.7 5.1 %collective-permute-start.10 = (bf16[256,128]{1,0:T(8,128)(2,1)S(1)}, bf16[256,128]{1,0:T(8,128)(2,1)S(1)}, u32[]{:S(2)}, u32[]{:S(2)}) collective-permute-start(bf16[256,128]{1,0:T(8,128)(2,1)S(1)} %get-tuple-element.68), channel_id=1, source_target_pairs={{16,0},{24,8},{0,16},{8,24},{17,1},{25,9},{1,17},{9,25},{18,2},{26... | collective-permute-start | bytes 196616 | tf_op jit(solution)/shard_map/ppermute | solution.py:73
  23.0 4.1 %collective-permute-start.12 = (bf16[192,128]{1,0:T(8,128)(2,1)S(1)}, bf16[192,128]{1,0:T(8,128)(2,1)S(1)}, u32[]{:S(2)}, u32[]{:S(2)}) collective-permute-start(bf16[192,128]{1,0:T(8,128)(2,1)S(1)} %get-tuple-element.70), channel_id=1, source_target_pairs={{4,0},{0,4},{5,1},{1,5},{6,2},{2,6},{7,3},{3,7},{12,8},{8,12},{13,... | collective-permute-start | bytes 147464 | tf_op jit(solution)/shard_map/ppermute | solution.py:73
  24.7 4.4 %collective-permute-start.15 = (bf16[192,128]{1,0:T(8,128)(2,1)S(1)}, bf16[192,128]{1,0:T(8,128)(2,1)S(1)}, u32[]{:S(2)}, u32[]{:S(2)}) collective-permute-start(bf16[192,128]{1,0:T(8,128)(2,1)S(1)} %shard_map.140.refs_0_), channel_id=1, source_target_pairs={{1,0},{0,1},{3,2},{2,3},{5,4},{4,5},{7,6},{6,7},{9,8},{8,9},{11,10... | collective-permute-start | bytes 147464 | tf_op jit(solution)/shard_map/ppermute | solution.py:73
  27.7 5.4 %copy-start.8 = (bf16[3,3,128,128]{3,2,1,0:T(8,128)(2,1)S(1)}, bf16[3,3,128,128]{3,2,1,0:T(8,128)(2,1)}, u32[]{:S(2)}) copy-start(bf16[3,3,128,128]{3,2,1,0:T(8,128)(2,1)} %refs_4_.3) | copy-start | bytes 884740
  27.8 3.7 %collective-permute-start.14 = (bf16[192,128]{1,0:T(8,128)(2,1)S(1)}, bf16[192,128]{1,0:T(8,128)(2,1)S(1)}, u32[]{:S(2)}, u32[]{:S(2)}) collective-permute-start(bf16[192,128]{1,0:T(8,128)(2,1)S(1)} %shard_map.139.refs_0_), channel_id=1, source_target_pairs={{1,0},{0,1},{3,2},{2,3},{5,4},{4,5},{7,6},{6,7},{9,8},{8,9},{11,10... | collective-permute-start | bytes 147464 | tf_op jit(solution)/shard_map/ppermute | solution.py:73
  29.1 5.7 %collective-permute-start.17 = (bf16[192,128]{1,0:T(8,128)(2,1)S(1)}, bf16[192,128]{1,0:T(8,128)(2,1)S(1)}, u32[]{:S(2)}, u32[]{:S(2)}) collective-permute-start(bf16[192,128]{1,0:T(8,128)(2,1)S(1)} %shard_map.143.refs_2_), channel_id=1, source_target_pairs={{2,0},{3,1},{0,2},{1,3},{6,4},{7,5},{4,6},{5,7},{10,8},{11,9},{8,1... | collective-permute-start | bytes 147464 | tf_op jit(solution)/shard_map/ppermute | solution.py:73
  31.5 5.0 %collective-permute-start.16 = (bf16[192,128]{1,0:T(8,128)(2,1)S(1)}, bf16[192,128]{1,0:T(8,128)(2,1)S(1)}, u32[]{:S(2)}, u32[]{:S(2)}) collective-permute-start(bf16[192,128]{1,0:T(8,128)(2,1)S(1)} %shard_map.141.refs_6_.refs_0_), channel_id=1, source_target_pairs={{2,0},{3,1},{0,2},{1,3},{6,4},{7,5},{4,6},{5,7},{10,8},{11,9},{8,1... | collective-permute-start | bytes 147464 | tf_op jit(solution)/shard_map/ppermute | solution.py:73
  36.5 5.2 %collective-permute-start.21 = (bf16[2,192,128]{2,1,0:T(8,128)(2,1)S(1)}, bf16[2,192,128]{2,1,0:T(8,128)(2,1)S(1)}, u32[]{:S(2)}, u32[]{:S(2)}) collective-permute-start(bf16[2,192,128]{2,1,0:T(8,128)(2,1)S(1)} %shard_map.144.refs_0_), channel_id=1, source_target_pairs={{16,0},{24,8},{0,16},{8,24},{17,1},{25,9},{1,17},{9,25},{18,2},{26... | collective-permute-start | bytes 294920 | tf_op jit(solution)/shard_map/ppermute | solution.py:73
  37.1 6.7 %collective-permute-start.20 = (bf16[2,192,128]{2,1,0:T(8,128)(2,1)S(1)}, bf16[2,192,128]{2,1,0:T(8,128)(2,1)S(1)}, u32[]{:S(2)}, u32[]{:S(2)}) collective-permute-start(bf16[2,192,128]{2,1,0:T(8,128)(2,1)S(1)} %shard_map.144.refs_0_), channel_id=1, source_target_pairs={{4,0},{0,4},{5,1},{1,5},{6,2},{2,6},{7,3},{3,7},{12,8},{8,12},{13,... | collective-permute-start | bytes 294920 | tf_op jit(solution)/shard_map/ppermute | solution.py:73
  38.0 5.9 %collective-permute-start.18 = (bf16[2,192,128]{2,1,0:T(8,128)(2,1)S(1)}, bf16[2,192,128]{2,1,0:T(8,128)(2,1)S(1)}, u32[]{:S(2)}, u32[]{:S(2)}) collective-permute-start(bf16[2,192,128]{2,1,0:T(8,128)(2,1)S(1)} %shard_map.144.refs_0_), channel_id=1, source_target_pairs={{20,0},{16,4},{28,8},{24,12},{4,16},{0,20},{12,24},{8,28},{21,1},{... | collective-permute-start | bytes 294920 | tf_op jit(solution)/shard_map/ppermute | solution.py:81
  39.2 6.7 %collective-permute-start.22 = (bf16[2,192,128]{2,1,0:T(8,128)(2,1)S(1)}, bf16[2,192,128]{2,1,0:T(8,128)(2,1)S(1)}, u32[]{:S(2)}, u32[]{:S(2)}) collective-permute-start(bf16[2,192,128]{2,1,0:T(8,128)(2,1)S(1)} %shard_map.144.refs_0_), channel_id=1, source_target_pairs={{8,0},{0,8},{24,16},{16,24},{9,1},{1,9},{25,17},{17,25},{10,2},{2,... | collective-permute-start | bytes 294920 | tf_op jit(solution)/shard_map/ppermute | solution.py:73
  41.7 4.2 %collective-permute-start.24 = (bf16[2,192,128]{2,1,0:T(8,128)(2,1)S(1)}, bf16[2,192,128]{2,1,0:T(8,128)(2,1)S(1)}, u32[]{:S(2)}, u32[]{:S(2)}) collective-permute-start(bf16[2,192,128]{2,1,0:T(8,128)(2,1)S(1)} %collective-permute-done.21.refs_2_), channel_id=1, source_target_pairs={{8,0},{0,8},{24,16},{16,24},{9,1},{1,9},{25,17},{17,25},{10,2},{2,... | collective-permute-start | bytes 294920 | tf_op jit(solution)/shard_map/ppermute | solution.py:73
  43.9 2.0 %collective-permute-start.23 = (bf16[2,192,128]{2,1,0:T(8,128)(2,1)S(1)}, bf16[2,192,128]{2,1,0:T(8,128)(2,1)S(1)}, u32[]{:S(2)}, u32[]{:S(2)}) collective-permute-start(bf16[2,192,128]{2,1,0:T(8,128)(2,1)S(1)} %collective-permute-done.20.refs_1_), channel_id=1, source_target_pairs={{8,0},{0,8},{24,16},{16,24},{9,1},{1,9},{25,17},{17,25},{10,2},{2,... | collective-permute-start | bytes 294920 | tf_op jit(solution)/shard_map/ppermute | solution.py:73
  43.9 3.2 %collective-permute-start.19 = (bf16[2,192,128]{2,1,0:T(8,128)(2,1)S(1)}, bf16[2,192,128]{2,1,0:T(8,128)(2,1)S(1)}, u32[]{:S(2)}, u32[]{:S(2)}) collective-permute-start(bf16[2,192,128]{2,1,0:T(8,128)(2,1)S(1)} %collective-permute-done.18.refs_6_), channel_id=1, source_target_pairs={{8,0},{0,8},{24,16},{16,24},{9,1},{1,9},{25,17},{17,25},{10,2},{2,... | collective-permute-start | bytes 294920 | tf_op jit(solution)/shard_map/ppermute | solution.py:73
  (2 other events, 3.5 us)

commit v19 on v17

--- a/solution.py
+++ b/solution.py
@@ -145,22 +145,29 @@
     sums = jnp.dot(shifts, views, preferred_element_type=jnp.float32)
     for ky in range(3):
         for kx in range(3):
-            here = slice(kx * ch, (kx + 1) * ch)
-            sums_ref[ky, here] = sums[ky * ch : (ky + 1) * ch, here]
+            value = sums[ky * ch : (ky + 1) * ch, kx * ch : (kx + 1) * ch]
+            sums_ref[(3 * ky + kx) * ch : (3 * ky + kx + 1) * ch] = value
+    steps = len(grads)
     grads = jnp.concatenate([grad.reshape(pixels, ch) for grad in grads], axis=1)
     sums = jnp.dot(sides_ref[3], grads, preferred_element_type=jnp.float32)
-    zeros = jnp.zeros((ch, ch), jnp.float32)
-    for k in range(3):
-        step = 2 - k
-        value = sums[:, step * ch : (step + 1) * ch] if step * ch < grads.shape[1] else zeros
-        sums_ref[3, k * ch : (k + 1) * ch] = jnp.where(is_last(), zeros, value) if step else value
+    for step in range(steps):
+        value = sums[:, step * ch : (step + 1) * ch]
+        start = (8 + steps - step) * ch
+        sums_ref[start : start + ch] = (
+            jnp.where(is_last(), jnp.zeros_like(value), value) if step else value
+        )
 
 
 def hand_out(sums_ref, keep_ref, *send_refs):
     odd = lax.rem(lax.axis_index("section"), 2)
+    height = keep_ref.shape[1]
+
+    def share(band):
+        return sums_ref[pl.ds(pl.multiple_of(band * height, height), height)]
+
     for n, send_ref in enumerate(send_refs):
-        keep_ref[n] = sums_ref[2 * n + odd]
-        send_ref[...] = sums_ref[2 * n + 1 - odd].astype(jnp.bfloat16)
+        keep_ref[n] = share(2 * n + odd)
+        send_ref[...] = share(2 * n + 1 - odd).astype(jnp.bfloat16)
 
 
 def pack_kernel(*refs):
@@ -296,7 +303,7 @@
     send_ref[size + cols : size + 2 * cols] = gpre_ref[odd * (rows - 1)]
     views = views_ref[...].reshape(rows * cols, 3 * ch)
     kernel_sums(sides_ref, [ref[...] for ref in mids], views, sums_ref)
-    height = sums_ref.shape[1]
+    height = keep_ref.shape[1]
     hand_out(sums_ref, keep_ref, send_ref.at[:height], send_ref.at[height : 2 * height])
 
 
@@ -430,60 +437,86 @@
         out_ref[block] = ((one + two) * factor).astype(jnp.bfloat16)
 
 
-def place_kernel(places, *refs):
-    shares, outs = refs[: len(places)], refs[-6:-2]
-    sums_ref, sems = refs[-2:]
+def place_kernel(places, skipped, zeros, *refs):
+    shares, outs = refs[: len(places)], refs[-8:-4]
+    sums_ref, sems, zeros_ref, zeros_sems = refs[-4:]
     band, frame = lax.axis_index("section"), lax.axis_index("video")
-    height = shares[0].shape[1]
+    _, rows, _ = shares[0].shape
+    size = outs[0].shape[0]
+    whole, cut = size // rows, size % rows
 
     def copies(n, block):
         flip, other = places[n]
-        place = jnp.bitwise_xor(band, flip)
-        half = 0 if other is None else jnp.bitwise_xor(frame, int(other))
-        here = pl.ds(pl.multiple_of(half * height, height), height)
+        at = jnp.bitwise_xor(band, flip)
+        if other is not None:
+            at = 2 * at + jnp.bitwise_xor(frame, int(other))
         spatial, temporal = outs[2 * block : 2 * block + 2]
-        source, sem = sums_ref.at[n, block], sems.at[n, block]
-        return (
-            (place < 3, lambda: pltpu.make_async_copy(source, spatial.at[place, here], sem)),
-            (place == 3, lambda: pltpu.make_async_copy(source, temporal.at[here], sem)),
-        )
-
-    for n, share in enumerate(shares):
-        for block in range(2):
-            sums_ref[n, block] = share[block].astype(jnp.float32)
-            for inside, copy in copies(n, block):
-                pl.when(inside)(lambda: copy().start())
-    for n in range(len(shares)):
-        for block in range(2):
-            for inside, copy in copies(n, block):
-                pl.when(inside)(lambda: copy().wait())
-
-
-def placed(shares, places, given=()):
-    _, height, ch = shares[0].shape
+        source = sums_ref.at[n, block]
+        start = pl.multiple_of(at * rows, 16)
+        inside = [(at < whole, [(source, spatial.at[pl.ds(start, rows)])])]
+        first = whole
+        if cut:
+            upper = source.at[pl.ds(0, cut)], spatial.at[pl.ds(whole * rows, cut)]
+            lower = source.at[pl.ds(cut, rows - cut)], temporal.at[pl.ds(skipped, rows - cut)]
+            inside.append((at == whole, [upper, lower]))
+            first += 1
+        start = pl.multiple_of((at - first) * rows + first * rows - size + skipped, 16)
+        inside.append((at >= first, [(source, temporal.at[pl.ds(start, rows)])]))
+        return [
+            (here, [(*pair, sems.at[n, block, part]) for part, pair in enumerate(pairs)])
+            for here, pairs in inside
+        ]
+
+    def each(act):
+        for n in range(len(shares)):
+            for block in range(2):
+                if act == "start":
+                    sums_ref[n, block] = shares[n][block].astype(jnp.float32)
+                for here, pairs in copies(n, block):
+
+                    @pl.when(here)
+                    def _():
+                        for pair in pairs:
+                            getattr(pltpu.make_async_copy(*pair), act)()
+
+        if zeros and skipped:
+            for block in range(2):
+                target = outs[2 * block + 1].at[pl.ds(0, skipped)]
+                copy = pltpu.make_async_copy(zeros_ref, target, zeros_sems.at[block])
+                getattr(copy, act)()
+
+    zeros_ref[...] = jnp.zeros(zeros_ref.shape, zeros_ref.dtype)
+    each("start")
+    each("wait")
+
+
+def placed(shares, places, skipped, given=()):
+    _, rows, ch = shares[0].shape
     count = len(shares)
-    outs = (f32(3, 3 * ch, ch), f32(3 * ch, ch)) * 2
+    outs = (f32(9 * ch, ch), f32(3 * ch, ch)) * 2
     vmem, spare = (pl.BlockSpec(memory_space=space) for space in (pltpu.VMEM, pl.ANY))
     return pl.pallas_call(
-        functools.partial(place_kernel, places),
+        functools.partial(place_kernel, places, skipped, not given),
         out_shape=outs,
         in_specs=[vmem] * count + [spare] * len(given),
         out_specs=(spare,) * 4,
         scratch_shapes=[
-            pltpu.VMEM((count, 2, height, ch), jnp.float32),
-            pltpu.SemaphoreType.DMA((count, 2)),
+            pltpu.VMEM((count, 2, rows, ch), jnp.float32),
+            pltpu.SemaphoreType.DMA((count, 2, 2)),
+            pltpu.VMEM((max(skipped, 8), ch), jnp.float32),
+            pltpu.SemaphoreType.DMA((2,)),
         ],
         input_output_aliases={count + n: n for n in range(len(given))},
         compiler_params=pltpu.CompilerParams(vmem_limit_bytes=24 * MIB),
         cost_estimate=pl.CostEstimate(
-            flops=0, bytes_accessed=6 * count * height * ch * 2, transcendentals=0
+            flops=0, bytes_accessed=6 * count * rows * ch * 2, transcendentals=0
         ),
     )(*shares, *given)
 
 
 def unpacked(sums):
     ch = sums[0].shape[-1]
-    return [x.reshape(3, 3, ch, ch) if x.ndim == 3 else x.reshape(3, ch, ch) for x in sums]
+    return [x.reshape((3,) * (1 + (x.shape[0] > 3 * ch)) + (ch, ch)) for x in sums]
 
 
 def on_device(
@@ -512,8 +545,12 @@
     edge_views = pltpu.VMEM((6, cols, 3 * ch), jnp.bfloat16)
     act = pltpu.VMEM((rows, cols, ch), jnp.bfloat16)
     sides = bf16(4, ch, rows * cols)
-    sums = pltpu.VMEM((4, 3 * ch, ch), jnp.float32)
-    handed = [f32(2, 3 * ch, ch)] + [bf16(3 * ch, ch)] * 2
+    blocks = 10 + later
+    height = blocks * ch // 4
+    half = height // 2
+    skipped = (2 - later) * ch
+    sums = pltpu.VMEM((blocks * ch, ch), jnp.float32)
+    handed = [f32(2, height, ch)] + [bf16(height, ch)] * 2
     inner_outs = [bf16(rows - 2, cols, ch), bf16(rows, cols, ch)]
     kernels = (temporal_two, spatial_two)
 
@@ -595,7 +632,6 @@
     sides_one = call(
         sides_kernel, [sides], [], conv // 8, saved_one, pre_one, *pairs, after=parts_two[:1]
     )
-    height, half = 3 * ch, 3 * ch // 2
     keep_two, low_two, high_two = parts_two
     own_two, send_two = call(
         pair_kernel,
@@ -610,7 +646,7 @@
     mid_inputs = (grad, *pairs, inner, gpre_two)
     one_inputs = (sides_one, pre_one)
     mid_outs = [bf16(rows, cols, ch)]
-    one_outs = [bf16(rows, cols, ch), f32(2, 3 * ch, ch), bf16(6 * ch + 2 * cols, ch)]
+    one_outs = [bf16(rows, cols, ch), f32(2, height, ch), bf16(2 * height + 2 * cols, ch)]
     if frames == 2:
         inners_one = call(
             one_inner_kernel,
@@ -718,8 +754,8 @@
         shares = [own, frame, across]
         shares += [flipped(share, "section", 1) for share in shares]
         places = [(0, False), (0, True), (2, False), (1, False), (1, True), (3, False)]
-        sums = placed([*shares, both], [*places, (2, True)])
-        sums = unpacked(placed([flipped(both, "section", 1)], [(3, True)], sums))
+        sums = placed([*shares, both], [*places, (2, True)], skipped)
+        sums = unpacked(placed([flipped(both, "section", 1)], [(3, True)], skipped, sums))
     else:
         own_one, send_one = call(
             pair_kernel,
@@ -738,7 +774,8 @@
         share = share.astype(jnp.bfloat16)
         shares = [share, flipped(share, "section", 2)]
         shares += [flipped(share, "section", 1) for share in shares]
-        sums = unpacked(placed(shares, [(0, None), (2, None), (1, None), (3, None)]))
+        places = [(0, None), (2, None), (1, None), (3, None)]
+        sums = unpacked(placed(shares, places, skipped))
     return (grad_in.reshape(shape), *sums)
 
 

time: 47.1 us -> 47 us (level)
  no operation moved by 1% of the time
where the time goes in v19:
time: 47 us; the launch traced here: 46.8 us
  starting transfers between devices  30.5 us (65%)
  Pallas kernels  9.43 us (20%)
  waiting for transfers between devices  6.01 us (13%)
  between operations  0.83 us (2%)
    ppermute x23, starting transfers between devices, flipped(): lax.ppermute(block, axis, [(place ^ flip, place) for place in range(count)])  27.4 us
    pallas_call x17, Pallas kernels, call(): pl.pallas_call(body, out_shape=outs[0] if single else tuple(outs), in_spe...  7.33 us
    ppermute x23, waiting for transfers between devices, flipped(): lax.ppermute(block, axis, [(place ^ flip, place) for place in range(count)])  6 us
    ppermute x2, starting transfers between devices, flipped_both(): return lax.ppermute(block, ('section', 'video'), pairs)  3.12 us
    pallas_call x2, Pallas kernels, placed(): pl.pallas_call(functools.partial(place_kernel, places, skipped, not given...  2.09 us
  transfers between devices with their start and end apart: 25, of which 6 were waited for; matrix products, arithmetic and copies ran while one was open for 0% of the time, Pallas kernels for 18%

profile of v19, /device:TPU:1, one launch (start us, length us, event | category | flops | bytes accessed | tf_op | source)
XLA Modules:
  0.0 46.8 jit_solution(11306546238113336975)
XLA Ops:
  0.6 2.1 %collective-permute-start.3 = (bf16[16,64,128]{2,1,0:T(8,128)(2,1)}, bf16[16,64,128]{2,1,0:T(8,128)(2,1)S(1)}, u32[]{:S(2)}, u32[]{:S(2)}) collective-permute-start(bf16[16,64,128]{2,1,0:T(8,128)(2,1)} %bitcast.10), channel_id=1, source_target_pairs={{4,0},{0,4},{5,1},{1,5},{6,2},{2,6},{7,3},{3,7},{12,8},{8,12},{13,... | collective-permute-start | bytes 786440 | tf_op jit(solution)/shard_map/ppermute | solution.py:73
  2.7 1.6 %shard_map.128 = (bf16[4,64,128]{2,1,0:T(8,128)(2,1)}, bf16[4,64,128]{2,1,0:T(8,128)(2,1)}) custom-call(bf16[16,64,128]{2,1,0:T(8,128)(2,1)} %bitcast.11, bf16[16,64,128]{2,1,0:T(8,128)(2,1)} %bitcast.17, bf16[16,64,128]{2,1,0:T(8,128)(2,1)} %bitcast.28, bf16[16,64,128]{2,1,0:T(8,128)(2,1)} %bitcast.25), custom_call_target="tpu_custom_call" | custom-call | flops 1 | bytes 1179648 | tf_op jit(solution)/shard_map/pallas_call | solution.py:38
  4.4 1.0 %collective-permute-start = (bf16[4,64,128]{2,1,0:T(8,128)(2,1)}, bf16[4,64,128]{2,1,0:T(8,128)(2,1)S(1)}, u32[]{:S(2)}, u32[]{:S(2)}) collective-permute-start(bf16[4,64,128]{2,1,0:T(8,128)(2,1)} %get-tuple-element.43), channel_id=1, source_target_pairs={{8,0},{0,8},{24,16},{16,24},{9,1},{1,9},{25,17},{17,25},{10,2},{2,... | collective-permute-start | bytes 196616 | tf_op jit(solution)/shard_map/ppermute | solution.py:73
  5.4 1.1 %collective-permute-done.refs_5_ = bf16[4,64,128]{2,1,0:T(8,128)(2,1)S(1)} collective-permute-done((bf16[4,64,128]{2,1,0:T(8,128)(2,1)}, bf16[4,64,128]{2,1,0:T(8,128)(2,1)S(1)}, u32[]{:S(2)}, u32[]{:S(2)}) %collective-permute-start) | collective-permute-done | bytes 65568 | tf_op jit(solution)/shard_map/ppermute | solution.py:73
  6.9 1.2 %collective-permute-start.2 = (bf16[4,64,128]{2,1,0:T(8,128)(2,1)S(1)}, bf16[4,64,128]{2,1,0:T(8,128)(2,1)S(1)}, u32[]{:S(2)}, u32[]{:S(2)}) collective-permute-start(bf16[4,64,128]{2,1,0:T(8,128)(2,1)S(1)} %collective-permute-done.refs_5_), channel_id=1, source_target_pairs={{16,0},{24,8},{0,16},{8,24},{17,1},{25,9},{1,17},{9,25},{18,2},{26... | collective-permute-start | bytes 196616 | tf_op jit(solution)/shard_map/ppermute | solution.py:73
  8.2 1.3 %collective-permute-start.4 = (bf16[14,64,128]{2,1,0:T(8,128)(2,1)S(1)}, bf16[14,64,128]{2,1,0:T(8,128)(2,1)S(1)}, u32[]{:S(2)}, u32[]{:S(2)}) collective-permute-start(bf16[14,64,128]{2,1,0:T(8,128)(2,1)S(1)} %get-tuple-element.45.refs_5_), channel_id=1, source_target_pairs={{4,0},{0,4},{5,1},{1,5},{6,2},{2,6},{7,3},{3,7},{12,8},{8,12},{13,... | collective-permute-start | bytes 688136 | tf_op jit(solution)/shard_map/ppermute | solution.py:73
  9.6 1.0 %shard_map.130 = (bf16[14,64,128]{2,1,0:T(8,128)(2,1)S(1)}, bf16[16,64,128]{2,1,0:T(8,128)(2,1)S(1)}) custom-call(bf16[16,64,128]{2,1,0:T(8,128)(2,1)S(1)} %bitcast.13, bf16[16,64,128]{2,1,0:T(8,128)(2,1)S(1)} %bitcast.19, bf16[16,64,128]{2,1,0:T(8,128)(2,1)S(1)} %collective-permute-done.3.refs_2_.refs_6_, bf16[3,128,128]{2,1,0:T(8,128)(2,1)S(1)} %copy-done.6, ...), custom_call_target="tpu_custom_call" | custom-call | tf_op jit(solution)/shard_map/pallas_call | solution.py:38
  10.6 0.8 %shard_map.132 = (f32[2,352,128]{2,1,0:T(8,128)S(1)}, bf16[352,128]{1,0:T(8,128)(2,1)S(1)}, bf16[352,128]{1,0:T(8,128)(2,1)S(1)}) custom-call(bf16[16,64,128]{2,1,0:T(8,128)(2,1)S(1)} %bitcast.30, bf16[16,64,128]{2,1,0:T(8,128)(2,1)S(1)} %bitcast.20, bf16[16,64,128]{2,1,0:T(8,128)(2,1)S(1)} %get-tuple-element.48.refs_6_.refs_2_.refs_4_, ...), custom_call_target="tpu_custom_call" | custom-call | flops 2415919104 | bytes 1982464 | tf_op jit(solution)/shard_map/pallas_call | solution.py:38
  11.5 0.9 %collective-permute-start.6 = (bf16[352,128]{1,0:T(8,128)(2,1)S(1)}, bf16[352,128]{1,0:T(8,128)(2,1)S(1)}, u32[]{:S(2)}, u32[]{:S(2)}) collective-permute-start(bf16[352,128]{1,0:T(8,128)(2,1)S(1)} %get-tuple-element.52), channel_id=1, source_target_pairs={{8,0},{0,8},{24,16},{16,24},{9,1},{1,9},{25,17},{17,25},{10,2},{2,... | collective-permute-start | bytes 270344 | tf_op jit(solution)/shard_map/ppermute | solution.py:73
  12.4 0.8 %collective-permute-start.5 = (bf16[4,64,128]{2,1,0:T(8,128)(2,1)S(1)}, bf16[4,64,128]{2,1,0:T(8,128)(2,1)S(1)}, u32[]{:S(2)}, u32[]{:S(2)}) collective-permute-start(bf16[4,64,128]{2,1,0:T(8,128)(2,1)S(1)} %shard_map.131.refs_7_), channel_id=1, source_target_pairs={{4,0},{0,4},{5,1},{1,5},{6,2},{2,6},{7,3},{3,7},{12,8},{8,12},{13,... | collective-permute-start | bytes 196616 | tf_op jit(solution)/shard_map/ppermute | solution.py:73
  13.7 1.4 %collective-permute-start.8 = (bf16[352,128]{1,0:T(8,128)(2,1)S(1)}, bf16[352,128]{1,0:T(8,128)(2,1)S(1)}, u32[]{:S(2)}, u32[]{:S(2)}) collective-permute-start(bf16[352,128]{1,0:T(8,128)(2,1)S(1)} %get-tuple-element.58), channel_id=1, source_target_pairs={{16,0},{24,8},{0,16},{8,24},{17,1},{25,9},{1,17},{9,25},{18,2},{26... | collective-permute-start | bytes 270344 | tf_op jit(solution)/shard_map/ppermute | solution.py:73
  15.6 1.0 %collective-permute-done.5.refs_6_ = bf16[4,64,128]{2,1,0:T(8,128)(2,1)S(1)} collective-permute-done((bf16[4,64,128]{2,1,0:T(8,128)(2,1)S(1)}, bf16[4,64,128]{2,1,0:T(8,128)(2,1)S(1)}, u32[]{:S(2)}, u32[]{:S(2)}) %collective-permute-start.5) | collective-permute-done | bytes 65568 | tf_op jit(solution)/shard_map/ppermute | solution.py:73
  16.6 1.3 %shard_map.136 = (bf16[16,64,128]{2,1,0:T(8,128)(2,1)S(1)}, bf16[16,64,128]{2,1,0:T(8,128)(2,1)S(1)}, f32[2,352,128]{2,1,0:T(8,128)S(1)}, bf16[832,128]{1,0:T(8,128)(2,1)S(1)}) custom-call(bf16[16,64,128]{2,1,0:T(8,128)(2,1)S(1)} %bitcast.16, bf16[4,64,128]{2,1,0:T(8,128)(2,1)S(1)} %collective-permute-done.1.refs_4_.refs_1_.refs_3_.refs_2_, ...), custom_call_target="tpu_custom_call" | custom-call | flops 2415919104 | bytes 4997120 | tf_op jit(solution)/shard_map/pallas_call | solution.py:38
  17.9 1.2 %collective-permute-start.9 = (bf16[832,128]{1,0:T(8,128)(2,1)S(1)}, bf16[832,128]{1,0:T(8,128)(2,1)S(1)}, u32[]{:S(2)}, u32[]{:S(2)}) collective-permute-start(bf16[832,128]{1,0:T(8,128)(2,1)S(1)} %get-tuple-element.59), channel_id=1, source_target_pairs={{8,0},{0,8},{24,16},{16,24},{9,1},{1,9},{25,17},{17,25},{10,2},{2,... | collective-permute-start | bytes 638984 | tf_op jit(solution)/shard_map/ppermute | solution.py:73
  19.1 1.3 %collective-permute-start.13 = (bf16[304,128]{1,0:T(8,128)(2,1)S(1)}, bf16[304,128]{1,0:T(8,128)(2,1)S(1)}, u32[]{:S(2)}, u32[]{:S(2)}) collective-permute-start(bf16[304,128]{1,0:T(8,128)(2,1)S(1)} %get-tuple-element.61.refs_2_), channel_id=1, source_target_pairs={{4,0},{0,4},{5,1},{1,5},{6,2},{2,6},{7,3},{3,7},{12,8},{8,12},{13,... | collective-permute-start | bytes 233480 | tf_op jit(solution)/shard_map/ppermute | solution.py:73
  20.5 1.9 %collective-permute-start.12 = (bf16[256,128]{1,0:T(8,128)(2,1)S(1)}, bf16[256,128]{1,0:T(8,128)(2,1)S(1)}, u32[]{:S(2)}, u32[]{:S(2)}) collective-permute-start(bf16[256,128]{1,0:T(8,128)(2,1)S(1)} %get-tuple-element.65), channel_id=1, source_target_pairs={{20,0},{16,4},{28,8},{24,12},{4,16},{0,20},{12,24},{8,28},{21,1},{... | collective-permute-start | bytes 196616 | tf_op jit(solution)/shard_map/ppermute | solution.py:81
  23.2 1.4 %collective-permute-start.15 = (bf16[176,128]{1,0:T(8,128)(2,1)S(1)}, bf16[176,128]{1,0:T(8,128)(2,1)S(1)}, u32[]{:S(2)}, u32[]{:S(2)}) collective-permute-start(bf16[176,128]{1,0:T(8,128)(2,1)S(1)} %shard_map.140.refs_0_), channel_id=1, source_target_pairs={{1,0},{0,1},{3,2},{2,3},{5,4},{4,5},{7,6},{6,7},{9,8},{8,9},{11,10... | collective-permute-start | bytes 135176 | tf_op jit(solution)/shard_map/ppermute | solution.py:73
  24.6 1.2 %collective-permute-done.11.refs_2_ = bf16[176,128]{1,0:T(8,128)(2,1)S(1)} collective-permute-done((bf16[176,128]{1,0:T(8,128)(2,1)S(1)}, bf16[176,128]{1,0:T(8,128)(2,1)S(1)}, u32[]{:S(2)}, u32[]{:S(2)}) %collective-permute-start.11) | collective-permute-done | bytes 45088 | tf_op jit(solution)/shard_map/ppermute | solution.py:73
  25.8 0.9 %collective-permute-done.10.refs_1_.refs_3_ = bf16[240,128]{1,0:T(8,128)(2,1)S(1)} collective-permute-done((bf16[240,128]{1,0:T(8,128)(2,1)S(1)}, bf16[240,128]{1,0:T(8,128)(2,1)S(1)}, u32[]{:S(2)}, u32[]{:S(2)}) %collective-permute-start.10) | collective-permute-done | bytes 61472 | tf_op jit(solution)/shard_map/ppermute | solution.py:73
  26.7 1.4 %collective-permute-start.14 = (bf16[176,128]{1,0:T(8,128)(2,1)S(1)}, bf16[176,128]{1,0:T(8,128)(2,1)S(1)}, u32[]{:S(2)}, u32[]{:S(2)}) collective-permute-start(bf16[176,128]{1,0:T(8,128)(2,1)S(1)} %shard_map.139.refs_0_), channel_id=1, source_target_pairs={{1,0},{0,1},{3,2},{2,3},{5,4},{4,5},{7,6},{6,7},{9,8},{8,9},{11,10... | collective-permute-start | bytes 135176 | tf_op jit(solution)/shard_map/ppermute | solution.py:73
  28.1 2.4 %collective-permute-start.17 = (bf16[176,128]{1,0:T(8,128)(2,1)S(1)}, bf16[176,128]{1,0:T(8,128)(2,1)S(1)}, u32[]{:S(2)}, u32[]{:S(2)}) collective-permute-start(bf16[176,128]{1,0:T(8,128)(2,1)S(1)} %shard_map.143.refs_2_), channel_id=1, source_target_pairs={{2,0},{3,1},{0,2},{1,3},{6,4},{7,5},{4,6},{5,7},{10,8},{11,9},{8,1... | collective-permute-start | bytes 135176 | tf_op jit(solution)/shard_map/ppermute | solution.py:73
  30.5 1.6 %collective-permute-start.16 = (bf16[176,128]{1,0:T(8,128)(2,1)S(1)}, bf16[176,128]{1,0:T(8,128)(2,1)S(1)}, u32[]{:S(2)}, u32[]{:S(2)}) collective-permute-start(bf16[176,128]{1,0:T(8,128)(2,1)S(1)} %shard_map.141.refs_5_.refs_0_), channel_id=1, source_target_pairs={{2,0},{3,1},{0,2},{1,3},{6,4},{7,5},{4,6},{5,7},{10,8},{11,9},{8,1... | collective-permute-start | bytes 135176 | tf_op jit(solution)/shard_map/ppermute | solution.py:73
  32.1 1.5 %shard_map.142 = (bf16[16,64,128]{2,1,0:T(8,128)(2,1)}, f32[8,128]{1,0:T(8,128)S(1)}) custom-call(bf16[16,64,128]{2,1,0:T(8,128)(2,1)S(1)} %get-tuple-element.55.refs_0_, bf16[16,64,128]{2,1,0:T(8,128)(2,1)S(1)} %get-tuple-element.56.refs_1_, bf16[832,128]{1,0:T(8,128)(2,1)S(1)} %collective-permute-done.9.refs_1_.refs_2_, ...), custom_call_target="tpu_custom_call" | custom-call | flops 301989888 | bytes 1359872 | tf_op jit(solution)/shard_map/pallas_call | solution.py:38
  33.6 1.7 %collective-permute-done.16.refs_1_ = bf16[176,128]{1,0:T(8,128)(2,1)S(1)} collective-permute-done((bf16[176,128]{1,0:T(8,128)(2,1)S(1)}, bf16[176,128]{1,0:T(8,128)(2,1)S(1)}, u32[]{:S(2)}, u32[]{:S(2)}) %collective-permute-start.16) | collective-permute-done | bytes 45088 | tf_op jit(solution)/shard_map/ppermute | solution.py:73
  35.3 0.8 %collective-permute-start.20 = (bf16[2,176,128]{2,1,0:T(8,128)(2,1)S(1)}, bf16[2,176,128]{2,1,0:T(8,128)(2,1)S(1)}, u32[]{:S(2)}, u32[]{:S(2)}) collective-permute-start(bf16[2,176,128]{2,1,0:T(8,128)(2,1)S(1)} %shard_map.144.refs_0_), channel_id=1, source_target_pairs={{4,0},{0,4},{5,1},{1,5},{6,2},{2,6},{7,3},{3,7},{12,8},{8,12},{13,... | collective-permute-start | bytes 270344 | tf_op jit(solution)/shard_map/ppermute | solution.py:73
  36.1 0.7 %collective-permute-start.21 = (bf16[2,176,128]{2,1,0:T(8,128)(2,1)S(1)}, bf16[2,176,128]{2,1,0:T(8,128)(2,1)S(1)}, u32[]{:S(2)}, u32[]{:S(2)}) collective-permute-start(bf16[2,176,128]{2,1,0:T(8,128)(2,1)S(1)} %shard_map.144.refs_0_), channel_id=1, source_target_pairs={{16,0},{24,8},{0,16},{8,24},{17,1},{25,9},{1,17},{9,25},{18,2},{26... | collective-permute-start | bytes 270344 | tf_op jit(solution)/shard_map/ppermute | solution.py:73
  36.8 1.2 %collective-permute-start.18 = (bf16[2,176,128]{2,1,0:T(8,128)(2,1)S(1)}, bf16[2,176,128]{2,1,0:T(8,128)(2,1)S(1)}, u32[]{:S(2)}, u32[]{:S(2)}) collective-permute-start(bf16[2,176,128]{2,1,0:T(8,128)(2,1)S(1)} %shard_map.144.refs_0_), channel_id=1, source_target_pairs={{20,0},{16,4},{28,8},{24,12},{4,16},{0,20},{12,24},{8,28},{21,1},{... | collective-permute-start | bytes 270344 | tf_op jit(solution)/shard_map/ppermute | solution.py:81
  38.0 2.7 %collective-permute-start.22 = (bf16[2,176,128]{2,1,0:T(8,128)(2,1)S(1)}, bf16[2,176,128]{2,1,0:T(8,128)(2,1)S(1)}, u32[]{:S(2)}, u32[]{:S(2)}) collective-permute-start(bf16[2,176,128]{2,1,0:T(8,128)(2,1)S(1)} %shard_map.144.refs_0_), channel_id=1, source_target_pairs={{8,0},{0,8},{24,16},{16,24},{9,1},{1,9},{25,17},{17,25},{10,2},{2,... | collective-permute-start | bytes 270344 | tf_op jit(solution)/shard_map/ppermute | solution.py:73
  40.7 1.6 %collective-permute-start.23 = (bf16[2,176,128]{2,1,0:T(8,128)(2,1)S(1)}, bf16[2,176,128]{2,1,0:T(8,128)(2,1)S(1)}, u32[]{:S(2)}, u32[]{:S(2)}) collective-permute-start(bf16[2,176,128]{2,1,0:T(8,128)(2,1)S(1)} %collective-permute-done.20.refs_1_), channel_id=1, source_target_pairs={{8,0},{0,8},{24,16},{16,24},{9,1},{1,9},{25,17},{17,25},{10,2},{2,... | collective-permute-start | bytes 270344 | tf_op jit(solution)/shard_map/ppermute | solution.py:73
  42.9 1.8 %collective-permute-start.19 = (bf16[2,176,128]{2,1,0:T(8,128)(2,1)S(1)}, bf16[2,176,128]{2,1,0:T(8,128)(2,1)S(1)}, u32[]{:S(2)}, u32[]{:S(2)}) collective-permute-start(bf16[2,176,128]{2,1,0:T(8,128)(2,1)S(1)} %collective-permute-done.18.refs_6_), channel_id=1, source_target_pairs={{8,0},{0,8},{24,16},{16,24},{9,1},{1,9},{25,17},{17,25},{10,2},{2,... | collective-permute-start | bytes 270344 | tf_op jit(solution)/shard_map/ppermute | solution.py:73
  44.7 1.4 %shard_map.145 = (f32[1152,128]{1,0:T(8,128)}, f32[384,128]{1,0:T(8,128)}, f32[1152,128]{1,0:T(8,128)}, f32[384,128]{1,0:T(8,128)}) custom-call(bf16[2,176,128]{2,1,0:T(8,128)(2,1)S(1)} %shard_map.144.refs_0_, bf16[2,176,128]{2,1,0:T(8,128)(2,1)S(1)} %collective-permute-done.20.refs_1_, bf16[2,176,128]{2,1,0:T(8,128)(2,1)S(1)} %collective-permute-done.21.refs_2_, ...), custom_call_target="tpu_custom_call" | custom-call | bytes 1892352 | tf_op jit(solution)/shard_map/pallas_call | solution.py:498
  46.1 0.7 %shard_map.146 = (f32[1152,128]{1,0:T(8,128)}, f32[384,128]{1,0:T(8,128)}, f32[1152,128]{1,0:T(8,128)}, f32[384,128]{1,0:T(8,128)}) custom-call(bf16[2,176,128]{2,1,0:T(8,128)(2,1)S(1)} %collective-permute-done.19.refs_0_, f32[1152,128]{1,0:T(8,128)} %get-tuple-element.71.refs_1_, ...), custom_call_target="tpu_custom_call", output_to_operand_aliasing={{0}: (1, {}), {1}: (2, {}), {2}: (3, {}), {3}: (4, {})} | custom-call | bytes 270336 | tf_op jit(solution)/shard_map/pallas_call | solution.py:498
  (55 shorter events, 3.1 us)
Async XLA Ops:
  0.6 8.9 %collective-permute-start.3 = (bf16[16,64,128]{2,1,0:T(8,128)(2,1)}, bf16[16,64,128]{2,1,0:T(8,128)(2,1)S(1)}, u32[]{:S(2)}, u32[]{:S(2)}) collective-permute-start(bf16[16,64,128]{2,1,0:T(8,128)(2,1)} %bitcast.10), channel_id=1, source_target_pairs={{4,0},{0,4},{5,1},{1,5},{6,2},{2,6},{7,3},{3,7},{12,8},{8,12},{13,... | collective-permute-start | bytes 786440 | tf_op jit(solution)/shard_map/ppermute | solution.py:73
  2.7 5.4 %copy-start = (bf16[1,1,16,64,128]{4,3,2,1,0:T(8,128)(2,1)S(1)}, bf16[1,1,16,64,128]{4,3,2,1,0:T(8,128)(2,1)}, u32[]{:S(2)}) copy-start(bf16[1,1,16,64,128]{4,3,2,1,0:T(8,128)(2,1)} %param.9) | copy-start | bytes 786436
  2.7 5.4 %copy-start.1 = (bf16[3,3,128,128]{3,2,1,0:T(8,128)(2,1)S(1)}, bf16[3,3,128,128]{3,2,1,0:T(8,128)(2,1)}, u32[]{:S(2)}) copy-start(bf16[3,3,128,128]{3,2,1,0:T(8,128)(2,1)} %refs_8_.1) | copy-start | bytes 884740
  2.7 5.4 %copy-start.2 = (bf16[1,1,16,64,128]{4,3,2,1,0:T(8,128)(2,1)S(1)}, bf16[1,1,16,64,128]{4,3,2,1,0:T(8,128)(2,1)}, u32[]{:S(2)}) copy-start(bf16[1,1,16,64,128]{4,3,2,1,0:T(8,128)(2,1)} %param.13) | copy-start | bytes 786436
  2.7 5.4 %copy-start.6 = (bf16[3,128,128]{2,1,0:T(8,128)(2,1)S(1)}, bf16[3,128,128]{2,1,0:T(8,128)(2,1)}, u32[]{:S(2)}) copy-start(bf16[3,128,128]{2,1,0:T(8,128)(2,1)} %refs_7_.1) | copy-start | bytes 294916
  4.4 2.1 %collective-permute-start = (bf16[4,64,128]{2,1,0:T(8,128)(2,1)}, bf16[4,64,128]{2,1,0:T(8,128)(2,1)S(1)}, u32[]{:S(2)}, u32[]{:S(2)}) collective-permute-start(bf16[4,64,128]{2,1,0:T(8,128)(2,1)} %get-tuple-element.43), channel_id=1, source_target_pairs={{8,0},{0,8},{24,16},{16,24},{9,1},{1,9},{25,17},{17,25},{10,2},{2,... | collective-permute-start | bytes 196616 | tf_op jit(solution)/shard_map/ppermute | solution.py:73
  6.5 3.0 %copy-start.5 = (bf16[1,1,16,64,128]{4,3,2,1,0:T(8,128)(2,1)S(1)}, bf16[1,1,16,64,128]{4,3,2,1,0:T(8,128)(2,1)}, u32[]{:S(2)}) copy-start(bf16[1,1,16,64,128]{4,3,2,1,0:T(8,128)(2,1)} %param.12) | copy-start | bytes 786436
  6.5 3.0 %copy-start.7 = (bf16[3,128,128]{2,1,0:T(8,128)(2,1)S(1)}, bf16[3,128,128]{2,1,0:T(8,128)(2,1)}, u32[]{:S(2)}) copy-start(bf16[3,128,128]{2,1,0:T(8,128)(2,1)} %refs_11_.1) | copy-start | bytes 294916
  6.5 1.7 %collective-permute-start.1 = (bf16[4,64,128]{2,1,0:T(8,128)(2,1)}, bf16[4,64,128]{2,1,0:T(8,128)(2,1)S(1)}, u32[]{:S(2)}, u32[]{:S(2)}) collective-permute-start(bf16[4,64,128]{2,1,0:T(8,128)(2,1)} %get-tuple-element.44), channel_id=1, source_target_pairs={{8,0},{0,8},{24,16},{16,24},{9,1},{1,9},{25,17},{17,25},{10,2},{2,... | collective-permute-start | bytes 196616 | tf_op jit(solution)/shard_map/ppermute | solution.py:73
  6.9 3.6 %collective-permute-start.2 = (bf16[4,64,128]{2,1,0:T(8,128)(2,1)S(1)}, bf16[4,64,128]{2,1,0:T(8,128)(2,1)S(1)}, u32[]{:S(2)}, u32[]{:S(2)}) collective-permute-start(bf16[4,64,128]{2,1,0:T(8,128)(2,1)S(1)} %collective-permute-done.refs_5_), channel_id=1, source_target_pairs={{16,0},{24,8},{0,16},{8,24},{17,1},{25,9},{1,17},{9,25},{18,2},{26... | collective-permute-start | bytes 196616 | tf_op jit(solution)/shard_map/ppermute | solution.py:73
  8.2 6.9 %collective-permute-start.4 = (bf16[14,64,128]{2,1,0:T(8,128)(2,1)S(1)}, bf16[14,64,128]{2,1,0:T(8,128)(2,1)S(1)}, u32[]{:S(2)}, u32[]{:S(2)}) collective-permute-start(bf16[14,64,128]{2,1,0:T(8,128)(2,1)S(1)} %get-tuple-element.45.refs_5_), channel_id=1, source_target_pairs={{4,0},{0,4},{5,1},{1,5},{6,2},{2,6},{7,3},{3,7},{12,8},{8,12},{13,... | collective-permute-start | bytes 688136 | tf_op jit(solution)/shard_map/ppermute | solution.py:73
  11.5 2.1 %collective-permute-start.6 = (bf16[352,128]{1,0:T(8,128)(2,1)S(1)}, bf16[352,128]{1,0:T(8,128)(2,1)S(1)}, u32[]{:S(2)}, u32[]{:S(2)}) collective-permute-start(bf16[352,128]{1,0:T(8,128)(2,1)S(1)} %get-tuple-element.52), channel_id=1, source_target_pairs={{8,0},{0,8},{24,16},{16,24},{9,1},{1,9},{25,17},{17,25},{10,2},{2,... | collective-permute-start | bytes 270344 | tf_op jit(solution)/shard_map/ppermute | solution.py:73
  12.3 1.3 %collective-permute-start.7 = (bf16[352,128]{1,0:T(8,128)(2,1)S(1)}, bf16[352,128]{1,0:T(8,128)(2,1)S(1)}, u32[]{:S(2)}, u32[]{:S(2)}) collective-permute-start(bf16[352,128]{1,0:T(8,128)(2,1)S(1)} %get-tuple-element.53), channel_id=1, source_target_pairs={{8,0},{0,8},{24,16},{16,24},{9,1},{1,9},{25,17},{17,25},{10,2},{2,... | collective-permute-start | bytes 270344 | tf_op jit(solution)/shard_map/ppermute | solution.py:73
  12.4 4.2 %collective-permute-start.5 = (bf16[4,64,128]{2,1,0:T(8,128)(2,1)S(1)}, bf16[4,64,128]{2,1,0:T(8,128)(2,1)S(1)}, u32[]{:S(2)}, u32[]{:S(2)}) collective-permute-start(bf16[4,64,128]{2,1,0:T(8,128)(2,1)S(1)} %shard_map.131.refs_7_), channel_id=1, source_target_pairs={{4,0},{0,4},{5,1},{1,5},{6,2},{2,6},{7,3},{3,7},{12,8},{8,12},{13,... | collective-permute-start | bytes 196616 | tf_op jit(solution)/shard_map/ppermute | solution.py:73
  13.7 4.2 %collective-permute-start.8 = (bf16[352,128]{1,0:T(8,128)(2,1)S(1)}, bf16[352,128]{1,0:T(8,128)(2,1)S(1)}, u32[]{:S(2)}, u32[]{:S(2)}) collective-permute-start(bf16[352,128]{1,0:T(8,128)(2,1)S(1)} %get-tuple-element.58), channel_id=1, source_target_pairs={{16,0},{24,8},{0,16},{8,24},{17,1},{25,9},{1,17},{9,25},{18,2},{26... | collective-permute-start | bytes 270344 | tf_op jit(solution)/shard_map/ppermute | solution.py:73
  17.9 2.5 %collective-permute-start.9 = (bf16[832,128]{1,0:T(8,128)(2,1)S(1)}, bf16[832,128]{1,0:T(8,128)(2,1)S(1)}, u32[]{:S(2)}, u32[]{:S(2)}) collective-permute-start(bf16[832,128]{1,0:T(8,128)(2,1)S(1)} %get-tuple-element.59), channel_id=1, source_target_pairs={{8,0},{0,8},{24,16},{16,24},{9,1},{1,9},{25,17},{17,25},{10,2},{2,... | collective-permute-start | bytes 638984 | tf_op jit(solution)/shard_map/ppermute | solution.py:73
  19.1 4.1 %collective-permute-start.13 = (bf16[304,128]{1,0:T(8,128)(2,1)S(1)}, bf16[304,128]{1,0:T(8,128)(2,1)S(1)}, u32[]{:S(2)}, u32[]{:S(2)}) collective-permute-start(bf16[304,128]{1,0:T(8,128)(2,1)S(1)} %get-tuple-element.61.refs_2_), channel_id=1, source_target_pairs={{4,0},{0,4},{5,1},{1,5},{6,2},{2,6},{7,3},{3,7},{12,8},{8,12},{13,... | collective-permute-start | bytes 233480 | tf_op jit(solution)/shard_map/ppermute | solution.py:73
  20.5 6.2 %collective-permute-start.12 = (bf16[256,128]{1,0:T(8,128)(2,1)S(1)}, bf16[256,128]{1,0:T(8,128)(2,1)S(1)}, u32[]{:S(2)}, u32[]{:S(2)}) collective-permute-start(bf16[256,128]{1,0:T(8,128)(2,1)S(1)} %get-tuple-element.65), channel_id=1, source_target_pairs={{20,0},{16,4},{28,8},{24,12},{4,16},{0,20},{12,24},{8,28},{21,1},{... | collective-permute-start | bytes 196616 | tf_op jit(solution)/shard_map/ppermute | solution.py:81
  22.4 4.3 %collective-permute-start.10 = (bf16[240,128]{1,0:T(8,128)(2,1)S(1)}, bf16[240,128]{1,0:T(8,128)(2,1)S(1)}, u32[]{:S(2)}, u32[]{:S(2)}) collective-permute-start(bf16[240,128]{1,0:T(8,128)(2,1)S(1)} %get-tuple-element.62), channel_id=1, source_target_pairs={{16,0},{24,8},{0,16},{8,24},{17,1},{25,9},{1,17},{9,25},{18,2},{26... | collective-permute-start | bytes 184328 | tf_op jit(solution)/shard_map/ppermute | solution.py:73
  22.7 3.1 %collective-permute-start.11 = (bf16[176,128]{1,0:T(8,128)(2,1)S(1)}, bf16[176,128]{1,0:T(8,128)(2,1)S(1)}, u32[]{:S(2)}, u32[]{:S(2)}) collective-permute-start(bf16[176,128]{1,0:T(8,128)(2,1)S(1)} %get-tuple-element.64), channel_id=1, source_target_pairs={{4,0},{0,4},{5,1},{1,5},{6,2},{2,6},{7,3},{3,7},{12,8},{8,12},{13,... | collective-permute-start | bytes 135176 | tf_op jit(solution)/shard_map/ppermute | solution.py:73
  23.2 8.9 %copy-start.8 = (bf16[3,3,128,128]{3,2,1,0:T(8,128)(2,1)S(1)}, bf16[3,3,128,128]{3,2,1,0:T(8,128)(2,1)}, u32[]{:S(2)}) copy-start(bf16[3,3,128,128]{3,2,1,0:T(8,128)(2,1)} %refs_4_.5) | copy-start | bytes 884740
  23.2 4.9 %collective-permute-start.15 = (bf16[176,128]{1,0:T(8,128)(2,1)S(1)}, bf16[176,128]{1,0:T(8,128)(2,1)S(1)}, u32[]{:S(2)}, u32[]{:S(2)}) collective-permute-start(bf16[176,128]{1,0:T(8,128)(2,1)S(1)} %shard_map.140.refs_0_), channel_id=1, source_target_pairs={{1,0},{0,1},{3,2},{2,3},{5,4},{4,5},{7,6},{6,7},{9,8},{8,9},{11,10... | collective-permute-start | bytes 135176 | tf_op jit(solution)/shard_map/ppermute | solution.py:73
  26.7 3.8 %collective-permute-start.14 = (bf16[176,128]{1,0:T(8,128)(2,1)S(1)}, bf16[176,128]{1,0:T(8,128)(2,1)S(1)}, u32[]{:S(2)}, u32[]{:S(2)}) collective-permute-start(bf16[176,128]{1,0:T(8,128)(2,1)S(1)} %shard_map.139.refs_0_), channel_id=1, source_target_pairs={{1,0},{0,1},{3,2},{2,3},{5,4},{4,5},{7,6},{6,7},{9,8},{8,9},{11,10... | collective-permute-start | bytes 135176 | tf_op jit(solution)/shard_map/ppermute | solution.py:73
  28.1 5.5 %collective-permute-start.17 = (bf16[176,128]{1,0:T(8,128)(2,1)S(1)}, bf16[176,128]{1,0:T(8,128)(2,1)S(1)}, u32[]{:S(2)}, u32[]{:S(2)}) collective-permute-start(bf16[176,128]{1,0:T(8,128)(2,1)S(1)} %shard_map.143.refs_2_), channel_id=1, source_target_pairs={{2,0},{3,1},{0,2},{1,3},{6,4},{7,5},{4,6},{5,7},{10,8},{11,9},{8,1... | collective-permute-start | bytes 135176 | tf_op jit(solution)/shard_map/ppermute | solution.py:73
  30.5 4.8 %collective-permute-start.16 = (bf16[176,128]{1,0:T(8,128)(2,1)S(1)}, bf16[176,128]{1,0:T(8,128)(2,1)S(1)}, u32[]{:S(2)}, u32[]{:S(2)}) collective-permute-start(bf16[176,128]{1,0:T(8,128)(2,1)S(1)} %shard_map.141.refs_5_.refs_0_), channel_id=1, source_target_pairs={{2,0},{3,1},{0,2},{1,3},{6,4},{7,5},{4,6},{5,7},{10,8},{11,9},{8,1... | collective-permute-start | bytes 135176 | tf_op jit(solution)/shard_map/ppermute | solution.py:73
  35.3 5.4 %collective-permute-start.20 = (bf16[2,176,128]{2,1,0:T(8,128)(2,1)S(1)}, bf16[2,176,128]{2,1,0:T(8,128)(2,1)S(1)}, u32[]{:S(2)}, u32[]{:S(2)}) collective-permute-start(bf16[2,176,128]{2,1,0:T(8,128)(2,1)S(1)} %shard_map.144.refs_0_), channel_id=1, source_target_pairs={{4,0},{0,4},{5,1},{1,5},{6,2},{2,6},{7,3},{3,7},{12,8},{8,12},{13,... | collective-permute-start | bytes 270344 | tf_op jit(solution)/shard_map/ppermute | solution.py:73
  36.1 6.2 %collective-permute-start.21 = (bf16[2,176,128]{2,1,0:T(8,128)(2,1)S(1)}, bf16[2,176,128]{2,1,0:T(8,128)(2,1)S(1)}, u32[]{:S(2)}, u32[]{:S(2)}) collective-permute-start(bf16[2,176,128]{2,1,0:T(8,128)(2,1)S(1)} %shard_map.144.refs_0_), channel_id=1, source_target_pairs={{16,0},{24,8},{0,16},{8,24},{17,1},{25,9},{1,17},{9,25},{18,2},{26... | collective-permute-start | bytes 270344 | tf_op jit(solution)/shard_map/ppermute | solution.py:73
  36.8 6.1 %collective-permute-start.18 = (bf16[2,176,128]{2,1,0:T(8,128)(2,1)S(1)}, bf16[2,176,128]{2,1,0:T(8,128)(2,1)S(1)}, u32[]{:S(2)}, u32[]{:S(2)}) collective-permute-start(bf16[2,176,128]{2,1,0:T(8,128)(2,1)S(1)} %shard_map.144.refs_0_), channel_id=1, source_target_pairs={{20,0},{16,4},{28,8},{24,12},{4,16},{0,20},{12,24},{8,28},{21,1},{... | collective-permute-start | bytes 270344 | tf_op jit(solution)/shard_map/ppermute | solution.py:81
  38.0 6.7 %collective-permute-start.22 = (bf16[2,176,128]{2,1,0:T(8,128)(2,1)S(1)}, bf16[2,176,128]{2,1,0:T(8,128)(2,1)S(1)}, u32[]{:S(2)}, u32[]{:S(2)}) collective-permute-start(bf16[2,176,128]{2,1,0:T(8,128)(2,1)S(1)} %shard_map.144.refs_0_), channel_id=1, source_target_pairs={{8,0},{0,8},{24,16},{16,24},{9,1},{1,9},{25,17},{17,25},{10,2},{2,... | collective-permute-start | bytes 270344 | tf_op jit(solution)/shard_map/ppermute | solution.py:73
  40.7 4.0 %collective-permute-start.23 = (bf16[2,176,128]{2,1,0:T(8,128)(2,1)S(1)}, bf16[2,176,128]{2,1,0:T(8,128)(2,1)S(1)}, u32[]{:S(2)}, u32[]{:S(2)}) collective-permute-start(bf16[2,176,128]{2,1,0:T(8,128)(2,1)S(1)} %collective-permute-done.20.refs_1_), channel_id=1, source_target_pairs={{8,0},{0,8},{24,16},{16,24},{9,1},{1,9},{25,17},{17,25},{10,2},{2,... | collective-permute-start | bytes 270344 | tf_op jit(solution)/shard_map/ppermute | solution.py:73
  42.3 2.4 %collective-permute-start.24 = (bf16[2,176,128]{2,1,0:T(8,128)(2,1)S(1)}, bf16[2,176,128]{2,1,0:T(8,128)(2,1)S(1)}, u32[]{:S(2)}, u32[]{:S(2)}) collective-permute-start(bf16[2,176,128]{2,1,0:T(8,128)(2,1)S(1)} %collective-permute-done.21.refs_2_), channel_id=1, source_target_pairs={{8,0},{0,8},{24,16},{16,24},{9,1},{1,9},{25,17},{17,25},{10,2},{2,... | collective-permute-start | bytes 270344 | tf_op jit(solution)/shard_map/ppermute | solution.py:73
  42.9 3.2 %collective-permute-start.19 = (bf16[2,176,128]{2,1,0:T(8,128)(2,1)S(1)}, bf16[2,176,128]{2,1,0:T(8,128)(2,1)S(1)}, u32[]{:S(2)}, u32[]{:S(2)}) collective-permute-start(bf16[2,176,128]{2,1,0:T(8,128)(2,1)S(1)} %collective-permute-done.18.refs_6_), channel_id=1, source_target_pairs={{8,0},{0,8},{24,16},{16,24},{9,1},{1,9},{25,17},{17,25},{10,2},{2,... | collective-permute-start | bytes 270344 | tf_op jit(solution)/shard_map/ppermute | solution.py:73
  (2 other events, 6.1 us)

commit v20 on v17

--- a/solution.py
+++ b/solution.py
@@ -424,17 +424,20 @@
 
 
 def scaled_kernel(factor, *refs):
-    out_ref = refs[-1]
+    out_ref, long_ref = refs[-2:]
+    height = out_ref.shape[1]
     for block in range(2):
         one, two = (ref[...].astype(jnp.float32) for ref in refs[2 * block : 2 * block + 2])
-        out_ref[block] = ((one + two) * factor).astype(jnp.bfloat16)
+        total = ((one + two) * factor).astype(jnp.bfloat16)
+        out_ref[block] = total
+        long_ref[block, :height] = total
 
 
 def place_kernel(places, *refs):
     shares, outs = refs[: len(places)], refs[-6:-2]
     sums_ref, sems = refs[-2:]
     band, frame = lax.axis_index("section"), lax.axis_index("video")
-    height = shares[0].shape[1]
+    height = sums_ref.shape[2]
 
     def copies(n, block):
         flip, other = places[n]
@@ -450,7 +453,7 @@
 
     for n, share in enumerate(shares):
         for block in range(2):
-            sums_ref[n, block] = share[block].astype(jnp.float32)
+            sums_ref[n, block] = share[block, :height].astype(jnp.float32)
             for inside, copy in copies(n, block):
                 pl.when(inside)(lambda: copy().start())
     for n in range(len(shares)):
@@ -460,7 +463,8 @@
 
 
 def placed(shares, places, given=()):
-    _, height, ch = shares[0].shape
+    ch = shares[0].shape[2]
+    height = 3 * ch if places[0][1] is None else 3 * ch // 2
     count = len(shares)
     outs = (f32(3, 3 * ch, ch), f32(3 * ch, ch)) * 2
     vmem, spare = (pl.BlockSpec(memory_space=space) for space in (pltpu.VMEM, pl.ANY))
@@ -703,9 +707,9 @@
         last_two = flipped(sum_two, "dp", 2)
         last_one = flipped(later_than(sum_one, sum_two), "dp", 2)
         grad_in, token = input_gradient(across, (sum_one,))
-        own = call(
+        own, longer = call(
             functools.partial(scaled_kernel, factor),
-            [bf16(2, half, ch)],
+            [bf16(2, half, ch), bf16(2, half + 16, ch)],
             [],
             height * ch,
             sum_one,
@@ -714,12 +718,12 @@
             last_two,
             after=(token,),
         )
-        frame, across, both = flipped(own, "video", 1), flipped(own, "section", 2), flipped_both(own)
-        shares = [own, frame, across]
+        shares = [own, flipped_both(longer), flipped(own, "video", 1)]
         shares += [flipped(share, "section", 1) for share in shares]
-        places = [(0, False), (0, True), (2, False), (1, False), (1, True), (3, False)]
-        sums = placed([*shares, both], [*places, (2, True)])
-        sums = unpacked(placed([flipped(both, "section", 1)], [(3, True)], sums))
+        across = flipped(own, "section", 2)
+        places = [(0, False), (2, True), (0, True), (1, False), (3, True), (1, True)]
+        sums = placed([*shares, across], [*places, (2, False)])
+        sums = unpacked(placed([flipped(across, "section", 1)], [(3, False)], sums))
     else:
         own_one, send_one = call(
             pair_kernel,

time: 47.1 us -> 47.3 us (level)
  starting transfers between devices: 30.4 us -> 28.5 us
  waiting for transfers between devices: 6.33 us -> 8.19 us
    ppermute x2, waiting for transfers between devices: 0.01 us -> 1.81 us  [flipped_both(): return lax.ppermute(block, ('section', 'video'), pairs)]
    ppermute x23, starting transfers between devices: 27.2 us -> 25.5 us  [flipped(): lax.ppermute(block, axis, [(place ^ flip, place) for place in range(count)])]
  transfers between devices with their start and end apart: 25 -> 25, of which waited for: 6 -> 8; matrix products, arithmetic and copies ran while one was open for 0% -> 0% of each run, Pallas kernels for 18% -> 18%
where the time goes in v20:
time: 47.3 us; the launch traced here: 46.8 us
  starting transfers between devices  28.5 us (60%)
  Pallas kernels  9.26 us (20%)
  waiting for transfers between devices  8.19 us (17%)
  between operations  0.83 us (2%)
    ppermute x23, starting transfers between devices, flipped(): lax.ppermute(block, axis, [(place ^ flip, place) for place in range(count)])  25.5 us
    pallas_call x17, Pallas kernels, call(): pl.pallas_call(body, out_shape=outs[0] if single else tuple(outs), in_spe...  7.36 us
    ppermute x23, waiting for transfers between devices, flipped(): lax.ppermute(block, axis, [(place ^ flip, place) for place in range(count)])  6.38 us
    ppermute x2, starting transfers between devices, flipped_both(): return lax.ppermute(block, ('section', 'video'), pairs)  3 us
    pallas_call x2, Pallas kernels, placed(): pl.pallas_call(functools.partial(place_kernel, places), out_shape=outs, i...  1.9 us
    ppermute x2, waiting for transfers between devices, flipped_both(): return lax.ppermute(block, ('section', 'video'), pairs)  1.81 us
  transfers between devices with their start and end apart: 25, of which 8 were waited for; matrix products, arithmetic and copies ran while one was open for 0% of the time, Pallas kernels for 18%

profile of v20, /device:TPU:1, one launch (start us, length us, event | category | flops | bytes accessed | tf_op | source)
XLA Modules:
  0.0 46.8 jit_solution(13719543157064302888)
XLA Ops:
  0.6 2.1 %collective-permute-start.3 = (bf16[16,64,128]{2,1,0:T(8,128)(2,1)}, bf16[16,64,128]{2,1,0:T(8,128)(2,1)S(1)}, u32[]{:S(2)}, u32[]{:S(2)}) collective-permute-start(bf16[16,64,128]{2,1,0:T(8,128)(2,1)} %bitcast.10), channel_id=1, source_target_pairs={{4,0},{0,4},{5,1},{1,5},{6,2},{2,6},{7,3},{3,7},{12,8},{8,12},{13,... | collective-permute-start | bytes 786440 | tf_op jit(solution)/shard_map/ppermute | solution.py:73
  2.7 1.6 %shard_map.128 = (bf16[4,64,128]{2,1,0:T(8,128)(2,1)}, bf16[4,64,128]{2,1,0:T(8,128)(2,1)}) custom-call(bf16[16,64,128]{2,1,0:T(8,128)(2,1)} %bitcast.11, bf16[16,64,128]{2,1,0:T(8,128)(2,1)} %bitcast.17, bf16[16,64,128]{2,1,0:T(8,128)(2,1)} %bitcast.28, bf16[16,64,128]{2,1,0:T(8,128)(2,1)} %bitcast.25), custom_call_target="tpu_custom_call" | custom-call | flops 1 | bytes 1179648 | tf_op jit(solution)/shard_map/pallas_call | solution.py:38
  4.4 1.0 %collective-permute-start = (bf16[4,64,128]{2,1,0:T(8,128)(2,1)}, bf16[4,64,128]{2,1,0:T(8,128)(2,1)S(1)}, u32[]{:S(2)}, u32[]{:S(2)}) collective-permute-start(bf16[4,64,128]{2,1,0:T(8,128)(2,1)} %get-tuple-element.45), channel_id=1, source_target_pairs={{8,0},{0,8},{24,16},{16,24},{9,1},{1,9},{25,17},{17,25},{10,2},{2,... | collective-permute-start | bytes 196616 | tf_op jit(solution)/shard_map/ppermute | solution.py:73
  5.4 1.1 %collective-permute-done.refs_5_ = bf16[4,64,128]{2,1,0:T(8,128)(2,1)S(1)} collective-permute-done((bf16[4,64,128]{2,1,0:T(8,128)(2,1)}, bf16[4,64,128]{2,1,0:T(8,128)(2,1)S(1)}, u32[]{:S(2)}, u32[]{:S(2)}) %collective-permute-start) | collective-permute-done | bytes 65568 | tf_op jit(solution)/shard_map/ppermute | solution.py:73
  6.9 1.2 %collective-permute-start.2 = (bf16[4,64,128]{2,1,0:T(8,128)(2,1)S(1)}, bf16[4,64,128]{2,1,0:T(8,128)(2,1)S(1)}, u32[]{:S(2)}, u32[]{:S(2)}) collective-permute-start(bf16[4,64,128]{2,1,0:T(8,128)(2,1)S(1)} %collective-permute-done.refs_5_), channel_id=1, source_target_pairs={{16,0},{24,8},{0,16},{8,24},{17,1},{25,9},{1,17},{9,25},{18,2},{26... | collective-permute-start | bytes 196616 | tf_op jit(solution)/shard_map/ppermute | solution.py:73
  8.2 1.3 %collective-permute-start.4 = (bf16[14,64,128]{2,1,0:T(8,128)(2,1)S(1)}, bf16[14,64,128]{2,1,0:T(8,128)(2,1)S(1)}, u32[]{:S(2)}, u32[]{:S(2)}) collective-permute-start(bf16[14,64,128]{2,1,0:T(8,128)(2,1)S(1)} %get-tuple-element.47.refs_5_), channel_id=1, source_target_pairs={{4,0},{0,4},{5,1},{1,5},{6,2},{2,6},{7,3},{3,7},{12,8},{8,12},{13,... | collective-permute-start | bytes 688136 | tf_op jit(solution)/shard_map/ppermute | solution.py:73
  9.6 1.0 %shard_map.130 = (bf16[14,64,128]{2,1,0:T(8,128)(2,1)S(1)}, bf16[16,64,128]{2,1,0:T(8,128)(2,1)S(1)}) custom-call(bf16[16,64,128]{2,1,0:T(8,128)(2,1)S(1)} %bitcast.13, bf16[16,64,128]{2,1,0:T(8,128)(2,1)S(1)} %bitcast.19, bf16[16,64,128]{2,1,0:T(8,128)(2,1)S(1)} %collective-permute-done.3.refs_2_.refs_6_, bf16[3,128,128]{2,1,0:T(8,128)(2,1)S(1)} %copy-done.6, ...), custom_call_target="tpu_custom_call" | custom-call | tf_op jit(solution)/shard_map/pallas_call | solution.py:38
  10.6 0.9 %shard_map.132 = (f32[2,384,128]{2,1,0:T(8,128)S(1)}, bf16[384,128]{1,0:T(8,128)(2,1)S(1)}, bf16[384,128]{1,0:T(8,128)(2,1)S(1)}) custom-call(bf16[16,64,128]{2,1,0:T(8,128)(2,1)S(1)} %bitcast.30, bf16[16,64,128]{2,1,0:T(8,128)(2,1)S(1)} %bitcast.20, bf16[16,64,128]{2,1,0:T(8,128)(2,1)S(1)} %get-tuple-element.50.refs_6_.refs_2_.refs_4_, ...), custom_call_target="tpu_custom_call" | custom-call | flops 2415919104 | bytes 2031616 | tf_op jit(solution)/shard_map/pallas_call | solution.py:38
  11.5 0.9 %collective-permute-start.6 = (bf16[384,128]{1,0:T(8,128)(2,1)S(1)}, bf16[384,128]{1,0:T(8,128)(2,1)S(1)}, u32[]{:S(2)}, u32[]{:S(2)}) collective-permute-start(bf16[384,128]{1,0:T(8,128)(2,1)S(1)} %get-tuple-element.54), channel_id=1, source_target_pairs={{8,0},{0,8},{24,16},{16,24},{9,1},{1,9},{25,17},{17,25},{10,2},{2,... | collective-permute-start | bytes 294920 | tf_op jit(solution)/shard_map/ppermute | solution.py:73
  12.4 0.8 %collective-permute-start.5 = (bf16[4,64,128]{2,1,0:T(8,128)(2,1)S(1)}, bf16[4,64,128]{2,1,0:T(8,128)(2,1)S(1)}, u32[]{:S(2)}, u32[]{:S(2)}) collective-permute-start(bf16[4,64,128]{2,1,0:T(8,128)(2,1)S(1)} %shard_map.131.refs_7_), channel_id=1, source_target_pairs={{4,0},{0,4},{5,1},{1,5},{6,2},{2,6},{7,3},{3,7},{12,8},{8,12},{13,... | collective-permute-start | bytes 196616 | tf_op jit(solution)/shard_map/ppermute | solution.py:73
  13.7 1.4 %collective-permute-start.8 = (bf16[384,128]{1,0:T(8,128)(2,1)S(1)}, bf16[384,128]{1,0:T(8,128)(2,1)S(1)}, u32[]{:S(2)}, u32[]{:S(2)}) collective-permute-start(bf16[384,128]{1,0:T(8,128)(2,1)S(1)} %get-tuple-element.60), channel_id=1, source_target_pairs={{16,0},{24,8},{0,16},{8,24},{17,1},{25,9},{1,17},{9,25},{18,2},{26... | collective-permute-start | bytes 294920 | tf_op jit(solution)/shard_map/ppermute | solution.py:73
  15.6 1.0 %collective-permute-done.5.refs_6_ = bf16[4,64,128]{2,1,0:T(8,128)(2,1)S(1)} collective-permute-done((bf16[4,64,128]{2,1,0:T(8,128)(2,1)S(1)}, bf16[4,64,128]{2,1,0:T(8,128)(2,1)S(1)}, u32[]{:S(2)}, u32[]{:S(2)}) %collective-permute-start.5) | collective-permute-done | bytes 65568 | tf_op jit(solution)/shard_map/ppermute | solution.py:73
  16.6 1.3 %shard_map.136 = (bf16[16,64,128]{2,1,0:T(8,128)(2,1)S(1)}, bf16[16,64,128]{2,1,0:T(8,128)(2,1)S(1)}, f32[2,384,128]{2,1,0:T(8,128)S(1)}, bf16[896,128]{1,0:T(8,128)(2,1)S(1)}) custom-call(bf16[16,64,128]{2,1,0:T(8,128)(2,1)S(1)} %bitcast.16, bf16[4,64,128]{2,1,0:T(8,128)(2,1)S(1)} %collective-permute-done.1.refs_4_.refs_1_.refs_3_.refs_2_, ...), custom_call_target="tpu_custom_call" | custom-call | flops 2415919104 | bytes 5046272 | tf_op jit(solution)/shard_map/pallas_call | solution.py:38
  17.9 1.2 %collective-permute-start.9 = (bf16[896,128]{1,0:T(8,128)(2,1)S(1)}, bf16[896,128]{1,0:T(8,128)(2,1)S(1)}, u32[]{:S(2)}, u32[]{:S(2)}) collective-permute-start(bf16[896,128]{1,0:T(8,128)(2,1)S(1)} %get-tuple-element.61), channel_id=1, source_target_pairs={{8,0},{0,8},{24,16},{16,24},{9,1},{1,9},{25,17},{17,25},{10,2},{2,... | collective-permute-start | bytes 688136 | tf_op jit(solution)/shard_map/ppermute | solution.py:73
  19.1 1.3 %collective-permute-start.13 = (bf16[320,128]{1,0:T(8,128)(2,1)S(1)}, bf16[320,128]{1,0:T(8,128)(2,1)S(1)}, u32[]{:S(2)}, u32[]{:S(2)}) collective-permute-start(bf16[320,128]{1,0:T(8,128)(2,1)S(1)} %get-tuple-element.63.refs_2_), channel_id=1, source_target_pairs={{4,0},{0,4},{5,1},{1,5},{6,2},{2,6},{7,3},{3,7},{12,8},{8,12},{13,... | collective-permute-start | bytes 245768 | tf_op jit(solution)/shard_map/ppermute | solution.py:73
  20.5 1.9 %collective-permute-start.12 = (bf16[272,128]{1,0:T(8,128)(2,1)S(1)}, bf16[272,128]{1,0:T(8,128)(2,1)S(1)}, u32[]{:S(2)}, u32[]{:S(2)}) collective-permute-start(bf16[272,128]{1,0:T(8,128)(2,1)S(1)} %get-tuple-element.67), channel_id=1, source_target_pairs={{20,0},{16,4},{28,8},{24,12},{4,16},{0,20},{12,24},{8,28},{21,1},{... | collective-permute-start | bytes 208904 | tf_op jit(solution)/shard_map/ppermute | solution.py:81
  23.3 1.4 %collective-permute-start.15 = (bf16[192,128]{1,0:T(8,128)(2,1)S(1)}, bf16[192,128]{1,0:T(8,128)(2,1)S(1)}, u32[]{:S(2)}, u32[]{:S(2)}) collective-permute-start(bf16[192,128]{1,0:T(8,128)(2,1)S(1)} %shard_map.140.refs_0_), channel_id=1, source_target_pairs={{1,0},{0,1},{3,2},{2,3},{5,4},{4,5},{7,6},{6,7},{9,8},{8,9},{11,10... | collective-permute-start | bytes 147464 | tf_op jit(solution)/shard_map/ppermute | solution.py:73
  24.6 1.5 %collective-permute-done.11.refs_2_ = bf16[192,128]{1,0:T(8,128)(2,1)S(1)} collective-permute-done((bf16[192,128]{1,0:T(8,128)(2,1)S(1)}, bf16[192,128]{1,0:T(8,128)(2,1)S(1)}, u32[]{:S(2)}, u32[]{:S(2)}) %collective-permute-start.11) | collective-permute-done | bytes 49184 | tf_op jit(solution)/shard_map/ppermute | solution.py:73
  26.1 1.3 %collective-permute-done.10.refs_1_.refs_3_ = bf16[256,128]{1,0:T(8,128)(2,1)S(1)} collective-permute-done((bf16[256,128]{1,0:T(8,128)(2,1)S(1)}, bf16[256,128]{1,0:T(8,128)(2,1)S(1)}, u32[]{:S(2)}, u32[]{:S(2)}) %collective-permute-start.10) | collective-permute-done | bytes 65568 | tf_op jit(solution)/shard_map/ppermute | solution.py:73
  27.4 1.3 %collective-permute-start.14 = (bf16[192,128]{1,0:T(8,128)(2,1)S(1)}, bf16[192,128]{1,0:T(8,128)(2,1)S(1)}, u32[]{:S(2)}, u32[]{:S(2)}) collective-permute-start(bf16[192,128]{1,0:T(8,128)(2,1)S(1)} %shard_map.139.refs_0_), channel_id=1, source_target_pairs={{1,0},{0,1},{3,2},{2,3},{5,4},{4,5},{7,6},{6,7},{9,8},{8,9},{11,10... | collective-permute-start | bytes 147464 | tf_op jit(solution)/shard_map/ppermute | solution.py:73
  28.8 2.4 %collective-permute-start.17 = (bf16[192,128]{1,0:T(8,128)(2,1)S(1)}, bf16[192,128]{1,0:T(8,128)(2,1)S(1)}, u32[]{:S(2)}, u32[]{:S(2)}) collective-permute-start(bf16[192,128]{1,0:T(8,128)(2,1)S(1)} %shard_map.143.refs_2_), channel_id=1, source_target_pairs={{2,0},{3,1},{0,2},{1,3},{6,4},{7,5},{4,6},{5,7},{10,8},{11,9},{8,1... | collective-permute-start | bytes 147464 | tf_op jit(solution)/shard_map/ppermute | solution.py:73
  31.2 1.6 %collective-permute-start.16 = (bf16[192,128]{1,0:T(8,128)(2,1)S(1)}, bf16[192,128]{1,0:T(8,128)(2,1)S(1)}, u32[]{:S(2)}, u32[]{:S(2)}) collective-permute-start(bf16[192,128]{1,0:T(8,128)(2,1)S(1)} %shard_map.141.refs_5_.refs_0_), channel_id=1, source_target_pairs={{2,0},{3,1},{0,2},{1,3},{6,4},{7,5},{4,6},{5,7},{10,8},{11,9},{8,1... | collective-permute-start | bytes 147464 | tf_op jit(solution)/shard_map/ppermute | solution.py:73
  32.8 1.5 %shard_map.142 = (bf16[16,64,128]{2,1,0:T(8,128)(2,1)}, f32[8,128]{1,0:T(8,128)S(1)}) custom-call(bf16[16,64,128]{2,1,0:T(8,128)(2,1)S(1)} %get-tuple-element.57.refs_0_, bf16[16,64,128]{2,1,0:T(8,128)(2,1)S(1)} %get-tuple-element.58.refs_1_, bf16[896,128]{1,0:T(8,128)(2,1)S(1)} %collective-permute-done.9.refs_1_.refs_2_, ...), custom_call_target="tpu_custom_call" | custom-call | flops 301989888 | bytes 1380352 | tf_op jit(solution)/shard_map/pallas_call | solution.py:38
  34.3 1.3 %collective-permute-done.16.refs_1_ = bf16[192,128]{1,0:T(8,128)(2,1)S(1)} collective-permute-done((bf16[192,128]{1,0:T(8,128)(2,1)S(1)}, bf16[192,128]{1,0:T(8,128)(2,1)S(1)}, u32[]{:S(2)}, u32[]{:S(2)}) %collective-permute-start.16) | collective-permute-done | bytes 49184 | tf_op jit(solution)/shard_map/ppermute | solution.py:73
  35.7 1.1 %collective-permute-start.20 = (bf16[2,208,128]{2,1,0:T(8,128)(2,1)S(1)}, bf16[2,208,128]{2,1,0:T(8,128)(2,1)S(1)}, u32[]{:S(2)}, u32[]{:S(2)}) collective-permute-start(bf16[2,208,128]{2,1,0:T(8,128)(2,1)S(1)} %get-tuple-element.74), channel_id=1, source_target_pairs={{20,0},{16,4},{28,8},{24,12},{4,16},{0,20},{12,24},{8,28},{21,1},{... | collective-permute-start | bytes 319496 | tf_op jit(solution)/shard_map/ppermute | solution.py:81
  36.8 1.1 %collective-permute-start.21 = (bf16[2,192,128]{2,1,0:T(8,128)(2,1)S(1)}, bf16[2,192,128]{2,1,0:T(8,128)(2,1)S(1)}, u32[]{:S(2)}, u32[]{:S(2)}) collective-permute-start(bf16[2,192,128]{2,1,0:T(8,128)(2,1)S(1)} %get-tuple-element.73.refs_0_), channel_id=1, source_target_pairs={{4,0},{0,4},{5,1},{1,5},{6,2},{2,6},{7,3},{3,7},{12,8},{8,12},{13,... | collective-permute-start | bytes 294920 | tf_op jit(solution)/shard_map/ppermute | solution.py:73
  38.4 1.8 %collective-permute-done.20.refs_1_ = bf16[2,208,128]{2,1,0:T(8,128)(2,1)S(1)} collective-permute-done((bf16[2,208,128]{2,1,0:T(8,128)(2,1)S(1)}, bf16[2,208,128]{2,1,0:T(8,128)(2,1)S(1)}, u32[]{:S(2)}, u32[]{:S(2)}) %collective-permute-start.20) | collective-permute-done | bytes 106528 | tf_op jit(solution)/shard_map/ppermute | solution.py:81
  40.2 2.9 %collective-permute-start.23 = (bf16[2,208,128]{2,1,0:T(8,128)(2,1)S(1)}, bf16[2,208,128]{2,1,0:T(8,128)(2,1)S(1)}, u32[]{:S(2)}, u32[]{:S(2)}) collective-permute-start(bf16[2,208,128]{2,1,0:T(8,128)(2,1)S(1)} %collective-permute-done.20.refs_1_), channel_id=1, source_target_pairs={{8,0},{0,8},{24,16},{16,24},{9,1},{1,9},{25,17},{17,25},{10,2},{2,... | collective-permute-start | bytes 319496 | tf_op jit(solution)/shard_map/ppermute | solution.py:73
  43.1 0.8 %collective-permute-start.24 = (bf16[2,192,128]{2,1,0:T(8,128)(2,1)S(1)}, bf16[2,192,128]{2,1,0:T(8,128)(2,1)S(1)}, u32[]{:S(2)}, u32[]{:S(2)}) collective-permute-start(bf16[2,192,128]{2,1,0:T(8,128)(2,1)S(1)} %collective-permute-done.21.refs_2_), channel_id=1, source_target_pairs={{8,0},{0,8},{24,16},{16,24},{9,1},{1,9},{25,17},{17,25},{10,2},{2,... | collective-permute-start | bytes 294920 | tf_op jit(solution)/shard_map/ppermute | solution.py:73
  43.9 0.9 %collective-permute-start.19 = (bf16[2,192,128]{2,1,0:T(8,128)(2,1)S(1)}, bf16[2,192,128]{2,1,0:T(8,128)(2,1)S(1)}, u32[]{:S(2)}, u32[]{:S(2)}) collective-permute-start(bf16[2,192,128]{2,1,0:T(8,128)(2,1)S(1)} %collective-permute-done.18.refs_6_), channel_id=1, source_target_pairs={{8,0},{0,8},{24,16},{16,24},{9,1},{1,9},{25,17},{17,25},{10,2},{2,... | collective-permute-start | bytes 294920 | tf_op jit(solution)/shard_map/ppermute | solution.py:73
  44.9 1.2 %shard_map.145 = (f32[3,384,128]{2,1,0:T(8,128)}, f32[384,128]{1,0:T(8,128)}, f32[3,384,128]{2,1,0:T(8,128)}, f32[384,128]{1,0:T(8,128)}) custom-call(bf16[2,192,128]{2,1,0:T(8,128)(2,1)S(1)} %get-tuple-element.73.refs_0_, bf16[2,208,128]{2,1,0:T(8,128)(2,1)S(1)} %collective-permute-done.20.refs_1_, ...), custom_call_target="tpu_custom_call" | custom-call | bytes 2064384 | tf_op jit(solution)/shard_map/pallas_call | solution.py:471
  46.1 0.7 %shard_map.146 = (f32[3,384,128]{2,1,0:T(8,128)}, f32[384,128]{1,0:T(8,128)}, f32[3,384,128]{2,1,0:T(8,128)}, f32[384,128]{1,0:T(8,128)}) custom-call(bf16[2,192,128]{2,1,0:T(8,128)(2,1)S(1)} %collective-permute-done.19.refs_0_, f32[3,384,128]{2,1,0:T(8,128)} %get-tuple-element.75.refs_1_, ...), custom_call_target="tpu_custom_call", output_to_operand_aliasing={{0}: (1, {}), {1}: (2, {}), {2}: (3, {}), {3}: (4, {})} | custom-call | bytes 294912 | tf_op jit(solution)/shard_map/pallas_call | solution.py:471
  (55 shorter events, 3.2 us)
Async XLA Ops:
  0.6 8.9 %collective-permute-start.3 = (bf16[16,64,128]{2,1,0:T(8,128)(2,1)}, bf16[16,64,128]{2,1,0:T(8,128)(2,1)S(1)}, u32[]{:S(2)}, u32[]{:S(2)}) collective-permute-start(bf16[16,64,128]{2,1,0:T(8,128)(2,1)} %bitcast.10), channel_id=1, source_target_pairs={{4,0},{0,4},{5,1},{1,5},{6,2},{2,6},{7,3},{3,7},{12,8},{8,12},{13,... | collective-permute-start | bytes 786440 | tf_op jit(solution)/shard_map/ppermute | solution.py:73
  2.7 5.4 %copy-start = (bf16[1,1,16,64,128]{4,3,2,1,0:T(8,128)(2,1)S(1)}, bf16[1,1,16,64,128]{4,3,2,1,0:T(8,128)(2,1)}, u32[]{:S(2)}) copy-start(bf16[1,1,16,64,128]{4,3,2,1,0:T(8,128)(2,1)} %param.9) | copy-start | bytes 786436
  2.7 5.4 %copy-start.1 = (bf16[3,3,128,128]{3,2,1,0:T(8,128)(2,1)S(1)}, bf16[3,3,128,128]{3,2,1,0:T(8,128)(2,1)}, u32[]{:S(2)}) copy-start(bf16[3,3,128,128]{3,2,1,0:T(8,128)(2,1)} %refs_8_.1) | copy-start | bytes 884740
  2.7 5.4 %copy-start.2 = (bf16[1,1,16,64,128]{4,3,2,1,0:T(8,128)(2,1)S(1)}, bf16[1,1,16,64,128]{4,3,2,1,0:T(8,128)(2,1)}, u32[]{:S(2)}) copy-start(bf16[1,1,16,64,128]{4,3,2,1,0:T(8,128)(2,1)} %param.13) | copy-start | bytes 786436
  2.7 5.4 %copy-start.6 = (bf16[3,128,128]{2,1,0:T(8,128)(2,1)S(1)}, bf16[3,128,128]{2,1,0:T(8,128)(2,1)}, u32[]{:S(2)}) copy-start(bf16[3,128,128]{2,1,0:T(8,128)(2,1)} %refs_7_.1) | copy-start | bytes 294916
  4.4 2.1 %collective-permute-start = (bf16[4,64,128]{2,1,0:T(8,128)(2,1)}, bf16[4,64,128]{2,1,0:T(8,128)(2,1)S(1)}, u32[]{:S(2)}, u32[]{:S(2)}) collective-permute-start(bf16[4,64,128]{2,1,0:T(8,128)(2,1)} %get-tuple-element.45), channel_id=1, source_target_pairs={{8,0},{0,8},{24,16},{16,24},{9,1},{1,9},{25,17},{17,25},{10,2},{2,... | collective-permute-start | bytes 196616 | tf_op jit(solution)/shard_map/ppermute | solution.py:73
  6.5 3.0 %copy-start.5 = (bf16[1,1,16,64,128]{4,3,2,1,0:T(8,128)(2,1)S(1)}, bf16[1,1,16,64,128]{4,3,2,1,0:T(8,128)(2,1)}, u32[]{:S(2)}) copy-start(bf16[1,1,16,64,128]{4,3,2,1,0:T(8,128)(2,1)} %param.12) | copy-start | bytes 786436
  6.5 3.0 %copy-start.7 = (bf16[3,128,128]{2,1,0:T(8,128)(2,1)S(1)}, bf16[3,128,128]{2,1,0:T(8,128)(2,1)}, u32[]{:S(2)}) copy-start(bf16[3,128,128]{2,1,0:T(8,128)(2,1)} %refs_11_.1) | copy-start | bytes 294916
  6.5 1.7 %collective-permute-start.1 = (bf16[4,64,128]{2,1,0:T(8,128)(2,1)}, bf16[4,64,128]{2,1,0:T(8,128)(2,1)S(1)}, u32[]{:S(2)}, u32[]{:S(2)}) collective-permute-start(bf16[4,64,128]{2,1,0:T(8,128)(2,1)} %get-tuple-element.46), channel_id=1, source_target_pairs={{8,0},{0,8},{24,16},{16,24},{9,1},{1,9},{25,17},{17,25},{10,2},{2,... | collective-permute-start | bytes 196616 | tf_op jit(solution)/shard_map/ppermute | solution.py:73
  6.9 3.6 %collective-permute-start.2 = (bf16[4,64,128]{2,1,0:T(8,128)(2,1)S(1)}, bf16[4,64,128]{2,1,0:T(8,128)(2,1)S(1)}, u32[]{:S(2)}, u32[]{:S(2)}) collective-permute-start(bf16[4,64,128]{2,1,0:T(8,128)(2,1)S(1)} %collective-permute-done.refs_5_), channel_id=1, source_target_pairs={{16,0},{24,8},{0,16},{8,24},{17,1},{25,9},{1,17},{9,25},{18,2},{26... | collective-permute-start | bytes 196616 | tf_op jit(solution)/shard_map/ppermute | solution.py:73
  8.2 6.9 %collective-permute-start.4 = (bf16[14,64,128]{2,1,0:T(8,128)(2,1)S(1)}, bf16[14,64,128]{2,1,0:T(8,128)(2,1)S(1)}, u32[]{:S(2)}, u32[]{:S(2)}) collective-permute-start(bf16[14,64,128]{2,1,0:T(8,128)(2,1)S(1)} %get-tuple-element.47.refs_5_), channel_id=1, source_target_pairs={{4,0},{0,4},{5,1},{1,5},{6,2},{2,6},{7,3},{3,7},{12,8},{8,12},{13,... | collective-permute-start | bytes 688136 | tf_op jit(solution)/shard_map/ppermute | solution.py:73
  11.5 2.1 %collective-permute-start.6 = (bf16[384,128]{1,0:T(8,128)(2,1)S(1)}, bf16[384,128]{1,0:T(8,128)(2,1)S(1)}, u32[]{:S(2)}, u32[]{:S(2)}) collective-permute-start(bf16[384,128]{1,0:T(8,128)(2,1)S(1)} %get-tuple-element.54), channel_id=1, source_target_pairs={{8,0},{0,8},{24,16},{16,24},{9,1},{1,9},{25,17},{17,25},{10,2},{2,... | collective-permute-start | bytes 294920 | tf_op jit(solution)/shard_map/ppermute | solution.py:73
  12.4 1.3 %collective-permute-start.7 = (bf16[384,128]{1,0:T(8,128)(2,1)S(1)}, bf16[384,128]{1,0:T(8,128)(2,1)S(1)}, u32[]{:S(2)}, u32[]{:S(2)}) collective-permute-start(bf16[384,128]{1,0:T(8,128)(2,1)S(1)} %get-tuple-element.55), channel_id=1, source_target_pairs={{8,0},{0,8},{24,16},{16,24},{9,1},{1,9},{25,17},{17,25},{10,2},{2,... | collective-permute-start | bytes 294920 | tf_op jit(solution)/shard_map/ppermute | solution.py:73
  12.4 4.2 %collective-permute-start.5 = (bf16[4,64,128]{2,1,0:T(8,128)(2,1)S(1)}, bf16[4,64,128]{2,1,0:T(8,128)(2,1)S(1)}, u32[]{:S(2)}, u32[]{:S(2)}) collective-permute-start(bf16[4,64,128]{2,1,0:T(8,128)(2,1)S(1)} %shard_map.131.refs_7_), channel_id=1, source_target_pairs={{4,0},{0,4},{5,1},{1,5},{6,2},{2,6},{7,3},{3,7},{12,8},{8,12},{13,... | collective-permute-start | bytes 196616 | tf_op jit(solution)/shard_map/ppermute | solution.py:73
  13.7 4.2 %collective-permute-start.8 = (bf16[384,128]{1,0:T(8,128)(2,1)S(1)}, bf16[384,128]{1,0:T(8,128)(2,1)S(1)}, u32[]{:S(2)}, u32[]{:S(2)}) collective-permute-start(bf16[384,128]{1,0:T(8,128)(2,1)S(1)} %get-tuple-element.60), channel_id=1, source_target_pairs={{16,0},{24,8},{0,16},{8,24},{17,1},{25,9},{1,17},{9,25},{18,2},{26... | collective-permute-start | bytes 294920 | tf_op jit(solution)/shard_map/ppermute | solution.py:73
  17.9 2.5 %collective-permute-start.9 = (bf16[896,128]{1,0:T(8,128)(2,1)S(1)}, bf16[896,128]{1,0:T(8,128)(2,1)S(1)}, u32[]{:S(2)}, u32[]{:S(2)}) collective-permute-start(bf16[896,128]{1,0:T(8,128)(2,1)S(1)} %get-tuple-element.61), channel_id=1, source_target_pairs={{8,0},{0,8},{24,16},{16,24},{9,1},{1,9},{25,17},{17,25},{10,2},{2,... | collective-permute-start | bytes 688136 | tf_op jit(solution)/shard_map/ppermute | solution.py:73
  19.1 4.1 %collective-permute-start.13 = (bf16[320,128]{1,0:T(8,128)(2,1)S(1)}, bf16[320,128]{1,0:T(8,128)(2,1)S(1)}, u32[]{:S(2)}, u32[]{:S(2)}) collective-permute-start(bf16[320,128]{1,0:T(8,128)(2,1)S(1)} %get-tuple-element.63.refs_2_), channel_id=1, source_target_pairs={{4,0},{0,4},{5,1},{1,5},{6,2},{2,6},{7,3},{3,7},{12,8},{8,12},{13,... | collective-permute-start | bytes 245768 | tf_op jit(solution)/shard_map/ppermute | solution.py:73
  20.5 6.9 %collective-permute-start.12 = (bf16[272,128]{1,0:T(8,128)(2,1)S(1)}, bf16[272,128]{1,0:T(8,128)(2,1)S(1)}, u32[]{:S(2)}, u32[]{:S(2)}) collective-permute-start(bf16[272,128]{1,0:T(8,128)(2,1)S(1)} %get-tuple-element.67), channel_id=1, source_target_pairs={{20,0},{16,4},{28,8},{24,12},{4,16},{0,20},{12,24},{8,28},{21,1},{... | collective-permute-start | bytes 208904 | tf_op jit(solution)/shard_map/ppermute | solution.py:81
  22.4 5.0 %collective-permute-start.10 = (bf16[256,128]{1,0:T(8,128)(2,1)S(1)}, bf16[256,128]{1,0:T(8,128)(2,1)S(1)}, u32[]{:S(2)}, u32[]{:S(2)}) collective-permute-start(bf16[256,128]{1,0:T(8,128)(2,1)S(1)} %get-tuple-element.64), channel_id=1, source_target_pairs={{16,0},{24,8},{0,16},{8,24},{17,1},{25,9},{1,17},{9,25},{18,2},{26... | collective-permute-start | bytes 196616 | tf_op jit(solution)/shard_map/ppermute | solution.py:73
  22.8 3.3 %collective-permute-start.11 = (bf16[192,128]{1,0:T(8,128)(2,1)S(1)}, bf16[192,128]{1,0:T(8,128)(2,1)S(1)}, u32[]{:S(2)}, u32[]{:S(2)}) collective-permute-start(bf16[192,128]{1,0:T(8,128)(2,1)S(1)} %get-tuple-element.66), channel_id=1, source_target_pairs={{4,0},{0,4},{5,1},{1,5},{6,2},{2,6},{7,3},{3,7},{12,8},{8,12},{13,... | collective-permute-start | bytes 147464 | tf_op jit(solution)/shard_map/ppermute | solution.py:73
  23.3 5.5 %collective-permute-start.15 = (bf16[192,128]{1,0:T(8,128)(2,1)S(1)}, bf16[192,128]{1,0:T(8,128)(2,1)S(1)}, u32[]{:S(2)}, u32[]{:S(2)}) collective-permute-start(bf16[192,128]{1,0:T(8,128)(2,1)S(1)} %shard_map.140.refs_0_), channel_id=1, source_target_pairs={{1,0},{0,1},{3,2},{2,3},{5,4},{4,5},{7,6},{6,7},{9,8},{8,9},{11,10... | collective-permute-start | bytes 147464 | tf_op jit(solution)/shard_map/ppermute | solution.py:73
  27.4 5.4 %copy-start.8 = (bf16[3,3,128,128]{3,2,1,0:T(8,128)(2,1)S(1)}, bf16[3,3,128,128]{3,2,1,0:T(8,128)(2,1)}, u32[]{:S(2)}) copy-start(bf16[3,3,128,128]{3,2,1,0:T(8,128)(2,1)} %refs_4_.5) | copy-start | bytes 884740
  27.4 3.7 %collective-permute-start.14 = (bf16[192,128]{1,0:T(8,128)(2,1)S(1)}, bf16[192,128]{1,0:T(8,128)(2,1)S(1)}, u32[]{:S(2)}, u32[]{:S(2)}) collective-permute-start(bf16[192,128]{1,0:T(8,128)(2,1)S(1)} %shard_map.139.refs_0_), channel_id=1, source_target_pairs={{1,0},{0,1},{3,2},{2,3},{5,4},{4,5},{7,6},{6,7},{9,8},{8,9},{11,10... | collective-permute-start | bytes 147464 | tf_op jit(solution)/shard_map/ppermute | solution.py:73
  28.8 5.5 %collective-permute-start.17 = (bf16[192,128]{1,0:T(8,128)(2,1)S(1)}, bf16[192,128]{1,0:T(8,128)(2,1)S(1)}, u32[]{:S(2)}, u32[]{:S(2)}) collective-permute-start(bf16[192,128]{1,0:T(8,128)(2,1)S(1)} %shard_map.143.refs_2_), channel_id=1, source_target_pairs={{2,0},{3,1},{0,2},{1,3},{6,4},{7,5},{4,6},{5,7},{10,8},{11,9},{8,1... | collective-permute-start | bytes 147464 | tf_op jit(solution)/shard_map/ppermute | solution.py:73
  31.2 4.4 %collective-permute-start.16 = (bf16[192,128]{1,0:T(8,128)(2,1)S(1)}, bf16[192,128]{1,0:T(8,128)(2,1)S(1)}, u32[]{:S(2)}, u32[]{:S(2)}) collective-permute-start(bf16[192,128]{1,0:T(8,128)(2,1)S(1)} %shard_map.141.refs_5_.refs_0_), channel_id=1, source_target_pairs={{2,0},{3,1},{0,2},{1,3},{6,4},{7,5},{4,6},{5,7},{10,8},{11,9},{8,1... | collective-permute-start | bytes 147464 | tf_op jit(solution)/shard_map/ppermute | solution.py:73
  35.7 4.5 %collective-permute-start.20 = (bf16[2,208,128]{2,1,0:T(8,128)(2,1)S(1)}, bf16[2,208,128]{2,1,0:T(8,128)(2,1)S(1)}, u32[]{:S(2)}, u32[]{:S(2)}) collective-permute-start(bf16[2,208,128]{2,1,0:T(8,128)(2,1)S(1)} %get-tuple-element.74), channel_id=1, source_target_pairs={{20,0},{16,4},{28,8},{24,12},{4,16},{0,20},{12,24},{8,28},{21,1},{... | collective-permute-start | bytes 319496 | tf_op jit(solution)/shard_map/ppermute | solution.py:81
  36.8 6.4 %collective-permute-start.21 = (bf16[2,192,128]{2,1,0:T(8,128)(2,1)S(1)}, bf16[2,192,128]{2,1,0:T(8,128)(2,1)S(1)}, u32[]{:S(2)}, u32[]{:S(2)}) collective-permute-start(bf16[2,192,128]{2,1,0:T(8,128)(2,1)S(1)} %get-tuple-element.73.refs_0_), channel_id=1, source_target_pairs={{4,0},{0,4},{5,1},{1,5},{6,2},{2,6},{7,3},{3,7},{12,8},{8,12},{13,... | collective-permute-start | bytes 294920 | tf_op jit(solution)/shard_map/ppermute | solution.py:73
  37.8 6.1 %collective-permute-start.18 = (bf16[2,192,128]{2,1,0:T(8,128)(2,1)S(1)}, bf16[2,192,128]{2,1,0:T(8,128)(2,1)S(1)}, u32[]{:S(2)}, u32[]{:S(2)}) collective-permute-start(bf16[2,192,128]{2,1,0:T(8,128)(2,1)S(1)} %get-tuple-element.73.refs_0_), channel_id=1, source_target_pairs={{16,0},{24,8},{0,16},{8,24},{17,1},{25,9},{1,17},{9,25},{18,2},{26... | collective-permute-start | bytes 294920 | tf_op jit(solution)/shard_map/ppermute | solution.py:73
  40.2 4.7 %collective-permute-start.23 = (bf16[2,208,128]{2,1,0:T(8,128)(2,1)S(1)}, bf16[2,208,128]{2,1,0:T(8,128)(2,1)S(1)}, u32[]{:S(2)}, u32[]{:S(2)}) collective-permute-start(bf16[2,208,128]{2,1,0:T(8,128)(2,1)S(1)} %collective-permute-done.20.refs_1_), channel_id=1, source_target_pairs={{8,0},{0,8},{24,16},{16,24},{9,1},{1,9},{25,17},{17,25},{10,2},{2,... | collective-permute-start | bytes 319496 | tf_op jit(solution)/shard_map/ppermute | solution.py:73
  43.1 1.7 %collective-permute-start.22 = (bf16[2,192,128]{2,1,0:T(8,128)(2,1)S(1)}, bf16[2,192,128]{2,1,0:T(8,128)(2,1)S(1)}, u32[]{:S(2)}, u32[]{:S(2)}) collective-permute-start(bf16[2,192,128]{2,1,0:T(8,128)(2,1)S(1)} %get-tuple-element.73.refs_0_), channel_id=1, source_target_pairs={{8,0},{0,8},{24,16},{16,24},{9,1},{1,9},{25,17},{17,25},{10,2},{2,... | collective-permute-start | bytes 294920 | tf_op jit(solution)/shard_map/ppermute | solution.py:73
  43.1 1.7 %collective-permute-start.24 = (bf16[2,192,128]{2,1,0:T(8,128)(2,1)S(1)}, bf16[2,192,128]{2,1,0:T(8,128)(2,1)S(1)}, u32[]{:S(2)}, u32[]{:S(2)}) collective-permute-start(bf16[2,192,128]{2,1,0:T(8,128)(2,1)S(1)} %collective-permute-done.21.refs_2_), channel_id=1, source_target_pairs={{8,0},{0,8},{24,16},{16,24},{9,1},{1,9},{25,17},{17,25},{10,2},{2,... | collective-permute-start | bytes 294920 | tf_op jit(solution)/shard_map/ppermute | solution.py:73
  43.9 2.2 %collective-permute-start.19 = (bf16[2,192,128]{2,1,0:T(8,128)(2,1)S(1)}, bf16[2,192,128]{2,1,0:T(8,128)(2,1)S(1)}, u32[]{:S(2)}, u32[]{:S(2)}) collective-permute-start(bf16[2,192,128]{2,1,0:T(8,128)(2,1)S(1)} %collective-permute-done.18.refs_6_), channel_id=1, source_target_pairs={{8,0},{0,8},{24,16},{16,24},{9,1},{1,9},{25,17},{17,25},{10,2},{2,... | collective-permute-start | bytes 294920 | tf_op jit(solution)/shard_map/ppermute | solution.py:73
  (2 other events, 6.1 us)

commit v21 on v20

--- a/solution.py
+++ b/solution.py
@@ -424,13 +424,13 @@
 
 
 def scaled_kernel(factor, *refs):
-    out_ref, long_ref = refs[-2:]
-    height = out_ref.shape[1]
+    outs = refs[4:]
+    height = outs[0].shape[1]
     for block in range(2):
         one, two = (ref[...].astype(jnp.float32) for ref in refs[2 * block : 2 * block + 2])
         total = ((one + two) * factor).astype(jnp.bfloat16)
-        out_ref[block] = total
-        long_ref[block, :height] = total
+        for out_ref in outs:
+            out_ref[block, :height] = total
 
 
 def place_kernel(places, *refs):
@@ -707,9 +707,9 @@
         last_two = flipped(sum_two, "dp", 2)
         last_one = flipped(later_than(sum_one, sum_two), "dp", 2)
         grad_in, token = input_gradient(across, (sum_one,))
-        own, longer = call(
+        own, longer, longest = call(
             functools.partial(scaled_kernel, factor),
-            [bf16(2, half, ch), bf16(2, half + 16, ch)],
+            [bf16(2, half + more, ch) for more in (0, 16, 32)],
             [],
             height * ch,
             sum_one,
@@ -718,12 +718,12 @@
             last_two,
             after=(token,),
         )
-        shares = [own, flipped_both(longer), flipped(own, "video", 1)]
+        frame, both = flipped(longest, "video", 1), flipped_both(longer)
+        shares = [own, frame, flipped(own, "section", 2)]
         shares += [flipped(share, "section", 1) for share in shares]
-        across = flipped(own, "section", 2)
-        places = [(0, False), (2, True), (0, True), (1, False), (3, True), (1, True)]
-        sums = placed([*shares, across], [*places, (2, False)])
-        sums = unpacked(placed([flipped(across, "section", 1)], [(3, False)], sums))
+        places = [(0, False), (0, True), (2, False), (1, False), (1, True), (3, False)]
+        sums = placed([*shares, both], [*places, (2, True)])
+        sums = unpacked(placed([flipped(both, "section", 1)], [(3, True)], sums))
     else:
         own_one, send_one = call(
             pair_kernel,

time: 47.3 us -> 48.7 us (1.030)
  starting transfers between devices: 28.5 us -> 29.8 us
    ppermute x23, waiting for transfers between devices: 6.38 us -> 8.26 us  [flipped(): lax.ppermute(block, axis, [(place ^ flip, place) for place in range(count)])]
    ppermute x2, waiting for transfers between devices: 1.81 us -> 0.01 us  [flipped_both(): return lax.ppermute(block, ('section', 'video'), pairs)]
    ppermute x23, starting transfers between devices: 25.5 us -> 26.5 us  [flipped(): lax.ppermute(block, axis, [(place ^ flip, place) for place in range(count)])]
  transfers between devices with their start and end apart: 25 -> 25, of which waited for: 8 -> 9; matrix products, arithmetic and copies ran while one was open for 0% -> 0% of each run, Pallas kernels for 18% -> 18%
where the time goes in v21:
time: 48.7 us; the launch traced here: 48.1 us
  starting transfers between devices  29.8 us (61%)
  Pallas kernels  9.26 us (19%)
  waiting for transfers between devices  8.26 us (17%)
  between operations  0.83 us (2%)
    ppermute x23, starting transfers between devices, flipped(): lax.ppermute(block, axis, [(place ^ flip, place) for place in range(count)])  26.5 us
    ppermute x23, waiting for transfers between devices, flipped(): lax.ppermute(block, axis, [(place ^ flip, place) for place in range(count)])  8.26 us
    pallas_call x17, Pallas kernels, call(): pl.pallas_call(body, out_shape=outs[0] if single else tuple(outs), in_spe...  7.36 us
    ppermute x2, starting transfers between devices, flipped_both(): return lax.ppermute(block, ('section', 'video'), pairs)  3.27 us
    pallas_call x2, Pallas kernels, placed(): pl.pallas_call(functools.partial(place_kernel, places), out_shape=outs, i...  1.9 us
  transfers between devices with their start and end apart: 25, of which 9 were waited for; matrix products, arithmetic and copies ran while one was open for 0% of the time, Pallas kernels for 18%

profile of v21, /device:TPU:1, one launch (start us, length us, event | category | flops | bytes accessed | tf_op | source)
XLA Modules:
  0.0 48.1 jit_solution(5566788333893644628)
XLA Ops:
  0.6 2.1 %collective-permute-start.3 = (bf16[16,64,128]{2,1,0:T(8,128)(2,1)}, bf16[16,64,128]{2,1,0:T(8,128)(2,1)S(1)}, u32[]{:S(2)}, u32[]{:S(2)}) collective-permute-start(bf16[16,64,128]{2,1,0:T(8,128)(2,1)} %bitcast.10), channel_id=1, source_target_pairs={{4,0},{0,4},{5,1},{1,5},{6,2},{2,6},{7,3},{3,7},{12,8},{8,12},{13,... | collective-permute-start | bytes 786440 | tf_op jit(solution)/shard_map/ppermute | solution.py:73
  2.7 1.6 %shard_map.128 = (bf16[4,64,128]{2,1,0:T(8,128)(2,1)}, bf16[4,64,128]{2,1,0:T(8,128)(2,1)}) custom-call(bf16[16,64,128]{2,1,0:T(8,128)(2,1)} %bitcast.11, bf16[16,64,128]{2,1,0:T(8,128)(2,1)} %bitcast.17, bf16[16,64,128]{2,1,0:T(8,128)(2,1)} %bitcast.28, bf16[16,64,128]{2,1,0:T(8,128)(2,1)} %bitcast.25), custom_call_target="tpu_custom_call" | custom-call | flops 1 | bytes 1179648 | tf_op jit(solution)/shard_map/pallas_call | solution.py:38
  4.4 1.0 %collective-permute-start = (bf16[4,64,128]{2,1,0:T(8,128)(2,1)}, bf16[4,64,128]{2,1,0:T(8,128)(2,1)S(1)}, u32[]{:S(2)}, u32[]{:S(2)}) collective-permute-start(bf16[4,64,128]{2,1,0:T(8,128)(2,1)} %get-tuple-element.46), channel_id=1, source_target_pairs={{8,0},{0,8},{24,16},{16,24},{9,1},{1,9},{25,17},{17,25},{10,2},{2,... | collective-permute-start | bytes 196616 | tf_op jit(solution)/shard_map/ppermute | solution.py:73
  5.4 1.1 %collective-permute-done.refs_5_ = bf16[4,64,128]{2,1,0:T(8,128)(2,1)S(1)} collective-permute-done((bf16[4,64,128]{2,1,0:T(8,128)(2,1)}, bf16[4,64,128]{2,1,0:T(8,128)(2,1)S(1)}, u32[]{:S(2)}, u32[]{:S(2)}) %collective-permute-start) | collective-permute-done | bytes 65568 | tf_op jit(solution)/shard_map/ppermute | solution.py:73
  6.9 1.2 %collective-permute-start.2 = (bf16[4,64,128]{2,1,0:T(8,128)(2,1)S(1)}, bf16[4,64,128]{2,1,0:T(8,128)(2,1)S(1)}, u32[]{:S(2)}, u32[]{:S(2)}) collective-permute-start(bf16[4,64,128]{2,1,0:T(8,128)(2,1)S(1)} %collective-permute-done.refs_5_), channel_id=1, source_target_pairs={{16,0},{24,8},{0,16},{8,24},{17,1},{25,9},{1,17},{9,25},{18,2},{26... | collective-permute-start | bytes 196616 | tf_op jit(solution)/shard_map/ppermute | solution.py:73
  8.2 1.3 %collective-permute-start.4 = (bf16[14,64,128]{2,1,0:T(8,128)(2,1)S(1)}, bf16[14,64,128]{2,1,0:T(8,128)(2,1)S(1)}, u32[]{:S(2)}, u32[]{:S(2)}) collective-permute-start(bf16[14,64,128]{2,1,0:T(8,128)(2,1)S(1)} %get-tuple-element.48.refs_5_), channel_id=1, source_target_pairs={{4,0},{0,4},{5,1},{1,5},{6,2},{2,6},{7,3},{3,7},{12,8},{8,12},{13,... | collective-permute-start | bytes 688136 | tf_op jit(solution)/shard_map/ppermute | solution.py:73
  9.6 1.0 %shard_map.130 = (bf16[14,64,128]{2,1,0:T(8,128)(2,1)S(1)}, bf16[16,64,128]{2,1,0:T(8,128)(2,1)S(1)}) custom-call(bf16[16,64,128]{2,1,0:T(8,128)(2,1)S(1)} %bitcast.13, bf16[16,64,128]{2,1,0:T(8,128)(2,1)S(1)} %bitcast.19, bf16[16,64,128]{2,1,0:T(8,128)(2,1)S(1)} %collective-permute-done.3.refs_2_.refs_6_, bf16[3,128,128]{2,1,0:T(8,128)(2,1)S(1)} %copy-done.6, ...), custom_call_target="tpu_custom_call" | custom-call | tf_op jit(solution)/shard_map/pallas_call | solution.py:38
  10.6 0.9 %shard_map.132 = (f32[2,384,128]{2,1,0:T(8,128)S(1)}, bf16[384,128]{1,0:T(8,128)(2,1)S(1)}, bf16[384,128]{1,0:T(8,128)(2,1)S(1)}) custom-call(bf16[16,64,128]{2,1,0:T(8,128)(2,1)S(1)} %bitcast.30, bf16[16,64,128]{2,1,0:T(8,128)(2,1)S(1)} %bitcast.20, bf16[16,64,128]{2,1,0:T(8,128)(2,1)S(1)} %get-tuple-element.51.refs_6_.refs_2_.refs_4_, ...), custom_call_target="tpu_custom_call" | custom-call | flops 2415919104 | bytes 2031616 | tf_op jit(solution)/shard_map/pallas_call | solution.py:38
  11.5 0.9 %collective-permute-start.6 = (bf16[384,128]{1,0:T(8,128)(2,1)S(1)}, bf16[384,128]{1,0:T(8,128)(2,1)S(1)}, u32[]{:S(2)}, u32[]{:S(2)}) collective-permute-start(bf16[384,128]{1,0:T(8,128)(2,1)S(1)} %get-tuple-element.55), channel_id=1, source_target_pairs={{8,0},{0,8},{24,16},{16,24},{9,1},{1,9},{25,17},{17,25},{10,2},{2,... | collective-permute-start | bytes 294920 | tf_op jit(solution)/shard_map/ppermute | solution.py:73
  12.4 0.8 %collective-permute-start.5 = (bf16[4,64,128]{2,1,0:T(8,128)(2,1)S(1)}, bf16[4,64,128]{2,1,0:T(8,128)(2,1)S(1)}, u32[]{:S(2)}, u32[]{:S(2)}) collective-permute-start(bf16[4,64,128]{2,1,0:T(8,128)(2,1)S(1)} %shard_map.131.refs_7_), channel_id=1, source_target_pairs={{4,0},{0,4},{5,1},{1,5},{6,2},{2,6},{7,3},{3,7},{12,8},{8,12},{13,... | collective-permute-start | bytes 196616 | tf_op jit(solution)/shard_map/ppermute | solution.py:73
  13.7 1.4 %collective-permute-start.8 = (bf16[384,128]{1,0:T(8,128)(2,1)S(1)}, bf16[384,128]{1,0:T(8,128)(2,1)S(1)}, u32[]{:S(2)}, u32[]{:S(2)}) collective-permute-start(bf16[384,128]{1,0:T(8,128)(2,1)S(1)} %get-tuple-element.61), channel_id=1, source_target_pairs={{16,0},{24,8},{0,16},{8,24},{17,1},{25,9},{1,17},{9,25},{18,2},{26... | collective-permute-start | bytes 294920 | tf_op jit(solution)/shard_map/ppermute | solution.py:73
  15.6 1.0 %collective-permute-done.5.refs_6_ = bf16[4,64,128]{2,1,0:T(8,128)(2,1)S(1)} collective-permute-done((bf16[4,64,128]{2,1,0:T(8,128)(2,1)S(1)}, bf16[4,64,128]{2,1,0:T(8,128)(2,1)S(1)}, u32[]{:S(2)}, u32[]{:S(2)}) %collective-permute-start.5) | collective-permute-done | bytes 65568 | tf_op jit(solution)/shard_map/ppermute | solution.py:73
  16.6 1.3 %shard_map.136 = (bf16[16,64,128]{2,1,0:T(8,128)(2,1)S(1)}, bf16[16,64,128]{2,1,0:T(8,128)(2,1)S(1)}, f32[2,384,128]{2,1,0:T(8,128)S(1)}, bf16[896,128]{1,0:T(8,128)(2,1)S(1)}) custom-call(bf16[16,64,128]{2,1,0:T(8,128)(2,1)S(1)} %bitcast.16, bf16[4,64,128]{2,1,0:T(8,128)(2,1)S(1)} %collective-permute-done.1.refs_4_.refs_1_.refs_3_.refs_2_, ...), custom_call_target="tpu_custom_call" | custom-call | flops 2415919104 | bytes 5046272 | tf_op jit(solution)/shard_map/pallas_call | solution.py:38
  17.9 1.2 %collective-permute-start.9 = (bf16[896,128]{1,0:T(8,128)(2,1)S(1)}, bf16[896,128]{1,0:T(8,128)(2,1)S(1)}, u32[]{:S(2)}, u32[]{:S(2)}) collective-permute-start(bf16[896,128]{1,0:T(8,128)(2,1)S(1)} %get-tuple-element.62), channel_id=1, source_target_pairs={{8,0},{0,8},{24,16},{16,24},{9,1},{1,9},{25,17},{17,25},{10,2},{2,... | collective-permute-start | bytes 688136 | tf_op jit(solution)/shard_map/ppermute | solution.py:73
  19.1 1.3 %collective-permute-start.13 = (bf16[320,128]{1,0:T(8,128)(2,1)S(1)}, bf16[320,128]{1,0:T(8,128)(2,1)S(1)}, u32[]{:S(2)}, u32[]{:S(2)}) collective-permute-start(bf16[320,128]{1,0:T(8,128)(2,1)S(1)} %get-tuple-element.64.refs_2_), channel_id=1, source_target_pairs={{4,0},{0,4},{5,1},{1,5},{6,2},{2,6},{7,3},{3,7},{12,8},{8,12},{13,... | collective-permute-start | bytes 245768 | tf_op jit(solution)/shard_map/ppermute | solution.py:73
  20.5 1.9 %collective-permute-start.12 = (bf16[272,128]{1,0:T(8,128)(2,1)S(1)}, bf16[272,128]{1,0:T(8,128)(2,1)S(1)}, u32[]{:S(2)}, u32[]{:S(2)}) collective-permute-start(bf16[272,128]{1,0:T(8,128)(2,1)S(1)} %get-tuple-element.68), channel_id=1, source_target_pairs={{20,0},{16,4},{28,8},{24,12},{4,16},{0,20},{12,24},{8,28},{21,1},{... | collective-permute-start | bytes 208904 | tf_op jit(solution)/shard_map/ppermute | solution.py:81
  23.3 1.4 %collective-permute-start.15 = (bf16[192,128]{1,0:T(8,128)(2,1)S(1)}, bf16[192,128]{1,0:T(8,128)(2,1)S(1)}, u32[]{:S(2)}, u32[]{:S(2)}) collective-permute-start(bf16[192,128]{1,0:T(8,128)(2,1)S(1)} %shard_map.140.refs_0_), channel_id=1, source_target_pairs={{1,0},{0,1},{3,2},{2,3},{5,4},{4,5},{7,6},{6,7},{9,8},{8,9},{11,10... | collective-permute-start | bytes 147464 | tf_op jit(solution)/shard_map/ppermute | solution.py:73
  24.6 1.5 %collective-permute-done.11.refs_2_ = bf16[192,128]{1,0:T(8,128)(2,1)S(1)} collective-permute-done((bf16[192,128]{1,0:T(8,128)(2,1)S(1)}, bf16[192,128]{1,0:T(8,128)(2,1)S(1)}, u32[]{:S(2)}, u32[]{:S(2)}) %collective-permute-start.11) | collective-permute-done | bytes 49184 | tf_op jit(solution)/shard_map/ppermute | solution.py:73
  26.1 1.3 %collective-permute-done.10.refs_1_.refs_3_ = bf16[256,128]{1,0:T(8,128)(2,1)S(1)} collective-permute-done((bf16[256,128]{1,0:T(8,128)(2,1)S(1)}, bf16[256,128]{1,0:T(8,128)(2,1)S(1)}, u32[]{:S(2)}, u32[]{:S(2)}) %collective-permute-start.10) | collective-permute-done | bytes 65568 | tf_op jit(solution)/shard_map/ppermute | solution.py:73
  27.4 1.3 %collective-permute-start.14 = (bf16[192,128]{1,0:T(8,128)(2,1)S(1)}, bf16[192,128]{1,0:T(8,128)(2,1)S(1)}, u32[]{:S(2)}, u32[]{:S(2)}) collective-permute-start(bf16[192,128]{1,0:T(8,128)(2,1)S(1)} %shard_map.139.refs_0_), channel_id=1, source_target_pairs={{1,0},{0,1},{3,2},{2,3},{5,4},{4,5},{7,6},{6,7},{9,8},{8,9},{11,10... | collective-permute-start | bytes 147464 | tf_op jit(solution)/shard_map/ppermute | solution.py:73
  28.8 2.4 %collective-permute-start.17 = (bf16[192,128]{1,0:T(8,128)(2,1)S(1)}, bf16[192,128]{1,0:T(8,128)(2,1)S(1)}, u32[]{:S(2)}, u32[]{:S(2)}) collective-permute-start(bf16[192,128]{1,0:T(8,128)(2,1)S(1)} %shard_map.143.refs_2_), channel_id=1, source_target_pairs={{2,0},{3,1},{0,2},{1,3},{6,4},{7,5},{4,6},{5,7},{10,8},{11,9},{8,1... | collective-permute-start | bytes 147464 | tf_op jit(solution)/shard_map/ppermute | solution.py:73
  31.2 1.6 %collective-permute-start.16 = (bf16[192,128]{1,0:T(8,128)(2,1)S(1)}, bf16[192,128]{1,0:T(8,128)(2,1)S(1)}, u32[]{:S(2)}, u32[]{:S(2)}) collective-permute-start(bf16[192,128]{1,0:T(8,128)(2,1)S(1)} %shard_map.141.refs_5_.refs_0_), channel_id=1, source_target_pairs={{2,0},{3,1},{0,2},{1,3},{6,4},{7,5},{4,6},{5,7},{10,8},{11,9},{8,1... | collective-permute-start | bytes 147464 | tf_op jit(solution)/shard_map/ppermute | solution.py:73
  32.8 1.5 %shard_map.142 = (bf16[16,64,128]{2,1,0:T(8,128)(2,1)}, f32[8,128]{1,0:T(8,128)S(1)}) custom-call(bf16[16,64,128]{2,1,0:T(8,128)(2,1)S(1)} %get-tuple-element.58.refs_0_, bf16[16,64,128]{2,1,0:T(8,128)(2,1)S(1)} %get-tuple-element.59.refs_1_, bf16[896,128]{1,0:T(8,128)(2,1)S(1)} %collective-permute-done.9.refs_1_.refs_2_, ...), custom_call_target="tpu_custom_call" | custom-call | flops 301989888 | bytes 1380352 | tf_op jit(solution)/shard_map/pallas_call | solution.py:38
  34.3 1.3 %collective-permute-done.16.refs_1_ = bf16[192,128]{1,0:T(8,128)(2,1)S(1)} collective-permute-done((bf16[192,128]{1,0:T(8,128)(2,1)S(1)}, bf16[192,128]{1,0:T(8,128)(2,1)S(1)}, u32[]{:S(2)}, u32[]{:S(2)}) %collective-permute-start.16) | collective-permute-done | bytes 49184 | tf_op jit(solution)/shard_map/ppermute | solution.py:73
  35.7 0.8 %collective-permute-start.20 = (bf16[2,224,128]{2,1,0:T(8,128)(2,1)S(1)}, bf16[2,224,128]{2,1,0:T(8,128)(2,1)S(1)}, u32[]{:S(2)}, u32[]{:S(2)}) collective-permute-start(bf16[2,224,128]{2,1,0:T(8,128)(2,1)S(1)} %get-tuple-element.76), channel_id=1, source_target_pairs={{4,0},{0,4},{5,1},{1,5},{6,2},{2,6},{7,3},{3,7},{12,8},{8,12},{13,... | collective-permute-start | bytes 344072 | tf_op jit(solution)/shard_map/ppermute | solution.py:73
  36.5 1.4 %collective-permute-start.18 = (bf16[2,208,128]{2,1,0:T(8,128)(2,1)S(1)}, bf16[2,208,128]{2,1,0:T(8,128)(2,1)S(1)}, u32[]{:S(2)}, u32[]{:S(2)}) collective-permute-start(bf16[2,208,128]{2,1,0:T(8,128)(2,1)S(1)} %get-tuple-element.74), channel_id=1, source_target_pairs={{20,0},{16,4},{28,8},{24,12},{4,16},{0,20},{12,24},{8,28},{21,1},{... | collective-permute-start | bytes 319496 | tf_op jit(solution)/shard_map/ppermute | solution.py:81
  38.4 1.0 %collective-permute-done.20.refs_1_ = bf16[2,224,128]{2,1,0:T(8,128)(2,1)S(1)} collective-permute-done((bf16[2,224,128]{2,1,0:T(8,128)(2,1)S(1)}, bf16[2,224,128]{2,1,0:T(8,128)(2,1)S(1)}, u32[]{:S(2)}, u32[]{:S(2)}) %collective-permute-start.20) | collective-permute-done | bytes 114720 | tf_op jit(solution)/shard_map/ppermute | solution.py:73
  39.4 3.1 %collective-permute-start.23 = (bf16[2,224,128]{2,1,0:T(8,128)(2,1)S(1)}, bf16[2,224,128]{2,1,0:T(8,128)(2,1)S(1)}, u32[]{:S(2)}, u32[]{:S(2)}) collective-permute-start(bf16[2,224,128]{2,1,0:T(8,128)(2,1)S(1)} %collective-permute-done.20.refs_1_), channel_id=1, source_target_pairs={{8,0},{0,8},{24,16},{16,24},{9,1},{1,9},{25,17},{17,25},{10,2},{2,... | collective-permute-start | bytes 344072 | tf_op jit(solution)/shard_map/ppermute | solution.py:73
  42.4 1.8 %collective-permute-start.19 = (bf16[2,208,128]{2,1,0:T(8,128)(2,1)S(1)}, bf16[2,208,128]{2,1,0:T(8,128)(2,1)S(1)}, u32[]{:S(2)}, u32[]{:S(2)}) collective-permute-start(bf16[2,208,128]{2,1,0:T(8,128)(2,1)S(1)} %collective-permute-done.18.refs_6_), channel_id=1, source_target_pairs={{8,0},{0,8},{24,16},{16,24},{9,1},{1,9},{25,17},{17,25},{10,2},{2,... | collective-permute-start | bytes 319496 | tf_op jit(solution)/shard_map/ppermute | solution.py:73
  44.3 1.0 %collective-permute-start.24 = (bf16[2,192,128]{2,1,0:T(8,128)(2,1)S(1)}, bf16[2,192,128]{2,1,0:T(8,128)(2,1)S(1)}, u32[]{:S(2)}, u32[]{:S(2)}) collective-permute-start(bf16[2,192,128]{2,1,0:T(8,128)(2,1)S(1)} %collective-permute-done.21.refs_2_), channel_id=1, source_target_pairs={{8,0},{0,8},{24,16},{16,24},{9,1},{1,9},{25,17},{17,25},{10,2},{2,... | collective-permute-start | bytes 294920 | tf_op jit(solution)/shard_map/ppermute | solution.py:73
  46.2 1.2 %shard_map.145 = (f32[3,384,128]{2,1,0:T(8,128)}, f32[384,128]{1,0:T(8,128)}, f32[3,384,128]{2,1,0:T(8,128)}, f32[384,128]{1,0:T(8,128)}) custom-call(bf16[2,192,128]{2,1,0:T(8,128)(2,1)S(1)} %get-tuple-element.75.refs_0_, bf16[2,224,128]{2,1,0:T(8,128)(2,1)S(1)} %collective-permute-done.20.refs_1_, ...), custom_call_target="tpu_custom_call" | custom-call | bytes 2064384 | tf_op jit(solution)/shard_map/pallas_call | solution.py:471
  47.4 0.7 %shard_map.146 = (f32[3,384,128]{2,1,0:T(8,128)}, f32[384,128]{1,0:T(8,128)}, f32[3,384,128]{2,1,0:T(8,128)}, f32[384,128]{1,0:T(8,128)}) custom-call(bf16[2,208,128]{2,1,0:T(8,128)(2,1)S(1)} %collective-permute-done.19.refs_0_, f32[3,384,128]{2,1,0:T(8,128)} %get-tuple-element.77.refs_1_, ...), custom_call_target="tpu_custom_call", output_to_operand_aliasing={{0}: (1, {}), {1}: (2, {}), {2}: (3, {}), {3}: (4, {})} | custom-call | bytes 294912 | tf_op jit(solution)/shard_map/pallas_call | solution.py:471
  (55 shorter events, 4.0 us)
Async XLA Ops:
  0.6 8.9 %collective-permute-start.3 = (bf16[16,64,128]{2,1,0:T(8,128)(2,1)}, bf16[16,64,128]{2,1,0:T(8,128)(2,1)S(1)}, u32[]{:S(2)}, u32[]{:S(2)}) collective-permute-start(bf16[16,64,128]{2,1,0:T(8,128)(2,1)} %bitcast.10), channel_id=1, source_target_pairs={{4,0},{0,4},{5,1},{1,5},{6,2},{2,6},{7,3},{3,7},{12,8},{8,12},{13,... | collective-permute-start | bytes 786440 | tf_op jit(solution)/shard_map/ppermute | solution.py:73
  2.7 5.4 %copy-start = (bf16[1,1,16,64,128]{4,3,2,1,0:T(8,128)(2,1)S(1)}, bf16[1,1,16,64,128]{4,3,2,1,0:T(8,128)(2,1)}, u32[]{:S(2)}) copy-start(bf16[1,1,16,64,128]{4,3,2,1,0:T(8,128)(2,1)} %param.9) | copy-start | bytes 786436
  2.7 5.4 %copy-start.1 = (bf16[3,3,128,128]{3,2,1,0:T(8,128)(2,1)S(1)}, bf16[3,3,128,128]{3,2,1,0:T(8,128)(2,1)}, u32[]{:S(2)}) copy-start(bf16[3,3,128,128]{3,2,1,0:T(8,128)(2,1)} %refs_8_.1) | copy-start | bytes 884740
  2.7 5.4 %copy-start.2 = (bf16[1,1,16,64,128]{4,3,2,1,0:T(8,128)(2,1)S(1)}, bf16[1,1,16,64,128]{4,3,2,1,0:T(8,128)(2,1)}, u32[]{:S(2)}) copy-start(bf16[1,1,16,64,128]{4,3,2,1,0:T(8,128)(2,1)} %param.13) | copy-start | bytes 786436
  2.7 5.4 %copy-start.6 = (bf16[3,128,128]{2,1,0:T(8,128)(2,1)S(1)}, bf16[3,128,128]{2,1,0:T(8,128)(2,1)}, u32[]{:S(2)}) copy-start(bf16[3,128,128]{2,1,0:T(8,128)(2,1)} %refs_7_.1) | copy-start | bytes 294916
  4.4 2.1 %collective-permute-start = (bf16[4,64,128]{2,1,0:T(8,128)(2,1)}, bf16[4,64,128]{2,1,0:T(8,128)(2,1)S(1)}, u32[]{:S(2)}, u32[]{:S(2)}) collective-permute-start(bf16[4,64,128]{2,1,0:T(8,128)(2,1)} %get-tuple-element.46), channel_id=1, source_target_pairs={{8,0},{0,8},{24,16},{16,24},{9,1},{1,9},{25,17},{17,25},{10,2},{2,... | collective-permute-start | bytes 196616 | tf_op jit(solution)/shard_map/ppermute | solution.py:73
  6.5 3.0 %copy-start.5 = (bf16[1,1,16,64,128]{4,3,2,1,0:T(8,128)(2,1)S(1)}, bf16[1,1,16,64,128]{4,3,2,1,0:T(8,128)(2,1)}, u32[]{:S(2)}) copy-start(bf16[1,1,16,64,128]{4,3,2,1,0:T(8,128)(2,1)} %param.12) | copy-start | bytes 786436
  6.5 3.0 %copy-start.7 = (bf16[3,128,128]{2,1,0:T(8,128)(2,1)S(1)}, bf16[3,128,128]{2,1,0:T(8,128)(2,1)}, u32[]{:S(2)}) copy-start(bf16[3,128,128]{2,1,0:T(8,128)(2,1)} %refs_11_.1) | copy-start | bytes 294916
  6.5 1.7 %collective-permute-start.1 = (bf16[4,64,128]{2,1,0:T(8,128)(2,1)}, bf16[4,64,128]{2,1,0:T(8,128)(2,1)S(1)}, u32[]{:S(2)}, u32[]{:S(2)}) collective-permute-start(bf16[4,64,128]{2,1,0:T(8,128)(2,1)} %get-tuple-element.47), channel_id=1, source_target_pairs={{8,0},{0,8},{24,16},{16,24},{9,1},{1,9},{25,17},{17,25},{10,2},{2,... | collective-permute-start | bytes 196616 | tf_op jit(solution)/shard_map/ppermute | solution.py:73
  6.9 3.6 %collective-permute-start.2 = (bf16[4,64,128]{2,1,0:T(8,128)(2,1)S(1)}, bf16[4,64,128]{2,1,0:T(8,128)(2,1)S(1)}, u32[]{:S(2)}, u32[]{:S(2)}) collective-permute-start(bf16[4,64,128]{2,1,0:T(8,128)(2,1)S(1)} %collective-permute-done.refs_5_), channel_id=1, source_target_pairs={{16,0},{24,8},{0,16},{8,24},{17,1},{25,9},{1,17},{9,25},{18,2},{26... | collective-permute-start | bytes 196616 | tf_op jit(solution)/shard_map/ppermute | solution.py:73
  8.2 6.9 %collective-permute-start.4 = (bf16[14,64,128]{2,1,0:T(8,128)(2,1)S(1)}, bf16[14,64,128]{2,1,0:T(8,128)(2,1)S(1)}, u32[]{:S(2)}, u32[]{:S(2)}) collective-permute-start(bf16[14,64,128]{2,1,0:T(8,128)(2,1)S(1)} %get-tuple-element.48.refs_5_), channel_id=1, source_target_pairs={{4,0},{0,4},{5,1},{1,5},{6,2},{2,6},{7,3},{3,7},{12,8},{8,12},{13,... | collective-permute-start | bytes 688136 | tf_op jit(solution)/shard_map/ppermute | solution.py:73
  11.5 2.1 %collective-permute-start.6 = (bf16[384,128]{1,0:T(8,128)(2,1)S(1)}, bf16[384,128]{1,0:T(8,128)(2,1)S(1)}, u32[]{:S(2)}, u32[]{:S(2)}) collective-permute-start(bf16[384,128]{1,0:T(8,128)(2,1)S(1)} %get-tuple-element.55), channel_id=1, source_target_pairs={{8,0},{0,8},{24,16},{16,24},{9,1},{1,9},{25,17},{17,25},{10,2},{2,... | collective-permute-start | bytes 294920 | tf_op jit(solution)/shard_map/ppermute | solution.py:73
  12.4 1.3 %collective-permute-start.7 = (bf16[384,128]{1,0:T(8,128)(2,1)S(1)}, bf16[384,128]{1,0:T(8,128)(2,1)S(1)}, u32[]{:S(2)}, u32[]{:S(2)}) collective-permute-start(bf16[384,128]{1,0:T(8,128)(2,1)S(1)} %get-tuple-element.56), channel_id=1, source_target_pairs={{8,0},{0,8},{24,16},{16,24},{9,1},{1,9},{25,17},{17,25},{10,2},{2,... | collective-permute-start | bytes 294920 | tf_op jit(solution)/shard_map/ppermute | solution.py:73
  12.4 4.2 %collective-permute-start.5 = (bf16[4,64,128]{2,1,0:T(8,128)(2,1)S(1)}, bf16[4,64,128]{2,1,0:T(8,128)(2,1)S(1)}, u32[]{:S(2)}, u32[]{:S(2)}) collective-permute-start(bf16[4,64,128]{2,1,0:T(8,128)(2,1)S(1)} %shard_map.131.refs_7_), channel_id=1, source_target_pairs={{4,0},{0,4},{5,1},{1,5},{6,2},{2,6},{7,3},{3,7},{12,8},{8,12},{13,... | collective-permute-start | bytes 196616 | tf_op jit(solution)/shard_map/ppermute | solution.py:73
  13.7 4.2 %collective-permute-start.8 = (bf16[384,128]{1,0:T(8,128)(2,1)S(1)}, bf16[384,128]{1,0:T(8,128)(2,1)S(1)}, u32[]{:S(2)}, u32[]{:S(2)}) collective-permute-start(bf16[384,128]{1,0:T(8,128)(2,1)S(1)} %get-tuple-element.61), channel_id=1, source_target_pairs={{16,0},{24,8},{0,16},{8,24},{17,1},{25,9},{1,17},{9,25},{18,2},{26... | collective-permute-start | bytes 294920 | tf_op jit(solution)/shard_map/ppermute | solution.py:73
  17.9 2.5 %collective-permute-start.9 = (bf16[896,128]{1,0:T(8,128)(2,1)S(1)}, bf16[896,128]{1,0:T(8,128)(2,1)S(1)}, u32[]{:S(2)}, u32[]{:S(2)}) collective-permute-start(bf16[896,128]{1,0:T(8,128)(2,1)S(1)} %get-tuple-element.62), channel_id=1, source_target_pairs={{8,0},{0,8},{24,16},{16,24},{9,1},{1,9},{25,17},{17,25},{10,2},{2,... | collective-permute-start | bytes 688136 | tf_op jit(solution)/shard_map/ppermute | solution.py:73
  19.1 4.1 %collective-permute-start.13 = (bf16[320,128]{1,0:T(8,128)(2,1)S(1)}, bf16[320,128]{1,0:T(8,128)(2,1)S(1)}, u32[]{:S(2)}, u32[]{:S(2)}) collective-permute-start(bf16[320,128]{1,0:T(8,128)(2,1)S(1)} %get-tuple-element.64.refs_2_), channel_id=1, source_target_pairs={{4,0},{0,4},{5,1},{1,5},{6,2},{2,6},{7,3},{3,7},{12,8},{8,12},{13,... | collective-permute-start | bytes 245768 | tf_op jit(solution)/shard_map/ppermute | solution.py:73
  20.5 6.9 %collective-permute-start.12 = (bf16[272,128]{1,0:T(8,128)(2,1)S(1)}, bf16[272,128]{1,0:T(8,128)(2,1)S(1)}, u32[]{:S(2)}, u32[]{:S(2)}) collective-permute-start(bf16[272,128]{1,0:T(8,128)(2,1)S(1)} %get-tuple-element.68), channel_id=1, source_target_pairs={{20,0},{16,4},{28,8},{24,12},{4,16},{0,20},{12,24},{8,28},{21,1},{... | collective-permute-start | bytes 208904 | tf_op jit(solution)/shard_map/ppermute | solution.py:81
  22.4 5.0 %collective-permute-start.10 = (bf16[256,128]{1,0:T(8,128)(2,1)S(1)}, bf16[256,128]{1,0:T(8,128)(2,1)S(1)}, u32[]{:S(2)}, u32[]{:S(2)}) collective-permute-start(bf16[256,128]{1,0:T(8,128)(2,1)S(1)} %get-tuple-element.65), channel_id=1, source_target_pairs={{16,0},{24,8},{0,16},{8,24},{17,1},{25,9},{1,17},{9,25},{18,2},{26... | collective-permute-start | bytes 196616 | tf_op jit(solution)/shard_map/ppermute | solution.py:73
  22.8 3.3 %collective-permute-start.11 = (bf16[192,128]{1,0:T(8,128)(2,1)S(1)}, bf16[192,128]{1,0:T(8,128)(2,1)S(1)}, u32[]{:S(2)}, u32[]{:S(2)}) collective-permute-start(bf16[192,128]{1,0:T(8,128)(2,1)S(1)} %get-tuple-element.67), channel_id=1, source_target_pairs={{4,0},{0,4},{5,1},{1,5},{6,2},{2,6},{7,3},{3,7},{12,8},{8,12},{13,... | collective-permute-start | bytes 147464 | tf_op jit(solution)/shard_map/ppermute | solution.py:73
  23.3 5.5 %collective-permute-start.15 = (bf16[192,128]{1,0:T(8,128)(2,1)S(1)}, bf16[192,128]{1,0:T(8,128)(2,1)S(1)}, u32[]{:S(2)}, u32[]{:S(2)}) collective-permute-start(bf16[192,128]{1,0:T(8,128)(2,1)S(1)} %shard_map.140.refs_0_), channel_id=1, source_target_pairs={{1,0},{0,1},{3,2},{2,3},{5,4},{4,5},{7,6},{6,7},{9,8},{8,9},{11,10... | collective-permute-start | bytes 147464 | tf_op jit(solution)/shard_map/ppermute | solution.py:73
  27.4 5.4 %copy-start.8 = (bf16[3,3,128,128]{3,2,1,0:T(8,128)(2,1)S(1)}, bf16[3,3,128,128]{3,2,1,0:T(8,128)(2,1)}, u32[]{:S(2)}) copy-start(bf16[3,3,128,128]{3,2,1,0:T(8,128)(2,1)} %refs_4_.5) | copy-start | bytes 884740
  27.4 3.7 %collective-permute-start.14 = (bf16[192,128]{1,0:T(8,128)(2,1)S(1)}, bf16[192,128]{1,0:T(8,128)(2,1)S(1)}, u32[]{:S(2)}, u32[]{:S(2)}) collective-permute-start(bf16[192,128]{1,0:T(8,128)(2,1)S(1)} %shard_map.139.refs_0_), channel_id=1, source_target_pairs={{1,0},{0,1},{3,2},{2,3},{5,4},{4,5},{7,6},{6,7},{9,8},{8,9},{11,10... | collective-permute-start | bytes 147464 | tf_op jit(solution)/shard_map/ppermute | solution.py:73
  28.8 5.5 %collective-permute-start.17 = (bf16[192,128]{1,0:T(8,128)(2,1)S(1)}, bf16[192,128]{1,0:T(8,128)(2,1)S(1)}, u32[]{:S(2)}, u32[]{:S(2)}) collective-permute-start(bf16[192,128]{1,0:T(8,128)(2,1)S(1)} %shard_map.143.refs_2_), channel_id=1, source_target_pairs={{2,0},{3,1},{0,2},{1,3},{6,4},{7,5},{4,6},{5,7},{10,8},{11,9},{8,1... | collective-permute-start | bytes 147464 | tf_op jit(solution)/shard_map/ppermute | solution.py:73
  31.2 4.4 %collective-permute-start.16 = (bf16[192,128]{1,0:T(8,128)(2,1)S(1)}, bf16[192,128]{1,0:T(8,128)(2,1)S(1)}, u32[]{:S(2)}, u32[]{:S(2)}) collective-permute-start(bf16[192,128]{1,0:T(8,128)(2,1)S(1)} %shard_map.141.refs_5_.refs_0_), channel_id=1, source_target_pairs={{2,0},{3,1},{0,2},{1,3},{6,4},{7,5},{4,6},{5,7},{10,8},{11,9},{8,1... | collective-permute-start | bytes 147464 | tf_op jit(solution)/shard_map/ppermute | solution.py:73
  35.7 3.7 %collective-permute-start.20 = (bf16[2,224,128]{2,1,0:T(8,128)(2,1)S(1)}, bf16[2,224,128]{2,1,0:T(8,128)(2,1)S(1)}, u32[]{:S(2)}, u32[]{:S(2)}) collective-permute-start(bf16[2,224,128]{2,1,0:T(8,128)(2,1)S(1)} %get-tuple-element.76), channel_id=1, source_target_pairs={{4,0},{0,4},{5,1},{1,5},{6,2},{2,6},{7,3},{3,7},{12,8},{8,12},{13,... | collective-permute-start | bytes 344072 | tf_op jit(solution)/shard_map/ppermute | solution.py:73
  36.5 6.0 %collective-permute-start.18 = (bf16[2,208,128]{2,1,0:T(8,128)(2,1)S(1)}, bf16[2,208,128]{2,1,0:T(8,128)(2,1)S(1)}, u32[]{:S(2)}, u32[]{:S(2)}) collective-permute-start(bf16[2,208,128]{2,1,0:T(8,128)(2,1)S(1)} %get-tuple-element.74), channel_id=1, source_target_pairs={{20,0},{16,4},{28,8},{24,12},{4,16},{0,20},{12,24},{8,28},{21,1},{... | collective-permute-start | bytes 319496 | tf_op jit(solution)/shard_map/ppermute | solution.py:81
  37.8 6.4 %collective-permute-start.21 = (bf16[2,192,128]{2,1,0:T(8,128)(2,1)S(1)}, bf16[2,192,128]{2,1,0:T(8,128)(2,1)S(1)}, u32[]{:S(2)}, u32[]{:S(2)}) collective-permute-start(bf16[2,192,128]{2,1,0:T(8,128)(2,1)S(1)} %get-tuple-element.75.refs_0_), channel_id=1, source_target_pairs={{16,0},{24,8},{0,16},{8,24},{17,1},{25,9},{1,17},{9,25},{18,2},{26... | collective-permute-start | bytes 294920 | tf_op jit(solution)/shard_map/ppermute | solution.py:73
  39.4 6.8 %collective-permute-start.23 = (bf16[2,224,128]{2,1,0:T(8,128)(2,1)S(1)}, bf16[2,224,128]{2,1,0:T(8,128)(2,1)S(1)}, u32[]{:S(2)}, u32[]{:S(2)}) collective-permute-start(bf16[2,224,128]{2,1,0:T(8,128)(2,1)S(1)} %collective-permute-done.20.refs_1_), channel_id=1, source_target_pairs={{8,0},{0,8},{24,16},{16,24},{9,1},{1,9},{25,17},{17,25},{10,2},{2,... | collective-permute-start | bytes 344072 | tf_op jit(solution)/shard_map/ppermute | solution.py:73
  42.4 5.0 %collective-permute-start.19 = (bf16[2,208,128]{2,1,0:T(8,128)(2,1)S(1)}, bf16[2,208,128]{2,1,0:T(8,128)(2,1)S(1)}, u32[]{:S(2)}, u32[]{:S(2)}) collective-permute-start(bf16[2,208,128]{2,1,0:T(8,128)(2,1)S(1)} %collective-permute-done.18.refs_6_), channel_id=1, source_target_pairs={{8,0},{0,8},{24,16},{16,24},{9,1},{1,9},{25,17},{17,25},{10,2},{2,... | collective-permute-start | bytes 319496 | tf_op jit(solution)/shard_map/ppermute | solution.py:73
  44.3 1.3 %collective-permute-start.22 = (bf16[2,192,128]{2,1,0:T(8,128)(2,1)S(1)}, bf16[2,192,128]{2,1,0:T(8,128)(2,1)S(1)}, u32[]{:S(2)}, u32[]{:S(2)}) collective-permute-start(bf16[2,192,128]{2,1,0:T(8,128)(2,1)S(1)} %get-tuple-element.75.refs_0_), channel_id=1, source_target_pairs={{8,0},{0,8},{24,16},{16,24},{9,1},{1,9},{25,17},{17,25},{10,2},{2,... | collective-permute-start | bytes 294920 | tf_op jit(solution)/shard_map/ppermute | solution.py:73
  44.3 1.9 %collective-permute-start.24 = (bf16[2,192,128]{2,1,0:T(8,128)(2,1)S(1)}, bf16[2,192,128]{2,1,0:T(8,128)(2,1)S(1)}, u32[]{:S(2)}, u32[]{:S(2)}) collective-permute-start(bf16[2,192,128]{2,1,0:T(8,128)(2,1)S(1)} %collective-permute-done.21.refs_2_), channel_id=1, source_target_pairs={{8,0},{0,8},{24,16},{16,24},{9,1},{1,9},{25,17},{17,25},{10,2},{2,... | collective-permute-start | bytes 294920 | tf_op jit(solution)/shard_map/ppermute | solution.py:73
  (2 other events, 6.1 us)

commit v22 on v17

--- a/solution.py
+++ b/solution.py
@@ -522,7 +522,7 @@
             return [flipped(x, "video", 1)]
         return [from_ahead(x, 0, n + 1) for n in range(later)]
 
-    wholes = from_later(grad)
+    wholes = [from_ahead(grad, 0, n + 1) for n in range(later)]
     packs = call(
         pack_kernel,
         [bf16(4, cols, ch)] * 2,

time: 47.1 us -> 49 us (1.040)
  starting transfers between devices: 30.4 us -> 31.9 us
    ppermute x0 -> x1, starting transfers between devices: none -> 1.29 us  [from_ahead(): return lax.ppermute(block, ('section', 'video'), pairs)]
    ppermute x23 -> x22, waiting for transfers between devices: 6.33 us -> 6.7 us  [flipped(): lax.ppermute(block, axis, [(place ^ flip, place) for place in range(count)])]
    ppermute x23 -> x22, starting transfers between devices: 27.2 us -> 27.5 us  [flipped(): lax.ppermute(block, axis, [(place ^ flip, place) for place in range(count)])]
  transfers between devices with their start and end apart: 25 -> 25, of which waited for: 6 -> 6; matrix products, arithmetic and copies ran while one was open for 0% -> 0% of each run, Pallas kernels for 18% -> 17%
where the time goes in v22:
time: 49 us; the launch traced here: 48.7 us
  starting transfers between devices  31.9 us (65%)
  Pallas kernels  9.23 us (19%)
  waiting for transfers between devices  6.7 us (14%)
  between operations  0.87 us (2%)
    ppermute x22, starting transfers between devices, flipped(): lax.ppermute(block, axis, [(place ^ flip, place) for place in range(count)])  27.5 us
    pallas_call x17, Pallas kernels, call(): pl.pallas_call(body, out_shape=outs[0] if single else tuple(outs), in_spe...  7.33 us
    ppermute x22, waiting for transfers between devices, flipped(): lax.ppermute(block, axis, [(place ^ flip, place) for place in range(count)])  6.7 us
    ppermute x2, starting transfers between devices, flipped_both(): return lax.ppermute(block, ('section', 'video'), pairs)  3.11 us
    pallas_call x2, Pallas kernels, placed(): pl.pallas_call(functools.partial(place_kernel, places), out_shape=outs, i...  1.91 us
    ppermute x1, starting transfers between devices, from_ahead(): return lax.ppermute(block, ('section', 'video'), pairs)  1.29 us
  transfers between devices with their start and end apart: 25, of which 6 were waited for; matrix products, arithmetic and copies ran while one was open for 0% of the time, Pallas kernels for 17%

profile of v22, /device:TPU:1, one launch (start us, length us, event | category | flops | bytes accessed | tf_op | source)
XLA Modules:
  0.0 48.7 jit_solution(16953886008071949862)
XLA Ops:
  0.6 1.3 %collective-permute-start.3 = (bf16[16,64,128]{2,1,0:T(8,128)(2,1)}, bf16[16,64,128]{2,1,0:T(8,128)(2,1)S(1)}, u32[]{:S(2)}, u32[]{:S(2)}) collective-permute-start(bf16[16,64,128]{2,1,0:T(8,128)(2,1)} %bitcast.10), channel_id=1, source_target_pairs={{4,0},{12,8},{20,16},{28,24},{5,1},{13,9},{21,17},{29,25},{6,2},{1... | collective-permute-start | bytes 786440 | tf_op jit(solution)/shard_map/ppermute | solution.py:59
  2.0 1.6 %shard_map.128 = (bf16[4,64,128]{2,1,0:T(8,128)(2,1)}, bf16[4,64,128]{2,1,0:T(8,128)(2,1)}) custom-call(bf16[16,64,128]{2,1,0:T(8,128)(2,1)} %bitcast.11, bf16[16,64,128]{2,1,0:T(8,128)(2,1)} %bitcast.17, bf16[16,64,128]{2,1,0:T(8,128)(2,1)} %bitcast.28, bf16[16,64,128]{2,1,0:T(8,128)(2,1)} %bitcast.25), custom_call_target="tpu_custom_call" | custom-call | flops 1 | bytes 1179648 | tf_op jit(solution)/shard_map/pallas_call | solution.py:38
  3.7 1.4 %collective-permute-done.refs_5_ = bf16[4,64,128]{2,1,0:T(8,128)(2,1)S(1)} collective-permute-done((bf16[4,64,128]{2,1,0:T(8,128)(2,1)}, bf16[4,64,128]{2,1,0:T(8,128)(2,1)S(1)}, u32[]{:S(2)}, u32[]{:S(2)}) %collective-permute-start) | collective-permute-done | bytes 65568 | tf_op jit(solution)/shard_map/ppermute | solution.py:73
  5.3 2.6 %collective-permute-start.2 = (bf16[4,64,128]{2,1,0:T(8,128)(2,1)S(1)}, bf16[4,64,128]{2,1,0:T(8,128)(2,1)S(1)}, u32[]{:S(2)}, u32[]{:S(2)}) collective-permute-start(bf16[4,64,128]{2,1,0:T(8,128)(2,1)S(1)} %collective-permute-done.refs_5_), channel_id=1, source_target_pairs={{16,0},{24,8},{0,16},{8,24},{17,1},{25,9},{1,17},{9,25},{18,2},{26... | collective-permute-start | bytes 196616 | tf_op jit(solution)/shard_map/ppermute | solution.py:73
  8.0 3.4 %collective-permute-start.4 = (bf16[14,64,128]{2,1,0:T(8,128)(2,1)S(1)}, bf16[14,64,128]{2,1,0:T(8,128)(2,1)S(1)}, u32[]{:S(2)}, u32[]{:S(2)}) collective-permute-start(bf16[14,64,128]{2,1,0:T(8,128)(2,1)S(1)} %get-tuple-element.45.refs_5_), channel_id=1, source_target_pairs={{4,0},{0,4},{5,1},{1,5},{6,2},{2,6},{7,3},{3,7},{12,8},{8,12},{13,... | collective-permute-start | bytes 688136 | tf_op jit(solution)/shard_map/ppermute | solution.py:73
  11.4 1.0 %shard_map.130 = (bf16[14,64,128]{2,1,0:T(8,128)(2,1)S(1)}, bf16[16,64,128]{2,1,0:T(8,128)(2,1)S(1)}) custom-call(bf16[16,64,128]{2,1,0:T(8,128)(2,1)S(1)} %bitcast.13, bf16[16,64,128]{2,1,0:T(8,128)(2,1)S(1)} %bitcast.19, bf16[16,64,128]{2,1,0:T(8,128)(2,1)S(1)} %collective-permute-done.3.refs_2_.refs_6_, bf16[3,128,128]{2,1,0:T(8,128)(2,1)S(1)} %copy-done.6, ...), custom_call_target="tpu_custom_call" | custom-call | tf_op jit(solution)/shard_map/pallas_call | solution.py:38
  12.5 0.9 %shard_map.132 = (f32[2,384,128]{2,1,0:T(8,128)S(1)}, bf16[384,128]{1,0:T(8,128)(2,1)S(1)}, bf16[384,128]{1,0:T(8,128)(2,1)S(1)}) custom-call(bf16[16,64,128]{2,1,0:T(8,128)(2,1)S(1)} %bitcast.30, bf16[16,64,128]{2,1,0:T(8,128)(2,1)S(1)} %bitcast.20, bf16[16,64,128]{2,1,0:T(8,128)(2,1)S(1)} %get-tuple-element.48.refs_6_.refs_2_.refs_4_, ...), custom_call_target="tpu_custom_call" | custom-call | flops 2415919104 | bytes 2031616 | tf_op jit(solution)/shard_map/pallas_call | solution.py:38
  13.4 0.8 %collective-permute-start.6 = (bf16[384,128]{1,0:T(8,128)(2,1)S(1)}, bf16[384,128]{1,0:T(8,128)(2,1)S(1)}, u32[]{:S(2)}, u32[]{:S(2)}) collective-permute-start(bf16[384,128]{1,0:T(8,128)(2,1)S(1)} %get-tuple-element.52), channel_id=1, source_target_pairs={{8,0},{0,8},{24,16},{16,24},{9,1},{1,9},{25,17},{17,25},{10,2},{2,... | collective-permute-start | bytes 294920 | tf_op jit(solution)/shard_map/ppermute | solution.py:73
  14.2 0.6 %collective-permute-start.5 = (bf16[4,64,128]{2,1,0:T(8,128)(2,1)S(1)}, bf16[4,64,128]{2,1,0:T(8,128)(2,1)S(1)}, u32[]{:S(2)}, u32[]{:S(2)}) collective-permute-start(bf16[4,64,128]{2,1,0:T(8,128)(2,1)S(1)} %shard_map.131.refs_7_), channel_id=1, source_target_pairs={{4,0},{0,4},{5,1},{1,5},{6,2},{2,6},{7,3},{3,7},{12,8},{8,12},{13,... | collective-permute-start | bytes 196616 | tf_op jit(solution)/shard_map/ppermute | solution.py:73
  15.5 1.4 %collective-permute-start.8 = (bf16[384,128]{1,0:T(8,128)(2,1)S(1)}, bf16[384,128]{1,0:T(8,128)(2,1)S(1)}, u32[]{:S(2)}, u32[]{:S(2)}) collective-permute-start(bf16[384,128]{1,0:T(8,128)(2,1)S(1)} %get-tuple-element.58), channel_id=1, source_target_pairs={{16,0},{24,8},{0,16},{8,24},{17,1},{25,9},{1,17},{9,25},{18,2},{26... | collective-permute-start | bytes 294920 | tf_op jit(solution)/shard_map/ppermute | solution.py:73
  17.4 1.0 %collective-permute-done.5.refs_6_ = bf16[4,64,128]{2,1,0:T(8,128)(2,1)S(1)} collective-permute-done((bf16[4,64,128]{2,1,0:T(8,128)(2,1)S(1)}, bf16[4,64,128]{2,1,0:T(8,128)(2,1)S(1)}, u32[]{:S(2)}, u32[]{:S(2)}) %collective-permute-start.5) | collective-permute-done | bytes 65568 | tf_op jit(solution)/shard_map/ppermute | solution.py:73
  18.4 1.3 %shard_map.136 = (bf16[16,64,128]{2,1,0:T(8,128)(2,1)S(1)}, bf16[16,64,128]{2,1,0:T(8,128)(2,1)S(1)}, f32[2,384,128]{2,1,0:T(8,128)S(1)}, bf16[896,128]{1,0:T(8,128)(2,1)S(1)}) custom-call(bf16[16,64,128]{2,1,0:T(8,128)(2,1)S(1)} %bitcast.16, bf16[4,64,128]{2,1,0:T(8,128)(2,1)S(1)} %collective-permute-done.1.refs_4_.refs_1_.refs_3_.refs_2_, ...), custom_call_target="tpu_custom_call" | custom-call | flops 2415919104 | bytes 5046272 | tf_op jit(solution)/shard_map/pallas_call | solution.py:38
  19.7 1.1 %collective-permute-start.9 = (bf16[896,128]{1,0:T(8,128)(2,1)S(1)}, bf16[896,128]{1,0:T(8,128)(2,1)S(1)}, u32[]{:S(2)}, u32[]{:S(2)}) collective-permute-start(bf16[896,128]{1,0:T(8,128)(2,1)S(1)} %get-tuple-element.59), channel_id=1, source_target_pairs={{8,0},{0,8},{24,16},{16,24},{9,1},{1,9},{25,17},{17,25},{10,2},{2,... | collective-permute-start | bytes 688136 | tf_op jit(solution)/shard_map/ppermute | solution.py:73
  20.8 1.5 %collective-permute-start.13 = (bf16[320,128]{1,0:T(8,128)(2,1)S(1)}, bf16[320,128]{1,0:T(8,128)(2,1)S(1)}, u32[]{:S(2)}, u32[]{:S(2)}) collective-permute-start(bf16[320,128]{1,0:T(8,128)(2,1)S(1)} %get-tuple-element.61.refs_2_), channel_id=1, source_target_pairs={{4,0},{0,4},{5,1},{1,5},{6,2},{2,6},{7,3},{3,7},{12,8},{8,12},{13,... | collective-permute-start | bytes 245768 | tf_op jit(solution)/shard_map/ppermute | solution.py:73
  22.4 1.9 %collective-permute-start.12 = (bf16[272,128]{1,0:T(8,128)(2,1)S(1)}, bf16[272,128]{1,0:T(8,128)(2,1)S(1)}, u32[]{:S(2)}, u32[]{:S(2)}) collective-permute-start(bf16[272,128]{1,0:T(8,128)(2,1)S(1)} %get-tuple-element.65), channel_id=1, source_target_pairs={{20,0},{16,4},{28,8},{24,12},{4,16},{0,20},{12,24},{8,28},{21,1},{... | collective-permute-start | bytes 208904 | tf_op jit(solution)/shard_map/ppermute | solution.py:81
  25.1 1.4 %collective-permute-start.15 = (bf16[192,128]{1,0:T(8,128)(2,1)S(1)}, bf16[192,128]{1,0:T(8,128)(2,1)S(1)}, u32[]{:S(2)}, u32[]{:S(2)}) collective-permute-start(bf16[192,128]{1,0:T(8,128)(2,1)S(1)} %shard_map.140.refs_0_), channel_id=1, source_target_pairs={{1,0},{0,1},{3,2},{2,3},{5,4},{4,5},{7,6},{6,7},{9,8},{8,9},{11,10... | collective-permute-start | bytes 147464 | tf_op jit(solution)/shard_map/ppermute | solution.py:73
  26.5 1.5 %collective-permute-done.11.refs_2_ = bf16[192,128]{1,0:T(8,128)(2,1)S(1)} collective-permute-done((bf16[192,128]{1,0:T(8,128)(2,1)S(1)}, bf16[192,128]{1,0:T(8,128)(2,1)S(1)}, u32[]{:S(2)}, u32[]{:S(2)}) %collective-permute-start.11) | collective-permute-done | bytes 49184 | tf_op jit(solution)/shard_map/ppermute | solution.py:73
  27.9 1.2 %collective-permute-done.10.refs_1_.refs_3_ = bf16[256,128]{1,0:T(8,128)(2,1)S(1)} collective-permute-done((bf16[256,128]{1,0:T(8,128)(2,1)S(1)}, bf16[256,128]{1,0:T(8,128)(2,1)S(1)}, u32[]{:S(2)}, u32[]{:S(2)}) %collective-permute-start.10) | collective-permute-done | bytes 65568 | tf_op jit(solution)/shard_map/ppermute | solution.py:73
  29.2 1.4 %collective-permute-start.14 = (bf16[192,128]{1,0:T(8,128)(2,1)S(1)}, bf16[192,128]{1,0:T(8,128)(2,1)S(1)}, u32[]{:S(2)}, u32[]{:S(2)}) collective-permute-start(bf16[192,128]{1,0:T(8,128)(2,1)S(1)} %shard_map.139.refs_0_), channel_id=1, source_target_pairs={{1,0},{0,1},{3,2},{2,3},{5,4},{4,5},{7,6},{6,7},{9,8},{8,9},{11,10... | collective-permute-start | bytes 147464 | tf_op jit(solution)/shard_map/ppermute | solution.py:73
  30.6 2.4 %collective-permute-start.17 = (bf16[192,128]{1,0:T(8,128)(2,1)S(1)}, bf16[192,128]{1,0:T(8,128)(2,1)S(1)}, u32[]{:S(2)}, u32[]{:S(2)}) collective-permute-start(bf16[192,128]{1,0:T(8,128)(2,1)S(1)} %shard_map.143.refs_2_), channel_id=1, source_target_pairs={{2,0},{3,1},{0,2},{1,3},{6,4},{7,5},{4,6},{5,7},{10,8},{11,9},{8,1... | collective-permute-start | bytes 147464 | tf_op jit(solution)/shard_map/ppermute | solution.py:73
  33.0 1.6 %collective-permute-start.16 = (bf16[192,128]{1,0:T(8,128)(2,1)S(1)}, bf16[192,128]{1,0:T(8,128)(2,1)S(1)}, u32[]{:S(2)}, u32[]{:S(2)}) collective-permute-start(bf16[192,128]{1,0:T(8,128)(2,1)S(1)} %shard_map.141.refs_5_.refs_0_), channel_id=1, source_target_pairs={{2,0},{3,1},{0,2},{1,3},{6,4},{7,5},{4,6},{5,7},{10,8},{11,9},{8,1... | collective-permute-start | bytes 147464 | tf_op jit(solution)/shard_map/ppermute | solution.py:73
  34.6 1.5 %shard_map.142 = (bf16[16,64,128]{2,1,0:T(8,128)(2,1)}, f32[8,128]{1,0:T(8,128)S(1)}) custom-call(bf16[16,64,128]{2,1,0:T(8,128)(2,1)S(1)} %get-tuple-element.55.refs_0_, bf16[16,64,128]{2,1,0:T(8,128)(2,1)S(1)} %get-tuple-element.56.refs_1_, bf16[896,128]{1,0:T(8,128)(2,1)S(1)} %collective-permute-done.9.refs_1_.refs_2_, ...), custom_call_target="tpu_custom_call" | custom-call | flops 301989888 | bytes 1380352 | tf_op jit(solution)/shard_map/pallas_call | solution.py:38
  36.1 1.3 %collective-permute-done.16.refs_1_ = bf16[192,128]{1,0:T(8,128)(2,1)S(1)} collective-permute-done((bf16[192,128]{1,0:T(8,128)(2,1)S(1)}, bf16[192,128]{1,0:T(8,128)(2,1)S(1)}, u32[]{:S(2)}, u32[]{:S(2)}) %collective-permute-start.16) | collective-permute-done | bytes 49184 | tf_op jit(solution)/shard_map/ppermute | solution.py:73
  37.4 0.9 %collective-permute-start.20 = (bf16[2,192,128]{2,1,0:T(8,128)(2,1)S(1)}, bf16[2,192,128]{2,1,0:T(8,128)(2,1)S(1)}, u32[]{:S(2)}, u32[]{:S(2)}) collective-permute-start(bf16[2,192,128]{2,1,0:T(8,128)(2,1)S(1)} %shard_map.144.refs_0_), channel_id=1, source_target_pairs={{4,0},{0,4},{5,1},{1,5},{6,2},{2,6},{7,3},{3,7},{12,8},{8,12},{13,... | collective-permute-start | bytes 294920 | tf_op jit(solution)/shard_map/ppermute | solution.py:73
  38.4 0.6 %collective-permute-start.21 = (bf16[2,192,128]{2,1,0:T(8,128)(2,1)S(1)}, bf16[2,192,128]{2,1,0:T(8,128)(2,1)S(1)}, u32[]{:S(2)}, u32[]{:S(2)}) collective-permute-start(bf16[2,192,128]{2,1,0:T(8,128)(2,1)S(1)} %shard_map.144.refs_0_), channel_id=1, source_target_pairs={{16,0},{24,8},{0,16},{8,24},{17,1},{25,9},{1,17},{9,25},{18,2},{26... | collective-permute-start | bytes 294920 | tf_op jit(solution)/shard_map/ppermute | solution.py:73
  38.9 1.2 %collective-permute-start.18 = (bf16[2,192,128]{2,1,0:T(8,128)(2,1)S(1)}, bf16[2,192,128]{2,1,0:T(8,128)(2,1)S(1)}, u32[]{:S(2)}, u32[]{:S(2)}) collective-permute-start(bf16[2,192,128]{2,1,0:T(8,128)(2,1)S(1)} %shard_map.144.refs_0_), channel_id=1, source_target_pairs={{20,0},{16,4},{28,8},{24,12},{4,16},{0,20},{12,24},{8,28},{21,1},{... | collective-permute-start | bytes 294920 | tf_op jit(solution)/shard_map/ppermute | solution.py:81
  40.2 2.6 %collective-permute-start.22 = (bf16[2,192,128]{2,1,0:T(8,128)(2,1)S(1)}, bf16[2,192,128]{2,1,0:T(8,128)(2,1)S(1)}, u32[]{:S(2)}, u32[]{:S(2)}) collective-permute-start(bf16[2,192,128]{2,1,0:T(8,128)(2,1)S(1)} %shard_map.144.refs_0_), channel_id=1, source_target_pairs={{8,0},{0,8},{24,16},{16,24},{9,1},{1,9},{25,17},{17,25},{10,2},{2,... | collective-permute-start | bytes 294920 | tf_op jit(solution)/shard_map/ppermute | solution.py:73
  42.8 2.0 %collective-permute-start.23 = (bf16[2,192,128]{2,1,0:T(8,128)(2,1)S(1)}, bf16[2,192,128]{2,1,0:T(8,128)(2,1)S(1)}, u32[]{:S(2)}, u32[]{:S(2)}) collective-permute-start(bf16[2,192,128]{2,1,0:T(8,128)(2,1)S(1)} %collective-permute-done.20.refs_1_), channel_id=1, source_target_pairs={{8,0},{0,8},{24,16},{16,24},{9,1},{1,9},{25,17},{17,25},{10,2},{2,... | collective-permute-start | bytes 294920 | tf_op jit(solution)/shard_map/ppermute | solution.py:73
  44.8 0.5 %collective-permute-start.24 = (bf16[2,192,128]{2,1,0:T(8,128)(2,1)S(1)}, bf16[2,192,128]{2,1,0:T(8,128)(2,1)S(1)}, u32[]{:S(2)}, u32[]{:S(2)}) collective-permute-start(bf16[2,192,128]{2,1,0:T(8,128)(2,1)S(1)} %collective-permute-done.21.refs_2_), channel_id=1, source_target_pairs={{8,0},{0,8},{24,16},{16,24},{9,1},{1,9},{25,17},{17,25},{10,2},{2,... | collective-permute-start | bytes 294920 | tf_op jit(solution)/shard_map/ppermute | solution.py:73
  45.3 1.5 %collective-permute-start.19 = (bf16[2,192,128]{2,1,0:T(8,128)(2,1)S(1)}, bf16[2,192,128]{2,1,0:T(8,128)(2,1)S(1)}, u32[]{:S(2)}, u32[]{:S(2)}) collective-permute-start(bf16[2,192,128]{2,1,0:T(8,128)(2,1)S(1)} %collective-permute-done.18.refs_6_), channel_id=1, source_target_pairs={{8,0},{0,8},{24,16},{16,24},{9,1},{1,9},{25,17},{17,25},{10,2},{2,... | collective-permute-start | bytes 294920 | tf_op jit(solution)/shard_map/ppermute | solution.py:73
  46.8 1.2 %shard_map.145 = (f32[3,384,128]{2,1,0:T(8,128)}, f32[384,128]{1,0:T(8,128)}, f32[3,384,128]{2,1,0:T(8,128)}, f32[384,128]{1,0:T(8,128)}) custom-call(bf16[2,192,128]{2,1,0:T(8,128)(2,1)S(1)} %shard_map.144.refs_0_, bf16[2,192,128]{2,1,0:T(8,128)(2,1)S(1)} %collective-permute-done.20.refs_1_, bf16[2,192,128]{2,1,0:T(8,128)(2,1)S(1)} %collective-permute-done.21.refs_2_, ...), custom_call_target="tpu_custom_call" | custom-call | bytes 2064384 | tf_op jit(solution)/shard_map/pallas_call | solution.py:467
  48.0 0.7 %shard_map.146 = (f32[3,384,128]{2,1,0:T(8,128)}, f32[384,128]{1,0:T(8,128)}, f32[3,384,128]{2,1,0:T(8,128)}, f32[384,128]{1,0:T(8,128)}) custom-call(bf16[2,192,128]{2,1,0:T(8,128)(2,1)S(1)} %collective-permute-done.19.refs_0_, f32[3,384,128]{2,1,0:T(8,128)} %get-tuple-element.71.refs_1_, ...), custom_call_target="tpu_custom_call", output_to_operand_aliasing={{0}: (1, {}), {1}: (2, {}), {2}: (3, {}), {3}: (4, {})} | custom-call | bytes 294912 | tf_op jit(solution)/shard_map/pallas_call | solution.py:467
  (55 shorter events, 2.7 us)
Async XLA Ops:
  0.6 10.8 %collective-permute-start.3 = (bf16[16,64,128]{2,1,0:T(8,128)(2,1)}, bf16[16,64,128]{2,1,0:T(8,128)(2,1)S(1)}, u32[]{:S(2)}, u32[]{:S(2)}) collective-permute-start(bf16[16,64,128]{2,1,0:T(8,128)(2,1)} %bitcast.10), channel_id=1, source_target_pairs={{4,0},{12,8},{20,16},{28,24},{5,1},{13,9},{21,17},{29,25},{6,2},{1... | collective-permute-start | bytes 786440 | tf_op jit(solution)/shard_map/ppermute | solution.py:59
  1.9 6.0 %copy-start = (bf16[1,1,16,64,128]{4,3,2,1,0:T(8,128)(2,1)S(1)}, bf16[1,1,16,64,128]{4,3,2,1,0:T(8,128)(2,1)}, u32[]{:S(2)}) copy-start(bf16[1,1,16,64,128]{4,3,2,1,0:T(8,128)(2,1)} %param.9) | copy-start | bytes 786436
  1.9 6.0 %copy-start.1 = (bf16[3,3,128,128]{3,2,1,0:T(8,128)(2,1)S(1)}, bf16[3,3,128,128]{3,2,1,0:T(8,128)(2,1)}, u32[]{:S(2)}) copy-start(bf16[3,3,128,128]{3,2,1,0:T(8,128)(2,1)} %refs_8_.1) | copy-start | bytes 884740
  2.0 6.0 %copy-start.2 = (bf16[1,1,16,64,128]{4,3,2,1,0:T(8,128)(2,1)S(1)}, bf16[1,1,16,64,128]{4,3,2,1,0:T(8,128)(2,1)}, u32[]{:S(2)}) copy-start(bf16[1,1,16,64,128]{4,3,2,1,0:T(8,128)(2,1)} %param.13) | copy-start | bytes 786436
  3.6 1.5 %collective-permute-start = (bf16[4,64,128]{2,1,0:T(8,128)(2,1)}, bf16[4,64,128]{2,1,0:T(8,128)(2,1)S(1)}, u32[]{:S(2)}, u32[]{:S(2)}) collective-permute-start(bf16[4,64,128]{2,1,0:T(8,128)(2,1)} %get-tuple-element.43), channel_id=1, source_target_pairs={{8,0},{0,8},{24,16},{16,24},{9,1},{1,9},{25,17},{17,25},{10,2},{2,... | collective-permute-start | bytes 196616 | tf_op jit(solution)/shard_map/ppermute | solution.py:73
  5.1 6.3 %copy-start.3 = (bf16[1,1,16,64,128]{4,3,2,1,0:T(8,128)(2,1)S(1)}, bf16[1,1,16,64,128]{4,3,2,1,0:T(8,128)(2,1)}, u32[]{:S(2)}) copy-start(bf16[1,1,16,64,128]{4,3,2,1,0:T(8,128)(2,1)} %param.11) | copy-start | bytes 786436
  5.1 6.3 %copy-start.4 = (bf16[1,1,16,64,128]{4,3,2,1,0:T(8,128)(2,1)S(1)}, bf16[1,1,16,64,128]{4,3,2,1,0:T(8,128)(2,1)}, u32[]{:S(2)}) copy-start(bf16[1,1,16,64,128]{4,3,2,1,0:T(8,128)(2,1)} %param.10) | copy-start | bytes 786436
  5.1 6.3 %copy-start.5 = (bf16[1,1,16,64,128]{4,3,2,1,0:T(8,128)(2,1)S(1)}, bf16[1,1,16,64,128]{4,3,2,1,0:T(8,128)(2,1)}, u32[]{:S(2)}) copy-start(bf16[1,1,16,64,128]{4,3,2,1,0:T(8,128)(2,1)} %param.12) | copy-start | bytes 786436
  5.1 6.3 %copy-start.7 = (bf16[3,128,128]{2,1,0:T(8,128)(2,1)S(1)}, bf16[3,128,128]{2,1,0:T(8,128)(2,1)}, u32[]{:S(2)}) copy-start(bf16[3,128,128]{2,1,0:T(8,128)(2,1)} %refs_11_.1) | copy-start | bytes 294916
  5.1 2.8 %collective-permute-start.1 = (bf16[4,64,128]{2,1,0:T(8,128)(2,1)}, bf16[4,64,128]{2,1,0:T(8,128)(2,1)S(1)}, u32[]{:S(2)}, u32[]{:S(2)}) collective-permute-start(bf16[4,64,128]{2,1,0:T(8,128)(2,1)} %get-tuple-element.44), channel_id=1, source_target_pairs={{8,0},{0,8},{24,16},{16,24},{9,1},{1,9},{25,17},{17,25},{10,2},{2,... | collective-permute-start | bytes 196616 | tf_op jit(solution)/shard_map/ppermute | solution.py:73
  5.3 7.1 %collective-permute-start.2 = (bf16[4,64,128]{2,1,0:T(8,128)(2,1)S(1)}, bf16[4,64,128]{2,1,0:T(8,128)(2,1)S(1)}, u32[]{:S(2)}, u32[]{:S(2)}) collective-permute-start(bf16[4,64,128]{2,1,0:T(8,128)(2,1)S(1)} %collective-permute-done.refs_5_), channel_id=1, source_target_pairs={{16,0},{24,8},{0,16},{8,24},{17,1},{25,9},{1,17},{9,25},{18,2},{26... | collective-permute-start | bytes 196616 | tf_op jit(solution)/shard_map/ppermute | solution.py:73
  8.0 9.0 %collective-permute-start.4 = (bf16[14,64,128]{2,1,0:T(8,128)(2,1)S(1)}, bf16[14,64,128]{2,1,0:T(8,128)(2,1)S(1)}, u32[]{:S(2)}, u32[]{:S(2)}) collective-permute-start(bf16[14,64,128]{2,1,0:T(8,128)(2,1)S(1)} %get-tuple-element.45.refs_5_), channel_id=1, source_target_pairs={{4,0},{0,4},{5,1},{1,5},{6,2},{2,6},{7,3},{3,7},{12,8},{8,12},{13,... | collective-permute-start | bytes 688136 | tf_op jit(solution)/shard_map/ppermute | solution.py:73
  13.4 1.8 %collective-permute-start.6 = (bf16[384,128]{1,0:T(8,128)(2,1)S(1)}, bf16[384,128]{1,0:T(8,128)(2,1)S(1)}, u32[]{:S(2)}, u32[]{:S(2)}) collective-permute-start(bf16[384,128]{1,0:T(8,128)(2,1)S(1)} %get-tuple-element.52), channel_id=1, source_target_pairs={{8,0},{0,8},{24,16},{16,24},{9,1},{1,9},{25,17},{17,25},{10,2},{2,... | collective-permute-start | bytes 294920 | tf_op jit(solution)/shard_map/ppermute | solution.py:73
  14.1 1.3 %collective-permute-start.7 = (bf16[384,128]{1,0:T(8,128)(2,1)S(1)}, bf16[384,128]{1,0:T(8,128)(2,1)S(1)}, u32[]{:S(2)}, u32[]{:S(2)}) collective-permute-start(bf16[384,128]{1,0:T(8,128)(2,1)S(1)} %get-tuple-element.53), channel_id=1, source_target_pairs={{8,0},{0,8},{24,16},{16,24},{9,1},{1,9},{25,17},{17,25},{10,2},{2,... | collective-permute-start | bytes 294920 | tf_op jit(solution)/shard_map/ppermute | solution.py:73
  14.2 4.2 %collective-permute-start.5 = (bf16[4,64,128]{2,1,0:T(8,128)(2,1)S(1)}, bf16[4,64,128]{2,1,0:T(8,128)(2,1)S(1)}, u32[]{:S(2)}, u32[]{:S(2)}) collective-permute-start(bf16[4,64,128]{2,1,0:T(8,128)(2,1)S(1)} %shard_map.131.refs_7_), channel_id=1, source_target_pairs={{4,0},{0,4},{5,1},{1,5},{6,2},{2,6},{7,3},{3,7},{12,8},{8,12},{13,... | collective-permute-start | bytes 196616 | tf_op jit(solution)/shard_map/ppermute | solution.py:73
  15.5 4.2 %collective-permute-start.8 = (bf16[384,128]{1,0:T(8,128)(2,1)S(1)}, bf16[384,128]{1,0:T(8,128)(2,1)S(1)}, u32[]{:S(2)}, u32[]{:S(2)}) collective-permute-start(bf16[384,128]{1,0:T(8,128)(2,1)S(1)} %get-tuple-element.58), channel_id=1, source_target_pairs={{16,0},{24,8},{0,16},{8,24},{17,1},{25,9},{1,17},{9,25},{18,2},{26... | collective-permute-start | bytes 294920 | tf_op jit(solution)/shard_map/ppermute | solution.py:73
  19.7 2.6 %collective-permute-start.9 = (bf16[896,128]{1,0:T(8,128)(2,1)S(1)}, bf16[896,128]{1,0:T(8,128)(2,1)S(1)}, u32[]{:S(2)}, u32[]{:S(2)}) collective-permute-start(bf16[896,128]{1,0:T(8,128)(2,1)S(1)} %get-tuple-element.59), channel_id=1, source_target_pairs={{8,0},{0,8},{24,16},{16,24},{9,1},{1,9},{25,17},{17,25},{10,2},{2,... | collective-permute-start | bytes 688136 | tf_op jit(solution)/shard_map/ppermute | solution.py:73
  20.8 4.3 %collective-permute-start.13 = (bf16[320,128]{1,0:T(8,128)(2,1)S(1)}, bf16[320,128]{1,0:T(8,128)(2,1)S(1)}, u32[]{:S(2)}, u32[]{:S(2)}) collective-permute-start(bf16[320,128]{1,0:T(8,128)(2,1)S(1)} %get-tuple-element.61.refs_2_), channel_id=1, source_target_pairs={{4,0},{0,4},{5,1},{1,5},{6,2},{2,6},{7,3},{3,7},{12,8},{8,12},{13,... | collective-permute-start | bytes 245768 | tf_op jit(solution)/shard_map/ppermute | solution.py:73
  22.4 6.8 %collective-permute-start.12 = (bf16[272,128]{1,0:T(8,128)(2,1)S(1)}, bf16[272,128]{1,0:T(8,128)(2,1)S(1)}, u32[]{:S(2)}, u32[]{:S(2)}) collective-permute-start(bf16[272,128]{1,0:T(8,128)(2,1)S(1)} %get-tuple-element.65), channel_id=1, source_target_pairs={{20,0},{16,4},{28,8},{24,12},{4,16},{0,20},{12,24},{8,28},{21,1},{... | collective-permute-start | bytes 208904 | tf_op jit(solution)/shard_map/ppermute | solution.py:81
  24.3 4.9 %collective-permute-start.10 = (bf16[256,128]{1,0:T(8,128)(2,1)S(1)}, bf16[256,128]{1,0:T(8,128)(2,1)S(1)}, u32[]{:S(2)}, u32[]{:S(2)}) collective-permute-start(bf16[256,128]{1,0:T(8,128)(2,1)S(1)} %get-tuple-element.62), channel_id=1, source_target_pairs={{16,0},{24,8},{0,16},{8,24},{17,1},{25,9},{1,17},{9,25},{18,2},{26... | collective-permute-start | bytes 196616 | tf_op jit(solution)/shard_map/ppermute | solution.py:73
  24.7 3.3 %collective-permute-start.11 = (bf16[192,128]{1,0:T(8,128)(2,1)S(1)}, bf16[192,128]{1,0:T(8,128)(2,1)S(1)}, u32[]{:S(2)}, u32[]{:S(2)}) collective-permute-start(bf16[192,128]{1,0:T(8,128)(2,1)S(1)} %get-tuple-element.64), channel_id=1, source_target_pairs={{4,0},{0,4},{5,1},{1,5},{6,2},{2,6},{7,3},{3,7},{12,8},{8,12},{13,... | collective-permute-start | bytes 147464 | tf_op jit(solution)/shard_map/ppermute | solution.py:73
  25.1 5.4 %collective-permute-start.15 = (bf16[192,128]{1,0:T(8,128)(2,1)S(1)}, bf16[192,128]{1,0:T(8,128)(2,1)S(1)}, u32[]{:S(2)}, u32[]{:S(2)}) collective-permute-start(bf16[192,128]{1,0:T(8,128)(2,1)S(1)} %shard_map.140.refs_0_), channel_id=1, source_target_pairs={{1,0},{0,1},{3,2},{2,3},{5,4},{4,5},{7,6},{6,7},{9,8},{8,9},{11,10... | collective-permute-start | bytes 147464 | tf_op jit(solution)/shard_map/ppermute | solution.py:73
  29.2 3.7 %collective-permute-start.14 = (bf16[192,128]{1,0:T(8,128)(2,1)S(1)}, bf16[192,128]{1,0:T(8,128)(2,1)S(1)}, u32[]{:S(2)}, u32[]{:S(2)}) collective-permute-start(bf16[192,128]{1,0:T(8,128)(2,1)S(1)} %shard_map.139.refs_0_), channel_id=1, source_target_pairs={{1,0},{0,1},{3,2},{2,3},{5,4},{4,5},{7,6},{6,7},{9,8},{8,9},{11,10... | collective-permute-start | bytes 147464 | tf_op jit(solution)/shard_map/ppermute | solution.py:73
  30.6 5.5 %collective-permute-start.17 = (bf16[192,128]{1,0:T(8,128)(2,1)S(1)}, bf16[192,128]{1,0:T(8,128)(2,1)S(1)}, u32[]{:S(2)}, u32[]{:S(2)}) collective-permute-start(bf16[192,128]{1,0:T(8,128)(2,1)S(1)} %shard_map.143.refs_2_), channel_id=1, source_target_pairs={{2,0},{3,1},{0,2},{1,3},{6,4},{7,5},{4,6},{5,7},{10,8},{11,9},{8,1... | collective-permute-start | bytes 147464 | tf_op jit(solution)/shard_map/ppermute | solution.py:73
  33.0 4.4 %collective-permute-start.16 = (bf16[192,128]{1,0:T(8,128)(2,1)S(1)}, bf16[192,128]{1,0:T(8,128)(2,1)S(1)}, u32[]{:S(2)}, u32[]{:S(2)}) collective-permute-start(bf16[192,128]{1,0:T(8,128)(2,1)S(1)} %shard_map.141.refs_5_.refs_0_), channel_id=1, source_target_pairs={{2,0},{3,1},{0,2},{1,3},{6,4},{7,5},{4,6},{5,7},{10,8},{11,9},{8,1... | collective-permute-start | bytes 147464 | tf_op jit(solution)/shard_map/ppermute | solution.py:73
  37.4 5.3 %collective-permute-start.20 = (bf16[2,192,128]{2,1,0:T(8,128)(2,1)S(1)}, bf16[2,192,128]{2,1,0:T(8,128)(2,1)S(1)}, u32[]{:S(2)}, u32[]{:S(2)}) collective-permute-start(bf16[2,192,128]{2,1,0:T(8,128)(2,1)S(1)} %shard_map.144.refs_0_), channel_id=1, source_target_pairs={{4,0},{0,4},{5,1},{1,5},{6,2},{2,6},{7,3},{3,7},{12,8},{8,12},{13,... | collective-permute-start | bytes 294920 | tf_op jit(solution)/shard_map/ppermute | solution.py:73
  38.4 6.4 %collective-permute-start.21 = (bf16[2,192,128]{2,1,0:T(8,128)(2,1)S(1)}, bf16[2,192,128]{2,1,0:T(8,128)(2,1)S(1)}, u32[]{:S(2)}, u32[]{:S(2)}) collective-permute-start(bf16[2,192,128]{2,1,0:T(8,128)(2,1)S(1)} %shard_map.144.refs_0_), channel_id=1, source_target_pairs={{16,0},{24,8},{0,16},{8,24},{17,1},{25,9},{1,17},{9,25},{18,2},{26... | collective-permute-start | bytes 294920 | tf_op jit(solution)/shard_map/ppermute | solution.py:73
  38.9 6.3 %collective-permute-start.18 = (bf16[2,192,128]{2,1,0:T(8,128)(2,1)S(1)}, bf16[2,192,128]{2,1,0:T(8,128)(2,1)S(1)}, u32[]{:S(2)}, u32[]{:S(2)}) collective-permute-start(bf16[2,192,128]{2,1,0:T(8,128)(2,1)S(1)} %shard_map.144.refs_0_), channel_id=1, source_target_pairs={{20,0},{16,4},{28,8},{24,12},{4,16},{0,20},{12,24},{8,28},{21,1},{... | collective-permute-start | bytes 294920 | tf_op jit(solution)/shard_map/ppermute | solution.py:81
  40.2 6.7 %collective-permute-start.22 = (bf16[2,192,128]{2,1,0:T(8,128)(2,1)S(1)}, bf16[2,192,128]{2,1,0:T(8,128)(2,1)S(1)}, u32[]{:S(2)}, u32[]{:S(2)}) collective-permute-start(bf16[2,192,128]{2,1,0:T(8,128)(2,1)S(1)} %shard_map.144.refs_0_), channel_id=1, source_target_pairs={{8,0},{0,8},{24,16},{16,24},{9,1},{1,9},{25,17},{17,25},{10,2},{2,... | collective-permute-start | bytes 294920 | tf_op jit(solution)/shard_map/ppermute | solution.py:73
  42.8 4.1 %collective-permute-start.23 = (bf16[2,192,128]{2,1,0:T(8,128)(2,1)S(1)}, bf16[2,192,128]{2,1,0:T(8,128)(2,1)S(1)}, u32[]{:S(2)}, u32[]{:S(2)}) collective-permute-start(bf16[2,192,128]{2,1,0:T(8,128)(2,1)S(1)} %collective-permute-done.20.refs_1_), channel_id=1, source_target_pairs={{8,0},{0,8},{24,16},{16,24},{9,1},{1,9},{25,17},{17,25},{10,2},{2,... | collective-permute-start | bytes 294920 | tf_op jit(solution)/shard_map/ppermute | solution.py:73
  44.8 2.1 %collective-permute-start.24 = (bf16[2,192,128]{2,1,0:T(8,128)(2,1)S(1)}, bf16[2,192,128]{2,1,0:T(8,128)(2,1)S(1)}, u32[]{:S(2)}, u32[]{:S(2)}) collective-permute-start(bf16[2,192,128]{2,1,0:T(8,128)(2,1)S(1)} %collective-permute-done.21.refs_2_), channel_id=1, source_target_pairs={{8,0},{0,8},{24,16},{16,24},{9,1},{1,9},{25,17},{17,25},{10,2},{2,... | collective-permute-start | bytes 294920 | tf_op jit(solution)/shard_map/ppermute | solution.py:73
  45.3 2.8 %collective-permute-start.19 = (bf16[2,192,128]{2,1,0:T(8,128)(2,1)S(1)}, bf16[2,192,128]{2,1,0:T(8,128)(2,1)S(1)}, u32[]{:S(2)}, u32[]{:S(2)}) collective-permute-start(bf16[2,192,128]{2,1,0:T(8,128)(2,1)S(1)} %collective-permute-done.18.refs_6_), channel_id=1, source_target_pairs={{8,0},{0,8},{24,16},{16,24},{9,1},{1,9},{25,17},{17,25},{10,2},{2,... | collective-permute-start | bytes 294920 | tf_op jit(solution)/shard_map/ppermute | solution.py:73
  (2 other events, 11.4 us)

commit v23 on v17

--- a/solution.py
+++ b/solution.py
@@ -682,14 +682,14 @@
 
         keep_two, send_two = call(
             band_kernel,
-            [f32(half, ch), bf16(half + 2 * cols, ch)],
+            [f32(half, ch), bf16(half + cols + 16, ch)],
             [],
             0,
             own_two,
             across_two,
         )
         sum_two = added(keep_two, flipped(send_two, "video", 1))
-        quarters = [f32(half, ch)] + [bf16(half + more, ch) for more in (cols, 0, cols + 16)]
+        quarters = [f32(half, ch)] + [bf16(half + more, ch) for more in (cols, 0, 16)]
         own_one, *sends = call(
             pair_quarter_kernel, quarters, [], 0, keep_one, pair_one, after=(send_two,)
         )

time: 47.1 us -> 47.4 us (level)
    ppermute x23, starting transfers between devices: 27.2 us -> 28.4 us  [flipped(): lax.ppermute(block, axis, [(place ^ flip, place) for place in range(count)])]
    ppermute x2, starting transfers between devices: 3.23 us -> 2.36 us  [flipped_both(): return lax.ppermute(block, ('section', 'video'), pairs)]
  transfers between devices with their start and end apart: 25 -> 25, of which waited for: 6 -> 5; matrix products, arithmetic and copies ran while one was open for 0% -> 0% of each run, Pallas kernels for 18% -> 18%
where the time goes in v23:
time: 47.4 us; the launch traced here: 47.2 us
  starting transfers between devices  30.8 us (65%)
  Pallas kernels  9.26 us (20%)
  waiting for transfers between devices  6.26 us (13%)
  between operations  0.83 us (2%)
    ppermute x23, starting transfers between devices, flipped(): lax.ppermute(block, axis, [(place ^ flip, place) for place in range(count)])  28.4 us
    pallas_call x17, Pallas kernels, call(): pl.pallas_call(body, out_shape=outs[0] if single else tuple(outs), in_spe...  7.36 us
    ppermute x23, waiting for transfers between devices, flipped(): lax.ppermute(block, axis, [(place ^ flip, place) for place in range(count)])  6.26 us
    ppermute x2, starting transfers between devices, flipped_both(): return lax.ppermute(block, ('section', 'video'), pairs)  2.36 us
    pallas_call x2, Pallas kernels, placed(): pl.pallas_call(functools.partial(place_kernel, places), out_shape=outs, i...  1.91 us
  transfers between devices with their start and end apart: 25, of which 5 were waited for; matrix products, arithmetic and copies ran while one was open for 0% of the time, Pallas kernels for 18%

profile of v23, /device:TPU:1, one launch (start us, length us, event | category | flops | bytes accessed | tf_op | source)
XLA Modules:
  0.0 47.2 jit_solution(11876374240591860749)
XLA Ops:
  0.6 2.1 %collective-permute-start.3 = (bf16[16,64,128]{2,1,0:T(8,128)(2,1)}, bf16[16,64,128]{2,1,0:T(8,128)(2,1)S(1)}, u32[]{:S(2)}, u32[]{:S(2)}) collective-permute-start(bf16[16,64,128]{2,1,0:T(8,128)(2,1)} %bitcast.10), channel_id=1, source_target_pairs={{4,0},{0,4},{5,1},{1,5},{6,2},{2,6},{7,3},{3,7},{12,8},{8,12},{13,... | collective-permute-start | bytes 786440 | tf_op jit(solution)/shard_map/ppermute | solution.py:73
  2.7 1.6 %shard_map.128 = (bf16[4,64,128]{2,1,0:T(8,128)(2,1)}, bf16[4,64,128]{2,1,0:T(8,128)(2,1)}) custom-call(bf16[16,64,128]{2,1,0:T(8,128)(2,1)} %bitcast.11, bf16[16,64,128]{2,1,0:T(8,128)(2,1)} %bitcast.17, bf16[16,64,128]{2,1,0:T(8,128)(2,1)} %bitcast.28, bf16[16,64,128]{2,1,0:T(8,128)(2,1)} %bitcast.25), custom_call_target="tpu_custom_call" | custom-call | flops 1 | bytes 1179648 | tf_op jit(solution)/shard_map/pallas_call | solution.py:38
  4.4 1.0 %collective-permute-start = (bf16[4,64,128]{2,1,0:T(8,128)(2,1)}, bf16[4,64,128]{2,1,0:T(8,128)(2,1)S(1)}, u32[]{:S(2)}, u32[]{:S(2)}) collective-permute-start(bf16[4,64,128]{2,1,0:T(8,128)(2,1)} %get-tuple-element.43), channel_id=1, source_target_pairs={{8,0},{0,8},{24,16},{16,24},{9,1},{1,9},{25,17},{17,25},{10,2},{2,... | collective-permute-start | bytes 196616 | tf_op jit(solution)/shard_map/ppermute | solution.py:73
  5.4 1.1 %collective-permute-done.refs_5_ = bf16[4,64,128]{2,1,0:T(8,128)(2,1)S(1)} collective-permute-done((bf16[4,64,128]{2,1,0:T(8,128)(2,1)}, bf16[4,64,128]{2,1,0:T(8,128)(2,1)S(1)}, u32[]{:S(2)}, u32[]{:S(2)}) %collective-permute-start) | collective-permute-done | bytes 65568 | tf_op jit(solution)/shard_map/ppermute | solution.py:73
  6.9 1.2 %collective-permute-start.2 = (bf16[4,64,128]{2,1,0:T(8,128)(2,1)S(1)}, bf16[4,64,128]{2,1,0:T(8,128)(2,1)S(1)}, u32[]{:S(2)}, u32[]{:S(2)}) collective-permute-start(bf16[4,64,128]{2,1,0:T(8,128)(2,1)S(1)} %collective-permute-done.refs_5_), channel_id=1, source_target_pairs={{16,0},{24,8},{0,16},{8,24},{17,1},{25,9},{1,17},{9,25},{18,2},{26... | collective-permute-start | bytes 196616 | tf_op jit(solution)/shard_map/ppermute | solution.py:73
  8.2 1.3 %collective-permute-start.4 = (bf16[14,64,128]{2,1,0:T(8,128)(2,1)S(1)}, bf16[14,64,128]{2,1,0:T(8,128)(2,1)S(1)}, u32[]{:S(2)}, u32[]{:S(2)}) collective-permute-start(bf16[14,64,128]{2,1,0:T(8,128)(2,1)S(1)} %get-tuple-element.45.refs_5_), channel_id=1, source_target_pairs={{4,0},{0,4},{5,1},{1,5},{6,2},{2,6},{7,3},{3,7},{12,8},{8,12},{13,... | collective-permute-start | bytes 688136 | tf_op jit(solution)/shard_map/ppermute | solution.py:73
  9.6 1.0 %shard_map.130 = (bf16[14,64,128]{2,1,0:T(8,128)(2,1)S(1)}, bf16[16,64,128]{2,1,0:T(8,128)(2,1)S(1)}) custom-call(bf16[16,64,128]{2,1,0:T(8,128)(2,1)S(1)} %bitcast.13, bf16[16,64,128]{2,1,0:T(8,128)(2,1)S(1)} %bitcast.19, bf16[16,64,128]{2,1,0:T(8,128)(2,1)S(1)} %collective-permute-done.3.refs_2_.refs_6_, bf16[3,128,128]{2,1,0:T(8,128)(2,1)S(1)} %copy-done.6, ...), custom_call_target="tpu_custom_call" | custom-call | tf_op jit(solution)/shard_map/pallas_call | solution.py:38
  10.6 0.9 %shard_map.132 = (f32[2,384,128]{2,1,0:T(8,128)S(1)}, bf16[384,128]{1,0:T(8,128)(2,1)S(1)}, bf16[384,128]{1,0:T(8,128)(2,1)S(1)}) custom-call(bf16[16,64,128]{2,1,0:T(8,128)(2,1)S(1)} %bitcast.30, bf16[16,64,128]{2,1,0:T(8,128)(2,1)S(1)} %bitcast.20, bf16[16,64,128]{2,1,0:T(8,128)(2,1)S(1)} %get-tuple-element.48.refs_6_.refs_2_.refs_4_, ...), custom_call_target="tpu_custom_call" | custom-call | flops 2415919104 | bytes 2031616 | tf_op jit(solution)/shard_map/pallas_call | solution.py:38
  11.5 0.9 %collective-permute-start.6 = (bf16[384,128]{1,0:T(8,128)(2,1)S(1)}, bf16[384,128]{1,0:T(8,128)(2,1)S(1)}, u32[]{:S(2)}, u32[]{:S(2)}) collective-permute-start(bf16[384,128]{1,0:T(8,128)(2,1)S(1)} %get-tuple-element.52), channel_id=1, source_target_pairs={{8,0},{0,8},{24,16},{16,24},{9,1},{1,9},{25,17},{17,25},{10,2},{2,... | collective-permute-start | bytes 294920 | tf_op jit(solution)/shard_map/ppermute | solution.py:73
  12.4 0.8 %collective-permute-start.5 = (bf16[4,64,128]{2,1,0:T(8,128)(2,1)S(1)}, bf16[4,64,128]{2,1,0:T(8,128)(2,1)S(1)}, u32[]{:S(2)}, u32[]{:S(2)}) collective-permute-start(bf16[4,64,128]{2,1,0:T(8,128)(2,1)S(1)} %shard_map.131.refs_7_), channel_id=1, source_target_pairs={{4,0},{0,4},{5,1},{1,5},{6,2},{2,6},{7,3},{3,7},{12,8},{8,12},{13,... | collective-permute-start | bytes 196616 | tf_op jit(solution)/shard_map/ppermute | solution.py:73
  13.7 1.4 %collective-permute-start.8 = (bf16[384,128]{1,0:T(8,128)(2,1)S(1)}, bf16[384,128]{1,0:T(8,128)(2,1)S(1)}, u32[]{:S(2)}, u32[]{:S(2)}) collective-permute-start(bf16[384,128]{1,0:T(8,128)(2,1)S(1)} %get-tuple-element.58), channel_id=1, source_target_pairs={{16,0},{24,8},{0,16},{8,24},{17,1},{25,9},{1,17},{9,25},{18,2},{26... | collective-permute-start | bytes 294920 | tf_op jit(solution)/shard_map/ppermute | solution.py:73
  15.6 1.0 %collective-permute-done.5.refs_6_ = bf16[4,64,128]{2,1,0:T(8,128)(2,1)S(1)} collective-permute-done((bf16[4,64,128]{2,1,0:T(8,128)(2,1)S(1)}, bf16[4,64,128]{2,1,0:T(8,128)(2,1)S(1)}, u32[]{:S(2)}, u32[]{:S(2)}) %collective-permute-start.5) | collective-permute-done | bytes 65568 | tf_op jit(solution)/shard_map/ppermute | solution.py:73
  16.6 1.3 %shard_map.136 = (bf16[16,64,128]{2,1,0:T(8,128)(2,1)S(1)}, bf16[16,64,128]{2,1,0:T(8,128)(2,1)S(1)}, f32[2,384,128]{2,1,0:T(8,128)S(1)}, bf16[896,128]{1,0:T(8,128)(2,1)S(1)}) custom-call(bf16[16,64,128]{2,1,0:T(8,128)(2,1)S(1)} %bitcast.16, bf16[4,64,128]{2,1,0:T(8,128)(2,1)S(1)} %collective-permute-done.1.refs_4_.refs_1_.refs_3_.refs_2_, ...), custom_call_target="tpu_custom_call" | custom-call | flops 2415919104 | bytes 5046272 | tf_op jit(solution)/shard_map/pallas_call | solution.py:38
  17.9 1.2 %collective-permute-start.9 = (bf16[896,128]{1,0:T(8,128)(2,1)S(1)}, bf16[896,128]{1,0:T(8,128)(2,1)S(1)}, u32[]{:S(2)}, u32[]{:S(2)}) collective-permute-start(bf16[896,128]{1,0:T(8,128)(2,1)S(1)} %get-tuple-element.59), channel_id=1, source_target_pairs={{8,0},{0,8},{24,16},{16,24},{9,1},{1,9},{25,17},{17,25},{10,2},{2,... | collective-permute-start | bytes 688136 | tf_op jit(solution)/shard_map/ppermute | solution.py:73
  19.1 1.3 %collective-permute-start.13 = (bf16[272,128]{1,0:T(8,128)(2,1)S(1)}, bf16[272,128]{1,0:T(8,128)(2,1)S(1)}, u32[]{:S(2)}, u32[]{:S(2)}) collective-permute-start(bf16[272,128]{1,0:T(8,128)(2,1)S(1)} %get-tuple-element.61.refs_2_), channel_id=1, source_target_pairs={{4,0},{0,4},{5,1},{1,5},{6,2},{2,6},{7,3},{3,7},{12,8},{8,12},{13,... | collective-permute-start | bytes 208904 | tf_op jit(solution)/shard_map/ppermute | solution.py:73
  20.5 1.2 %collective-permute-start.10 = (bf16[256,128]{1,0:T(8,128)(2,1)S(1)}, bf16[256,128]{1,0:T(8,128)(2,1)S(1)}, u32[]{:S(2)}, u32[]{:S(2)}) collective-permute-start(bf16[256,128]{1,0:T(8,128)(2,1)S(1)} %get-tuple-element.62), channel_id=1, source_target_pairs={{16,0},{24,8},{0,16},{8,24},{17,1},{25,9},{1,17},{9,25},{18,2},{26... | collective-permute-start | bytes 196616 | tf_op jit(solution)/shard_map/ppermute | solution.py:73
  21.7 1.1 %collective-permute-start.12 = (bf16[208,128]{1,0:T(8,128)(2,1)S(1)}, bf16[208,128]{1,0:T(8,128)(2,1)S(1)}, u32[]{:S(2)}, u32[]{:S(2)}) collective-permute-start(bf16[208,128]{1,0:T(8,128)(2,1)S(1)} %get-tuple-element.65), channel_id=1, source_target_pairs={{20,0},{16,4},{28,8},{24,12},{4,16},{0,20},{12,24},{8,28},{21,1},{... | collective-permute-start | bytes 159752 | tf_op jit(solution)/shard_map/ppermute | solution.py:81
  23.2 1.4 %collective-permute-start.15 = (bf16[192,128]{1,0:T(8,128)(2,1)S(1)}, bf16[192,128]{1,0:T(8,128)(2,1)S(1)}, u32[]{:S(2)}, u32[]{:S(2)}) collective-permute-start(bf16[192,128]{1,0:T(8,128)(2,1)S(1)} %shard_map.140.refs_0_), channel_id=1, source_target_pairs={{1,0},{0,1},{3,2},{2,3},{5,4},{4,5},{7,6},{6,7},{9,8},{8,9},{11,10... | collective-permute-start | bytes 147464 | tf_op jit(solution)/shard_map/ppermute | solution.py:73
  24.6 1.9 %collective-permute-done.11.refs_2_ = bf16[192,128]{1,0:T(8,128)(2,1)S(1)} collective-permute-done((bf16[192,128]{1,0:T(8,128)(2,1)S(1)}, bf16[192,128]{1,0:T(8,128)(2,1)S(1)}, u32[]{:S(2)}, u32[]{:S(2)}) %collective-permute-start.11) | collective-permute-done | bytes 49184 | tf_op jit(solution)/shard_map/ppermute | solution.py:73
  26.6 1.4 %collective-permute-start.14 = (bf16[192,128]{1,0:T(8,128)(2,1)S(1)}, bf16[192,128]{1,0:T(8,128)(2,1)S(1)}, u32[]{:S(2)}, u32[]{:S(2)}) collective-permute-start(bf16[192,128]{1,0:T(8,128)(2,1)S(1)} %shard_map.139.refs_0_), channel_id=1, source_target_pairs={{1,0},{0,1},{3,2},{2,3},{5,4},{4,5},{7,6},{6,7},{9,8},{8,9},{11,10... | collective-permute-start | bytes 147464 | tf_op jit(solution)/shard_map/ppermute | solution.py:73
  27.9 2.4 %collective-permute-start.17 = (bf16[192,128]{1,0:T(8,128)(2,1)S(1)}, bf16[192,128]{1,0:T(8,128)(2,1)S(1)}, u32[]{:S(2)}, u32[]{:S(2)}) collective-permute-start(bf16[192,128]{1,0:T(8,128)(2,1)S(1)} %shard_map.143.refs_2_), channel_id=1, source_target_pairs={{2,0},{3,1},{0,2},{1,3},{6,4},{7,5},{4,6},{5,7},{10,8},{11,9},{8,1... | collective-permute-start | bytes 147464 | tf_op jit(solution)/shard_map/ppermute | solution.py:73
  30.3 1.6 %collective-permute-start.16 = (bf16[192,128]{1,0:T(8,128)(2,1)S(1)}, bf16[192,128]{1,0:T(8,128)(2,1)S(1)}, u32[]{:S(2)}, u32[]{:S(2)}) collective-permute-start(bf16[192,128]{1,0:T(8,128)(2,1)S(1)} %shard_map.141.refs_5_.refs_0_), channel_id=1, source_target_pairs={{2,0},{3,1},{0,2},{1,3},{6,4},{7,5},{4,6},{5,7},{10,8},{11,9},{8,1... | collective-permute-start | bytes 147464 | tf_op jit(solution)/shard_map/ppermute | solution.py:73
  32.0 1.5 %shard_map.142 = (bf16[16,64,128]{2,1,0:T(8,128)(2,1)}, f32[8,128]{1,0:T(8,128)S(1)}) custom-call(bf16[16,64,128]{2,1,0:T(8,128)(2,1)S(1)} %get-tuple-element.55.refs_0_, bf16[16,64,128]{2,1,0:T(8,128)(2,1)S(1)} %get-tuple-element.56.refs_1_, bf16[896,128]{1,0:T(8,128)(2,1)S(1)} %collective-permute-done.9.refs_1_.refs_2_, ...), custom_call_target="tpu_custom_call" | custom-call | flops 301989888 | bytes 1380352 | tf_op jit(solution)/shard_map/pallas_call | solution.py:38
  33.5 2.1 %collective-permute-done.16.refs_1_ = bf16[192,128]{1,0:T(8,128)(2,1)S(1)} collective-permute-done((bf16[192,128]{1,0:T(8,128)(2,1)S(1)}, bf16[192,128]{1,0:T(8,128)(2,1)S(1)}, u32[]{:S(2)}, u32[]{:S(2)}) %collective-permute-start.16) | collective-permute-done | bytes 49184 | tf_op jit(solution)/shard_map/ppermute | solution.py:73
  36.1 1.0 %collective-permute-start.21 = (bf16[2,192,128]{2,1,0:T(8,128)(2,1)S(1)}, bf16[2,192,128]{2,1,0:T(8,128)(2,1)S(1)}, u32[]{:S(2)}, u32[]{:S(2)}) collective-permute-start(bf16[2,192,128]{2,1,0:T(8,128)(2,1)S(1)} %shard_map.144.refs_0_), channel_id=1, source_target_pairs={{16,0},{24,8},{0,16},{8,24},{17,1},{25,9},{1,17},{9,25},{18,2},{26... | collective-permute-start | bytes 294920 | tf_op jit(solution)/shard_map/ppermute | solution.py:73
  37.1 1.3 %collective-permute-start.18 = (bf16[2,192,128]{2,1,0:T(8,128)(2,1)S(1)}, bf16[2,192,128]{2,1,0:T(8,128)(2,1)S(1)}, u32[]{:S(2)}, u32[]{:S(2)}) collective-permute-start(bf16[2,192,128]{2,1,0:T(8,128)(2,1)S(1)} %shard_map.144.refs_0_), channel_id=1, source_target_pairs={{20,0},{16,4},{28,8},{24,12},{4,16},{0,20},{12,24},{8,28},{21,1},{... | collective-permute-start | bytes 294920 | tf_op jit(solution)/shard_map/ppermute | solution.py:81
  38.3 2.5 %collective-permute-start.22 = (bf16[2,192,128]{2,1,0:T(8,128)(2,1)S(1)}, bf16[2,192,128]{2,1,0:T(8,128)(2,1)S(1)}, u32[]{:S(2)}, u32[]{:S(2)}) collective-permute-start(bf16[2,192,128]{2,1,0:T(8,128)(2,1)S(1)} %shard_map.144.refs_0_), channel_id=1, source_target_pairs={{8,0},{0,8},{24,16},{16,24},{9,1},{1,9},{25,17},{17,25},{10,2},{2,... | collective-permute-start | bytes 294920 | tf_op jit(solution)/shard_map/ppermute | solution.py:73
  40.8 1.7 %collective-permute-start.23 = (bf16[2,192,128]{2,1,0:T(8,128)(2,1)S(1)}, bf16[2,192,128]{2,1,0:T(8,128)(2,1)S(1)}, u32[]{:S(2)}, u32[]{:S(2)}) collective-permute-start(bf16[2,192,128]{2,1,0:T(8,128)(2,1)S(1)} %collective-permute-done.20.refs_1_), channel_id=1, source_target_pairs={{8,0},{0,8},{24,16},{16,24},{9,1},{1,9},{25,17},{17,25},{10,2},{2,... | collective-permute-start | bytes 294920 | tf_op jit(solution)/shard_map/ppermute | solution.py:73
  42.5 0.9 %collective-permute-start.24 = (bf16[2,192,128]{2,1,0:T(8,128)(2,1)S(1)}, bf16[2,192,128]{2,1,0:T(8,128)(2,1)S(1)}, u32[]{:S(2)}, u32[]{:S(2)}) collective-permute-start(bf16[2,192,128]{2,1,0:T(8,128)(2,1)S(1)} %collective-permute-done.21.refs_2_), channel_id=1, source_target_pairs={{8,0},{0,8},{24,16},{16,24},{9,1},{1,9},{25,17},{17,25},{10,2},{2,... | collective-permute-start | bytes 294920 | tf_op jit(solution)/shard_map/ppermute | solution.py:73
  43.4 1.8 %collective-permute-start.19 = (bf16[2,192,128]{2,1,0:T(8,128)(2,1)S(1)}, bf16[2,192,128]{2,1,0:T(8,128)(2,1)S(1)}, u32[]{:S(2)}, u32[]{:S(2)}) collective-permute-start(bf16[2,192,128]{2,1,0:T(8,128)(2,1)S(1)} %collective-permute-done.18.refs_6_), channel_id=1, source_target_pairs={{8,0},{0,8},{24,16},{16,24},{9,1},{1,9},{25,17},{17,25},{10,2},{2,... | collective-permute-start | bytes 294920 | tf_op jit(solution)/shard_map/ppermute | solution.py:73
  45.3 1.2 %shard_map.145 = (f32[3,384,128]{2,1,0:T(8,128)}, f32[384,128]{1,0:T(8,128)}, f32[3,384,128]{2,1,0:T(8,128)}, f32[384,128]{1,0:T(8,128)}) custom-call(bf16[2,192,128]{2,1,0:T(8,128)(2,1)S(1)} %shard_map.144.refs_0_, bf16[2,192,128]{2,1,0:T(8,128)(2,1)S(1)} %collective-permute-done.20.refs_1_, bf16[2,192,128]{2,1,0:T(8,128)(2,1)S(1)} %collective-permute-done.21.refs_2_, ...), custom_call_target="tpu_custom_call" | custom-call | bytes 2064384 | tf_op jit(solution)/shard_map/pallas_call | solution.py:467
  46.5 0.7 %shard_map.146 = (f32[3,384,128]{2,1,0:T(8,128)}, f32[384,128]{1,0:T(8,128)}, f32[3,384,128]{2,1,0:T(8,128)}, f32[384,128]{1,0:T(8,128)}) custom-call(bf16[2,192,128]{2,1,0:T(8,128)(2,1)S(1)} %collective-permute-done.19.refs_0_, f32[3,384,128]{2,1,0:T(8,128)} %get-tuple-element.71.refs_1_, ...), custom_call_target="tpu_custom_call", output_to_operand_aliasing={{0}: (1, {}), {1}: (2, {}), {2}: (3, {}), {3}: (4, {})} | custom-call | bytes 294912 | tf_op jit(solution)/shard_map/pallas_call | solution.py:467
  (55 shorter events, 2.7 us)
Async XLA Ops:
  0.6 8.9 %collective-permute-start.3 = (bf16[16,64,128]{2,1,0:T(8,128)(2,1)}, bf16[16,64,128]{2,1,0:T(8,128)(2,1)S(1)}, u32[]{:S(2)}, u32[]{:S(2)}) collective-permute-start(bf16[16,64,128]{2,1,0:T(8,128)(2,1)} %bitcast.10), channel_id=1, source_target_pairs={{4,0},{0,4},{5,1},{1,5},{6,2},{2,6},{7,3},{3,7},{12,8},{8,12},{13,... | collective-permute-start | bytes 786440 | tf_op jit(solution)/shard_map/ppermute | solution.py:73
  2.7 5.4 %copy-start = (bf16[1,1,16,64,128]{4,3,2,1,0:T(8,128)(2,1)S(1)}, bf16[1,1,16,64,128]{4,3,2,1,0:T(8,128)(2,1)}, u32[]{:S(2)}) copy-start(bf16[1,1,16,64,128]{4,3,2,1,0:T(8,128)(2,1)} %param.9) | copy-start | bytes 786436
  2.7 5.4 %copy-start.1 = (bf16[3,3,128,128]{3,2,1,0:T(8,128)(2,1)S(1)}, bf16[3,3,128,128]{3,2,1,0:T(8,128)(2,1)}, u32[]{:S(2)}) copy-start(bf16[3,3,128,128]{3,2,1,0:T(8,128)(2,1)} %refs_8_.1) | copy-start | bytes 884740
  2.7 5.4 %copy-start.2 = (bf16[1,1,16,64,128]{4,3,2,1,0:T(8,128)(2,1)S(1)}, bf16[1,1,16,64,128]{4,3,2,1,0:T(8,128)(2,1)}, u32[]{:S(2)}) copy-start(bf16[1,1,16,64,128]{4,3,2,1,0:T(8,128)(2,1)} %param.13) | copy-start | bytes 786436
  2.7 5.4 %copy-start.6 = (bf16[3,128,128]{2,1,0:T(8,128)(2,1)S(1)}, bf16[3,128,128]{2,1,0:T(8,128)(2,1)}, u32[]{:S(2)}) copy-start(bf16[3,128,128]{2,1,0:T(8,128)(2,1)} %refs_7_.1) | copy-start | bytes 294916
  4.4 2.1 %collective-permute-start = (bf16[4,64,128]{2,1,0:T(8,128)(2,1)}, bf16[4,64,128]{2,1,0:T(8,128)(2,1)S(1)}, u32[]{:S(2)}, u32[]{:S(2)}) collective-permute-start(bf16[4,64,128]{2,1,0:T(8,128)(2,1)} %get-tuple-element.43), channel_id=1, source_target_pairs={{8,0},{0,8},{24,16},{16,24},{9,1},{1,9},{25,17},{17,25},{10,2},{2,... | collective-permute-start | bytes 196616 | tf_op jit(solution)/shard_map/ppermute | solution.py:73
  6.5 3.0 %copy-start.5 = (bf16[1,1,16,64,128]{4,3,2,1,0:T(8,128)(2,1)S(1)}, bf16[1,1,16,64,128]{4,3,2,1,0:T(8,128)(2,1)}, u32[]{:S(2)}) copy-start(bf16[1,1,16,64,128]{4,3,2,1,0:T(8,128)(2,1)} %param.12) | copy-start | bytes 786436
  6.5 3.0 %copy-start.7 = (bf16[3,128,128]{2,1,0:T(8,128)(2,1)S(1)}, bf16[3,128,128]{2,1,0:T(8,128)(2,1)}, u32[]{:S(2)}) copy-start(bf16[3,128,128]{2,1,0:T(8,128)(2,1)} %refs_11_.1) | copy-start | bytes 294916
  6.5 1.7 %collective-permute-start.1 = (bf16[4,64,128]{2,1,0:T(8,128)(2,1)}, bf16[4,64,128]{2,1,0:T(8,128)(2,1)S(1)}, u32[]{:S(2)}, u32[]{:S(2)}) collective-permute-start(bf16[4,64,128]{2,1,0:T(8,128)(2,1)} %get-tuple-element.44), channel_id=1, source_target_pairs={{8,0},{0,8},{24,16},{16,24},{9,1},{1,9},{25,17},{17,25},{10,2},{2,... | collective-permute-start | bytes 196616 | tf_op jit(solution)/shard_map/ppermute | solution.py:73
  6.9 3.6 %collective-permute-start.2 = (bf16[4,64,128]{2,1,0:T(8,128)(2,1)S(1)}, bf16[4,64,128]{2,1,0:T(8,128)(2,1)S(1)}, u32[]{:S(2)}, u32[]{:S(2)}) collective-permute-start(bf16[4,64,128]{2,1,0:T(8,128)(2,1)S(1)} %collective-permute-done.refs_5_), channel_id=1, source_target_pairs={{16,0},{24,8},{0,16},{8,24},{17,1},{25,9},{1,17},{9,25},{18,2},{26... | collective-permute-start | bytes 196616 | tf_op jit(solution)/shard_map/ppermute | solution.py:73
  8.2 6.9 %collective-permute-start.4 = (bf16[14,64,128]{2,1,0:T(8,128)(2,1)S(1)}, bf16[14,64,128]{2,1,0:T(8,128)(2,1)S(1)}, u32[]{:S(2)}, u32[]{:S(2)}) collective-permute-start(bf16[14,64,128]{2,1,0:T(8,128)(2,1)S(1)} %get-tuple-element.45.refs_5_), channel_id=1, source_target_pairs={{4,0},{0,4},{5,1},{1,5},{6,2},{2,6},{7,3},{3,7},{12,8},{8,12},{13,... | collective-permute-start | bytes 688136 | tf_op jit(solution)/shard_map/ppermute | solution.py:73
  11.5 2.1 %collective-permute-start.6 = (bf16[384,128]{1,0:T(8,128)(2,1)S(1)}, bf16[384,128]{1,0:T(8,128)(2,1)S(1)}, u32[]{:S(2)}, u32[]{:S(2)}) collective-permute-start(bf16[384,128]{1,0:T(8,128)(2,1)S(1)} %get-tuple-element.52), channel_id=1, source_target_pairs={{8,0},{0,8},{24,16},{16,24},{9,1},{1,9},{25,17},{17,25},{10,2},{2,... | collective-permute-start | bytes 294920 | tf_op jit(solution)/shard_map/ppermute | solution.py:73
  12.4 1.3 %collective-permute-start.7 = (bf16[384,128]{1,0:T(8,128)(2,1)S(1)}, bf16[384,128]{1,0:T(8,128)(2,1)S(1)}, u32[]{:S(2)}, u32[]{:S(2)}) collective-permute-start(bf16[384,128]{1,0:T(8,128)(2,1)S(1)} %get-tuple-element.53), channel_id=1, source_target_pairs={{8,0},{0,8},{24,16},{16,24},{9,1},{1,9},{25,17},{17,25},{10,2},{2,... | collective-permute-start | bytes 294920 | tf_op jit(solution)/shard_map/ppermute | solution.py:73
  12.4 4.2 %collective-permute-start.5 = (bf16[4,64,128]{2,1,0:T(8,128)(2,1)S(1)}, bf16[4,64,128]{2,1,0:T(8,128)(2,1)S(1)}, u32[]{:S(2)}, u32[]{:S(2)}) collective-permute-start(bf16[4,64,128]{2,1,0:T(8,128)(2,1)S(1)} %shard_map.131.refs_7_), channel_id=1, source_target_pairs={{4,0},{0,4},{5,1},{1,5},{6,2},{2,6},{7,3},{3,7},{12,8},{8,12},{13,... | collective-permute-start | bytes 196616 | tf_op jit(solution)/shard_map/ppermute | solution.py:73
  13.7 4.2 %collective-permute-start.8 = (bf16[384,128]{1,0:T(8,128)(2,1)S(1)}, bf16[384,128]{1,0:T(8,128)(2,1)S(1)}, u32[]{:S(2)}, u32[]{:S(2)}) collective-permute-start(bf16[384,128]{1,0:T(8,128)(2,1)S(1)} %get-tuple-element.58), channel_id=1, source_target_pairs={{16,0},{24,8},{0,16},{8,24},{17,1},{25,9},{1,17},{9,25},{18,2},{26... | collective-permute-start | bytes 294920 | tf_op jit(solution)/shard_map/ppermute | solution.py:73
  17.9 2.5 %collective-permute-start.9 = (bf16[896,128]{1,0:T(8,128)(2,1)S(1)}, bf16[896,128]{1,0:T(8,128)(2,1)S(1)}, u32[]{:S(2)}, u32[]{:S(2)}) collective-permute-start(bf16[896,128]{1,0:T(8,128)(2,1)S(1)} %get-tuple-element.59), channel_id=1, source_target_pairs={{8,0},{0,8},{24,16},{16,24},{9,1},{1,9},{25,17},{17,25},{10,2},{2,... | collective-permute-start | bytes 688136 | tf_op jit(solution)/shard_map/ppermute | solution.py:73
  19.1 4.1 %collective-permute-start.13 = (bf16[272,128]{1,0:T(8,128)(2,1)S(1)}, bf16[272,128]{1,0:T(8,128)(2,1)S(1)}, u32[]{:S(2)}, u32[]{:S(2)}) collective-permute-start(bf16[272,128]{1,0:T(8,128)(2,1)S(1)} %get-tuple-element.61.refs_2_), channel_id=1, source_target_pairs={{4,0},{0,4},{5,1},{1,5},{6,2},{2,6},{7,3},{3,7},{12,8},{8,12},{13,... | collective-permute-start | bytes 208904 | tf_op jit(solution)/shard_map/ppermute | solution.py:73
  20.5 6.0 %collective-permute-start.10 = (bf16[256,128]{1,0:T(8,128)(2,1)S(1)}, bf16[256,128]{1,0:T(8,128)(2,1)S(1)}, u32[]{:S(2)}, u32[]{:S(2)}) collective-permute-start(bf16[256,128]{1,0:T(8,128)(2,1)S(1)} %get-tuple-element.62), channel_id=1, source_target_pairs={{16,0},{24,8},{0,16},{8,24},{17,1},{25,9},{1,17},{9,25},{18,2},{26... | collective-permute-start | bytes 196616 | tf_op jit(solution)/shard_map/ppermute | solution.py:73
  21.7 4.8 %collective-permute-start.12 = (bf16[208,128]{1,0:T(8,128)(2,1)S(1)}, bf16[208,128]{1,0:T(8,128)(2,1)S(1)}, u32[]{:S(2)}, u32[]{:S(2)}) collective-permute-start(bf16[208,128]{1,0:T(8,128)(2,1)S(1)} %get-tuple-element.65), channel_id=1, source_target_pairs={{20,0},{16,4},{28,8},{24,12},{4,16},{0,20},{12,24},{8,28},{21,1},{... | collective-permute-start | bytes 159752 | tf_op jit(solution)/shard_map/ppermute | solution.py:81
  22.8 3.7 %collective-permute-start.11 = (bf16[192,128]{1,0:T(8,128)(2,1)S(1)}, bf16[192,128]{1,0:T(8,128)(2,1)S(1)}, u32[]{:S(2)}, u32[]{:S(2)}) collective-permute-start(bf16[192,128]{1,0:T(8,128)(2,1)S(1)} %get-tuple-element.64), channel_id=1, source_target_pairs={{4,0},{0,4},{5,1},{1,5},{6,2},{2,6},{7,3},{3,7},{12,8},{8,12},{13,... | collective-permute-start | bytes 147464 | tf_op jit(solution)/shard_map/ppermute | solution.py:73
  23.2 4.7 %collective-permute-start.15 = (bf16[192,128]{1,0:T(8,128)(2,1)S(1)}, bf16[192,128]{1,0:T(8,128)(2,1)S(1)}, u32[]{:S(2)}, u32[]{:S(2)}) collective-permute-start(bf16[192,128]{1,0:T(8,128)(2,1)S(1)} %shard_map.140.refs_0_), channel_id=1, source_target_pairs={{1,0},{0,1},{3,2},{2,3},{5,4},{4,5},{7,6},{6,7},{9,8},{8,9},{11,10... | collective-permute-start | bytes 147464 | tf_op jit(solution)/shard_map/ppermute | solution.py:73
  26.5 5.4 %copy-start.8 = (bf16[3,3,128,128]{3,2,1,0:T(8,128)(2,1)S(1)}, bf16[3,3,128,128]{3,2,1,0:T(8,128)(2,1)}, u32[]{:S(2)}) copy-start(bf16[3,3,128,128]{3,2,1,0:T(8,128)(2,1)} %refs_4_.5) | copy-start | bytes 884740
  26.6 3.8 %collective-permute-start.14 = (bf16[192,128]{1,0:T(8,128)(2,1)S(1)}, bf16[192,128]{1,0:T(8,128)(2,1)S(1)}, u32[]{:S(2)}, u32[]{:S(2)}) collective-permute-start(bf16[192,128]{1,0:T(8,128)(2,1)S(1)} %shard_map.139.refs_0_), channel_id=1, source_target_pairs={{1,0},{0,1},{3,2},{2,3},{5,4},{4,5},{7,6},{6,7},{9,8},{8,9},{11,10... | collective-permute-start | bytes 147464 | tf_op jit(solution)/shard_map/ppermute | solution.py:73
  27.9 5.5 %collective-permute-start.17 = (bf16[192,128]{1,0:T(8,128)(2,1)S(1)}, bf16[192,128]{1,0:T(8,128)(2,1)S(1)}, u32[]{:S(2)}, u32[]{:S(2)}) collective-permute-start(bf16[192,128]{1,0:T(8,128)(2,1)S(1)} %shard_map.143.refs_2_), channel_id=1, source_target_pairs={{2,0},{3,1},{0,2},{1,3},{6,4},{7,5},{4,6},{5,7},{10,8},{11,9},{8,1... | collective-permute-start | bytes 147464 | tf_op jit(solution)/shard_map/ppermute | solution.py:73
  30.3 5.2 %collective-permute-start.16 = (bf16[192,128]{1,0:T(8,128)(2,1)S(1)}, bf16[192,128]{1,0:T(8,128)(2,1)S(1)}, u32[]{:S(2)}, u32[]{:S(2)}) collective-permute-start(bf16[192,128]{1,0:T(8,128)(2,1)S(1)} %shard_map.141.refs_5_.refs_0_), channel_id=1, source_target_pairs={{2,0},{3,1},{0,2},{1,3},{6,4},{7,5},{4,6},{5,7},{10,8},{11,9},{8,1... | collective-permute-start | bytes 147464 | tf_op jit(solution)/shard_map/ppermute | solution.py:73
  35.6 5.2 %collective-permute-start.20 = (bf16[2,192,128]{2,1,0:T(8,128)(2,1)S(1)}, bf16[2,192,128]{2,1,0:T(8,128)(2,1)S(1)}, u32[]{:S(2)}, u32[]{:S(2)}) collective-permute-start(bf16[2,192,128]{2,1,0:T(8,128)(2,1)S(1)} %shard_map.144.refs_0_), channel_id=1, source_target_pairs={{4,0},{0,4},{5,1},{1,5},{6,2},{2,6},{7,3},{3,7},{12,8},{8,12},{13,... | collective-permute-start | bytes 294920 | tf_op jit(solution)/shard_map/ppermute | solution.py:73
  36.1 6.4 %collective-permute-start.21 = (bf16[2,192,128]{2,1,0:T(8,128)(2,1)S(1)}, bf16[2,192,128]{2,1,0:T(8,128)(2,1)S(1)}, u32[]{:S(2)}, u32[]{:S(2)}) collective-permute-start(bf16[2,192,128]{2,1,0:T(8,128)(2,1)S(1)} %shard_map.144.refs_0_), channel_id=1, source_target_pairs={{16,0},{24,8},{0,16},{8,24},{17,1},{25,9},{1,17},{9,25},{18,2},{26... | collective-permute-start | bytes 294920 | tf_op jit(solution)/shard_map/ppermute | solution.py:73
  37.1 6.3 %collective-permute-start.18 = (bf16[2,192,128]{2,1,0:T(8,128)(2,1)S(1)}, bf16[2,192,128]{2,1,0:T(8,128)(2,1)S(1)}, u32[]{:S(2)}, u32[]{:S(2)}) collective-permute-start(bf16[2,192,128]{2,1,0:T(8,128)(2,1)S(1)} %shard_map.144.refs_0_), channel_id=1, source_target_pairs={{20,0},{16,4},{28,8},{24,12},{4,16},{0,20},{12,24},{8,28},{21,1},{... | collective-permute-start | bytes 294920 | tf_op jit(solution)/shard_map/ppermute | solution.py:81
  38.3 6.9 %collective-permute-start.22 = (bf16[2,192,128]{2,1,0:T(8,128)(2,1)S(1)}, bf16[2,192,128]{2,1,0:T(8,128)(2,1)S(1)}, u32[]{:S(2)}, u32[]{:S(2)}) collective-permute-start(bf16[2,192,128]{2,1,0:T(8,128)(2,1)S(1)} %shard_map.144.refs_0_), channel_id=1, source_target_pairs={{8,0},{0,8},{24,16},{16,24},{9,1},{1,9},{25,17},{17,25},{10,2},{2,... | collective-permute-start | bytes 294920 | tf_op jit(solution)/shard_map/ppermute | solution.py:73
  40.8 4.4 %collective-permute-start.23 = (bf16[2,192,128]{2,1,0:T(8,128)(2,1)S(1)}, bf16[2,192,128]{2,1,0:T(8,128)(2,1)S(1)}, u32[]{:S(2)}, u32[]{:S(2)}) collective-permute-start(bf16[2,192,128]{2,1,0:T(8,128)(2,1)S(1)} %collective-permute-done.20.refs_1_), channel_id=1, source_target_pairs={{8,0},{0,8},{24,16},{16,24},{9,1},{1,9},{25,17},{17,25},{10,2},{2,... | collective-permute-start | bytes 294920 | tf_op jit(solution)/shard_map/ppermute | solution.py:73
  42.5 2.8 %collective-permute-start.24 = (bf16[2,192,128]{2,1,0:T(8,128)(2,1)S(1)}, bf16[2,192,128]{2,1,0:T(8,128)(2,1)S(1)}, u32[]{:S(2)}, u32[]{:S(2)}) collective-permute-start(bf16[2,192,128]{2,1,0:T(8,128)(2,1)S(1)} %collective-permute-done.21.refs_2_), channel_id=1, source_target_pairs={{8,0},{0,8},{24,16},{16,24},{9,1},{1,9},{25,17},{17,25},{10,2},{2,... | collective-permute-start | bytes 294920 | tf_op jit(solution)/shard_map/ppermute | solution.py:73
  43.4 3.1 %collective-permute-start.19 = (bf16[2,192,128]{2,1,0:T(8,128)(2,1)S(1)}, bf16[2,192,128]{2,1,0:T(8,128)(2,1)S(1)}, u32[]{:S(2)}, u32[]{:S(2)}) collective-permute-start(bf16[2,192,128]{2,1,0:T(8,128)(2,1)S(1)} %collective-permute-done.18.refs_6_), channel_id=1, source_target_pairs={{8,0},{0,8},{24,16},{16,24},{9,1},{1,9},{25,17},{17,25},{10,2},{2,... | collective-permute-start | bytes 294920 | tf_op jit(solution)/shard_map/ppermute | solution.py:73
  (2 other events, 6.1 us)

commit v24 on v21

--- a/solution.py
+++ b/solution.py
@@ -707,9 +707,9 @@
         last_two = flipped(sum_two, "dp", 2)
         last_one = flipped(later_than(sum_one, sum_two), "dp", 2)
         grad_in, token = input_gradient(across, (sum_one,))
-        own, longer, longest = call(
+        own, longer = call(
             functools.partial(scaled_kernel, factor),
-            [bf16(2, half + more, ch) for more in (0, 16, 32)],
+            [bf16(2, half, ch), bf16(2, half + 16, ch)],
             [],
             height * ch,
             sum_one,
@@ -718,8 +718,8 @@
             last_two,
             after=(token,),
         )
-        frame, both = flipped(longest, "video", 1), flipped_both(longer)
-        shares = [own, frame, flipped(own, "section", 2)]
+        frame, across, both = flipped(own, "video", 1), flipped(longer, "section", 2), flipped_both(own)
+        shares = [own, frame, across]
         shares += [flipped(share, "section", 1) for share in shares]
         places = [(0, False), (0, True), (2, False), (1, False), (1, True), (3, False)]
         sums = placed([*shares, both], [*places, (2, True)])

time: 48.7 us -> 47.1 us (0.967)
  waiting for transfers between devices: 8.26 us -> 7.24 us
    ppermute x23, waiting for transfers between devices: 8.26 us -> 7.23 us  [flipped(): lax.ppermute(block, axis, [(place ^ flip, place) for place in range(count)])]
  transfers between devices with their start and end apart: 25 -> 25, of which waited for: 9 -> 7; matrix products, arithmetic and copies ran while one was open for 0% -> 0% of each run, Pallas kernels for 18% -> 18%
where the time goes in v24:
time: 47.1 us; the launch traced here: 46.9 us
  starting transfers between devices  29.5 us (63%)
  Pallas kernels  9.27 us (20%)
  waiting for transfers between devices  7.24 us (15%)
  between operations  0.83 us (2%)
    ppermute x23, starting transfers between devices, flipped(): lax.ppermute(block, axis, [(place ^ flip, place) for place in range(count)])  26.3 us
    pallas_call x17, Pallas kernels, call(): pl.pallas_call(body, out_shape=outs[0] if single else tuple(outs), in_spe...  7.36 us
    ppermute x23, waiting for transfers between devices, flipped(): lax.ppermute(block, axis, [(place ^ flip, place) for place in range(count)])  7.23 us
    ppermute x2, starting transfers between devices, flipped_both(): return lax.ppermute(block, ('section', 'video'), pairs)  3.23 us
    pallas_call x2, Pallas kernels, placed(): pl.pallas_call(functools.partial(place_kernel, places), out_shape=outs, i...  1.91 us
  transfers between devices with their start and end apart: 25, of which 7 were waited for; matrix products, arithmetic and copies ran while one was open for 0% of the time, Pallas kernels for 18%

profile of v24, /device:TPU:1, one launch (start us, length us, event | category | flops | bytes accessed | tf_op | source)
XLA Modules:
  0.0 46.9 jit_solution(10454672460635266253)
XLA Ops:
  0.6 2.1 %collective-permute-start.3 = (bf16[16,64,128]{2,1,0:T(8,128)(2,1)}, bf16[16,64,128]{2,1,0:T(8,128)(2,1)S(1)}, u32[]{:S(2)}, u32[]{:S(2)}) collective-permute-start(bf16[16,64,128]{2,1,0:T(8,128)(2,1)} %bitcast.10), channel_id=1, source_target_pairs={{4,0},{0,4},{5,1},{1,5},{6,2},{2,6},{7,3},{3,7},{12,8},{8,12},{13,... | collective-permute-start | bytes 786440 | tf_op jit(solution)/shard_map/ppermute | solution.py:73
  2.7 1.6 %shard_map.128 = (bf16[4,64,128]{2,1,0:T(8,128)(2,1)}, bf16[4,64,128]{2,1,0:T(8,128)(2,1)}) custom-call(bf16[16,64,128]{2,1,0:T(8,128)(2,1)} %bitcast.11, bf16[16,64,128]{2,1,0:T(8,128)(2,1)} %bitcast.17, bf16[16,64,128]{2,1,0:T(8,128)(2,1)} %bitcast.28, bf16[16,64,128]{2,1,0:T(8,128)(2,1)} %bitcast.25), custom_call_target="tpu_custom_call" | custom-call | flops 1 | bytes 1179648 | tf_op jit(solution)/shard_map/pallas_call | solution.py:38
  4.4 1.0 %collective-permute-start = (bf16[4,64,128]{2,1,0:T(8,128)(2,1)}, bf16[4,64,128]{2,1,0:T(8,128)(2,1)S(1)}, u32[]{:S(2)}, u32[]{:S(2)}) collective-permute-start(bf16[4,64,128]{2,1,0:T(8,128)(2,1)} %get-tuple-element.45), channel_id=1, source_target_pairs={{8,0},{0,8},{24,16},{16,24},{9,1},{1,9},{25,17},{17,25},{10,2},{2,... | collective-permute-start | bytes 196616 | tf_op jit(solution)/shard_map/ppermute | solution.py:73
  5.4 1.1 %collective-permute-done.refs_5_ = bf16[4,64,128]{2,1,0:T(8,128)(2,1)S(1)} collective-permute-done((bf16[4,64,128]{2,1,0:T(8,128)(2,1)}, bf16[4,64,128]{2,1,0:T(8,128)(2,1)S(1)}, u32[]{:S(2)}, u32[]{:S(2)}) %collective-permute-start) | collective-permute-done | bytes 65568 | tf_op jit(solution)/shard_map/ppermute | solution.py:73
  6.9 1.2 %collective-permute-start.2 = (bf16[4,64,128]{2,1,0:T(8,128)(2,1)S(1)}, bf16[4,64,128]{2,1,0:T(8,128)(2,1)S(1)}, u32[]{:S(2)}, u32[]{:S(2)}) collective-permute-start(bf16[4,64,128]{2,1,0:T(8,128)(2,1)S(1)} %collective-permute-done.refs_5_), channel_id=1, source_target_pairs={{16,0},{24,8},{0,16},{8,24},{17,1},{25,9},{1,17},{9,25},{18,2},{26... | collective-permute-start | bytes 196616 | tf_op jit(solution)/shard_map/ppermute | solution.py:73
  8.2 1.3 %collective-permute-start.4 = (bf16[14,64,128]{2,1,0:T(8,128)(2,1)S(1)}, bf16[14,64,128]{2,1,0:T(8,128)(2,1)S(1)}, u32[]{:S(2)}, u32[]{:S(2)}) collective-permute-start(bf16[14,64,128]{2,1,0:T(8,128)(2,1)S(1)} %get-tuple-element.47.refs_5_), channel_id=1, source_target_pairs={{4,0},{0,4},{5,1},{1,5},{6,2},{2,6},{7,3},{3,7},{12,8},{8,12},{13,... | collective-permute-start | bytes 688136 | tf_op jit(solution)/shard_map/ppermute | solution.py:73
  9.6 1.0 %shard_map.130 = (bf16[14,64,128]{2,1,0:T(8,128)(2,1)S(1)}, bf16[16,64,128]{2,1,0:T(8,128)(2,1)S(1)}) custom-call(bf16[16,64,128]{2,1,0:T(8,128)(2,1)S(1)} %bitcast.13, bf16[16,64,128]{2,1,0:T(8,128)(2,1)S(1)} %bitcast.19, bf16[16,64,128]{2,1,0:T(8,128)(2,1)S(1)} %collective-permute-done.3.refs_2_.refs_6_, bf16[3,128,128]{2,1,0:T(8,128)(2,1)S(1)} %copy-done.6, ...), custom_call_target="tpu_custom_call" | custom-call | tf_op jit(solution)/shard_map/pallas_call | solution.py:38
  10.6 0.9 %shard_map.132 = (f32[2,384,128]{2,1,0:T(8,128)S(1)}, bf16[384,128]{1,0:T(8,128)(2,1)S(1)}, bf16[384,128]{1,0:T(8,128)(2,1)S(1)}) custom-call(bf16[16,64,128]{2,1,0:T(8,128)(2,1)S(1)} %bitcast.30, bf16[16,64,128]{2,1,0:T(8,128)(2,1)S(1)} %bitcast.20, bf16[16,64,128]{2,1,0:T(8,128)(2,1)S(1)} %get-tuple-element.50.refs_6_.refs_2_.refs_4_, ...), custom_call_target="tpu_custom_call" | custom-call | flops 2415919104 | bytes 2031616 | tf_op jit(solution)/shard_map/pallas_call | solution.py:38
  11.5 0.9 %collective-permute-start.6 = (bf16[384,128]{1,0:T(8,128)(2,1)S(1)}, bf16[384,128]{1,0:T(8,128)(2,1)S(1)}, u32[]{:S(2)}, u32[]{:S(2)}) collective-permute-start(bf16[384,128]{1,0:T(8,128)(2,1)S(1)} %get-tuple-element.54), channel_id=1, source_target_pairs={{8,0},{0,8},{24,16},{16,24},{9,1},{1,9},{25,17},{17,25},{10,2},{2,... | collective-permute-start | bytes 294920 | tf_op jit(solution)/shard_map/ppermute | solution.py:73
  12.4 0.8 %collective-permute-start.5 = (bf16[4,64,128]{2,1,0:T(8,128)(2,1)S(1)}, bf16[4,64,128]{2,1,0:T(8,128)(2,1)S(1)}, u32[]{:S(2)}, u32[]{:S(2)}) collective-permute-start(bf16[4,64,128]{2,1,0:T(8,128)(2,1)S(1)} %shard_map.131.refs_7_), channel_id=1, source_target_pairs={{4,0},{0,4},{5,1},{1,5},{6,2},{2,6},{7,3},{3,7},{12,8},{8,12},{13,... | collective-permute-start | bytes 196616 | tf_op jit(solution)/shard_map/ppermute | solution.py:73
  13.7 1.4 %collective-permute-start.8 = (bf16[384,128]{1,0:T(8,128)(2,1)S(1)}, bf16[384,128]{1,0:T(8,128)(2,1)S(1)}, u32[]{:S(2)}, u32[]{:S(2)}) collective-permute-start(bf16[384,128]{1,0:T(8,128)(2,1)S(1)} %get-tuple-element.60), channel_id=1, source_target_pairs={{16,0},{24,8},{0,16},{8,24},{17,1},{25,9},{1,17},{9,25},{18,2},{26... | collective-permute-start | bytes 294920 | tf_op jit(solution)/shard_map/ppermute | solution.py:73
  15.6 1.0 %collective-permute-done.5.refs_6_ = bf16[4,64,128]{2,1,0:T(8,128)(2,1)S(1)} collective-permute-done((bf16[4,64,128]{2,1,0:T(8,128)(2,1)S(1)}, bf16[4,64,128]{2,1,0:T(8,128)(2,1)S(1)}, u32[]{:S(2)}, u32[]{:S(2)}) %collective-permute-start.5) | collective-permute-done | bytes 65568 | tf_op jit(solution)/shard_map/ppermute | solution.py:73
  16.6 1.3 %shard_map.136 = (bf16[16,64,128]{2,1,0:T(8,128)(2,1)S(1)}, bf16[16,64,128]{2,1,0:T(8,128)(2,1)S(1)}, f32[2,384,128]{2,1,0:T(8,128)S(1)}, bf16[896,128]{1,0:T(8,128)(2,1)S(1)}) custom-call(bf16[16,64,128]{2,1,0:T(8,128)(2,1)S(1)} %bitcast.16, bf16[4,64,128]{2,1,0:T(8,128)(2,1)S(1)} %collective-permute-done.1.refs_4_.refs_1_.refs_3_.refs_2_, ...), custom_call_target="tpu_custom_call" | custom-call | flops 2415919104 | bytes 5046272 | tf_op jit(solution)/shard_map/pallas_call | solution.py:38
  17.9 1.2 %collective-permute-start.9 = (bf16[896,128]{1,0:T(8,128)(2,1)S(1)}, bf16[896,128]{1,0:T(8,128)(2,1)S(1)}, u32[]{:S(2)}, u32[]{:S(2)}) collective-permute-start(bf16[896,128]{1,0:T(8,128)(2,1)S(1)} %get-tuple-element.61), channel_id=1, source_target_pairs={{8,0},{0,8},{24,16},{16,24},{9,1},{1,9},{25,17},{17,25},{10,2},{2,... | collective-permute-start | bytes 688136 | tf_op jit(solution)/shard_map/ppermute | solution.py:73
  19.1 1.3 %collective-permute-start.13 = (bf16[320,128]{1,0:T(8,128)(2,1)S(1)}, bf16[320,128]{1,0:T(8,128)(2,1)S(1)}, u32[]{:S(2)}, u32[]{:S(2)}) collective-permute-start(bf16[320,128]{1,0:T(8,128)(2,1)S(1)} %get-tuple-element.63.refs_2_), channel_id=1, source_target_pairs={{4,0},{0,4},{5,1},{1,5},{6,2},{2,6},{7,3},{3,7},{12,8},{8,12},{13,... | collective-permute-start | bytes 245768 | tf_op jit(solution)/shard_map/ppermute | solution.py:73
  20.5 1.9 %collective-permute-start.12 = (bf16[272,128]{1,0:T(8,128)(2,1)S(1)}, bf16[272,128]{1,0:T(8,128)(2,1)S(1)}, u32[]{:S(2)}, u32[]{:S(2)}) collective-permute-start(bf16[272,128]{1,0:T(8,128)(2,1)S(1)} %get-tuple-element.67), channel_id=1, source_target_pairs={{20,0},{16,4},{28,8},{24,12},{4,16},{0,20},{12,24},{8,28},{21,1},{... | collective-permute-start | bytes 208904 | tf_op jit(solution)/shard_map/ppermute | solution.py:81
  23.3 1.4 %collective-permute-start.15 = (bf16[192,128]{1,0:T(8,128)(2,1)S(1)}, bf16[192,128]{1,0:T(8,128)(2,1)S(1)}, u32[]{:S(2)}, u32[]{:S(2)}) collective-permute-start(bf16[192,128]{1,0:T(8,128)(2,1)S(1)} %shard_map.140.refs_0_), channel_id=1, source_target_pairs={{1,0},{0,1},{3,2},{2,3},{5,4},{4,5},{7,6},{6,7},{9,8},{8,9},{11,10... | collective-permute-start | bytes 147464 | tf_op jit(solution)/shard_map/ppermute | solution.py:73
  24.6 1.5 %collective-permute-done.11.refs_2_ = bf16[192,128]{1,0:T(8,128)(2,1)S(1)} collective-permute-done((bf16[192,128]{1,0:T(8,128)(2,1)S(1)}, bf16[192,128]{1,0:T(8,128)(2,1)S(1)}, u32[]{:S(2)}, u32[]{:S(2)}) %collective-permute-start.11) | collective-permute-done | bytes 49184 | tf_op jit(solution)/shard_map/ppermute | solution.py:73
  26.1 1.3 %collective-permute-done.10.refs_1_.refs_3_ = bf16[256,128]{1,0:T(8,128)(2,1)S(1)} collective-permute-done((bf16[256,128]{1,0:T(8,128)(2,1)S(1)}, bf16[256,128]{1,0:T(8,128)(2,1)S(1)}, u32[]{:S(2)}, u32[]{:S(2)}) %collective-permute-start.10) | collective-permute-done | bytes 65568 | tf_op jit(solution)/shard_map/ppermute | solution.py:73
  27.4 1.3 %collective-permute-start.14 = (bf16[192,128]{1,0:T(8,128)(2,1)S(1)}, bf16[192,128]{1,0:T(8,128)(2,1)S(1)}, u32[]{:S(2)}, u32[]{:S(2)}) collective-permute-start(bf16[192,128]{1,0:T(8,128)(2,1)S(1)} %shard_map.139.refs_0_), channel_id=1, source_target_pairs={{1,0},{0,1},{3,2},{2,3},{5,4},{4,5},{7,6},{6,7},{9,8},{8,9},{11,10... | collective-permute-start | bytes 147464 | tf_op jit(solution)/shard_map/ppermute | solution.py:73
  28.8 2.4 %collective-permute-start.17 = (bf16[192,128]{1,0:T(8,128)(2,1)S(1)}, bf16[192,128]{1,0:T(8,128)(2,1)S(1)}, u32[]{:S(2)}, u32[]{:S(2)}) collective-permute-start(bf16[192,128]{1,0:T(8,128)(2,1)S(1)} %shard_map.143.refs_2_), channel_id=1, source_target_pairs={{2,0},{3,1},{0,2},{1,3},{6,4},{7,5},{4,6},{5,7},{10,8},{11,9},{8,1... | collective-permute-start | bytes 147464 | tf_op jit(solution)/shard_map/ppermute | solution.py:73
  31.2 1.6 %collective-permute-start.16 = (bf16[192,128]{1,0:T(8,128)(2,1)S(1)}, bf16[192,128]{1,0:T(8,128)(2,1)S(1)}, u32[]{:S(2)}, u32[]{:S(2)}) collective-permute-start(bf16[192,128]{1,0:T(8,128)(2,1)S(1)} %shard_map.141.refs_5_.refs_0_), channel_id=1, source_target_pairs={{2,0},{3,1},{0,2},{1,3},{6,4},{7,5},{4,6},{5,7},{10,8},{11,9},{8,1... | collective-permute-start | bytes 147464 | tf_op jit(solution)/shard_map/ppermute | solution.py:73
  32.8 1.5 %shard_map.142 = (bf16[16,64,128]{2,1,0:T(8,128)(2,1)}, f32[8,128]{1,0:T(8,128)S(1)}) custom-call(bf16[16,64,128]{2,1,0:T(8,128)(2,1)S(1)} %get-tuple-element.57.refs_0_, bf16[16,64,128]{2,1,0:T(8,128)(2,1)S(1)} %get-tuple-element.58.refs_1_, bf16[896,128]{1,0:T(8,128)(2,1)S(1)} %collective-permute-done.9.refs_1_.refs_2_, ...), custom_call_target="tpu_custom_call" | custom-call | flops 301989888 | bytes 1380352 | tf_op jit(solution)/shard_map/pallas_call | solution.py:38
  34.3 1.3 %collective-permute-done.16.refs_1_ = bf16[192,128]{1,0:T(8,128)(2,1)S(1)} collective-permute-done((bf16[192,128]{1,0:T(8,128)(2,1)S(1)}, bf16[192,128]{1,0:T(8,128)(2,1)S(1)}, u32[]{:S(2)}, u32[]{:S(2)}) %collective-permute-start.16) | collective-permute-done | bytes 49184 | tf_op jit(solution)/shard_map/ppermute | solution.py:73
  35.7 1.0 %collective-permute-start.21 = (bf16[2,208,128]{2,1,0:T(8,128)(2,1)S(1)}, bf16[2,208,128]{2,1,0:T(8,128)(2,1)S(1)}, u32[]{:S(2)}, u32[]{:S(2)}) collective-permute-start(bf16[2,208,128]{2,1,0:T(8,128)(2,1)S(1)} %get-tuple-element.74), channel_id=1, source_target_pairs={{16,0},{24,8},{0,16},{8,24},{17,1},{25,9},{1,17},{9,25},{18,2},{26... | collective-permute-start | bytes 319496 | tf_op jit(solution)/shard_map/ppermute | solution.py:73
  37.1 1.3 %collective-permute-start.18 = (bf16[2,192,128]{2,1,0:T(8,128)(2,1)S(1)}, bf16[2,192,128]{2,1,0:T(8,128)(2,1)S(1)}, u32[]{:S(2)}, u32[]{:S(2)}) collective-permute-start(bf16[2,192,128]{2,1,0:T(8,128)(2,1)S(1)} %get-tuple-element.73.refs_0_), channel_id=1, source_target_pairs={{20,0},{16,4},{28,8},{24,12},{4,16},{0,20},{12,24},{8,28},{21,1},{... | collective-permute-start | bytes 294920 | tf_op jit(solution)/shard_map/ppermute | solution.py:81
  38.4 0.9 %collective-permute-done.21.refs_2_ = bf16[2,208,128]{2,1,0:T(8,128)(2,1)S(1)} collective-permute-done((bf16[2,208,128]{2,1,0:T(8,128)(2,1)S(1)}, bf16[2,208,128]{2,1,0:T(8,128)(2,1)S(1)}, u32[]{:S(2)}, u32[]{:S(2)}) %collective-permute-start.21) | collective-permute-done | bytes 106528 | tf_op jit(solution)/shard_map/ppermute | solution.py:73
  39.3 3.9 %collective-permute-start.24 = (bf16[2,208,128]{2,1,0:T(8,128)(2,1)S(1)}, bf16[2,208,128]{2,1,0:T(8,128)(2,1)S(1)}, u32[]{:S(2)}, u32[]{:S(2)}) collective-permute-start(bf16[2,208,128]{2,1,0:T(8,128)(2,1)S(1)} %collective-permute-done.21.refs_2_), channel_id=1, source_target_pairs={{8,0},{0,8},{24,16},{16,24},{9,1},{1,9},{25,17},{17,25},{10,2},{2,... | collective-permute-start | bytes 319496 | tf_op jit(solution)/shard_map/ppermute | solution.py:73
  43.2 0.5 %collective-permute-start.23 = (bf16[2,192,128]{2,1,0:T(8,128)(2,1)S(1)}, bf16[2,192,128]{2,1,0:T(8,128)(2,1)S(1)}, u32[]{:S(2)}, u32[]{:S(2)}) collective-permute-start(bf16[2,192,128]{2,1,0:T(8,128)(2,1)S(1)} %collective-permute-done.20.refs_1_), channel_id=1, source_target_pairs={{8,0},{0,8},{24,16},{16,24},{9,1},{1,9},{25,17},{17,25},{10,2},{2,... | collective-permute-start | bytes 294920 | tf_op jit(solution)/shard_map/ppermute | solution.py:73
  43.7 1.2 %collective-permute-start.19 = (bf16[2,192,128]{2,1,0:T(8,128)(2,1)S(1)}, bf16[2,192,128]{2,1,0:T(8,128)(2,1)S(1)}, u32[]{:S(2)}, u32[]{:S(2)}) collective-permute-start(bf16[2,192,128]{2,1,0:T(8,128)(2,1)S(1)} %collective-permute-done.18.refs_6_), channel_id=1, source_target_pairs={{8,0},{0,8},{24,16},{16,24},{9,1},{1,9},{25,17},{17,25},{10,2},{2,... | collective-permute-start | bytes 294920 | tf_op jit(solution)/shard_map/ppermute | solution.py:73
  44.9 1.2 %shard_map.145 = (f32[3,384,128]{2,1,0:T(8,128)}, f32[384,128]{1,0:T(8,128)}, f32[3,384,128]{2,1,0:T(8,128)}, f32[384,128]{1,0:T(8,128)}) custom-call(bf16[2,192,128]{2,1,0:T(8,128)(2,1)S(1)} %get-tuple-element.73.refs_0_, bf16[2,192,128]{2,1,0:T(8,128)(2,1)S(1)} %collective-permute-done.20.refs_1_, ...), custom_call_target="tpu_custom_call" | custom-call | bytes 2064384 | tf_op jit(solution)/shard_map/pallas_call | solution.py:471
  46.2 0.7 %shard_map.146 = (f32[3,384,128]{2,1,0:T(8,128)}, f32[384,128]{1,0:T(8,128)}, f32[3,384,128]{2,1,0:T(8,128)}, f32[384,128]{1,0:T(8,128)}) custom-call(bf16[2,192,128]{2,1,0:T(8,128)(2,1)S(1)} %collective-permute-done.19.refs_0_, f32[3,384,128]{2,1,0:T(8,128)} %get-tuple-element.75.refs_1_, ...), custom_call_target="tpu_custom_call", output_to_operand_aliasing={{0}: (1, {}), {1}: (2, {}), {2}: (3, {}), {3}: (4, {})} | custom-call | bytes 294912 | tf_op jit(solution)/shard_map/pallas_call | solution.py:471
  (55 shorter events, 3.0 us)
Async XLA Ops:
  0.6 8.9 %collective-permute-start.3 = (bf16[16,64,128]{2,1,0:T(8,128)(2,1)}, bf16[16,64,128]{2,1,0:T(8,128)(2,1)S(1)}, u32[]{:S(2)}, u32[]{:S(2)}) collective-permute-start(bf16[16,64,128]{2,1,0:T(8,128)(2,1)} %bitcast.10), channel_id=1, source_target_pairs={{4,0},{0,4},{5,1},{1,5},{6,2},{2,6},{7,3},{3,7},{12,8},{8,12},{13,... | collective-permute-start | bytes 786440 | tf_op jit(solution)/shard_map/ppermute | solution.py:73
  2.7 5.4 %copy-start = (bf16[1,1,16,64,128]{4,3,2,1,0:T(8,128)(2,1)S(1)}, bf16[1,1,16,64,128]{4,3,2,1,0:T(8,128)(2,1)}, u32[]{:S(2)}) copy-start(bf16[1,1,16,64,128]{4,3,2,1,0:T(8,128)(2,1)} %param.9) | copy-start | bytes 786436
  2.7 5.4 %copy-start.1 = (bf16[3,3,128,128]{3,2,1,0:T(8,128)(2,1)S(1)}, bf16[3,3,128,128]{3,2,1,0:T(8,128)(2,1)}, u32[]{:S(2)}) copy-start(bf16[3,3,128,128]{3,2,1,0:T(8,128)(2,1)} %refs_8_.1) | copy-start | bytes 884740
  2.7 5.4 %copy-start.2 = (bf16[1,1,16,64,128]{4,3,2,1,0:T(8,128)(2,1)S(1)}, bf16[1,1,16,64,128]{4,3,2,1,0:T(8,128)(2,1)}, u32[]{:S(2)}) copy-start(bf16[1,1,16,64,128]{4,3,2,1,0:T(8,128)(2,1)} %param.13) | copy-start | bytes 786436
  2.7 5.4 %copy-start.6 = (bf16[3,128,128]{2,1,0:T(8,128)(2,1)S(1)}, bf16[3,128,128]{2,1,0:T(8,128)(2,1)}, u32[]{:S(2)}) copy-start(bf16[3,128,128]{2,1,0:T(8,128)(2,1)} %refs_7_.1) | copy-start | bytes 294916
  4.4 2.1 %collective-permute-start = (bf16[4,64,128]{2,1,0:T(8,128)(2,1)}, bf16[4,64,128]{2,1,0:T(8,128)(2,1)S(1)}, u32[]{:S(2)}, u32[]{:S(2)}) collective-permute-start(bf16[4,64,128]{2,1,0:T(8,128)(2,1)} %get-tuple-element.45), channel_id=1, source_target_pairs={{8,0},{0,8},{24,16},{16,24},{9,1},{1,9},{25,17},{17,25},{10,2},{2,... | collective-permute-start | bytes 196616 | tf_op jit(solution)/shard_map/ppermute | solution.py:73
  6.5 3.0 %copy-start.5 = (bf16[1,1,16,64,128]{4,3,2,1,0:T(8,128)(2,1)S(1)}, bf16[1,1,16,64,128]{4,3,2,1,0:T(8,128)(2,1)}, u32[]{:S(2)}) copy-start(bf16[1,1,16,64,128]{4,3,2,1,0:T(8,128)(2,1)} %param.12) | copy-start | bytes 786436
  6.5 3.0 %copy-start.7 = (bf16[3,128,128]{2,1,0:T(8,128)(2,1)S(1)}, bf16[3,128,128]{2,1,0:T(8,128)(2,1)}, u32[]{:S(2)}) copy-start(bf16[3,128,128]{2,1,0:T(8,128)(2,1)} %refs_11_.1) | copy-start | bytes 294916
  6.5 1.7 %collective-permute-start.1 = (bf16[4,64,128]{2,1,0:T(8,128)(2,1)}, bf16[4,64,128]{2,1,0:T(8,128)(2,1)S(1)}, u32[]{:S(2)}, u32[]{:S(2)}) collective-permute-start(bf16[4,64,128]{2,1,0:T(8,128)(2,1)} %get-tuple-element.46), channel_id=1, source_target_pairs={{8,0},{0,8},{24,16},{16,24},{9,1},{1,9},{25,17},{17,25},{10,2},{2,... | collective-permute-start | bytes 196616 | tf_op jit(solution)/shard_map/ppermute | solution.py:73
  6.9 3.6 %collective-permute-start.2 = (bf16[4,64,128]{2,1,0:T(8,128)(2,1)S(1)}, bf16[4,64,128]{2,1,0:T(8,128)(2,1)S(1)}, u32[]{:S(2)}, u32[]{:S(2)}) collective-permute-start(bf16[4,64,128]{2,1,0:T(8,128)(2,1)S(1)} %collective-permute-done.refs_5_), channel_id=1, source_target_pairs={{16,0},{24,8},{0,16},{8,24},{17,1},{25,9},{1,17},{9,25},{18,2},{26... | collective-permute-start | bytes 196616 | tf_op jit(solution)/shard_map/ppermute | solution.py:73
  8.2 6.9 %collective-permute-start.4 = (bf16[14,64,128]{2,1,0:T(8,128)(2,1)S(1)}, bf16[14,64,128]{2,1,0:T(8,128)(2,1)S(1)}, u32[]{:S(2)}, u32[]{:S(2)}) collective-permute-start(bf16[14,64,128]{2,1,0:T(8,128)(2,1)S(1)} %get-tuple-element.47.refs_5_), channel_id=1, source_target_pairs={{4,0},{0,4},{5,1},{1,5},{6,2},{2,6},{7,3},{3,7},{12,8},{8,12},{13,... | collective-permute-start | bytes 688136 | tf_op jit(solution)/shard_map/ppermute | solution.py:73
  11.5 2.1 %collective-permute-start.6 = (bf16[384,128]{1,0:T(8,128)(2,1)S(1)}, bf16[384,128]{1,0:T(8,128)(2,1)S(1)}, u32[]{:S(2)}, u32[]{:S(2)}) collective-permute-start(bf16[384,128]{1,0:T(8,128)(2,1)S(1)} %get-tuple-element.54), channel_id=1, source_target_pairs={{8,0},{0,8},{24,16},{16,24},{9,1},{1,9},{25,17},{17,25},{10,2},{2,... | collective-permute-start | bytes 294920 | tf_op jit(solution)/shard_map/ppermute | solution.py:73
  12.4 1.3 %collective-permute-start.7 = (bf16[384,128]{1,0:T(8,128)(2,1)S(1)}, bf16[384,128]{1,0:T(8,128)(2,1)S(1)}, u32[]{:S(2)}, u32[]{:S(2)}) collective-permute-start(bf16[384,128]{1,0:T(8,128)(2,1)S(1)} %get-tuple-element.55), channel_id=1, source_target_pairs={{8,0},{0,8},{24,16},{16,24},{9,1},{1,9},{25,17},{17,25},{10,2},{2,... | collective-permute-start | bytes 294920 | tf_op jit(solution)/shard_map/ppermute | solution.py:73
  12.4 4.2 %collective-permute-start.5 = (bf16[4,64,128]{2,1,0:T(8,128)(2,1)S(1)}, bf16[4,64,128]{2,1,0:T(8,128)(2,1)S(1)}, u32[]{:S(2)}, u32[]{:S(2)}) collective-permute-start(bf16[4,64,128]{2,1,0:T(8,128)(2,1)S(1)} %shard_map.131.refs_7_), channel_id=1, source_target_pairs={{4,0},{0,4},{5,1},{1,5},{6,2},{2,6},{7,3},{3,7},{12,8},{8,12},{13,... | collective-permute-start | bytes 196616 | tf_op jit(solution)/shard_map/ppermute | solution.py:73
  13.7 4.2 %collective-permute-start.8 = (bf16[384,128]{1,0:T(8,128)(2,1)S(1)}, bf16[384,128]{1,0:T(8,128)(2,1)S(1)}, u32[]{:S(2)}, u32[]{:S(2)}) collective-permute-start(bf16[384,128]{1,0:T(8,128)(2,1)S(1)} %get-tuple-element.60), channel_id=1, source_target_pairs={{16,0},{24,8},{0,16},{8,24},{17,1},{25,9},{1,17},{9,25},{18,2},{26... | collective-permute-start | bytes 294920 | tf_op jit(solution)/shard_map/ppermute | solution.py:73
  17.9 2.5 %collective-permute-start.9 = (bf16[896,128]{1,0:T(8,128)(2,1)S(1)}, bf16[896,128]{1,0:T(8,128)(2,1)S(1)}, u32[]{:S(2)}, u32[]{:S(2)}) collective-permute-start(bf16[896,128]{1,0:T(8,128)(2,1)S(1)} %get-tuple-element.61), channel_id=1, source_target_pairs={{8,0},{0,8},{24,16},{16,24},{9,1},{1,9},{25,17},{17,25},{10,2},{2,... | collective-permute-start | bytes 688136 | tf_op jit(solution)/shard_map/ppermute | solution.py:73
  19.1 4.1 %collective-permute-start.13 = (bf16[320,128]{1,0:T(8,128)(2,1)S(1)}, bf16[320,128]{1,0:T(8,128)(2,1)S(1)}, u32[]{:S(2)}, u32[]{:S(2)}) collective-permute-start(bf16[320,128]{1,0:T(8,128)(2,1)S(1)} %get-tuple-element.63.refs_2_), channel_id=1, source_target_pairs={{4,0},{0,4},{5,1},{1,5},{6,2},{2,6},{7,3},{3,7},{12,8},{8,12},{13,... | collective-permute-start | bytes 245768 | tf_op jit(solution)/shard_map/ppermute | solution.py:73
  20.5 6.9 %collective-permute-start.12 = (bf16[272,128]{1,0:T(8,128)(2,1)S(1)}, bf16[272,128]{1,0:T(8,128)(2,1)S(1)}, u32[]{:S(2)}, u32[]{:S(2)}) collective-permute-start(bf16[272,128]{1,0:T(8,128)(2,1)S(1)} %get-tuple-element.67), channel_id=1, source_target_pairs={{20,0},{16,4},{28,8},{24,12},{4,16},{0,20},{12,24},{8,28},{21,1},{... | collective-permute-start | bytes 208904 | tf_op jit(solution)/shard_map/ppermute | solution.py:81
  22.4 5.0 %collective-permute-start.10 = (bf16[256,128]{1,0:T(8,128)(2,1)S(1)}, bf16[256,128]{1,0:T(8,128)(2,1)S(1)}, u32[]{:S(2)}, u32[]{:S(2)}) collective-permute-start(bf16[256,128]{1,0:T(8,128)(2,1)S(1)} %get-tuple-element.64), channel_id=1, source_target_pairs={{16,0},{24,8},{0,16},{8,24},{17,1},{25,9},{1,17},{9,25},{18,2},{26... | collective-permute-start | bytes 196616 | tf_op jit(solution)/shard_map/ppermute | solution.py:73
  22.8 3.3 %collective-permute-start.11 = (bf16[192,128]{1,0:T(8,128)(2,1)S(1)}, bf16[192,128]{1,0:T(8,128)(2,1)S(1)}, u32[]{:S(2)}, u32[]{:S(2)}) collective-permute-start(bf16[192,128]{1,0:T(8,128)(2,1)S(1)} %get-tuple-element.66), channel_id=1, source_target_pairs={{4,0},{0,4},{5,1},{1,5},{6,2},{2,6},{7,3},{3,7},{12,8},{8,12},{13,... | collective-permute-start | bytes 147464 | tf_op jit(solution)/shard_map/ppermute | solution.py:73
  23.3 5.5 %collective-permute-start.15 = (bf16[192,128]{1,0:T(8,128)(2,1)S(1)}, bf16[192,128]{1,0:T(8,128)(2,1)S(1)}, u32[]{:S(2)}, u32[]{:S(2)}) collective-permute-start(bf16[192,128]{1,0:T(8,128)(2,1)S(1)} %shard_map.140.refs_0_), channel_id=1, source_target_pairs={{1,0},{0,1},{3,2},{2,3},{5,4},{4,5},{7,6},{6,7},{9,8},{8,9},{11,10... | collective-permute-start | bytes 147464 | tf_op jit(solution)/shard_map/ppermute | solution.py:73
  27.4 5.4 %copy-start.8 = (bf16[3,3,128,128]{3,2,1,0:T(8,128)(2,1)S(1)}, bf16[3,3,128,128]{3,2,1,0:T(8,128)(2,1)}, u32[]{:S(2)}) copy-start(bf16[3,3,128,128]{3,2,1,0:T(8,128)(2,1)} %refs_4_.5) | copy-start | bytes 884740
  27.4 3.7 %collective-permute-start.14 = (bf16[192,128]{1,0:T(8,128)(2,1)S(1)}, bf16[192,128]{1,0:T(8,128)(2,1)S(1)}, u32[]{:S(2)}, u32[]{:S(2)}) collective-permute-start(bf16[192,128]{1,0:T(8,128)(2,1)S(1)} %shard_map.139.refs_0_), channel_id=1, source_target_pairs={{1,0},{0,1},{3,2},{2,3},{5,4},{4,5},{7,6},{6,7},{9,8},{8,9},{11,10... | collective-permute-start | bytes 147464 | tf_op jit(solution)/shard_map/ppermute | solution.py:73
  28.8 5.5 %collective-permute-start.17 = (bf16[192,128]{1,0:T(8,128)(2,1)S(1)}, bf16[192,128]{1,0:T(8,128)(2,1)S(1)}, u32[]{:S(2)}, u32[]{:S(2)}) collective-permute-start(bf16[192,128]{1,0:T(8,128)(2,1)S(1)} %shard_map.143.refs_2_), channel_id=1, source_target_pairs={{2,0},{3,1},{0,2},{1,3},{6,4},{7,5},{4,6},{5,7},{10,8},{11,9},{8,1... | collective-permute-start | bytes 147464 | tf_op jit(solution)/shard_map/ppermute | solution.py:73
  31.2 4.4 %collective-permute-start.16 = (bf16[192,128]{1,0:T(8,128)(2,1)S(1)}, bf16[192,128]{1,0:T(8,128)(2,1)S(1)}, u32[]{:S(2)}, u32[]{:S(2)}) collective-permute-start(bf16[192,128]{1,0:T(8,128)(2,1)S(1)} %shard_map.141.refs_5_.refs_0_), channel_id=1, source_target_pairs={{2,0},{3,1},{0,2},{1,3},{6,4},{7,5},{4,6},{5,7},{10,8},{11,9},{8,1... | collective-permute-start | bytes 147464 | tf_op jit(solution)/shard_map/ppermute | solution.py:73
  35.7 3.6 %collective-permute-start.21 = (bf16[2,208,128]{2,1,0:T(8,128)(2,1)S(1)}, bf16[2,208,128]{2,1,0:T(8,128)(2,1)S(1)}, u32[]{:S(2)}, u32[]{:S(2)}) collective-permute-start(bf16[2,208,128]{2,1,0:T(8,128)(2,1)S(1)} %get-tuple-element.74), channel_id=1, source_target_pairs={{16,0},{24,8},{0,16},{8,24},{17,1},{25,9},{1,17},{9,25},{18,2},{26... | collective-permute-start | bytes 319496 | tf_op jit(solution)/shard_map/ppermute | solution.py:73
  36.7 6.5 %collective-permute-start.20 = (bf16[2,192,128]{2,1,0:T(8,128)(2,1)S(1)}, bf16[2,192,128]{2,1,0:T(8,128)(2,1)S(1)}, u32[]{:S(2)}, u32[]{:S(2)}) collective-permute-start(bf16[2,192,128]{2,1,0:T(8,128)(2,1)S(1)} %get-tuple-element.73.refs_0_), channel_id=1, source_target_pairs={{4,0},{0,4},{5,1},{1,5},{6,2},{2,6},{7,3},{3,7},{12,8},{8,12},{13,... | collective-permute-start | bytes 294920 | tf_op jit(solution)/shard_map/ppermute | solution.py:73
  37.1 6.7 %collective-permute-start.18 = (bf16[2,192,128]{2,1,0:T(8,128)(2,1)S(1)}, bf16[2,192,128]{2,1,0:T(8,128)(2,1)S(1)}, u32[]{:S(2)}, u32[]{:S(2)}) collective-permute-start(bf16[2,192,128]{2,1,0:T(8,128)(2,1)S(1)} %get-tuple-element.73.refs_0_), channel_id=1, source_target_pairs={{20,0},{16,4},{28,8},{24,12},{4,16},{0,20},{12,24},{8,28},{21,1},{... | collective-permute-start | bytes 294920 | tf_op jit(solution)/shard_map/ppermute | solution.py:81
  39.3 5.6 %collective-permute-start.24 = (bf16[2,208,128]{2,1,0:T(8,128)(2,1)S(1)}, bf16[2,208,128]{2,1,0:T(8,128)(2,1)S(1)}, u32[]{:S(2)}, u32[]{:S(2)}) collective-permute-start(bf16[2,208,128]{2,1,0:T(8,128)(2,1)S(1)} %collective-permute-done.21.refs_2_), channel_id=1, source_target_pairs={{8,0},{0,8},{24,16},{16,24},{9,1},{1,9},{25,17},{17,25},{10,2},{2,... | collective-permute-start | bytes 319496 | tf_op jit(solution)/shard_map/ppermute | solution.py:73
  43.2 1.7 %collective-permute-start.22 = (bf16[2,192,128]{2,1,0:T(8,128)(2,1)S(1)}, bf16[2,192,128]{2,1,0:T(8,128)(2,1)S(1)}, u32[]{:S(2)}, u32[]{:S(2)}) collective-permute-start(bf16[2,192,128]{2,1,0:T(8,128)(2,1)S(1)} %get-tuple-element.73.refs_0_), channel_id=1, source_target_pairs={{8,0},{0,8},{24,16},{16,24},{9,1},{1,9},{25,17},{17,25},{10,2},{2,... | collective-permute-start | bytes 294920 | tf_op jit(solution)/shard_map/ppermute | solution.py:73
  43.2 1.7 %collective-permute-start.23 = (bf16[2,192,128]{2,1,0:T(8,128)(2,1)S(1)}, bf16[2,192,128]{2,1,0:T(8,128)(2,1)S(1)}, u32[]{:S(2)}, u32[]{:S(2)}) collective-permute-start(bf16[2,192,128]{2,1,0:T(8,128)(2,1)S(1)} %collective-permute-done.20.refs_1_), channel_id=1, source_target_pairs={{8,0},{0,8},{24,16},{16,24},{9,1},{1,9},{25,17},{17,25},{10,2},{2,... | collective-permute-start | bytes 294920 | tf_op jit(solution)/shard_map/ppermute | solution.py:73
  43.7 2.4 %collective-permute-start.19 = (bf16[2,192,128]{2,1,0:T(8,128)(2,1)S(1)}, bf16[2,192,128]{2,1,0:T(8,128)(2,1)S(1)}, u32[]{:S(2)}, u32[]{:S(2)}) collective-permute-start(bf16[2,192,128]{2,1,0:T(8,128)(2,1)S(1)} %collective-permute-done.18.refs_6_), channel_id=1, source_target_pairs={{8,0},{0,8},{24,16},{16,24},{9,1},{1,9},{25,17},{17,25},{10,2},{2,... | collective-permute-start | bytes 294920 | tf_op jit(solution)/shard_map/ppermute | solution.py:73
  (2 other events, 6.1 us)

commit v25 on v17

--- a/solution.py
+++ b/solution.py
@@ -682,7 +682,7 @@
 
         keep_two, send_two = call(
             band_kernel,
-            [f32(half, ch), bf16(half + 2 * cols, ch)],
+            [f32(half, ch), bf16(half + cols + 32, ch)],
             [],
             0,
             own_two,

time: 47.1 us -> 47.1 us (level)
  no operation moved by 1% of the time
where the time goes in v25:
time: 47.1 us; the launch traced here: 46.8 us
  starting transfers between devices  30.5 us (65%)
  Pallas kernels  9.26 us (20%)
  waiting for transfers between devices  6.16 us (13%)
  between operations  0.83 us (2%)
    ppermute x23, starting transfers between devices, flipped(): lax.ppermute(block, axis, [(place ^ flip, place) for place in range(count)])  27.5 us
    pallas_call x17, Pallas kernels, call(): pl.pallas_call(body, out_shape=outs[0] if single else tuple(outs), in_spe...  7.35 us
    ppermute x23, waiting for transfers between devices, flipped(): lax.ppermute(block, axis, [(place ^ flip, place) for place in range(count)])  6.15 us
    ppermute x2, starting transfers between devices, flipped_both(): return lax.ppermute(block, ('section', 'video'), pairs)  3.08 us
    pallas_call x2, Pallas kernels, placed(): pl.pallas_call(functools.partial(place_kernel, places), out_shape=outs, i...  1.91 us
  transfers between devices with their start and end apart: 25, of which 6 were waited for; matrix products, arithmetic and copies ran while one was open for 0% of the time, Pallas kernels for 18%

profile of v25, /device:TPU:1, one launch (start us, length us, event | category | flops | bytes accessed | tf_op | source)
XLA Modules:
  0.0 46.8 jit_solution(2850368692376524139)
XLA Ops:
  0.6 2.1 %collective-permute-start.3 = (bf16[16,64,128]{2,1,0:T(8,128)(2,1)}, bf16[16,64,128]{2,1,0:T(8,128)(2,1)S(1)}, u32[]{:S(2)}, u32[]{:S(2)}) collective-permute-start(bf16[16,64,128]{2,1,0:T(8,128)(2,1)} %bitcast.10), channel_id=1, source_target_pairs={{4,0},{0,4},{5,1},{1,5},{6,2},{2,6},{7,3},{3,7},{12,8},{8,12},{13,... | collective-permute-start | bytes 786440 | tf_op jit(solution)/shard_map/ppermute | solution.py:73
  2.7 1.6 %shard_map.128 = (bf16[4,64,128]{2,1,0:T(8,128)(2,1)}, bf16[4,64,128]{2,1,0:T(8,128)(2,1)}) custom-call(bf16[16,64,128]{2,1,0:T(8,128)(2,1)} %bitcast.11, bf16[16,64,128]{2,1,0:T(8,128)(2,1)} %bitcast.17, bf16[16,64,128]{2,1,0:T(8,128)(2,1)} %bitcast.28, bf16[16,64,128]{2,1,0:T(8,128)(2,1)} %bitcast.25), custom_call_target="tpu_custom_call" | custom-call | flops 1 | bytes 1179648 | tf_op jit(solution)/shard_map/pallas_call | solution.py:38
  4.4 1.0 %collective-permute-start = (bf16[4,64,128]{2,1,0:T(8,128)(2,1)}, bf16[4,64,128]{2,1,0:T(8,128)(2,1)S(1)}, u32[]{:S(2)}, u32[]{:S(2)}) collective-permute-start(bf16[4,64,128]{2,1,0:T(8,128)(2,1)} %get-tuple-element.43), channel_id=1, source_target_pairs={{8,0},{0,8},{24,16},{16,24},{9,1},{1,9},{25,17},{17,25},{10,2},{2,... | collective-permute-start | bytes 196616 | tf_op jit(solution)/shard_map/ppermute | solution.py:73
  5.4 1.1 %collective-permute-done.refs_5_ = bf16[4,64,128]{2,1,0:T(8,128)(2,1)S(1)} collective-permute-done((bf16[4,64,128]{2,1,0:T(8,128)(2,1)}, bf16[4,64,128]{2,1,0:T(8,128)(2,1)S(1)}, u32[]{:S(2)}, u32[]{:S(2)}) %collective-permute-start) | collective-permute-done | bytes 65568 | tf_op jit(solution)/shard_map/ppermute | solution.py:73
  6.9 1.2 %collective-permute-start.2 = (bf16[4,64,128]{2,1,0:T(8,128)(2,1)S(1)}, bf16[4,64,128]{2,1,0:T(8,128)(2,1)S(1)}, u32[]{:S(2)}, u32[]{:S(2)}) collective-permute-start(bf16[4,64,128]{2,1,0:T(8,128)(2,1)S(1)} %collective-permute-done.refs_5_), channel_id=1, source_target_pairs={{16,0},{24,8},{0,16},{8,24},{17,1},{25,9},{1,17},{9,25},{18,2},{26... | collective-permute-start | bytes 196616 | tf_op jit(solution)/shard_map/ppermute | solution.py:73
  8.2 1.3 %collective-permute-start.4 = (bf16[14,64,128]{2,1,0:T(8,128)(2,1)S(1)}, bf16[14,64,128]{2,1,0:T(8,128)(2,1)S(1)}, u32[]{:S(2)}, u32[]{:S(2)}) collective-permute-start(bf16[14,64,128]{2,1,0:T(8,128)(2,1)S(1)} %get-tuple-element.45.refs_5_), channel_id=1, source_target_pairs={{4,0},{0,4},{5,1},{1,5},{6,2},{2,6},{7,3},{3,7},{12,8},{8,12},{13,... | collective-permute-start | bytes 688136 | tf_op jit(solution)/shard_map/ppermute | solution.py:73
  9.6 1.0 %shard_map.130 = (bf16[14,64,128]{2,1,0:T(8,128)(2,1)S(1)}, bf16[16,64,128]{2,1,0:T(8,128)(2,1)S(1)}) custom-call(bf16[16,64,128]{2,1,0:T(8,128)(2,1)S(1)} %bitcast.13, bf16[16,64,128]{2,1,0:T(8,128)(2,1)S(1)} %bitcast.19, bf16[16,64,128]{2,1,0:T(8,128)(2,1)S(1)} %collective-permute-done.3.refs_2_.refs_6_, bf16[3,128,128]{2,1,0:T(8,128)(2,1)S(1)} %copy-done.6, ...), custom_call_target="tpu_custom_call" | custom-call | tf_op jit(solution)/shard_map/pallas_call | solution.py:38
  10.6 0.9 %shard_map.132 = (f32[2,384,128]{2,1,0:T(8,128)S(1)}, bf16[384,128]{1,0:T(8,128)(2,1)S(1)}, bf16[384,128]{1,0:T(8,128)(2,1)S(1)}) custom-call(bf16[16,64,128]{2,1,0:T(8,128)(2,1)S(1)} %bitcast.30, bf16[16,64,128]{2,1,0:T(8,128)(2,1)S(1)} %bitcast.20, bf16[16,64,128]{2,1,0:T(8,128)(2,1)S(1)} %get-tuple-element.48.refs_6_.refs_2_.refs_4_, ...), custom_call_target="tpu_custom_call" | custom-call | flops 2415919104 | bytes 2031616 | tf_op jit(solution)/shard_map/pallas_call | solution.py:38
  11.5 0.9 %collective-permute-start.6 = (bf16[384,128]{1,0:T(8,128)(2,1)S(1)}, bf16[384,128]{1,0:T(8,128)(2,1)S(1)}, u32[]{:S(2)}, u32[]{:S(2)}) collective-permute-start(bf16[384,128]{1,0:T(8,128)(2,1)S(1)} %get-tuple-element.52), channel_id=1, source_target_pairs={{8,0},{0,8},{24,16},{16,24},{9,1},{1,9},{25,17},{17,25},{10,2},{2,... | collective-permute-start | bytes 294920 | tf_op jit(solution)/shard_map/ppermute | solution.py:73
  12.4 0.8 %collective-permute-start.5 = (bf16[4,64,128]{2,1,0:T(8,128)(2,1)S(1)}, bf16[4,64,128]{2,1,0:T(8,128)(2,1)S(1)}, u32[]{:S(2)}, u32[]{:S(2)}) collective-permute-start(bf16[4,64,128]{2,1,0:T(8,128)(2,1)S(1)} %shard_map.131.refs_7_), channel_id=1, source_target_pairs={{4,0},{0,4},{5,1},{1,5},{6,2},{2,6},{7,3},{3,7},{12,8},{8,12},{13,... | collective-permute-start | bytes 196616 | tf_op jit(solution)/shard_map/ppermute | solution.py:73
  13.7 1.4 %collective-permute-start.8 = (bf16[384,128]{1,0:T(8,128)(2,1)S(1)}, bf16[384,128]{1,0:T(8,128)(2,1)S(1)}, u32[]{:S(2)}, u32[]{:S(2)}) collective-permute-start(bf16[384,128]{1,0:T(8,128)(2,1)S(1)} %get-tuple-element.58), channel_id=1, source_target_pairs={{16,0},{24,8},{0,16},{8,24},{17,1},{25,9},{1,17},{9,25},{18,2},{26... | collective-permute-start | bytes 294920 | tf_op jit(solution)/shard_map/ppermute | solution.py:73
  15.6 1.0 %collective-permute-done.5.refs_6_ = bf16[4,64,128]{2,1,0:T(8,128)(2,1)S(1)} collective-permute-done((bf16[4,64,128]{2,1,0:T(8,128)(2,1)S(1)}, bf16[4,64,128]{2,1,0:T(8,128)(2,1)S(1)}, u32[]{:S(2)}, u32[]{:S(2)}) %collective-permute-start.5) | collective-permute-done | bytes 65568 | tf_op jit(solution)/shard_map/ppermute | solution.py:73
  16.6 1.3 %shard_map.136 = (bf16[16,64,128]{2,1,0:T(8,128)(2,1)S(1)}, bf16[16,64,128]{2,1,0:T(8,128)(2,1)S(1)}, f32[2,384,128]{2,1,0:T(8,128)S(1)}, bf16[896,128]{1,0:T(8,128)(2,1)S(1)}) custom-call(bf16[16,64,128]{2,1,0:T(8,128)(2,1)S(1)} %bitcast.16, bf16[4,64,128]{2,1,0:T(8,128)(2,1)S(1)} %collective-permute-done.1.refs_4_.refs_1_.refs_3_.refs_2_, ...), custom_call_target="tpu_custom_call" | custom-call | flops 2415919104 | bytes 5046272 | tf_op jit(solution)/shard_map/pallas_call | solution.py:38
  17.9 1.2 %collective-permute-start.9 = (bf16[896,128]{1,0:T(8,128)(2,1)S(1)}, bf16[896,128]{1,0:T(8,128)(2,1)S(1)}, u32[]{:S(2)}, u32[]{:S(2)}) collective-permute-start(bf16[896,128]{1,0:T(8,128)(2,1)S(1)} %get-tuple-element.59), channel_id=1, source_target_pairs={{8,0},{0,8},{24,16},{16,24},{9,1},{1,9},{25,17},{17,25},{10,2},{2,... | collective-permute-start | bytes 688136 | tf_op jit(solution)/shard_map/ppermute | solution.py:73
  19.1 1.3 %collective-permute-start.13 = (bf16[288,128]{1,0:T(8,128)(2,1)S(1)}, bf16[288,128]{1,0:T(8,128)(2,1)S(1)}, u32[]{:S(2)}, u32[]{:S(2)}) collective-permute-start(bf16[288,128]{1,0:T(8,128)(2,1)S(1)} %get-tuple-element.61.refs_2_), channel_id=1, source_target_pairs={{4,0},{0,4},{5,1},{1,5},{6,2},{2,6},{7,3},{3,7},{12,8},{8,12},{13,... | collective-permute-start | bytes 221192 | tf_op jit(solution)/shard_map/ppermute | solution.py:73
  20.5 1.9 %collective-permute-start.12 = (bf16[272,128]{1,0:T(8,128)(2,1)S(1)}, bf16[272,128]{1,0:T(8,128)(2,1)S(1)}, u32[]{:S(2)}, u32[]{:S(2)}) collective-permute-start(bf16[272,128]{1,0:T(8,128)(2,1)S(1)} %get-tuple-element.65), channel_id=1, source_target_pairs={{20,0},{16,4},{28,8},{24,12},{4,16},{0,20},{12,24},{8,28},{21,1},{... | collective-permute-start | bytes 208904 | tf_op jit(solution)/shard_map/ppermute | solution.py:81
  23.2 1.4 %collective-permute-start.15 = (bf16[192,128]{1,0:T(8,128)(2,1)S(1)}, bf16[192,128]{1,0:T(8,128)(2,1)S(1)}, u32[]{:S(2)}, u32[]{:S(2)}) collective-permute-start(bf16[192,128]{1,0:T(8,128)(2,1)S(1)} %shard_map.140.refs_0_), channel_id=1, source_target_pairs={{1,0},{0,1},{3,2},{2,3},{5,4},{4,5},{7,6},{6,7},{9,8},{8,9},{11,10... | collective-permute-start | bytes 147464 | tf_op jit(solution)/shard_map/ppermute | solution.py:73
  24.6 1.3 %collective-permute-done.11.refs_2_ = bf16[192,128]{1,0:T(8,128)(2,1)S(1)} collective-permute-done((bf16[192,128]{1,0:T(8,128)(2,1)S(1)}, bf16[192,128]{1,0:T(8,128)(2,1)S(1)}, u32[]{:S(2)}, u32[]{:S(2)}) %collective-permute-start.11) | collective-permute-done | bytes 49184 | tf_op jit(solution)/shard_map/ppermute | solution.py:73
  25.9 1.1 %collective-permute-done.10.refs_1_.refs_3_ = bf16[256,128]{1,0:T(8,128)(2,1)S(1)} collective-permute-done((bf16[256,128]{1,0:T(8,128)(2,1)S(1)}, bf16[256,128]{1,0:T(8,128)(2,1)S(1)}, u32[]{:S(2)}, u32[]{:S(2)}) %collective-permute-start.10) | collective-permute-done | bytes 65568 | tf_op jit(solution)/shard_map/ppermute | solution.py:73
  27.1 1.3 %collective-permute-start.14 = (bf16[192,128]{1,0:T(8,128)(2,1)S(1)}, bf16[192,128]{1,0:T(8,128)(2,1)S(1)}, u32[]{:S(2)}, u32[]{:S(2)}) collective-permute-start(bf16[192,128]{1,0:T(8,128)(2,1)S(1)} %shard_map.139.refs_0_), channel_id=1, source_target_pairs={{1,0},{0,1},{3,2},{2,3},{5,4},{4,5},{7,6},{6,7},{9,8},{8,9},{11,10... | collective-permute-start | bytes 147464 | tf_op jit(solution)/shard_map/ppermute | solution.py:73
  28.5 2.4 %collective-permute-start.17 = (bf16[192,128]{1,0:T(8,128)(2,1)S(1)}, bf16[192,128]{1,0:T(8,128)(2,1)S(1)}, u32[]{:S(2)}, u32[]{:S(2)}) collective-permute-start(bf16[192,128]{1,0:T(8,128)(2,1)S(1)} %shard_map.143.refs_2_), channel_id=1, source_target_pairs={{2,0},{3,1},{0,2},{1,3},{6,4},{7,5},{4,6},{5,7},{10,8},{11,9},{8,1... | collective-permute-start | bytes 147464 | tf_op jit(solution)/shard_map/ppermute | solution.py:73
  30.9 1.6 %collective-permute-start.16 = (bf16[192,128]{1,0:T(8,128)(2,1)S(1)}, bf16[192,128]{1,0:T(8,128)(2,1)S(1)}, u32[]{:S(2)}, u32[]{:S(2)}) collective-permute-start(bf16[192,128]{1,0:T(8,128)(2,1)S(1)} %shard_map.141.refs_5_.refs_0_), channel_id=1, source_target_pairs={{2,0},{3,1},{0,2},{1,3},{6,4},{7,5},{4,6},{5,7},{10,8},{11,9},{8,1... | collective-permute-start | bytes 147464 | tf_op jit(solution)/shard_map/ppermute | solution.py:73
  32.5 1.5 %shard_map.142 = (bf16[16,64,128]{2,1,0:T(8,128)(2,1)}, f32[8,128]{1,0:T(8,128)S(1)}) custom-call(bf16[16,64,128]{2,1,0:T(8,128)(2,1)S(1)} %get-tuple-element.55.refs_0_, bf16[16,64,128]{2,1,0:T(8,128)(2,1)S(1)} %get-tuple-element.56.refs_1_, bf16[896,128]{1,0:T(8,128)(2,1)S(1)} %collective-permute-done.9.refs_1_.refs_2_, ...), custom_call_target="tpu_custom_call" | custom-call | flops 301989888 | bytes 1380352 | tf_op jit(solution)/shard_map/pallas_call | solution.py:38
  34.0 1.5 %collective-permute-done.16.refs_1_ = bf16[192,128]{1,0:T(8,128)(2,1)S(1)} collective-permute-done((bf16[192,128]{1,0:T(8,128)(2,1)S(1)}, bf16[192,128]{1,0:T(8,128)(2,1)S(1)}, u32[]{:S(2)}, u32[]{:S(2)}) %collective-permute-start.16) | collective-permute-done | bytes 49184 | tf_op jit(solution)/shard_map/ppermute | solution.py:73
  35.5 0.9 %collective-permute-start.20 = (bf16[2,192,128]{2,1,0:T(8,128)(2,1)S(1)}, bf16[2,192,128]{2,1,0:T(8,128)(2,1)S(1)}, u32[]{:S(2)}, u32[]{:S(2)}) collective-permute-start(bf16[2,192,128]{2,1,0:T(8,128)(2,1)S(1)} %shard_map.144.refs_0_), channel_id=1, source_target_pairs={{4,0},{0,4},{5,1},{1,5},{6,2},{2,6},{7,3},{3,7},{12,8},{8,12},{13,... | collective-permute-start | bytes 294920 | tf_op jit(solution)/shard_map/ppermute | solution.py:73
  36.4 0.6 %collective-permute-start.21 = (bf16[2,192,128]{2,1,0:T(8,128)(2,1)S(1)}, bf16[2,192,128]{2,1,0:T(8,128)(2,1)S(1)}, u32[]{:S(2)}, u32[]{:S(2)}) collective-permute-start(bf16[2,192,128]{2,1,0:T(8,128)(2,1)S(1)} %shard_map.144.refs_0_), channel_id=1, source_target_pairs={{16,0},{24,8},{0,16},{8,24},{17,1},{25,9},{1,17},{9,25},{18,2},{26... | collective-permute-start | bytes 294920 | tf_op jit(solution)/shard_map/ppermute | solution.py:73
  37.0 1.2 %collective-permute-start.18 = (bf16[2,192,128]{2,1,0:T(8,128)(2,1)S(1)}, bf16[2,192,128]{2,1,0:T(8,128)(2,1)S(1)}, u32[]{:S(2)}, u32[]{:S(2)}) collective-permute-start(bf16[2,192,128]{2,1,0:T(8,128)(2,1)S(1)} %shard_map.144.refs_0_), channel_id=1, source_target_pairs={{20,0},{16,4},{28,8},{24,12},{4,16},{0,20},{12,24},{8,28},{21,1},{... | collective-permute-start | bytes 294920 | tf_op jit(solution)/shard_map/ppermute | solution.py:81
  38.2 2.6 %collective-permute-start.22 = (bf16[2,192,128]{2,1,0:T(8,128)(2,1)S(1)}, bf16[2,192,128]{2,1,0:T(8,128)(2,1)S(1)}, u32[]{:S(2)}, u32[]{:S(2)}) collective-permute-start(bf16[2,192,128]{2,1,0:T(8,128)(2,1)S(1)} %shard_map.144.refs_0_), channel_id=1, source_target_pairs={{8,0},{0,8},{24,16},{16,24},{9,1},{1,9},{25,17},{17,25},{10,2},{2,... | collective-permute-start | bytes 294920 | tf_op jit(solution)/shard_map/ppermute | solution.py:73
  40.8 2.0 %collective-permute-start.23 = (bf16[2,192,128]{2,1,0:T(8,128)(2,1)S(1)}, bf16[2,192,128]{2,1,0:T(8,128)(2,1)S(1)}, u32[]{:S(2)}, u32[]{:S(2)}) collective-permute-start(bf16[2,192,128]{2,1,0:T(8,128)(2,1)S(1)} %collective-permute-done.20.refs_1_), channel_id=1, source_target_pairs={{8,0},{0,8},{24,16},{16,24},{9,1},{1,9},{25,17},{17,25},{10,2},{2,... | collective-permute-start | bytes 294920 | tf_op jit(solution)/shard_map/ppermute | solution.py:73
  43.3 1.6 %collective-permute-start.19 = (bf16[2,192,128]{2,1,0:T(8,128)(2,1)S(1)}, bf16[2,192,128]{2,1,0:T(8,128)(2,1)S(1)}, u32[]{:S(2)}, u32[]{:S(2)}) collective-permute-start(bf16[2,192,128]{2,1,0:T(8,128)(2,1)S(1)} %collective-permute-done.18.refs_6_), channel_id=1, source_target_pairs={{8,0},{0,8},{24,16},{16,24},{9,1},{1,9},{25,17},{17,25},{10,2},{2,... | collective-permute-start | bytes 294920 | tf_op jit(solution)/shard_map/ppermute | solution.py:73
  44.9 1.2 %shard_map.145 = (f32[3,384,128]{2,1,0:T(8,128)}, f32[384,128]{1,0:T(8,128)}, f32[3,384,128]{2,1,0:T(8,128)}, f32[384,128]{1,0:T(8,128)}) custom-call(bf16[2,192,128]{2,1,0:T(8,128)(2,1)S(1)} %shard_map.144.refs_0_, bf16[2,192,128]{2,1,0:T(8,128)(2,1)S(1)} %collective-permute-done.20.refs_1_, bf16[2,192,128]{2,1,0:T(8,128)(2,1)S(1)} %collective-permute-done.21.refs_2_, ...), custom_call_target="tpu_custom_call" | custom-call | bytes 2064384 | tf_op jit(solution)/shard_map/pallas_call | solution.py:467
  46.1 0.7 %shard_map.146 = (f32[3,384,128]{2,1,0:T(8,128)}, f32[384,128]{1,0:T(8,128)}, f32[3,384,128]{2,1,0:T(8,128)}, f32[384,128]{1,0:T(8,128)}) custom-call(bf16[2,192,128]{2,1,0:T(8,128)(2,1)S(1)} %collective-permute-done.19.refs_0_, f32[3,384,128]{2,1,0:T(8,128)} %get-tuple-element.71.refs_1_, ...), custom_call_target="tpu_custom_call", output_to_operand_aliasing={{0}: (1, {}), {1}: (2, {}), {2}: (3, {}), {3}: (4, {})} | custom-call | bytes 294912 | tf_op jit(solution)/shard_map/pallas_call | solution.py:467
  (55 shorter events, 3.1 us)
Async XLA Ops:
  0.6 8.9 %collective-permute-start.3 = (bf16[16,64,128]{2,1,0:T(8,128)(2,1)}, bf16[16,64,128]{2,1,0:T(8,128)(2,1)S(1)}, u32[]{:S(2)}, u32[]{:S(2)}) collective-permute-start(bf16[16,64,128]{2,1,0:T(8,128)(2,1)} %bitcast.10), channel_id=1, source_target_pairs={{4,0},{0,4},{5,1},{1,5},{6,2},{2,6},{7,3},{3,7},{12,8},{8,12},{13,... | collective-permute-start | bytes 786440 | tf_op jit(solution)/shard_map/ppermute | solution.py:73
  2.7 5.4 %copy-start = (bf16[1,1,16,64,128]{4,3,2,1,0:T(8,128)(2,1)S(1)}, bf16[1,1,16,64,128]{4,3,2,1,0:T(8,128)(2,1)}, u32[]{:S(2)}) copy-start(bf16[1,1,16,64,128]{4,3,2,1,0:T(8,128)(2,1)} %param.9) | copy-start | bytes 786436
  2.7 5.4 %copy-start.1 = (bf16[3,3,128,128]{3,2,1,0:T(8,128)(2,1)S(1)}, bf16[3,3,128,128]{3,2,1,0:T(8,128)(2,1)}, u32[]{:S(2)}) copy-start(bf16[3,3,128,128]{3,2,1,0:T(8,128)(2,1)} %refs_8_.1) | copy-start | bytes 884740
  2.7 5.4 %copy-start.2 = (bf16[1,1,16,64,128]{4,3,2,1,0:T(8,128)(2,1)S(1)}, bf16[1,1,16,64,128]{4,3,2,1,0:T(8,128)(2,1)}, u32[]{:S(2)}) copy-start(bf16[1,1,16,64,128]{4,3,2,1,0:T(8,128)(2,1)} %param.13) | copy-start | bytes 786436
  2.7 5.4 %copy-start.6 = (bf16[3,128,128]{2,1,0:T(8,128)(2,1)S(1)}, bf16[3,128,128]{2,1,0:T(8,128)(2,1)}, u32[]{:S(2)}) copy-start(bf16[3,128,128]{2,1,0:T(8,128)(2,1)} %refs_7_.1) | copy-start | bytes 294916
  4.4 2.1 %collective-permute-start = (bf16[4,64,128]{2,1,0:T(8,128)(2,1)}, bf16[4,64,128]{2,1,0:T(8,128)(2,1)S(1)}, u32[]{:S(2)}, u32[]{:S(2)}) collective-permute-start(bf16[4,64,128]{2,1,0:T(8,128)(2,1)} %get-tuple-element.43), channel_id=1, source_target_pairs={{8,0},{0,8},{24,16},{16,24},{9,1},{1,9},{25,17},{17,25},{10,2},{2,... | collective-permute-start | bytes 196616 | tf_op jit(solution)/shard_map/ppermute | solution.py:73
  6.5 3.0 %copy-start.5 = (bf16[1,1,16,64,128]{4,3,2,1,0:T(8,128)(2,1)S(1)}, bf16[1,1,16,64,128]{4,3,2,1,0:T(8,128)(2,1)}, u32[]{:S(2)}) copy-start(bf16[1,1,16,64,128]{4,3,2,1,0:T(8,128)(2,1)} %param.12) | copy-start | bytes 786436
  6.5 3.0 %copy-start.7 = (bf16[3,128,128]{2,1,0:T(8,128)(2,1)S(1)}, bf16[3,128,128]{2,1,0:T(8,128)(2,1)}, u32[]{:S(2)}) copy-start(bf16[3,128,128]{2,1,0:T(8,128)(2,1)} %refs_11_.1) | copy-start | bytes 294916
  6.5 1.7 %collective-permute-start.1 = (bf16[4,64,128]{2,1,0:T(8,128)(2,1)}, bf16[4,64,128]{2,1,0:T(8,128)(2,1)S(1)}, u32[]{:S(2)}, u32[]{:S(2)}) collective-permute-start(bf16[4,64,128]{2,1,0:T(8,128)(2,1)} %get-tuple-element.44), channel_id=1, source_target_pairs={{8,0},{0,8},{24,16},{16,24},{9,1},{1,9},{25,17},{17,25},{10,2},{2,... | collective-permute-start | bytes 196616 | tf_op jit(solution)/shard_map/ppermute | solution.py:73
  6.9 3.6 %collective-permute-start.2 = (bf16[4,64,128]{2,1,0:T(8,128)(2,1)S(1)}, bf16[4,64,128]{2,1,0:T(8,128)(2,1)S(1)}, u32[]{:S(2)}, u32[]{:S(2)}) collective-permute-start(bf16[4,64,128]{2,1,0:T(8,128)(2,1)S(1)} %collective-permute-done.refs_5_), channel_id=1, source_target_pairs={{16,0},{24,8},{0,16},{8,24},{17,1},{25,9},{1,17},{9,25},{18,2},{26... | collective-permute-start | bytes 196616 | tf_op jit(solution)/shard_map/ppermute | solution.py:73
  8.2 6.9 %collective-permute-start.4 = (bf16[14,64,128]{2,1,0:T(8,128)(2,1)S(1)}, bf16[14,64,128]{2,1,0:T(8,128)(2,1)S(1)}, u32[]{:S(2)}, u32[]{:S(2)}) collective-permute-start(bf16[14,64,128]{2,1,0:T(8,128)(2,1)S(1)} %get-tuple-element.45.refs_5_), channel_id=1, source_target_pairs={{4,0},{0,4},{5,1},{1,5},{6,2},{2,6},{7,3},{3,7},{12,8},{8,12},{13,... | collective-permute-start | bytes 688136 | tf_op jit(solution)/shard_map/ppermute | solution.py:73
  11.5 2.1 %collective-permute-start.6 = (bf16[384,128]{1,0:T(8,128)(2,1)S(1)}, bf16[384,128]{1,0:T(8,128)(2,1)S(1)}, u32[]{:S(2)}, u32[]{:S(2)}) collective-permute-start(bf16[384,128]{1,0:T(8,128)(2,1)S(1)} %get-tuple-element.52), channel_id=1, source_target_pairs={{8,0},{0,8},{24,16},{16,24},{9,1},{1,9},{25,17},{17,25},{10,2},{2,... | collective-permute-start | bytes 294920 | tf_op jit(solution)/shard_map/ppermute | solution.py:73
  12.4 1.3 %collective-permute-start.7 = (bf16[384,128]{1,0:T(8,128)(2,1)S(1)}, bf16[384,128]{1,0:T(8,128)(2,1)S(1)}, u32[]{:S(2)}, u32[]{:S(2)}) collective-permute-start(bf16[384,128]{1,0:T(8,128)(2,1)S(1)} %get-tuple-element.53), channel_id=1, source_target_pairs={{8,0},{0,8},{24,16},{16,24},{9,1},{1,9},{25,17},{17,25},{10,2},{2,... | collective-permute-start | bytes 294920 | tf_op jit(solution)/shard_map/ppermute | solution.py:73
  12.4 4.2 %collective-permute-start.5 = (bf16[4,64,128]{2,1,0:T(8,128)(2,1)S(1)}, bf16[4,64,128]{2,1,0:T(8,128)(2,1)S(1)}, u32[]{:S(2)}, u32[]{:S(2)}) collective-permute-start(bf16[4,64,128]{2,1,0:T(8,128)(2,1)S(1)} %shard_map.131.refs_7_), channel_id=1, source_target_pairs={{4,0},{0,4},{5,1},{1,5},{6,2},{2,6},{7,3},{3,7},{12,8},{8,12},{13,... | collective-permute-start | bytes 196616 | tf_op jit(solution)/shard_map/ppermute | solution.py:73
  13.7 4.2 %collective-permute-start.8 = (bf16[384,128]{1,0:T(8,128)(2,1)S(1)}, bf16[384,128]{1,0:T(8,128)(2,1)S(1)}, u32[]{:S(2)}, u32[]{:S(2)}) collective-permute-start(bf16[384,128]{1,0:T(8,128)(2,1)S(1)} %get-tuple-element.58), channel_id=1, source_target_pairs={{16,0},{24,8},{0,16},{8,24},{17,1},{25,9},{1,17},{9,25},{18,2},{26... | collective-permute-start | bytes 294920 | tf_op jit(solution)/shard_map/ppermute | solution.py:73
  17.9 2.5 %collective-permute-start.9 = (bf16[896,128]{1,0:T(8,128)(2,1)S(1)}, bf16[896,128]{1,0:T(8,128)(2,1)S(1)}, u32[]{:S(2)}, u32[]{:S(2)}) collective-permute-start(bf16[896,128]{1,0:T(8,128)(2,1)S(1)} %get-tuple-element.59), channel_id=1, source_target_pairs={{8,0},{0,8},{24,16},{16,24},{9,1},{1,9},{25,17},{17,25},{10,2},{2,... | collective-permute-start | bytes 688136 | tf_op jit(solution)/shard_map/ppermute | solution.py:73
  19.1 4.1 %collective-permute-start.13 = (bf16[288,128]{1,0:T(8,128)(2,1)S(1)}, bf16[288,128]{1,0:T(8,128)(2,1)S(1)}, u32[]{:S(2)}, u32[]{:S(2)}) collective-permute-start(bf16[288,128]{1,0:T(8,128)(2,1)S(1)} %get-tuple-element.61.refs_2_), channel_id=1, source_target_pairs={{4,0},{0,4},{5,1},{1,5},{6,2},{2,6},{7,3},{3,7},{12,8},{8,12},{13,... | collective-permute-start | bytes 221192 | tf_op jit(solution)/shard_map/ppermute | solution.py:73
  20.5 6.6 %collective-permute-start.12 = (bf16[272,128]{1,0:T(8,128)(2,1)S(1)}, bf16[272,128]{1,0:T(8,128)(2,1)S(1)}, u32[]{:S(2)}, u32[]{:S(2)}) collective-permute-start(bf16[272,128]{1,0:T(8,128)(2,1)S(1)} %get-tuple-element.65), channel_id=1, source_target_pairs={{20,0},{16,4},{28,8},{24,12},{4,16},{0,20},{12,24},{8,28},{21,1},{... | collective-permute-start | bytes 208904 | tf_op jit(solution)/shard_map/ppermute | solution.py:81
  22.4 4.6 %collective-permute-start.10 = (bf16[256,128]{1,0:T(8,128)(2,1)S(1)}, bf16[256,128]{1,0:T(8,128)(2,1)S(1)}, u32[]{:S(2)}, u32[]{:S(2)}) collective-permute-start(bf16[256,128]{1,0:T(8,128)(2,1)S(1)} %get-tuple-element.62), channel_id=1, source_target_pairs={{16,0},{24,8},{0,16},{8,24},{17,1},{25,9},{1,17},{9,25},{18,2},{26... | collective-permute-start | bytes 196616 | tf_op jit(solution)/shard_map/ppermute | solution.py:73
  22.8 3.2 %collective-permute-start.11 = (bf16[192,128]{1,0:T(8,128)(2,1)S(1)}, bf16[192,128]{1,0:T(8,128)(2,1)S(1)}, u32[]{:S(2)}, u32[]{:S(2)}) collective-permute-start(bf16[192,128]{1,0:T(8,128)(2,1)S(1)} %get-tuple-element.64), channel_id=1, source_target_pairs={{4,0},{0,4},{5,1},{1,5},{6,2},{2,6},{7,3},{3,7},{12,8},{8,12},{13,... | collective-permute-start | bytes 147464 | tf_op jit(solution)/shard_map/ppermute | solution.py:73
  23.2 5.2 %collective-permute-start.15 = (bf16[192,128]{1,0:T(8,128)(2,1)S(1)}, bf16[192,128]{1,0:T(8,128)(2,1)S(1)}, u32[]{:S(2)}, u32[]{:S(2)}) collective-permute-start(bf16[192,128]{1,0:T(8,128)(2,1)S(1)} %shard_map.140.refs_0_), channel_id=1, source_target_pairs={{1,0},{0,1},{3,2},{2,3},{5,4},{4,5},{7,6},{6,7},{9,8},{8,9},{11,10... | collective-permute-start | bytes 147464 | tf_op jit(solution)/shard_map/ppermute | solution.py:73
  27.1 5.4 %copy-start.8 = (bf16[3,3,128,128]{3,2,1,0:T(8,128)(2,1)S(1)}, bf16[3,3,128,128]{3,2,1,0:T(8,128)(2,1)}, u32[]{:S(2)}) copy-start(bf16[3,3,128,128]{3,2,1,0:T(8,128)(2,1)} %refs_4_.5) | copy-start | bytes 884740
  27.1 3.7 %collective-permute-start.14 = (bf16[192,128]{1,0:T(8,128)(2,1)S(1)}, bf16[192,128]{1,0:T(8,128)(2,1)S(1)}, u32[]{:S(2)}, u32[]{:S(2)}) collective-permute-start(bf16[192,128]{1,0:T(8,128)(2,1)S(1)} %shard_map.139.refs_0_), channel_id=1, source_target_pairs={{1,0},{0,1},{3,2},{2,3},{5,4},{4,5},{7,6},{6,7},{9,8},{8,9},{11,10... | collective-permute-start | bytes 147464 | tf_op jit(solution)/shard_map/ppermute | solution.py:73
  28.5 5.5 %collective-permute-start.17 = (bf16[192,128]{1,0:T(8,128)(2,1)S(1)}, bf16[192,128]{1,0:T(8,128)(2,1)S(1)}, u32[]{:S(2)}, u32[]{:S(2)}) collective-permute-start(bf16[192,128]{1,0:T(8,128)(2,1)S(1)} %shard_map.143.refs_2_), channel_id=1, source_target_pairs={{2,0},{3,1},{0,2},{1,3},{6,4},{7,5},{4,6},{5,7},{10,8},{11,9},{8,1... | collective-permute-start | bytes 147464 | tf_op jit(solution)/shard_map/ppermute | solution.py:73
  30.9 4.6 %collective-permute-start.16 = (bf16[192,128]{1,0:T(8,128)(2,1)S(1)}, bf16[192,128]{1,0:T(8,128)(2,1)S(1)}, u32[]{:S(2)}, u32[]{:S(2)}) collective-permute-start(bf16[192,128]{1,0:T(8,128)(2,1)S(1)} %shard_map.141.refs_5_.refs_0_), channel_id=1, source_target_pairs={{2,0},{3,1},{0,2},{1,3},{6,4},{7,5},{4,6},{5,7},{10,8},{11,9},{8,1... | collective-permute-start | bytes 147464 | tf_op jit(solution)/shard_map/ppermute | solution.py:73
  35.5 5.3 %collective-permute-start.20 = (bf16[2,192,128]{2,1,0:T(8,128)(2,1)S(1)}, bf16[2,192,128]{2,1,0:T(8,128)(2,1)S(1)}, u32[]{:S(2)}, u32[]{:S(2)}) collective-permute-start(bf16[2,192,128]{2,1,0:T(8,128)(2,1)S(1)} %shard_map.144.refs_0_), channel_id=1, source_target_pairs={{4,0},{0,4},{5,1},{1,5},{6,2},{2,6},{7,3},{3,7},{12,8},{8,12},{13,... | collective-permute-start | bytes 294920 | tf_op jit(solution)/shard_map/ppermute | solution.py:73
  36.4 6.4 %collective-permute-start.21 = (bf16[2,192,128]{2,1,0:T(8,128)(2,1)S(1)}, bf16[2,192,128]{2,1,0:T(8,128)(2,1)S(1)}, u32[]{:S(2)}, u32[]{:S(2)}) collective-permute-start(bf16[2,192,128]{2,1,0:T(8,128)(2,1)S(1)} %shard_map.144.refs_0_), channel_id=1, source_target_pairs={{16,0},{24,8},{0,16},{8,24},{17,1},{25,9},{1,17},{9,25},{18,2},{26... | collective-permute-start | bytes 294920 | tf_op jit(solution)/shard_map/ppermute | solution.py:73
  37.0 6.3 %collective-permute-start.18 = (bf16[2,192,128]{2,1,0:T(8,128)(2,1)S(1)}, bf16[2,192,128]{2,1,0:T(8,128)(2,1)S(1)}, u32[]{:S(2)}, u32[]{:S(2)}) collective-permute-start(bf16[2,192,128]{2,1,0:T(8,128)(2,1)S(1)} %shard_map.144.refs_0_), channel_id=1, source_target_pairs={{20,0},{16,4},{28,8},{24,12},{4,16},{0,20},{12,24},{8,28},{21,1},{... | collective-permute-start | bytes 294920 | tf_op jit(solution)/shard_map/ppermute | solution.py:81
  38.2 6.7 %collective-permute-start.22 = (bf16[2,192,128]{2,1,0:T(8,128)(2,1)S(1)}, bf16[2,192,128]{2,1,0:T(8,128)(2,1)S(1)}, u32[]{:S(2)}, u32[]{:S(2)}) collective-permute-start(bf16[2,192,128]{2,1,0:T(8,128)(2,1)S(1)} %shard_map.144.refs_0_), channel_id=1, source_target_pairs={{8,0},{0,8},{24,16},{16,24},{9,1},{1,9},{25,17},{17,25},{10,2},{2,... | collective-permute-start | bytes 294920 | tf_op jit(solution)/shard_map/ppermute | solution.py:73
  40.8 4.1 %collective-permute-start.23 = (bf16[2,192,128]{2,1,0:T(8,128)(2,1)S(1)}, bf16[2,192,128]{2,1,0:T(8,128)(2,1)S(1)}, u32[]{:S(2)}, u32[]{:S(2)}) collective-permute-start(bf16[2,192,128]{2,1,0:T(8,128)(2,1)S(1)} %collective-permute-done.20.refs_1_), channel_id=1, source_target_pairs={{8,0},{0,8},{24,16},{16,24},{9,1},{1,9},{25,17},{17,25},{10,2},{2,... | collective-permute-start | bytes 294920 | tf_op jit(solution)/shard_map/ppermute | solution.py:73
  42.8 2.1 %collective-permute-start.24 = (bf16[2,192,128]{2,1,0:T(8,128)(2,1)S(1)}, bf16[2,192,128]{2,1,0:T(8,128)(2,1)S(1)}, u32[]{:S(2)}, u32[]{:S(2)}) collective-permute-start(bf16[2,192,128]{2,1,0:T(8,128)(2,1)S(1)} %collective-permute-done.21.refs_2_), channel_id=1, source_target_pairs={{8,0},{0,8},{24,16},{16,24},{9,1},{1,9},{25,17},{17,25},{10,2},{2,... | collective-permute-start | bytes 294920 | tf_op jit(solution)/shard_map/ppermute | solution.py:73
  43.3 2.8 %collective-permute-start.19 = (bf16[2,192,128]{2,1,0:T(8,128)(2,1)S(1)}, bf16[2,192,128]{2,1,0:T(8,128)(2,1)S(1)}, u32[]{:S(2)}, u32[]{:S(2)}) collective-permute-start(bf16[2,192,128]{2,1,0:T(8,128)(2,1)S(1)} %collective-permute-done.18.refs_6_), channel_id=1, source_target_pairs={{8,0},{0,8},{24,16},{16,24},{9,1},{1,9},{25,17},{17,25},{10,2},{2,... | collective-permute-start | bytes 294920 | tf_op jit(solution)/shard_map/ppermute | solution.py:73
  (2 other events, 6.1 us)
